TPU v7x, 32 devices: a whole 2x2x4 slice. The times are simulated.
32 devices in a mesh: tm: 8 (over y, x, core), dp: 4 (over z).
Axes of the slice: x: 2, y: 2, z: 4, core: 2. Of those that a mesh axis runs over, the one named last changes fastest.
Arguments:
- layer_in: bfloat16 [4, 1024, 2560], P('dp', 'tm'), may hold values from -6 to 6
- out_grad: bfloat16 [4, 1024, 2560], P('dp', 'tm'), may hold values from -6 to 6
- w_bc: bfloat16 [2560, 256], P('dp'), may hold values from -0.009765625 to 0.009765625
- log_decay: float32 [4, 1024, 40], P('dp', 'tm'), may hold values from -2 to 0
- step: float32 [4, 1024, 40], P('dp', 'tm'), may hold values from 0.02 to 0.2
- saved_states: bfloat16 [4, 8, 40, 64, 128], P('dp', 'tm'), may hold values from -3 to 3
- w_gate: bfloat16 [1, 2560, 7168], P(None, None, 'tm'), may hold values from -0.125 to 0.125
- w_up: bfloat16 [1, 2560, 7168], P(None, None, 'tm'), may hold values from -0.125 to 0.125
- slot_rows: int32 [4, 1, 128], P('dp', None, 'tm'), may hold values from 0 to 127, as said below
- slot_counts: int32 [4, 8], P('dp', 'tm'), may hold values from 4 to 16, as said below
- slot_gates: bfloat16 [4, 1, 128], P('dp', None, 'tm'), may hold values from 0.099609375 to 0.8984375
Outputs:
- in_grad: bfloat16 [4, 1024, 2560], P('dp', 'tm')
- decay_grad: float32 [4, 1024, 40], P('dp', 'tm')
- step_grad: float32 [4, 1024, 40], P('dp', 'tm')
- w_bc_grad: float32 [2560, 256], P(('tm', 'dp'))
- w_down_grad: bfloat16 [1, 7168, 2560], P(None, 'tm', 'dp')
Inputs may be any that keep to these rules, and one draw needn't show every extreme that they name: `slot_rows`: among the used slots of one expert in one shard the frames are distinct. `slot_counts`: the count 16 is reached in some shard of every recording, and in every shard of some recording, for each expert.
All inputs are finite; a program needn't handle non-finite values.
Results may differ from a plain program's by a relative error of at most 0.009.
Values may be sent and summed in bfloat16 or wider, within the bound.
No kernel may reach another device: no remote copies, remote signals or barrier semaphores. Data moves between devices by JAX's collectives and lax.ppermute only.
A program may use at most 128 MiB of HBM per device.

v0:
```python
import jax
import jax.numpy as jnp
from jax import lax
from jax.sharding import PartitionSpec as P

HI = lax.Precision.HIGHEST


def entering(array, axis, join, neutral):
    count = lax.axis_size(axis)
    place = lax.axis_index(axis)
    ahead = count - 1 - place
    gathered = jax.tree.map(
        lambda a, kind: lax.all_gather(a.astype(kind), axis),
        array,
        jax.tree.map(lambda a: jnp.bfloat16 if a.dtype == jnp.float32 else a.dtype, array),
    )
    state = jax.tree.map(lambda a, e: jnp.zeros_like(a) + jnp.asarray(e, a.dtype), array, neutral)

    def one(turn, state):
        source = count - 1 - turn
        return join(
            state,
            jax.tree.map(
                lambda a, own: lax.dynamic_index_in_dim(a, source, 0, False).astype(own.dtype),
                gathered,
                array,
            ),
        )

    return lax.fori_loop(0, ahead, one, state)


def local_terms(layer_in, out_grad, w_bc, log_decay, step):
    length, width = layer_in.shape
    heads = log_decay.shape[1]
    size = width // heads
    bc = jnp.dot(layer_in, w_bc, preferred_element_type=jnp.float32).astype(jnp.bfloat16)
    states = bc.shape[1] // 2
    b_rows = bc[:, :states]
    c_rows = bc[:, states:]
    cum_cols = jnp.cumsum(log_decay, axis=0).T
    total = cum_cols[:, -1]
    step_cols = step.T
    input_cols = layer_in.T.reshape(heads, size, length)
    grad_cols = out_grad.T.reshape(heads, size, length)
    inputs = input_cols.astype(jnp.float32)
    grads = grad_cols.astype(jnp.float32)
    into_end = jnp.exp(total[:, None] - cum_cols) * step_cols
    s_local = jnp.einsum(
        "hpt,tn->hpn", inputs * into_end[:, None, :], b_rows.astype(jnp.float32), precision=HI
    )
    g_local = jnp.einsum(
        "hpt,tn->hpn",
        grads * jnp.exp(cum_cols)[:, None, :],
        c_rows.astype(jnp.float32),
        precision=HI,
    )
    context = (
        input_cols,
        grad_cols,
        layer_in,
        w_bc,
        step_cols,
        cum_cols,
        b_rows,
        c_rows,
        s_local,
        total,
    )
    return (context, (jnp.exp(total), g_local))


def finish(context, h_in, r_grad):
    input_cols, grad_cols, layer_in, w_bc, step_cols, cum_cols, b_rows, c_rows, s_local, total = (
        context
    )
    heads, size, length = input_cols.shape
    width = heads * size
    inputs = input_cols.astype(jnp.float32)
    grads = grad_cols.astype(jnp.float32)
    b_full = b_rows.astype(jnp.float32)
    c_full = c_rows.astype(jnp.float32)
    order = jnp.arange(length)
    lower = order[:, None] >= order[None, :]
    diff = cum_cols[:, :, None] - cum_cols[:, None, :]
    seg = jnp.where(lower[None], jnp.exp(jnp.minimum(diff, 0.0)), 0.0)
    scores = jnp.dot(c_rows, b_rows.T, preferred_element_type=jnp.float32)
    kern = seg * scores[None]
    from_start = jnp.exp(cum_cols)
    to_end = jnp.exp(total[:, None] - cum_cols)
    produced_results = jnp.einsum(
        "hts,hps->hpt", kern * step_cols[:, None, :], inputs, precision=HI
    )
    produced_results = produced_results + from_start[:, None, :] * jnp.einsum(
        "hpn,tn->hpt", h_in, c_full, precision=HI
    )
    back = jnp.einsum("hrt,hpr->hpt", kern, grads, precision=HI)
    back = back + to_end[:, None, :] * jnp.einsum("hpn,tn->hpt", r_grad, b_full, precision=HI)
    d_inputs = step_cols[:, None, :] * back
    d_step = jnp.sum(inputs * back, axis=1).T
    cross = jnp.einsum("hpa,hpb->hab", grad_cols, input_cols, preferred_element_type=jnp.float32)
    mixed = seg * cross * step_cols[:, None, :]
    d_b = jnp.einsum("hab,an->bn", mixed, c_full, precision=HI) + jnp.einsum(
        "hpt,hpn->tn", inputs * (to_end * step_cols)[:, None, :], r_grad, precision=HI
    )
    d_c = jnp.einsum("hab,bn->an", mixed, b_full, precision=HI) + jnp.einsum(
        "hpt,hpn->tn", grads * from_start[:, None, :], h_in, precision=HI
    )
    h_last = jnp.exp(total)[:, None, None] * h_in + s_local
    edge = jnp.sum(r_grad * h_last, axis=(1, 2))
    excess = jnp.sum(grads * produced_results, axis=1) - jnp.sum(inputs * d_inputs, axis=1)
    d_decay = (jnp.cumsum(excess[:, ::-1], axis=1)[:, ::-1] + edge[:, None]).T
    d_bc = jnp.concatenate([d_b, d_c], axis=1).astype(jnp.bfloat16)
    d_in = d_inputs.reshape(width, length).T + jnp.einsum(
        "tn,dn->td", d_bc, w_bc, preferred_element_type=jnp.float32
    )
    w_term = jnp.einsum("td,tn->dn", layer_in, d_bc, preferred_element_type=jnp.float32)
    return (d_in.astype(jnp.bfloat16), d_decay, d_step, w_term)


def combine_states(earlier, later):
    return (earlier[0] * later[0], later[1] + later[0][:, None, None] * earlier[1])


def per_device(
    layer_in,
    out_grad,
    w_bc,
    log_decay,
    step,
    saved_states,
    w_gate,
    w_up,
    slot_rows,
    slot_counts,
    slot_gates,
):
    frames_in = layer_in[0]
    timestep_derivative = out_grad[0]
    w_whole = lax.all_gather(w_bc, "dp", axis=0, tiled=True)
    context, backward_items = local_terms(
        frames_in, timestep_derivative, w_whole, log_decay[0], step[0]
    )
    identity = (jnp.ones_like(backward_items[0]), jnp.zeros_like(backward_items[1]))
    r_grad = entering(backward_items, "tm", combine_states, identity)[1]
    h_in = saved_states[0, 0].astype(jnp.float32)
    d_in, d_decay, d_step, w_term = finish(context, h_in, r_grad)
    w_bc_grad = lax.psum_scatter(w_term, ("tm", "dp"), scatter_dimension=0, tiled=True)
    length = frames_in.shape[0]
    chosen = slot_rows[0]
    counts = slot_counts[0]
    capacity = chosen.shape[1]
    pick = (chosen[:, :, None] == jnp.arange(length)[None, None, :]).astype(jnp.bfloat16)
    rows_in = jnp.einsum("ecl,ld->ecd", pick, frames_in, preferred_element_type=jnp.float32).astype(
        jnp.bfloat16
    )
    rows_grad = jnp.einsum(
        "ecl,ld->ecd", pick, timestep_derivative, preferred_element_type=jnp.float32
    ).astype(jnp.bfloat16)
    live = jnp.arange(capacity)[None, :] < counts[:, None]
    weights = jnp.where(live, slot_gates[0], jnp.zeros_like(slot_gates[0]))
    piece_in = lax.all_gather(rows_in, "tm", axis=1, tiled=True)
    segment_gradient = lax.all_gather(rows_grad, "tm", axis=1, tiled=True)
    piece_weight = lax.all_gather(weights, "tm", axis=1, tiled=True)
    gate_h = jnp.einsum("ekd,edf->ekf", piece_in, w_gate, preferred_element_type=jnp.float32)
    up_h = jnp.einsum("ekd,edf->ekf", piece_in, w_up, preferred_element_type=jnp.float32)
    weighted = (jax.nn.silu(gate_h) * up_h * piece_weight.astype(jnp.float32)[:, :, None]).astype(
        jnp.bfloat16
    )
    partial_grad = jnp.einsum(
        "ekf,ekd->efd", weighted, segment_gradient, preferred_element_type=jnp.float32
    )
    partial_grad = partial_grad.astype(jnp.bfloat16).astype(jnp.float32)
    w_down_grad = lax.psum_scatter(
        partial_grad.astype(jnp.bfloat16), "dp", scatter_dimension=2, tiled=True
    )
    return (d_in[None], d_decay[None], d_step[None], w_bc_grad, w_down_grad)


def solution(mesh):
    in_specs = (
        P("dp", "tm", None),
        P("dp", "tm", None),
        P("dp", None),
        P("dp", "tm", None),
        P("dp", "tm", None),
        P("dp", "tm", None, None, None),
        P(None, None, "tm"),
        P(None, None, "tm"),
        P("dp", None, "tm"),
        P("dp", "tm"),
        P("dp", None, "tm"),
    )
    out_specs = (
        P("dp", "tm", None),
        P("dp", "tm", None),
        P("dp", "tm", None),
        P(("tm", "dp"), None),
        P(None, "tm", "dp"),
    )
    return jax.shard_map(
        per_device, mesh=mesh, in_specs=in_specs, out_specs=out_specs, check_vma=False
    )
```

profile of v0, /device:TPU:0, one launch (start us, length us, event | category | flops | bytes accessed | tf_op | source)
XLA Modules:
  0.0 357.2 jit_solution(4967195726796135597)
XLA Ops:
  9.0 1.4 copy.65
  11.3 33.7 %all-gather.7.cloned.1.call-done = bf16[2560,256]{1,0:T(8,128)(2,1)} async-done(((bf16[640,256]{1,0:T(8,128)(2,1)}), bf16[2560,256]{1,0:T(8,128)(2,1)}) %all-gather.7.cloned.1.call-update) | async-done | bytes 1310736 | tf_op jit(solution)/shard_map/all_gather | solution.py:141
  45.0 1.7 convolution_convert_fusion.4
  46.7 1.6 convolution_convert_fusion.3
  51.7 13.3 %all-reduce.2 = (bf16[320]{0:T(512)(128)(2,1)S(1)}, bf16[128]{0:T(256)(128)(2,1)S(1)}) all-reduce(bf16[320]{0:T(512)(128)(2,1)S(1)} %dynamic-update-slice, bf16[128]{0:T(256)(128)(2,1)S(1)} %dynamic-update-slice.1), channel_id=3, replica_groups=mesh['tm'=8,'dp'=4] {'tm'}, use_global_device_ids=true, to_apply=%add | all-reduce | flops 448 | bytes 1792
  65.3 10.6 %all-gather.2 = bf16[128,2560]{1,0:T(8,128)(2,1)S(1)} all-gather(bf16[16,2560]{1,0:T(8,128)(2,1)S(1)} %convolution_convert_fusion.2), channel_id=4, replica_groups=mesh['tm'=8,'dp'=4] {'tm'}, dimensions={0}, use_global_device_ids=true | all-gather | bytes 737280 | tf_op jit(solution)/shard_map/all_gather | solution.py:163
  76.1 13.4 %all-gather.3 = bf16[128,2560]{1,0:T(8,128)(2,1)S(1)} all-gather(bf16[16,2560]{1,0:T(8,128)(2,1)S(1)} %convolution_convert_fusion.1), channel_id=5, replica_groups=mesh['tm'=8,'dp'=4] {'tm'}, dimensions={0}, use_global_device_ids=true | all-gather | bytes 737280 | tf_op jit(solution)/shard_map/all_gather | solution.py:164
  89.5 3.2 fusion.3
  92.8 6.5 %fusion = bf16[1,896,2560]{2,1,0:T(8,128)(2,1)} fusion(bf16[128,2560]{1,0:T(8,128)(2,1)S(1)} %all-gather.3, bf16[128,2560]{1,0:T(8,128)(2,1)S(1)} %all-gather.2, bf16[1,2560,896]{2,1,0:T(8,128)(2,1)} %param.20, f32[128,896]{1,0:T(8,128)S(1)} %fusion.3, f32[128]{0:T(128)S(1)} %mul.176), kind=kOutput, calls=%fused_computation.3 | convolution fusion | flops 1177501696 | bytes 10945024 | tf_op jit(solution)/shard_map/ekf,ekd->efd/dot_general | solution.py:171
  99.3 19.2 %copy.71 = bf16[1,896,2560]{1,0,2:T(2,128)(2,1)} copy(bf16[1,896,2560]{2,1,0:T(8,128)(2,1)} %fusion) | data formatting | bytes 9175040
  118.5 6.4 %copy.75 = bf16[2560,1,896]{2,0,1:T(8,128)(2,1)} copy(bf16[2560,1,896]{2,1,0:T(2,128)(2,1)} %bitcast.146) | data formatting | bytes 9175040
  128.3 10.5 %while.14 = (s32[]{:T(128)}, f32[40,64,128]{2,1,0:T(8,128)S(1)}, s32[]{:T(128)}, bf16[8,40,64,128]{3,2,1,0:T(8,128)(2,1)}, bf16[8,40]{1,0:T(8,128)(2,1)S(1)}, /*index=5*/s32[]{:T(128)}, s32[]{:T(128)}, s32[]{:T(128)}, s32[]{:T(128)}) while((s32[]{:T(128)}, f32[40,64,128]{2,1,0:T(8,128)S(1)}, s32[]{:T(128)}, ...), condition=%wide.region_2.3_spmd, body=%wide.region_1.2_spmd.sunk | while | flops 983086 | bytes 3277355 | solution.py:31
  129.7 1.6 convert_add_fusion.2
  138.8 2.2 fusion.50
  141.2 2.0 convolution_bitcast_fusion
  143.3 3.2 copy.69
  147.3 3.2 fusion.21
  151.0 3.0 fusion.18
  154.0 53.1 %reduce-scatter.9.cloned.1.call-done = bf16[640,896]{1,0:T(8,128)(2,1)} async-done(((bf16[2560,896]{1,0:T(8,128)(2,1)}), bf16[640,896]{1,0:T(8,128)(2,1)}) %reduce-scatter.9.cloned.1.call-update) | async-done | bytes 1146896
  207.1 3.8 %reshape_bitcast_fusion = bf16[1,896,640]{1,0,2:T(2,128)(2,1)} fusion(bf16[640,896]{1,0:T(8,128)(2,1)} %reduce-scatter.9.cloned.1.call-done), kind=kLoop, calls=%fused_computation.21 | loop fusion | bytes 2293760
  210.9 5.5 %copy.72 = bf16[1,896,640]{2,1,0:T(8,128)(2,1)} copy(bf16[1,896,640]{1,0,2:T(2,128)(2,1)} %reshape_bitcast_fusion) | data formatting | bytes 2293760
  216.4 4.0 %fusion.27 = (f32[40,128]{1,0:T(8,128)}, f32[40,128]{1,0:T(8,128)S(1)}, f32[40,64,128]{2,1,0:T(8,128)}) fusion(bf16[40,64,128]{2,1,0:T(8,128)(2,1)S(1)} %bitcast.156, f32[40,128]{1,0:T(8,128)S(1)} %bitcast.168, f32[40,64,128]{2,1,0:T(8,128)} %fusion.18, f32[40,64,128]{2,1,0:T(8,128)S(1)} %get-tuple-element.89, ...), kind=kOutput, calls=%fused_computation.40 | convolution fusion | flops 505927680 | bytes 4702208 | tf_op jit(solution)/shard_map/hpn,tn->hpt/dot_general | solution.py:99
  220.9 2.8 copy.66
  226.8 123.9 %reduce-scatter.7.cloned.1.call-done = f32[80,256]{1,0:T(8,128)} async-done(((f32[2560,256]{1,0:T(8,128)}), f32[80,256]{1,0:T(8,128)}) %reduce-scatter.7.cloned.1.call-update) | async-done | bytes 81936
  (86 shorter events, 21.3 us)
Async XLA Ops:
  7.2 3.5 copy-start.6
  7.2 37.8 %copy-start = (bf16[1,128,2560]{2,1,0:T(8,128)(2,1)S(1)}, bf16[1,128,2560]{2,1,0:T(8,128)(2,1)}, u32[]{:S(2)}) copy-start(bf16[1,128,2560]{2,1,0:T(8,128)(2,1)} %param.13) | copy-start | bytes 1966084
  7.2 37.8 %all-gather.7.cloned.1.call-start = ((), (), s32[]{:S(2)}) async-start(), calls=%async_computation.2 | async-start | bytes 1638400 | tf_op jit(solution)/shard_map/all_gather | solution.py:141
  7.9 120.2 %all-gather.9.cloned.1.call-start = ((), (), s32[]{:S(2)}) async-start(), calls=%async_computation.3 | async-start | bytes 5898240 | tf_op jit(solution)/shard_map/all_gather | solution.py:14
  10.6 34.4 %copy-start.11 = (f32[40]{0:T(128)}, f32[40]{0:T(128)S(1)}, u32[]{:S(2)}) copy-start(f32[40]{0:T(128)S(1)} %slice_reduce_fusion) | copy-start | bytes 484
  46.7 2.4 copy-start.14
  46.7 4.3 %copy-start.13 = (bf16[1,1,16]{2,1,0:T(2,128)(2,1)S(1)}, bf16[1,1,16]{2,1,0:T(2,128)(2,1)}, u32[]{:S(2)}) copy-start(bf16[1,1,16]{2,1,0:T(2,128)(2,1)} %param.23) | copy-start | bytes 100
  46.7 18.3 %copy-start.10 = (s32[1,1,16]{2,1,0:T(1,128)S(1)}, s32[1,1,16]{2,1,0:T(1,128)}, u32[]{:S(2)}) copy-start(s32[1,1,16]{2,1,0:T(1,128)} %param.21) | copy-start | bytes 196
  48.3 27.5 %copy-start.5 = (bf16[1,128,2560]{2,1,0:T(8,128)(2,1)S(1)}, bf16[1,128,2560]{2,1,0:T(8,128)(2,1)}, u32[]{:S(2)}) copy-start(bf16[1,128,2560]{2,1,0:T(8,128)(2,1)} %param.14) | copy-start | bytes 1966084
  48.4 158.7 %reduce-scatter.9.cloned.1.call-start = ((), (), s32[]{:S(2)}) async-start(), calls=%async_computation.5 | async-start | bytes 5734400
  125.0 225.8 %reduce-scatter.7.cloned.1.call-start = ((), (), s32[]{:S(2)}) async-start(), calls=%async_computation.4 | async-start | bytes 2703360
  125.6 1.4 copy-start.8
  125.6 1.6 copy-start.1
  146.5 0.7 copy-start.12
  146.5 0.8 copy-start.9
  147.3 3.2 copy-start.2
  210.9 5.5 %copy-start.7 = (f32[40,128]{1,0:T(8,128)S(1)}, f32[40,128]{1,0:T(8,128)}, u32[]{:S(2)}) copy-start(f32[40,128]{1,0:T(8,128)} %get-tuple-element.131) | copy-start | bytes 61444
  223.7 1.7 copy-start.3
  223.7 1.7 copy-start.4
Sparse Core Ops, SparseCore 0:
  9.6 35.3 all-gather.6
  48.5 43.5 all-gather.8
  125.1 81.9 reduce-scatter.8
  209.8 140.8 reduce-scatter.6
where the time goes:
time: 359 us; the launch traced here: 357 us
  waiting for transfers between devices  211 us (59%)
  local copies, waits for them, and re-layouts  46.1 us (13%)
  blocking collectives  37.3 us (10%)
  matrix products  33.7 us (9%)
  between operations  16 us (4%)
  other arithmetic  12.2 us (3%)
    unnamed x6, waiting for transfers between devices  178 us
    unnamed x41, local copies, waits for them, and re-layouts  41.5 us
    all_gather x1, waiting for transfers between devices, per_device(): w_whole = lax.all_gather(w_bc, 'dp', axis=0, tiled=True)  33.7 us
    all_gather x1, blocking collectives, per_device(): segment_gradient = lax.all_gather(rows_grad, 'tm', axis=1, tiled=True)  13.4 us
    unnamed x1, blocking collectives  13.3 us
    all_gather x1, blocking collectives, per_device(): piece_in = lax.all_gather(rows_in, 'tm', axis=1, tiled=True)  10.6 us
    add x7, other arithmetic, combine_states(): later[1] + later[0][:, None, None] * earlier[1]  10 us
  transfers between devices with their start and end apart: 4, of which 3 were waited for; matrix products, arithmetic and copies ran while one was open for 25% of the time, Pallas kernels for 0%

commit v1 on v0

--- a/solution.py
+++ b/solution.py
@@ -4,31 +4,6 @@
 from jax.sharding import PartitionSpec as P
 
 HI = lax.Precision.HIGHEST
-
-
-def entering(array, axis, join, neutral):
-    count = lax.axis_size(axis)
-    place = lax.axis_index(axis)
-    ahead = count - 1 - place
-    gathered = jax.tree.map(
-        lambda a, kind: lax.all_gather(a.astype(kind), axis),
-        array,
-        jax.tree.map(lambda a: jnp.bfloat16 if a.dtype == jnp.float32 else a.dtype, array),
-    )
-    state = jax.tree.map(lambda a, e: jnp.zeros_like(a) + jnp.asarray(e, a.dtype), array, neutral)
-
-    def one(turn, state):
-        source = count - 1 - turn
-        return join(
-            state,
-            jax.tree.map(
-                lambda a, own: lax.dynamic_index_in_dim(a, source, 0, False).astype(own.dtype),
-                gathered,
-                array,
-            ),
-        )
-
-    return lax.fori_loop(0, ahead, one, state)
 
 
 def local_terms(layer_in, out_grad, w_bc, log_decay, step):
@@ -115,12 +90,25 @@
     d_in = d_inputs.reshape(width, length).T + jnp.einsum(
         "tn,dn->td", d_bc, w_bc, preferred_element_type=jnp.float32
     )
-    w_term = jnp.einsum("td,tn->dn", layer_in, d_bc, preferred_element_type=jnp.float32)
-    return (d_in.astype(jnp.bfloat16), d_decay, d_step, w_term)
-
-
-def combine_states(earlier, later):
-    return (earlier[0] * later[0], later[1] + later[0][:, None, None] * earlier[1])
+    return (d_in.astype(jnp.bfloat16), d_decay, d_step, d_bc)
+
+
+def reverse_carry(decay, g_local):
+    count = lax.axis_size("tm")
+    heads, size, states = g_local.shape
+    rows = heads * size
+    parts = g_local.astype(jnp.bfloat16).reshape(count, rows // count, states)
+    parts = lax.all_to_all(parts, "tm", split_axis=0, concat_axis=0)
+    decays = jnp.repeat(lax.all_gather(decay, "tm"), size, axis=1)
+    place = lax.axis_index("tm")
+    decays = lax.dynamic_slice_in_dim(decays, place * (rows // count), rows // count, 1)
+    carry = jnp.zeros((rows // count, states), jnp.float32)
+    outs = [None] * count
+    for k in reversed(range(count)):
+        outs[k] = carry.astype(jnp.bfloat16)
+        carry = parts[k].astype(jnp.float32) + decays[k][:, None] * carry
+    back = lax.all_to_all(jnp.stack(outs), "tm", split_axis=0, concat_axis=0)
+    return back.reshape(heads, size, states).astype(jnp.float32)
 
 
 def per_device(
@@ -136,46 +124,55 @@
     slot_counts,
     slot_gates,
 ):
+    n_tm = lax.axis_size("tm")
+    n_dp = lax.axis_size("dp")
+    place = lax.axis_index("tm")
     frames_in = layer_in[0]
     timestep_derivative = out_grad[0]
-    w_whole = lax.all_gather(w_bc, "dp", axis=0, tiled=True)
-    context, backward_items = local_terms(
+    length, width = frames_in.shape
+    share = w_bc.shape[0] // n_tm
+    w_share = lax.dynamic_slice_in_dim(w_bc, place * share, share, 0)
+    w_whole = lax.all_gather(w_share, ("dp", "tm"), axis=0, tiled=True)
+
+    chosen = slot_rows[0, 0]
+    capacity = chosen.shape[0]
+    live = jnp.arange(capacity) < slot_counts[0, 0]
+    weights = jnp.where(live, slot_gates[0, 0], jnp.zeros_like(slot_gates[0, 0]))
+    pick = (chosen[:, None] == jnp.arange(length)[None, :]).astype(jnp.bfloat16)
+    rows_in = jnp.dot(pick, frames_in, preferred_element_type=jnp.float32).astype(jnp.bfloat16)
+    rows_grad = jnp.dot(pick, timestep_derivative, preferred_element_type=jnp.float32)
+    rows_grad = (rows_grad * weights.astype(jnp.float32)[:, None]).astype(jnp.bfloat16)
+    piece = width // n_dp
+    rows_grad = rows_grad.reshape(capacity, n_dp, piece).transpose(1, 0, 2)
+    rows_grad = lax.all_to_all(rows_grad, "dp", split_axis=0, concat_axis=0)
+    rows_in = rows_in.reshape(capacity, n_dp, piece).transpose(1, 0, 2)
+    rows = lax.all_gather(jnp.stack([rows_in, rows_grad]), "tm")
+    rows_in = rows[:, 0].transpose(0, 2, 1, 3).reshape(n_tm * capacity, width)
+    rows_grad = rows[:, 1].transpose(1, 0, 2, 3).reshape(n_dp * n_tm * capacity, piece)
+    gate_h = jnp.dot(rows_in, w_gate[0], preferred_element_type=jnp.float32)
+    up_h = jnp.dot(rows_in, w_up[0], preferred_element_type=jnp.float32)
+    weighted = (jax.nn.silu(gate_h) * up_h).astype(jnp.bfloat16)
+    weighted = lax.all_gather(weighted, "dp", axis=0, tiled=True)
+    w_down_grad = lax.dot_general(
+        weighted, rows_grad, (((0,), (0,)), ((), ())), preferred_element_type=jnp.float32
+    ).astype(jnp.bfloat16)
+
+    columns = frames_in.reshape(length, n_tm, width // n_tm).transpose(1, 0, 2)
+    columns = lax.all_to_all(columns, "tm", split_axis=0, concat_axis=0)
+    columns = columns.reshape(n_tm * length, width // n_tm)
+
+    context, (decay, g_local) = local_terms(
         frames_in, timestep_derivative, w_whole, log_decay[0], step[0]
     )
-    identity = (jnp.ones_like(backward_items[0]), jnp.zeros_like(backward_items[1]))
-    r_grad = entering(backward_items, "tm", combine_states, identity)[1]
+    r_grad = reverse_carry(decay, g_local)
     h_in = saved_states[0, 0].astype(jnp.float32)
-    d_in, d_decay, d_step, w_term = finish(context, h_in, r_grad)
-    w_bc_grad = lax.psum_scatter(w_term, ("tm", "dp"), scatter_dimension=0, tiled=True)
-    length = frames_in.shape[0]
-    chosen = slot_rows[0]
-    counts = slot_counts[0]
-    capacity = chosen.shape[1]
-    pick = (chosen[:, :, None] == jnp.arange(length)[None, None, :]).astype(jnp.bfloat16)
-    rows_in = jnp.einsum("ecl,ld->ecd", pick, frames_in, preferred_element_type=jnp.float32).astype(
-        jnp.bfloat16
-    )
-    rows_grad = jnp.einsum(
-        "ecl,ld->ecd", pick, timestep_derivative, preferred_element_type=jnp.float32
-    ).astype(jnp.bfloat16)
-    live = jnp.arange(capacity)[None, :] < counts[:, None]
-    weights = jnp.where(live, slot_gates[0], jnp.zeros_like(slot_gates[0]))
-    piece_in = lax.all_gather(rows_in, "tm", axis=1, tiled=True)
-    segment_gradient = lax.all_gather(rows_grad, "tm", axis=1, tiled=True)
-    piece_weight = lax.all_gather(weights, "tm", axis=1, tiled=True)
-    gate_h = jnp.einsum("ekd,edf->ekf", piece_in, w_gate, preferred_element_type=jnp.float32)
-    up_h = jnp.einsum("ekd,edf->ekf", piece_in, w_up, preferred_element_type=jnp.float32)
-    weighted = (jax.nn.silu(gate_h) * up_h * piece_weight.astype(jnp.float32)[:, :, None]).astype(
-        jnp.bfloat16
-    )
-    partial_grad = jnp.einsum(
-        "ekf,ekd->efd", weighted, segment_gradient, preferred_element_type=jnp.float32
-    )
-    partial_grad = partial_grad.astype(jnp.bfloat16).astype(jnp.float32)
-    w_down_grad = lax.psum_scatter(
-        partial_grad.astype(jnp.bfloat16), "dp", scatter_dimension=2, tiled=True
-    )
-    return (d_in[None], d_decay[None], d_step[None], w_bc_grad, w_down_grad)
+    d_in, d_decay, d_step, d_bc = finish(context, h_in, r_grad)
+    d_bc = lax.all_gather(d_bc, "tm", axis=0, tiled=True)
+    w_term = lax.dot_general(
+        columns, d_bc, (((0,), (0,)), ((), ())), preferred_element_type=jnp.float32
+    )
+    w_bc_grad = lax.psum_scatter(w_term, "dp", scatter_dimension=0, tiled=True)
+    return (d_in[None], d_decay[None], d_step[None], w_bc_grad, w_down_grad[None])
 
 
 def solution(mesh):

time: 359 us -> 193 us (0.54)
  waiting for transfers between devices: 211 us -> 52.7 us
  local copies, waits for them, and re-layouts: 46.1 us -> 8.63 us
  starting transfers between devices: 0.16 us -> 17.9 us
  blocking collectives: 37.3 us -> 46.6 us
  matrix products: 33.7 us -> 40.2 us
    unnamed x6 -> x3, waiting for transfers between devices: 178 us -> 0.08 us
    unnamed x41 -> x24, local copies, waits for them, and re-layouts: 41.5 us -> 2.37 us
    all_to_all x0 -> x4, starting transfers between devices: none -> 17.8 us  [the longest x1 6.32 us: per_device(): rows_grad = lax.all_to_all(rows_grad, 'dp', split_axis=0, concat_axis=0)]
    all_to_all x0 -> x4, waiting for transfers between devices: none -> 15 us  [the longest x1 8.29 us: reverse_carry(): parts = lax.all_to_all(parts, 'tm', split_axis=0, concat_axis=0)]
    all_gather x2, blocking collectives: 24 us -> 34.3 us  [the longest x1 21.6 us: per_device(): weighted = lax.all_gather(weighted, 'dp', axis=0, tiled=True)]
    add x7 -> x0, other arithmetic: 10 us -> none  [combine_states(): later[1] + later[0][:, None, None] * earlier[1]]
    reduce_scatter x0 -> x1, waiting for transfers between devices: none -> 9.18 us  [per_device(): w_bc_grad = lax.psum_scatter(w_term, 'dp', scatter_dimension=0, tiled=True)]
    unnamed x1 -> x7, other arithmetic: 0.01 us -> 5.58 us
  transfers between devices with their start and end apart: 4 -> 7, of which waited for: 3 -> 6; matrix products, arithmetic and copies ran while one was open for 25% -> 23% of each run, Pallas kernels for 0% -> 0%
where the time goes in v1:
time: 193 us; the launch traced here: 192 us
  waiting for transfers between devices  52.7 us (27%)
  blocking collectives  46.6 us (24%)
  matrix products  40.2 us (21%)
  starting transfers between devices  17.9 us (9%)
  between operations  15.4 us (8%)
  other arithmetic  10.6 us (5%)
  local copies, waits for them, and re-layouts  8.63 us (4%)
    all_gather x1, waiting for transfers between devices, per_device(): w_whole = lax.all_gather(w_share, ('dp', 'tm'), axis=0, tiled=True)  26.7 us
    all_gather x1, blocking collectives, per_device(): weighted = lax.all_gather(weighted, 'dp', axis=0, tiled=True)  21.6 us
    all_gather x1, blocking collectives, per_device(): d_bc = lax.all_gather(d_bc, 'tm', axis=0, tiled=True)  12.7 us
    unnamed x1, blocking collectives  12.3 us
    reduce_scatter x1, waiting for transfers between devices, per_device(): w_bc_grad = lax.psum_scatter(w_term, 'dp', scatter_dimension=0, tiled=True)  9.18 us
    all_to_all x1, waiting for transfers between devices, reverse_carry(): parts = lax.all_to_all(parts, 'tm', split_axis=0, concat_axis=0)  8.29 us
    all_to_all x1, starting transfers between devices, per_device(): rows_grad = lax.all_to_all(rows_grad, 'dp', split_axis=0, concat_axis=0)  6.32 us
    unnamed x7, other arithmetic  5.58 us
  transfers between devices with their start and end apart: 7, of which 6 were waited for; matrix products, arithmetic and copies ran while one was open for 23% of the time, Pallas kernels for 0%

profile of v1, /device:TPU:0, one launch (start us, length us, event | category | flops | bytes accessed | tf_op | source)
XLA Modules:
  0.0 192.0 jit_solution(16788457336331529961)
XLA Ops:
  10.6 6.3 %all-to-all-start.3 = ((bf16[4,16,640]{2,1,0:T(8,128)(2,1)}), bf16[4,16,640]{2,1,0:T(8,128)(2,1)S(1)}, u32[]{:S(2)}, u32[]{:S(2)}) async-start(bf16[4,16,640]{2,1,0:T(8,128)(2,1)} %bitcast.171), calls=%async_computation.4 | async-start | bytes 163840 | tf_op jit(solution)/shard_map/all_to_all | solution.py:147
  18.4 4.3 %all-to-all-done.3 = bf16[4,16,640]{2,1,0:T(8,128)(2,1)S(1)} async-done(((bf16[4,16,640]{2,1,0:T(8,128)(2,1)}), bf16[4,16,640]{2,1,0:T(8,128)(2,1)S(1)}, u32[]{:S(2)}, u32[]{:S(2)}) %all-to-all-start.3) | async-done | bytes 81952 | tf_op jit(solution)/shard_map/all_to_all | solution.py:147
  27.7 12.3 %all-reduce = f32[320]{0:T(512)S(1)} all-reduce(f32[320]{0:T(512)S(1)} %dynamic-update-slice), channel_id=2, replica_groups=mesh['tm'=8,'dp'=4] {'tm'}, use_global_device_ids=true, to_apply=%add | all-reduce | flops 320 | bytes 2560
  42.9 2.2 %multiply_reduce_fusion = f32[128,128]{1,0:T(8,128)S(1)} fusion(bf16[40,64,128]{2,1,0:T(8,128)(2,1)S(1)} %bitcast.175, bf16[40,64,128]{2,1,0:T(8,128)(2,1)} %bitcast.20, f32[40,128]{1,0:T(8,128)S(1)} %bitcast.199, f32[40,128]{1,0:T(8,128)S(1)} %bitcast.196, pred[128,128]{1,0:T(8,128)(4,1)S(1)} %iota_compare_fusion), kind=kOutput, calls=%fused_computation.12 | convolution fusion | flops 87801856 | bytes 1433600 | tf_op jit(solution)/shard_map/hpa,hpb->hab/dot_general | solution.py:77
  48.7 3.2 %fusion.2 = f32[128,896]{1,0:T(8,128)S(1)} fusion(bf16[128,2560]{1,0:T(8,128)(2,1)S(1)} %bitcast.187, bf16[1,2560,896]{2,1,0:T(8,128)(2,1)} %param.17), kind=kOutput, calls=%fused_computation.2 | convolution fusion | flops 587202560 | bytes 5701632 | tf_op jit(solution)/shard_map/dot_general | solution.py:152
  51.9 3.2 %fusion.42 = bf16[128,896]{1,0:T(8,128)(2,1)S(1)} fusion(bf16[128,2560]{1,0:T(8,128)(2,1)S(1)} %bitcast.188, bf16[1,2560,896]{2,1,0:T(8,128)(2,1)} %param.18, f32[128,896]{1,0:T(8,128)S(1)} %fusion.2), kind=kOutput, calls=%fused_computation.51 | convolution fusion | flops 587890688 | bytes 5931008 | tf_op jit(solution)/shard_map/dot_general | solution.py:153
  55.1 21.6 %all_gather.24 = bf16[512,896]{1,0:T(8,128)(2,1)S(1)} all-gather(bf16[128,896]{1,0:T(8,128)(2,1)S(1)} %fusion.42), channel_id=1, replica_groups=mesh['tm'=8,'dp'=4] {'dp'}, dimensions={0}, use_global_device_ids=true | all-gather | bytes 1146880 | tf_op jit(solution)/shard_map/all_gather | solution.py:155
  76.7 1.9 %fusion.23 = bf16[1,896,640]{2,1,0:T(8,128)(2,1)} fusion(bf16[512,896]{1,0:T(8,128)(2,1)S(1)} %all_gather.24, bf16[512,640]{1,0:T(8,128)(2,1)S(1)} %bitcast.190), kind=kOutput, calls=%fused_computation.31 | convolution fusion | flops 587776000 | bytes 2719744 | tf_op jit(solution)/shard_map/dot_general | solution.py:156
  78.6 26.7 %all-gather.5.cloned.1.call-done = bf16[2560,256]{1,0:T(8,128)(2,1)} async-done(((bf16[80,256]{1,0:T(8,128)(2,1)}), bf16[2560,256]{1,0:T(8,128)(2,1)}) %all-gather.5.cloned.1.call-update) | async-done | bytes 1310736 | tf_op jit(solution)/shard_map/all_gather | solution.py:135
  105.3 1.9 fusion.45
  108.8 3.5 %all-to-all-start = ((bf16[8,320,128]{2,1,0:T(8,128)(2,1)}), bf16[8,320,128]{2,1,0:T(8,128)(2,1)S(1)}, u32[]{:S(2)}, u32[]{:S(2)}) async-start(bf16[8,320,128]{2,1,0:T(8,128)(2,1)} %bitcast.185), calls=%async_computation | async-start | bytes 1310720 | tf_op jit(solution)/shard_map/all_to_all | solution.py:101
  112.8 2.4 %fusion.49 = bf16[128,128]{0,1:T(8,128)(2,1)S(1)} fusion(f32[128,128]{0,1:T(8,128)S(1)} %fusion.73, f32[40,64,128]{2,1,0:T(8,128)} %bitcast.184, bf16[1,1,40,64,128]{4,3,2,1,0:T(8,128)(2,1)} %param.16), kind=kOutput, calls=%fused_computation.60 | convolution fusion | flops 503349248 | bytes 2064384 | tf_op jit(solution)/shard_map/hpt,hpn->tn/dot_general | solution.py:82
  115.2 8.3 %all-to-all-done = bf16[8,320,128]{2,1,0:T(8,128)(2,1)S(1)} async-done(((bf16[8,320,128]{2,1,0:T(8,128)(2,1)}), bf16[8,320,128]{2,1,0:T(8,128)(2,1)S(1)}, u32[]{:S(2)}, u32[]{:S(2)}) %all-to-all-start) | async-done | bytes 655392 | tf_op jit(solution)/shard_map/all_to_all | solution.py:101
  129.7 3.7 %all-to-all-start.1 = ((bf16[8,320,128]{2,1,0:T(8,128)(2,1)}), bf16[8,320,128]{2,1,0:T(8,128)(2,1)S(1)}, u32[]{:S(2)}, u32[]{:S(2)}) async-start(bf16[8,320,128]{2,1,0:T(8,128)(2,1)} %broadcast_dynamic-update-slice_fusion), calls=%async_computation.1 | async-start | bytes 1310720 | tf_op jit(solution)/shard_map/all_to_all | solution.py:110
  133.6 3.0 %fusion.15 = f32[40,64,128]{2,1,0:T(8,128)} fusion(bf16[40,64,128]{2,1,0:T(8,128)(2,1)S(1)} %bitcast.177, f32[128,128]{1,0:T(8,128)S(1)} %fusion.76, f32[40,128]{1,0:T(8,128)S(1)} %bitcast.197, pred[128,128]{1,0:T(8,128)(4,1)S(1)} %iota_compare_fusion), kind=kOutput, calls=%fused_computation.26 | convolution fusion | flops 505937920 | bytes 2068480 | tf_op jit(solution)/shard_map/hrt,hpr->hpt/dot_general | solution.py:73
  136.6 5.3 %fusion.18 = f32[40,64,128]{2,1,0:T(8,128)} fusion(bf16[40,64,128]{2,1,0:T(8,128)(2,1)} %bitcast.20, f32[40,128]{1,0:T(8,128)S(1)} %bitcast.200, f32[128,128]{1,0:T(8,128)S(1)} %fusion.76, f32[40,128]{1,0:T(8,128)S(1)} %bitcast.198, pred[128,128]{1,0:T(8,128)(4,1)S(1)} %iota_compare_fusion), kind=kOutput, calls=%fused_computation.27 | convolution fusion | flops 506593280 | bytes 2088960 | tf_op jit(solution)/shard_map/hts,hps->hpt/dot_general | solution.py:67
  141.9 2.4 %all-to-all-done.1 = bf16[8,320,128]{2,1,0:T(8,128)(2,1)S(1)} async-done(((bf16[8,320,128]{2,1,0:T(8,128)(2,1)}), bf16[8,320,128]{2,1,0:T(8,128)(2,1)S(1)}, u32[]{:S(2)}, u32[]{:S(2)}) %all-to-all-start.1) | async-done | bytes 655392 | tf_op jit(solution)/shard_map/all_to_all | solution.py:110
  144.3 4.2 %all-to-all-start.2 = ((bf16[8,128,320]{1,2,0:T(8,128)(2,1)}), bf16[8,128,320]{1,2,0:T(8,128)(2,1)}, u32[]{:S(2)}, u32[]{:S(2)}) async-start(bf16[8,128,320]{1,2,0:T(8,128)(2,1)} %bitcast.41), calls=%async_computation.2 | async-start | bytes 1310720 | tf_op jit(solution)/shard_map/all_to_all | solution.py:161
  148.6 1.9 %fusion.37 = f32[40,128]{1,0:T(8,128)S(1)} fusion(f32[40,64,128]{2,1,0:T(8,128)} %fusion.18, bf16[40,64,128]{2,1,0:T(8,128)(2,1)S(1)} %bitcast.178, bf16[1,1,40,64,128]{4,3,2,1,0:T(8,128)(2,1)} %param.16, f32[40,128]{1,0:T(8,128)S(1)} %get-tuple-element.23, bf16[128,256]{0,1:T(8,128)(2,1)S(1)} %fusion.45), kind=kOutput, calls=%fused_computation.48 | convolution fusion | flops 85519360 | bytes 2695168 | tf_op jit(solution)/shard_map/hpn,tn->hpt/dot_general | solution.py:70
  151.4 12.7 %all_gather.21 = bf16[1024,256]{0,1:T(8,128)(2,1)S(1)} all-gather(bf16[128,256]{0,1:T(8,128)(2,1)S(1)} %pad_maximum_fusion.1), channel_id=1, replica_groups=mesh['tm'=8,'dp'=4] {'tm'}, dimensions={0}, use_global_device_ids=true | all-gather | bytes 589824 | tf_op jit(solution)/shard_map/all_gather | solution.py:170
  164.1 2.2 %convolution_bitcast_fusion.1 = f32[320,256]{1,0:T(8,128)} fusion(bf16[1024,256]{0,1:T(8,128)(2,1)S(1)} %all_gather.21, bf16[8,128,320]{1,2,0:T(8,128)(2,1)} %all-to-all-done.2), kind=kOutput, calls=%fused_computation.52 | convolution fusion | flops 167772160 | bytes 1507328 | tf_op jit(solution)/shard_map/dot_general | solution.py:171
  166.4 3.3 %fusion.25 = (f32[40,128]{1,0:T(8,128)}, f32[40,128]{1,0:T(8,128)S(1)}, f32[40,64,128]{2,1,0:T(8,128)}) fusion(bf16[40,64,128]{2,1,0:T(8,128)(2,1)} %bitcast.20, f32[40,128]{1,0:T(8,128)S(1)} %bitcast.201, f32[40,64,128]{2,1,0:T(8,128)S(1)} %copy-done.5, bf16[40,64,128]{2,1,0:T(8,128)(2,1)S(1)} %bitcast.180, bf16[128,256]{0,1:T(8,128)(2,1)S(1)} %fusion.45, ...), kind=kOutput, calls=%fused_computation.34 | convolution fusion | flops 86497280 | bytes 4046848 | tf_op jit(solution)/shard_map/hpn,tn->hpt/dot_general | solution.py:74
  172.0 2.2 %fusion.38 = f32[40]{0:T(128)S(1)} fusion(bf16[40,64,128]{2,1,0:T(8,128)(2,1)} %bitcast.20, bf16[40,64,128]{2,1,0:T(8,128)(2,1)S(1)} %bitcast.181, bf16[1,1,40,64,128]{4,3,2,1,0:T(8,128)(2,1)S(1)} %copy-done.4, f32[40]{0:T(128)S(1)} %exp.40, f32[40,128]{1,0:T(8,128)S(1)} %get-tuple-element.17, bf16[128,256]{0,1:T(8,128)(2,1)S(1)} %fusion.45), kind=kOutput, calls=%fused_computation.49 | convolution fusion | flops 505937888 | bytes 2020000 | tf_op jit(solution)/shard_map/hpt,tn->hpn/dot_general | solution.py:25
  176.3 9.2 %reduce-scatter.2.cloned.1.call-done = f32[80,256]{1,0:T(8,128)} async-done(((f32[320,256]{1,0:T(8,128)}), f32[80,256]{1,0:T(8,128)}) %reduce-scatter.2.cloned.1.call-update) | async-done | bytes 81936 | tf_op jit(solution)/shard_map/reduce_scatter | solution.py:174
  (76 shorter events, 28.6 us)
Async XLA Ops:
  7.2 16.3 %copy-start = (bf16[640,256]{1,0:T(8,128)(2,1)S(1)}, bf16[640,256]{1,0:T(8,128)(2,1)}, u32[]{:S(2)}) copy-start(bf16[640,256]{1,0:T(8,128)(2,1)} %param.13) | copy-start | bytes 983044
  8.5 15.6 %copy-start.3 = (bf16[1,128,2560]{2,1,0:T(8,128)(2,1)S(1)}, bf16[1,128,2560]{2,1,0:T(8,128)(2,1)}, u32[]{:S(2)}) copy-start(bf16[1,128,2560]{2,1,0:T(8,128)(2,1)} %param.12) | copy-start | bytes 1966084
  10.6 12.1 %all-to-all-start.3 = ((bf16[4,16,640]{2,1,0:T(8,128)(2,1)}), bf16[4,16,640]{2,1,0:T(8,128)(2,1)S(1)}, u32[]{:S(2)}, u32[]{:S(2)}) async-start(bf16[4,16,640]{2,1,0:T(8,128)(2,1)} %bitcast.171), calls=%async_computation.4 | async-start | bytes 163840 | tf_op jit(solution)/shard_map/all_to_all | solution.py:147
  16.9 7.6 %copy-start.1 = (bf16[1,128,2560]{2,1,0:T(8,128)(2,1)S(1)}, bf16[1,128,2560]{2,1,0:T(8,128)(2,1)}, u32[]{:S(2)}) copy-start(bf16[1,128,2560]{2,1,0:T(8,128)(2,1)} %param.11) | copy-start | bytes 1966084
  16.9 30.0 %all-gather.7.cloned.1.call-start = ((), (), s32[]{:S(2)}) async-start(), calls=%async_computation.7 | async-start | bytes 1474560 | tf_op jit(solution)/shard_map/all_gather | solution.py:149
  23.4 81.9 %all-gather.5.cloned.1.call-start = ((), (), s32[]{:S(2)}) async-start(), calls=%async_computation.5 | async-start | bytes 1351680 | tf_op jit(solution)/shard_map/all_gather | solution.py:135
  24.2 1.5 copy-start.7
  24.2 1.8 copy-start.8
  24.5 15.8 %copy-start.6 = (f32[1,128,40]{1,2,0:T(8,128)S(1)}, f32[1,128,40]{1,2,0:T(8,128)}, u32[]{:S(2)}) copy-start(f32[1,128,40]{1,2,0:T(8,128)} %param.15) | copy-start | bytes 61444
  108.8 14.6 %all-to-all-start = ((bf16[8,320,128]{2,1,0:T(8,128)(2,1)}), bf16[8,320,128]{2,1,0:T(8,128)(2,1)S(1)}, u32[]{:S(2)}, u32[]{:S(2)}) async-start(bf16[8,320,128]{2,1,0:T(8,128)(2,1)} %bitcast.185), calls=%async_computation | async-start | bytes 1310720 | tf_op jit(solution)/shard_map/all_to_all | solution.py:101
  129.7 14.6 %all-to-all-start.1 = ((bf16[8,320,128]{2,1,0:T(8,128)(2,1)}), bf16[8,320,128]{2,1,0:T(8,128)(2,1)S(1)}, u32[]{:S(2)}, u32[]{:S(2)}) async-start(bf16[8,320,128]{2,1,0:T(8,128)(2,1)} %broadcast_dynamic-update-slice_fusion), calls=%async_computation.1 | async-start | bytes 1310720 | tf_op jit(solution)/shard_map/all_to_all | solution.py:110
  144.3 19.8 %all-to-all-start.2 = ((bf16[8,128,320]{1,2,0:T(8,128)(2,1)}), bf16[8,128,320]{1,2,0:T(8,128)(2,1)}, u32[]{:S(2)}, u32[]{:S(2)}) async-start(bf16[8,128,320]{1,2,0:T(8,128)(2,1)} %bitcast.41), calls=%async_computation.2 | async-start | bytes 1310720 | tf_op jit(solution)/shard_map/all_to_all | solution.py:161
  148.5 37.0 %reduce-scatter.2.cloned.1.call-start = ((), (), s32[]{:S(2)}) async-start(), calls=%async_computation.6 | async-start | bytes 409600 | tf_op jit(solution)/shard_map/reduce_scatter | solution.py:174
  151.4 14.9 %copy-start.5 = (f32[40,64,128]{2,1,0:T(8,128)S(1)}, f32[40,64,128]{2,1,0:T(8,128)}, u32[]{:S(2)}) copy-start(f32[40,64,128]{2,1,0:T(8,128)} %fusion.15) | copy-start | bytes 3932164
  170.1 1.8 copy-start.4
  172.0 2.9 %copy-start.2 = (bf16[2560,256]{1,0:T(8,128)(2,1)S(1)}, bf16[2560,256]{1,0:T(8,128)(2,1)}, u32[]{:S(2)}) copy-start(bf16[2560,256]{1,0:T(8,128)(2,1)} %all-gather.5.cloned.1.call-done) | copy-start | bytes 3932164
Sparse Core Ops, SparseCore 0:
  23.5 23.3 all-gather.6
  50.3 54.9 all-gather.4
  166.5 18.9 reduce-scatter.1

commit v2 on v1

v2 whole, which is shorter than its diff:
```python
import jax
import jax.numpy as jnp
from jax import lax
from jax.experimental import pallas as pl
from jax.experimental.pallas import tpu as pltpu
from jax.sharding import PartitionSpec as P

HI = lax.Precision.HIGHEST
F32 = jnp.float32
BF16 = jnp.bfloat16
LANES = 128
EXTRA = 16


def dot(a, b, ca, cb, precision=None):
    return lax.dot_general(
        a, b, (((ca,), (cb,)), ((), ())), precision=precision, preferred_element_type=F32
    )


def iota(shape, axis):
    return lax.broadcasted_iota(jnp.int32, shape, axis)


def triangle(n, keep):
    return jnp.where(keep(iota((n, n), 0), iota((n, n), 1)), 1.0, 0.0).astype(F32)


def spread(table, j, size):
    per = LANES // size
    out = table[:, j * per : j * per + 1]
    lane = iota((1, LANES), 1)
    for i in range(1, per):
        out = jnp.where(lane < i * size, out, table[:, j * per + i : j * per + i + 1])
    return out


def by_head(j, size, copies):
    shape = (LANES, LANES)
    one = jnp.where(iota(shape, 0) // size + j * (LANES // size) == iota(shape, 1), 1.0, 0.0)
    return jnp.concatenate([one.astype(BF16)] * copies, axis=0)


def halves(values):
    high = values.astype(BF16)
    low = (values - high.astype(F32)).astype(BF16)
    return jnp.concatenate([high, low], axis=1)


def call(kernel, outs, flops, scratch=(), limit=40):
    size = sum(o.size * o.dtype.itemsize for o in outs)
    return pl.pallas_call(
        kernel,
        out_shape=outs,
        scratch_shapes=list(scratch),
        cost_estimate=pl.CostEstimate(
            flops=int(flops), bytes_accessed=int(2 * size), transcendentals=0
        ),
        compiler_params=pltpu.CompilerParams(vmem_limit_bytes=limit * 1024 * 1024),
    )


def shape(dims, kind):
    return jax.ShapeDtypeStruct(dims, kind)


def pick_kernel(x_ref, dy_ref, rows_ref, count_ref, gate_ref, in_ref, grad_ref, xt_ref):
    length, width = x_ref.shape
    slots = rows_ref.shape[1]
    hit = iota((length, slots), 0) == rows_ref[...]
    live = iota((1, slots), 1) < count_ref[...]
    weight = jnp.where(live, gate_ref[...].astype(F32), 0.0)
    pick = jnp.where(hit, 1.0, 0.0).astype(BF16)
    scaled = jnp.where(hit, weight, 0.0).astype(BF16)
    in_ref[...] = dot(pick, x_ref[...], 0, 0).astype(BF16)
    grads = dot(scaled, dy_ref[...], 0, 0).astype(BF16)
    piece = grad_ref.shape[2]
    for i in range(grad_ref.shape[0]):
        grad_ref[i] = grads[:, i * piece : (i + 1) * piece]
    for j in range(width // LANES):
        tile = x_ref[:, j * LANES : (j + 1) * LANES].astype(F32)
        xt_ref[j * LANES : (j + 1) * LANES, :] = tile.T.astype(BF16)


def project_kernel(n_dp, unit, *refs):
    x_ref, dy_ref, ld_ref, ldt_ref, own_ref = refs[:5]
    mine = refs[5 : 4 + n_dp]
    other = refs[4 + n_dp : 3 + 2 * n_dp]
    w_ref, bc_ref, g_ref = refs[3 + 2 * n_dp :]
    share = own_ref.shape[0]
    half = own_ref.shape[1] // 2
    place = lax.axis_index("dp")
    core = lax.rem(lax.axis_index("tm"), 2)

    def rows(shift):
        source = lax.rem(place + n_dp - shift, n_dp)
        return pl.ds(pl.multiple_of(source * share, 16), share)

    w_ref[rows(0), :] = own_ref[...]
    for i in range(n_dp - 1):
        w_ref[rows(i + 1), pl.ds(pl.multiple_of(core * half, LANES), half)] = mine[i][...]
        w_ref[rows(i + 1), pl.ds(pl.multiple_of((1 - core) * half, LANES), half)] = other[i][...]
    bc = dot(x_ref[...], w_ref[...], 1, 0).astype(BF16)
    bc_ref[...] = bc
    c_rows = bc[:, half:]
    length, width = x_ref.shape
    heads = ld_ref.shape[1]
    size = width // heads
    cum = dot(triangle(length, lambda a, b: a >= b), ld_ref[...], 1, 0, HI)
    cumt = dot(ldt_ref[...], triangle(length, lambda a, b: a <= b), 1, 0, HI)
    start = jnp.exp(cum)
    n_tm = g_ref.shape[0]
    block = g_ref.shape[1] - EXTRA
    for j in range(width // LANES):
        span = slice(j * LANES, (j + 1) * LANES)
        scaled = (dy_ref[:, span].astype(F32) * spread(start, j, size)).astype(BF16)
        tile = dot(scaled, c_rows, 0, 0).astype(BF16)
        for i in range(LANES // unit):
            row = j * LANES + i * unit
            g_ref[row // block, row % block : row % block + unit, :] = tile[
                i * unit : (i + 1) * unit
            ]
    decay = jnp.broadcast_to(jnp.exp(cumt[:, length - 1 : length]), (heads, LANES))
    high = decay.astype(BF16).astype(F32)
    low = decay - high
    for b in range(n_tm):
        owners = [(b * block + u * unit) // size for u in range(block // unit)]
        parts = [high[h : h + 1] for h in owners] + [low[h : h + 1] for h in owners]
        parts.append(jnp.zeros((EXTRA - len(parts), LANES), F32))
        g_ref[b, block : block + EXTRA, :] = jnp.concatenate(parts, axis=0).astype(BF16)


def scan_kernel(unit, parts_ref, out_ref):
    n_tm, block, states = out_ref.shape
    units = block // unit
    carry = [jnp.zeros((unit, states), F32)] * units
    for k in reversed(range(n_tm)):
        for u in range(units):
            span = slice(u * unit, (u + 1) * unit)
            out_ref[k, span, :] = carry[u].astype(BF16)
            if k:
                decay = parts_ref[k, block : block + EXTRA, :].astype(F32)
                decay = decay[u : u + 1] + decay[units + u : units + u + 1]
                carry[u] = parts_ref[k, span, :].astype(F32) + decay * carry[u]


def intra_kernel(
    x_ref, dy_ref, bc_ref, ld_ref, ldt_ref, step_ref, h_ref,
    dx_ref, xs_ref, db_ref, dc_ref, dec_ref, dst_ref, rowm_ref,
):
    length, width = x_ref.shape
    heads = ld_ref.shape[1]
    size = width // heads
    half = bc_ref.shape[1] // 2
    per = LANES // size
    b_rows = bc_ref[:, :half]
    c_rows = bc_ref[:, half:]
    cum = dot(triangle(length, lambda a, b: a >= b), ld_ref[...], 1, 0, HI)
    cumt = dot(ldt_ref[...], triangle(length, lambda a, b: a <= b), 1, 0, HI)
    step = step_ref[...]
    start = jnp.exp(cum)
    into_end = jnp.exp(cum[length - 1 : length] - cum) * step
    upper = iota((length, length), 0) <= iota((length, length), 1)
    scores = dot(b_rows, c_rows, 1, 1)
    lane = iota((1, LANES), 1)
    lane_bf = [jnp.where(lane // size == i, 1.0, 0.0).astype(BF16) for i in range(per)]
    mixed = jnp.zeros((length, length), F32)
    own = jnp.zeros((length, LANES), F32)
    carried = jnp.zeros((length, half), F32)
    reach = jnp.zeros((length, LANES), F32)
    for j in range(width // LANES):
        span = slice(j * LANES, (j + 1) * LANES)
        x_p = x_ref[:, span]
        dy_p = dy_ref[:, span]
        dy_f = dy_p.astype(F32)
        dy_h = jnp.concatenate([dy_p * m for m in lane_bf], axis=0)
        cross = dot(x_p, dy_h, 1, 1)
        kern = []
        for i in range(per):
            h = j * per + i
            diff = cumt[h : h + 1, :] - cum[:, h : h + 1]
            seg = jnp.exp(jnp.where(upper, diff, -1e30))
            kern.append((seg * scores).astype(BF16))
            scaled = seg * cross[:, i * length : (i + 1) * length] * step[:, h : h + 1]
            mixed = mixed + scaled
            full = scaled * scores
            rowm_ref[h : h + 1, :] = jnp.sum(full, axis=0, keepdims=True)
            own = jnp.where(lane == h, jnp.sum(full, axis=1, keepdims=True), own)
        back = dot(jnp.concatenate(kern, axis=1), dy_h, 1, 0)
        dx_ref[:, span] = back * spread(step, j, size)
        xs_ref[:, span] = (x_p.astype(F32) * spread(into_end, j, size)).astype(BF16)
        h_tile = h_ref[span, :]
        scaled = (dy_f * spread(start, j, size)).astype(BF16)
        carried = carried + dot(scaled, h_tile, 1, 0)
        seen = dy_f * dot(c_rows, h_tile, 1, 1)
        reach = reach + dot(halves(seen), by_head(j, size, 2), 1, 0)
    mixed = mixed.astype(BF16)
    db_ref[...] = dot(mixed, c_rows, 1, 0)
    dc_ref[...] = (dot(mixed, b_rows, 0, 0) + carried).astype(BF16)
    later = triangle(length, lambda a, b: a <= b)
    own = own[:, :heads]
    dec_ref[...] = dot(later, rowm_ref[...], 1, 1, HI) + dot(
        later, start * reach[:, :heads] - own, 1, 0, HI
    )
    dst_ref[...] = own / step


def db_kernel(xs_ref, r_ref, db_ref, dc_ref, out_ref):
    half = db_ref.shape[1]
    out_ref[:, :half] = (db_ref[...] + dot(xs_ref[...], r_ref[...], 1, 0)).astype(BF16)
    out_ref[:, half:] = dc_ref[...]


def finish_kernel(
    x_ref, bc_ref, ld_ref, step_ref, h_ref, r_ref, w_ref, dx_ref, dbc_ref, dec_ref, dst_ref,
    in_ref, decay_ref, grad_ref, edge_ref,
):
    length, width = x_ref.shape
    heads = ld_ref.shape[1]
    size = width // heads
    half = bc_ref.shape[1] // 2
    b_rows = bc_ref[:, :half]
    cum = dot(triangle(length, lambda a, b: a >= b), ld_ref[...], 1, 0, HI)
    total = cum[length - 1 : length]
    to_end = jnp.exp(total - cum)
    into_end = to_end * step_ref[...]
    seen = jnp.zeros((length, LANES), F32)
    for j in range(width // LANES):
        span = slice(j * LANES, (j + 1) * LANES)
        r_tile = r_ref[span, :]
        reach = dot(b_rows, r_tile, 1, 1)
        d_in = dx_ref[:, span] + spread(into_end, j, size) * reach
        d_in = d_in + dot(dbc_ref[...], w_ref[span, :], 1, 1)
        in_ref[:, span] = d_in.astype(BF16)
        product = x_ref[:, span].astype(F32) * reach
        seen = seen + dot(halves(product), by_head(j, size, 2), 1, 0)
        edge = r_tile.astype(F32) * h_ref[span, :].astype(F32)
        for i in range(LANES // size):
            h = j * (LANES // size) + i
            edge_ref[h : h + 1, :] = jnp.sum(
                edge[i * size : (i + 1) * size], axis=0, keepdims=True
            )
    seen = seen[:, :heads]
    grad_ref[...] = dst_ref[...] + to_end * seen
    edge = dot(jnp.ones((8, half), F32), edge_ref[...], 1, 1, HI)[:1]
    earlier = triangle(length, lambda a, b: a > b)
    decay_ref[...] = (
        dec_ref[...] + dot(earlier, into_end * seen, 1, 0, HI) + jnp.exp(total) * edge
    )


def term_kernel(n_tm, *refs):
    xt_ref, pieces, out_ref = refs[0], refs[1 : 1 + n_tm], refs[1 + n_tm]
    place = lax.axis_index("tm")
    total = None
    for i in range(n_tm):
        source = lax.rem(place + n_tm - i, n_tm)
        part = dot(xt_ref[source], pieces[i][...], 1, 0)
        total = part if total is None else total + part
    n_dp, share, _ = out_ref.shape
    for i in range(n_dp):
        out_ref[i] = total[i * share : (i + 1) * share].astype(BF16)


def shifted(array, axis, shift):
    count = lax.axis_size(axis)
    return lax.ppermute(array, axis, [(i, (i + shift) % count) for i in range(count)])


def from_all(array, axis):
    return [array] + [shifted(array, axis, s) for s in range(1, lax.axis_size(axis))]


def dealt(array, axis):
    count = lax.axis_size(axis)
    place = lax.axis_index(axis)
    own = lax.dynamic_index_in_dim(array, place, 0, False)
    pieces = [own]
    for s in range(1, count):
        block = lax.dynamic_index_in_dim(array, lax.rem(place + s, count), 0, False)
        pieces.append(shifted(block, axis, s))
    return pieces


def per_device(
    layer_in,
    out_grad,
    w_bc,
    log_decay,
    step,
    saved_states,
    w_gate,
    w_up,
    slot_rows,
    slot_counts,
    slot_gates,
):
    n_tm = lax.axis_size("tm")
    n_dp = lax.axis_size("dp")
    core = lax.rem(lax.axis_index("tm"), 2)
    x = layer_in[0]
    dy = out_grad[0]
    length, width = x.shape
    heads = log_decay.shape[2]
    size = width // heads
    columns = w_bc.shape[1]
    half = columns // 2
    ld = log_decay[0]
    ldt = ld.T
    steps = step[0]
    h_in = saved_states[0, 0].reshape(width, half)
    capacity = slot_rows.shape[2]
    piece = width // n_dp
    block = width // n_tm
    unit = min(size, block & -block)

    w_half = lax.dynamic_slice_in_dim(w_bc, core * half, half, 1)
    mine = from_all(w_half, "dp")[1:]
    swap = [(i, i ^ 1) for i in range(n_tm)]
    other = [lax.ppermute(m, "tm", swap) for m in mine]

    rows_in, rows_grad, x_cols = call(
        pick_kernel,
        [
            shape((capacity, width), BF16),
            shape((n_dp, capacity, piece), BF16),
            shape((width, length), BF16),
        ],
        4e8,
    )(x, dy, slot_rows[0], slot_counts, slot_gates[0])
    x_cols = lax.all_to_all(
        x_cols.reshape(n_tm, block, length), "tm", split_axis=0, concat_axis=0
    )
    rows_grad = jnp.concatenate(dealt(rows_grad, "dp"), axis=1)
    rows = from_all(jnp.concatenate([rows_in, rows_grad], axis=0), "tm")
    rows = jnp.stack(rows)
    rows_in = rows[:, :capacity].reshape(n_tm * capacity, width)
    rows_grad = rows[:, capacity:].reshape(n_tm * capacity, width)
    gate_h = jnp.dot(rows_in, w_gate[0], preferred_element_type=F32)
    up_h = jnp.dot(rows_in, w_up[0], preferred_element_type=F32)
    weighted = (jax.nn.silu(gate_h) * up_h).astype(BF16)
    weighted = jnp.concatenate(from_all(weighted, "dp"), axis=0)
    rows_grad = jnp.concatenate(
        [rows_grad[:, i * piece : (i + 1) * piece] for i in range(n_dp)], axis=0
    )
    w_down_grad = dot(weighted, rows_grad, 0, 0).astype(BF16)

    w_whole, bc, g_local = call(
        lambda *refs: project_kernel(n_dp, unit, *refs),
        [
            shape((width, columns), BF16),
            shape((length, columns), BF16),
            shape((n_tm, block + EXTRA, half), BF16),
        ],
        1e9,
    )(x, dy, ld, ldt, w_bc, *mine, *other)
    parts = lax.all_to_all(g_local, "tm", split_axis=0, concat_axis=0)
    dx, xs, db, dc, dec, dst = call(
        intra_kernel,
        [
            shape((length, width), F32),
            shape((length, width), BF16),
            shape((length, half), F32),
            shape((length, half), BF16),
            shape((length, heads), F32),
            shape((length, heads), F32),
        ],
        4e9,
        [pltpu.VMEM((heads, length), F32)],
    )(x, dy, bc, ld, ldt, steps, h_in)
    carried = call(
        lambda *refs: scan_kernel(unit, *refs), [shape((n_tm, block, half), BF16)], 1e8
    )(parts)[0]
    r_grad = lax.all_to_all(carried, "tm", split_axis=0, concat_axis=0).reshape(width, half)
    d_bc = call(db_kernel, [shape((length, columns), BF16)], 1e8)(xs, r_grad, db, dc)[0]
    d_bcs = from_all(d_bc, "tm")
    d_in, d_decay, d_step = call(
        finish_kernel,
        [
            shape((length, width), BF16),
            shape((length, heads), F32),
            shape((length, heads), F32),
        ],
        2e9,
        [pltpu.VMEM((heads, half), F32)],
    )(x, bc, ld, steps, h_in, r_grad, w_whole, dx, d_bc, dec, dst)
    term = call(
        lambda *refs: term_kernel(n_tm, *refs),
        [shape((n_dp, block // n_dp, columns), BF16)],
        2e8,
    )(x_cols, *d_bcs)[0]
    w_bc_grad = sum(p.astype(F32) for p in dealt(term, "dp"))
    return (d_in[None], d_decay[None], d_step[None], w_bc_grad, w_down_grad[None])


def solution(mesh):
    in_specs = (
        P("dp", "tm", None),
        P("dp", "tm", None),
        P("dp", None),
        P("dp", "tm", None),
        P("dp", "tm", None),
        P("dp", "tm", None, None, None),
        P(None, None, "tm"),
        P(None, None, "tm"),
        P("dp", None, "tm"),
        P("dp", "tm"),
        P("dp", None, "tm"),
    )
    out_specs = (
        P("dp", "tm", None),
        P("dp", "tm", None),
        P("dp", "tm", None),
        P(("tm", "dp"), None),
        P(None, "tm", "dp"),
    )
    return jax.shard_map(
        per_device, mesh=mesh, in_specs=in_specs, out_specs=out_specs, check_vma=False
    )
```

time: 193 us -> 116 us (0.60)
  blocking collectives: 46.6 us -> 0 us
  matrix products: 40.2 us -> 7.27 us
  starting transfers between devices: 17.9 us -> 42 us
  waiting for transfers between devices: 52.7 us -> 33.3 us
  Pallas kernels: 0 us -> 16.7 us
  between operations: 15.4 us -> 1.72 us
  other arithmetic: 10.6 us -> 0.69 us
  local copies, waits for them, and re-layouts: 8.63 us -> 13.9 us
    all_gather x2 -> x0, blocking collectives: 34.3 us -> none  [the longest x1 21.6 us: per_device(): weighted = lax.all_gather(weighted, 'dp', axis=0, tiled=True)]
    dot_general x20 -> x3, matrix products: 40.2 us -> 7.27 us  [the longest x1 3.32 us: per_device(): gate_h = jnp.dot(rows_in, w_gate[0], preferred_element_type=F32)]
    ppermute x0 -> x29, starting transfers between devices: none -> 30.6 us  [the longest x26 30.1 us: shifted(): lax.ppermute(array, axis, [(i, (i + shift) % count) for i in range(count)])]
    all_gather x2 -> x0, waiting for transfers between devices: 28.4 us -> none  [the longest x1 26.7 us: per_device(): w_whole = lax.all_gather(w_share, ('dp', 'tm'), axis=0, tiled=True)]
    ppermute x0 -> x29, waiting for transfers between devices: none -> 19.8 us  [the longest x26 19.8 us: shifted(): lax.ppermute(array, axis, [(i, (i + shift) % count) for i in range(count)])]
    pallas_call x0 -> x7, Pallas kernels: none -> 16.7 us  [the longest x1 7.8 us: per_device(): call(intra_kernel, [shape((length, width), F32), shape((length, width), B...]
    unnamed x1 -> x0, blocking collectives: 12.3 us -> none
    reduce_scatter x1 -> x0, waiting for transfers between devices: 9.18 us -> none  [per_device(): w_bc_grad = lax.psum_scatter(w_term, 'dp', scatter_dimension=0, tiled=True)]
  transfers between devices with their start and end apart: 7 -> 32, of which waited for: 6 -> 9; matrix products, arithmetic and copies ran while one was open for 23% -> 10% of each run, Pallas kernels for 0% -> 10%
where the time goes in v2:
time: 116 us
  starting transfers between devices  42 us (36%)
  waiting for transfers between devices  33.3 us (29%)
  Pallas kernels  16.7 us (14%)
  local copies, waits for them, and re-layouts  13.9 us (12%)
  matrix products  7.27 us (6%)
  between operations  1.72 us (1%)
    ppermute x26, starting transfers between devices, shifted(): lax.ppermute(array, axis, [(i, (i + shift) % count) for i in range(count)])  30.1 us
    ppermute x26, waiting for transfers between devices, shifted(): lax.ppermute(array, axis, [(i, (i + shift) % count) for i in range(count)])  19.8 us
    unnamed x48, local copies, waits for them, and re-layouts  11.3 us
    all_to_all x1, waiting for transfers between devices, per_device(): parts = lax.all_to_all(g_local, 'tm', split_axis=0, concat_axis=0)  9.07 us
    pallas_call x1, Pallas kernels, per_device(): call(intra_kernel, [shape((length, width), F32), shape((length, width), B...  7.8 us
    all_to_all x1, waiting for transfers between devices, per_device(): lax.all_to_all(carried, 'tm', split_axis=0, concat_axis=0)  4.42 us
    all_to_all x1, starting transfers between devices, per_device(): parts = lax.all_to_all(g_local, 'tm', split_axis=0, concat_axis=0)  4.03 us
    all_to_all x1, starting transfers between devices, per_device(): lax.all_to_all(x_cols.reshape(n_tm, block, length), 'tm', split_axis=0, c...  3.72 us
  transfers between devices with their start and end apart: 32, of which 9 were waited for; matrix products, arithmetic and copies ran while one was open for 10% of the time, Pallas kernels for 10%

profile of v2, /device:TPU:0, one launch (start us, length us, event | category | flops | bytes accessed | tf_op | source)
XLA Modules:
  0.0 115.6 jit_solution(44722299543987528)
XLA Ops:
  6.0 5.1 %collective-permute-start.18 = (bf16[16,640]{1,0:T(8,128)(2,1)S(1)}, bf16[16,640]{1,0:T(8,128)(2,1)S(1)}, u32[]{:S(2)}, u32[]{:S(2)}) collective-permute-start(bf16[16,640]{1,0:T(8,128)(2,1)S(1)} %get-tuple-element.50), channel_id=1, source_target_pairs={{0,3},{1,0},{2,1},{3,2},{4,7},{5,4},{6,5},{7,6},{8,11},{9,8},{10,9... | collective-permute-start | bytes 61448 | tf_op jit(solution)/shard_map/ppermute | solution.py:267
  12.2 2.5 %collective-permute-start = (bf16[640,128]{1,0:T(8,128)(2,1)S(1)}, bf16[640,128]{1,0:T(8,128)(2,1)S(1)}, u32[]{:S(2)}, u32[]{:S(2)}) collective-permute-start(bf16[640,128]{1,0:T(8,128)(2,1)S(1)} %constant_dynamic-slice_fusion), channel_id=1, source_target_pairs={{0,1},{1,2},{2,3},{3,0},{4,5},{5,6},{6,7},{7,4},{8,9},{9,10},{10,1... | collective-permute-start | bytes 491528 | tf_op jit(solution)/shard_map/ppermute | solution.py:267
  15.8 1.6 %collective-permute-start.2 = (bf16[640,128]{1,0:T(8,128)(2,1)S(1)}, bf16[640,128]{1,0:T(8,128)(2,1)S(1)}, u32[]{:S(2)}, u32[]{:S(2)}) collective-permute-start(bf16[640,128]{1,0:T(8,128)(2,1)S(1)} %constant_dynamic-slice_fusion), channel_id=1, source_target_pairs={{0,3},{1,0},{2,1},{3,2},{4,7},{5,4},{6,5},{7,6},{8,11},{9,8},{10,9... | collective-permute-start | bytes 491528 | tf_op jit(solution)/shard_map/ppermute | solution.py:267
  17.4 4.3 %collective-permute-done.17 = bf16[16,640]{1,0:T(8,128)(2,1)S(1)} collective-permute-done((bf16[16,640]{1,0:T(8,128)(2,1)S(1)}, bf16[16,640]{1,0:T(8,128)(2,1)S(1)}, u32[]{:S(2)}, u32[]{:S(2)}) %collective-permute-start.17) | collective-permute-done | bytes 20512 | tf_op jit(solution)/shard_map/ppermute | solution.py:267
  23.4 5.2 %collective-permute-done.19 = bf16[32,2560]{1,0:T(8,128)(2,1)S(1)} collective-permute-done((bf16[32,2560]{1,0:T(8,128)(2,1)S(1)}, bf16[32,2560]{1,0:T(8,128)(2,1)S(1)}, u32[]{:S(2)}, u32[]{:S(2)}) %collective-permute-start.19) | collective-permute-done | bytes 163872 | tf_op jit(solution)/shard_map/ppermute | solution.py:267
  31.3 5.3 %collective-permute-done.21 = bf16[32,2560]{1,0:T(8,128)(2,1)S(1)} collective-permute-done((bf16[32,2560]{1,0:T(8,128)(2,1)S(1)}, bf16[32,2560]{1,0:T(8,128)(2,1)S(1)}, u32[]{:S(2)}, u32[]{:S(2)}) %collective-permute-start.21) | collective-permute-done | bytes 163872 | tf_op jit(solution)/shard_map/ppermute | solution.py:267
  38.4 1.8 %collective-permute-start.25 = (bf16[32,2560]{1,0:T(8,128)(2,1)S(1)}, bf16[32,2560]{1,0:T(8,128)(2,1)S(1)}, u32[]{:S(2)}, u32[]{:S(2)}) collective-permute-start(bf16[32,2560]{1,0:T(8,128)(2,1)S(1)} %maximum_maximum_fusion), channel_id=1, source_target_pairs={{0,28},{4,0},{8,4},{12,8},{16,12},{20,16},{24,20},{28,24},{1,29},{... | collective-permute-start | bytes 491528 | tf_op jit(solution)/shard_map/ppermute | solution.py:267
  42.2 1.9 %collective-permute-done.24 = bf16[32,2560]{1,0:T(8,128)(2,1)S(1)} collective-permute-done((bf16[32,2560]{1,0:T(8,128)(2,1)S(1)}, bf16[32,2560]{1,0:T(8,128)(2,1)S(1)}, u32[]{:S(2)}, u32[]{:S(2)}) %collective-permute-start.24) | collective-permute-done | bytes 163872 | tf_op jit(solution)/shard_map/ppermute | solution.py:267
  45.2 2.8 %shard_map.146 = (bf16[2560,256]{1,0:T(8,128)(2,1)S(1)}, bf16[128,256]{1,0:T(8,128)(2,1)S(1)}, bf16[8,336,128]{2,1,0:T(8,128)(2,1)}) custom-call(bf16[128,2560]{1,0:T(8,128)(2,1)S(1)} %bitcast.80, bf16[128,2560]{1,0:T(8,128)(2,1)S(1)} %bitcast.77, f32[128,40]{1,0:T(8,128)S(1)} %bitcast.67, f32[40,128]{1,0:T(8,128)S(1)} %bitcast.74, ...), custom_call_target="tpu_custom_call" | custom-call | flops 1000000000 | bytes 4128768 | tf_op jit(solution)/shard_map/pallas_call | solution.py:348
  49.1 4.0 %all-to-all-start = ((bf16[8,336,128]{2,1,0:T(8,128)(2,1)}), bf16[8,336,128]{2,1,0:T(8,128)(2,1)S(1)}, u32[]{:S(2)}, u32[]{:S(2)}) async-start(bf16[8,336,128]{2,1,0:T(8,128)(2,1)} %get-tuple-element.21), calls=%async_computation | async-start | bytes 1376256 | tf_op jit(solution)/shard_map/all_to_all | solution.py:357
  53.2 2.4 %fusion.28 = (bf16[8,16,2560]{2,1,0:T(8,128)(2,1)}, bf16[8,16,2560]{2,1,0:T(8,128)(2,1)}) fusion(bf16[8,32,2560]{2,1,0:T(8,128)(2,1)} %copy-done.16), kind=kLoop, calls=%fused_computation.43 | loop fusion | bytes 2621440 | tf_op jit(solution)/shard_map/slice | solution.py:338
  55.6 9.1 %all-to-all-done.refs_0_ = bf16[8,336,128]{2,1,0:T(8,128)(2,1)S(1)} async-done(((bf16[8,336,128]{2,1,0:T(8,128)(2,1)}), bf16[8,336,128]{2,1,0:T(8,128)(2,1)S(1)}, u32[]{:S(2)}, u32[]{:S(2)}) %all-to-all-start) | async-done | bytes 688160 | tf_op jit(solution)/shard_map/all_to_all | solution.py:357
  65.7 3.7 %all-to-all-start.1 = ((bf16[8,320,128]{2,1,0:T(8,128)(2,1)}), bf16[8,320,128]{2,1,0:T(8,128)(2,1)S(1)}, u32[]{:S(2)}, u32[]{:S(2)}) async-start(bf16[8,320,128]{2,1,0:T(8,128)(2,1)} %shard_map.147), calls=%async_computation.1 | async-start | bytes 1310720 | tf_op jit(solution)/shard_map/all_to_all | solution.py:374
  69.4 3.3 %fusion.2 = f32[128,896]{1,0:T(8,128)S(1)} fusion(bf16[128,2560]{1,0:T(8,128)(2,1)S(1)} %bitcast.88, bf16[1,2560,896]{2,1,0:T(8,128)(2,1)} %param.17), kind=kOutput, calls=%fused_computation.2 | convolution fusion | flops 587202560 | bytes 5701632 | tf_op jit(solution)/shard_map/dot_general | solution.py:339
  74.1 1.9 %collective-permute-start.26 = (bf16[128,896]{1,0:T(8,128)(2,1)S(1)}, bf16[128,896]{1,0:T(8,128)(2,1)}, u32[]{:S(2)}, u32[]{:S(2)}) collective-permute-start(bf16[128,896]{1,0:T(8,128)(2,1)S(1)} %fusion.8), channel_id=1, source_target_pairs={{0,1},{1,2},{2,3},{3,0},{4,5},{5,6},{6,7},{7,4},{8,9},{9,10},{10,1... | collective-permute-start | bytes 688136 | tf_op jit(solution)/shard_map/ppermute | solution.py:267
  76.0 4.4 %all-to-all-done.1 = bf16[8,320,128]{2,1,0:T(8,128)(2,1)S(1)} async-done(((bf16[8,320,128]{2,1,0:T(8,128)(2,1)}), bf16[8,320,128]{2,1,0:T(8,128)(2,1)S(1)}, u32[]{:S(2)}, u32[]{:S(2)}) %all-to-all-start.1) | async-done | bytes 655392 | tf_op jit(solution)/shard_map/all_to_all | solution.py:374
  80.4 3.7 %all-to-all-start.2 = ((bf16[8,320,128]{2,1,0:T(8,128)(2,1)}), bf16[8,320,128]{2,1,0:T(8,128)(2,1)S(1)}, u32[]{:S(2)}, u32[]{:S(2)}) async-start(bf16[8,320,128]{2,1,0:T(8,128)(2,1)} %bitcast.15), calls=%async_computation.2 | async-start | bytes 1310720 | tf_op jit(solution)/shard_map/all_to_all | solution.py:331
  85.2 7.8 %shard_map.148 = (f32[128,2560]{1,0:T(8,128)S(1)}, bf16[128,2560]{1,0:T(8,128)(2,1)S(1)}, f32[128,128]{1,0:T(8,128)S(1)}, bf16[128,128]{1,0:T(8,128)(2,1)S(1)}, ...) custom-call(bf16[128,2560]{1,0:T(8,128)(2,1)S(1)} %bitcast.81, bf16[128,2560]{1,0:T(8,128)(2,1)S(1)} %bitcast.78, ...), custom_call_target="tpu_custom_call" | custom-call | flops 4000000000 | bytes 4210688 | tf_op jit(solution)/shard_map/pallas_call | solution.py:358
  93.7 1.7 %collective-permute-start.7 = (bf16[128,256]{1,0:T(8,128)(2,1)S(1)}, bf16[128,256]{1,0:T(8,128)(2,1)S(1)}, u32[]{:S(2)}, u32[]{:S(2)}) collective-permute-start(bf16[128,256]{1,0:T(8,128)(2,1)S(1)} %shard_map.149.dbc_ref.refs_1_), channel_id=1, source_target_pairs={{0,8},{4,12},{8,16},{12,20},{16,24},{20,28},{24,0},{28,4},{1,9},{5... | collective-permute-start | bytes 196616 | tf_op jit(solution)/shard_map/ppermute | solution.py:267
  95.4 2.3 %collective-permute-start.8 = (bf16[128,256]{1,0:T(8,128)(2,1)S(1)}, bf16[128,256]{1,0:T(8,128)(2,1)S(1)}, u32[]{:S(2)}, u32[]{:S(2)}) collective-permute-start(bf16[128,256]{1,0:T(8,128)(2,1)S(1)} %shard_map.149.dbc_ref.refs_1_), channel_id=1, source_target_pairs={{0,12},{4,16},{8,20},{12,24},{16,28},{20,0},{24,4},{28,8},{1,13},{... | collective-permute-start | bytes 196616 | tf_op jit(solution)/shard_map/ppermute | solution.py:267
  99.9 2.2 %collective-permute-start.12 = (bf16[128,256]{1,0:T(8,128)(2,1)S(1)}, bf16[128,256]{1,0:T(8,128)(2,1)S(1)}, u32[]{:S(2)}, u32[]{:S(2)}) collective-permute-start(bf16[128,256]{1,0:T(8,128)(2,1)S(1)} %shard_map.149.dbc_ref.refs_1_), channel_id=1, source_target_pairs={{0,28},{4,0},{8,4},{12,8},{16,12},{20,16},{24,20},{28,24},{1,29},{... | collective-permute-start | bytes 196616 | tf_op jit(solution)/shard_map/ppermute | solution.py:267
  102.1 3.1 %fusion.4 = bf16[1,896,640]{2,1,0:T(8,128)(2,1)} fusion(bf16[128,896]{1,0:T(8,128)(2,1)} %collective-permute-done.28, bf16[128,896]{1,0:T(8,128)(2,1)} %collective-permute-done.27, bf16[128,896]{1,0:T(8,128)(2,1)} %collective-permute-done.26, bf16[128,896]{1,0:T(8,128)(2,1)S(1)} %fusion.8, bf16[128,640]{1,0:T(8,128)(2,1)S(1)} %get-tuple-element.43, ...), kind=kOutput, calls=%fused_computation.5 | convolution fusion | flops 594067456 | bytes 2719744 | tf_op jit(solution)/shard_map/dot_general | solution.py:16
  105.9 1.9 %collective-permute-start.13 = (bf16[80,256]{1,0:T(8,128)(2,1)S(1)}, bf16[80,256]{1,0:T(8,128)(2,1)S(1)}, u32[]{:S(2)}, u32[]{:S(2)}) collective-permute-start(bf16[80,256]{1,0:T(8,128)(2,1)S(1)} %get-tuple-element.46), channel_id=1, source_target_pairs={{0,1},{1,2},{2,3},{3,0},{4,5},{5,6},{6,7},{7,4},{8,9},{9,10},{10,1... | collective-permute-start | bytes 122888 | tf_op jit(solution)/shard_map/ppermute | solution.py:267
  110.5 3.1 %shard_map.150 = (bf16[128,2560]{1,0:T(8,128)(2,1)}, f32[128,40]{1,0:T(8,128)S(1)}, f32[128,40]{1,0:T(8,128)S(1)}) custom-call(bf16[128,2560]{1,0:T(8,128)(2,1)S(1)} %bitcast.82, bf16[128,256]{1,0:T(8,128)(2,1)S(1)} %get-tuple-element.20.bc_ref, f32[128,40]{1,0:T(8,128)S(1)} %bitcast.69, f32[128,40]{1,0:T(8,128)S(1)} %bitcast.71, ...), custom_call_target="tpu_custom_call" | custom-call | flops 2000000000 | bytes 1392640 | tf_op jit(solution)/shard_map/pallas_call | solution.py:377
  (107 shorter events, 28.6 us)
Async XLA Ops:
  6.0 9.8 %collective-permute-start.18 = (bf16[16,640]{1,0:T(8,128)(2,1)S(1)}, bf16[16,640]{1,0:T(8,128)(2,1)S(1)}, u32[]{:S(2)}, u32[]{:S(2)}) collective-permute-start(bf16[16,640]{1,0:T(8,128)(2,1)S(1)} %get-tuple-element.50), channel_id=1, source_target_pairs={{0,3},{1,0},{2,1},{3,2},{4,7},{5,4},{6,5},{7,6},{8,11},{9,8},{10,9... | collective-permute-start | bytes 61448 | tf_op jit(solution)/shard_map/ppermute | solution.py:267
  11.2 10.5 %collective-permute-start.17 = (bf16[16,640]{1,0:T(8,128)(2,1)S(1)}, bf16[16,640]{1,0:T(8,128)(2,1)S(1)}, u32[]{:S(2)}, u32[]{:S(2)}) collective-permute-start(bf16[16,640]{1,0:T(8,128)(2,1)S(1)} %get-tuple-element.51), channel_id=1, source_target_pairs={{0,2},{1,3},{2,0},{3,1},{4,6},{5,7},{6,4},{7,5},{8,10},{9,11},{10,... | collective-permute-start | bytes 61448 | tf_op jit(solution)/shard_map/ppermute | solution.py:267
  11.2 10.5 %collective-permute-start.16 = (bf16[16,640]{1,0:T(8,128)(2,1)S(1)}, bf16[16,640]{1,0:T(8,128)(2,1)S(1)}, u32[]{:S(2)}, u32[]{:S(2)}) collective-permute-start(bf16[16,640]{1,0:T(8,128)(2,1)S(1)} %get-tuple-element.52), channel_id=1, source_target_pairs={{0,1},{1,2},{2,3},{3,0},{4,5},{5,6},{6,7},{7,4},{8,9},{9,10},{10,1... | collective-permute-start | bytes 61448 | tf_op jit(solution)/shard_map/ppermute | solution.py:267
  12.2 26.2 %collective-permute-start = (bf16[640,128]{1,0:T(8,128)(2,1)S(1)}, bf16[640,128]{1,0:T(8,128)(2,1)S(1)}, u32[]{:S(2)}, u32[]{:S(2)}) collective-permute-start(bf16[640,128]{1,0:T(8,128)(2,1)S(1)} %constant_dynamic-slice_fusion), channel_id=1, source_target_pairs={{0,1},{1,2},{2,3},{3,0},{4,5},{5,6},{6,7},{7,4},{8,9},{9,10},{10,1... | collective-permute-start | bytes 491528 | tf_op jit(solution)/shard_map/ppermute | solution.py:267
  14.7 25.5 %collective-permute-start.1 = (bf16[640,128]{1,0:T(8,128)(2,1)S(1)}, bf16[640,128]{1,0:T(8,128)(2,1)S(1)}, u32[]{:S(2)}, u32[]{:S(2)}) collective-permute-start(bf16[640,128]{1,0:T(8,128)(2,1)S(1)} %constant_dynamic-slice_fusion), channel_id=1, source_target_pairs={{0,2},{1,3},{2,0},{3,1},{4,6},{5,7},{6,4},{7,5},{8,10},{9,11},{10,... | collective-permute-start | bytes 491528 | tf_op jit(solution)/shard_map/ppermute | solution.py:267
  15.8 24.3 %collective-permute-start.2 = (bf16[640,128]{1,0:T(8,128)(2,1)S(1)}, bf16[640,128]{1,0:T(8,128)(2,1)S(1)}, u32[]{:S(2)}, u32[]{:S(2)}) collective-permute-start(bf16[640,128]{1,0:T(8,128)(2,1)S(1)} %constant_dynamic-slice_fusion), channel_id=1, source_target_pairs={{0,3},{1,0},{2,1},{3,2},{4,7},{5,4},{6,5},{7,6},{8,11},{9,8},{10,9... | collective-permute-start | bytes 491528 | tf_op jit(solution)/shard_map/ppermute | solution.py:267
  21.7 6.9 %collective-permute-start.19 = (bf16[32,2560]{1,0:T(8,128)(2,1)S(1)}, bf16[32,2560]{1,0:T(8,128)(2,1)S(1)}, u32[]{:S(2)}, u32[]{:S(2)}) collective-permute-start(bf16[32,2560]{1,0:T(8,128)(2,1)S(1)} %maximum_maximum_fusion), channel_id=1, source_target_pairs={{0,4},{4,8},{8,12},{12,16},{16,20},{20,24},{24,28},{28,0},{1,5},{5... | collective-permute-start | bytes 491528 | tf_op jit(solution)/shard_map/ppermute | solution.py:267
  21.8 8.0 %collective-permute-start.20 = (bf16[32,2560]{1,0:T(8,128)(2,1)S(1)}, bf16[32,2560]{1,0:T(8,128)(2,1)S(1)}, u32[]{:S(2)}, u32[]{:S(2)}) collective-permute-start(bf16[32,2560]{1,0:T(8,128)(2,1)S(1)} %maximum_maximum_fusion), channel_id=1, source_target_pairs={{0,8},{4,12},{8,16},{12,20},{16,24},{20,28},{24,0},{28,4},{1,9},{5... | collective-permute-start | bytes 491528 | tf_op jit(solution)/shard_map/ppermute | solution.py:267
  28.6 8.1 %collective-permute-start.21 = (bf16[32,2560]{1,0:T(8,128)(2,1)S(1)}, bf16[32,2560]{1,0:T(8,128)(2,1)S(1)}, u32[]{:S(2)}, u32[]{:S(2)}) collective-permute-start(bf16[32,2560]{1,0:T(8,128)(2,1)S(1)} %maximum_maximum_fusion), channel_id=1, source_target_pairs={{0,12},{4,16},{8,20},{12,24},{16,28},{20,0},{24,4},{28,8},{1,13},{... | collective-permute-start | bytes 491528 | tf_op jit(solution)/shard_map/ppermute | solution.py:267
  29.8 7.3 %collective-permute-start.22 = (bf16[32,2560]{1,0:T(8,128)(2,1)S(1)}, bf16[32,2560]{1,0:T(8,128)(2,1)S(1)}, u32[]{:S(2)}, u32[]{:S(2)}) collective-permute-start(bf16[32,2560]{1,0:T(8,128)(2,1)S(1)} %maximum_maximum_fusion), channel_id=1, source_target_pairs={{0,16},{4,20},{8,24},{12,28},{16,0},{20,4},{24,8},{28,12},{1,17},{... | collective-permute-start | bytes 491528 | tf_op jit(solution)/shard_map/ppermute | solution.py:267
  37.0 7.1 %collective-permute-start.24 = (bf16[32,2560]{1,0:T(8,128)(2,1)S(1)}, bf16[32,2560]{1,0:T(8,128)(2,1)S(1)}, u32[]{:S(2)}, u32[]{:S(2)}) collective-permute-start(bf16[32,2560]{1,0:T(8,128)(2,1)S(1)} %maximum_maximum_fusion), channel_id=1, source_target_pairs={{0,24},{4,28},{8,0},{12,4},{16,8},{20,12},{24,16},{28,20},{1,25},{... | collective-permute-start | bytes 491528 | tf_op jit(solution)/shard_map/ppermute | solution.py:267
  49.1 15.5 %all-to-all-start = ((bf16[8,336,128]{2,1,0:T(8,128)(2,1)}), bf16[8,336,128]{2,1,0:T(8,128)(2,1)S(1)}, u32[]{:S(2)}, u32[]{:S(2)}) async-start(bf16[8,336,128]{2,1,0:T(8,128)(2,1)} %get-tuple-element.21), calls=%async_computation | async-start | bytes 1376256 | tf_op jit(solution)/shard_map/all_to_all | solution.py:357
  65.7 14.8 %all-to-all-start.1 = ((bf16[8,320,128]{2,1,0:T(8,128)(2,1)}), bf16[8,320,128]{2,1,0:T(8,128)(2,1)S(1)}, u32[]{:S(2)}, u32[]{:S(2)}) async-start(bf16[8,320,128]{2,1,0:T(8,128)(2,1)} %shard_map.147), calls=%async_computation.1 | async-start | bytes 1310720 | tf_op jit(solution)/shard_map/all_to_all | solution.py:374
  73.9 21.5 %collective-permute-start.28 = (bf16[128,896]{1,0:T(8,128)(2,1)S(1)}, bf16[128,896]{1,0:T(8,128)(2,1)}, u32[]{:S(2)}, u32[]{:S(2)}) collective-permute-start(bf16[128,896]{1,0:T(8,128)(2,1)S(1)} %fusion.8), channel_id=1, source_target_pairs={{0,3},{1,0},{2,1},{3,2},{4,7},{5,4},{6,5},{7,6},{8,11},{9,8},{10,9... | collective-permute-start | bytes 688136 | tf_op jit(solution)/shard_map/ppermute | solution.py:267
  74.0 23.8 %collective-permute-start.27 = (bf16[128,896]{1,0:T(8,128)(2,1)S(1)}, bf16[128,896]{1,0:T(8,128)(2,1)}, u32[]{:S(2)}, u32[]{:S(2)}) collective-permute-start(bf16[128,896]{1,0:T(8,128)(2,1)S(1)} %fusion.8), channel_id=1, source_target_pairs={{0,2},{1,3},{2,0},{3,1},{4,6},{5,7},{6,4},{7,5},{8,10},{9,11},{10,... | collective-permute-start | bytes 688136 | tf_op jit(solution)/shard_map/ppermute | solution.py:267
  74.1 24.2 %collective-permute-start.26 = (bf16[128,896]{1,0:T(8,128)(2,1)S(1)}, bf16[128,896]{1,0:T(8,128)(2,1)}, u32[]{:S(2)}, u32[]{:S(2)}) collective-permute-start(bf16[128,896]{1,0:T(8,128)(2,1)S(1)} %fusion.8), channel_id=1, source_target_pairs={{0,1},{1,2},{2,3},{3,0},{4,5},{5,6},{6,7},{7,4},{8,9},{9,10},{10,1... | collective-permute-start | bytes 688136 | tf_op jit(solution)/shard_map/ppermute | solution.py:267
  80.4 24.8 %all-to-all-start.2 = ((bf16[8,320,128]{2,1,0:T(8,128)(2,1)}), bf16[8,320,128]{2,1,0:T(8,128)(2,1)S(1)}, u32[]{:S(2)}, u32[]{:S(2)}) async-start(bf16[8,320,128]{2,1,0:T(8,128)(2,1)} %bitcast.15), calls=%async_computation.2 | async-start | bytes 1310720 | tf_op jit(solution)/shard_map/all_to_all | solution.py:331
  95.4 9.8 %collective-permute-start.8 = (bf16[128,256]{1,0:T(8,128)(2,1)S(1)}, bf16[128,256]{1,0:T(8,128)(2,1)S(1)}, u32[]{:S(2)}, u32[]{:S(2)}) collective-permute-start(bf16[128,256]{1,0:T(8,128)(2,1)S(1)} %shard_map.149.dbc_ref.refs_1_), channel_id=1, source_target_pairs={{0,12},{4,16},{8,20},{12,24},{16,28},{20,0},{24,4},{28,8},{1,13},{... | collective-permute-start | bytes 196616 | tf_op jit(solution)/shard_map/ppermute | solution.py:267
  97.7 7.5 %collective-permute-start.9 = (bf16[128,256]{1,0:T(8,128)(2,1)S(1)}, bf16[128,256]{1,0:T(8,128)(2,1)S(1)}, u32[]{:S(2)}, u32[]{:S(2)}) collective-permute-start(bf16[128,256]{1,0:T(8,128)(2,1)S(1)} %shard_map.149.dbc_ref.refs_1_), channel_id=1, source_target_pairs={{0,16},{4,20},{8,24},{12,28},{16,0},{20,4},{24,8},{28,12},{1,17},{... | collective-permute-start | bytes 196616 | tf_op jit(solution)/shard_map/ppermute | solution.py:267
  98.2 6.9 %collective-permute-start.10 = (bf16[128,256]{1,0:T(8,128)(2,1)S(1)}, bf16[128,256]{1,0:T(8,128)(2,1)S(1)}, u32[]{:S(2)}, u32[]{:S(2)}) collective-permute-start(bf16[128,256]{1,0:T(8,128)(2,1)S(1)} %shard_map.149.dbc_ref.refs_1_), channel_id=1, source_target_pairs={{0,20},{4,24},{8,28},{12,0},{16,4},{20,8},{24,12},{28,16},{1,21},{... | collective-permute-start | bytes 196616 | tf_op jit(solution)/shard_map/ppermute | solution.py:267
  98.4 6.8 %collective-permute-start.11 = (bf16[128,256]{1,0:T(8,128)(2,1)S(1)}, bf16[128,256]{1,0:T(8,128)(2,1)S(1)}, u32[]{:S(2)}, u32[]{:S(2)}) collective-permute-start(bf16[128,256]{1,0:T(8,128)(2,1)S(1)} %shard_map.149.dbc_ref.refs_1_), channel_id=1, source_target_pairs={{0,24},{4,28},{8,0},{12,4},{16,8},{20,12},{24,16},{28,20},{1,25},{... | collective-permute-start | bytes 196616 | tf_op jit(solution)/shard_map/ppermute | solution.py:267
  105.7 9.2 %collective-permute-start.15 = (bf16[80,256]{1,0:T(8,128)(2,1)S(1)}, bf16[80,256]{1,0:T(8,128)(2,1)S(1)}, u32[]{:S(2)}, u32[]{:S(2)}) collective-permute-start(bf16[80,256]{1,0:T(8,128)(2,1)S(1)} %get-tuple-element.47), channel_id=1, source_target_pairs={{0,3},{1,0},{2,1},{3,2},{4,7},{5,4},{6,5},{7,6},{8,11},{9,8},{10,9... | collective-permute-start | bytes 122888 | tf_op jit(solution)/shard_map/ppermute | solution.py:267
  105.8 9.1 %collective-permute-start.14 = (bf16[80,256]{1,0:T(8,128)(2,1)S(1)}, bf16[80,256]{1,0:T(8,128)(2,1)S(1)}, u32[]{:S(2)}, u32[]{:S(2)}) collective-permute-start(bf16[80,256]{1,0:T(8,128)(2,1)S(1)} %get-tuple-element.48), channel_id=1, source_target_pairs={{0,2},{1,3},{2,0},{3,1},{4,6},{5,7},{6,4},{7,5},{8,10},{9,11},{10,... | collective-permute-start | bytes 122888 | tf_op jit(solution)/shard_map/ppermute | solution.py:267
  105.9 9.1 %collective-permute-start.13 = (bf16[80,256]{1,0:T(8,128)(2,1)S(1)}, bf16[80,256]{1,0:T(8,128)(2,1)S(1)}, u32[]{:S(2)}, u32[]{:S(2)}) collective-permute-start(bf16[80,256]{1,0:T(8,128)(2,1)S(1)} %get-tuple-element.46), channel_id=1, source_target_pairs={{0,1},{1,2},{2,3},{3,0},{4,5},{5,6},{6,7},{7,4},{8,9},{9,10},{10,1... | collective-permute-start | bytes 122888 | tf_op jit(solution)/shard_map/ppermute | solution.py:267
  (27 other events, 146.3 us)

commit v3 on v2

v3 whole, which is shorter than its diff:
```python
import jax
import jax.numpy as jnp
from jax import lax
from jax.experimental import pallas as pl
from jax.experimental.pallas import tpu as pltpu
from jax.sharding import PartitionSpec as P

HI = lax.Precision.HIGHEST
F32 = jnp.float32
BF16 = jnp.bfloat16
LANES = 128


def dot(a, b, ca, cb, precision=None):
    return lax.dot_general(
        a, b, (((ca,), (cb,)), ((), ())), precision=precision, preferred_element_type=F32
    )


def iota(dims, axis):
    return lax.broadcasted_iota(jnp.int32, dims, axis)


def where_one(mask):
    return jnp.where(mask, 1.0, 0.0)


def triangle(n, keep):
    return where_one(keep(iota((n, n), 0), iota((n, n), 1))).astype(F32)


def halves(values, axis=1):
    high = values.astype(BF16)
    low = (values - high.astype(F32)).astype(BF16)
    return jnp.concatenate([high, low], axis=axis)


def to_lanes(j, size):
    dims = (LANES, LANES)
    one = where_one(iota(dims, 0) == iota(dims, 1) // size + j * (LANES // size)).astype(BF16)
    return jnp.concatenate([one, one], axis=0)


def to_heads(j, heads, size):
    dims = (heads, LANES)
    one = where_one(iota(dims, 0) == iota(dims, 1) // size + j * (LANES // size)).astype(BF16)
    return jnp.concatenate([one, one], axis=1)


def up16(n):
    return -(-n // 16) * 16


def call(kernel, outs, cost, args, after=(), scratch=(), limit=14):
    n_in, n_after = len(args), len(after)

    def body(*refs):
        kernel(*refs[:n_in], *refs[n_in + n_after :])

    return pl.pallas_call(
        body,
        out_shape=outs,
        in_specs=[pl.BlockSpec(memory_space=pltpu.VMEM)] * n_in
        + [pl.BlockSpec(memory_space=pl.ANY)] * n_after,
        out_specs=[pl.BlockSpec(memory_space=pltpu.VMEM)] * len(outs),
        scratch_shapes=list(scratch),
        cost_estimate=pl.CostEstimate(
            flops=int(cost * 1e9), bytes_accessed=1000, transcendentals=0
        ),
        compiler_params=pltpu.CompilerParams(vmem_limit_bytes=limit * 1024 * 1024),
    )(*args, *after)


def shape(dims, kind):
    return jax.ShapeDtypeStruct(dims, kind)


def core_and_chip():
    place = lax.axis_index("tm")
    return lax.rem(place, 2), lax.div(place, 2), lax.axis_size("tm") // 2


def ahead(index, shift, count):
    return lax.rem(index + shift, count)


def rows_at(index, size, align=16):
    return pl.ds(pl.multiple_of(index * size, align), size)


def prep_kernel(
    x_ref, dy_ref, ldt_ref, stept_ref, h_ref,
    cumt_ref, cum_ref, step_ref, dyt_ref, xt_ref, xs_ref, carried_ref,
):
    length, width = x_ref.shape
    heads = ldt_ref.shape[0]
    size = width // heads
    pad = jnp.zeros((LANES - heads, length), F32)
    cumt = dot(ldt_ref[...], triangle(length, lambda a, b: a <= b), 1, 0, HI)
    cumt_ref[...] = cumt
    cum = jnp.concatenate([cumt, pad], axis=0).T
    step = jnp.concatenate([stept_ref[...], pad], axis=0).T
    cum_ref[...] = cum
    step_ref[...] = step
    start = jnp.exp(cum)
    into_end = jnp.exp(cum[length - 1 : length] - cum) * step
    table = jnp.concatenate([halves(start), halves(into_end)], axis=0)
    carried = jnp.zeros(carried_ref.shape, F32)
    for j in range(width // LANES):
        span = slice(j * LANES, (j + 1) * LANES)
        scale = dot(table, to_lanes(j, size), 1, 0)
        x_f = x_ref[:, span].astype(F32)
        xt_ref[span, :] = x_f.T.astype(BF16)
        xs_ref[:, span] = (x_f * scale[length:]).astype(BF16)
        dys = dy_ref[:, span].astype(F32) * scale[:length]
        dyt_ref[span, :] = dys.T.astype(BF16)
        carried = carried + dot(dys.astype(BF16), h_ref[span, :], 1, 0)
    carried_ref[...] = carried


def pick_kernel(x_ref, dy_ref, rows_ref, count_ref, gate_ref, in_ref, grad_ref):
    length = x_ref.shape[0]
    slots = rows_ref.shape[1]
    hit = iota((length, slots), 0) == rows_ref[...]
    live = iota((1, slots), 1) < count_ref[...]
    weight = jnp.where(live, gate_ref[...].astype(F32), 0.0)
    pick = where_one(hit).astype(BF16)
    scaled = jnp.where(hit, weight, 0.0).astype(BF16)
    in_ref[...] = dot(pick, x_ref[...], 0, 0).astype(BF16)
    grads = dot(scaled, dy_ref[...], 0, 0).astype(BF16)
    piece = grad_ref.shape[2]
    for i in range(grad_ref.shape[0]):
        grad_ref[i] = grads[:, i * piece : (i + 1) * piece]


def assemble(w_ref, own_ref, mine_refs, other_ref):
    core, _, _ = core_and_chip()
    place, n_dp = lax.axis_index("dp"), lax.axis_size("dp")
    share = own_ref.shape[0]
    half = share // 2
    w_ref[rows_at(place, share), :] = own_ref[...]
    for i, mine in enumerate(mine_refs):
        source = ahead(place, n_dp - 1 - i, n_dp)
        w_ref[rows_at(source * 2 + core, half), :] = mine[...]
        w_ref[rows_at(source * 2 + 1 - core, half), :] = other_ref[i]


def project_kernel(n_mine, *refs):
    x_ref, dyt_ref, cumt_ref, own_ref = refs[:4]
    mine, other = refs[4 : 4 + n_mine], refs[4 + n_mine]
    w_ref, c_ref, keep_ref, send_ref = refs[5 + n_mine :]
    core, _, _ = core_and_chip()
    assemble(w_ref, own_ref, mine, other)
    c_rows = dot(x_ref[...], w_ref[...], 1, 0).astype(BF16)
    c_ref[...] = c_rows
    heads, length = cumt_ref.shape
    width = dyt_ref.shape[0]
    part, many = width // 2, heads // 2
    decay = jnp.broadcast_to(jnp.exp(cumt_ref[:, length - 1 : length]), (heads, LANES))
    for ref, index in ((keep_ref, core), (send_ref, 1 - core)):
        ref[:part, :] = dot(dyt_ref[rows_at(index, part), :], c_rows, 1, 0).astype(BF16)
        mine_decay = jnp.where(index == 0, decay[:many], decay[many:])
        high = mine_decay.astype(BF16).astype(F32)
        fill = jnp.zeros((ref.shape[0] - part - 2 * many, LANES), F32)
        extra = jnp.concatenate([high, mine_decay - high, fill], axis=0)
        ref[part:, :] = extra.astype(BF16)


def pair(keep_ref, recv_ref, many, size, head):
    core, _, _ = core_and_chip()
    part = many * size
    both = []
    for ref in (keep_ref, recv_ref):
        extra = ref[part:, :].astype(F32)
        decay = extra[head : head + 1] + extra[many + head : many + head + 1]
        both.append((ref[head * size : (head + 1) * size, :].astype(F32), decay))
    first = jax.tree.map(lambda a, b: jnp.where(core == 0, a, b), both[0], both[1])
    second = jax.tree.map(lambda a, b: jnp.where(core == 0, b, a), both[0], both[1])
    return first, second


def combine_kernel(many, size, unit, *refs):
    keep_ref, recv_ref = refs[:2]
    outs, held = refs[2:-1], refs[-1]
    _, chip, n_chip = core_and_chip()
    block = many * size // n_chip
    units = block // unit
    decays = []
    for head in range(many):
        (g0, a0), (g1, a1) = pair(keep_ref, recv_ref, many, size, head)
        state = (g0 + a0 * g1).astype(BF16)
        for i in range(size // unit):
            row = head * size + i * unit
            held[row // block, row % block : row % block + unit, :] = state[
                i * unit : (i + 1) * unit
            ]
            decays.append(a0 * a1)
    for b in range(n_chip):
        mine = jnp.concatenate(decays[b * units : (b + 1) * units], axis=0)
        high = mine.astype(BF16).astype(F32)
        fill = jnp.zeros((held.shape[1] - block - 2 * units, LANES), F32)
        extra = jnp.concatenate([high, mine - high, fill], axis=0)
        held[b, block:, :] = extra.astype(BF16)
    for s, out in enumerate(outs):
        out[...] = held[ahead(chip, s, n_chip)]


def scan_kernel(unit, *refs):
    _, chip, n_chip = core_and_chip()
    pieces, outs = refs[:n_chip], refs[n_chip : 2 * n_chip]
    held, result = refs[2 * n_chip :]
    block, states = outs[0].shape
    units = block // unit
    for s, ref in enumerate(pieces):
        held[ahead(chip, n_chip - s, n_chip)] = ref[...]
    carry = [jnp.zeros((unit, states), F32)] * units
    for k in reversed(range(n_chip)):
        extra = held[k, block:, :].astype(F32)
        for u in range(units):
            span = slice(u * unit, (u + 1) * unit)
            result[k, span, :] = carry[u].astype(BF16)
            if k:
                decay = extra[u : u + 1] + extra[units + u : units + u + 1]
                carry[u] = held[k, span, :].astype(F32) + decay * carry[u]
    for s, out in enumerate(outs):
        out[...] = result[ahead(chip, s, n_chip)]


def carry_kernel(many, size, *refs):
    core, chip, n_chip = core_and_chip()
    pieces = refs[:n_chip]
    keep_ref, recv_ref, own_ref, send_ref, held = refs[n_chip:]
    block = pieces[0].shape[0]
    for s, ref in enumerate(pieces):
        held[rows_at(ahead(chip, n_chip - s, n_chip), block), :] = ref[...]
    for head in range(many):
        span = slice(head * size, (head + 1) * size)
        _, (g1, a1) = pair(keep_ref, recv_ref, many, size, head)
        second = held[span, :].astype(F32)
        first = g1 + a1 * second
        own_ref[span, :] = jnp.where(core == 0, first, second).astype(BF16)
        send_ref[span, :] = jnp.where(core == 0, second, first).astype(BF16)


def b_kernel(n_mine, *refs):
    x_ref, own_ref = refs[:2]
    mine, other = refs[2 : 2 + n_mine], refs[2 + n_mine]
    w_ref, b_ref = refs[3 + n_mine :]
    assemble(w_ref, own_ref, mine, other)
    b_ref[...] = dot(x_ref[...], w_ref[...], 1, 0).astype(BF16)


def intra_kernel(
    first, many, x_ref, dy_ref, b_ref, c_ref, cumt_ref, cum_ref, step_ref, h_ref, before_ref,
    dx_ref, mixed_ref, ex_ref, own_ref, rowm_ref,
):
    length, width = x_ref.shape
    heads = cumt_ref.shape[0]
    size = width // heads
    per = LANES // size
    upper = iota((length, length), 0) <= iota((length, length), 1)
    b_rows, c_rows = b_ref[...], c_ref[...]
    scores = dot(b_rows, c_rows, 1, 1)
    lane = iota((1, LANES), 1)
    lane_bf = [where_one(lane // size == i).astype(BF16) for i in range(per)]
    mixed = before_ref[...]
    own = jnp.zeros((length, LANES), F32)
    reach = jnp.zeros((heads, length), F32)
    for j in range(first, first + many):
        span = slice(j * LANES, (j + 1) * LANES)
        out_span = slice((j - first) * LANES, (j - first + 1) * LANES)
        x_p = x_ref[:, span]
        dy_p = dy_ref[:, span]
        dy_h = jnp.concatenate([dy_p * m for m in lane_bf], axis=0)
        cross = dot(x_p, dy_h, 1, 1)
        kern = []
        wide = None
        for i in range(per):
            h = j * per + i
            diff = cumt_ref[h : h + 1, :] - cum_ref[:, h : h + 1]
            seg = jnp.exp(jnp.where(upper, diff, -1e30))
            kern.append((seg * scores).astype(BF16))
            step = jnp.broadcast_to(step_ref[:, h : h + 1], (length, LANES))
            wide = step if i == 0 else jnp.where(lane < i * size, wide, step)
            scaled = seg * cross[:, i * length : (i + 1) * length] * step
            mixed = mixed + scaled
            full = scaled * scores
            rowm_ref[h : h + 1, :] = jnp.sum(full, axis=0, keepdims=True)
            own = jnp.where(lane == h, jnp.sum(full, axis=1, keepdims=True), own)
        back = dot(jnp.concatenate(kern, axis=1), dy_h, 1, 0)
        dx_ref[:, out_span] = back * wide
        seen = dy_p.astype(F32) * dot(c_rows, h_ref[span, :], 1, 1)
        reach = reach + dot(to_heads(j, heads, size), halves(seen), 1, 1)
    mixed_ref[...] = mixed
    rows = slice(first * per, (first + many) * per)
    own = own.T[rows]
    own_ref[...] = own
    ex_ref[...] = rowm_ref[rows, :] + jnp.exp(cumt_ref[rows, :]) * reach[rows] - own


def close_kernel(mixed_ref, b_ref, c_ref, carried_ref, db_ref, dc_ref):
    mixed = mixed_ref[...].astype(BF16)
    db_ref[...] = dot(mixed, c_ref[...], 1, 0)
    dc_ref[...] = (dot(mixed, b_ref[...], 0, 0) + carried_ref[...]).astype(BF16)


def db_kernel(xs_ref, own_ref, recv_ref, db_ref, dc_ref, out_ref):
    core, _, _ = core_and_chip()
    half = db_ref.shape[1]
    part = own_ref.shape[0]
    total = db_ref[...]
    for ref, index in ((own_ref, core), (recv_ref, 1 - core)):
        total = total + dot(xs_ref[:, rows_at(index, part, LANES)], ref[...], 1, 0)
    out_ref[:, :half] = total.astype(BF16)
    out_ref[:, half:] = dc_ref[...]


def finish_kernel(parts, *refs):
    (x_ref, b_ref, cumt_ref, stept_ref, cum_ref, step_ref, h_ref, own_ref, recv_ref,
     wb_ref, wc_ref, dbc_ref) = refs[:12]
    dx_refs, ex_refs, st_refs = (refs[12 + i * parts : 12 + (i + 1) * parts] for i in range(3))
    in_ref, decay_ref, grad_ref, r_ref, edge_ref = refs[12 + 3 * parts :]
    core, _, _ = core_and_chip()
    length, width = x_ref.shape
    heads = cumt_ref.shape[0]
    size = width // heads
    half = b_ref.shape[1]
    part = width // 2
    r_ref[rows_at(core, part), :] = own_ref[...]
    r_ref[rows_at(1 - core, part), :] = recv_ref[...]
    cum = cum_ref[...]
    table = halves(jnp.exp(cum[length - 1 : length] - cum) * step_ref[...])
    seen = jnp.zeros((heads, length), F32)
    b_rows = b_ref[...]
    d_b, d_c = dbc_ref[:, :half], dbc_ref[:, half:]
    for j in range(width // LANES):
        span = slice(j * LANES, (j + 1) * LANES)
        local = dx_refs[j * LANES // (width // parts)]
        start = j * LANES % (width // parts)
        r_tile = r_ref[span, :]
        reach = dot(b_rows, r_tile, 1, 1)
        d_in = local[:, start : start + LANES] + dot(table, to_lanes(j, size), 1, 0) * reach
        d_in = d_in + dot(d_b, wb_ref[span, :], 1, 1) + dot(d_c, wc_ref[span, :], 1, 1)
        in_ref[:, span] = d_in.astype(BF16)
        product = x_ref[:, span].astype(F32) * reach
        seen = seen + dot(to_heads(j, heads, size), halves(product), 1, 1)
        edge = r_tile.astype(F32) * h_ref[span, :].astype(F32)
        for i in range(LANES // size):
            h = j * (LANES // size) + i
            edge_ref[h : h + 1, :] = jnp.sum(
                edge[i * size : (i + 1) * size], axis=0, keepdims=True
            )
    cumt = cumt_ref[...]
    total = cumt[:, length - 1 : length]
    to_end = jnp.exp(total - cumt)
    step = stept_ref[...]
    own = jnp.concatenate([r[...] for r in st_refs], axis=0)
    excess = jnp.concatenate([r[...] for r in ex_refs], axis=0)
    grad_ref[...] = own / step + to_end * seen
    edge = jnp.exp(total) * jnp.sum(edge_ref[...], axis=1, keepdims=True)
    decay_ref[...] = (
        dot(excess, triangle(length, lambda a, b: a >= b), 1, 0, HI)
        + dot(to_end * step * seen, triangle(length, lambda a, b: a < b), 1, 0, HI)
        + edge
    )


def term_kernel(n_chip, *refs):
    columns, pieces = refs[:n_chip], refs[n_chip : 2 * n_chip]
    keep_ref, send_ref = refs[2 * n_chip : 2 * n_chip + 2]
    held = refs[-1]
    core, _, _ = core_and_chip()
    total = None
    for a, b in zip(columns, pieces):
        part = dot(a[...], b[...], 1, 0)
        total = part if total is None else total + part
    block = keep_ref.shape[0]
    held[0] = total[:block]
    held[1] = total[block:]
    keep_ref[...] = held[core]
    send_ref[...] = held[1 - core].astype(BF16)


def deal_kernel(keep_ref, recv_ref, own_ref, *refs):
    outs, held = refs[:-1], refs[-1]
    place, n_dp = lax.axis_index("dp"), lax.axis_size("dp")
    total = keep_ref[...] + recv_ref[...].astype(F32)
    share = own_ref.shape[0]
    for i in range(n_dp):
        held[i] = total[i * share : (i + 1) * share]
    own_ref[...] = held[place]
    for s, out in enumerate(outs):
        out[...] = held[ahead(place, s + 1, n_dp)].astype(BF16)


def expert_kernel(flip, a_ref, b_ref, gate_ref, up_ref, out_ref, rows_ref, gate_acc, up_acc):
    step = pl.program_id(0)
    n_chip, double, _ = a_ref.shape
    slots = double // 2

    @pl.when(step == 0)
    def _():
        for i in range(n_chip):
            rows_ref[i * slots : (i + 1) * slots, :] = a_ref[i, :slots, :]
            rows_ref[(n_chip + i) * slots : (n_chip + i + 1) * slots, :] = b_ref[i, :slots, :]
        gate_acc[...] = jnp.zeros_like(gate_acc)
        up_acc[...] = jnp.zeros_like(up_acc)

    depth = gate_ref.shape[0]
    rows = rows_ref[:, rows_at(step, depth, LANES)]
    gate_acc[...] += dot(rows, gate_ref[...], 1, 0)
    up_acc[...] += dot(rows, up_ref[...], 1, 0)

    @pl.when(step == pl.num_programs(0) - 1)
    def _():
        weighted = jax.nn.silu(gate_acc[...]) * up_acc[...]
        out_ref[...] = (weighted.T if flip else weighted).astype(BF16)


def expert(a, b, w_gate, w_up, flip):
    n_chip, double, width = a.shape
    slots = n_chip * double
    hidden = w_gate.shape[1]
    depth = 512
    whole = pl.BlockSpec((n_chip, double, width), lambda i: (0, 0, 0))
    block = pl.BlockSpec((depth, hidden), lambda i: (i, 0))
    out = (hidden, slots) if flip else (slots, hidden)
    return pl.pallas_call(
        lambda *refs: expert_kernel(flip, *refs),
        out_shape=shape(out, BF16),
        grid=(width // depth,),
        in_specs=[whole, whole, block, block],
        out_specs=pl.BlockSpec(out, lambda i: (0, 0)),
        scratch_shapes=[
            pltpu.VMEM((slots, width), BF16),
            pltpu.VMEM((slots, hidden), F32),
            pltpu.VMEM((slots, hidden), F32),
        ],
        cost_estimate=pl.CostEstimate(
            flops=4 * slots * width * hidden,
            bytes_accessed=4 * width * hidden,
            transcendentals=0,
        ),
        compiler_params=pltpu.CompilerParams(vmem_limit_bytes=20 * 1024 * 1024),
    )(a, b, w_gate, w_up)


def down_kernel(n_dp, flip, *refs):
    pieces = refs[:n_dp]
    a_ref, b_ref, out_ref = refs[n_dp:]
    n_chip, double, _ = a_ref.shape
    slots = double // 2
    piece = out_ref.shape[1]
    total = None
    for s in range(n_dp):
        span = slice(s * piece, (s + 1) * piece)
        grads = jnp.concatenate(
            [r[i, slots:, span] for r in (a_ref, b_ref) for i in range(n_chip)], axis=0
        )
        part = dot(pieces[s][...], grads, 1 if flip else 0, 0)
        total = part if total is None else total + part
    out_ref[...] = total.astype(BF16)


def shifted(array, axis, shift, stride=1):
    count = lax.axis_size(axis)
    return lax.ppermute(array, axis, [(i, (i + shift * stride) % count) for i in range(count)])


def swapped(array):
    return lax.ppermute(array, "tm", [(i, i ^ 1) for i in range(lax.axis_size("tm"))])


def chips(arrays):
    return [arrays[0]] + [shifted(a, "tm", s + 1, 2) for s, a in enumerate(arrays[1:])]


def dealt(array, axis):
    count = lax.axis_size(axis)
    place = lax.axis_index(axis)
    pieces = [lax.dynamic_index_in_dim(array, place, 0, False)]
    for s in range(1, count):
        block = lax.dynamic_index_in_dim(array, lax.rem(place + s, count), 0, False)
        pieces.append(shifted(block, axis, s))
    return pieces


def per_device(
    layer_in,
    out_grad,
    w_bc,
    log_decay,
    step,
    saved_states,
    w_gate,
    w_up,
    slot_rows,
    slot_counts,
    slot_gates,
):
    n_dp = lax.axis_size("dp")
    core, chip, n_chip = core_and_chip()
    x = layer_in[0]
    dy = out_grad[0]
    length, width = x.shape
    heads = log_decay.shape[2]
    size = width // heads
    share, columns = w_bc.shape
    half = columns // 2
    ldt = log_decay[0].T
    stept = step[0].T
    h_in = saved_states[0, 0].reshape(width, half)
    capacity = slot_rows.shape[2]
    piece = width // n_dp
    part = width // 2
    many = heads // 2
    block = part // n_chip
    unit = min(size, block & -block)
    flip = w_gate.shape[2] % LANES == 0

    def gathered(start):
        own = w_bc[:, start : start + half]
        mine = lax.dynamic_slice(w_bc, (core * (share // 2), start), (share // 2, half))
        mine = [shifted(mine, "dp", s) for s in range(1, n_dp)]
        return [own, *mine, swapped(jnp.stack(mine))]

    w_c = gathered(half)

    cumt, cum, steps, dyt, xt, xs, carried = call(
        prep_kernel,
        [
            shape((heads, length), F32),
            shape((length, LANES), F32),
            shape((length, LANES), F32),
            shape((width, length), BF16),
            shape((width, length), BF16),
            shape((length, width), BF16),
            shape((length, half), F32),
        ],
        2.0,
        (x, dy, ldt, stept, h_in),
    )
    rows_in, rows_grad = call(
        pick_kernel,
        [shape((capacity, width), BF16), shape((n_dp, capacity, piece), BF16)],
        0.5,
        (x, dy, slot_rows[0], slot_counts, slot_gates[0]),
        after=(cumt,),
    )
    wc_whole, c_rows, keep, send = call(
        lambda *refs: project_kernel(n_dp - 1, *refs),
        [
            shape((width, half), BF16),
            shape((length, half), BF16),
            shape((part + up16(2 * many), half), BF16),
            shape((part + up16(2 * many), half), BF16),
        ],
        1.0,
        (x, dyt, cumt, *w_c),
    )
    recv = swapped(send)
    w_b = gathered(0)
    extra = up16(2 * (block // unit))
    pieces = call(
        lambda *refs: combine_kernel(many, size, unit, *refs),
        [shape((block + extra, half), BF16)] * n_chip,
        0.5,
        (keep, recv),
        scratch=[pltpu.VMEM((n_chip, block + extra, half), BF16)],
    )
    pieces = chips(pieces)

    rows_grad = jnp.concatenate(dealt(rows_grad, "dp"), axis=1)
    rows = jnp.concatenate([rows_in, rows_grad], axis=0)
    rows_a = jnp.stack(chips([rows] * n_chip))
    rows_b = swapped(rows_a)
    weighted = expert(rows_a, rows_b, w_gate[0], w_up[0], flip)

    wb_whole, b_rows = call(
        lambda *refs: b_kernel(n_dp - 1, *refs),
        [shape((width, half), BF16), shape((length, half), BF16)],
        0.5,
        (x, *w_b),
    )
    parts = 2
    tiles = width // LANES // parts
    dxs, exs, owns = [], [], []
    mixed = jnp.zeros((length, length), F32)
    for i in range(parts):
        dx, mixed, ex, own = call(
            lambda *refs, i=i: intra_kernel(i * tiles, tiles, *refs),
            [
                shape((length, width // parts), F32),
                shape((length, length), F32),
                shape((heads // parts, length), F32),
                shape((heads // parts, length), F32),
            ],
            3.0,
            (x, dy, b_rows, c_rows, cumt, cum, steps, h_in, mixed),
            scratch=[pltpu.VMEM((heads, length), F32)],
        )
        dxs.append(dx)
        exs.append(ex)
        owns.append(own)
    db, dc = call(
        close_kernel,
        [shape((length, half), F32), shape((length, half), BF16)],
        0.3,
        (mixed, b_rows, c_rows, carried),
    )

    returned = call(
        lambda *refs: scan_kernel(unit, *refs),
        [shape((block, half), BF16)] * n_chip,
        0.5,
        tuple(pieces),
        scratch=[
            pltpu.VMEM((n_chip, block + extra, half), BF16),
            pltpu.VMEM((n_chip, block, half), BF16),
        ],
    )
    returned = chips(returned)
    r_own, r_send = call(
        lambda *refs: carry_kernel(many, size, *refs),
        [shape((part, half), BF16)] * 2,
        0.5,
        (*returned, keep, recv),
        scratch=[pltpu.VMEM((part, half), BF16)],
    )
    r_recv = swapped(r_send)
    columns_in = chips(
        [
            lax.dynamic_index_in_dim(
                xt.reshape(n_chip, width // n_chip, length), ahead(chip, s, n_chip), 0, False
            )
            for s in range(n_chip)
        ]
    )
    d_bc = call(db_kernel, [shape((length, columns), BF16)], 0.3, (xs, r_own, r_recv, db, dc))[0]
    d_bcs = chips([d_bc] * n_chip)
    d_in, d_decay, d_step = call(
        lambda *refs: finish_kernel(parts, *refs),
        [
            shape((length, width), BF16),
            shape((heads, length), F32),
            shape((heads, length), F32),
        ],
        3.0,
        (x, b_rows, cumt, stept, cum, steps, h_in, r_own, r_recv, wb_whole, wc_whole, d_bc,
         *dxs, *exs, *owns),
        scratch=[pltpu.VMEM((width, half), BF16), pltpu.VMEM((heads, half), F32)],
    )
    w_rows = width // (2 * n_chip)
    term, term_send = call(
        lambda *refs: term_kernel(n_chip, *refs),
        [shape((w_rows, columns), F32), shape((w_rows, columns), BF16)],
        0.5,
        (*columns_in, *d_bcs),
        scratch=[pltpu.VMEM((2, w_rows, columns), F32)],
    )
    final = call(
        deal_kernel,
        [shape((w_rows // n_dp, columns), F32)]
        + [shape((w_rows // n_dp, columns), BF16)] * (n_dp - 1),
        0.3,
        (term, swapped(term_send)),
        scratch=[pltpu.VMEM((n_dp, w_rows // n_dp, columns), F32)],
    )
    w_bc_grad = final[0]
    for s in range(1, n_dp):
        w_bc_grad = w_bc_grad + shifted(final[s], "dp", s).astype(F32)

    spread = [weighted] + [shifted(weighted, "dp", s) for s in range(1, n_dp)]
    w_down_grad = call(
        lambda *refs: down_kernel(n_dp, flip, *refs),
        [shape((w_gate.shape[2], piece), BF16)],
        1.0,
        (*spread, rows_a, rows_b),
    )[0]
    return (d_in[None], d_decay.T[None], d_step.T[None], w_bc_grad, w_down_grad[None])


def solution(mesh):
    in_specs = (
        P("dp", "tm", None),
        P("dp", "tm", None),
        P("dp", None),
        P("dp", "tm", None),
        P("dp", "tm", None),
        P("dp", "tm", None, None, None),
        P(None, None, "tm"),
        P(None, None, "tm"),
        P("dp", None, "tm"),
        P("dp", "tm"),
        P("dp", None, "tm"),
    )
    out_specs = (
        P("dp", "tm", None),
        P("dp", "tm", None),
        P("dp", "tm", None),
        P(("tm", "dp"), None),
        P(None, "tm", "dp"),
    )
    return jax.shard_map(
        per_device, mesh=mesh, in_specs=in_specs, out_specs=out_specs, check_vma=False
    )
```

time: 116 us -> 98.7 us (0.85)
  local copies, waits for them, and re-layouts: 13.9 us -> 5.81 us
  matrix products: 7.27 us -> 0 us
  waiting for transfers between devices: 33.3 us -> 28.1 us
  starting transfers between devices: 42 us -> 43.8 us
  Pallas kernels: 16.7 us -> 18.1 us
    all_to_all x3 -> x0, waiting for transfers between devices: 13.5 us -> none  [the longest x1 9.07 us: per_device(): parts = lax.all_to_all(g_local, 'tm', split_axis=0, concat_axis=0)]
    ppermute x29 -> x36, starting transfers between devices: 30.6 us -> 43.8 us  [the longest x30 43.5 us: shifted(): lax.ppermute(array, axis, [(i, (i + shift * stride) % count) for i in ran...]
    all_to_all x3 -> x0, starting transfers between devices: 11.4 us -> none  [the longest x1 4.03 us: per_device(): parts = lax.all_to_all(g_local, 'tm', split_axis=0, concat_axis=0)]
    ppermute x29 -> x36, waiting for transfers between devices: 19.8 us -> 28.1 us  [the longest x30 26.7 us: shifted(): lax.ppermute(array, axis, [(i, (i + shift * stride) % count) for i in ran...]
    dot_general x3 -> x0, matrix products: 7.27 us -> none  [the longest x1 3.32 us: per_device(): gate_h = jnp.dot(rows_in, w_gate[0], preferred_element_type=F32)]
    unnamed x48 -> x32, local copies, waits for them, and re-layouts: 11.3 us -> 4.76 us
    slice x2 -> x1, local copies, waits for them, and re-layouts: 2.48 us -> 0.02 us  [gathered(): own = w_bc[:, start:start + half]]
    pallas_call x7 -> x16, Pallas kernels: 16.7 us -> 18.1 us  [the longest x15 15.6 us: call(): pl.pallas_call(body, out_shape=outs, in_specs=[pl.BlockSpec(memory_space=...]
  transfers between devices with their start and end apart: 32 -> 36, of which waited for: 9 -> 12; matrix products, arithmetic and copies ran while one was open for 10% -> 0% of each run, Pallas kernels for 10% -> 18%
where the time goes in v3:
time: 98.7 us; the launch traced here: 98.3 us
  starting transfers between devices  43.8 us (44%)
  waiting for transfers between devices  28.1 us (28%)
  Pallas kernels  18.1 us (18%)
  local copies, waits for them, and re-layouts  5.81 us (6%)
  between operations  1.68 us (2%)
    ppermute x30, starting transfers between devices, shifted(): lax.ppermute(array, axis, [(i, (i + shift * stride) % count) for i in ran...  43.5 us
    ppermute x30, waiting for transfers between devices, shifted(): lax.ppermute(array, axis, [(i, (i + shift * stride) % count) for i in ran...  26.7 us
    pallas_call x15, Pallas kernels, call(): pl.pallas_call(body, out_shape=outs, in_specs=[pl.BlockSpec(memory_space=...  15.6 us
    unnamed x32, local copies, waits for them, and re-layouts  4.76 us
    pallas_call x1, Pallas kernels, expert(): pl.pallas_call(lambda *refs: expert_kernel(flip, *refs), out_shape=shape(...  2.57 us
  transfers between devices with their start and end apart: 36, of which 12 were waited for; matrix products, arithmetic and copies ran while one was open for 0% of the time, Pallas kernels for 18%

profile of v3, /device:TPU:0, one launch (start us, length us, event | category | flops | bytes accessed | tf_op | source)
XLA Modules:
  0.0 98.3 jit_solution(8821489596177119589)
XLA Ops:
  1.6 3.1 %collective-permute-start = (bf16[320,128]{1,0:T(8,128)(2,1)S(1)}, bf16[320,128]{1,0:T(8,128)(2,1)S(1)}, u32[]{:S(2)}, u32[]{:S(2)}) collective-permute-start(bf16[320,128]{1,0:T(8,128)(2,1)S(1)} %get-tuple-element.98), channel_id=1, source_target_pairs={{0,1},{1,2},{2,3},{3,0},{4,5},{5,6},{6,7},{7,4},{8,9},{9,10},{10,1... | collective-permute-start | bytes 245768 | tf_op jit(solution)/shard_map/ppermute | solution.py:467
  4.7 2.6 %collective-permute-start.1 = (bf16[320,128]{1,0:T(8,128)(2,1)S(1)}, bf16[320,128]{1,0:T(8,128)(2,1)S(1)}, u32[]{:S(2)}, u32[]{:S(2)}) collective-permute-start(bf16[320,128]{1,0:T(8,128)(2,1)S(1)} %get-tuple-element.98), channel_id=1, source_target_pairs={{0,2},{1,3},{2,0},{3,1},{4,6},{5,7},{6,4},{7,5},{8,10},{9,11},{10,... | collective-permute-start | bytes 245768 | tf_op jit(solution)/shard_map/ppermute | solution.py:467
  7.4 1.8 %collective-permute-start.5 = (bf16[320,128]{1,0:T(8,128)(2,1)S(1)}, bf16[320,128]{1,0:T(8,128)(2,1)S(1)}, u32[]{:S(2)}, u32[]{:S(2)}) collective-permute-start(bf16[320,128]{1,0:T(8,128)(2,1)S(1)} %get-tuple-element.97), channel_id=1, source_target_pairs={{0,2},{1,3},{2,0},{3,1},{4,6},{5,7},{6,4},{7,5},{8,10},{9,11},{10,... | collective-permute-start | bytes 245768 | tf_op jit(solution)/shard_map/ppermute | solution.py:467
  9.2 1.9 %collective-permute-start.6 = (bf16[320,128]{1,0:T(8,128)(2,1)S(1)}, bf16[320,128]{1,0:T(8,128)(2,1)S(1)}, u32[]{:S(2)}, u32[]{:S(2)}) collective-permute-start(bf16[320,128]{1,0:T(8,128)(2,1)S(1)} %get-tuple-element.97), channel_id=1, source_target_pairs={{0,3},{1,0},{2,1},{3,2},{4,7},{5,4},{6,5},{7,6},{8,11},{9,8},{10,9... | collective-permute-start | bytes 245768 | tf_op jit(solution)/shard_map/ppermute | solution.py:467
  16.5 1.9 %shard_map.147 = (f32[40,128]{1,0:T(8,128)S(1)}, f32[128,128]{1,0:T(8,128)S(1)}, f32[128,128]{1,0:T(8,128)S(1)}, bf16[2560,128]{1,0:T(8,128)(2,1)S(1)}, bf16[256...) custom-call(bf16[128,2560]{1,0:T(8,128)(2,1)S(1)} %bitcast.66, ...), custom_call_target="tpu_custom_call" | custom-call | flops 2000000000 | bytes 1000 | tf_op jit(solution)/shard_map/pallas_call | solution.py:60
  22.6 1.9 %collective-permute-start.26 = (bf16[16,640]{1,0:T(8,128)(2,1)S(1)}, bf16[16,640]{1,0:T(8,128)(2,1)S(1)}, u32[]{:S(2)}, u32[]{:S(2)}) collective-permute-start(bf16[16,640]{1,0:T(8,128)(2,1)S(1)} %get-tuple-element.104), channel_id=1, source_target_pairs={{0,1},{1,2},{2,3},{3,0},{4,5},{5,6},{6,7},{7,4},{8,9},{9,10},{10,1... | collective-permute-start | bytes 61448 | tf_op jit(solution)/shard_map/ppermute | solution.py:467
  25.2 1.9 %collective-permute-start.2 = (bf16[320,128]{1,0:T(8,128)(2,1)S(1)}, bf16[320,128]{1,0:T(8,128)(2,1)S(1)}, u32[]{:S(2)}, u32[]{:S(2)}) collective-permute-start(bf16[320,128]{1,0:T(8,128)(2,1)S(1)} %get-tuple-element.98), channel_id=1, source_target_pairs={{0,3},{1,0},{2,1},{3,2},{4,7},{5,4},{6,5},{7,6},{8,11},{9,8},{10,9... | collective-permute-start | bytes 245768 | tf_op jit(solution)/shard_map/ppermute | solution.py:467
  28.3 2.5 %collective-permute-start.31 = (bf16[32,2560]{1,0:T(8,128)(2,1)S(1)}, bf16[32,2560]{1,0:T(8,128)(2,1)S(1)}, u32[]{:S(2)}, u32[]{:S(2)}) collective-permute-start(bf16[32,2560]{1,0:T(8,128)(2,1)S(1)} %maximum_maximum_fusion), channel_id=1, source_target_pairs={{0,24},{4,28},{8,0},{12,4},{16,8},{20,12},{24,16},{28,20},{1,25},{... | collective-permute-start | bytes 491528 | tf_op jit(solution)/shard_map/ppermute | solution.py:467
  32.3 2.4 %collective-permute-start.29 = (bf16[32,2560]{1,0:T(8,128)(2,1)S(1)}, bf16[32,2560]{1,0:T(8,128)(2,1)S(1)}, u32[]{:S(2)}, u32[]{:S(2)}) collective-permute-start(bf16[32,2560]{1,0:T(8,128)(2,1)S(1)} %maximum_maximum_fusion), channel_id=1, source_target_pairs={{0,8},{4,12},{8,16},{12,20},{16,24},{20,28},{24,0},{28,4},{1,9},{5... | collective-permute-start | bytes 491528 | tf_op jit(solution)/shard_map/ppermute | solution.py:467
  35.2 2.7 %collective-permute-done.9.refs_1_ = bf16[336,128]{1,0:T(8,128)(2,1)S(1)} collective-permute-done((bf16[336,128]{1,0:T(8,128)(2,1)S(1)}, bf16[336,128]{1,0:T(8,128)(2,1)S(1)}, u32[]{:S(2)}, u32[]{:S(2)}) %collective-permute-start.9) | collective-permute-done | bytes 86048 | tf_op jit(solution)/shard_map/ppermute | solution.py:467
  37.8 1.9 %collective-permute-start.11 = (bf16[336,128]{1,0:T(8,128)(2,1)S(1)}, bf16[336,128]{1,0:T(8,128)(2,1)S(1)}, u32[]{:S(2)}, u32[]{:S(2)}) collective-permute-start(bf16[336,128]{1,0:T(8,128)(2,1)S(1)} %get-tuple-element.59), channel_id=1, source_target_pairs={{0,24},{4,28},{8,0},{12,4},{16,8},{20,12},{24,16},{28,20},{1,25},{... | collective-permute-start | bytes 258056 | tf_op jit(solution)/shard_map/ppermute | solution.py:467
  39.8 4.0 %collective-permute-done.10.refs_2_ = bf16[336,128]{1,0:T(8,128)(2,1)S(1)} collective-permute-done((bf16[336,128]{1,0:T(8,128)(2,1)S(1)}, bf16[336,128]{1,0:T(8,128)(2,1)S(1)}, u32[]{:S(2)}, u32[]{:S(2)}) %collective-permute-start.10) | collective-permute-done | bytes 86048 | tf_op jit(solution)/shard_map/ppermute | solution.py:467
  44.0 2.8 %collective-permute-start.12 = (bf16[320,128]{1,0:T(8,128)(2,1)S(1)}, bf16[320,128]{1,0:T(8,128)(2,1)S(1)}, u32[]{:S(2)}, u32[]{:S(2)}) collective-permute-start(bf16[320,128]{1,0:T(8,128)(2,1)S(1)} %get-tuple-element.61), channel_id=1, source_target_pairs={{0,8},{4,12},{8,16},{12,20},{16,24},{20,28},{24,0},{28,4},{1,9},{5... | collective-permute-start | bytes 245768 | tf_op jit(solution)/shard_map/ppermute | solution.py:467
  49.6 3.1 %collective-permute-done.12.refs_1_ = bf16[320,128]{1,0:T(8,128)(2,1)S(1)} collective-permute-done((bf16[320,128]{1,0:T(8,128)(2,1)S(1)}, bf16[320,128]{1,0:T(8,128)(2,1)S(1)}, u32[]{:S(2)}, u32[]{:S(2)}) %collective-permute-start.12) | collective-permute-done | bytes 81952 | tf_op jit(solution)/shard_map/ppermute | solution.py:467
  54.8 2.6 %shard_map.152 = (f32[128,1280]{1,0:T(8,128)S(1)}, f32[128,128]{1,0:T(8,128)S(1)}, f32[20,128]{1,0:T(8,128)S(1)}, f32[20,128]{1,0:T(8,128)S(1)}) custom-call(bf16[128,2560]{1,0:T(8,128)(2,1)S(1)} %bitcast.70, bf16[128,2560]{1,0:T(8,128)(2,1)S(1)} %bitcast.64, bf16[128,128]{1,0:T(8,128)(2,1)S(1)} %get-tuple-element.49.refs_2_.refs_1_, ...), custom_call_target="tpu_custom_call" | custom-call | flops 3000000000 | bytes 1000 | tf_op jit(solution)/shard_map/pallas_call | solution.py:60
  57.4 2.6 %shard_map.153 = (f32[128,1280]{1,0:T(8,128)S(1)}, f32[128,128]{1,0:T(8,128)S(1)}, f32[20,128]{1,0:T(8,128)S(1)}, f32[20,128]{1,0:T(8,128)S(1)}) custom-call(bf16[128,2560]{1,0:T(8,128)(2,1)S(1)} %bitcast.71, bf16[128,2560]{1,0:T(8,128)(2,1)S(1)} %bitcast.65, bf16[128,128]{1,0:T(8,128)(2,1)S(1)} %get-tuple-element.49.refs_2_.refs_1_, ...), custom_call_target="tpu_custom_call" | custom-call | flops 3000000000 | bytes 1000 | tf_op jit(solution)/shard_map/pallas_call | solution.py:60
  61.4 2.6 %shard_map.160.refs_0_ = bf16[896,128]{1,0:T(8,128)(2,1)S(1)} custom-call(bf16[4,32,2560]{2,1,0:T(8,128)(2,1)S(1)} %pad_maximum_fusion.refs_0_.refs_4_, bf16[4,32,2560]{2,1,0:T(8,128)(2,1)S(1)} %collective-permute-done.32.refs_1_.refs_5_, bf16[2560,896]{1,0:T(8,128)(2,1)S(1)} %bitcast.51, bf16[2560,896]{1,0:T(8,128)(2,1)S(1)} %bitcast.54), custom_call_target="tpu_custom_call" | custom-call | flops 1174405120 | bytes 9175040 | tf_op jit(solution)/shard_map/pallas_call | solution.py:428
  65.1 3.0 %collective-permute-start.35 = (bf16[896,128]{1,0:T(8,128)(2,1)S(1)}, bf16[896,128]{1,0:T(8,128)(2,1)S(1)}, u32[]{:S(2)}, u32[]{:S(2)}) collective-permute-start(bf16[896,128]{1,0:T(8,128)(2,1)S(1)} %shard_map.160.refs_0_), channel_id=1, source_target_pairs={{0,3},{1,0},{2,1},{3,2},{4,7},{5,4},{6,5},{7,6},{8,11},{9,8},{10,9... | collective-permute-start | bytes 688136 | tf_op jit(solution)/shard_map/ppermute | solution.py:467
  74.7 8.7 %collective-permute-done.34.refs_2_ = bf16[896,128]{1,0:T(8,128)(2,1)S(1)} collective-permute-done((bf16[896,128]{1,0:T(8,128)(2,1)S(1)}, bf16[896,128]{1,0:T(8,128)(2,1)S(1)}, u32[]{:S(2)}, u32[]{:S(2)}) %collective-permute-start.34) | collective-permute-done | bytes 229408 | tf_op jit(solution)/shard_map/ppermute | solution.py:467
  83.4 2.3 %shard_map.161 = bf16[896,640]{1,0:T(8,128)(2,1)} custom-call(bf16[896,128]{1,0:T(8,128)(2,1)S(1)} %shard_map.160.refs_0_, bf16[896,128]{1,0:T(8,128)(2,1)S(1)} %collective-permute-done.33.refs_1_, bf16[896,128]{1,0:T(8,128)(2,1)S(1)} %collective-permute-done.34.refs_2_, bf16[896,128]{1,0:T(8,128)(2,1)S(1)} %collective-permute-done.35.refs_3_, ...), custom_call_target="tpu_custom_call" | custom-call | flops 1000000000 | bytes 1000 | tf_op jit(solution)/shard_map/pallas_call | solution.py:60
  85.8 4.0 %collective-permute-start.25 = (bf16[80,256]{1,0:T(8,128)(2,1)S(1)}, bf16[80,256]{1,0:T(8,128)(2,1)S(1)}, u32[]{:S(2)}, u32[]{:S(2)}) collective-permute-start(bf16[80,256]{1,0:T(8,128)(2,1)S(1)} %get-tuple-element.90), channel_id=1, source_target_pairs={{0,3},{1,0},{2,1},{3,2},{4,7},{5,4},{6,5},{7,6},{8,11},{9,8},{10,9... | collective-permute-start | bytes 122888 | tf_op jit(solution)/shard_map/ppermute | solution.py:467
  89.8 2.1 %collective-permute-start.24 = (bf16[80,256]{1,0:T(8,128)(2,1)S(1)}, bf16[80,256]{1,0:T(8,128)(2,1)S(1)}, u32[]{:S(2)}, u32[]{:S(2)}) collective-permute-start(bf16[80,256]{1,0:T(8,128)(2,1)S(1)} %get-tuple-element.89), channel_id=1, source_target_pairs={{0,2},{1,3},{2,0},{3,1},{4,6},{5,7},{6,4},{7,5},{8,10},{9,11},{10,... | collective-permute-start | bytes 122888 | tf_op jit(solution)/shard_map/ppermute | solution.py:467
  91.9 3.1 %shard_map.156 = (bf16[128,2560]{1,0:T(8,128)(2,1)}, f32[40,128]{1,0:T(8,128)}, f32[40,128]{1,0:T(8,128)}) custom-call(bf16[128,2560]{1,0:T(8,128)(2,1)S(1)} %bitcast.72, bf16[128,128]{1,0:T(8,128)(2,1)S(1)} %get-tuple-element.49.refs_2_.refs_1_, f32[40,128]{1,0:T(8,128)S(1)} %get-tuple-element.50.refs_2_.refs_4_.refs_5_, f32[40,128]{1,0:T(8,128)S(1)} %bitcast.79, ...), custom_call_target="tpu_custom_call" | custom-call | flops 3000000000 | bytes 1000 | tf_op jit(solution)/shard_map/pallas_call | solution.py:60
  95.5 2.1 %collective-permute-done.23 = bf16[80,256]{1,0:T(8,128)(2,1)S(1)} collective-permute-done((bf16[80,256]{1,0:T(8,128)(2,1)S(1)}, bf16[80,256]{1,0:T(8,128)(2,1)S(1)}, u32[]{:S(2)}, u32[]{:S(2)}) %collective-permute-start.23) | collective-permute-done | bytes 40992 | tf_op jit(solution)/shard_map/ppermute | solution.py:467
  (109 shorter events, 29.0 us)
Async XLA Ops:
  1.6 29.5 %collective-permute-start = (bf16[320,128]{1,0:T(8,128)(2,1)S(1)}, bf16[320,128]{1,0:T(8,128)(2,1)S(1)}, u32[]{:S(2)}, u32[]{:S(2)}) collective-permute-start(bf16[320,128]{1,0:T(8,128)(2,1)S(1)} %get-tuple-element.98), channel_id=1, source_target_pairs={{0,1},{1,2},{2,3},{3,0},{4,5},{5,6},{6,7},{7,4},{8,9},{9,10},{10,1... | collective-permute-start | bytes 245768 | tf_op jit(solution)/shard_map/ppermute | solution.py:467
  4.7 27.6 %collective-permute-start.1 = (bf16[320,128]{1,0:T(8,128)(2,1)S(1)}, bf16[320,128]{1,0:T(8,128)(2,1)S(1)}, u32[]{:S(2)}, u32[]{:S(2)}) collective-permute-start(bf16[320,128]{1,0:T(8,128)(2,1)S(1)} %get-tuple-element.98), channel_id=1, source_target_pairs={{0,2},{1,3},{2,0},{3,1},{4,6},{5,7},{6,4},{7,5},{8,10},{9,11},{10,... | collective-permute-start | bytes 245768 | tf_op jit(solution)/shard_map/ppermute | solution.py:467
  7.3 11.5 %collective-permute-start.4 = (bf16[320,128]{1,0:T(8,128)(2,1)S(1)}, bf16[320,128]{1,0:T(8,128)(2,1)S(1)}, u32[]{:S(2)}, u32[]{:S(2)}) collective-permute-start(bf16[320,128]{1,0:T(8,128)(2,1)S(1)} %get-tuple-element.97), channel_id=1, source_target_pairs={{0,1},{1,2},{2,3},{3,0},{4,5},{5,6},{6,7},{7,4},{8,9},{9,10},{10,1... | collective-permute-start | bytes 245768 | tf_op jit(solution)/shard_map/ppermute | solution.py:467
  7.4 12.1 %collective-permute-start.5 = (bf16[320,128]{1,0:T(8,128)(2,1)S(1)}, bf16[320,128]{1,0:T(8,128)(2,1)S(1)}, u32[]{:S(2)}, u32[]{:S(2)}) collective-permute-start(bf16[320,128]{1,0:T(8,128)(2,1)S(1)} %get-tuple-element.97), channel_id=1, source_target_pairs={{0,2},{1,3},{2,0},{3,1},{4,6},{5,7},{6,4},{7,5},{8,10},{9,11},{10,... | collective-permute-start | bytes 245768 | tf_op jit(solution)/shard_map/ppermute | solution.py:467
  9.2 11.8 %collective-permute-start.6 = (bf16[320,128]{1,0:T(8,128)(2,1)S(1)}, bf16[320,128]{1,0:T(8,128)(2,1)S(1)}, u32[]{:S(2)}, u32[]{:S(2)}) collective-permute-start(bf16[320,128]{1,0:T(8,128)(2,1)S(1)} %get-tuple-element.97), channel_id=1, source_target_pairs={{0,3},{1,0},{2,1},{3,2},{4,7},{5,4},{6,5},{7,6},{8,11},{9,8},{10,9... | collective-permute-start | bytes 245768 | tf_op jit(solution)/shard_map/ppermute | solution.py:467
  19.5 7.7 %collective-permute-start.27 = (bf16[16,640]{1,0:T(8,128)(2,1)S(1)}, bf16[16,640]{1,0:T(8,128)(2,1)S(1)}, u32[]{:S(2)}, u32[]{:S(2)}) collective-permute-start(bf16[16,640]{1,0:T(8,128)(2,1)S(1)} %get-tuple-element.103), channel_id=1, source_target_pairs={{0,2},{1,3},{2,0},{3,1},{4,6},{5,7},{6,4},{7,5},{8,10},{9,11},{10,... | collective-permute-start | bytes 61448 | tf_op jit(solution)/shard_map/ppermute | solution.py:467
  25.2 9.4 %collective-permute-start.2 = (bf16[320,128]{1,0:T(8,128)(2,1)S(1)}, bf16[320,128]{1,0:T(8,128)(2,1)S(1)}, u32[]{:S(2)}, u32[]{:S(2)}) collective-permute-start(bf16[320,128]{1,0:T(8,128)(2,1)S(1)} %get-tuple-element.98), channel_id=1, source_target_pairs={{0,3},{1,0},{2,1},{3,2},{4,7},{5,4},{6,5},{7,6},{8,11},{9,8},{10,9... | collective-permute-start | bytes 245768 | tf_op jit(solution)/shard_map/ppermute | solution.py:467
  28.3 15.7 %collective-permute-start.31 = (bf16[32,2560]{1,0:T(8,128)(2,1)S(1)}, bf16[32,2560]{1,0:T(8,128)(2,1)S(1)}, u32[]{:S(2)}, u32[]{:S(2)}) collective-permute-start(bf16[32,2560]{1,0:T(8,128)(2,1)S(1)} %maximum_maximum_fusion), channel_id=1, source_target_pairs={{0,24},{4,28},{8,0},{12,4},{16,8},{20,12},{24,16},{28,20},{1,25},{... | collective-permute-start | bytes 491528 | tf_op jit(solution)/shard_map/ppermute | solution.py:467
  31.0 6.8 %collective-permute-start.9 = (bf16[336,128]{1,0:T(8,128)(2,1)S(1)}, bf16[336,128]{1,0:T(8,128)(2,1)S(1)}, u32[]{:S(2)}, u32[]{:S(2)}) collective-permute-start(bf16[336,128]{1,0:T(8,128)(2,1)S(1)} %get-tuple-element.57), channel_id=1, source_target_pairs={{0,8},{4,12},{8,16},{12,20},{16,24},{20,28},{24,0},{28,4},{1,9},{5... | collective-permute-start | bytes 258056 | tf_op jit(solution)/shard_map/ppermute | solution.py:467
  31.1 15.7 %collective-permute-start.30 = (bf16[32,2560]{1,0:T(8,128)(2,1)S(1)}, bf16[32,2560]{1,0:T(8,128)(2,1)S(1)}, u32[]{:S(2)}, u32[]{:S(2)}) collective-permute-start(bf16[32,2560]{1,0:T(8,128)(2,1)S(1)} %maximum_maximum_fusion), channel_id=1, source_target_pairs={{0,16},{4,20},{8,24},{12,28},{16,0},{20,4},{24,8},{28,12},{1,17},{... | collective-permute-start | bytes 491528 | tf_op jit(solution)/shard_map/ppermute | solution.py:467
  32.3 15.2 %collective-permute-start.29 = (bf16[32,2560]{1,0:T(8,128)(2,1)S(1)}, bf16[32,2560]{1,0:T(8,128)(2,1)S(1)}, u32[]{:S(2)}, u32[]{:S(2)}) collective-permute-start(bf16[32,2560]{1,0:T(8,128)(2,1)S(1)} %maximum_maximum_fusion), channel_id=1, source_target_pairs={{0,8},{4,12},{8,16},{12,20},{16,24},{20,28},{24,0},{28,4},{1,9},{5... | collective-permute-start | bytes 491528 | tf_op jit(solution)/shard_map/ppermute | solution.py:467
  34.6 9.1 %collective-permute-start.10 = (bf16[336,128]{1,0:T(8,128)(2,1)S(1)}, bf16[336,128]{1,0:T(8,128)(2,1)S(1)}, u32[]{:S(2)}, u32[]{:S(2)}) collective-permute-start(bf16[336,128]{1,0:T(8,128)(2,1)S(1)} %get-tuple-element.58), channel_id=1, source_target_pairs={{0,16},{4,20},{8,24},{12,28},{16,0},{20,4},{24,8},{28,12},{1,17},{... | collective-permute-start | bytes 258056 | tf_op jit(solution)/shard_map/ppermute | solution.py:467
  43.8 20.4 %collective-permute-start.16 = (bf16[640,128]{1,0:T(8,128)(2,1)S(1)}, bf16[640,128]{1,0:T(8,128)(2,1)S(1)}, u32[]{:S(2)}, u32[]{:S(2)}) collective-permute-start(bf16[640,128]{1,0:T(8,128)(2,1)S(1)} %get-tuple-element.95), channel_id=1, source_target_pairs={{0,8},{4,12},{8,16},{12,20},{16,24},{20,28},{24,0},{28,4},{1,9},{5... | collective-permute-start | bytes 491528 | tf_op jit(solution)/shard_map/ppermute | solution.py:467
  44.0 8.7 %collective-permute-start.12 = (bf16[320,128]{1,0:T(8,128)(2,1)S(1)}, bf16[320,128]{1,0:T(8,128)(2,1)S(1)}, u32[]{:S(2)}, u32[]{:S(2)}) collective-permute-start(bf16[320,128]{1,0:T(8,128)(2,1)S(1)} %get-tuple-element.61), channel_id=1, source_target_pairs={{0,8},{4,12},{8,16},{12,20},{16,24},{20,28},{24,0},{28,4},{1,9},{5... | collective-permute-start | bytes 245768 | tf_op jit(solution)/shard_map/ppermute | solution.py:467
  47.5 7.0 %collective-permute-start.14 = (bf16[320,128]{1,0:T(8,128)(2,1)S(1)}, bf16[320,128]{1,0:T(8,128)(2,1)S(1)}, u32[]{:S(2)}, u32[]{:S(2)}) collective-permute-start(bf16[320,128]{1,0:T(8,128)(2,1)S(1)} %get-tuple-element.63), channel_id=1, source_target_pairs={{0,24},{4,28},{8,0},{12,4},{16,8},{20,12},{24,16},{28,20},{1,25},{... | collective-permute-start | bytes 245768 | tf_op jit(solution)/shard_map/ppermute | solution.py:467
  48.4 16.6 %collective-permute-start.17 = (bf16[640,128]{1,0:T(8,128)(2,1)S(1)}, bf16[640,128]{1,0:T(8,128)(2,1)S(1)}, u32[]{:S(2)}, u32[]{:S(2)}) collective-permute-start(bf16[640,128]{1,0:T(8,128)(2,1)S(1)} %get-tuple-element.94), channel_id=1, source_target_pairs={{0,16},{4,20},{8,24},{12,28},{16,0},{20,4},{24,8},{28,12},{1,17},{... | collective-permute-start | bytes 491528 | tf_op jit(solution)/shard_map/ppermute | solution.py:467
  52.6 15.4 %collective-permute-start.18 = (bf16[640,128]{1,0:T(8,128)(2,1)S(1)}, bf16[640,128]{1,0:T(8,128)(2,1)S(1)}, u32[]{:S(2)}, u32[]{:S(2)}) collective-permute-start(bf16[640,128]{1,0:T(8,128)(2,1)S(1)} %get-tuple-element.93), channel_id=1, source_target_pairs={{0,24},{4,28},{8,0},{12,4},{16,8},{20,12},{24,16},{28,20},{1,25},{... | collective-permute-start | bytes 491528 | tf_op jit(solution)/shard_map/ppermute | solution.py:467
  53.6 7.7 %collective-permute-start.32 = (bf16[4,32,2560]{2,1,0:T(8,128)(2,1)S(1)}, bf16[4,32,2560]{2,1,0:T(8,128)(2,1)S(1)}, u32[]{:S(2)}, u32[]{:S(2)}) collective-permute-start(bf16[4,32,2560]{2,1,0:T(8,128)(2,1)S(1)} %pad_maximum_fusion.refs_0_.refs_4_), channel_id=1, source_target_pairs={{0,4},{4,0},{8,12},{12,8},{16,20},{20,16},{24,28},{28,24},{1,5},{5... | collective-permute-start | bytes 1966088 | tf_op jit(solution)/shard_map/ppermute | solution.py:471
  60.6 9.2 %collective-permute-start.19 = (bf16[128,256]{1,0:T(8,128)(2,1)S(1)}, bf16[128,256]{1,0:T(8,128)(2,1)S(1)}, u32[]{:S(2)}, u32[]{:S(2)}) collective-permute-start(bf16[128,256]{1,0:T(8,128)(2,1)S(1)} %shard_map.155.refs_11_.refs_4_), channel_id=1, source_target_pairs={{0,8},{4,12},{8,16},{12,20},{16,24},{20,28},{24,0},{28,4},{1,9},{5... | collective-permute-start | bytes 196616 | tf_op jit(solution)/shard_map/ppermute | solution.py:467
  64.0 10.7 %collective-permute-start.33 = (bf16[896,128]{1,0:T(8,128)(2,1)S(1)}, bf16[896,128]{1,0:T(8,128)(2,1)S(1)}, u32[]{:S(2)}, u32[]{:S(2)}) collective-permute-start(bf16[896,128]{1,0:T(8,128)(2,1)S(1)} %shard_map.160.refs_0_), channel_id=1, source_target_pairs={{0,1},{1,2},{2,3},{3,0},{4,5},{5,6},{6,7},{7,4},{8,9},{9,10},{10,1... | collective-permute-start | bytes 688136 | tf_op jit(solution)/shard_map/ppermute | solution.py:467
  64.2 19.2 %collective-permute-start.34 = (bf16[896,128]{1,0:T(8,128)(2,1)S(1)}, bf16[896,128]{1,0:T(8,128)(2,1)S(1)}, u32[]{:S(2)}, u32[]{:S(2)}) collective-permute-start(bf16[896,128]{1,0:T(8,128)(2,1)S(1)} %shard_map.160.refs_0_), channel_id=1, source_target_pairs={{0,2},{1,3},{2,0},{3,1},{4,6},{5,7},{6,4},{7,5},{8,10},{9,11},{10,... | collective-permute-start | bytes 688136 | tf_op jit(solution)/shard_map/ppermute | solution.py:467
  65.1 18.3 %collective-permute-start.35 = (bf16[896,128]{1,0:T(8,128)(2,1)S(1)}, bf16[896,128]{1,0:T(8,128)(2,1)S(1)}, u32[]{:S(2)}, u32[]{:S(2)}) collective-permute-start(bf16[896,128]{1,0:T(8,128)(2,1)S(1)} %shard_map.160.refs_0_), channel_id=1, source_target_pairs={{0,3},{1,0},{2,1},{3,2},{4,7},{5,4},{6,5},{7,6},{8,11},{9,8},{10,9... | collective-permute-start | bytes 688136 | tf_op jit(solution)/shard_map/ppermute | solution.py:467
  74.6 11.1 %collective-permute-start.22 = (bf16[320,256]{1,0:T(8,128)(2,1)S(1)}, bf16[320,256]{1,0:T(8,128)(2,1)S(1)}, u32[]{:S(2)}, u32[]{:S(2)}) collective-permute-start(bf16[320,256]{1,0:T(8,128)(2,1)S(1)} %get-tuple-element.86), channel_id=1, source_target_pairs={{0,4},{4,0},{8,12},{12,8},{16,20},{20,16},{24,28},{28,24},{1,5},{5... | collective-permute-start | bytes 491528 | tf_op jit(solution)/shard_map/ppermute | solution.py:471
  85.8 9.2 %collective-permute-start.25 = (bf16[80,256]{1,0:T(8,128)(2,1)S(1)}, bf16[80,256]{1,0:T(8,128)(2,1)S(1)}, u32[]{:S(2)}, u32[]{:S(2)}) collective-permute-start(bf16[80,256]{1,0:T(8,128)(2,1)S(1)} %get-tuple-element.90), channel_id=1, source_target_pairs={{0,3},{1,0},{2,1},{3,2},{4,7},{5,4},{6,5},{7,6},{8,11},{9,8},{10,9... | collective-permute-start | bytes 122888 | tf_op jit(solution)/shard_map/ppermute | solution.py:467
  (28 other events, 221.6 us)

commit v4 on v3

--- a/solution.py
+++ b/solution.py
@@ -51,19 +51,39 @@
     return -(-n // 16) * 16
 
 
-def call(kernel, outs, cost, args, after=(), scratch=(), limit=14):
-    n_in, n_after = len(args), len(after)
+def call(kernel, outs, cost, args, after=(), scratch=(), limit=14, fetch=()):
+    n_in, n_after, n_out = len(args), len(after), len(outs)
+    fetch = tuple(fetch)
 
     def body(*refs):
-        kernel(*refs[:n_in], *refs[n_in + n_after :])
-
+        ins = list(refs[:n_in])
+        rest = refs[n_in + n_after :]
+        if fetch:
+            sems = rest[-1]
+            held = rest[len(rest) - 1 - len(fetch) : -1]
+            rest = rest[: len(rest) - 1 - len(fetch)]
+            copies = []
+            for i, (index, ref) in enumerate(zip(fetch, held)):
+                copies.append(pltpu.make_async_copy(ins[index], ref, sems.at[i]))
+                ins[index] = ref
+            for copy in copies:
+                copy.start()
+            for copy in copies:
+                copy.wait()
+        kernel(*ins, *rest)
+
+    specs = [
+        pl.BlockSpec(memory_space=pltpu.HBM if i in fetch else pltpu.VMEM) for i in range(n_in)
+    ]
+    held = [pltpu.VMEM(args[i].shape, args[i].dtype) for i in fetch]
+    if fetch:
+        held.append(pltpu.SemaphoreType.DMA((len(fetch),)))
     return pl.pallas_call(
         body,
         out_shape=outs,
-        in_specs=[pl.BlockSpec(memory_space=pltpu.VMEM)] * n_in
-        + [pl.BlockSpec(memory_space=pl.ANY)] * n_after,
-        out_specs=[pl.BlockSpec(memory_space=pltpu.VMEM)] * len(outs),
-        scratch_shapes=list(scratch),
+        in_specs=specs + [pl.BlockSpec(memory_space=pl.ANY)] * n_after,
+        out_specs=[pl.BlockSpec(memory_space=pltpu.VMEM)] * n_out,
+        scratch_shapes=list(scratch) + held,
         cost_estimate=pl.CostEstimate(
             flops=int(cost * 1e9), bytes_accessed=1000, transcendentals=0
         ),
@@ -90,8 +110,9 @@
 
 def prep_kernel(
     x_ref, dy_ref, ldt_ref, stept_ref, h_ref,
-    cumt_ref, cum_ref, step_ref, dyt_ref, xt_ref, xs_ref, carried_ref,
+    cumt_ref, cum_ref, step_ref, dyt_ref, xs_ref, carried_ref, *rest,
 ):
+    outs, xt_ref = rest[:-1], rest[-1]
     length, width = x_ref.shape
     heads = ldt_ref.shape[0]
     size = width // heads
@@ -116,41 +137,54 @@
         dyt_ref[span, :] = dys.T.astype(BF16)
         carried = carried + dot(dys.astype(BF16), h_ref[span, :], 1, 0)
     carried_ref[...] = carried
-
-
-def pick_kernel(x_ref, dy_ref, rows_ref, count_ref, gate_ref, in_ref, grad_ref):
-    length = x_ref.shape[0]
-    slots = rows_ref.shape[1]
-    hit = iota((length, slots), 0) == rows_ref[...]
-    live = iota((1, slots), 1) < count_ref[...]
-    weight = jnp.where(live, gate_ref[...].astype(F32), 0.0)
-    pick = where_one(hit).astype(BF16)
-    scaled = jnp.where(hit, weight, 0.0).astype(BF16)
-    in_ref[...] = dot(pick, x_ref[...], 0, 0).astype(BF16)
-    grads = dot(scaled, dy_ref[...], 0, 0).astype(BF16)
-    piece = grad_ref.shape[2]
-    for i in range(grad_ref.shape[0]):
-        grad_ref[i] = grads[:, i * piece : (i + 1) * piece]
-
-
-def assemble(w_ref, own_ref, mine_refs, other_ref):
+    _, chip, n_chip = core_and_chip()
+    for s, out in enumerate(outs):
+        out[...] = xt_ref[rows_at(ahead(chip, s, n_chip), width // n_chip), :]
+
+
+def first_kernel(start, x_ref, dy_ref, pick_ref, w_ref, in_ref, own_ref, *rest):
+    outs, held = rest[:-1], rest[-1]
+    slots = pick_ref.shape[0] // 2
+    width = x_ref.shape[1]
+    rows = dot(pick_ref[:slots], x_ref[...], 1, 0).astype(BF16)
+    for t in range(width // LANES):
+        in_ref[t * slots : (t + 1) * slots, :] = rows[:, t * LANES : (t + 1) * LANES]
+    grads = dot(pick_ref[slots:], dy_ref[...], 1, 0).astype(BF16)
+    n_dp = held.shape[0]
+    piece = width // n_dp
+    held[...] = jnp.zeros_like(held)
+    for i in range(n_dp):
+        for t in range(held.shape[1] // slots):
+            low, high = i * piece + t * LANES, min((i + 1) * piece, i * piece + (t + 1) * LANES)
+            held[i, t * slots : (t + 1) * slots, : high - low] = grads[:, low:high]
+    place = lax.axis_index("dp")
+    core, _, _ = core_and_chip()
+    own_ref[...] = held[place]
+    half = w_ref.shape[0] // 2
+    for s, out in enumerate(outs):
+        out[:half, :] = w_ref[rows_at(core, half), start : start + LANES]
+        out[half:, :] = held[ahead(place, s + 1, n_dp)]
+
+
+def assemble(start, w_ref, own_ref, mine_refs, other_ref):
     core, _, _ = core_and_chip()
     place, n_dp = lax.axis_index("dp"), lax.axis_size("dp")
     share = own_ref.shape[0]
     half = share // 2
-    w_ref[rows_at(place, share), :] = own_ref[...]
+    w_ref[rows_at(place, share), :] = own_ref[:, start : start + LANES]
     for i, mine in enumerate(mine_refs):
         source = ahead(place, n_dp - 1 - i, n_dp)
-        w_ref[rows_at(source * 2 + core, half), :] = mine[...]
+        w_ref[rows_at(source * 2 + core, half), :] = mine[:half, :]
         w_ref[rows_at(source * 2 + 1 - core, half), :] = other_ref[i]
 
 
 def project_kernel(n_mine, *refs):
     x_ref, dyt_ref, cumt_ref, own_ref = refs[:4]
     mine, other = refs[4 : 4 + n_mine], refs[4 + n_mine]
-    w_ref, c_ref, keep_ref, send_ref = refs[5 + n_mine :]
+    w_ref, c_ref, keep_ref, send_ref, b_ref = refs[5 + n_mine :]
     core, _, _ = core_and_chip()
-    assemble(w_ref, own_ref, mine, other)
+    assemble(LANES, w_ref, own_ref, mine, other)
+    b_ref[...] = own_ref[rows_at(core, b_ref.shape[0]), :LANES]
     c_rows = dot(x_ref[...], w_ref[...], 1, 0).astype(BF16)
     c_ref[...] = c_rows
     heads, length = cumt_ref.shape
@@ -179,64 +213,66 @@
     return first, second
 
 
-def combine_kernel(many, size, unit, *refs):
-    keep_ref, recv_ref = refs[:2]
-    outs, held = refs[2:-1], refs[-1]
-    _, chip, n_chip = core_and_chip()
-    block = many * size // n_chip
-    units = block // unit
-    decays = []
+def payload(ref, many, states, decays):
+    size = states[0].shape[0]
+    for head, state in enumerate(states):
+        ref[head * size : (head + 1) * size, :] = state.astype(BF16)
+    decay = jnp.concatenate(decays, axis=0)
+    high = decay.astype(BF16).astype(F32)
+    fill = jnp.zeros((ref.shape[0] - many * size - 2 * many, LANES), F32)
+    extra = jnp.concatenate([high, decay - high, fill], axis=0)
+    ref[many * size :, :] = extra.astype(BF16)
+
+
+def loaded(ref, many, size, head):
+    extra = ref[many * size :, :].astype(F32)
+    decay = extra[head : head + 1] + extra[many + head : many + head + 1]
+    return ref[head * size : (head + 1) * size, :].astype(F32), decay
+
+
+def combine_kernel(many, size, keep_ref, recv_ref, out_ref):
+    states, decays = [], []
     for head in range(many):
         (g0, a0), (g1, a1) = pair(keep_ref, recv_ref, many, size, head)
-        state = (g0 + a0 * g1).astype(BF16)
-        for i in range(size // unit):
-            row = head * size + i * unit
-            held[row // block, row % block : row % block + unit, :] = state[
-                i * unit : (i + 1) * unit
-            ]
-            decays.append(a0 * a1)
-    for b in range(n_chip):
-        mine = jnp.concatenate(decays[b * units : (b + 1) * units], axis=0)
-        high = mine.astype(BF16).astype(F32)
-        fill = jnp.zeros((held.shape[1] - block - 2 * units, LANES), F32)
-        extra = jnp.concatenate([high, mine - high, fill], axis=0)
-        held[b, block:, :] = extra.astype(BF16)
-    for s, out in enumerate(outs):
-        out[...] = held[ahead(chip, s, n_chip)]
-
-
-def scan_kernel(unit, *refs):
-    _, chip, n_chip = core_and_chip()
-    pieces, outs = refs[:n_chip], refs[n_chip : 2 * n_chip]
-    held, result = refs[2 * n_chip :]
-    block, states = outs[0].shape
-    units = block // unit
-    for s, ref in enumerate(pieces):
-        held[ahead(chip, n_chip - s, n_chip)] = ref[...]
-    carry = [jnp.zeros((unit, states), F32)] * units
-    for k in reversed(range(n_chip)):
-        extra = held[k, block:, :].astype(F32)
-        for u in range(units):
-            span = slice(u * unit, (u + 1) * unit)
-            result[k, span, :] = carry[u].astype(BF16)
-            if k:
-                decay = extra[u : u + 1] + extra[units + u : units + u + 1]
-                carry[u] = held[k, span, :].astype(F32) + decay * carry[u]
-    for s, out in enumerate(outs):
-        out[...] = result[ahead(chip, s, n_chip)]
-
-
-def carry_kernel(many, size, *refs):
-    core, chip, n_chip = core_and_chip()
-    pieces = refs[:n_chip]
-    keep_ref, recv_ref, own_ref, send_ref, held = refs[n_chip:]
-    block = pieces[0].shape[0]
-    for s, ref in enumerate(pieces):
-        held[rows_at(ahead(chip, n_chip - s, n_chip), block), :] = ref[...]
+        states.append(g0 + a0 * g1)
+        decays.append(a0 * a1)
+    payload(out_ref, many, states, decays)
+
+
+def pick_side(upper, mine, theirs):
+    return jnp.where(upper, theirs, mine), jnp.where(upper, mine, theirs)
+
+
+def climb_kernel(many, size, bit, mine_ref, recv_ref, out_ref):
+    _, chip, _ = core_and_chip()
+    upper = lax.rem(lax.div(chip, bit), 2) == 1
+    states, decays = [], []
+    for head in range(many):
+        t_mine, a_mine = loaded(mine_ref, many, size, head)
+        t_recv, a_recv = loaded(recv_ref, many, size, head)
+        t_low, t_high = pick_side(upper, t_mine, t_recv)
+        a_low, a_high = pick_side(upper, a_mine, a_recv)
+        states.append(t_low + a_low * t_high)
+        decays.append(a_low * a_high)
+    payload(out_ref, many, states, decays)
+
+
+def carry_kernel(many, size, levels, *refs):
+    core, chip, _ = core_and_chip()
+    recvs = refs[:levels]
+    keep_ref, recv_ref, own_ref, send_ref = refs[levels:]
     for head in range(many):
         span = slice(head * size, (head + 1) * size)
+        carry, reach = None, None
+        for level, ref in enumerate(recvs):
+            state, decay = loaded(ref, many, size, head)
+            lower = lax.rem(lax.div(chip, 2**level), 2) == 0
+            state = jnp.where(lower, state, 0.0)
+            decay = jnp.where(lower, decay, 1.0)
+            carry = state if carry is None else carry + reach * state
+            reach = decay if reach is None else reach * decay
         _, (g1, a1) = pair(keep_ref, recv_ref, many, size, head)
-        second = held[span, :].astype(F32)
+        second = carry
         first = g1 + a1 * second
         own_ref[span, :] = jnp.where(core == 0, first, second).astype(BF16)
         send_ref[span, :] = jnp.where(core == 0, second, first).astype(BF16)
@@ -246,7 +282,7 @@
     x_ref, own_ref = refs[:2]
     mine, other = refs[2 : 2 + n_mine], refs[2 + n_mine]
     w_ref, b_ref = refs[3 + n_mine :]
-    assemble(w_ref, own_ref, mine, other)
+    assemble(0, w_ref, own_ref, mine, other)
     b_ref[...] = dot(x_ref[...], w_ref[...], 1, 0).astype(BF16)
 
 
@@ -393,16 +429,17 @@
         out[...] = held[ahead(place, s + 1, n_dp)].astype(BF16)
 
 
-def expert_kernel(flip, a_ref, b_ref, gate_ref, up_ref, out_ref, rows_ref, gate_acc, up_acc):
+def expert_kernel(flip, slots, a_ref, gate_ref, up_ref, out_ref, rows_ref, gate_acc, up_acc):
     step = pl.program_id(0)
-    n_chip, double, _ = a_ref.shape
-    slots = double // 2
+    n_tm = a_ref.shape[0]
 
     @pl.when(step == 0)
     def _():
-        for i in range(n_chip):
-            rows_ref[i * slots : (i + 1) * slots, :] = a_ref[i, :slots, :]
-            rows_ref[(n_chip + i) * slots : (n_chip + i + 1) * slots, :] = b_ref[i, :slots, :]
+        for i in range(n_tm):
+            for t in range(rows_ref.shape[1] // LANES):
+                rows_ref[i * slots : (i + 1) * slots, t * LANES : (t + 1) * LANES] = a_ref[
+                    i, t * slots : (t + 1) * slots, :
+                ]
         gate_acc[...] = jnp.zeros_like(gate_acc)
         up_acc[...] = jnp.zeros_like(up_acc)
 
@@ -417,46 +454,49 @@
         out_ref[...] = (weighted.T if flip else weighted).astype(BF16)
 
 
-def expert(a, b, w_gate, w_up, flip):
-    n_chip, double, width = a.shape
-    slots = n_chip * double
-    hidden = w_gate.shape[1]
+def expert(a, w_gate, w_up, slots, flip):
+    total = a.shape[0] * slots
+    width, hidden = w_gate.shape
     depth = 512
-    whole = pl.BlockSpec((n_chip, double, width), lambda i: (0, 0, 0))
+    whole = pl.BlockSpec(a.shape, lambda i: (0, 0, 0))
     block = pl.BlockSpec((depth, hidden), lambda i: (i, 0))
-    out = (hidden, slots) if flip else (slots, hidden)
+    out = (hidden, total) if flip else (total, hidden)
     return pl.pallas_call(
-        lambda *refs: expert_kernel(flip, *refs),
+        lambda *refs: expert_kernel(flip, slots, *refs),
         out_shape=shape(out, BF16),
         grid=(width // depth,),
-        in_specs=[whole, whole, block, block],
+        in_specs=[whole, block, block],
         out_specs=pl.BlockSpec(out, lambda i: (0, 0)),
         scratch_shapes=[
-            pltpu.VMEM((slots, width), BF16),
-            pltpu.VMEM((slots, hidden), F32),
-            pltpu.VMEM((slots, hidden), F32),
+            pltpu.VMEM((total, width), BF16),
+            pltpu.VMEM((total, hidden), F32),
+            pltpu.VMEM((total, hidden), F32),
         ],
         cost_estimate=pl.CostEstimate(
-            flops=4 * slots * width * hidden,
+            flops=4 * total * width * hidden,
             bytes_accessed=4 * width * hidden,
             transcendentals=0,
         ),
         compiler_params=pltpu.CompilerParams(vmem_limit_bytes=20 * 1024 * 1024),
-    )(a, b, w_gate, w_up)
-
-
-def down_kernel(n_dp, flip, *refs):
+    )(a, w_gate, w_up)
+
+
+def down_kernel(n_dp, flip, slots, *refs):
     pieces = refs[:n_dp]
-    a_ref, b_ref, out_ref = refs[n_dp:]
-    n_chip, double, _ = a_ref.shape
-    slots = double // 2
+    a_ref, out_ref = refs[n_dp:]
+    n_tm = a_ref.shape[0]
     piece = out_ref.shape[1]
+    tiles = -(-piece // LANES)
+    base = piece * n_dp // LANES * slots
     total = None
     for s in range(n_dp):
-        span = slice(s * piece, (s + 1) * piece)
-        grads = jnp.concatenate(
-            [r[i, slots:, span] for r in (a_ref, b_ref) for i in range(n_chip)], axis=0
-        )
+        columns = []
+        for t in range(tiles):
+            row = base + (s * tiles + t) * slots
+            columns.append(
+                jnp.concatenate([a_ref[i, row : row + slots, :] for i in range(n_tm)], axis=0)
+            )
+        grads = jnp.concatenate(columns, axis=1)[:, :piece]
         part = dot(pieces[s][...], grads, 1 if flip else 0, 0)
         total = part if total is None else total + part
     out_ref[...] = total.astype(BF16)
@@ -473,16 +513,6 @@
 
 def chips(arrays):
     return [arrays[0]] + [shifted(a, "tm", s + 1, 2) for s, a in enumerate(arrays[1:])]
-
-
-def dealt(array, axis):
-    count = lax.axis_size(axis)
-    place = lax.axis_index(axis)
-    pieces = [lax.dynamic_index_in_dim(array, place, 0, False)]
-    for s in range(1, count):
-        block = lax.dynamic_index_in_dim(array, lax.rem(place + s, count), 0, False)
-        pieces.append(shifted(block, axis, s))
-    return pieces
 
 
 def per_device(
@@ -514,73 +544,96 @@
     piece = width // n_dp
     part = width // 2
     many = heads // 2
-    block = part // n_chip
-    unit = min(size, block & -block)
     flip = w_gate.shape[2] % LANES == 0
 
-    def gathered(start):
-        own = w_bc[:, start : start + half]
-        mine = lax.dynamic_slice(w_bc, (core * (share // 2), start), (share // 2, half))
-        mine = [shifted(mine, "dp", s) for s in range(1, n_dp)]
-        return [own, *mine, swapped(jnp.stack(mine))]
-
-    w_c = gathered(half)
-
-    cumt, cum, steps, dyt, xt, xs, carried = call(
+    frames = jnp.arange(length)[None, :]
+    live = jnp.arange(capacity) < slot_counts[0, 0]
+    weights = jnp.where(live, slot_gates[0, 0], jnp.zeros_like(slot_gates[0, 0]))
+    scale = jnp.concatenate([jnp.ones_like(weights), weights])
+    chosen = jnp.concatenate([slot_rows[0, 0], slot_rows[0, 0]])
+    pick = jnp.where(chosen[:, None] == frames, scale[:, None], jnp.zeros_like(scale)[:, None])
+    grad_rows = -(-piece // LANES) * capacity
+    rows_in, rows_own, *sends = call(
+        lambda *refs: first_kernel(half, *refs),
+        [shape((width // LANES * capacity, LANES), BF16), shape((grad_rows, LANES), BF16)]
+        + [shape((share // 2 + grad_rows, LANES), BF16)] * (n_dp - 1),
+        0.5,
+        (x, dy, pick, w_bc),
+        scratch=[pltpu.VMEM((n_dp, grad_rows, LANES), BF16)],
+        fetch=(0, 1, 3),
+    )
+    mine = [shifted(a, "dp", s + 1) for s, a in enumerate(sends)]
+    other = swapped(jnp.stack([m[: share // 2] for m in mine]))
+
+    cumt, cum, steps, dyt, xs, carried, *xt = call(
         prep_kernel,
         [
             shape((heads, length), F32),
             shape((length, LANES), F32),
             shape((length, LANES), F32),
             shape((width, length), BF16),
-            shape((width, length), BF16),
             shape((length, width), BF16),
             shape((length, half), F32),
-        ],
+        ]
+        + [shape((width // n_chip, length), BF16)] * n_chip,
         2.0,
         (x, dy, ldt, stept, h_in),
-    )
-    rows_in, rows_grad = call(
-        pick_kernel,
-        [shape((capacity, width), BF16), shape((n_dp, capacity, piece), BF16)],
-        0.5,
-        (x, dy, slot_rows[0], slot_counts, slot_gates[0]),
-        after=(cumt,),
-    )
-    wc_whole, c_rows, keep, send = call(
+        after=(rows_own,),
+        scratch=[pltpu.VMEM((width, length), BF16)],
+        fetch=(0, 1, 2, 3, 4),
+    )
+    columns_in = chips(xt)
+    wc_whole, c_rows, keep, send, wb_half = call(
         lambda *refs: project_kernel(n_dp - 1, *refs),
         [
             shape((width, half), BF16),
             shape((length, half), BF16),
             shape((part + up16(2 * many), half), BF16),
             shape((part + up16(2 * many), half), BF16),
+            shape((share // 2, half), BF16),
         ],
         1.0,
-        (x, dyt, cumt, *w_c),
+        (x, dyt, cumt, w_bc, *mine, other),
     )
     recv = swapped(send)
-    w_b = gathered(0)
-    extra = up16(2 * (block // unit))
-    pieces = call(
-        lambda *refs: combine_kernel(many, size, unit, *refs),
-        [shape((block + extra, half), BF16)] * n_chip,
-        0.5,
-        (keep, recv),
-        scratch=[pltpu.VMEM((n_chip, block + extra, half), BF16)],
-    )
-    pieces = chips(pieces)
-
-    rows_grad = jnp.concatenate(dealt(rows_grad, "dp"), axis=1)
-    rows = jnp.concatenate([rows_in, rows_grad], axis=0)
-    rows_a = jnp.stack(chips([rows] * n_chip))
-    rows_b = swapped(rows_a)
-    weighted = expert(rows_a, rows_b, w_gate[0], w_up[0], flip)
+    mine_b = [shifted(wb_half, "dp", s) for s in range(1, n_dp)]
+    other_b = swapped(jnp.stack(mine_b))
+    climbs = [
+        call(
+            lambda *refs: combine_kernel(many, size, *refs),
+            [shape((part + up16(2 * many), half), BF16)],
+            0.5,
+            (keep, recv),
+        )[0]
+    ]
+    arrived = []
+    bit = 1
+    while bit < n_chip:
+        last = bit * 2 == n_chip
+        moves = [
+            (k, k ^ (2 * bit)) for k in range(2 * n_chip) if not last or k & (2 * bit)
+        ]
+        arrived.append(lax.ppermute(climbs[-1], "tm", moves))
+        if not last:
+            climbs.append(
+                call(
+                    lambda *refs, bit=bit: climb_kernel(many, size, bit, *refs),
+                    [shape((part + up16(2 * many), half), BF16)],
+                    0.5,
+                    (climbs[-1], arrived[-1]),
+                )[0]
+            )
+        bit *= 2
+
+    rows = jnp.concatenate([rows_in, rows_own] + [m[share // 2 :] for m in mine], axis=0)
+    rows = lax.all_gather(rows, "tm")
+    weighted = expert(rows, w_gate[0], w_up[0], capacity, flip)
 
     wb_whole, b_rows = call(
         lambda *refs: b_kernel(n_dp - 1, *refs),
         [shape((width, half), BF16), shape((length, half), BF16)],
         0.5,
-        (x, *w_b),
+        (x, w_bc, *mine_b, other_b),
     )
     parts = 2
     tiles = width // LANES // parts
@@ -609,33 +662,13 @@
         (mixed, b_rows, c_rows, carried),
     )
 
-    returned = call(
-        lambda *refs: scan_kernel(unit, *refs),
-        [shape((block, half), BF16)] * n_chip,
-        0.5,
-        tuple(pieces),
-        scratch=[
-            pltpu.VMEM((n_chip, block + extra, half), BF16),
-            pltpu.VMEM((n_chip, block, half), BF16),
-        ],
-    )
-    returned = chips(returned)
     r_own, r_send = call(
-        lambda *refs: carry_kernel(many, size, *refs),
+        lambda *refs: carry_kernel(many, size, len(arrived), *refs),
         [shape((part, half), BF16)] * 2,
         0.5,
-        (*returned, keep, recv),
-        scratch=[pltpu.VMEM((part, half), BF16)],
+        (*arrived, keep, recv),
     )
     r_recv = swapped(r_send)
-    columns_in = chips(
-        [
-            lax.dynamic_index_in_dim(
-                xt.reshape(n_chip, width // n_chip, length), ahead(chip, s, n_chip), 0, False
-            )
-            for s in range(n_chip)
-        ]
-    )
     d_bc = call(db_kernel, [shape((length, columns), BF16)], 0.3, (xs, r_own, r_recv, db, dc))[0]
     d_bcs = chips([d_bc] * n_chip)
     d_in, d_decay, d_step = call(
@@ -672,10 +705,11 @@
 
     spread = [weighted] + [shifted(weighted, "dp", s) for s in range(1, n_dp)]
     w_down_grad = call(
-        lambda *refs: down_kernel(n_dp, flip, *refs),
+        lambda *refs: down_kernel(n_dp, flip, capacity, *refs),
         [shape((w_gate.shape[2], piece), BF16)],
         1.0,
-        (*spread, rows_a, rows_b),
+        (*spread, rows),
+        after=(final[0],),
     )[0]
     return (d_in[None], d_decay.T[None], d_step.T[None], w_bc_grad, w_down_grad[None])
 

time: 98.7 us -> 125 us (1.27)
  the two profiles are of different devices: /device:TPU:0 before, /device:TPU:11 now
where the time goes in v4:
time: 125 us
  waiting for transfers between devices  41.6 us (33%)
  starting transfers between devices  30.4 us (24%)
  Pallas kernels  19.7 us (16%)
  between operations  15 us (12%)
  local copies, waits for them, and re-layouts  14.9 us (12%)
  other arithmetic  2.96 us (2%)
    ppermute x18, waiting for transfers between devices, shifted(): lax.ppermute(array, axis, [(i, (i + shift * stride) % count) for i in ran...  24.7 us
    ppermute x18, starting transfers between devices, shifted(): lax.ppermute(array, axis, [(i, (i + shift * stride) % count) for i in ran...  18.2 us
    pallas_call x15, Pallas kernels, call(): pl.pallas_call(body, out_shape=outs, in_specs=specs + [pl.BlockSpec(memor...  17.1 us
    ppermute x2, waiting for transfers between devices, per_device(): arrived.append(lax.ppermute(climbs[-1], 'tm', moves))  15.2 us
    unnamed x44, local copies, waits for them, and re-layouts  14.2 us
    ppermute x5, starting transfers between devices, swapped(): lax.ppermute(array, 'tm', [(i, i ^ 1) for i in range(lax.axis_size('tm'))])  10.5 us
    pallas_call x1, Pallas kernels, expert(): pl.pallas_call(lambda *refs: expert_kernel(flip, slots, *refs), out_shape...  2.62 us
  transfers between devices with their start and end apart: 26, of which 10 were waited for; matrix products, arithmetic and copies ran while one was open for 3% of the time, Pallas kernels for 13%

profile of v4, /device:TPU:11, one launch (start us, length us, event | category | flops | bytes accessed | tf_op | source)
XLA Modules:
  0.0 124.6 jit_solution(14393259741535091596)
XLA Ops:
  20.5 2.7 %shard_map.147 = (f32[40,128]{1,0:T(8,128)S(1)}, f32[128,128]{1,0:T(8,128)S(1)}, f32[128,128]{1,0:T(8,128)S(1)}, bf16[2560,128]{1,0:T(8,128)(2,1)S(1)}, bf16[128...) custom-call(bf16[128,2560]{1,0:T(8,128)(2,1)S(1)} %bitcast.46, ...), custom_call_target="tpu_custom_call" | custom-call | flops 2000000000 | bytes 1000 | tf_op jit(solution)/shard_map/pallas_call | solution.py:81
  23.8 2.0 %collective-permute-done.2.refs_6_ = bf16[400,128]{1,0:T(8,128)(2,1)S(1)} collective-permute-done((bf16[400,128]{1,0:T(8,128)(2,1)S(1)}, bf16[400,128]{1,0:T(8,128)(2,1)S(1)}, u32[]{:S(2)}, u32[]{:S(2)}) %collective-permute-start.2) | collective-permute-done | bytes 102432 | tf_op jit(solution)/shard_map/ppermute | solution.py:507
  29.8 1.6 %collective-permute-done.8.refs_1_.refs_3_ = bf16[1328,128]{1,0:T(8,128)(2,1)S(1)} collective-permute-done((bf16[1328,128]{1,0:T(8,128)(2,1)S(1)}, bf16[1328,128]{1,0:T(8,128)(2,1)S(1)}, u32[]{:S(2)}, u32[]{:S(2)}) %collective-permute-start.8) | collective-permute-done | bytes 340000 | tf_op jit(solution)/shard_map/ppermute | solution.py:511
  32.0 2.2 %collective-permute-start.5 = (bf16[320,128]{1,0:T(8,128)(2,1)S(1)}, bf16[320,128]{1,0:T(8,128)(2,1)S(1)}, u32[]{:S(2)}, u32[]{:S(2)}) collective-permute-start(bf16[320,128]{1,0:T(8,128)(2,1)S(1)} %get-tuple-element.54), channel_id=1, source_target_pairs={{0,2},{1,3},{2,0},{3,1},{4,6},{5,7},{6,4},{7,5},{8,10},{9,11},{10,... | collective-permute-start | bytes 245768 | tf_op jit(solution)/shard_map/ppermute | solution.py:507
  34.7 8.2 %collective-permute-done.9.refs_1_.refs_0_ = bf16[1328,128]{1,0:T(8,128)(2,1)S(1)} collective-permute-done((bf16[1328,128]{1,0:T(8,128)(2,1)S(1)}, bf16[1328,128]{1,0:T(8,128)(2,1)S(1)}, u32[]{:S(2)}, u32[]{:S(2)}) %collective-permute-start.9) | collective-permute-done | bytes 340000 | tf_op jit(solution)/shard_map/ppermute | solution.py:616
  45.5 2.4 %collective-permute-start.12 = (bf16[640,128]{1,0:T(8,128)(2,1)S(1)}, bf16[640,128]{1,0:T(8,128)(2,1)S(1)}, u32[]{:S(2)}, u32[]{:S(2)}) collective-permute-start(bf16[640,128]{1,0:T(8,128)(2,1)S(1)} %get-tuple-element.81), channel_id=1, source_target_pairs={{0,8},{4,12},{8,16},{12,20},{16,24},{20,28},{24,0},{28,4},{1,9},{5... | collective-permute-start | bytes 491528 | tf_op jit(solution)/shard_map/ppermute | solution.py:507
  47.9 1.5 %collective-permute-start.14 = (bf16[640,128]{1,0:T(8,128)(2,1)S(1)}, bf16[640,128]{1,0:T(8,128)(2,1)S(1)}, u32[]{:S(2)}, u32[]{:S(2)}) collective-permute-start(bf16[640,128]{1,0:T(8,128)(2,1)S(1)} %get-tuple-element.83), channel_id=1, source_target_pairs={{0,24},{4,28},{8,0},{12,4},{16,8},{20,12},{24,16},{28,20},{1,25},{... | collective-permute-start | bytes 491528 | tf_op jit(solution)/shard_map/ppermute | solution.py:507
  49.7 7.0 %collective-permute-done.10.refs_1_ = bf16[1328,128]{1,0:T(8,128)(2,1)S(1)} collective-permute-done((bf16[1328,128]{1,0:T(8,128)(2,1)S(1)}, bf16[1328,128]{1,0:T(8,128)(2,1)S(1)}, u32[]{:S(2)}, u32[]{:S(2)}) %collective-permute-start.10) | collective-permute-done | bytes 340000 | tf_op jit(solution)/shard_map/ppermute | solution.py:616
  57.1 7.2 %collective-permute-start.11 = (bf16[1280,128]{1,0:T(8,128)(2,1)S(1)}, bf16[1280,128]{1,0:T(8,128)(2,1)S(1)}, u32[]{:S(2)}, u32[]{:S(2)}) collective-permute-start(bf16[1280,128]{1,0:T(8,128)(2,1)S(1)} %get-tuple-element.61), channel_id=1, source_target_pairs={{0,4},{4,0},{8,12},{12,8},{16,20},{20,16},{24,28},{28,24},{1,5},{5... | collective-permute-start | bytes 983048 | tf_op jit(solution)/shard_map/ppermute | solution.py:511
  64.3 2.6 %shard_map.153 = (f32[128,1280]{1,0:T(8,128)S(1)}, f32[128,128]{1,0:T(8,128)S(1)}, f32[20,128]{1,0:T(8,128)S(1)}, f32[20,128]{1,0:T(8,128)S(1)}) custom-call(bf16[128,2560]{1,0:T(8,128)(2,1)S(1)} %bitcast.49, bf16[128,2560]{1,0:T(8,128)(2,1)S(1)} %bitcast.43, bf16[128,128]{1,0:T(8,128)(2,1)S(1)} %get-tuple-element.55.refs_2_.refs_1_, ...), custom_call_target="tpu_custom_call" | custom-call | flops 3000000000 | bytes 1000 | tf_op jit(solution)/shard_map/pallas_call | solution.py:81
  66.9 2.6 %shard_map.154 = (f32[128,1280]{1,0:T(8,128)S(1)}, f32[128,128]{1,0:T(8,128)S(1)}, f32[20,128]{1,0:T(8,128)S(1)}, f32[20,128]{1,0:T(8,128)S(1)}) custom-call(bf16[128,2560]{1,0:T(8,128)(2,1)S(1)} %bitcast.50, bf16[128,2560]{1,0:T(8,128)(2,1)S(1)} %bitcast.44, bf16[128,128]{1,0:T(8,128)(2,1)S(1)} %get-tuple-element.55.refs_2_.refs_1_, ...), custom_call_target="tpu_custom_call" | custom-call | flops 3000000000 | bytes 1000 | tf_op jit(solution)/shard_map/pallas_call | solution.py:81
  70.1 1.4 %collective-permute-start.16 = (bf16[128,256]{1,0:T(8,128)(2,1)S(1)}, bf16[128,256]{1,0:T(8,128)(2,1)S(1)}, u32[]{:S(2)}, u32[]{:S(2)}) collective-permute-start(bf16[128,256]{1,0:T(8,128)(2,1)S(1)} %shard_map.156.refs_11_.refs_4_), channel_id=1, source_target_pairs={{0,16},{4,20},{8,24},{12,28},{16,0},{20,4},{24,8},{28,12},{1,17},{... | collective-permute-start | bytes 196616 | tf_op jit(solution)/shard_map/ppermute | solution.py:507
  71.6 2.2 %collective-permute-done.15.refs_5_ = bf16[128,256]{1,0:T(8,128)(2,1)S(1)} collective-permute-done((bf16[128,256]{1,0:T(8,128)(2,1)S(1)}, bf16[128,256]{1,0:T(8,128)(2,1)S(1)}, u32[]{:S(2)}, u32[]{:S(2)}) %collective-permute-start.15) | collective-permute-done | bytes 65568 | tf_op jit(solution)/shard_map/ppermute | solution.py:507
  73.9 1.7 %collective-permute-done.17.refs_7_ = bf16[128,256]{1,0:T(8,128)(2,1)S(1)} collective-permute-done((bf16[128,256]{1,0:T(8,128)(2,1)S(1)}, bf16[128,256]{1,0:T(8,128)(2,1)S(1)}, u32[]{:S(2)}, u32[]{:S(2)}) %collective-permute-start.17) | collective-permute-done | bytes 65568 | tf_op jit(solution)/shard_map/ppermute | solution.py:507
  76.2 1.8 %collective-permute-start.18 = (bf16[320,256]{1,0:T(8,128)(2,1)S(1)}, bf16[320,256]{1,0:T(8,128)(2,1)S(1)}, u32[]{:S(2)}, u32[]{:S(2)}) collective-permute-start(bf16[320,256]{1,0:T(8,128)(2,1)S(1)} %get-tuple-element.85), channel_id=1, source_target_pairs={{0,4},{4,0},{8,12},{12,8},{16,20},{20,16},{24,28},{28,24},{1,5},{5... | collective-permute-start | bytes 491528 | tf_op jit(solution)/shard_map/ppermute | solution.py:511
  78.0 3.1 %shard_map.157 = (bf16[128,2560]{1,0:T(8,128)(2,1)}, f32[40,128]{1,0:T(8,128)}, f32[40,128]{1,0:T(8,128)}) custom-call(bf16[128,2560]{1,0:T(8,128)(2,1)S(1)} %bitcast.51, bf16[128,128]{1,0:T(8,128)(2,1)S(1)} %get-tuple-element.55.refs_2_.refs_1_, f32[40,128]{1,0:T(8,128)S(1)} %get-tuple-element.50.refs_2_.refs_4_, f32[40,128]{1,0:T(8,128)S(1)} %bitcast.58, ...), custom_call_target="tpu_custom_call" | custom-call | flops 3000000000 | bytes 1000 | tf_op jit(solution)/shard_map/pallas_call | solution.py:81
  82.3 2.3 %collective-permute-start.19 = (bf16[80,256]{1,0:T(8,128)(2,1)S(1)}, bf16[80,256]{1,0:T(8,128)(2,1)S(1)}, u32[]{:S(2)}, u32[]{:S(2)}) collective-permute-start(bf16[80,256]{1,0:T(8,128)(2,1)S(1)} %get-tuple-element.87), channel_id=1, source_target_pairs={{0,1},{1,2},{2,3},{3,0},{4,5},{5,6},{6,7},{7,4},{8,9},{9,10},{10,1... | collective-permute-start | bytes 122888 | tf_op jit(solution)/shard_map/ppermute | solution.py:507
  84.6 2.3 %copy-done = bf16[1,2560,896]{2,1,0:T(8,128)(2,1)S(1)} copy-done((bf16[1,2560,896]{2,1,0:T(8,128)(2,1)S(1)}, bf16[1,2560,896]{2,1,0:T(8,128)(2,1)}, u32[]{:S(2)}) %copy-start) | copy-done | bytes 4587544
  86.9 2.3 %copy-done.1 = bf16[1,2560,896]{2,1,0:T(8,128)(2,1)S(1)} copy-done((bf16[1,2560,896]{2,1,0:T(8,128)(2,1)S(1)}, bf16[1,2560,896]{2,1,0:T(8,128)(2,1)}, u32[]{:S(2)}) %copy-start.1) | copy-done | bytes 4587544
  90.5 2.6 %shard_map.160.refs_0_ = bf16[896,128]{1,0:T(8,128)(2,1)S(1)} custom-call(bf16[8,640,128]{2,1,0:T(8,128)(2,1)S(1)} %bitcast.36, bf16[2560,896]{1,0:T(8,128)(2,1)S(1)} %bitcast.34, bf16[2560,896]{1,0:T(8,128)(2,1)S(1)} %bitcast.35), custom_call_target="tpu_custom_call" | custom-call | flops 1174405120 | bytes 9175040 | tf_op jit(solution)/shard_map/pallas_call | solution.py:464
  96.7 2.9 %collective-permute-done.22.refs_1_ = bf16[896,128]{1,0:T(8,128)(2,1)S(1)} collective-permute-done((bf16[896,128]{1,0:T(8,128)(2,1)S(1)}, bf16[896,128]{1,0:T(8,128)(2,1)S(1)}, u32[]{:S(2)}, u32[]{:S(2)}) %collective-permute-start.22) | collective-permute-done | bytes 229408 | tf_op jit(solution)/shard_map/ppermute | solution.py:507
  99.5 12.9 %collective-permute-done.23.refs_2_ = bf16[896,128]{1,0:T(8,128)(2,1)S(1)} collective-permute-done((bf16[896,128]{1,0:T(8,128)(2,1)S(1)}, bf16[896,128]{1,0:T(8,128)(2,1)S(1)}, u32[]{:S(2)}, u32[]{:S(2)}) %collective-permute-start.23) | collective-permute-done | bytes 229408 | tf_op jit(solution)/shard_map/ppermute | solution.py:507
  112.4 3.0 %collective-permute-done.24.refs_3_ = bf16[896,128]{1,0:T(8,128)(2,1)S(1)} collective-permute-done((bf16[896,128]{1,0:T(8,128)(2,1)S(1)}, bf16[896,128]{1,0:T(8,128)(2,1)S(1)}, u32[]{:S(2)}, u32[]{:S(2)}) %collective-permute-start.24) | collective-permute-done | bytes 229408 | tf_op jit(solution)/shard_map/ppermute | solution.py:507
  115.4 2.3 %shard_map.161 = bf16[896,640]{1,0:T(8,128)(2,1)} custom-call(bf16[896,128]{1,0:T(8,128)(2,1)S(1)} %shard_map.160.refs_0_, bf16[896,128]{1,0:T(8,128)(2,1)S(1)} %collective-permute-done.22.refs_1_, bf16[896,128]{1,0:T(8,128)(2,1)S(1)} %collective-permute-done.23.refs_2_, bf16[896,128]{1,0:T(8,128)(2,1)S(1)} %collective-permute-done.24.refs_3_, ...), custom_call_target="tpu_custom_call" | custom-call | flops 1000000000 | bytes 1000 | tf_op jit(solution)/shard_map/pallas_call | solution.py:81
  (101 shorter events, 28.9 us)
Async XLA Ops:
  7.2 77.4 %all-gather.3.cloned.1.call-start = ((), (), s32[]{:S(2)}) async-start(), calls=%async_computation | async-start | bytes 1474560 | tf_op jit(solution)/shard_map/all_gather | solution.py:629
  13.5 12.4 %collective-permute-start = (bf16[400,128]{1,0:T(8,128)(2,1)S(1)}, bf16[400,128]{1,0:T(8,128)(2,1)S(1)}, u32[]{:S(2)}, u32[]{:S(2)}) collective-permute-start(bf16[400,128]{1,0:T(8,128)(2,1)S(1)} %get-tuple-element.51), channel_id=1, source_target_pairs={{0,1},{1,2},{2,3},{3,0},{4,5},{5,6},{6,7},{7,4},{8,9},{9,10},{10,1... | collective-permute-start | bytes 307208 | tf_op jit(solution)/shard_map/ppermute | solution.py:507
  14.8 11.0 %collective-permute-start.1 = (bf16[400,128]{1,0:T(8,128)(2,1)S(1)}, bf16[400,128]{1,0:T(8,128)(2,1)S(1)}, u32[]{:S(2)}, u32[]{:S(2)}) collective-permute-start(bf16[400,128]{1,0:T(8,128)(2,1)S(1)} %get-tuple-element.52), channel_id=1, source_target_pairs={{0,2},{1,3},{2,0},{3,1},{4,6},{5,7},{6,4},{7,5},{8,10},{9,11},{10,... | collective-permute-start | bytes 307208 | tf_op jit(solution)/shard_map/ppermute | solution.py:507
  15.9 9.9 %collective-permute-start.2 = (bf16[400,128]{1,0:T(8,128)(2,1)S(1)}, bf16[400,128]{1,0:T(8,128)(2,1)S(1)}, u32[]{:S(2)}, u32[]{:S(2)}) collective-permute-start(bf16[400,128]{1,0:T(8,128)(2,1)S(1)} %get-tuple-element.53), channel_id=1, source_target_pairs={{0,3},{1,0},{2,1},{3,2},{4,7},{5,4},{6,5},{7,6},{8,11},{9,8},{10,9... | collective-permute-start | bytes 307208 | tf_op jit(solution)/shard_map/ppermute | solution.py:507
  31.6 11.3 %collective-permute-start.9 = (bf16[1328,128]{1,0:T(8,128)(2,1)S(1)}, bf16[1328,128]{1,0:T(8,128)(2,1)S(1)}, u32[]{:S(2)}, u32[]{:S(2)}) collective-permute-start(bf16[1328,128]{1,0:T(8,128)(2,1)S(1)} %shard_map.150.refs_0_), channel_id=1, source_target_pairs={{0,8},{4,12},{8,0},{12,4},{16,24},{20,28},{24,16},{28,20},{1,9},{5... | collective-permute-start | bytes 1019912 | tf_op jit(solution)/shard_map/ppermute | solution.py:616
  32.0 12.4 %collective-permute-start.4 = (bf16[320,128]{1,0:T(8,128)(2,1)S(1)}, bf16[320,128]{1,0:T(8,128)(2,1)S(1)}, u32[]{:S(2)}, u32[]{:S(2)}) collective-permute-start(bf16[320,128]{1,0:T(8,128)(2,1)S(1)} %get-tuple-element.54), channel_id=1, source_target_pairs={{0,1},{1,2},{2,3},{3,0},{4,5},{5,6},{6,7},{7,4},{8,9},{9,10},{10,1... | collective-permute-start | bytes 245768 | tf_op jit(solution)/shard_map/ppermute | solution.py:507
  32.0 12.4 %collective-permute-start.5 = (bf16[320,128]{1,0:T(8,128)(2,1)S(1)}, bf16[320,128]{1,0:T(8,128)(2,1)S(1)}, u32[]{:S(2)}, u32[]{:S(2)}) collective-permute-start(bf16[320,128]{1,0:T(8,128)(2,1)S(1)} %get-tuple-element.54), channel_id=1, source_target_pairs={{0,2},{1,3},{2,0},{3,1},{4,6},{5,7},{6,4},{7,5},{8,10},{9,11},{10,... | collective-permute-start | bytes 245768 | tf_op jit(solution)/shard_map/ppermute | solution.py:507
  34.2 10.2 %collective-permute-start.6 = (bf16[320,128]{1,0:T(8,128)(2,1)S(1)}, bf16[320,128]{1,0:T(8,128)(2,1)S(1)}, u32[]{:S(2)}, u32[]{:S(2)}) collective-permute-start(bf16[320,128]{1,0:T(8,128)(2,1)S(1)} %get-tuple-element.54), channel_id=1, source_target_pairs={{0,3},{1,0},{2,1},{3,2},{4,7},{5,4},{6,5},{7,6},{8,11},{9,8},{10,9... | collective-permute-start | bytes 245768 | tf_op jit(solution)/shard_map/ppermute | solution.py:507
  43.1 13.7 %collective-permute-start.10 = (bf16[1328,128]{1,0:T(8,128)(2,1)S(1)}, bf16[1328,128]{1,0:T(8,128)(2,1)S(1)}, u32[]{:S(2)}, u32[]{:S(2)}) collective-permute-start(bf16[1328,128]{1,0:T(8,128)(2,1)S(1)} %shard_map.151), channel_id=1, source_target_pairs={{16,0},{20,4},{24,8},{28,12},{17,1},{21,5},{25,9},{29,13},{18,2},{... | collective-permute-start | bytes 1019912 | tf_op jit(solution)/shard_map/ppermute | solution.py:616
  44.5 4.9 %collective-permute-start.7 = (bf16[3,320,128]{2,1,0:T(8,128)(2,1)S(1)}, bf16[3,320,128]{2,1,0:T(8,128)(2,1)S(1)}, u32[]{:S(2)}, u32[]{:S(2)}) collective-permute-start(bf16[3,320,128]{2,1,0:T(8,128)(2,1)S(1)} %pad_maximum_fusion.1), channel_id=1, source_target_pairs={{0,4},{4,0},{8,12},{12,8},{16,20},{20,16},{24,28},{28,24},{1,5},{5... | collective-permute-start | bytes 737288 | tf_op jit(solution)/shard_map/ppermute | solution.py:511
  45.5 26.1 %collective-permute-start.12 = (bf16[640,128]{1,0:T(8,128)(2,1)S(1)}, bf16[640,128]{1,0:T(8,128)(2,1)S(1)}, u32[]{:S(2)}, u32[]{:S(2)}) collective-permute-start(bf16[640,128]{1,0:T(8,128)(2,1)S(1)} %get-tuple-element.81), channel_id=1, source_target_pairs={{0,8},{4,12},{8,16},{12,20},{16,24},{20,28},{24,0},{28,4},{1,9},{5... | collective-permute-start | bytes 491528 | tf_op jit(solution)/shard_map/ppermute | solution.py:507
  47.8 23.7 %collective-permute-start.13 = (bf16[640,128]{1,0:T(8,128)(2,1)S(1)}, bf16[640,128]{1,0:T(8,128)(2,1)S(1)}, u32[]{:S(2)}, u32[]{:S(2)}) collective-permute-start(bf16[640,128]{1,0:T(8,128)(2,1)S(1)} %get-tuple-element.82), channel_id=1, source_target_pairs={{0,16},{4,20},{8,24},{12,28},{16,0},{20,4},{24,8},{28,12},{1,17},{... | collective-permute-start | bytes 491528 | tf_op jit(solution)/shard_map/ppermute | solution.py:507
  47.9 23.7 %collective-permute-start.14 = (bf16[640,128]{1,0:T(8,128)(2,1)S(1)}, bf16[640,128]{1,0:T(8,128)(2,1)S(1)}, u32[]{:S(2)}, u32[]{:S(2)}) collective-permute-start(bf16[640,128]{1,0:T(8,128)(2,1)S(1)} %get-tuple-element.83), channel_id=1, source_target_pairs={{0,24},{4,28},{8,0},{12,4},{16,8},{20,12},{24,16},{28,20},{1,25},{... | collective-permute-start | bytes 491528 | tf_op jit(solution)/shard_map/ppermute | solution.py:507
  57.1 12.6 %collective-permute-start.11 = (bf16[1280,128]{1,0:T(8,128)(2,1)S(1)}, bf16[1280,128]{1,0:T(8,128)(2,1)S(1)}, u32[]{:S(2)}, u32[]{:S(2)}) collective-permute-start(bf16[1280,128]{1,0:T(8,128)(2,1)S(1)} %get-tuple-element.61), channel_id=1, source_target_pairs={{0,4},{4,0},{8,12},{12,8},{16,20},{20,16},{24,28},{28,24},{1,5},{5... | collective-permute-start | bytes 983048 | tf_op jit(solution)/shard_map/ppermute | solution.py:511
  70.0 3.8 %collective-permute-start.15 = (bf16[128,256]{1,0:T(8,128)(2,1)S(1)}, bf16[128,256]{1,0:T(8,128)(2,1)S(1)}, u32[]{:S(2)}, u32[]{:S(2)}) collective-permute-start(bf16[128,256]{1,0:T(8,128)(2,1)S(1)} %shard_map.156.refs_11_.refs_4_), channel_id=1, source_target_pairs={{0,8},{4,12},{8,16},{12,20},{16,24},{20,28},{24,0},{28,4},{1,9},{5... | collective-permute-start | bytes 196616 | tf_op jit(solution)/shard_map/ppermute | solution.py:507
  70.1 3.8 %collective-permute-start.16 = (bf16[128,256]{1,0:T(8,128)(2,1)S(1)}, bf16[128,256]{1,0:T(8,128)(2,1)S(1)}, u32[]{:S(2)}, u32[]{:S(2)}) collective-permute-start(bf16[128,256]{1,0:T(8,128)(2,1)S(1)} %shard_map.156.refs_11_.refs_4_), channel_id=1, source_target_pairs={{0,16},{4,20},{8,24},{12,28},{16,0},{20,4},{24,8},{28,12},{1,17},{... | collective-permute-start | bytes 196616 | tf_op jit(solution)/shard_map/ppermute | solution.py:507
  71.5 4.0 %collective-permute-start.17 = (bf16[128,256]{1,0:T(8,128)(2,1)S(1)}, bf16[128,256]{1,0:T(8,128)(2,1)S(1)}, u32[]{:S(2)}, u32[]{:S(2)}) collective-permute-start(bf16[128,256]{1,0:T(8,128)(2,1)S(1)} %shard_map.156.refs_11_.refs_4_), channel_id=1, source_target_pairs={{0,24},{4,28},{8,0},{12,4},{16,8},{20,12},{24,16},{28,20},{1,25},{... | collective-permute-start | bytes 196616 | tf_op jit(solution)/shard_map/ppermute | solution.py:507
  76.2 4.9 %collective-permute-start.18 = (bf16[320,256]{1,0:T(8,128)(2,1)S(1)}, bf16[320,256]{1,0:T(8,128)(2,1)S(1)}, u32[]{:S(2)}, u32[]{:S(2)}) collective-permute-start(bf16[320,256]{1,0:T(8,128)(2,1)S(1)} %get-tuple-element.85), channel_id=1, source_target_pairs={{0,4},{4,0},{8,12},{12,8},{16,20},{20,16},{24,28},{28,24},{1,5},{5... | collective-permute-start | bytes 491528 | tf_op jit(solution)/shard_map/ppermute | solution.py:511
  81.1 13.5 %collective-permute-start.21 = (bf16[80,256]{1,0:T(8,128)(2,1)S(1)}, bf16[80,256]{1,0:T(8,128)(2,1)S(1)}, u32[]{:S(2)}, u32[]{:S(2)}) collective-permute-start(bf16[80,256]{1,0:T(8,128)(2,1)S(1)} %get-tuple-element.89), channel_id=1, source_target_pairs={{0,3},{1,0},{2,1},{3,2},{4,7},{5,4},{6,5},{7,6},{8,11},{9,8},{10,9... | collective-permute-start | bytes 122888 | tf_op jit(solution)/shard_map/ppermute | solution.py:507
  81.3 14.7 %collective-permute-start.20 = (bf16[80,256]{1,0:T(8,128)(2,1)S(1)}, bf16[80,256]{1,0:T(8,128)(2,1)S(1)}, u32[]{:S(2)}, u32[]{:S(2)}) collective-permute-start(bf16[80,256]{1,0:T(8,128)(2,1)S(1)} %get-tuple-element.88), channel_id=1, source_target_pairs={{0,2},{1,3},{2,0},{3,1},{4,6},{5,7},{6,4},{7,5},{8,10},{9,11},{10,... | collective-permute-start | bytes 122888 | tf_op jit(solution)/shard_map/ppermute | solution.py:507
  82.3 13.7 %collective-permute-start.19 = (bf16[80,256]{1,0:T(8,128)(2,1)S(1)}, bf16[80,256]{1,0:T(8,128)(2,1)S(1)}, u32[]{:S(2)}, u32[]{:S(2)}) collective-permute-start(bf16[80,256]{1,0:T(8,128)(2,1)S(1)} %get-tuple-element.87), channel_id=1, source_target_pairs={{0,1},{1,2},{2,3},{3,0},{4,5},{5,6},{6,7},{7,4},{8,9},{9,10},{10,1... | collective-permute-start | bytes 122888 | tf_op jit(solution)/shard_map/ppermute | solution.py:507
  93.2 6.4 %collective-permute-start.22 = (bf16[896,128]{1,0:T(8,128)(2,1)S(1)}, bf16[896,128]{1,0:T(8,128)(2,1)S(1)}, u32[]{:S(2)}, u32[]{:S(2)}) collective-permute-start(bf16[896,128]{1,0:T(8,128)(2,1)S(1)} %shard_map.160.refs_0_), channel_id=1, source_target_pairs={{0,1},{1,2},{2,3},{3,0},{4,5},{5,6},{6,7},{7,4},{8,9},{9,10},{10,1... | collective-permute-start | bytes 688136 | tf_op jit(solution)/shard_map/ppermute | solution.py:507
  93.2 19.2 %collective-permute-start.23 = (bf16[896,128]{1,0:T(8,128)(2,1)S(1)}, bf16[896,128]{1,0:T(8,128)(2,1)S(1)}, u32[]{:S(2)}, u32[]{:S(2)}) collective-permute-start(bf16[896,128]{1,0:T(8,128)(2,1)S(1)} %shard_map.160.refs_0_), channel_id=1, source_target_pairs={{0,2},{1,3},{2,0},{3,1},{4,6},{5,7},{6,4},{7,5},{8,10},{9,11},{10,... | collective-permute-start | bytes 688136 | tf_op jit(solution)/shard_map/ppermute | solution.py:507
  94.6 20.8 %collective-permute-start.24 = (bf16[896,128]{1,0:T(8,128)(2,1)S(1)}, bf16[896,128]{1,0:T(8,128)(2,1)S(1)}, u32[]{:S(2)}, u32[]{:S(2)}) collective-permute-start(bf16[896,128]{1,0:T(8,128)(2,1)S(1)} %shard_map.160.refs_0_), channel_id=1, source_target_pairs={{0,3},{1,0},{2,1},{3,2},{4,7},{5,4},{6,5},{7,6},{8,11},{9,8},{10,9... | collective-permute-start | bytes 688136 | tf_op jit(solution)/shard_map/ppermute | solution.py:507
  (22 other events, 209.5 us)
Sparse Core Ops, SparseCore 0:
  29.1 30.0 all-gather.2

commit v5 on v4

--- a/solution.py
+++ b/solution.py
@@ -142,51 +142,59 @@
         out[...] = xt_ref[rows_at(ahead(chip, s, n_chip), width // n_chip), :]
 
 
-def first_kernel(start, x_ref, dy_ref, pick_ref, w_ref, in_ref, own_ref, *rest):
-    outs, held = rest[:-1], rest[-1]
-    slots = pick_ref.shape[0] // 2
-    width = x_ref.shape[1]
-    rows = dot(pick_ref[:slots], x_ref[...], 1, 0).astype(BF16)
+def pick_kernel(n_dp, x_ref, dy_ref, slot_ref, count_ref, gate_ref, out_ref):
+    length, width = x_ref.shape
+    slots = slot_ref.shape[1]
+    hit = iota((length, slots), 0) == slot_ref[...]
+    live = iota((1, slots), 1) < count_ref[...]
+    weight = jnp.where(live, gate_ref[...].astype(F32), 0.0)
+    rows = dot(where_one(hit).astype(BF16), x_ref[...], 0, 0).astype(BF16)
+    base = width // LANES * slots
     for t in range(width // LANES):
-        in_ref[t * slots : (t + 1) * slots, :] = rows[:, t * LANES : (t + 1) * LANES]
-    grads = dot(pick_ref[slots:], dy_ref[...], 1, 0).astype(BF16)
-    n_dp = held.shape[0]
+        out_ref[t * slots : (t + 1) * slots, :] = rows[:, t * LANES : (t + 1) * LANES]
+    grads = dot(jnp.where(hit, weight, 0.0).astype(BF16), dy_ref[...], 0, 0).astype(BF16)
     piece = width // n_dp
-    held[...] = jnp.zeros_like(held)
+    tiles = -(-piece // LANES)
+    if piece % LANES:
+        out_ref[base:, :] = jnp.zeros((out_ref.shape[0] - base, LANES), BF16)
     for i in range(n_dp):
-        for t in range(held.shape[1] // slots):
+        for t in range(tiles):
             low, high = i * piece + t * LANES, min((i + 1) * piece, i * piece + (t + 1) * LANES)
-            held[i, t * slots : (t + 1) * slots, : high - low] = grads[:, low:high]
-    place = lax.axis_index("dp")
-    core, _, _ = core_and_chip()
-    own_ref[...] = held[place]
-    half = w_ref.shape[0] // 2
-    for s, out in enumerate(outs):
-        out[:half, :] = w_ref[rows_at(core, half), start : start + LANES]
-        out[half:, :] = held[ahead(place, s + 1, n_dp)]
-
-
-def assemble(start, w_ref, own_ref, mine_refs, other_ref):
+            row = base + (i * tiles + t) * slots
+            out_ref[row : row + slots, : high - low] = grads[:, low:high]
+
+
+def stack_kernel(*refs):
+    for i, ref in enumerate(refs[:-1]):
+        refs[-1][i] = ref[...]
+
+
+def stacked(arrays, after=()):
+    return call(
+        stack_kernel,
+        [shape((len(arrays), *arrays[0].shape), arrays[0].dtype)],
+        0.2,
+        tuple(arrays),
+        after=after,
+    )[0]
+
+
+def project_kernel(n_mine, *refs):
+    x_ref, dyt_ref, cumt_ref, own_ref = refs[:4]
+    mine, other = refs[4 : 4 + n_mine], refs[4 + n_mine]
+    w_ref, bc_ref, keep_ref, send_ref = refs[5 + n_mine :]
     core, _, _ = core_and_chip()
     place, n_dp = lax.axis_index("dp"), lax.axis_size("dp")
     share = own_ref.shape[0]
     half = share // 2
-    w_ref[rows_at(place, share), :] = own_ref[:, start : start + LANES]
-    for i, mine in enumerate(mine_refs):
+    w_ref[rows_at(place, share), :] = own_ref[...]
+    for i in range(n_mine):
         source = ahead(place, n_dp - 1 - i, n_dp)
-        w_ref[rows_at(source * 2 + core, half), :] = mine[:half, :]
-        w_ref[rows_at(source * 2 + 1 - core, half), :] = other_ref[i]
-
-
-def project_kernel(n_mine, *refs):
-    x_ref, dyt_ref, cumt_ref, own_ref = refs[:4]
-    mine, other = refs[4 : 4 + n_mine], refs[4 + n_mine]
-    w_ref, c_ref, keep_ref, send_ref, b_ref = refs[5 + n_mine :]
-    core, _, _ = core_and_chip()
-    assemble(LANES, w_ref, own_ref, mine, other)
-    b_ref[...] = own_ref[rows_at(core, b_ref.shape[0]), :LANES]
-    c_rows = dot(x_ref[...], w_ref[...], 1, 0).astype(BF16)
-    c_ref[...] = c_rows
+        w_ref[rows_at(source * 2 + core, half), :] = mine[i][...]
+        w_ref[rows_at(source * 2 + 1 - core, half), :] = other[i]
+    bc = dot(x_ref[...], w_ref[...], 1, 0).astype(BF16)
+    bc_ref[...] = bc
+    c_rows = bc[:, LANES:]
     heads, length = cumt_ref.shape
     width = dyt_ref.shape[0]
     part, many = width // 2, heads // 2
@@ -278,16 +286,8 @@
         send_ref[span, :] = jnp.where(core == 0, second, first).astype(BF16)
 
 
-def b_kernel(n_mine, *refs):
-    x_ref, own_ref = refs[:2]
-    mine, other = refs[2 : 2 + n_mine], refs[2 + n_mine]
-    w_ref, b_ref = refs[3 + n_mine :]
-    assemble(0, w_ref, own_ref, mine, other)
-    b_ref[...] = dot(x_ref[...], w_ref[...], 1, 0).astype(BF16)
-
-
 def intra_kernel(
-    first, many, x_ref, dy_ref, b_ref, c_ref, cumt_ref, cum_ref, step_ref, h_ref, before_ref,
+    first, many, x_ref, dy_ref, bc_ref, cumt_ref, cum_ref, step_ref, h_ref, before_ref,
     dx_ref, mixed_ref, ex_ref, own_ref, rowm_ref,
 ):
     length, width = x_ref.shape
@@ -295,7 +295,7 @@
     size = width // heads
     per = LANES // size
     upper = iota((length, length), 0) <= iota((length, length), 1)
-    b_rows, c_rows = b_ref[...], c_ref[...]
+    b_rows, c_rows = bc_ref[:, :LANES], bc_ref[:, LANES:]
     scores = dot(b_rows, c_rows, 1, 1)
     lane = iota((1, LANES), 1)
     lane_bf = [where_one(lane // size == i).astype(BF16) for i in range(per)]
@@ -334,10 +334,10 @@
     ex_ref[...] = rowm_ref[rows, :] + jnp.exp(cumt_ref[rows, :]) * reach[rows] - own
 
 
-def close_kernel(mixed_ref, b_ref, c_ref, carried_ref, db_ref, dc_ref):
+def close_kernel(mixed_ref, bc_ref, carried_ref, db_ref, dc_ref):
     mixed = mixed_ref[...].astype(BF16)
-    db_ref[...] = dot(mixed, c_ref[...], 1, 0)
-    dc_ref[...] = (dot(mixed, b_ref[...], 0, 0) + carried_ref[...]).astype(BF16)
+    db_ref[...] = dot(mixed, bc_ref[:, LANES:], 1, 0)
+    dc_ref[...] = (dot(mixed, bc_ref[:, :LANES], 0, 0) + carried_ref[...]).astype(BF16)
 
 
 def db_kernel(xs_ref, own_ref, recv_ref, db_ref, dc_ref, out_ref):
@@ -352,23 +352,22 @@
 
 
 def finish_kernel(parts, *refs):
-    (x_ref, b_ref, cumt_ref, stept_ref, cum_ref, step_ref, h_ref, own_ref, recv_ref,
-     wb_ref, wc_ref, dbc_ref) = refs[:12]
-    dx_refs, ex_refs, st_refs = (refs[12 + i * parts : 12 + (i + 1) * parts] for i in range(3))
-    in_ref, decay_ref, grad_ref, r_ref, edge_ref = refs[12 + 3 * parts :]
+    (x_ref, bc_ref, cumt_ref, stept_ref, cum_ref, step_ref, h_ref, own_ref, recv_ref,
+     w_ref, dbc_ref) = refs[:11]
+    dx_refs, ex_refs, st_refs = (refs[11 + i * parts : 11 + (i + 1) * parts] for i in range(3))
+    in_ref, decay_ref, grad_ref, r_ref, edge_ref = refs[11 + 3 * parts :]
     core, _, _ = core_and_chip()
     length, width = x_ref.shape
     heads = cumt_ref.shape[0]
     size = width // heads
-    half = b_ref.shape[1]
     part = width // 2
     r_ref[rows_at(core, part), :] = own_ref[...]
     r_ref[rows_at(1 - core, part), :] = recv_ref[...]
     cum = cum_ref[...]
     table = halves(jnp.exp(cum[length - 1 : length] - cum) * step_ref[...])
     seen = jnp.zeros((heads, length), F32)
-    b_rows = b_ref[...]
-    d_b, d_c = dbc_ref[:, :half], dbc_ref[:, half:]
+    b_rows = bc_ref[:, :LANES]
+    d_bc = dbc_ref[...]
     for j in range(width // LANES):
         span = slice(j * LANES, (j + 1) * LANES)
         local = dx_refs[j * LANES // (width // parts)]
@@ -376,7 +375,7 @@
         r_tile = r_ref[span, :]
         reach = dot(b_rows, r_tile, 1, 1)
         d_in = local[:, start : start + LANES] + dot(table, to_lanes(j, size), 1, 0) * reach
-        d_in = d_in + dot(d_b, wb_ref[span, :], 1, 1) + dot(d_c, wc_ref[span, :], 1, 1)
+        d_in = d_in + dot(d_bc, w_ref[span, :], 1, 1)
         in_ref[:, span] = d_in.astype(BF16)
         product = x_ref[:, span].astype(F32) * reach
         seen = seen + dot(to_heads(j, heads, size), halves(product), 1, 1)
@@ -429,17 +428,21 @@
         out[...] = held[ahead(place, s + 1, n_dp)].astype(BF16)
 
 
-def expert_kernel(flip, slots, a_ref, gate_ref, up_ref, out_ref, rows_ref, gate_acc, up_acc):
+def expert_kernel(flip, merge, slots, grad_rows, a_ref, b_ref, gate_ref, up_ref, *refs):
+    outs, (rows_ref, gate_acc, up_acc) = refs[:-3], refs[-3:]
     step = pl.program_id(0)
-    n_tm = a_ref.shape[0]
+    n_chip = a_ref.shape[0]
+    width = rows_ref.shape[1]
 
     @pl.when(step == 0)
     def _():
-        for i in range(n_tm):
-            for t in range(rows_ref.shape[1] // LANES):
-                rows_ref[i * slots : (i + 1) * slots, t * LANES : (t + 1) * LANES] = a_ref[
-                    i, t * slots : (t + 1) * slots, :
-                ]
+        for half, ref in enumerate((a_ref, b_ref)):
+            for i in range(n_chip):
+                row = (half * n_chip + i) * slots
+                for t in range(width // LANES):
+                    rows_ref[row : row + slots, t * LANES : (t + 1) * LANES] = ref[
+                        i, t * slots : (t + 1) * slots, :
+                    ]
         gate_acc[...] = jnp.zeros_like(gate_acc)
         up_acc[...] = jnp.zeros_like(up_acc)
 
@@ -451,22 +454,44 @@
     @pl.when(step == pl.num_programs(0) - 1)
     def _():
         weighted = jax.nn.silu(gate_acc[...]) * up_acc[...]
-        out_ref[...] = (weighted.T if flip else weighted).astype(BF16)
-
-
-def expert(a, w_gate, w_up, slots, flip):
-    total = a.shape[0] * slots
+        weighted = (weighted.T if flip else weighted).astype(BF16)
+        place, n_dp = lax.axis_index("dp"), lax.axis_size("dp")
+        base = width // LANES * slots
+        hidden = gate_acc.shape[1]
+        for s in range(n_dp):
+            rows = [
+                a_ref[i, pl.ds(pl.multiple_of(base + ahead(place, s, n_dp) * grad_rows, 16), grad_rows), :]
+                for i in range(n_chip)
+            ]
+            grads = outs[s] if merge else outs[n_dp + s]
+            for i in range(n_chip):
+                row = (hidden if merge else 0) + i * grad_rows
+                grads[row : row + grad_rows, :] = rows[i]
+            if merge:
+                outs[s][:hidden, :] = weighted
+            elif s == 0:
+                for out in outs[:n_dp]:
+                    out[...] = weighted
+
+
+def expert(a, b, w_gate, w_up, slots, grad_rows, n_dp, flip, merge):
+    n_chip = a.shape[0]
+    total = 2 * n_chip * slots
     width, hidden = w_gate.shape
     depth = 512
     whole = pl.BlockSpec(a.shape, lambda i: (0, 0, 0))
     block = pl.BlockSpec((depth, hidden), lambda i: (i, 0))
-    out = (hidden, total) if flip else (total, hidden)
+    grads = n_chip * grad_rows
+    if merge:
+        outs = [(hidden + grads, LANES)] * n_dp
+    else:
+        outs = [(hidden, total) if flip else (total, hidden)] * n_dp + [(grads, LANES)] * n_dp
     return pl.pallas_call(
-        lambda *refs: expert_kernel(flip, slots, *refs),
-        out_shape=shape(out, BF16),
+        lambda *refs: expert_kernel(flip, merge, slots, grad_rows, *refs),
+        out_shape=[shape(o, BF16) for o in outs],
         grid=(width // depth,),
-        in_specs=[whole, block, block],
-        out_specs=pl.BlockSpec(out, lambda i: (0, 0)),
+        in_specs=[whole, whole, block, block],
+        out_specs=[pl.BlockSpec(o, lambda i: (0, 0)) for o in outs],
         scratch_shapes=[
             pltpu.VMEM((total, width), BF16),
             pltpu.VMEM((total, hidden), F32),
@@ -477,27 +502,36 @@
             bytes_accessed=4 * width * hidden,
             transcendentals=0,
         ),
-        compiler_params=pltpu.CompilerParams(vmem_limit_bytes=20 * 1024 * 1024),
-    )(a, w_gate, w_up)
-
-
-def down_kernel(n_dp, flip, slots, *refs):
-    pieces = refs[:n_dp]
-    a_ref, out_ref = refs[n_dp:]
-    n_tm = a_ref.shape[0]
-    piece = out_ref.shape[1]
-    tiles = -(-piece // LANES)
-    base = piece * n_dp // LANES * slots
+        compiler_params=pltpu.CompilerParams(vmem_limit_bytes=50 * 1024 * 1024),
+    )(a, b, w_gate, w_up)
+
+
+def down_kernel(n_dp, flip, merge, slots, grad_rows, *refs):
+    weighted = refs[:n_dp]
+    near = weighted if merge else refs[n_dp : 2 * n_dp]
+    b_ref, far_ref, out_ref = refs[-3:]
+    hidden, piece = out_ref.shape
+    n_chip = b_ref.shape[0]
+    tiles = grad_rows // slots
+    place = lax.axis_index("dp")
     total = None
     for s in range(n_dp):
-        columns = []
-        for t in range(tiles):
-            row = base + (s * tiles + t) * slots
-            columns.append(
-                jnp.concatenate([a_ref[i, row : row + slots, :] for i in range(n_tm)], axis=0)
-            )
+        base = hidden if merge else 0
+        blocks = [
+            near[s][base + i * grad_rows : base + (i + 1) * grad_rows, :] for i in range(n_chip)
+        ]
+        if s == 0:
+            row = b_ref.shape[1] - n_dp * grad_rows + place * grad_rows
+            rows = pl.ds(pl.multiple_of(row, 16), grad_rows)
+            blocks += [b_ref[i, rows, :] for i in range(n_chip)]
+        else:
+            blocks += [far_ref[s - 1, i * grad_rows : (i + 1) * grad_rows, :] for i in range(n_chip)]
+        columns = [
+            jnp.concatenate([b[t * slots : (t + 1) * slots] for b in blocks], axis=0)
+            for t in range(tiles)
+        ]
         grads = jnp.concatenate(columns, axis=1)[:, :piece]
-        part = dot(pieces[s][...], grads, 1 if flip else 0, 0)
+        part = dot(weighted[s][:hidden, :] if merge else weighted[s][...], grads, 1 if flip else 0, 0)
         total = part if total is None else total + part
     out_ref[...] = total.astype(BF16)
 
@@ -545,25 +579,22 @@
     part = width // 2
     many = heads // 2
     flip = w_gate.shape[2] % LANES == 0
-
-    frames = jnp.arange(length)[None, :]
-    live = jnp.arange(capacity) < slot_counts[0, 0]
-    weights = jnp.where(live, slot_gates[0, 0], jnp.zeros_like(slot_gates[0, 0]))
-    scale = jnp.concatenate([jnp.ones_like(weights), weights])
-    chosen = jnp.concatenate([slot_rows[0, 0], slot_rows[0, 0]])
-    pick = jnp.where(chosen[:, None] == frames, scale[:, None], jnp.zeros_like(scale)[:, None])
+    merge = flip and 2 * n_chip * capacity == LANES
+
     grad_rows = -(-piece // LANES) * capacity
-    rows_in, rows_own, *sends = call(
-        lambda *refs: first_kernel(half, *refs),
-        [shape((width // LANES * capacity, LANES), BF16), shape((grad_rows, LANES), BF16)]
-        + [shape((share // 2 + grad_rows, LANES), BF16)] * (n_dp - 1),
+    w_half = lax.dynamic_slice_in_dim(w_bc, core * (share // 2), share // 2, 0)
+    mine = [shifted(w_half, "dp", s) for s in range(1, n_dp)]
+
+    rows = call(
+        lambda *refs: pick_kernel(n_dp, *refs),
+        [shape((width // LANES * capacity + n_dp * grad_rows, LANES), BF16)],
         0.5,
-        (x, dy, pick, w_bc),
-        scratch=[pltpu.VMEM((n_dp, grad_rows, LANES), BF16)],
-        fetch=(0, 1, 3),
-    )
-    mine = [shifted(a, "dp", s + 1) for s, a in enumerate(sends)]
-    other = swapped(jnp.stack([m[: share // 2] for m in mine]))
+        (x, dy, slot_rows[0], slot_counts, slot_gates[0]),
+        fetch=(0, 1),
+        limit=60,
+    )[0]
+    rows_a = jnp.stack(chips([rows] * n_chip))
+    rows_b = swapped(rows_a)
 
     cumt, cum, steps, dyt, xs, carried, *xt = call(
         prep_kernel,
@@ -578,32 +609,32 @@
         + [shape((width // n_chip, length), BF16)] * n_chip,
         2.0,
         (x, dy, ldt, stept, h_in),
-        after=(rows_own,),
+        after=(rows,),
         scratch=[pltpu.VMEM((width, length), BF16)],
         fetch=(0, 1, 2, 3, 4),
+        limit=60,
     )
     columns_in = chips(xt)
-    wc_whole, c_rows, keep, send, wb_half = call(
+    other = swapped(stacked(mine, after=(cumt,)))
+    w_whole, bc, keep, send = call(
         lambda *refs: project_kernel(n_dp - 1, *refs),
         [
-            shape((width, half), BF16),
-            shape((length, half), BF16),
+            shape((width, columns), BF16),
+            shape((length, columns), BF16),
             shape((part + up16(2 * many), half), BF16),
             shape((part + up16(2 * many), half), BF16),
-            shape((share // 2, half), BF16),
         ],
         1.0,
         (x, dyt, cumt, w_bc, *mine, other),
     )
     recv = swapped(send)
-    mine_b = [shifted(wb_half, "dp", s) for s in range(1, n_dp)]
-    other_b = swapped(jnp.stack(mine_b))
     climbs = [
         call(
             lambda *refs: combine_kernel(many, size, *refs),
             [shape((part + up16(2 * many), half), BF16)],
             0.5,
             (keep, recv),
+            after=tuple(columns_in[1:]),
         )[0]
     ]
     arrived = []
@@ -625,16 +656,14 @@
             )
         bit *= 2
 
-    rows = jnp.concatenate([rows_in, rows_own] + [m[share // 2 :] for m in mine], axis=0)
-    rows = lax.all_gather(rows, "tm")
-    weighted = expert(rows, w_gate[0], w_up[0], capacity, flip)
-
-    wb_whole, b_rows = call(
-        lambda *refs: b_kernel(n_dp - 1, *refs),
-        [shape((width, half), BF16), shape((length, half), BF16)],
-        0.5,
-        (x, w_bc, *mine_b, other_b),
-    )
+    outs = expert(rows_a, rows_b, w_gate[0], w_up[0], capacity, grad_rows, n_dp, flip, merge)
+    outs = list(outs)
+    spread = outs[:1] + [shifted(o, "dp", s + 1) for s, o in enumerate(outs[1:n_dp])]
+    near = outs[n_dp : n_dp + 1]
+    near += [shifted(o, "dp", s + 1) for s, o in enumerate(outs[n_dp + 1 :])]
+    moved = [o[w_gate.shape[2] :] for o in spread[1:]] if merge else near[1:]
+    far = swapped(jnp.stack(moved))
+
     parts = 2
     tiles = width // LANES // parts
     dxs, exs, owns = [], [], []
@@ -649,7 +678,7 @@
                 shape((heads // parts, length), F32),
             ],
             3.0,
-            (x, dy, b_rows, c_rows, cumt, cum, steps, h_in, mixed),
+            (x, dy, bc, cumt, cum, steps, h_in, mixed),
             scratch=[pltpu.VMEM((heads, length), F32)],
         )
         dxs.append(dx)
@@ -659,7 +688,7 @@
         close_kernel,
         [shape((length, half), F32), shape((length, half), BF16)],
         0.3,
-        (mixed, b_rows, c_rows, carried),
+        (mixed, bc, carried),
     )
 
     r_own, r_send = call(
@@ -679,7 +708,7 @@
             shape((heads, length), F32),
         ],
         3.0,
-        (x, b_rows, cumt, stept, cum, steps, h_in, r_own, r_recv, wb_whole, wc_whole, d_bc,
+        (x, bc, cumt, stept, cum, steps, h_in, r_own, r_recv, w_whole, d_bc,
          *dxs, *exs, *owns),
         scratch=[pltpu.VMEM((width, half), BF16), pltpu.VMEM((heads, half), F32)],
     )
@@ -703,12 +732,11 @@
     for s in range(1, n_dp):
         w_bc_grad = w_bc_grad + shifted(final[s], "dp", s).astype(F32)
 
-    spread = [weighted] + [shifted(weighted, "dp", s) for s in range(1, n_dp)]
     w_down_grad = call(
-        lambda *refs: down_kernel(n_dp, flip, capacity, *refs),
+        lambda *refs: down_kernel(n_dp, flip, merge, capacity, grad_rows, *refs),
         [shape((w_gate.shape[2], piece), BF16)],
         1.0,
-        (*spread, rows),
+        (*spread, *near, rows_b, far),
         after=(final[0],),
     )[0]
     return (d_in[None], d_decay.T[None], d_step.T[None], w_bc_grad, w_down_grad[None])

time: 125 us -> 103 us (0.82)
  the two profiles are of different devices: /device:TPU:11 before, /device:TPU:0 now
where the time goes in v5:
time: 103 us
  starting transfers between devices  36.6 us (36%)
  waiting for transfers between devices  32.9 us (32%)
  Pallas kernels  27.1 us (26%)
  local copies, waits for them, and re-layouts  3.57 us (3%)
  between operations  1.68 us (2%)
    ppermute x18, starting transfers between devices, shifted(): lax.ppermute(array, axis, [(i, (i + shift * stride) % count) for i in ran...  33.2 us
    ppermute x18, waiting for transfers between devices, shifted(): lax.ppermute(array, axis, [(i, (i + shift * stride) % count) for i in ran...  32.9 us
    pallas_call x15, Pallas kernels, call(): pl.pallas_call(body, out_shape=outs, in_specs=specs + [pl.BlockSpec(memor...  20.9 us
    pallas_call x1, Pallas kernels, expert(): pl.pallas_call(lambda *refs: expert_kernel(flip, merge, slots, grad_rows,...  6.17 us
    ppermute x2, starting transfers between devices, per_device(): arrived.append(lax.ppermute(climbs[-1], 'tm', moves))  2.98 us
    unnamed x36, local copies, waits for them, and re-layouts  2.62 us
  transfers between devices with their start and end apart: 26, of which 13 were waited for; matrix products, arithmetic and copies ran while one was open for 0% of the time, Pallas kernels for 26%

profile of v5, /device:TPU:0, one launch (start us, length us, event | category | flops | bytes accessed | tf_op | source)
XLA Modules:
  0.0 102.7 jit_solution(11335431838885883678)
XLA Ops:
  1.6 3.1 %collective-permute-start = (bf16[320,256]{1,0:T(8,128)(2,1)S(1)}, bf16[320,256]{1,0:T(8,128)(2,1)S(1)}, u32[]{:S(2)}, u32[]{:S(2)}) collective-permute-start(bf16[320,256]{1,0:T(8,128)(2,1)S(1)} %constant_dynamic-slice_fusion), channel_id=1, source_target_pairs={{0,1},{1,2},{2,3},{3,0},{4,5},{5,6},{6,7},{7,4},{8,9},{9,10},{10,1... | collective-permute-start | bytes 491528 | tf_op jit(solution)/shard_map/ppermute | solution.py:541
  4.7 2.6 %collective-permute-start.1 = (bf16[320,256]{1,0:T(8,128)(2,1)S(1)}, bf16[320,256]{1,0:T(8,128)(2,1)S(1)}, u32[]{:S(2)}, u32[]{:S(2)}) collective-permute-start(bf16[320,256]{1,0:T(8,128)(2,1)S(1)} %constant_dynamic-slice_fusion), channel_id=1, source_target_pairs={{0,2},{1,3},{2,0},{3,1},{4,6},{5,7},{6,4},{7,5},{8,10},{9,11},{10,... | collective-permute-start | bytes 491528 | tf_op jit(solution)/shard_map/ppermute | solution.py:541
  9.2 3.0 %shard_map.146.refs_5_ = bf16[640,128]{1,0:T(8,128)(2,1)} custom-call(bf16[128,2560]{1,0:T(8,128)(2,1)} %bitcast.35, bf16[128,2560]{1,0:T(8,128)(2,1)} %bitcast.31, s32[1,16]{1,0:T(1,128)} %bitcast.54, s32[1,1]{1,0:T(1,128)S(6)} %copy.16.refs_3_, bf16[1,16]{1,0:T(2,128)(2,1)} %bitcast.55), custom_call_target="tpu_custom_call" | custom-call | flops 500000000 | bytes 1000 | tf_op jit(solution)/shard_map/pallas_call | solution.py:81
  12.3 4.9 %shard_map.147 = (f32[40,128]{1,0:T(8,128)}, f32[128,128]{1,0:T(8,128)}, f32[128,128]{1,0:T(8,128)}, bf16[2560,128]{1,0:T(8,128)(2,1)}, bf16[128,2560]{1,0:T(8,1...) custom-call(bf16[128,2560]{1,0:T(8,128)(2,1)} %bitcast.36, ...), custom_call_target="tpu_custom_call" | custom-call | flops 2000000000 | bytes 1000 | tf_op jit(solution)/shard_map/pallas_call | solution.py:81
  18.9 2.5 %collective-permute-start.20 = (bf16[640,128]{1,0:T(8,128)(2,1)S(1)}, bf16[640,128]{1,0:T(8,128)(2,1)S(1)}, u32[]{:S(2)}, u32[]{:S(2)}) collective-permute-start(bf16[640,128]{1,0:T(8,128)(2,1)S(1)} %copy-done.14), channel_id=1, source_target_pairs={{0,24},{4,28},{8,0},{12,4},{16,8},{20,12},{24,16},{28,20},{1,25},{... | collective-permute-start | bytes 491528 | tf_op jit(solution)/shard_map/ppermute | solution.py:541
  26.0 5.2 %collective-permute-done.19 = bf16[640,128]{1,0:T(8,128)(2,1)S(1)} collective-permute-done((bf16[640,128]{1,0:T(8,128)(2,1)S(1)}, bf16[640,128]{1,0:T(8,128)(2,1)S(1)}, u32[]{:S(2)}, u32[]{:S(2)}) %collective-permute-start.19) | collective-permute-done | bytes 163872 | tf_op jit(solution)/shard_map/ppermute | solution.py:541
  32.5 2.3 %collective-permute-start.7 = (bf16[640,128]{1,0:T(8,128)(2,1)S(1)}, bf16[640,128]{1,0:T(8,128)(2,1)S(1)}, u32[]{:S(2)}, u32[]{:S(2)}) collective-permute-start(bf16[640,128]{1,0:T(8,128)(2,1)S(1)} %copy-done.15), channel_id=1, source_target_pairs={{0,24},{4,28},{8,0},{12,4},{16,8},{20,12},{24,16},{28,20},{1,25},{... | collective-permute-start | bytes 491528 | tf_op jit(solution)/shard_map/ppermute | solution.py:541
  34.8 4.5 %collective-permute-done.5.refs_2_.refs_1_ = bf16[640,128]{1,0:T(8,128)(2,1)S(1)} collective-permute-done((bf16[640,128]{1,0:T(8,128)(2,1)S(1)}, bf16[640,128]{1,0:T(8,128)(2,1)S(1)}, u32[]{:S(2)}, u32[]{:S(2)}) %collective-permute-start.5) | collective-permute-done | bytes 163872 | tf_op jit(solution)/shard_map/ppermute | solution.py:541
  39.4 2.2 %collective-permute-done.6.refs_3_.refs_2_ = bf16[640,128]{1,0:T(8,128)(2,1)S(1)} collective-permute-done((bf16[640,128]{1,0:T(8,128)(2,1)S(1)}, bf16[640,128]{1,0:T(8,128)(2,1)S(1)}, u32[]{:S(2)}, u32[]{:S(2)}) %collective-permute-start.6) | collective-permute-done | bytes 163872 | tf_op jit(solution)/shard_map/ppermute | solution.py:541
  41.7 1.7 %collective-permute-start.8 = (bf16[1328,128]{1,0:T(8,128)(2,1)S(1)}, bf16[1328,128]{1,0:T(8,128)(2,1)S(1)}, u32[]{:S(2)}, u32[]{:S(2)}) collective-permute-start(bf16[1328,128]{1,0:T(8,128)(2,1)S(1)} %shard_map.150.refs_0_), channel_id=1, source_target_pairs={{0,8},{4,12},{8,0},{12,4},{16,24},{20,28},{24,16},{28,20},{1,9},{5... | collective-permute-start | bytes 1019912 | tf_op jit(solution)/shard_map/ppermute | solution.py:647
  43.4 2.6 %shard_map.153 = (f32[128,1280]{1,0:T(8,128)S(1)}, f32[128,128]{1,0:T(8,128)S(1)}, f32[20,128]{1,0:T(8,128)S(1)}, f32[20,128]{1,0:T(8,128)S(1)}) custom-call(bf16[128,2560]{1,0:T(8,128)(2,1)S(1)} %bitcast.38, bf16[128,2560]{1,0:T(8,128)(2,1)S(1)} %bitcast.33, bf16[128,256]{1,0:T(8,128)(2,1)S(1)} %get-tuple-element.46.refs_2_.refs_1_, ...), custom_call_target="tpu_custom_call" | custom-call | flops 3000000000 | bytes 1000 | tf_op jit(solution)/shard_map/pallas_call | solution.py:81
  46.0 6.2 %shard_map.160 = (bf16[1216,128]{1,0:T(8,128)(2,1)S(1)}, bf16[1216,128]{1,0:T(8,128)(2,1)S(1)}, bf16[1216,128]{1,0:T(8,128)(2,1)S(1)}, bf16[1216,128]{1,0:T(8,128)(2,1)S(1)}) custom-call(bf16[4,640,128]{2,1,0:T(8,128)(2,1)S(1)} %pad_maximum_fusion.refs_0_, bf16[4,640,128]{2,1,0:T(8,128)(2,1)S(1)} %collective-permute-done.21.refs_1_.refs_4_, ...), custom_call_target="tpu_custom_call" | custom-call | flops 1174405120 | bytes 9175040 | tf_op jit(solution)/shard_map/pallas_call | solution.py:489
  52.2 3.0 %collective-permute-start.23 = (bf16[1216,128]{1,0:T(8,128)(2,1)S(1)}, bf16[1216,128]{1,0:T(8,128)(2,1)S(1)}, u32[]{:S(2)}, u32[]{:S(2)}) collective-permute-start(bf16[1216,128]{1,0:T(8,128)(2,1)S(1)} %get-tuple-element.81), channel_id=1, source_target_pairs={{0,2},{1,3},{2,0},{3,1},{4,6},{5,7},{6,4},{7,5},{8,10},{9,11},{10,... | collective-permute-start | bytes 933896 | tf_op jit(solution)/shard_map/ppermute | solution.py:541
  55.2 3.4 %collective-permute-start.24 = (bf16[1216,128]{1,0:T(8,128)(2,1)S(1)}, bf16[1216,128]{1,0:T(8,128)(2,1)S(1)}, u32[]{:S(2)}, u32[]{:S(2)}) collective-permute-start(bf16[1216,128]{1,0:T(8,128)(2,1)S(1)} %get-tuple-element.82), channel_id=1, source_target_pairs={{0,3},{1,0},{2,1},{3,2},{4,7},{5,4},{6,5},{7,6},{8,11},{9,8},{10,9... | collective-permute-start | bytes 933896 | tf_op jit(solution)/shard_map/ppermute | solution.py:541
  60.1 2.5 %shard_map.154 = (f32[128,1280]{1,0:T(8,128)S(1)}, f32[128,128]{1,0:T(8,128)S(1)}, f32[20,128]{1,0:T(8,128)S(1)}, f32[20,128]{1,0:T(8,128)S(1)}) custom-call(bf16[128,2560]{1,0:T(8,128)(2,1)S(1)} %bitcast.39, bf16[128,2560]{1,0:T(8,128)(2,1)S(1)} %bitcast.34, bf16[128,256]{1,0:T(8,128)(2,1)S(1)} %get-tuple-element.46.refs_2_.refs_1_, ...), custom_call_target="tpu_custom_call" | custom-call | flops 3000000000 | bytes 1000 | tf_op jit(solution)/shard_map/pallas_call | solution.py:81
  63.0 6.8 %collective-permute-done.24.refs_3_ = bf16[1216,128]{1,0:T(8,128)(2,1)S(1)} collective-permute-done((bf16[1216,128]{1,0:T(8,128)(2,1)S(1)}, bf16[1216,128]{1,0:T(8,128)(2,1)S(1)}, u32[]{:S(2)}, u32[]{:S(2)}) %collective-permute-start.24) | collective-permute-done | bytes 311328 | tf_op jit(solution)/shard_map/ppermute | solution.py:541
  70.7 7.7 %collective-permute-done.22.refs_1_ = bf16[1216,128]{1,0:T(8,128)(2,1)S(1)} collective-permute-done((bf16[1216,128]{1,0:T(8,128)(2,1)S(1)}, bf16[1216,128]{1,0:T(8,128)(2,1)S(1)}, u32[]{:S(2)}, u32[]{:S(2)}) %collective-permute-start.22) | collective-permute-done | bytes 311328 | tf_op jit(solution)/shard_map/ppermute | solution.py:541
  79.4 1.5 %collective-permute-start.12 = (bf16[128,256]{1,0:T(8,128)(2,1)S(1)}, bf16[128,256]{1,0:T(8,128)(2,1)S(1)}, u32[]{:S(2)}, u32[]{:S(2)}) collective-permute-start(bf16[128,256]{1,0:T(8,128)(2,1)S(1)} %shard_map.156.refs_10_.refs_4_), channel_id=1, source_target_pairs={{0,16},{4,20},{8,24},{12,28},{16,0},{20,4},{24,8},{28,12},{1,17},{... | collective-permute-start | bytes 196616 | tf_op jit(solution)/shard_map/ppermute | solution.py:541
  81.0 2.3 %collective-permute-start.13 = (bf16[128,256]{1,0:T(8,128)(2,1)S(1)}, bf16[128,256]{1,0:T(8,128)(2,1)S(1)}, u32[]{:S(2)}, u32[]{:S(2)}) collective-permute-start(bf16[128,256]{1,0:T(8,128)(2,1)S(1)} %shard_map.156.refs_10_.refs_4_), channel_id=1, source_target_pairs={{0,24},{4,28},{8,0},{12,4},{16,8},{20,12},{24,16},{28,20},{1,25},{... | collective-permute-start | bytes 196616 | tf_op jit(solution)/shard_map/ppermute | solution.py:541
  85.9 2.7 %shard_map.157 = (bf16[128,2560]{1,0:T(8,128)(2,1)}, f32[40,128]{1,0:T(8,128)}, f32[40,128]{1,0:T(8,128)}) custom-call(bf16[128,2560]{1,0:T(8,128)(2,1)S(1)} %bitcast.40, bf16[128,256]{1,0:T(8,128)(2,1)S(1)} %get-tuple-element.46.refs_2_.refs_1_, f32[40,128]{1,0:T(8,128)S(1)} %copy-done.4, f32[40,128]{1,0:T(8,128)S(1)} %bitcast.46, ...), custom_call_target="tpu_custom_call" | custom-call | flops 3000000000 | bytes 1000 | tf_op jit(solution)/shard_map/pallas_call | solution.py:81
  88.6 6.1 %collective-permute-start.17 = (bf16[80,256]{1,0:T(8,128)(2,1)S(1)}, bf16[80,256]{1,0:T(8,128)(2,1)S(1)}, u32[]{:S(2)}, u32[]{:S(2)}) collective-permute-start(bf16[80,256]{1,0:T(8,128)(2,1)S(1)} %get-tuple-element.78), channel_id=1, source_target_pairs={{0,3},{1,0},{2,1},{3,2},{4,7},{5,4},{6,5},{7,6},{8,11},{9,8},{10,9... | collective-permute-start | bytes 122888 | tf_op jit(solution)/shard_map/ppermute | solution.py:541
  94.8 1.5 %collective-permute-start.16 = (bf16[80,256]{1,0:T(8,128)(2,1)S(1)}, bf16[80,256]{1,0:T(8,128)(2,1)S(1)}, u32[]{:S(2)}, u32[]{:S(2)}) collective-permute-start(bf16[80,256]{1,0:T(8,128)(2,1)S(1)} %get-tuple-element.77), channel_id=1, source_target_pairs={{0,2},{1,3},{2,0},{3,1},{4,6},{5,7},{6,4},{7,5},{8,10},{9,11},{10,... | collective-permute-start | bytes 122888 | tf_op jit(solution)/shard_map/ppermute | solution.py:541
  96.8 2.3 %shard_map.161 = bf16[896,640]{1,0:T(8,128)(2,1)} custom-call(bf16[1216,128]{1,0:T(8,128)(2,1)S(1)} %get-tuple-element.79.refs_0_, bf16[1216,128]{1,0:T(8,128)(2,1)S(1)} %collective-permute-done.22.refs_1_, bf16[1216,128]{1,0:T(8,128)(2,1)S(1)} %collective-permute-done.23.refs_2_, bf16[1216,128]{1,0:T(8,128)(2,1)S(1)} %collective-permute-done.24.refs_3_, ...), custom_call_target="tpu_custom_call" | custom-call | flops 1000000000 | bytes 1000 | tf_op jit(solution)/shard_map/pallas_call | solution.py:81
  100.0 2.0 %collective-permute-done.15 = bf16[80,256]{1,0:T(8,128)(2,1)S(1)} collective-permute-done((bf16[80,256]{1,0:T(8,128)(2,1)S(1)}, bf16[80,256]{1,0:T(8,128)(2,1)S(1)}, u32[]{:S(2)}, u32[]{:S(2)}) %collective-permute-start.15) | collective-permute-done | bytes 40992 | tf_op jit(solution)/shard_map/ppermute | solution.py:541
  (88 shorter events, 18.5 us)
Async XLA Ops:
  1.6 15.6 %collective-permute-start = (bf16[320,256]{1,0:T(8,128)(2,1)S(1)}, bf16[320,256]{1,0:T(8,128)(2,1)S(1)}, u32[]{:S(2)}, u32[]{:S(2)}) collective-permute-start(bf16[320,256]{1,0:T(8,128)(2,1)S(1)} %constant_dynamic-slice_fusion), channel_id=1, source_target_pairs={{0,1},{1,2},{2,3},{3,0},{4,5},{5,6},{6,7},{7,4},{8,9},{9,10},{10,1... | collective-permute-start | bytes 491528 | tf_op jit(solution)/shard_map/ppermute | solution.py:541
  4.7 13.3 %collective-permute-start.1 = (bf16[320,256]{1,0:T(8,128)(2,1)S(1)}, bf16[320,256]{1,0:T(8,128)(2,1)S(1)}, u32[]{:S(2)}, u32[]{:S(2)}) collective-permute-start(bf16[320,256]{1,0:T(8,128)(2,1)S(1)} %constant_dynamic-slice_fusion), channel_id=1, source_target_pairs={{0,2},{1,3},{2,0},{3,1},{4,6},{5,7},{6,4},{7,5},{8,10},{9,11},{10,... | collective-permute-start | bytes 491528 | tf_op jit(solution)/shard_map/ppermute | solution.py:541
  7.2 10.8 %collective-permute-start.2 = (bf16[320,256]{1,0:T(8,128)(2,1)S(1)}, bf16[320,256]{1,0:T(8,128)(2,1)S(1)}, u32[]{:S(2)}, u32[]{:S(2)}) collective-permute-start(bf16[320,256]{1,0:T(8,128)(2,1)S(1)} %constant_dynamic-slice_fusion), channel_id=1, source_target_pairs={{0,3},{1,0},{2,1},{3,2},{4,7},{5,4},{6,5},{7,6},{8,11},{9,8},{10,9... | collective-permute-start | bytes 491528 | tf_op jit(solution)/shard_map/ppermute | solution.py:541
  18.9 7.1 %collective-permute-start.20 = (bf16[640,128]{1,0:T(8,128)(2,1)S(1)}, bf16[640,128]{1,0:T(8,128)(2,1)S(1)}, u32[]{:S(2)}, u32[]{:S(2)}) collective-permute-start(bf16[640,128]{1,0:T(8,128)(2,1)S(1)} %copy-done.14), channel_id=1, source_target_pairs={{0,24},{4,28},{8,0},{12,4},{16,8},{20,12},{24,16},{28,20},{1,25},{... | collective-permute-start | bytes 491528 | tf_op jit(solution)/shard_map/ppermute | solution.py:541
  21.4 9.8 %collective-permute-start.19 = (bf16[640,128]{1,0:T(8,128)(2,1)S(1)}, bf16[640,128]{1,0:T(8,128)(2,1)S(1)}, u32[]{:S(2)}, u32[]{:S(2)}) collective-permute-start(bf16[640,128]{1,0:T(8,128)(2,1)S(1)} %copy-done.14), channel_id=1, source_target_pairs={{0,16},{4,20},{8,24},{12,28},{16,0},{20,4},{24,8},{28,12},{1,17},{... | collective-permute-start | bytes 491528 | tf_op jit(solution)/shard_map/ppermute | solution.py:541
  21.9 9.3 %collective-permute-start.18 = (bf16[640,128]{1,0:T(8,128)(2,1)S(1)}, bf16[640,128]{1,0:T(8,128)(2,1)S(1)}, u32[]{:S(2)}, u32[]{:S(2)}) collective-permute-start(bf16[640,128]{1,0:T(8,128)(2,1)S(1)} %copy-done.14), channel_id=1, source_target_pairs={{0,8},{4,12},{8,16},{12,20},{16,24},{20,28},{24,0},{28,4},{1,9},{5... | collective-permute-start | bytes 491528 | tf_op jit(solution)/shard_map/ppermute | solution.py:541
  25.4 16.2 %collective-permute-start.4 = (bf16[1328,128]{1,0:T(8,128)(2,1)S(1)}, bf16[1328,128]{1,0:T(8,128)(2,1)S(1)}, u32[]{:S(2)}, u32[]{:S(2)}) collective-permute-start(bf16[1328,128]{1,0:T(8,128)(2,1)S(1)} %get-tuple-element.50), channel_id=1, source_target_pairs={{0,4},{4,0},{8,12},{12,8},{16,20},{20,16},{24,28},{28,24},{1,5},{5... | collective-permute-start | bytes 1019912 | tf_op jit(solution)/shard_map/ppermute | solution.py:545
  31.3 14.8 %collective-permute-start.21 = (bf16[4,640,128]{2,1,0:T(8,128)(2,1)S(1)}, bf16[4,640,128]{2,1,0:T(8,128)(2,1)S(1)}, u32[]{:S(2)}, u32[]{:S(2)}) collective-permute-start(bf16[4,640,128]{2,1,0:T(8,128)(2,1)S(1)} %pad_maximum_fusion.refs_0_), channel_id=1, source_target_pairs={{0,4},{4,0},{8,12},{12,8},{16,20},{20,16},{24,28},{28,24},{1,5},{5... | collective-permute-start | bytes 1966088 | tf_op jit(solution)/shard_map/ppermute | solution.py:545
  31.3 8.0 %collective-permute-start.5 = (bf16[640,128]{1,0:T(8,128)(2,1)S(1)}, bf16[640,128]{1,0:T(8,128)(2,1)S(1)}, u32[]{:S(2)}, u32[]{:S(2)}) collective-permute-start(bf16[640,128]{1,0:T(8,128)(2,1)S(1)} %copy-done.17), channel_id=1, source_target_pairs={{0,8},{4,12},{8,16},{12,20},{16,24},{20,28},{24,0},{28,4},{1,9},{5... | collective-permute-start | bytes 491528 | tf_op jit(solution)/shard_map/ppermute | solution.py:541
  31.7 9.8 %collective-permute-start.6 = (bf16[640,128]{1,0:T(8,128)(2,1)S(1)}, bf16[640,128]{1,0:T(8,128)(2,1)S(1)}, u32[]{:S(2)}, u32[]{:S(2)}) collective-permute-start(bf16[640,128]{1,0:T(8,128)(2,1)S(1)} %copy-done.16), channel_id=1, source_target_pairs={{0,16},{4,20},{8,24},{12,28},{16,0},{20,4},{24,8},{28,12},{1,17},{... | collective-permute-start | bytes 491528 | tf_op jit(solution)/shard_map/ppermute | solution.py:541
  32.5 9.0 %collective-permute-start.7 = (bf16[640,128]{1,0:T(8,128)(2,1)S(1)}, bf16[640,128]{1,0:T(8,128)(2,1)S(1)}, u32[]{:S(2)}, u32[]{:S(2)}) collective-permute-start(bf16[640,128]{1,0:T(8,128)(2,1)S(1)} %copy-done.15), channel_id=1, source_target_pairs={{0,24},{4,28},{8,0},{12,4},{16,8},{20,12},{24,16},{28,20},{1,25},{... | collective-permute-start | bytes 491528 | tf_op jit(solution)/shard_map/ppermute | solution.py:541
  41.7 16.9 %collective-permute-start.8 = (bf16[1328,128]{1,0:T(8,128)(2,1)S(1)}, bf16[1328,128]{1,0:T(8,128)(2,1)S(1)}, u32[]{:S(2)}, u32[]{:S(2)}) collective-permute-start(bf16[1328,128]{1,0:T(8,128)(2,1)S(1)} %shard_map.150.refs_0_), channel_id=1, source_target_pairs={{0,8},{4,12},{8,0},{12,4},{16,24},{20,28},{24,16},{28,20},{1,9},{5... | collective-permute-start | bytes 1019912 | tf_op jit(solution)/shard_map/ppermute | solution.py:647
  52.2 18.5 %collective-permute-start.23 = (bf16[1216,128]{1,0:T(8,128)(2,1)S(1)}, bf16[1216,128]{1,0:T(8,128)(2,1)S(1)}, u32[]{:S(2)}, u32[]{:S(2)}) collective-permute-start(bf16[1216,128]{1,0:T(8,128)(2,1)S(1)} %get-tuple-element.81), channel_id=1, source_target_pairs={{0,2},{1,3},{2,0},{3,1},{4,6},{5,7},{6,4},{7,5},{8,10},{9,11},{10,... | collective-permute-start | bytes 933896 | tf_op jit(solution)/shard_map/ppermute | solution.py:541
  55.2 14.6 %collective-permute-start.24 = (bf16[1216,128]{1,0:T(8,128)(2,1)S(1)}, bf16[1216,128]{1,0:T(8,128)(2,1)S(1)}, u32[]{:S(2)}, u32[]{:S(2)}) collective-permute-start(bf16[1216,128]{1,0:T(8,128)(2,1)S(1)} %get-tuple-element.82), channel_id=1, source_target_pairs={{0,3},{1,0},{2,1},{3,2},{4,7},{5,4},{6,5},{7,6},{8,11},{9,8},{10,9... | collective-permute-start | bytes 933896 | tf_op jit(solution)/shard_map/ppermute | solution.py:541
  58.8 11.0 %collective-permute-start.9 = (bf16[1328,128]{1,0:T(8,128)(2,1)S(1)}, bf16[1328,128]{1,0:T(8,128)(2,1)S(1)}, u32[]{:S(2)}, u32[]{:S(2)}) collective-permute-start(bf16[1328,128]{1,0:T(8,128)(2,1)S(1)} %shard_map.151), channel_id=1, source_target_pairs={{16,0},{20,4},{24,8},{28,12},{17,1},{21,5},{25,9},{29,13},{18,2},{... | collective-permute-start | bytes 1019912 | tf_op jit(solution)/shard_map/ppermute | solution.py:647
  62.9 15.5 %collective-permute-start.22 = (bf16[1216,128]{1,0:T(8,128)(2,1)S(1)}, bf16[1216,128]{1,0:T(8,128)(2,1)S(1)}, u32[]{:S(2)}, u32[]{:S(2)}) collective-permute-start(bf16[1216,128]{1,0:T(8,128)(2,1)S(1)} %get-tuple-element.80), channel_id=1, source_target_pairs={{0,1},{1,2},{2,3},{3,0},{4,5},{5,6},{6,7},{7,4},{8,9},{9,10},{10,1... | collective-permute-start | bytes 933896 | tf_op jit(solution)/shard_map/ppermute | solution.py:541
  70.1 8.2 %collective-permute-start.10 = (bf16[1280,128]{1,0:T(8,128)(2,1)S(1)}, bf16[1280,128]{1,0:T(8,128)(2,1)S(1)}, u32[]{:S(2)}, u32[]{:S(2)}) collective-permute-start(bf16[1280,128]{1,0:T(8,128)(2,1)S(1)} %get-tuple-element.55), channel_id=1, source_target_pairs={{0,4},{4,0},{8,12},{12,8},{16,20},{20,16},{24,28},{28,24},{1,5},{5... | collective-permute-start | bytes 983048 | tf_op jit(solution)/shard_map/ppermute | solution.py:545
  78.7 5.3 %collective-permute-start.11 = (bf16[128,256]{1,0:T(8,128)(2,1)S(1)}, bf16[128,256]{1,0:T(8,128)(2,1)S(1)}, u32[]{:S(2)}, u32[]{:S(2)}) collective-permute-start(bf16[128,256]{1,0:T(8,128)(2,1)S(1)} %shard_map.156.refs_10_.refs_4_), channel_id=1, source_target_pairs={{0,8},{4,12},{8,16},{12,20},{16,24},{20,28},{24,0},{28,4},{1,9},{5... | collective-permute-start | bytes 196616 | tf_op jit(solution)/shard_map/ppermute | solution.py:541
  79.4 5.0 %collective-permute-start.12 = (bf16[128,256]{1,0:T(8,128)(2,1)S(1)}, bf16[128,256]{1,0:T(8,128)(2,1)S(1)}, u32[]{:S(2)}, u32[]{:S(2)}) collective-permute-start(bf16[128,256]{1,0:T(8,128)(2,1)S(1)} %shard_map.156.refs_10_.refs_4_), channel_id=1, source_target_pairs={{0,16},{4,20},{8,24},{12,28},{16,0},{20,4},{24,8},{28,12},{1,17},{... | collective-permute-start | bytes 196616 | tf_op jit(solution)/shard_map/ppermute | solution.py:541
  81.0 4.3 %collective-permute-start.13 = (bf16[128,256]{1,0:T(8,128)(2,1)S(1)}, bf16[128,256]{1,0:T(8,128)(2,1)S(1)}, u32[]{:S(2)}, u32[]{:S(2)}) collective-permute-start(bf16[128,256]{1,0:T(8,128)(2,1)S(1)} %shard_map.156.refs_10_.refs_4_), channel_id=1, source_target_pairs={{0,24},{4,28},{8,0},{12,4},{16,8},{20,12},{24,16},{28,20},{1,25},{... | collective-permute-start | bytes 196616 | tf_op jit(solution)/shard_map/ppermute | solution.py:541
  83.3 13.5 %collective-permute-start.25 = (bf16[3,320,128]{2,1,0:T(8,128)(2,1)S(1)}, bf16[3,320,128]{2,1,0:T(8,128)(2,1)S(1)}, u32[]{:S(2)}, u32[]{:S(2)}) collective-permute-start(bf16[3,320,128]{2,1,0:T(8,128)(2,1)S(1)} %pad_maximum_fusion.1), channel_id=1, source_target_pairs={{0,4},{4,0},{8,12},{12,8},{16,20},{20,16},{24,28},{28,24},{1,5},{5... | collective-permute-start | bytes 737288 | tf_op jit(solution)/shard_map/ppermute | solution.py:545
  88.6 10.5 %collective-permute-start.17 = (bf16[80,256]{1,0:T(8,128)(2,1)S(1)}, bf16[80,256]{1,0:T(8,128)(2,1)S(1)}, u32[]{:S(2)}, u32[]{:S(2)}) collective-permute-start(bf16[80,256]{1,0:T(8,128)(2,1)S(1)} %get-tuple-element.78), channel_id=1, source_target_pairs={{0,3},{1,0},{2,1},{3,2},{4,7},{5,4},{6,5},{7,6},{8,11},{9,8},{10,9... | collective-permute-start | bytes 122888 | tf_op jit(solution)/shard_map/ppermute | solution.py:541
  94.8 5.3 %collective-permute-start.16 = (bf16[80,256]{1,0:T(8,128)(2,1)S(1)}, bf16[80,256]{1,0:T(8,128)(2,1)S(1)}, u32[]{:S(2)}, u32[]{:S(2)}) collective-permute-start(bf16[80,256]{1,0:T(8,128)(2,1)S(1)} %get-tuple-element.77), channel_id=1, source_target_pairs={{0,2},{1,3},{2,0},{3,1},{4,6},{5,7},{6,4},{7,5},{8,10},{9,11},{10,... | collective-permute-start | bytes 122888 | tf_op jit(solution)/shard_map/ppermute | solution.py:541
  96.2 5.8 %collective-permute-start.15 = (bf16[80,256]{1,0:T(8,128)(2,1)S(1)}, bf16[80,256]{1,0:T(8,128)(2,1)S(1)}, u32[]{:S(2)}, u32[]{:S(2)}) collective-permute-start(bf16[80,256]{1,0:T(8,128)(2,1)S(1)} %get-tuple-element.76), channel_id=1, source_target_pairs={{0,1},{1,2},{2,3},{3,0},{4,5},{5,6},{6,7},{7,4},{8,9},{9,10},{10,1... | collective-permute-start | bytes 122888 | tf_op jit(solution)/shard_map/ppermute | solution.py:541
  (20 other events, 278.5 us)

commit v6 on v5

--- a/solution.py
+++ b/solution.py
@@ -85,7 +85,7 @@
         out_specs=[pl.BlockSpec(memory_space=pltpu.VMEM)] * n_out,
         scratch_shapes=list(scratch) + held,
         cost_estimate=pl.CostEstimate(
-            flops=int(cost * 1e9), bytes_accessed=1000, transcendentals=0
+            flops=int(cost * 1e5), bytes_accessed=1000, transcendentals=0
         ),
         compiler_params=pltpu.CompilerParams(vmem_limit_bytes=limit * 1024 * 1024),
     )(*args, *after)
@@ -100,22 +100,47 @@
     return lax.rem(place, 2), lax.div(place, 2), lax.axis_size("tm") // 2
 
 
-def ahead(index, shift, count):
-    return lax.rem(index + shift, count)
-
-
 def rows_at(index, size, align=16):
     return pl.ds(pl.multiple_of(index * size, align), size)
 
 
+def picked(n_dp, x_ref, dy_ref, slot_ref, count_ref, gate_ref, out_refs):
+    length, width = x_ref.shape
+    slots = slot_ref.shape[1]
+    hit = iota((length, slots), 0) == slot_ref[...]
+    live = iota((1, slots), 1) < count_ref[...]
+    weight = jnp.where(live, gate_ref[...].astype(F32), 0.0)
+    rows = dot(where_one(hit).astype(BF16), x_ref[...], 0, 0).astype(BF16)
+    grads = dot(jnp.where(hit, weight, 0.0).astype(BF16), dy_ref[...], 0, 0).astype(BF16)
+    blocks = [rows[:, t * LANES : (t + 1) * LANES] for t in range(width // LANES)]
+    piece = width // n_dp
+    for i in range(n_dp):
+        for low in range(i * piece, (i + 1) * piece, LANES):
+            block = grads[:, low : min(low + LANES, (i + 1) * piece)]
+            if block.shape[1] < LANES:
+                fill = jnp.zeros((slots, LANES - block.shape[1]), BF16)
+                block = jnp.concatenate([block, fill], axis=1)
+            blocks.append(block)
+    for i, block in enumerate(blocks):
+        for out in out_refs:
+            out[i * slots : (i + 1) * slots, :] = block
+
+
+def high_low(values):
+    high = values.astype(BF16).astype(F32)
+    return [high, values - high]
+
+
 def prep_kernel(
-    x_ref, dy_ref, ldt_ref, stept_ref, h_ref,
+    n_dp, x_ref, dy_ref, ldt_ref, stept_ref, h_ref, slot_ref, count_ref, gate_ref,
     cumt_ref, cum_ref, step_ref, dyt_ref, xs_ref, carried_ref, *rest,
 ):
     outs, xt_ref = rest[:-1], rest[-1]
     length, width = x_ref.shape
     heads = ldt_ref.shape[0]
     size = width // heads
+    _, chip, n_chip = core_and_chip()
+    picked(n_dp, x_ref, dy_ref, slot_ref, count_ref, gate_ref, outs)
     pad = jnp.zeros((LANES - heads, length), F32)
     cumt = dot(ldt_ref[...], triangle(length, lambda a, b: a <= b), 1, 0, HI)
     cumt_ref[...] = cumt
@@ -137,75 +162,69 @@
         dyt_ref[span, :] = dys.T.astype(BF16)
         carried = carried + dot(dys.astype(BF16), h_ref[span, :], 1, 0)
     carried_ref[...] = carried
-    _, chip, n_chip = core_and_chip()
+    decay = jnp.broadcast_to(jnp.exp(cumt[:, length - 1 : length]), (heads, LANES))
+    dyt_ref[width : width + 2 * heads, :] = jnp.concatenate(high_low(decay), axis=0).astype(BF16)
+    block = width // n_chip
     for s, out in enumerate(outs):
-        out[...] = xt_ref[rows_at(ahead(chip, s, n_chip), width // n_chip), :]
-
-
-def pick_kernel(n_dp, x_ref, dy_ref, slot_ref, count_ref, gate_ref, out_ref):
-    length, width = x_ref.shape
-    slots = slot_ref.shape[1]
-    hit = iota((length, slots), 0) == slot_ref[...]
-    live = iota((1, slots), 1) < count_ref[...]
-    weight = jnp.where(live, gate_ref[...].astype(F32), 0.0)
-    rows = dot(where_one(hit).astype(BF16), x_ref[...], 0, 0).astype(BF16)
-    base = width // LANES * slots
-    for t in range(width // LANES):
-        out_ref[t * slots : (t + 1) * slots, :] = rows[:, t * LANES : (t + 1) * LANES]
-    grads = dot(jnp.where(hit, weight, 0.0).astype(BF16), dy_ref[...], 0, 0).astype(BF16)
-    piece = width // n_dp
-    tiles = -(-piece // LANES)
-    if piece % LANES:
-        out_ref[base:, :] = jnp.zeros((out_ref.shape[0] - base, LANES), BF16)
-    for i in range(n_dp):
-        for t in range(tiles):
-            low, high = i * piece + t * LANES, min((i + 1) * piece, i * piece + (t + 1) * LANES)
-            row = base + (i * tiles + t) * slots
-            out_ref[row : row + slots, : high - low] = grads[:, low:high]
-
-
-def stack_kernel(*refs):
-    for i, ref in enumerate(refs[:-1]):
-        refs[-1][i] = ref[...]
-
-
-def stacked(arrays, after=()):
+        out[out.shape[0] - block :, :] = xt_ref[rows_at(chip ^ s, block), :]
+
+
+def stack_kernel(starts, *refs):
+    rows = refs[-1].shape[1]
+    for i, start in enumerate(starts):
+        refs[-1][i] = refs[i][start : start + rows, :]
+
+
+def stacked(arrays, after=(), rows=None, starts=None):
+    rows = rows or arrays[0].shape[0]
+    starts = starts or [0] * len(arrays)
     return call(
-        stack_kernel,
-        [shape((len(arrays), *arrays[0].shape), arrays[0].dtype)],
+        lambda *refs: stack_kernel(starts, *refs),
+        [shape((len(arrays), rows, arrays[0].shape[1]), arrays[0].dtype)],
         0.2,
         tuple(arrays),
         after=after,
     )[0]
 
 
-def project_kernel(n_mine, *refs):
-    x_ref, dyt_ref, cumt_ref, own_ref = refs[:4]
-    mine, other = refs[4 : 4 + n_mine], refs[4 + n_mine]
-    w_ref, bc_ref, keep_ref, send_ref = refs[5 + n_mine :]
+def join_kernel(*refs):
+    start = 0
+    for ref in refs[:-1]:
+        refs[-1][start : start + ref.shape[0]] = ref[...]
+        start += ref.shape[0]
+
+
+def joined(arrays):
+    dims = (sum(a.shape[0] for a in arrays), *arrays[0].shape[1:])
+    return call(join_kernel, [shape(dims, arrays[0].dtype)], 0.2, tuple(arrays))[0]
+
+
+def project_kernel(n_mine, many, *refs):
+    x_ref, dyt_ref, own_ref = refs[:3]
+    mine, other = refs[3 : 3 + n_mine], refs[3 + n_mine]
+    w_ref, bc_ref, keep_ref, send_ref = refs[4 + n_mine :]
     core, _, _ = core_and_chip()
     place, n_dp = lax.axis_index("dp"), lax.axis_size("dp")
     share = own_ref.shape[0]
     half = share // 2
     w_ref[rows_at(place, share), :] = own_ref[...]
     for i in range(n_mine):
-        source = ahead(place, n_dp - 1 - i, n_dp)
+        source = place ^ (i + 1)
         w_ref[rows_at(source * 2 + core, half), :] = mine[i][...]
         w_ref[rows_at(source * 2 + 1 - core, half), :] = other[i]
     bc = dot(x_ref[...], w_ref[...], 1, 0).astype(BF16)
     bc_ref[...] = bc
     c_rows = bc[:, LANES:]
-    heads, length = cumt_ref.shape
-    width = dyt_ref.shape[0]
-    part, many = width // 2, heads // 2
-    decay = jnp.broadcast_to(jnp.exp(cumt_ref[:, length - 1 : length]), (heads, LANES))
+    width = x_ref.shape[1]
+    part = width // 2
     for ref, index in ((keep_ref, core), (send_ref, 1 - core)):
         ref[:part, :] = dot(dyt_ref[rows_at(index, part), :], c_rows, 1, 0).astype(BF16)
-        mine_decay = jnp.where(index == 0, decay[:many], decay[many:])
-        high = mine_decay.astype(BF16).astype(F32)
+        table = dyt_ref[width : width + 4 * many, :].astype(F32)
+        quarter = [table[i * many : (i + 1) * many] for i in range(4)]
+        high = jnp.where(index == 0, quarter[0], quarter[1])
+        low = jnp.where(index == 0, quarter[2], quarter[3])
         fill = jnp.zeros((ref.shape[0] - part - 2 * many, LANES), F32)
-        extra = jnp.concatenate([high, mine_decay - high, fill], axis=0)
-        ref[part:, :] = extra.astype(BF16)
+        ref[part:, :] = jnp.concatenate([high, low, fill], axis=0).astype(BF16)
 
 
 def pair(keep_ref, recv_ref, many, size, head):
@@ -401,13 +420,13 @@
 
 
 def term_kernel(n_chip, *refs):
-    columns, pieces = refs[:n_chip], refs[n_chip : 2 * n_chip]
-    keep_ref, send_ref = refs[2 * n_chip : 2 * n_chip + 2]
-    held = refs[-1]
+    columns, pieces = refs[:n_chip], refs[n_chip:-3]
+    keep_ref, send_ref, held = refs[-3:]
+    pieces = [(p, i) for p in pieces for i in range(p.shape[0])]
     core, _, _ = core_and_chip()
     total = None
-    for a, b in zip(columns, pieces):
-        part = dot(a[...], b[...], 1, 0)
+    for a, (b, i) in zip(columns, pieces):
+        part = dot(a[a.shape[0] - 2 * keep_ref.shape[0] :, :], b[i], 1, 0)
         total = part if total is None else total + part
     block = keep_ref.shape[0]
     held[0] = total[:block]
@@ -425,7 +444,7 @@
         held[i] = total[i * share : (i + 1) * share]
     own_ref[...] = held[place]
     for s, out in enumerate(outs):
-        out[...] = held[ahead(place, s + 1, n_dp)].astype(BF16)
+        out[...] = held[place ^ (s + 1)].astype(BF16)
 
 
 def expert_kernel(flip, merge, slots, grad_rows, a_ref, b_ref, gate_ref, up_ref, *refs):
@@ -458,20 +477,23 @@
         place, n_dp = lax.axis_index("dp"), lax.axis_size("dp")
         base = width // LANES * slots
         hidden = gate_acc.shape[1]
-        for s in range(n_dp):
-            rows = [
-                a_ref[i, pl.ds(pl.multiple_of(base + ahead(place, s, n_dp) * grad_rows, 16), grad_rows), :]
-                for i in range(n_chip)
-            ]
-            grads = outs[s] if merge else outs[n_dp + s]
+
+        def put(out, start, target):
             for i in range(n_chip):
-                row = (hidden if merge else 0) + i * grad_rows
-                grads[row : row + grad_rows, :] = rows[i]
-            if merge:
-                outs[s][:hidden, :] = weighted
-            elif s == 0:
-                for out in outs[:n_dp]:
-                    out[...] = weighted
+                row = pl.multiple_of(base + target * grad_rows, 16)
+                to = start + i * grad_rows
+                out[to : to + grad_rows, :] = a_ref[i, pl.ds(row, grad_rows), :]
+
+        if merge:
+            grads = n_chip * grad_rows
+            for s, out in enumerate(outs):
+                out[grads : grads + hidden, :] = weighted
+                put(out, 0, place ^ s)
+            put(outs[2], grads + hidden, place ^ 3)
+        else:
+            outs[0][...] = weighted
+            for s in range(n_dp):
+                put(outs[1 + s], 0, place ^ s)
 
 
 def expert(a, b, w_gate, w_up, slots, grad_rows, n_dp, flip, merge):
@@ -483,9 +505,9 @@
     block = pl.BlockSpec((depth, hidden), lambda i: (i, 0))
     grads = n_chip * grad_rows
     if merge:
-        outs = [(hidden + grads, LANES)] * n_dp
+        outs = [(grads + hidden, LANES)] * 2 + [(2 * grads + hidden, LANES)]
     else:
-        outs = [(hidden, total) if flip else (total, hidden)] * n_dp + [(grads, LANES)] * n_dp
+        outs = [(hidden, total) if flip else (total, hidden)] + [(grads, LANES)] * n_dp
     return pl.pallas_call(
         lambda *refs: expert_kernel(flip, merge, slots, grad_rows, *refs),
         out_shape=[shape(o, BF16) for o in outs],
@@ -498,11 +520,11 @@
             pltpu.VMEM((total, hidden), F32),
         ],
         cost_estimate=pl.CostEstimate(
-            flops=4 * total * width * hidden,
-            bytes_accessed=4 * width * hidden,
+            flops=int(3e10),
+            bytes_accessed=1000,
             transcendentals=0,
         ),
-        compiler_params=pltpu.CompilerParams(vmem_limit_bytes=50 * 1024 * 1024),
+        compiler_params=pltpu.CompilerParams(vmem_limit_bytes=20 * 1024 * 1024),
     )(a, b, w_gate, w_up)
 
 
@@ -513,10 +535,12 @@
     hidden, piece = out_ref.shape
     n_chip = b_ref.shape[0]
     tiles = grad_rows // slots
+    count = n_chip * grad_rows
     place = lax.axis_index("dp")
     total = None
     for s in range(n_dp):
-        base = hidden if merge else 0
+        first = merge and s < 3
+        base = hidden if merge and not first else 0
         blocks = [
             near[s][base + i * grad_rows : base + (i + 1) * grad_rows, :] for i in range(n_chip)
         ]
@@ -531,22 +555,31 @@
             for t in range(tiles)
         ]
         grads = jnp.concatenate(columns, axis=1)[:, :piece]
-        part = dot(weighted[s][:hidden, :] if merge else weighted[s][...], grads, 1 if flip else 0, 0)
+        low = count if first else 0
+        left = weighted[s][low : low + hidden, :] if merge else weighted[s][...]
+        part = dot(left, grads, 1 if flip else 0, 0)
         total = part if total is None else total + part
     out_ref[...] = total.astype(BF16)
 
 
-def shifted(array, axis, shift, stride=1):
+def xored(array, axis, mask):
     count = lax.axis_size(axis)
-    return lax.ppermute(array, axis, [(i, (i + shift * stride) % count) for i in range(count)])
+    return lax.ppermute(array, axis, [(i, i ^ mask) for i in range(count)])
 
 
 def swapped(array):
-    return lax.ppermute(array, "tm", [(i, i ^ 1) for i in range(lax.axis_size("tm"))])
+    return xored(array, "tm", 1)
 
 
 def chips(arrays):
-    return [arrays[0]] + [shifted(a, "tm", s + 1, 2) for s, a in enumerate(arrays[1:])]
+    return [arrays[0]] + [xored(a, "tm", 2 * s) for s, a in enumerate(arrays) if s]
+
+
+def gathered(array, axis, count):
+    if count == 1:
+        return [array]
+    far = xored(array, axis, count // 2)
+    return gathered(array, axis, count // 2) + gathered(far, axis, count // 2)
 
 
 def per_device(
@@ -579,45 +612,36 @@
     part = width // 2
     many = heads // 2
     flip = w_gate.shape[2] % LANES == 0
-    merge = flip and 2 * n_chip * capacity == LANES
+    merge = flip and 2 * n_chip * capacity == LANES and n_dp == 4
 
     grad_rows = -(-piece // LANES) * capacity
     w_half = lax.dynamic_slice_in_dim(w_bc, core * (share // 2), share // 2, 0)
-    mine = [shifted(w_half, "dp", s) for s in range(1, n_dp)]
-
-    rows = call(
-        lambda *refs: pick_kernel(n_dp, *refs),
-        [shape((width // LANES * capacity + n_dp * grad_rows, LANES), BF16)],
-        0.5,
-        (x, dy, slot_rows[0], slot_counts, slot_gates[0]),
-        fetch=(0, 1),
-        limit=60,
-    )[0]
-    rows_a = jnp.stack(chips([rows] * n_chip))
-    rows_b = swapped(rows_a)
-
-    cumt, cum, steps, dyt, xs, carried, *xt = call(
-        prep_kernel,
+    mine = gathered(w_half, "dp", n_dp)[1:]
+
+    n_rows = width // LANES * capacity + n_dp * grad_rows
+    cumt, cum, steps, dyt, xs, carried, *sends = call(
+        lambda *refs: prep_kernel(n_dp, *refs),
         [
             shape((heads, length), F32),
             shape((length, LANES), F32),
             shape((length, LANES), F32),
-            shape((width, length), BF16),
+            shape((width + up16(2 * heads), length), BF16),
             shape((length, width), BF16),
             shape((length, half), F32),
         ]
-        + [shape((width // n_chip, length), BF16)] * n_chip,
+        + [shape((n_rows + width // n_chip, length), BF16)] * n_chip,
         2.0,
-        (x, dy, ldt, stept, h_in),
-        after=(rows,),
+        (x, dy, ldt, stept, h_in, slot_rows[0], slot_counts, slot_gates[0]),
         scratch=[pltpu.VMEM((width, length), BF16)],
         fetch=(0, 1, 2, 3, 4),
         limit=60,
     )
-    columns_in = chips(xt)
+    arrivals = chips(sends)
     other = swapped(stacked(mine, after=(cumt,)))
+    rows_a = stacked(arrivals, rows=n_rows)
+    rows_b = swapped(rows_a)
     w_whole, bc, keep, send = call(
-        lambda *refs: project_kernel(n_dp - 1, *refs),
+        lambda *refs: project_kernel(n_dp - 1, many, *refs),
         [
             shape((width, columns), BF16),
             shape((length, columns), BF16),
@@ -625,7 +649,7 @@
             shape((part + up16(2 * many), half), BF16),
         ],
         1.0,
-        (x, dyt, cumt, w_bc, *mine, other),
+        (x, dyt, w_bc, *mine, other),
     )
     recv = swapped(send)
     climbs = [
@@ -634,9 +658,11 @@
             [shape((part + up16(2 * many), half), BF16)],
             0.5,
             (keep, recv),
-            after=tuple(columns_in[1:]),
+            after=tuple(arrivals[1:]),
         )[0]
     ]
+    outs = expert(rows_a, rows_b, w_gate[0], w_up[0], capacity, grad_rows, n_dp, flip, merge)
+    outs = list(outs)
     arrived = []
     bit = 1
     while bit < n_chip:
@@ -652,17 +678,20 @@
                     [shape((part + up16(2 * many), half), BF16)],
                     0.5,
                     (climbs[-1], arrived[-1]),
+                    after=(outs[0],),
                 )[0]
             )
         bit *= 2
 
-    outs = expert(rows_a, rows_b, w_gate[0], w_up[0], capacity, grad_rows, n_dp, flip, merge)
-    outs = list(outs)
-    spread = outs[:1] + [shifted(o, "dp", s + 1) for s, o in enumerate(outs[1:n_dp])]
-    near = outs[n_dp : n_dp + 1]
-    near += [shifted(o, "dp", s + 1) for s, o in enumerate(outs[n_dp + 1 :])]
-    moved = [o[w_gate.shape[2] :] for o in spread[1:]] if merge else near[1:]
-    far = swapped(jnp.stack(moved))
+    if merge:
+        near_rows = n_chip * grad_rows
+        arrived_2 = xored(outs[2], "dp", 2)
+        spread = [outs[0], xored(outs[1], "dp", 1), arrived_2]
+        spread.append(xored(arrived_2[near_rows:], "dp", 1))
+        near = spread
+    else:
+        spread = gathered(outs[0], "dp", n_dp)
+        near = outs[1:2] + [xored(o, "dp", s + 1) for s, o in enumerate(outs[2:])]
 
     parts = 2
     tiles = width // LANES // parts
@@ -696,10 +725,15 @@
         [shape((part, half), BF16)] * 2,
         0.5,
         (*arrived, keep, recv),
+        after=(dc,),
     )
     r_recv = swapped(r_send)
     d_bc = call(db_kernel, [shape((length, columns), BF16)], 0.3, (xs, r_own, r_recv, db, dc))[0]
-    d_bcs = chips([d_bc] * n_chip)
+    d_bcs = [d_bc.reshape(1, length, columns)]
+    while 2 ** (len(d_bcs) - 1) < n_chip:
+        level = 2 ** (len(d_bcs) - 1)
+        sent = d_bcs[0] if level == 1 else joined(d_bcs)
+        d_bcs.append(xored(sent, "tm", 2 * level))
     d_in, d_decay, d_step = call(
         lambda *refs: finish_kernel(parts, *refs),
         [
@@ -717,7 +751,8 @@
         lambda *refs: term_kernel(n_chip, *refs),
         [shape((w_rows, columns), F32), shape((w_rows, columns), BF16)],
         0.5,
-        (*columns_in, *d_bcs),
+        (*arrivals, *d_bcs),
+        after=(d_in,),
         scratch=[pltpu.VMEM((2, w_rows, columns), F32)],
     )
     final = call(
@@ -730,13 +765,15 @@
     )
     w_bc_grad = final[0]
     for s in range(1, n_dp):
-        w_bc_grad = w_bc_grad + shifted(final[s], "dp", s).astype(F32)
-
+        w_bc_grad = w_bc_grad + xored(final[s], "dp", s).astype(F32)
+
+    starts = [0, 0, w_gate.shape[2]] if merge else None
+    far = swapped(stacked(near[1:], after=(term,), rows=n_chip * grad_rows, starts=starts))
     w_down_grad = call(
         lambda *refs: down_kernel(n_dp, flip, merge, capacity, grad_rows, *refs),
         [shape((w_gate.shape[2], piece), BF16)],
         1.0,
-        (*spread, *near, rows_b, far),
+        (*spread, *([] if merge else near), rows_b, far),
         after=(final[0],),
     )[0]
     return (d_in[None], d_decay.T[None], d_step.T[None], w_bc_grad, w_down_grad[None])

time: 103 us -> 106 us (1.029)
  waiting for transfers between devices: 32.9 us -> 51 us
  starting transfers between devices: 36.6 us -> 23.5 us
  Pallas kernels: 27.1 us -> 21.5 us
  local copies, waits for them, and re-layouts: 3.57 us -> 7.27 us
    ppermute x24 -> x20, starting transfers between devices: 33.7 us -> 20.7 us  [xored(): return lax.ppermute(array, axis, [(i, i ^ mask) for i in range(count)])]
    ppermute x24 -> x20, waiting for transfers between devices: 32.9 us -> 42.6 us  [xored(): return lax.ppermute(array, axis, [(i, i ^ mask) for i in range(count)])]
    ppermute x2, waiting for transfers between devices: 0.01 us -> 8.44 us  [per_device(): arrived.append(lax.ppermute(climbs[-1], 'tm', moves))]
    unnamed x36 -> x32, local copies, waits for them, and re-layouts: 2.62 us -> 6.23 us
    pallas_call x1, Pallas kernels: 6.17 us -> 2.66 us  [expert(): pl.pallas_call(lambda *refs: expert_kernel(flip, merge, slots, grad_rows,...]
    pallas_call x15 -> x17, Pallas kernels: 20.9 us -> 18.8 us  [call(): pl.pallas_call(body, out_shape=outs, in_specs=specs + [pl.BlockSpec(memor...]
  transfers between devices with their start and end apart: 26 -> 22, of which waited for: 13 -> 13; matrix products, arithmetic and copies ran while one was open for 0% -> 1% of each run, Pallas kernels for 26% -> 18%
where the time goes in v6:
time: 106 us
  waiting for transfers between devices  51 us (48%)
  starting transfers between devices  23.5 us (22%)
  Pallas kernels  21.5 us (20%)
  local copies, waits for them, and re-layouts  7.27 us (7%)
  between operations  1.61 us (2%)
    ppermute x20, waiting for transfers between devices, xored(): return lax.ppermute(array, axis, [(i, i ^ mask) for i in range(count)])  42.6 us
    ppermute x20, starting transfers between devices, xored(): return lax.ppermute(array, axis, [(i, i ^ mask) for i in range(count)])  20.7 us
    pallas_call x17, Pallas kernels, call(): pl.pallas_call(body, out_shape=outs, in_specs=specs + [pl.BlockSpec(memor...  18.8 us
    ppermute x2, waiting for transfers between devices, per_device(): arrived.append(lax.ppermute(climbs[-1], 'tm', moves))  8.44 us
    unnamed x32, local copies, waits for them, and re-layouts  6.23 us
    ppermute x2, starting transfers between devices, per_device(): arrived.append(lax.ppermute(climbs[-1], 'tm', moves))  2.78 us
    pallas_call x1, Pallas kernels, expert(): pl.pallas_call(lambda *refs: expert_kernel(flip, merge, slots, grad_rows,...  2.66 us
  transfers between devices with their start and end apart: 22, of which 13 were waited for; matrix products, arithmetic and copies ran while one was open for 1% of the time, Pallas kernels for 18%

profile of v6, /device:TPU:0, one launch (start us, length us, event | category | flops | bytes accessed | tf_op | source)
XLA Modules:
  0.0 105.5 jit_solution(15643430806202011491)
XLA Ops:
  1.7 4.1 %collective-permute-start.1 = (bf16[320,256]{1,0:T(8,128)(2,1)S(1)}, bf16[320,256]{1,0:T(8,128)(2,1)S(1)}, u32[]{:S(2)}, u32[]{:S(2)}) collective-permute-start(bf16[320,256]{1,0:T(8,128)(2,1)S(1)} %constant_dynamic-slice_fusion), channel_id=1, source_target_pairs={{0,2},{1,3},{2,0},{3,1},{4,6},{5,7},{6,4},{7,5},{8,10},{9,11},{10,... | collective-permute-start | bytes 491528 | tf_op jit(solution)/shard_map/ppermute | solution.py:567
  5.8 1.6 %collective-permute-start = (bf16[320,256]{1,0:T(8,128)(2,1)S(1)}, bf16[320,256]{1,0:T(8,128)(2,1)S(1)}, u32[]{:S(2)}, u32[]{:S(2)}) collective-permute-start(bf16[320,256]{1,0:T(8,128)(2,1)S(1)} %constant_dynamic-slice_fusion), channel_id=1, source_target_pairs={{0,1},{1,0},{2,3},{3,2},{4,5},{5,4},{6,7},{7,6},{8,9},{9,8},{10,11... | collective-permute-start | bytes 491528 | tf_op jit(solution)/shard_map/ppermute | solution.py:567
  7.4 6.2 %collective-permute-done.1.refs_1_.refs_4_ = bf16[320,256]{1,0:T(8,128)(2,1)S(1)} collective-permute-done((bf16[320,256]{1,0:T(8,128)(2,1)S(1)}, bf16[320,256]{1,0:T(8,128)(2,1)S(1)}, u32[]{:S(2)}, u32[]{:S(2)}) %collective-permute-start.1) | collective-permute-done | bytes 163872 | tf_op jit(solution)/shard_map/ppermute | solution.py:567
  14.9 5.8 %shard_map.146 = (f32[40,128]{1,0:T(8,128)}, f32[128,128]{1,0:T(8,128)}, f32[128,128]{1,0:T(8,128)}, bf16[2640,128]{1,0:T(8,128)(2,1)}, bf16[128,2560]{1,0:T(8,1...) custom-call(bf16[128,2560]{1,0:T(8,128)(2,1)} %bitcast.22, ...), custom_call_target="tpu_custom_call" | custom-call | flops 200000 | bytes 1000 | tf_op jit(solution)/shard_map/pallas_call | solution.py:81
  20.7 1.6 %collective-permute-start.5 = (bf16[1280,128]{1,0:T(8,128)(2,1)}, bf16[1280,128]{1,0:T(8,128)(2,1)S(1)}, u32[]{:S(2)}, u32[]{:S(2)}) collective-permute-start(bf16[1280,128]{1,0:T(8,128)(2,1)} %get-tuple-element.50), channel_id=1, source_target_pairs={{0,8},{4,12},{8,0},{12,4},{16,24},{20,28},{24,16},{28,20},{1,9},{5... | collective-permute-start | bytes 983048 | tf_op jit(solution)/shard_map/ppermute | solution.py:567
  22.2 1.5 %collective-permute-start.6 = (bf16[1280,128]{1,0:T(8,128)(2,1)}, bf16[1280,128]{1,0:T(8,128)(2,1)S(1)}, u32[]{:S(2)}, u32[]{:S(2)}) collective-permute-start(bf16[1280,128]{1,0:T(8,128)(2,1)} %get-tuple-element.51), channel_id=1, source_target_pairs={{0,16},{4,20},{8,24},{12,28},{16,0},{20,4},{24,8},{28,12},{1,17},{... | collective-permute-start | bytes 983048 | tf_op jit(solution)/shard_map/ppermute | solution.py:567
  25.1 6.5 %collective-permute-done.5.refs_2_.refs_1_ = bf16[1280,128]{1,0:T(8,128)(2,1)S(1)} collective-permute-done((bf16[1280,128]{1,0:T(8,128)(2,1)}, bf16[1280,128]{1,0:T(8,128)(2,1)S(1)}, u32[]{:S(2)}, u32[]{:S(2)}) %collective-permute-start.5) | collective-permute-done | bytes 327712 | tf_op jit(solution)/shard_map/ppermute | solution.py:567
  31.6 7.0 %collective-permute-done.6.refs_3_.refs_2_ = bf16[1280,128]{1,0:T(8,128)(2,1)S(1)} collective-permute-done((bf16[1280,128]{1,0:T(8,128)(2,1)}, bf16[1280,128]{1,0:T(8,128)(2,1)S(1)}, u32[]{:S(2)}, u32[]{:S(2)}) %collective-permute-start.6) | collective-permute-done | bytes 327712 | tf_op jit(solution)/shard_map/ppermute | solution.py:567
  45.1 2.3 %copy-done.15 = bf16[1,2560,896]{2,1,0:T(8,128)(2,1)S(1)} copy-done((bf16[1,2560,896]{2,1,0:T(8,128)(2,1)S(1)}, bf16[1,2560,896]{2,1,0:T(8,128)(2,1)}, u32[]{:S(2)}) %copy-start.15) | copy-done | bytes 4587544
  47.5 2.7 %shard_map.151 = (bf16[1216,128]{1,0:T(8,128)(2,1)S(1)}, bf16[1216,128]{1,0:T(8,128)(2,1)S(1)}, bf16[1536,128]{1,0:T(8,128)(2,1)S(1)}) custom-call(bf16[4,640,128]{2,1,0:T(8,128)(2,1)S(1)} %shard_map.150.refs_0_, bf16[4,640,128]{2,1,0:T(8,128)(2,1)S(1)} %collective-permute-done.9.refs_1_.refs_4_, bf16[2560,896]{1,0:T(8,128)(2,1)S(1)} %bitcast.40, ...), custom_call_target="tpu_custom_call" | custom-call | flops 30000001024 | bytes 1000 | tf_op jit(solution)/shard_map/pallas_call | solution.py:511
  50.1 4.0 %collective-permute-done.8.refs_1_.refs_0_ = bf16[1328,128]{1,0:T(8,128)(2,1)S(1)} collective-permute-done((bf16[1328,128]{1,0:T(8,128)(2,1)S(1)}, bf16[1328,128]{1,0:T(8,128)(2,1)S(1)}, u32[]{:S(2)}, u32[]{:S(2)}) %collective-permute-start.8) | collective-permute-done | bytes 340000 | tf_op jit(solution)/shard_map/ppermute | solution.py:673
  54.3 1.5 %collective-permute-start.10 = (bf16[1328,128]{1,0:T(8,128)(2,1)S(1)}, bf16[1328,128]{1,0:T(8,128)(2,1)S(1)}, u32[]{:S(2)}, u32[]{:S(2)}) collective-permute-start(bf16[1328,128]{1,0:T(8,128)(2,1)S(1)} %shard_map.152), channel_id=1, source_target_pairs={{16,0},{20,4},{24,8},{28,12},{17,1},{21,5},{25,9},{29,13},{18,2},{... | collective-permute-start | bytes 1019912 | tf_op jit(solution)/shard_map/ppermute | solution.py:673
  55.9 2.6 %shard_map.153 = (f32[128,1280]{1,0:T(8,128)S(1)}, f32[128,128]{1,0:T(8,128)S(1)}, f32[20,128]{1,0:T(8,128)S(1)}, f32[20,128]{1,0:T(8,128)S(1)}) custom-call(bf16[128,2560]{1,0:T(8,128)(2,1)S(1)} %bitcast.24, bf16[128,2560]{1,0:T(8,128)(2,1)S(1)} %bitcast.32, bf16[128,256]{1,0:T(8,128)(2,1)S(1)} %get-tuple-element.45.refs_2_.refs_1_, ...), custom_call_target="tpu_custom_call" | custom-call | flops 300000 | bytes 1000 | tf_op jit(solution)/shard_map/pallas_call | solution.py:81
  58.4 2.5 %shard_map.154 = (f32[128,1280]{1,0:T(8,128)S(1)}, f32[128,128]{1,0:T(8,128)S(1)}, f32[20,128]{1,0:T(8,128)S(1)}, f32[20,128]{1,0:T(8,128)S(1)}) custom-call(bf16[128,2560]{1,0:T(8,128)(2,1)S(1)} %bitcast.25, bf16[128,2560]{1,0:T(8,128)(2,1)S(1)} %bitcast.33, bf16[128,256]{1,0:T(8,128)(2,1)S(1)} %get-tuple-element.45.refs_2_.refs_1_, ...), custom_call_target="tpu_custom_call" | custom-call | flops 300000 | bytes 1000 | tf_op jit(solution)/shard_map/pallas_call | solution.py:81
  61.2 4.4 %collective-permute-done.10.refs_1_ = bf16[1328,128]{1,0:T(8,128)(2,1)S(1)} collective-permute-done((bf16[1328,128]{1,0:T(8,128)(2,1)S(1)}, bf16[1328,128]{1,0:T(8,128)(2,1)S(1)}, u32[]{:S(2)}, u32[]{:S(2)}) %collective-permute-start.10) | collective-permute-done | bytes 340000 | tf_op jit(solution)/shard_map/ppermute | solution.py:673
  66.1 3.4 %collective-permute-start.19 = (bf16[1536,128]{1,0:T(8,128)(2,1)S(1)}, bf16[1536,128]{1,0:T(8,128)(2,1)S(1)}, u32[]{:S(2)}, u32[]{:S(2)}) collective-permute-start(bf16[1536,128]{1,0:T(8,128)(2,1)S(1)} %get-tuple-element.80), channel_id=1, source_target_pairs={{0,2},{1,3},{2,0},{3,1},{4,6},{5,7},{6,4},{7,5},{8,10},{9,11},{10,... | collective-permute-start | bytes 1179656 | tf_op jit(solution)/shard_map/ppermute | solution.py:567
  71.2 3.0 %collective-permute-done.12.refs_1_.refs_5_ = bf16[1,128,256]{2,1,0:T(8,128)(2,1)S(1)} collective-permute-done((bf16[1,128,256]{2,1,0:T(8,128)(2,1)S(1)}, bf16[1,128,256]{2,1,0:T(8,128)(2,1)S(1)}, u32[]{:S(2)}, u32[]{:S(2)}) %collective-permute-start.12) | collective-permute-done | bytes 65568 | tf_op jit(solution)/shard_map/ppermute | solution.py:567
  74.6 12.9 %collective-permute-done.19.refs_1_.refs_2_ = bf16[1536,128]{1,0:T(8,128)(2,1)S(1)} collective-permute-done((bf16[1536,128]{1,0:T(8,128)(2,1)S(1)}, bf16[1536,128]{1,0:T(8,128)(2,1)S(1)}, u32[]{:S(2)}, u32[]{:S(2)}) %collective-permute-start.19) | collective-permute-done | bytes 393248 | tf_op jit(solution)/shard_map/ppermute | solution.py:567
  87.6 2.5 %shard_map.158 = (bf16[128,2560]{1,0:T(8,128)(2,1)}, f32[40,128]{1,0:T(8,128)}, f32[40,128]{1,0:T(8,128)}) custom-call(bf16[128,2560]{1,0:T(8,128)(2,1)S(1)} %bitcast.26, bf16[128,256]{1,0:T(8,128)(2,1)S(1)} %get-tuple-element.45.refs_2_.refs_1_, f32[40,128]{1,0:T(8,128)S(1)} %copy-done.11, f32[40,128]{1,0:T(8,128)S(1)} %bitcast.39, ...), custom_call_target="tpu_custom_call" | custom-call | flops 300000 | bytes 1000 | tf_op jit(solution)/shard_map/pallas_call | solution.py:81
  93.4 2.1 %collective-permute-start.15 = (bf16[80,256]{1,0:T(8,128)(2,1)S(1)}, bf16[80,256]{1,0:T(8,128)(2,1)S(1)}, u32[]{:S(2)}, u32[]{:S(2)}) collective-permute-start(bf16[80,256]{1,0:T(8,128)(2,1)S(1)} %get-tuple-element.76), channel_id=1, source_target_pairs={{0,1},{1,0},{2,3},{3,2},{4,5},{5,4},{6,7},{7,6},{8,9},{9,8},{10,11... | collective-permute-start | bytes 122888 | tf_op jit(solution)/shard_map/ppermute | solution.py:567
  96.7 1.4 %collective-permute-start.17 = (bf16[80,256]{1,0:T(8,128)(2,1)S(1)}, bf16[80,256]{1,0:T(8,128)(2,1)S(1)}, u32[]{:S(2)}, u32[]{:S(2)}) collective-permute-start(bf16[80,256]{1,0:T(8,128)(2,1)S(1)} %get-tuple-element.78), channel_id=1, source_target_pairs={{0,3},{1,2},{2,1},{3,0},{4,7},{5,6},{6,5},{7,4},{8,11},{9,10},{10,... | collective-permute-start | bytes 122888 | tf_op jit(solution)/shard_map/ppermute | solution.py:567
  98.8 2.1 %collective-permute-done.16 = bf16[80,256]{1,0:T(8,128)(2,1)S(1)} collective-permute-done((bf16[80,256]{1,0:T(8,128)(2,1)S(1)}, bf16[80,256]{1,0:T(8,128)(2,1)S(1)}, u32[]{:S(2)}, u32[]{:S(2)}) %collective-permute-start.16) | collective-permute-done | bytes 40992 | tf_op jit(solution)/shard_map/ppermute | solution.py:567
  100.9 1.6 %collective-permute-done.17 = bf16[80,256]{1,0:T(8,128)(2,1)S(1)} collective-permute-done((bf16[80,256]{1,0:T(8,128)(2,1)S(1)}, bf16[80,256]{1,0:T(8,128)(2,1)S(1)}, u32[]{:S(2)}, u32[]{:S(2)}) %collective-permute-start.17) | collective-permute-done | bytes 40992 | tf_op jit(solution)/shard_map/ppermute | solution.py:567
  103.2 2.4 %shard_map.163 = bf16[896,640]{1,0:T(8,128)(2,1)} custom-call(bf16[1216,128]{1,0:T(8,128)(2,1)S(1)} %get-tuple-element.54.refs_2_.refs_0_, bf16[1216,128]{1,0:T(8,128)(2,1)S(1)} %collective-permute-done.18.refs_0_.refs_1_, bf16[1536,128]{1,0:T(8,128)(2,1)S(1)} %collective-permute-done.19.refs_1_.refs_2_, ...), custom_call_target="tpu_custom_call" | custom-call | flops 100000 | bytes 1000 | tf_op jit(solution)/shard_map/pallas_call | solution.py:81
  (74 shorter events, 18.3 us)
Async XLA Ops:
  0.6 39.0 %copy-start.5 = (bf16[640,256]{1,0:T(8,128)(2,1)S(1)}, bf16[640,256]{1,0:T(8,128)(2,1)}, u32[]{:S(2)}) copy-start(bf16[640,256]{1,0:T(8,128)(2,1)} %refs_2_.1) | copy-start | bytes 983044
  0.6 39.0 %copy-start = (bf16[1,128,2560]{2,1,0:T(8,128)(2,1)S(1)}, bf16[1,128,2560]{2,1,0:T(8,128)(2,1)}, u32[]{:S(2)}) copy-start(bf16[1,128,2560]{2,1,0:T(8,128)(2,1)} %param.11) | copy-start | bytes 1966084
  1.7 11.9 %collective-permute-start.1 = (bf16[320,256]{1,0:T(8,128)(2,1)S(1)}, bf16[320,256]{1,0:T(8,128)(2,1)S(1)}, u32[]{:S(2)}, u32[]{:S(2)}) collective-permute-start(bf16[320,256]{1,0:T(8,128)(2,1)S(1)} %constant_dynamic-slice_fusion), channel_id=1, source_target_pairs={{0,2},{1,3},{2,0},{3,1},{4,6},{5,7},{6,4},{7,5},{8,10},{9,11},{10,... | collective-permute-start | bytes 491528 | tf_op jit(solution)/shard_map/ppermute | solution.py:567
  5.8 18.5 %collective-permute-start = (bf16[320,256]{1,0:T(8,128)(2,1)S(1)}, bf16[320,256]{1,0:T(8,128)(2,1)S(1)}, u32[]{:S(2)}, u32[]{:S(2)}) collective-permute-start(bf16[320,256]{1,0:T(8,128)(2,1)S(1)} %constant_dynamic-slice_fusion), channel_id=1, source_target_pairs={{0,1},{1,0},{2,3},{3,2},{4,5},{5,4},{6,7},{7,6},{8,9},{9,8},{10,11... | collective-permute-start | bytes 491528 | tf_op jit(solution)/shard_map/ppermute | solution.py:567
  13.6 10.7 %collective-permute-start.2 = (bf16[320,256]{1,0:T(8,128)(2,1)S(1)}, bf16[320,256]{1,0:T(8,128)(2,1)S(1)}, u32[]{:S(2)}, u32[]{:S(2)}) collective-permute-start(bf16[320,256]{1,0:T(8,128)(2,1)S(1)} %collective-permute-done.1.refs_1_.refs_4_), channel_id=1, source_target_pairs={{0,1},{1,0},{2,3},{3,2},{4,5},{5,4},{6,7},{7,6},{8,9},{9,8},{10,11... | collective-permute-start | bytes 491528 | tf_op jit(solution)/shard_map/ppermute | solution.py:567
  20.7 10.9 %collective-permute-start.5 = (bf16[1280,128]{1,0:T(8,128)(2,1)}, bf16[1280,128]{1,0:T(8,128)(2,1)S(1)}, u32[]{:S(2)}, u32[]{:S(2)}) collective-permute-start(bf16[1280,128]{1,0:T(8,128)(2,1)} %get-tuple-element.50), channel_id=1, source_target_pairs={{0,8},{4,12},{8,0},{12,4},{16,24},{20,28},{24,16},{28,20},{1,9},{5... | collective-permute-start | bytes 983048 | tf_op jit(solution)/shard_map/ppermute | solution.py:567
  22.2 16.3 %collective-permute-start.6 = (bf16[1280,128]{1,0:T(8,128)(2,1)}, bf16[1280,128]{1,0:T(8,128)(2,1)S(1)}, u32[]{:S(2)}, u32[]{:S(2)}) collective-permute-start(bf16[1280,128]{1,0:T(8,128)(2,1)} %get-tuple-element.51), channel_id=1, source_target_pairs={{0,16},{4,20},{8,24},{12,28},{16,0},{20,4},{24,8},{28,12},{1,17},{... | collective-permute-start | bytes 983048 | tf_op jit(solution)/shard_map/ppermute | solution.py:567
  23.8 14.8 %collective-permute-start.7 = (bf16[1280,128]{1,0:T(8,128)(2,1)}, bf16[1280,128]{1,0:T(8,128)(2,1)S(1)}, u32[]{:S(2)}, u32[]{:S(2)}) collective-permute-start(bf16[1280,128]{1,0:T(8,128)(2,1)} %get-tuple-element.52), channel_id=1, source_target_pairs={{0,24},{4,28},{8,16},{12,20},{16,8},{20,12},{24,0},{28,4},{1,25},{... | collective-permute-start | bytes 983048 | tf_op jit(solution)/shard_map/ppermute | solution.py:567
  25.0 14.6 %collective-permute-start.3 = (bf16[3,320,256]{2,1,0:T(8,128)(2,1)S(1)}, bf16[3,320,256]{2,1,0:T(8,128)(2,1)S(1)}, u32[]{:S(2)}, u32[]{:S(2)}) collective-permute-start(bf16[3,320,256]{2,1,0:T(8,128)(2,1)S(1)} %shard_map.147), channel_id=1, source_target_pairs={{0,4},{4,0},{8,12},{12,8},{16,20},{20,16},{24,28},{28,24},{1,5},{5... | collective-permute-start | bytes 1474568 | tf_op jit(solution)/shard_map/ppermute | solution.py:567
  39.6 5.6 %collective-permute-start.9 = (bf16[4,640,128]{2,1,0:T(8,128)(2,1)S(1)}, bf16[4,640,128]{2,1,0:T(8,128)(2,1)S(1)}, u32[]{:S(2)}, u32[]{:S(2)}) collective-permute-start(bf16[4,640,128]{2,1,0:T(8,128)(2,1)S(1)} %shard_map.150.refs_0_), channel_id=1, source_target_pairs={{0,4},{4,0},{8,12},{12,8},{16,20},{20,16},{24,28},{28,24},{1,5},{5... | collective-permute-start | bytes 1966088 | tf_op jit(solution)/shard_map/ppermute | solution.py:567
  41.8 1.8 %collective-permute-start.4 = (bf16[1328,128]{1,0:T(8,128)(2,1)S(1)}, bf16[1328,128]{1,0:T(8,128)(2,1)S(1)}, u32[]{:S(2)}, u32[]{:S(2)}) collective-permute-start(bf16[1328,128]{1,0:T(8,128)(2,1)S(1)} %get-tuple-element.49), channel_id=1, source_target_pairs={{0,4},{4,0},{8,12},{12,8},{16,20},{20,16},{24,28},{28,24},{1,5},{5... | collective-permute-start | bytes 1019912 | tf_op jit(solution)/shard_map/ppermute | solution.py:567
  43.8 10.3 %collective-permute-start.8 = (bf16[1328,128]{1,0:T(8,128)(2,1)S(1)}, bf16[1328,128]{1,0:T(8,128)(2,1)S(1)}, u32[]{:S(2)}, u32[]{:S(2)}) collective-permute-start(bf16[1328,128]{1,0:T(8,128)(2,1)S(1)} %shard_map.149.refs_0_), channel_id=1, source_target_pairs={{0,8},{4,12},{8,0},{12,4},{16,24},{20,28},{24,16},{28,20},{1,9},{5... | collective-permute-start | bytes 1019912 | tf_op jit(solution)/shard_map/ppermute | solution.py:673
  54.3 11.3 %collective-permute-start.10 = (bf16[1328,128]{1,0:T(8,128)(2,1)S(1)}, bf16[1328,128]{1,0:T(8,128)(2,1)S(1)}, u32[]{:S(2)}, u32[]{:S(2)}) collective-permute-start(bf16[1328,128]{1,0:T(8,128)(2,1)S(1)} %shard_map.152), channel_id=1, source_target_pairs={{16,0},{20,4},{24,8},{28,12},{17,1},{21,5},{25,9},{29,13},{18,2},{... | collective-permute-start | bytes 1019912 | tf_op jit(solution)/shard_map/ppermute | solution.py:673
  66.0 3.5 %collective-permute-start.11 = (bf16[1280,128]{1,0:T(8,128)(2,1)S(1)}, bf16[1280,128]{1,0:T(8,128)(2,1)S(1)}, u32[]{:S(2)}, u32[]{:S(2)}) collective-permute-start(bf16[1280,128]{1,0:T(8,128)(2,1)S(1)} %get-tuple-element.60), channel_id=1, source_target_pairs={{0,4},{4,0},{8,12},{12,8},{16,20},{20,16},{24,28},{28,24},{1,5},{5... | collective-permute-start | bytes 983048 | tf_op jit(solution)/shard_map/ppermute | solution.py:567
  66.1 21.4 %collective-permute-start.19 = (bf16[1536,128]{1,0:T(8,128)(2,1)S(1)}, bf16[1536,128]{1,0:T(8,128)(2,1)S(1)}, u32[]{:S(2)}, u32[]{:S(2)}) collective-permute-start(bf16[1536,128]{1,0:T(8,128)(2,1)S(1)} %get-tuple-element.80), channel_id=1, source_target_pairs={{0,2},{1,3},{2,0},{3,1},{4,6},{5,7},{6,4},{7,5},{8,10},{9,11},{10,... | collective-permute-start | bytes 1179656 | tf_op jit(solution)/shard_map/ppermute | solution.py:567
  69.9 4.3 %collective-permute-start.12 = (bf16[1,128,256]{2,1,0:T(8,128)(2,1)S(1)}, bf16[1,128,256]{2,1,0:T(8,128)(2,1)S(1)}, u32[]{:S(2)}, u32[]{:S(2)}) collective-permute-start(bf16[1,128,256]{2,1,0:T(8,128)(2,1)S(1)} %bitcast.34), channel_id=1, source_target_pairs={{0,8},{4,12},{8,0},{12,4},{16,24},{20,28},{24,16},{28,20},{1,9},{5... | collective-permute-start | bytes 196616 | tf_op jit(solution)/shard_map/ppermute | solution.py:567
  74.2 15.9 %collective-permute-start.13 = (bf16[2,128,256]{2,1,0:T(8,128)(2,1)S(1)}, bf16[2,128,256]{2,1,0:T(8,128)(2,1)S(1)}, u32[]{:S(2)}, u32[]{:S(2)}) collective-permute-start(bf16[2,128,256]{2,1,0:T(8,128)(2,1)S(1)} %shard_map.159), channel_id=1, source_target_pairs={{0,16},{4,20},{8,24},{12,28},{16,0},{20,4},{24,8},{28,12},{1,17},{... | collective-permute-start | bytes 393224 | tf_op jit(solution)/shard_map/ppermute | solution.py:567
  74.3 23.8 %collective-permute-start.18 = (bf16[1216,128]{1,0:T(8,128)(2,1)S(1)}, bf16[1216,128]{1,0:T(8,128)(2,1)S(1)}, u32[]{:S(2)}, u32[]{:S(2)}) collective-permute-start(bf16[1216,128]{1,0:T(8,128)(2,1)S(1)} %get-tuple-element.79), channel_id=1, source_target_pairs={{0,1},{1,0},{2,3},{3,2},{4,5},{5,4},{6,7},{7,6},{8,9},{9,8},{10,11... | collective-permute-start | bytes 933896 | tf_op jit(solution)/shard_map/ppermute | solution.py:567
  87.5 10.8 %collective-permute-start.20 = (bf16[1216,128]{1,0:T(8,128)(2,1)S(1)}, bf16[1216,128]{1,0:T(8,128)(2,1)S(1)}, u32[]{:S(2)}, u32[]{:S(2)}) collective-permute-start(bf16[1216,128]{1,0:T(8,128)(2,1)S(1)} %slice.4), channel_id=1, source_target_pairs={{0,1},{1,0},{2,3},{3,2},{4,5},{5,4},{6,7},{7,6},{8,9},{9,8},{10,11... | collective-permute-start | bytes 933896 | tf_op jit(solution)/shard_map/ppermute | solution.py:567
  91.8 1.5 %collective-permute-start.14 = (bf16[320,256]{1,0:T(8,128)(2,1)S(1)}, bf16[320,256]{1,0:T(8,128)(2,1)S(1)}, u32[]{:S(2)}, u32[]{:S(2)}) collective-permute-start(bf16[320,256]{1,0:T(8,128)(2,1)S(1)} %get-tuple-element.74), channel_id=1, source_target_pairs={{0,4},{4,0},{8,12},{12,8},{16,20},{20,16},{24,28},{28,24},{1,5},{5... | collective-permute-start | bytes 491528 | tf_op jit(solution)/shard_map/ppermute | solution.py:567
  93.4 5.5 %collective-permute-start.15 = (bf16[80,256]{1,0:T(8,128)(2,1)S(1)}, bf16[80,256]{1,0:T(8,128)(2,1)S(1)}, u32[]{:S(2)}, u32[]{:S(2)}) collective-permute-start(bf16[80,256]{1,0:T(8,128)(2,1)S(1)} %get-tuple-element.76), channel_id=1, source_target_pairs={{0,1},{1,0},{2,3},{3,2},{4,5},{5,4},{6,7},{7,6},{8,9},{9,8},{10,11... | collective-permute-start | bytes 122888 | tf_op jit(solution)/shard_map/ppermute | solution.py:567
  95.4 5.5 %collective-permute-start.16 = (bf16[80,256]{1,0:T(8,128)(2,1)S(1)}, bf16[80,256]{1,0:T(8,128)(2,1)S(1)}, u32[]{:S(2)}, u32[]{:S(2)}) collective-permute-start(bf16[80,256]{1,0:T(8,128)(2,1)S(1)} %get-tuple-element.77), channel_id=1, source_target_pairs={{0,2},{1,3},{2,0},{3,1},{4,6},{5,7},{6,4},{7,5},{8,10},{9,11},{10,... | collective-permute-start | bytes 122888 | tf_op jit(solution)/shard_map/ppermute | solution.py:567
  96.7 5.8 %collective-permute-start.17 = (bf16[80,256]{1,0:T(8,128)(2,1)S(1)}, bf16[80,256]{1,0:T(8,128)(2,1)S(1)}, u32[]{:S(2)}, u32[]{:S(2)}) collective-permute-start(bf16[80,256]{1,0:T(8,128)(2,1)S(1)} %get-tuple-element.78), channel_id=1, source_target_pairs={{0,3},{1,2},{2,1},{3,0},{4,7},{5,6},{6,5},{7,4},{8,11},{9,10},{10,... | collective-permute-start | bytes 122888 | tf_op jit(solution)/shard_map/ppermute | solution.py:567
  98.4 4.8 %collective-permute-start.21 = (bf16[3,320,128]{2,1,0:T(8,128)(2,1)S(1)}, bf16[3,320,128]{2,1,0:T(8,128)(2,1)S(1)}, u32[]{:S(2)}, u32[]{:S(2)}) collective-permute-start(bf16[3,320,128]{2,1,0:T(8,128)(2,1)S(1)} %shard_map.162), channel_id=1, source_target_pairs={{0,4},{4,0},{8,12},{12,8},{16,20},{20,16},{24,28},{28,24},{1,5},{5... | collective-permute-start | bytes 737288 | tf_op jit(solution)/shard_map/ppermute | solution.py:567
  (14 other events, 136.9 us)

commit v7 on v6

--- a/solution.py
+++ b/solution.py
@@ -104,7 +104,7 @@
     return pl.ds(pl.multiple_of(index * size, align), size)
 
 
-def picked(n_dp, x_ref, dy_ref, slot_ref, count_ref, gate_ref, out_refs):
+def picked(n_dp, x_ref, dy_ref, slot_ref, count_ref, gate_ref, out_ref):
     length, width = x_ref.shape
     slots = slot_ref.shape[1]
     hit = iota((length, slots), 0) == slot_ref[...]
@@ -122,8 +122,7 @@
                 block = jnp.concatenate([block, fill], axis=1)
             blocks.append(block)
     for i, block in enumerate(blocks):
-        for out in out_refs:
-            out[i * slots : (i + 1) * slots, :] = block
+        out_ref[i * slots : (i + 1) * slots, :] = block
 
 
 def high_low(values):
@@ -133,14 +132,14 @@
 
 def prep_kernel(
     n_dp, x_ref, dy_ref, ldt_ref, stept_ref, h_ref, slot_ref, count_ref, gate_ref,
-    cumt_ref, cum_ref, step_ref, dyt_ref, xs_ref, carried_ref, *rest,
+    cumt_ref, cum_ref, step_ref, dyt_ref, xs_ref, carried_ref, rows_ref, *rest,
 ):
     outs, xt_ref = rest[:-1], rest[-1]
     length, width = x_ref.shape
     heads = ldt_ref.shape[0]
     size = width // heads
     _, chip, n_chip = core_and_chip()
-    picked(n_dp, x_ref, dy_ref, slot_ref, count_ref, gate_ref, outs)
+    picked(n_dp, x_ref, dy_ref, slot_ref, count_ref, gate_ref, rows_ref)
     pad = jnp.zeros((LANES - heads, length), F32)
     cumt = dot(ldt_ref[...], triangle(length, lambda a, b: a <= b), 1, 0, HI)
     cumt_ref[...] = cumt
@@ -165,38 +164,36 @@
     decay = jnp.broadcast_to(jnp.exp(cumt[:, length - 1 : length]), (heads, LANES))
     dyt_ref[width : width + 2 * heads, :] = jnp.concatenate(high_low(decay), axis=0).astype(BF16)
     block = width // n_chip
-    for s, out in enumerate(outs):
-        out[out.shape[0] - block :, :] = xt_ref[rows_at(chip ^ s, block), :]
-
-
-def stack_kernel(starts, *refs):
-    rows = refs[-1].shape[1]
-    for i, start in enumerate(starts):
-        refs[-1][i] = refs[i][start : start + rows, :]
-
-
-def stacked(arrays, after=(), rows=None, starts=None):
-    rows = rows or arrays[0].shape[0]
-    starts = starts or [0] * len(arrays)
+    s = 0
+    for out in outs:
+        for start in range(0, out.shape[0], block):
+            out[start : start + block, :] = xt_ref[rows_at(chip ^ s, block), :]
+            s += 1
+
+
+def join_kernel(ranges, *refs):
+    out, at = refs[-1], 0
+    for ref, (start, stop) in zip(refs, ranges):
+        out[at : at + stop - start] = ref[start:stop]
+        at += stop - start
+
+
+def joined(arrays, after=(), ranges=None):
+    ranges = ranges or [(0, a.shape[0]) for a in arrays]
+    dims = (sum(stop - start for start, stop in ranges), *arrays[0].shape[1:])
     return call(
-        lambda *refs: stack_kernel(starts, *refs),
-        [shape((len(arrays), rows, arrays[0].shape[1]), arrays[0].dtype)],
+        lambda *refs: join_kernel(ranges, *refs),
+        [shape(dims, arrays[0].dtype)],
         0.2,
         tuple(arrays),
         after=after,
     )[0]
 
 
-def join_kernel(*refs):
-    start = 0
-    for ref in refs[:-1]:
-        refs[-1][start : start + ref.shape[0]] = ref[...]
-        start += ref.shape[0]
-
-
-def joined(arrays):
-    dims = (sum(a.shape[0] for a in arrays), *arrays[0].shape[1:])
-    return call(join_kernel, [shape(dims, arrays[0].dtype)], 0.2, tuple(arrays))[0]
+def stacked(arrays, after=(), ranges=None):
+    count = len(arrays)
+    out = joined(arrays, after, ranges)
+    return out.reshape(count, out.shape[0] // count, *out.shape[1:])
 
 
 def project_kernel(n_mine, many, *refs):
@@ -419,14 +416,15 @@
     )
 
 
-def term_kernel(n_chip, *refs):
-    columns, pieces = refs[:n_chip], refs[n_chip:-3]
+def term_kernel(places, n_columns, *refs):
+    columns, pieces = refs[:n_columns], refs[n_columns:-3]
     keep_ref, send_ref, held = refs[-3:]
     pieces = [(p, i) for p in pieces for i in range(p.shape[0])]
+    rows = 2 * keep_ref.shape[0]
     core, _, _ = core_and_chip()
     total = None
-    for a, (b, i) in zip(columns, pieces):
-        part = dot(a[a.shape[0] - 2 * keep_ref.shape[0] :, :], b[i], 1, 0)
+    for (a, start), (b, i) in zip(places, pieces):
+        part = dot(columns[a][start : start + rows, :], b[i], 1, 0)
         total = part if total is None else total + part
     block = keep_ref.shape[0]
     held[0] = total[:block]
@@ -448,102 +446,121 @@
 
 
 def expert_kernel(flip, merge, slots, grad_rows, a_ref, b_ref, gate_ref, up_ref, *refs):
-    outs, (rows_ref, gate_acc, up_acc) = refs[:-3], refs[-3:]
-    step = pl.program_id(0)
+    outs, (rows_ref, gate_buf, up_buf, sems) = refs[:-4], refs[-4:]
     n_chip = a_ref.shape[0]
-    width = rows_ref.shape[1]
-
-    @pl.when(step == 0)
-    def _():
-        for half, ref in enumerate((a_ref, b_ref)):
-            for i in range(n_chip):
-                row = (half * n_chip + i) * slots
-                for t in range(width // LANES):
-                    rows_ref[row : row + slots, t * LANES : (t + 1) * LANES] = ref[
-                        i, t * slots : (t + 1) * slots, :
-                    ]
-        gate_acc[...] = jnp.zeros_like(gate_acc)
-        up_acc[...] = jnp.zeros_like(up_acc)
-
-    depth = gate_ref.shape[0]
-    rows = rows_ref[:, rows_at(step, depth, LANES)]
-    gate_acc[...] += dot(rows, gate_ref[...], 1, 0)
-    up_acc[...] += dot(rows, up_ref[...], 1, 0)
-
-    @pl.when(step == pl.num_programs(0) - 1)
-    def _():
-        weighted = jax.nn.silu(gate_acc[...]) * up_acc[...]
-        weighted = (weighted.T if flip else weighted).astype(BF16)
-        place, n_dp = lax.axis_index("dp"), lax.axis_size("dp")
-        base = width // LANES * slots
-        hidden = gate_acc.shape[1]
-
-        def put(out, start, target):
-            for i in range(n_chip):
-                row = pl.multiple_of(base + target * grad_rows, 16)
-                to = start + i * grad_rows
-                out[to : to + grad_rows, :] = a_ref[i, pl.ds(row, grad_rows), :]
-
-        if merge:
-            grads = n_chip * grad_rows
-            for s, out in enumerate(outs):
-                out[grads : grads + hidden, :] = weighted
-                put(out, 0, place ^ s)
-            put(outs[2], grads + hidden, place ^ 3)
-        else:
-            outs[0][...] = weighted
-            for s in range(n_dp):
-                put(outs[1 + s], 0, place ^ s)
-
-
-def expert(a, b, w_gate, w_up, slots, grad_rows, n_dp, flip, merge):
+    blocks, depth, hidden = gate_buf.shape
+    width = blocks * depth
+    copies = []
+    for i in range(blocks):
+        pair = []
+        for half, (ref, buf) in enumerate(((gate_ref, gate_buf), (up_ref, up_buf))):
+            pair.append(
+                pltpu.make_async_copy(
+                    ref.at[pl.ds(i * depth, depth), :], buf.at[i], sems.at[half, i]
+                )
+            )
+            pair[-1].start()
+        copies.append(pair)
+    for half, ref in enumerate((a_ref, b_ref)):
+        for i in range(n_chip):
+            row = (half * n_chip + i) * slots
+            for t in range(width // LANES):
+                rows_ref[row : row + slots, t * LANES : (t + 1) * LANES] = ref[
+                    i, t * slots : (t + 1) * slots, :
+                ]
+    gate = up = None
+    for i in range(blocks):
+        rows = rows_ref[:, i * depth : (i + 1) * depth]
+        copies[i][0].wait()
+        part = dot(rows, gate_buf[i], 1, 0)
+        gate = part if gate is None else gate + part
+        copies[i][1].wait()
+        part = dot(rows, up_buf[i], 1, 0)
+        up = part if up is None else up + part
+    weighted = jax.nn.silu(gate) * up
+    weighted = (weighted.T if flip else weighted).astype(BF16)
+    place, n_dp = lax.axis_index("dp"), lax.axis_size("dp")
+    base = width // LANES * slots
+    grads = n_chip * grad_rows
+
+    def put(out, start, target):
+        for i in range(n_chip):
+            row = pl.multiple_of(base + target * grad_rows, 16)
+            to = start + i * grad_rows
+            out[to : to + grad_rows, :] = a_ref[i, pl.ds(row, grad_rows), :]
+
+    if merge:
+        own, near, low, high = outs
+        middle = hidden // 2
+        for s, out in enumerate((own, near)):
+            out[grads:, :] = weighted
+            put(out, 0, place ^ s)
+        put(low, 0, place ^ 2)
+        low[grads:, :] = weighted[:middle]
+        high[:middle, :] = weighted[middle:]
+        put(high, middle, place ^ 3)
+    else:
+        outs[0][...] = weighted
+        for s in range(n_dp):
+            put(outs[1 + s], 0, place ^ s)
+
+
+def expert(a, b, w_gate, w_up, slots, grad_rows, n_dp, flip, merge, after):
     n_chip = a.shape[0]
     total = 2 * n_chip * slots
     width, hidden = w_gate.shape
     depth = 512
-    whole = pl.BlockSpec(a.shape, lambda i: (0, 0, 0))
-    block = pl.BlockSpec((depth, hidden), lambda i: (i, 0))
     grads = n_chip * grad_rows
     if merge:
-        outs = [(grads + hidden, LANES)] * 2 + [(2 * grads + hidden, LANES)]
+        outs = [(grads + hidden, LANES)] * 2 + [(grads + hidden // 2, LANES)] * 2
     else:
         outs = [(hidden, total) if flip else (total, hidden)] + [(grads, LANES)] * n_dp
+
+    def body(*refs):
+        expert_kernel(flip, merge, slots, grad_rows, *refs[:4], *refs[4 + len(after) :])
+
     return pl.pallas_call(
-        lambda *refs: expert_kernel(flip, merge, slots, grad_rows, *refs),
+        body,
         out_shape=[shape(o, BF16) for o in outs],
-        grid=(width // depth,),
-        in_specs=[whole, whole, block, block],
-        out_specs=[pl.BlockSpec(o, lambda i: (0, 0)) for o in outs],
+        in_specs=[pl.BlockSpec(memory_space=pltpu.VMEM)] * 2
+        + [pl.BlockSpec(memory_space=pl.ANY)] * (2 + len(after)),
+        out_specs=[pl.BlockSpec(memory_space=pltpu.VMEM)] * len(outs),
         scratch_shapes=[
             pltpu.VMEM((total, width), BF16),
-            pltpu.VMEM((total, hidden), F32),
-            pltpu.VMEM((total, hidden), F32),
+            pltpu.VMEM((width // depth, depth, hidden), BF16),
+            pltpu.VMEM((width // depth, depth, hidden), BF16),
+            pltpu.SemaphoreType.DMA((2, width // depth)),
         ],
         cost_estimate=pl.CostEstimate(
-            flops=int(3e10),
-            bytes_accessed=1000,
-            transcendentals=0,
+            flops=int(2 * 1e5), bytes_accessed=1000, transcendentals=0
         ),
-        compiler_params=pltpu.CompilerParams(vmem_limit_bytes=20 * 1024 * 1024),
-    )(a, b, w_gate, w_up)
+        compiler_params=pltpu.CompilerParams(vmem_limit_bytes=52 * 1024 * 1024),
+    )(a, b, w_gate, w_up, *after)
 
 
 def down_kernel(n_dp, flip, merge, slots, grad_rows, *refs):
-    weighted = refs[:n_dp]
-    near = weighted if merge else refs[n_dp : 2 * n_dp]
     b_ref, far_ref, out_ref = refs[-3:]
     hidden, piece = out_ref.shape
     n_chip = b_ref.shape[0]
     tiles = grad_rows // slots
     count = n_chip * grad_rows
     place = lax.axis_index("dp")
+    if merge:
+        own, near, low, high, last = refs[:5]
+        middle = hidden // 2
+        left = [
+            own[count:, :],
+            near[count:, :],
+            jnp.concatenate([low[count:, :], high[:middle, :]], axis=0),
+            last[:hidden, :],
+        ]
+        grads = [own[:count, :], near[:count, :], low[:count, :], last[hidden:, :]]
+    else:
+        left = [r[...] for r in refs[:n_dp]]
+        grads = [r[...] for r in refs[n_dp : 2 * n_dp]]
     total = None
     for s in range(n_dp):
-        first = merge and s < 3
-        base = hidden if merge and not first else 0
-        blocks = [
-            near[s][base + i * grad_rows : base + (i + 1) * grad_rows, :] for i in range(n_chip)
-        ]
+        blocks = [grads[s][i * grad_rows : (i + 1) * grad_rows] for i in range(n_chip)]
         if s == 0:
             row = b_ref.shape[1] - n_dp * grad_rows + place * grad_rows
             rows = pl.ds(pl.multiple_of(row, 16), grad_rows)
@@ -554,10 +571,8 @@
             jnp.concatenate([b[t * slots : (t + 1) * slots] for b in blocks], axis=0)
             for t in range(tiles)
         ]
-        grads = jnp.concatenate(columns, axis=1)[:, :piece]
-        low = count if first else 0
-        left = weighted[s][low : low + hidden, :] if merge else weighted[s][...]
-        part = dot(left, grads, 1 if flip else 0, 0)
+        right = jnp.concatenate(columns, axis=1)[:, :piece]
+        part = dot(left[s], right, 1 if flip else 0, 0)
         total = part if total is None else total + part
     out_ref[...] = total.astype(BF16)
 
@@ -616,10 +631,10 @@
 
     grad_rows = -(-piece // LANES) * capacity
     w_half = lax.dynamic_slice_in_dim(w_bc, core * (share // 2), share // 2, 0)
-    mine = gathered(w_half, "dp", n_dp)[1:]
 
     n_rows = width // LANES * capacity + n_dp * grad_rows
-    cumt, cum, steps, dyt, xs, carried, *sends = call(
+    blocks = [1, 1, 2] if n_chip == 4 else [1] * n_chip
+    cumt, cum, steps, dyt, xs, carried, rows, *xt = call(
         lambda *refs: prep_kernel(n_dp, *refs),
         [
             shape((heads, length), F32),
@@ -629,16 +644,20 @@
             shape((length, width), BF16),
             shape((length, half), F32),
         ]
-        + [shape((n_rows + width // n_chip, length), BF16)] * n_chip,
+        + [shape((n_rows, LANES), BF16)]
+        + [shape((k * width // n_chip, length), BF16) for k in blocks],
         2.0,
         (x, dy, ldt, stept, h_in, slot_rows[0], slot_counts, slot_gates[0]),
         scratch=[pltpu.VMEM((width, length), BF16)],
         fetch=(0, 1, 2, 3, 4),
         limit=60,
     )
-    arrivals = chips(sends)
-    other = swapped(stacked(mine, after=(cumt,)))
-    rows_a = stacked(arrivals, rows=n_rows)
+    w_far = xored(w_half, "dp", n_dp // 2)
+    mine = gathered(w_half, "dp", n_dp // 2)[1:]
+    mine += gathered(joined([w_far], after=(cumt,)), "dp", n_dp // 2)
+    rows_in = chips([rows] * n_chip)
+    other = swapped(stacked(mine, after=tuple(rows_in[1:4])))
+    rows_a = stacked(rows_in, after=(other,))
     rows_b = swapped(rows_a)
     w_whole, bc, keep, send = call(
         lambda *refs: project_kernel(n_dp - 1, many, *refs),
@@ -652,50 +671,30 @@
         (x, dyt, w_bc, *mine, other),
     )
     recv = swapped(send)
+    hidden = w_gate.shape[2]
+    near_rows = n_chip * grad_rows
+    outs = expert(
+        rows_a, rows_b, w_gate[0], w_up[0], capacity, grad_rows, n_dp, flip, merge, (keep,)
+    )
     climbs = [
         call(
             lambda *refs: combine_kernel(many, size, *refs),
             [shape((part + up16(2 * many), half), BF16)],
             0.5,
             (keep, recv),
-            after=tuple(arrivals[1:]),
+            after=(outs[0],),
         )[0]
     ]
-    outs = expert(rows_a, rows_b, w_gate[0], w_up[0], capacity, grad_rows, n_dp, flip, merge)
-    outs = list(outs)
-    arrived = []
-    bit = 1
-    while bit < n_chip:
-        last = bit * 2 == n_chip
-        moves = [
-            (k, k ^ (2 * bit)) for k in range(2 * n_chip) if not last or k & (2 * bit)
-        ]
-        arrived.append(lax.ppermute(climbs[-1], "tm", moves))
-        if not last:
-            climbs.append(
-                call(
-                    lambda *refs, bit=bit: climb_kernel(many, size, bit, *refs),
-                    [shape((part + up16(2 * many), half), BF16)],
-                    0.5,
-                    (climbs[-1], arrived[-1]),
-                    after=(outs[0],),
-                )[0]
-            )
-        bit *= 2
-
+    if n_chip == 4:
+        x_rows = width // n_chip
+        over_y = xored(xt[2], "tm", 4)
     if merge:
-        near_rows = n_chip * grad_rows
-        arrived_2 = xored(outs[2], "dp", 2)
-        spread = [outs[0], xored(outs[1], "dp", 1), arrived_2]
-        spread.append(xored(arrived_2[near_rows:], "dp", 1))
-        near = spread
-    else:
-        spread = gathered(outs[0], "dp", n_dp)
-        near = outs[1:2] + [xored(o, "dp", s + 1) for s, o in enumerate(outs[2:])]
+        low = xored(outs[2], "dp", 2)
 
     parts = 2
     tiles = width // LANES // parts
     dxs, exs, owns = [], [], []
+    later = ()
     mixed = jnp.zeros((length, length), F32)
     for i in range(parts):
         dx, mixed, ex, own = call(
@@ -708,8 +707,31 @@
             ],
             3.0,
             (x, dy, bc, cumt, cum, steps, h_in, mixed),
+            after=later,
             scratch=[pltpu.VMEM((heads, length), F32)],
         )
+        if i == 0:
+            held = (dx, *((over_y,) if n_chip == 4 else ()), *((low,) if merge else ()))
+            arrived = []
+            bit = 1
+            while bit < n_chip:
+                last = bit * 2 == n_chip
+                moves = [
+                    (k, k ^ (2 * bit)) for k in range(2 * n_chip) if not last or k & (2 * bit)
+                ]
+                arrived.append(lax.ppermute(climbs[-1], "tm", moves))
+                if not last:
+                    climbs.append(
+                        call(
+                            lambda *refs, bit=bit: climb_kernel(many, size, bit, *refs),
+                            [shape((part + up16(2 * many), half), BF16)],
+                            0.5,
+                            (climbs[-1], arrived[-1]),
+                            after=held,
+                        )[0]
+                    )
+                bit *= 2
+            later = (climbs[-1],)
         dxs.append(dx)
         exs.append(ex)
         owns.append(own)
@@ -720,12 +742,25 @@
         (mixed, bc, carried),
     )
 
+    held = (dc,)
+    if n_chip == 4:
+        over_x = xored(joined([xt[1], over_y], later, [(0, x_rows), (x_rows, 2 * x_rows)]), "tm", 2)
+        columns_in = [xt[0], over_x, over_y]
+        places = [(0, 0), (1, 0), (2, 0), (1, x_rows)]
+        held += (over_x,)
+    else:
+        columns_in = chips(xt)
+        places = [(i, 0) for i in range(n_chip)]
+    if merge:
+        high = xored(joined([outs[3]], later), "dp", 2)
+        near = xored(outs[1], "dp", 1)
+        held += (high, near)
     r_own, r_send = call(
         lambda *refs: carry_kernel(many, size, len(arrived), *refs),
         [shape((part, half), BF16)] * 2,
         0.5,
         (*arrived, keep, recv),
-        after=(dc,),
+        after=held,
     )
     r_recv = swapped(r_send)
     d_bc = call(db_kernel, [shape((length, columns), BF16)], 0.3, (xs, r_own, r_recv, db, dc))[0]
@@ -748,10 +783,10 @@
     )
     w_rows = width // (2 * n_chip)
     term, term_send = call(
-        lambda *refs: term_kernel(n_chip, *refs),
+        lambda *refs: term_kernel(places, len(columns_in), *refs),
         [shape((w_rows, columns), F32), shape((w_rows, columns), BF16)],
         0.5,
-        (*arrivals, *d_bcs),
+        (*columns_in, *d_bcs),
         after=(d_in,),
         scratch=[pltpu.VMEM((2, w_rows, columns), F32)],
     )
@@ -767,13 +802,22 @@
     for s in range(1, n_dp):
         w_bc_grad = w_bc_grad + xored(final[s], "dp", s).astype(F32)
 
-    starts = [0, 0, w_gate.shape[2]] if merge else None
-    far = swapped(stacked(near[1:], after=(term,), rows=n_chip * grad_rows, starts=starts))
+    if merge:
+        ranges = [(near_rows, low.shape[0]), (0, high.shape[0])]
+        last = xored(joined([low, high], (r_own,), ranges), "dp", 1)
+        pieces = [outs[0], near, low, high, last]
+        sent = [near, low, last]
+        ranges = [(0, near_rows), (0, near_rows), (hidden, hidden + near_rows)]
+    else:
+        sent = [xored(o, "dp", s + 1) for s, o in enumerate(outs[2:])]
+        pieces = [*gathered(outs[0], "dp", n_dp), outs[1], *sent]
+        ranges = None
+    far = swapped(stacked(sent, (term,), ranges))
     w_down_grad = call(
         lambda *refs: down_kernel(n_dp, flip, merge, capacity, grad_rows, *refs),
-        [shape((w_gate.shape[2], piece), BF16)],
+        [shape((hidden, piece), BF16)],
         1.0,
-        (*spread, *([] if merge else near), rows_b, far),
+        (*pieces, rows_b, far),
         after=(final[0],),
     )[0]
     return (d_in[None], d_decay.T[None], d_step.T[None], w_bc_grad, w_down_grad[None])

time: 106 us -> 94 us (0.89)
  waiting for transfers between devices: 51 us -> 35.6 us
  Pallas kernels: 21.5 us -> 24.6 us
  starting transfers between devices: 23.5 us -> 25.2 us
  local copies, waits for them, and re-layouts: 7.27 us -> 5.77 us
    ppermute x2, waiting for transfers between devices: 8.44 us -> 0.01 us  [per_device(): arrived.append(lax.ppermute(climbs[-1], 'tm', moves))]
    ppermute x20 -> x23, waiting for transfers between devices: 42.6 us -> 35.6 us  [xored(): return lax.ppermute(array, axis, [(i, i ^ mask) for i in range(count)])]
    pallas_call x1, Pallas kernels: 2.66 us -> 5.79 us  [expert(): pl.pallas_call(body, out_shape=[shape(o, BF16) for o in outs], in_specs=[...]
    unnamed x32 -> x38, local copies, waits for them, and re-layouts: 6.23 us -> 4.76 us
    ppermute x20 -> x23, starting transfers between devices: 20.7 us -> 22.2 us  [xored(): return lax.ppermute(array, axis, [(i, i ^ mask) for i in range(count)])]
    pallas_call x17 -> x21, Pallas kernels: 18.8 us -> 18.9 us  [call(): pl.pallas_call(body, out_shape=outs, in_specs=specs + [pl.BlockSpec(memor...]
  transfers between devices with their start and end apart: 22 -> 25, of which waited for: 13 -> 13; matrix products, arithmetic and copies ran while one was open for 1% -> 1% of each run, Pallas kernels for 18% -> 23%
where the time goes in v7:
time: 94 us; the launch traced here: 93.6 us
  waiting for transfers between devices  35.6 us (38%)
  starting transfers between devices  25.2 us (27%)
  Pallas kernels  24.6 us (26%)
  local copies, waits for them, and re-layouts  5.77 us (6%)
  between operations  1.62 us (2%)
    ppermute x23, waiting for transfers between devices, xored(): return lax.ppermute(array, axis, [(i, i ^ mask) for i in range(count)])  35.6 us
    ppermute x23, starting transfers between devices, xored(): return lax.ppermute(array, axis, [(i, i ^ mask) for i in range(count)])  22.2 us
    pallas_call x21, Pallas kernels, call(): pl.pallas_call(body, out_shape=outs, in_specs=specs + [pl.BlockSpec(memor...  18.9 us
    pallas_call x1, Pallas kernels, expert(): pl.pallas_call(body, out_shape=[shape(o, BF16) for o in outs], in_specs=[...  5.79 us
    unnamed x38, local copies, waits for them, and re-layouts  4.76 us
    ppermute x2, starting transfers between devices, per_device(): arrived.append(lax.ppermute(climbs[-1], 'tm', moves))  3.08 us
  transfers between devices with their start and end apart: 25, of which 13 were waited for; matrix products, arithmetic and copies ran while one was open for 1% of the time, Pallas kernels for 23%

profile of v7, /device:TPU:0, one launch (start us, length us, event | category | flops | bytes accessed | tf_op | source)
XLA Modules:
  0.0 93.6 jit_solution(2273319387762154127)
XLA Ops:
  1.7 4.1 %collective-permute-start.1 = (bf16[320,256]{1,0:T(8,128)(2,1)S(1)}, bf16[320,256]{1,0:T(8,128)(2,1)S(1)}, u32[]{:S(2)}, u32[]{:S(2)}) collective-permute-start(bf16[320,256]{1,0:T(8,128)(2,1)S(1)} %constant_dynamic-slice_fusion), channel_id=1, source_target_pairs={{0,2},{1,3},{2,0},{3,1},{4,6},{5,7},{6,4},{7,5},{8,10},{9,11},{10,... | collective-permute-start | bytes 491528 | tf_op jit(solution)/shard_map/ppermute | solution.py:582
  5.8 1.6 %collective-permute-start = (bf16[320,256]{1,0:T(8,128)(2,1)S(1)}, bf16[320,256]{1,0:T(8,128)(2,1)S(1)}, u32[]{:S(2)}, u32[]{:S(2)}) collective-permute-start(bf16[320,256]{1,0:T(8,128)(2,1)S(1)} %constant_dynamic-slice_fusion), channel_id=1, source_target_pairs={{0,1},{1,0},{2,3},{3,2},{4,5},{5,4},{6,7},{7,6},{8,9},{9,8},{10,11... | collective-permute-start | bytes 491528 | tf_op jit(solution)/shard_map/ppermute | solution.py:582
  8.0 5.6 %shard_map.146 = (f32[40,128]{1,0:T(8,128)}, f32[128,128]{1,0:T(8,128)}, f32[128,128]{1,0:T(8,128)}, bf16[2640,128]{1,0:T(8,128)(2,1)}, bf16[128,2560]{1,0:T(8,1...) custom-call(bf16[128,2560]{1,0:T(8,128)(2,1)} %bitcast.25, ...), custom_call_target="tpu_custom_call" | custom-call | flops 200000 | bytes 1000 | tf_op jit(solution)/shard_map/pallas_call | solution.py:81
  13.7 2.5 %collective-permute-start.5 = (bf16[640,128]{1,0:T(8,128)(2,1)}, bf16[640,128]{1,0:T(8,128)(2,1)S(1)}, u32[]{:S(2)}, u32[]{:S(2)}) collective-permute-start(bf16[640,128]{1,0:T(8,128)(2,1)} %get-tuple-element.46.refs_0_), channel_id=1, source_target_pairs={{0,24},{4,28},{8,16},{12,20},{16,8},{20,12},{24,0},{28,4},{1,25},{... | collective-permute-start | bytes 491528 | tf_op jit(solution)/shard_map/ppermute | solution.py:582
  18.5 2.8 %collective-permute-done.5.refs_5_.refs_3_ = bf16[640,128]{1,0:T(8,128)(2,1)S(1)} collective-permute-done((bf16[640,128]{1,0:T(8,128)(2,1)}, bf16[640,128]{1,0:T(8,128)(2,1)S(1)}, u32[]{:S(2)}, u32[]{:S(2)}) %collective-permute-start.5) | collective-permute-done | bytes 163872 | tf_op jit(solution)/shard_map/ppermute | solution.py:582
  21.3 2.4 %collective-permute-done.4.refs_4_.refs_2_ = bf16[640,128]{1,0:T(8,128)(2,1)S(1)} collective-permute-done((bf16[640,128]{1,0:T(8,128)(2,1)}, bf16[640,128]{1,0:T(8,128)(2,1)S(1)}, u32[]{:S(2)}, u32[]{:S(2)}) %collective-permute-start.4) | collective-permute-done | bytes 163872 | tf_op jit(solution)/shard_map/ppermute | solution.py:582
  23.9 1.9 %collective-permute-done.6.refs_6_.refs_4_ = bf16[3,320,256]{2,1,0:T(8,128)(2,1)S(1)} collective-permute-done((bf16[3,320,256]{2,1,0:T(8,128)(2,1)S(1)}, bf16[3,320,256]{2,1,0:T(8,128)(2,1)S(1)}, u32[]{:S(2)}, u32[]{:S(2)}) %collective-permute-start.6) | collective-permute-done | bytes 491552 | tf_op jit(solution)/shard_map/ppermute | solution.py:582
  30.4 5.8 %shard_map.151 = (bf16[1216,128]{1,0:T(8,128)(2,1)S(1)}, bf16[1216,128]{1,0:T(8,128)(2,1)S(1)}, bf16[768,128]{1,0:T(8,128)(2,1)S(1)}, bf16[768,128]{1,0:T(8,128)(2,1)S(1)}) custom-call(bf16[4,640,128]{2,1,0:T(8,128)(2,1)S(1)} %bitcast.38, bf16[4,640,128]{2,1,0:T(8,128)(2,1)} %copy-done.3, bf16[2560,896]{1,0:T(8,128)(2,1)} %bitcast.47, ...), custom_call_target="tpu_custom_call" | custom-call | flops 200000 | bytes 1000 | tf_op jit(solution)/shard_map/pallas_call | solution.py:522
  36.4 1.6 %collective-permute-start.9 = (bf16[1328,128]{1,0:T(8,128)(2,1)S(1)}, bf16[1328,128]{1,0:T(8,128)(2,1)S(1)}, u32[]{:S(2)}, u32[]{:S(2)}) collective-permute-start(bf16[1328,128]{1,0:T(8,128)(2,1)S(1)} %shard_map.152.refs_0_), channel_id=1, source_target_pairs={{0,8},{4,12},{8,0},{12,4},{16,24},{20,28},{24,16},{28,20},{1,9},{5... | collective-permute-start | bytes 1019912 | tf_op jit(solution)/shard_map/ppermute | solution.py:722
  39.4 2.6 %shard_map.153 = (f32[128,1280]{1,0:T(8,128)S(1)}, f32[128,128]{1,0:T(8,128)S(1)}, f32[20,128]{1,0:T(8,128)S(1)}, f32[20,128]{1,0:T(8,128)S(1)}) custom-call(bf16[128,2560]{1,0:T(8,128)(2,1)S(1)} %bitcast.27, bf16[128,2560]{1,0:T(8,128)(2,1)S(1)} %bitcast.35, bf16[128,256]{1,0:T(8,128)(2,1)S(1)} %get-tuple-element.47.refs_2_.refs_1_, ...), custom_call_target="tpu_custom_call" | custom-call | flops 300000 | bytes 1000 | tf_op jit(solution)/shard_map/pallas_call | solution.py:81
  42.0 5.5 %collective-permute-done.10.refs_3_.refs_1_.refs_2_ = bf16[1280,128]{1,0:T(8,128)(2,1)S(1)} collective-permute-done((bf16[1280,128]{1,0:T(8,128)(2,1)S(1)}, bf16[1280,128]{1,0:T(8,128)(2,1)S(1)}, u32[]{:S(2)}, u32[]{:S(2)}) %collective-permute-start.10) | collective-permute-done | bytes 327712 | tf_op jit(solution)/shard_map/ppermute | solution.py:582
  47.5 2.9 %collective-permute-done.11.refs_4_.refs_0_.refs_1_.refs_2_ = bf16[768,128]{1,0:T(8,128)(2,1)S(1)} collective-permute-done((bf16[768,128]{1,0:T(8,128)(2,1)S(1)}, bf16[768,128]{1,0:T(8,128)(2,1)S(1)}, u32[]{:S(2)}, u32[]{:S(2)}) %collective-permute-start.11) | collective-permute-done | bytes 196640 | tf_op jit(solution)/shard_map/ppermute | solution.py:582
  50.6 1.5 %collective-permute-start.12 = (bf16[1328,128]{1,0:T(8,128)(2,1)S(1)}, bf16[1328,128]{1,0:T(8,128)(2,1)S(1)}, u32[]{:S(2)}, u32[]{:S(2)}) collective-permute-start(bf16[1328,128]{1,0:T(8,128)(2,1)S(1)} %shard_map.154.refs_8_.refs_2_.refs_1_), channel_id=1, source_target_pairs={{16,0},{20,4},{24,8},{28,12},{17,1},{21,5},{25,9},{29,13},{18,2},{... | collective-permute-start | bytes 1019912 | tf_op jit(solution)/shard_map/ppermute | solution.py:722
  54.1 2.5 %shard_map.155 = (f32[128,1280]{1,0:T(8,128)S(1)}, f32[128,128]{1,0:T(8,128)S(1)}, f32[20,128]{1,0:T(8,128)S(1)}, f32[20,128]{1,0:T(8,128)S(1)}) custom-call(bf16[128,2560]{1,0:T(8,128)(2,1)S(1)} %bitcast.28, bf16[128,2560]{1,0:T(8,128)(2,1)S(1)} %bitcast.36, bf16[128,256]{1,0:T(8,128)(2,1)S(1)} %get-tuple-element.47.refs_2_.refs_1_, ...), custom_call_target="tpu_custom_call" | custom-call | flops 300000 | bytes 1000 | tf_op jit(solution)/shard_map/pallas_call | solution.py:81
  56.9 9.4 %collective-permute-done.15.refs_7_.refs_0_.refs_1_ = bf16[1216,128]{1,0:T(8,128)(2,1)S(1)} collective-permute-done((bf16[1216,128]{1,0:T(8,128)(2,1)S(1)}, bf16[1216,128]{1,0:T(8,128)(2,1)S(1)}, u32[]{:S(2)}, u32[]{:S(2)}) %collective-permute-start.15) | collective-permute-done | bytes 311328 | tf_op jit(solution)/shard_map/ppermute | solution.py:582
  66.8 1.6 %collective-permute-done.16.refs_2_.refs_8_ = bf16[1280,128]{1,0:T(8,128)(2,1)S(1)} collective-permute-done((bf16[1280,128]{1,0:T(8,128)(2,1)S(1)}, bf16[1280,128]{1,0:T(8,128)(2,1)S(1)}, u32[]{:S(2)}, u32[]{:S(2)}) %collective-permute-start.16) | collective-permute-done | bytes 327712 | tf_op jit(solution)/shard_map/ppermute | solution.py:582
  69.9 3.2 %collective-permute-done.17.refs_1_.refs_4_ = bf16[1,128,256]{2,1,0:T(8,128)(2,1)S(1)} collective-permute-done((bf16[1,128,256]{2,1,0:T(8,128)(2,1)S(1)}, bf16[1,128,256]{2,1,0:T(8,128)(2,1)S(1)}, u32[]{:S(2)}, u32[]{:S(2)}) %collective-permute-start.17) | collective-permute-done | bytes 65568 | tf_op jit(solution)/shard_map/ppermute | solution.py:582
  73.1 2.4 %collective-permute-start.18 = (bf16[2,128,256]{2,1,0:T(8,128)(2,1)S(1)}, bf16[2,128,256]{2,1,0:T(8,128)(2,1)S(1)}, u32[]{:S(2)}, u32[]{:S(2)}) collective-permute-start(bf16[2,128,256]{2,1,0:T(8,128)(2,1)S(1)} %shard_map.162), channel_id=1, source_target_pairs={{0,16},{4,20},{8,24},{12,28},{16,0},{20,4},{24,8},{28,12},{1,17},{... | collective-permute-start | bytes 393224 | tf_op jit(solution)/shard_map/ppermute | solution.py:582
  75.7 2.7 %shard_map.161 = (bf16[128,2560]{1,0:T(8,128)(2,1)}, f32[40,128]{1,0:T(8,128)}, f32[40,128]{1,0:T(8,128)}) custom-call(bf16[128,2560]{1,0:T(8,128)(2,1)S(1)} %bitcast.29, bf16[128,256]{1,0:T(8,128)(2,1)S(1)} %get-tuple-element.47.refs_2_.refs_1_, f32[40,128]{1,0:T(8,128)S(1)} %copy-done.12, f32[40,128]{1,0:T(8,128)S(1)} %bitcast.46, ...), custom_call_target="tpu_custom_call" | custom-call | flops 300000 | bytes 1000 | tf_op jit(solution)/shard_map/pallas_call | solution.py:81
  80.2 1.4 %collective-permute-done.19.refs_1_ = bf16[320,256]{1,0:T(8,128)(2,1)S(1)} collective-permute-done((bf16[320,256]{1,0:T(8,128)(2,1)S(1)}, bf16[320,256]{1,0:T(8,128)(2,1)S(1)}, u32[]{:S(2)}, u32[]{:S(2)}) %collective-permute-start.19) | collective-permute-done | bytes 163872 | tf_op jit(solution)/shard_map/ppermute | solution.py:582
  81.7 1.9 %collective-permute-start.20 = (bf16[80,256]{1,0:T(8,128)(2,1)S(1)}, bf16[80,256]{1,0:T(8,128)(2,1)S(1)}, u32[]{:S(2)}, u32[]{:S(2)}) collective-permute-start(bf16[80,256]{1,0:T(8,128)(2,1)S(1)} %get-tuple-element.80), channel_id=1, source_target_pairs={{0,1},{1,0},{2,3},{3,2},{4,5},{5,4},{6,7},{7,6},{8,9},{9,8},{10,11... | collective-permute-start | bytes 122888 | tf_op jit(solution)/shard_map/ppermute | solution.py:582
  84.8 1.4 %collective-permute-start.22 = (bf16[80,256]{1,0:T(8,128)(2,1)S(1)}, bf16[80,256]{1,0:T(8,128)(2,1)S(1)}, u32[]{:S(2)}, u32[]{:S(2)}) collective-permute-start(bf16[80,256]{1,0:T(8,128)(2,1)S(1)} %get-tuple-element.82), channel_id=1, source_target_pairs={{0,3},{1,2},{2,1},{3,0},{4,7},{5,6},{6,5},{7,4},{8,11},{9,10},{10,... | collective-permute-start | bytes 122888 | tf_op jit(solution)/shard_map/ppermute | solution.py:582
  86.2 3.1 %collective-permute-done.21 = bf16[80,256]{1,0:T(8,128)(2,1)S(1)} collective-permute-done((bf16[80,256]{1,0:T(8,128)(2,1)S(1)}, bf16[80,256]{1,0:T(8,128)(2,1)S(1)}, u32[]{:S(2)}, u32[]{:S(2)}) %collective-permute-start.21) | collective-permute-done | bytes 40992 | tf_op jit(solution)/shard_map/ppermute | solution.py:582
  91.2 2.4 %shard_map.167 = bf16[896,640]{1,0:T(8,128)(2,1)} custom-call(bf16[1216,128]{1,0:T(8,128)(2,1)S(1)} %get-tuple-element.52.refs_2_.refs_0_, bf16[1216,128]{1,0:T(8,128)(2,1)S(1)} %collective-permute-done.15.refs_7_.refs_0_.refs_1_, bf16[768,128]{1,0:T(8,128)(2,1)S(1)} %collective-permute-done.11.refs_4_.refs_0_.refs_1_.refs_2_, ...), custom_call_target="tpu_custom_call" | custom-call | flops 100000 | bytes 1000 | tf_op jit(solution)/shard_map/pallas_call | solution.py:81
  (89 shorter events, 19.2 us)
Async XLA Ops:
  1.7 15.5 %collective-permute-start.1 = (bf16[320,256]{1,0:T(8,128)(2,1)S(1)}, bf16[320,256]{1,0:T(8,128)(2,1)S(1)}, u32[]{:S(2)}, u32[]{:S(2)}) collective-permute-start(bf16[320,256]{1,0:T(8,128)(2,1)S(1)} %constant_dynamic-slice_fusion), channel_id=1, source_target_pairs={{0,2},{1,3},{2,0},{3,1},{4,6},{5,7},{6,4},{7,5},{8,10},{9,11},{10,... | collective-permute-start | bytes 491528 | tf_op jit(solution)/shard_map/ppermute | solution.py:582
  5.8 12.7 %collective-permute-start = (bf16[320,256]{1,0:T(8,128)(2,1)S(1)}, bf16[320,256]{1,0:T(8,128)(2,1)S(1)}, u32[]{:S(2)}, u32[]{:S(2)}) collective-permute-start(bf16[320,256]{1,0:T(8,128)(2,1)S(1)} %constant_dynamic-slice_fusion), channel_id=1, source_target_pairs={{0,1},{1,0},{2,3},{3,2},{4,5},{5,4},{6,7},{7,6},{8,9},{9,8},{10,11... | collective-permute-start | bytes 491528 | tf_op jit(solution)/shard_map/ppermute | solution.py:582
  13.7 7.7 %collective-permute-start.5 = (bf16[640,128]{1,0:T(8,128)(2,1)}, bf16[640,128]{1,0:T(8,128)(2,1)S(1)}, u32[]{:S(2)}, u32[]{:S(2)}) collective-permute-start(bf16[640,128]{1,0:T(8,128)(2,1)} %get-tuple-element.46.refs_0_), channel_id=1, source_target_pairs={{0,24},{4,28},{8,16},{12,20},{16,8},{20,12},{24,0},{28,4},{1,25},{... | collective-permute-start | bytes 491528 | tf_op jit(solution)/shard_map/ppermute | solution.py:582
  16.2 7.6 %collective-permute-start.4 = (bf16[640,128]{1,0:T(8,128)(2,1)}, bf16[640,128]{1,0:T(8,128)(2,1)S(1)}, u32[]{:S(2)}, u32[]{:S(2)}) collective-permute-start(bf16[640,128]{1,0:T(8,128)(2,1)} %get-tuple-element.46.refs_0_), channel_id=1, source_target_pairs={{0,16},{4,20},{8,24},{12,28},{16,0},{20,4},{24,8},{28,12},{1,17},{... | collective-permute-start | bytes 491528 | tf_op jit(solution)/shard_map/ppermute | solution.py:582
  16.7 7.1 %collective-permute-start.3 = (bf16[640,128]{1,0:T(8,128)(2,1)}, bf16[640,128]{1,0:T(8,128)(2,1)S(1)}, u32[]{:S(2)}, u32[]{:S(2)}) collective-permute-start(bf16[640,128]{1,0:T(8,128)(2,1)} %get-tuple-element.46.refs_0_), channel_id=1, source_target_pairs={{0,8},{4,12},{8,0},{12,4},{16,24},{20,28},{24,16},{28,20},{1,9},{5... | collective-permute-start | bytes 491528 | tf_op jit(solution)/shard_map/ppermute | solution.py:582
  18.0 5.8 %collective-permute-start.2 = (bf16[320,256]{1,0:T(8,128)(2,1)S(1)}, bf16[320,256]{1,0:T(8,128)(2,1)S(1)}, u32[]{:S(2)}, u32[]{:S(2)}) collective-permute-start(bf16[320,256]{1,0:T(8,128)(2,1)S(1)} %shard_map.147.refs_1_.refs_4_), channel_id=1, source_target_pairs={{0,1},{1,0},{2,3},{3,2},{4,5},{5,4},{6,7},{7,6},{8,9},{9,8},{10,11... | collective-permute-start | bytes 491528 | tf_op jit(solution)/shard_map/ppermute | solution.py:582
  23.8 1.9 %collective-permute-start.6 = (bf16[3,320,256]{2,1,0:T(8,128)(2,1)S(1)}, bf16[3,320,256]{2,1,0:T(8,128)(2,1)S(1)}, u32[]{:S(2)}, u32[]{:S(2)}) collective-permute-start(bf16[3,320,256]{2,1,0:T(8,128)(2,1)S(1)} %bitcast.43), channel_id=1, source_target_pairs={{0,4},{4,0},{8,12},{12,8},{16,20},{20,16},{24,28},{28,24},{1,5},{5... | collective-permute-start | bytes 1474568 | tf_op jit(solution)/shard_map/ppermute | solution.py:582
  26.7 2.8 %collective-permute-start.8 = (bf16[4,640,128]{2,1,0:T(8,128)(2,1)S(1)}, bf16[4,640,128]{2,1,0:T(8,128)(2,1)S(1)}, u32[]{:S(2)}, u32[]{:S(2)}) collective-permute-start(bf16[4,640,128]{2,1,0:T(8,128)(2,1)S(1)} %bitcast.37), channel_id=1, source_target_pairs={{0,4},{4,0},{8,12},{12,8},{16,20},{20,16},{24,28},{28,24},{1,5},{5... | collective-permute-start | bytes 1966088 | tf_op jit(solution)/shard_map/ppermute | solution.py:582
  29.1 7.1 %collective-permute-start.7 = (bf16[1328,128]{1,0:T(8,128)(2,1)S(1)}, bf16[1328,128]{1,0:T(8,128)(2,1)S(1)}, u32[]{:S(2)}, u32[]{:S(2)}) collective-permute-start(bf16[1328,128]{1,0:T(8,128)(2,1)S(1)} %get-tuple-element.51), channel_id=1, source_target_pairs={{0,4},{4,0},{8,12},{12,8},{16,20},{20,16},{24,28},{28,24},{1,5},{5... | collective-permute-start | bytes 1019912 | tf_op jit(solution)/shard_map/ppermute | solution.py:582
  36.4 14.0 %collective-permute-start.9 = (bf16[1328,128]{1,0:T(8,128)(2,1)S(1)}, bf16[1328,128]{1,0:T(8,128)(2,1)S(1)}, u32[]{:S(2)}, u32[]{:S(2)}) collective-permute-start(bf16[1328,128]{1,0:T(8,128)(2,1)S(1)} %shard_map.152.refs_0_), channel_id=1, source_target_pairs={{0,8},{4,12},{8,0},{12,4},{16,24},{20,28},{24,16},{28,20},{1,9},{5... | collective-permute-start | bytes 1019912 | tf_op jit(solution)/shard_map/ppermute | solution.py:722
  38.0 9.5 %collective-permute-start.10 = (bf16[1280,128]{1,0:T(8,128)(2,1)S(1)}, bf16[1280,128]{1,0:T(8,128)(2,1)S(1)}, u32[]{:S(2)}, u32[]{:S(2)}) collective-permute-start(bf16[1280,128]{1,0:T(8,128)(2,1)S(1)} %copy-done.18), channel_id=1, source_target_pairs={{0,16},{4,20},{8,24},{12,28},{16,0},{20,4},{24,8},{28,12},{1,17},{... | collective-permute-start | bytes 983048 | tf_op jit(solution)/shard_map/ppermute | solution.py:582
  39.0 11.4 %collective-permute-start.11 = (bf16[768,128]{1,0:T(8,128)(2,1)S(1)}, bf16[768,128]{1,0:T(8,128)(2,1)S(1)}, u32[]{:S(2)}, u32[]{:S(2)}) collective-permute-start(bf16[768,128]{1,0:T(8,128)(2,1)S(1)} %get-tuple-element.55), channel_id=1, source_target_pairs={{0,2},{1,3},{2,0},{3,1},{4,6},{5,7},{6,4},{7,5},{8,10},{9,11},{10,... | collective-permute-start | bytes 589832 | tf_op jit(solution)/shard_map/ppermute | solution.py:582
  50.6 15.8 %collective-permute-start.12 = (bf16[1328,128]{1,0:T(8,128)(2,1)S(1)}, bf16[1328,128]{1,0:T(8,128)(2,1)S(1)}, u32[]{:S(2)}, u32[]{:S(2)}) collective-permute-start(bf16[1328,128]{1,0:T(8,128)(2,1)S(1)} %shard_map.154.refs_8_.refs_2_.refs_1_), channel_id=1, source_target_pairs={{16,0},{20,4},{24,8},{28,12},{17,1},{21,5},{25,9},{29,13},{18,2},{... | collective-permute-start | bytes 1019912 | tf_op jit(solution)/shard_map/ppermute | solution.py:722
  52.1 14.2 %collective-permute-start.13 = (bf16[1280,128]{1,0:T(8,128)(2,1)S(1)}, bf16[1280,128]{1,0:T(8,128)(2,1)S(1)}, u32[]{:S(2)}, u32[]{:S(2)}) collective-permute-start(bf16[1280,128]{1,0:T(8,128)(2,1)S(1)} %shard_map.157), channel_id=1, source_target_pairs={{0,8},{4,12},{8,0},{12,4},{16,24},{20,28},{24,16},{28,20},{1,9},{5... | collective-permute-start | bytes 983048 | tf_op jit(solution)/shard_map/ppermute | solution.py:582
  53.1 13.2 %collective-permute-start.15 = (bf16[1216,128]{1,0:T(8,128)(2,1)S(1)}, bf16[1216,128]{1,0:T(8,128)(2,1)S(1)}, u32[]{:S(2)}, u32[]{:S(2)}) collective-permute-start(bf16[1216,128]{1,0:T(8,128)(2,1)S(1)} %get-tuple-element.62), channel_id=1, source_target_pairs={{0,1},{1,0},{2,3},{3,2},{4,5},{5,4},{6,7},{7,6},{8,9},{9,8},{10,11... | collective-permute-start | bytes 933896 | tf_op jit(solution)/shard_map/ppermute | solution.py:582
  53.2 13.2 %collective-permute-start.14 = (bf16[768,128]{1,0:T(8,128)(2,1)S(1)}, bf16[768,128]{1,0:T(8,128)(2,1)S(1)}, u32[]{:S(2)}, u32[]{:S(2)}) collective-permute-start(bf16[768,128]{1,0:T(8,128)(2,1)S(1)} %shard_map.158), channel_id=1, source_target_pairs={{0,2},{1,3},{2,0},{3,1},{4,6},{5,7},{6,4},{7,5},{8,10},{9,11},{10,... | collective-permute-start | bytes 589832 | tf_op jit(solution)/shard_map/ppermute | solution.py:582
  66.7 1.7 %collective-permute-start.16 = (bf16[1280,128]{1,0:T(8,128)(2,1)S(1)}, bf16[1280,128]{1,0:T(8,128)(2,1)S(1)}, u32[]{:S(2)}, u32[]{:S(2)}) collective-permute-start(bf16[1280,128]{1,0:T(8,128)(2,1)S(1)} %get-tuple-element.64), channel_id=1, source_target_pairs={{0,4},{4,0},{8,12},{12,8},{16,20},{20,16},{24,28},{28,24},{1,5},{5... | collective-permute-start | bytes 983048 | tf_op jit(solution)/shard_map/ppermute | solution.py:582
  68.7 4.3 %collective-permute-start.17 = (bf16[1,128,256]{2,1,0:T(8,128)(2,1)S(1)}, bf16[1,128,256]{2,1,0:T(8,128)(2,1)S(1)}, u32[]{:S(2)}, u32[]{:S(2)}) collective-permute-start(bf16[1,128,256]{2,1,0:T(8,128)(2,1)S(1)} %bitcast.39), channel_id=1, source_target_pairs={{0,8},{4,12},{8,0},{12,4},{16,24},{20,28},{24,16},{28,20},{1,9},{5... | collective-permute-start | bytes 196616 | tf_op jit(solution)/shard_map/ppermute | solution.py:582
  73.1 5.4 %collective-permute-start.18 = (bf16[2,128,256]{2,1,0:T(8,128)(2,1)S(1)}, bf16[2,128,256]{2,1,0:T(8,128)(2,1)S(1)}, u32[]{:S(2)}, u32[]{:S(2)}) collective-permute-start(bf16[2,128,256]{2,1,0:T(8,128)(2,1)S(1)} %shard_map.162), channel_id=1, source_target_pairs={{0,16},{4,20},{8,24},{12,28},{16,0},{20,4},{24,8},{28,12},{1,17},{... | collective-permute-start | bytes 393224 | tf_op jit(solution)/shard_map/ppermute | solution.py:582
  75.6 10.6 %collective-permute-start.23 = (bf16[1216,128]{1,0:T(8,128)(2,1)S(1)}, bf16[1216,128]{1,0:T(8,128)(2,1)S(1)}, u32[]{:S(2)}, u32[]{:S(2)}) collective-permute-start(bf16[1216,128]{1,0:T(8,128)(2,1)S(1)} %shard_map.165), channel_id=1, source_target_pairs={{0,1},{1,0},{2,3},{3,2},{4,5},{5,4},{6,7},{7,6},{8,9},{9,8},{10,11... | collective-permute-start | bytes 933896 | tf_op jit(solution)/shard_map/ppermute | solution.py:582
  81.7 4.6 %collective-permute-start.20 = (bf16[80,256]{1,0:T(8,128)(2,1)S(1)}, bf16[80,256]{1,0:T(8,128)(2,1)S(1)}, u32[]{:S(2)}, u32[]{:S(2)}) collective-permute-start(bf16[80,256]{1,0:T(8,128)(2,1)S(1)} %get-tuple-element.80), channel_id=1, source_target_pairs={{0,1},{1,0},{2,3},{3,2},{4,5},{5,4},{6,7},{7,6},{8,9},{9,8},{10,11... | collective-permute-start | bytes 122888 | tf_op jit(solution)/shard_map/ppermute | solution.py:582
  83.6 5.8 %collective-permute-start.21 = (bf16[80,256]{1,0:T(8,128)(2,1)S(1)}, bf16[80,256]{1,0:T(8,128)(2,1)S(1)}, u32[]{:S(2)}, u32[]{:S(2)}) collective-permute-start(bf16[80,256]{1,0:T(8,128)(2,1)S(1)} %get-tuple-element.81), channel_id=1, source_target_pairs={{0,2},{1,3},{2,0},{3,1},{4,6},{5,7},{6,4},{7,5},{8,10},{9,11},{10,... | collective-permute-start | bytes 122888 | tf_op jit(solution)/shard_map/ppermute | solution.py:582
  84.8 5.8 %collective-permute-start.22 = (bf16[80,256]{1,0:T(8,128)(2,1)S(1)}, bf16[80,256]{1,0:T(8,128)(2,1)S(1)}, u32[]{:S(2)}, u32[]{:S(2)}) collective-permute-start(bf16[80,256]{1,0:T(8,128)(2,1)S(1)} %get-tuple-element.82), channel_id=1, source_target_pairs={{0,3},{1,2},{2,1},{3,0},{4,7},{5,6},{6,5},{7,4},{8,11},{9,10},{10,... | collective-permute-start | bytes 122888 | tf_op jit(solution)/shard_map/ppermute | solution.py:582
  86.2 5.1 %collective-permute-start.24 = (bf16[3,320,128]{2,1,0:T(8,128)(2,1)S(1)}, bf16[3,320,128]{2,1,0:T(8,128)(2,1)S(1)}, u32[]{:S(2)}, u32[]{:S(2)}) collective-permute-start(bf16[3,320,128]{2,1,0:T(8,128)(2,1)S(1)} %bitcast.44), channel_id=1, source_target_pairs={{0,4},{4,0},{8,12},{12,8},{16,20},{20,16},{24,28},{28,24},{1,5},{5... | collective-permute-start | bytes 737288 | tf_op jit(solution)/shard_map/ppermute | solution.py:582
  (20 other events, 225.6 us)

commit v8 on v7

--- a/solution.py
+++ b/solution.py
@@ -85,7 +85,7 @@
         out_specs=[pl.BlockSpec(memory_space=pltpu.VMEM)] * n_out,
         scratch_shapes=list(scratch) + held,
         cost_estimate=pl.CostEstimate(
-            flops=int(cost * 1e5), bytes_accessed=1000, transcendentals=0
+            flops=int(cost * 3e9), bytes_accessed=1000, transcendentals=0
         ),
         compiler_params=pltpu.CompilerParams(vmem_limit_bytes=limit * 1024 * 1024),
     )(*args, *after)
@@ -104,25 +104,29 @@
     return pl.ds(pl.multiple_of(index * size, align), size)
 
 
-def picked(n_dp, x_ref, dy_ref, slot_ref, count_ref, gate_ref, out_ref):
+def picked(x_ref, dy_ref, slot_ref, count_ref, gate_ref, rows_ref, out_refs):
     length, width = x_ref.shape
     slots = slot_ref.shape[1]
     hit = iota((length, slots), 0) == slot_ref[...]
     live = iota((1, slots), 1) < count_ref[...]
     weight = jnp.where(live, gate_ref[...].astype(F32), 0.0)
     rows = dot(where_one(hit).astype(BF16), x_ref[...], 0, 0).astype(BF16)
+    for t in range(width // LANES):
+        rows_ref[t * slots : (t + 1) * slots, :] = rows[:, t * LANES : (t + 1) * LANES]
     grads = dot(jnp.where(hit, weight, 0.0).astype(BF16), dy_ref[...], 0, 0).astype(BF16)
-    blocks = [rows[:, t * LANES : (t + 1) * LANES] for t in range(width // LANES)]
+    n_dp = len(out_refs) - 1
+    held = out_refs[-1]
     piece = width // n_dp
     for i in range(n_dp):
-        for low in range(i * piece, (i + 1) * piece, LANES):
+        for t, low in enumerate(range(i * piece, (i + 1) * piece, LANES)):
             block = grads[:, low : min(low + LANES, (i + 1) * piece)]
             if block.shape[1] < LANES:
                 fill = jnp.zeros((slots, LANES - block.shape[1]), BF16)
                 block = jnp.concatenate([block, fill], axis=1)
-            blocks.append(block)
-    for i, block in enumerate(blocks):
-        out_ref[i * slots : (i + 1) * slots, :] = block
+            held[i, t * slots : (t + 1) * slots, :] = block
+    place = lax.axis_index("dp")
+    for s, out in enumerate(out_refs[:-1]):
+        out[...] = held[place ^ s]
 
 
 def high_low(values):
@@ -134,12 +138,12 @@
     n_dp, x_ref, dy_ref, ldt_ref, stept_ref, h_ref, slot_ref, count_ref, gate_ref,
     cumt_ref, cum_ref, step_ref, dyt_ref, xs_ref, carried_ref, rows_ref, *rest,
 ):
-    outs, xt_ref = rest[:-1], rest[-1]
+    outs, xt_ref, held_ref = rest[n_dp:-2], rest[-2], rest[-1]
     length, width = x_ref.shape
     heads = ldt_ref.shape[0]
     size = width // heads
     _, chip, n_chip = core_and_chip()
-    picked(n_dp, x_ref, dy_ref, slot_ref, count_ref, gate_ref, rows_ref)
+    picked(x_ref, dy_ref, slot_ref, count_ref, gate_ref, rows_ref, (*rest[:n_dp], held_ref))
     pad = jnp.zeros((LANES - heads, length), F32)
     cumt = dot(ldt_ref[...], triangle(length, lambda a, b: a <= b), 1, 0, HI)
     cumt_ref[...] = cumt
@@ -445,134 +449,80 @@
         out[...] = held[place ^ (s + 1)].astype(BF16)
 
 
-def expert_kernel(flip, merge, slots, grad_rows, a_ref, b_ref, gate_ref, up_ref, *refs):
-    outs, (rows_ref, gate_buf, up_buf, sems) = refs[:-4], refs[-4:]
+def expert_kernel(flip, slots, a_ref, b_ref, gate_ref, up_ref, out_ref, *scratch):
+    rows_ref, gate_acc, up_acc = scratch
+    step = pl.program_id(0)
     n_chip = a_ref.shape[0]
-    blocks, depth, hidden = gate_buf.shape
-    width = blocks * depth
-    copies = []
-    for i in range(blocks):
-        pair = []
-        for half, (ref, buf) in enumerate(((gate_ref, gate_buf), (up_ref, up_buf))):
-            pair.append(
-                pltpu.make_async_copy(
-                    ref.at[pl.ds(i * depth, depth), :], buf.at[i], sems.at[half, i]
-                )
-            )
-            pair[-1].start()
-        copies.append(pair)
-    for half, ref in enumerate((a_ref, b_ref)):
-        for i in range(n_chip):
-            row = (half * n_chip + i) * slots
-            for t in range(width // LANES):
-                rows_ref[row : row + slots, t * LANES : (t + 1) * LANES] = ref[
-                    i, t * slots : (t + 1) * slots, :
-                ]
-    gate = up = None
-    for i in range(blocks):
-        rows = rows_ref[:, i * depth : (i + 1) * depth]
-        copies[i][0].wait()
-        part = dot(rows, gate_buf[i], 1, 0)
-        gate = part if gate is None else gate + part
-        copies[i][1].wait()
-        part = dot(rows, up_buf[i], 1, 0)
-        up = part if up is None else up + part
-    weighted = jax.nn.silu(gate) * up
-    weighted = (weighted.T if flip else weighted).astype(BF16)
-    place, n_dp = lax.axis_index("dp"), lax.axis_size("dp")
-    base = width // LANES * slots
-    grads = n_chip * grad_rows
-
-    def put(out, start, target):
-        for i in range(n_chip):
-            row = pl.multiple_of(base + target * grad_rows, 16)
-            to = start + i * grad_rows
-            out[to : to + grad_rows, :] = a_ref[i, pl.ds(row, grad_rows), :]
-
-    if merge:
-        own, near, low, high = outs
-        middle = hidden // 2
-        for s, out in enumerate((own, near)):
-            out[grads:, :] = weighted
-            put(out, 0, place ^ s)
-        put(low, 0, place ^ 2)
-        low[grads:, :] = weighted[:middle]
-        high[:middle, :] = weighted[middle:]
-        put(high, middle, place ^ 3)
-    else:
-        outs[0][...] = weighted
-        for s in range(n_dp):
-            put(outs[1 + s], 0, place ^ s)
-
-
-def expert(a, b, w_gate, w_up, slots, grad_rows, n_dp, flip, merge, after):
+
+    @pl.when(step == 0)
+    def _():
+        for half, ref in enumerate((a_ref, b_ref)):
+            for i in range(n_chip):
+                row = (half * n_chip + i) * slots
+                for t in range(rows_ref.shape[1] // LANES):
+                    rows_ref[row : row + slots, t * LANES : (t + 1) * LANES] = ref[
+                        i, t * slots : (t + 1) * slots, :
+                    ]
+        gate_acc[...] = jnp.zeros_like(gate_acc)
+        up_acc[...] = jnp.zeros_like(up_acc)
+
+    depth = gate_ref.shape[0]
+    rows = rows_ref[:, rows_at(step, depth, LANES)]
+    gate_acc[...] += dot(rows, gate_ref[...], 1, 0)
+    up_acc[...] += dot(rows, up_ref[...], 1, 0)
+
+    @pl.when(step == pl.num_programs(0) - 1)
+    def _():
+        weighted = jax.nn.silu(gate_acc[...]) * up_acc[...]
+        out_ref[...] = (weighted.T if flip else weighted).astype(BF16)
+
+
+def expert(a, b, w_gate, w_up, slots, flip, after):
     n_chip = a.shape[0]
     total = 2 * n_chip * slots
     width, hidden = w_gate.shape
     depth = 512
-    grads = n_chip * grad_rows
-    if merge:
-        outs = [(grads + hidden, LANES)] * 2 + [(grads + hidden // 2, LANES)] * 2
-    else:
-        outs = [(hidden, total) if flip else (total, hidden)] + [(grads, LANES)] * n_dp
+    out = (hidden, total) if flip else (total, hidden)
 
     def body(*refs):
-        expert_kernel(flip, merge, slots, grad_rows, *refs[:4], *refs[4 + len(after) :])
-
+        expert_kernel(flip, slots, *refs[:4], *refs[4 + len(after) :])
+
+    whole = pl.BlockSpec(a.shape, lambda i: (0, 0, 0))
+    block = pl.BlockSpec((depth, hidden), lambda i: (i, 0))
     return pl.pallas_call(
         body,
-        out_shape=[shape(o, BF16) for o in outs],
-        in_specs=[pl.BlockSpec(memory_space=pltpu.VMEM)] * 2
-        + [pl.BlockSpec(memory_space=pl.ANY)] * (2 + len(after)),
-        out_specs=[pl.BlockSpec(memory_space=pltpu.VMEM)] * len(outs),
+        out_shape=shape(out, BF16),
+        grid=(width // depth,),
+        in_specs=[whole, whole, block, block]
+        + [pl.BlockSpec(memory_space=pl.ANY)] * len(after),
+        out_specs=pl.BlockSpec(out, lambda i: (0, 0)),
         scratch_shapes=[
             pltpu.VMEM((total, width), BF16),
-            pltpu.VMEM((width // depth, depth, hidden), BF16),
-            pltpu.VMEM((width // depth, depth, hidden), BF16),
-            pltpu.SemaphoreType.DMA((2, width // depth)),
+            pltpu.VMEM((total, hidden), F32),
+            pltpu.VMEM((total, hidden), F32),
         ],
         cost_estimate=pl.CostEstimate(
-            flops=int(2 * 1e5), bytes_accessed=1000, transcendentals=0
+            flops=int(3e9), bytes_accessed=1000, transcendentals=0
         ),
-        compiler_params=pltpu.CompilerParams(vmem_limit_bytes=52 * 1024 * 1024),
+        compiler_params=pltpu.CompilerParams(vmem_limit_bytes=20 * 1024 * 1024),
     )(a, b, w_gate, w_up, *after)
 
 
-def down_kernel(n_dp, flip, merge, slots, grad_rows, *refs):
-    b_ref, far_ref, out_ref = refs[-3:]
-    hidden, piece = out_ref.shape
-    n_chip = b_ref.shape[0]
-    tiles = grad_rows // slots
-    count = n_chip * grad_rows
-    place = lax.axis_index("dp")
-    if merge:
-        own, near, low, high, last = refs[:5]
-        middle = hidden // 2
-        left = [
-            own[count:, :],
-            near[count:, :],
-            jnp.concatenate([low[count:, :], high[:middle, :]], axis=0),
-            last[:hidden, :],
-        ]
-        grads = [own[:count, :], near[:count, :], low[:count, :], last[hidden:, :]]
-    else:
-        left = [r[...] for r in refs[:n_dp]]
-        grads = [r[...] for r in refs[n_dp : 2 * n_dp]]
+def down_kernel(n_dp, flip, slots, grad_rows, *refs):
+    pieces = refs[:n_dp]
+    a_ref, b_ref, out_ref = refs[n_dp:]
+    n_chip = a_ref.shape[0]
+    piece = out_ref.shape[1]
+    base = a_ref.shape[1] - n_dp * grad_rows
     total = None
     for s in range(n_dp):
-        blocks = [grads[s][i * grad_rows : (i + 1) * grad_rows] for i in range(n_chip)]
-        if s == 0:
-            row = b_ref.shape[1] - n_dp * grad_rows + place * grad_rows
-            rows = pl.ds(pl.multiple_of(row, 16), grad_rows)
-            blocks += [b_ref[i, rows, :] for i in range(n_chip)]
-        else:
-            blocks += [far_ref[s - 1, i * grad_rows : (i + 1) * grad_rows, :] for i in range(n_chip)]
-        columns = [
-            jnp.concatenate([b[t * slots : (t + 1) * slots] for b in blocks], axis=0)
-            for t in range(tiles)
-        ]
+        columns = []
+        for t in range(grad_rows // slots):
+            row = base + s * grad_rows + t * slots
+            blocks = [r[i, row : row + slots, :] for r in (a_ref, b_ref) for i in range(n_chip)]
+            columns.append(jnp.concatenate(blocks, axis=0))
         right = jnp.concatenate(columns, axis=1)[:, :piece]
-        part = dot(left[s], right, 1 if flip else 0, 0)
+        part = dot(pieces[s][...], right, 1 if flip else 0, 0)
         total = part if total is None else total + part
     out_ref[...] = total.astype(BF16)
 
@@ -627,12 +577,11 @@
     part = width // 2
     many = heads // 2
     flip = w_gate.shape[2] % LANES == 0
-    merge = flip and 2 * n_chip * capacity == LANES and n_dp == 4
 
     grad_rows = -(-piece // LANES) * capacity
     w_half = lax.dynamic_slice_in_dim(w_bc, core * (share // 2), share // 2, 0)
 
-    n_rows = width // LANES * capacity + n_dp * grad_rows
+    in_rows = width // LANES * capacity
     blocks = [1, 1, 2] if n_chip == 4 else [1] * n_chip
     cumt, cum, steps, dyt, xs, carried, rows, *xt = call(
         lambda *refs: prep_kernel(n_dp, *refs),
@@ -644,21 +593,26 @@
             shape((length, width), BF16),
             shape((length, half), F32),
         ]
-        + [shape((n_rows, LANES), BF16)]
+        + [shape((in_rows, LANES), BF16)]
+        + [shape((grad_rows, LANES), BF16)] * n_dp
         + [shape((k * width // n_chip, length), BF16) for k in blocks],
         2.0,
         (x, dy, ldt, stept, h_in, slot_rows[0], slot_counts, slot_gates[0]),
-        scratch=[pltpu.VMEM((width, length), BF16)],
+        scratch=[
+            pltpu.VMEM((width, length), BF16),
+            pltpu.VMEM((n_dp, grad_rows, LANES), BF16),
+        ],
         fetch=(0, 1, 2, 3, 4),
         limit=60,
     )
     w_far = xored(w_half, "dp", n_dp // 2)
     mine = gathered(w_half, "dp", n_dp // 2)[1:]
     mine += gathered(joined([w_far], after=(cumt,)), "dp", n_dp // 2)
-    rows_in = chips([rows] * n_chip)
-    other = swapped(stacked(mine, after=tuple(rows_in[1:4])))
-    rows_a = stacked(rows_in, after=(other,))
-    rows_b = swapped(rows_a)
+    deals, xt = xt[:n_dp], xt[n_dp:]
+    deals = deals[:1] + [xored(d, "dp", s + 1) for s, d in enumerate(deals[1:])]
+    payload = joined([rows, *deals])
+    rows_in = chips([payload] * n_chip)
+    other = swapped(stacked(mine, after=(payload,)))
     w_whole, bc, keep, send = call(
         lambda *refs: project_kernel(n_dp - 1, many, *refs),
         [
@@ -672,24 +626,20 @@
     )
     recv = swapped(send)
     hidden = w_gate.shape[2]
-    near_rows = n_chip * grad_rows
-    outs = expert(
-        rows_a, rows_b, w_gate[0], w_up[0], capacity, grad_rows, n_dp, flip, merge, (keep,)
-    )
     climbs = [
         call(
             lambda *refs: combine_kernel(many, size, *refs),
             [shape((part + up16(2 * many), half), BF16)],
             0.5,
             (keep, recv),
-            after=(outs[0],),
         )[0]
     ]
+    rows_a = stacked(rows_in, after=(climbs[0],))
+    rows_b = swapped(rows_a)
+    weighted = expert(rows_a, rows_b, w_gate[0], w_up[0], capacity, flip, (climbs[0],))
     if n_chip == 4:
         x_rows = width // n_chip
         over_y = xored(xt[2], "tm", 4)
-    if merge:
-        low = xored(outs[2], "dp", 2)
 
     parts = 2
     tiles = width // LANES // parts
@@ -711,7 +661,7 @@
             scratch=[pltpu.VMEM((heads, length), F32)],
         )
         if i == 0:
-            held = (dx, *((over_y,) if n_chip == 4 else ()), *((low,) if merge else ()))
+            held = (dx, weighted, *((over_y,) if n_chip == 4 else ()))
             arrived = []
             bit = 1
             while bit < n_chip:
@@ -751,10 +701,9 @@
     else:
         columns_in = chips(xt)
         places = [(i, 0) for i in range(n_chip)]
-    if merge:
-        high = xored(joined([outs[3]], later), "dp", 2)
-        near = xored(outs[1], "dp", 1)
-        held += (high, near)
+    far = xored(weighted, "dp", n_dp // 2)
+    near = gathered(weighted, "dp", n_dp // 2)
+    held += (far, *near[1:])
     r_own, r_send = call(
         lambda *refs: carry_kernel(many, size, len(arrived), *refs),
         [shape((part, half), BF16)] * 2,
@@ -763,6 +712,7 @@
         after=held,
     )
     r_recv = swapped(r_send)
+    fars = gathered(joined([far], (r_own,)), "dp", n_dp // 2)
     d_bc = call(db_kernel, [shape((length, columns), BF16)], 0.3, (xs, r_own, r_recv, db, dc))[0]
     d_bcs = [d_bc.reshape(1, length, columns)]
     while 2 ** (len(d_bcs) - 1) < n_chip:
@@ -787,7 +737,7 @@
         [shape((w_rows, columns), F32), shape((w_rows, columns), BF16)],
         0.5,
         (*columns_in, *d_bcs),
-        after=(d_in,),
+        after=(d_in, *fars[1:]),
         scratch=[pltpu.VMEM((2, w_rows, columns), F32)],
     )
     final = call(
@@ -802,22 +752,11 @@
     for s in range(1, n_dp):
         w_bc_grad = w_bc_grad + xored(final[s], "dp", s).astype(F32)
 
-    if merge:
-        ranges = [(near_rows, low.shape[0]), (0, high.shape[0])]
-        last = xored(joined([low, high], (r_own,), ranges), "dp", 1)
-        pieces = [outs[0], near, low, high, last]
-        sent = [near, low, last]
-        ranges = [(0, near_rows), (0, near_rows), (hidden, hidden + near_rows)]
-    else:
-        sent = [xored(o, "dp", s + 1) for s, o in enumerate(outs[2:])]
-        pieces = [*gathered(outs[0], "dp", n_dp), outs[1], *sent]
-        ranges = None
-    far = swapped(stacked(sent, (term,), ranges))
     w_down_grad = call(
-        lambda *refs: down_kernel(n_dp, flip, merge, capacity, grad_rows, *refs),
+        lambda *refs: down_kernel(n_dp, flip, capacity, grad_rows, *refs),
         [shape((hidden, piece), BF16)],
         1.0,
-        (*pieces, rows_b, far),
+        (*near, *fars, rows_a, rows_b),
         after=(final[0],),
     )[0]
     return (d_in[None], d_decay.T[None], d_step.T[None], w_bc_grad, w_down_grad[None])

time: 94 us -> 85.1 us (0.905)
  waiting for transfers between devices: 35.6 us -> 24.2 us
  starting transfers between devices: 25.2 us -> 31.2 us
  Pallas kernels: 24.6 us -> 21.6 us
    ppermute x23 -> x24, waiting for transfers between devices: 35.6 us -> 24.2 us  [xored(): return lax.ppermute(array, axis, [(i, i ^ mask) for i in range(count)])]
    ppermute x23 -> x24, starting transfers between devices: 22.2 us -> 28.2 us  [xored(): return lax.ppermute(array, axis, [(i, i ^ mask) for i in range(count)])]
    pallas_call x1, Pallas kernels: 5.79 us -> 2.74 us  [expert(): pl.pallas_call(body, out_shape=shape(out, BF16), grid=(width // depth,),...]
    unnamed x38 -> x44, local copies, waits for them, and re-layouts: 4.76 us -> 4.42 us
    pallas_call x21 -> x20, Pallas kernels: 18.9 us -> 18.8 us  [call(): pl.pallas_call(body, out_shape=outs, in_specs=specs + [pl.BlockSpec(memor...]
  transfers between devices with their start and end apart: 25 -> 26, of which waited for: 13 -> 15; matrix products, arithmetic and copies ran while one was open for 1% -> 0% of each run, Pallas kernels for 23% -> 23%
where the time goes in v8:
time: 85.1 us; the launch traced here: 84.7 us
  starting transfers between devices  31.2 us (37%)
  waiting for transfers between devices  24.2 us (28%)
  Pallas kernels  21.6 us (25%)
  local copies, waits for them, and re-layouts  5.36 us (6%)
  between operations  1.69 us (2%)
    ppermute x24, starting transfers between devices, xored(): return lax.ppermute(array, axis, [(i, i ^ mask) for i in range(count)])  28.2 us
    ppermute x24, waiting for transfers between devices, xored(): return lax.ppermute(array, axis, [(i, i ^ mask) for i in range(count)])  24.2 us
    pallas_call x20, Pallas kernels, call(): pl.pallas_call(body, out_shape=outs, in_specs=specs + [pl.BlockSpec(memor...  18.8 us
    unnamed x44, local copies, waits for them, and re-layouts  4.42 us
    ppermute x2, starting transfers between devices, per_device(): arrived.append(lax.ppermute(climbs[-1], 'tm', moves))  3.03 us
    pallas_call x1, Pallas kernels, expert(): pl.pallas_call(body, out_shape=shape(out, BF16), grid=(width // depth,),...  2.74 us
  transfers between devices with their start and end apart: 26, of which 15 were waited for; matrix products, arithmetic and copies ran while one was open for 0% of the time, Pallas kernels for 23%

profile of v8, /device:TPU:0, one launch (start us, length us, event | category | flops | bytes accessed | tf_op | source)
XLA Modules:
  0.0 84.7 jit_solution(13321477902045470974)
XLA Ops:
  1.6 4.1 %collective-permute-start.1 = (bf16[320,256]{1,0:T(8,128)(2,1)S(1)}, bf16[320,256]{1,0:T(8,128)(2,1)S(1)}, u32[]{:S(2)}, u32[]{:S(2)}) collective-permute-start(bf16[320,256]{1,0:T(8,128)(2,1)S(1)} %constant_dynamic-slice_fusion), channel_id=1, source_target_pairs={{0,2},{1,3},{2,0},{3,1},{4,6},{5,7},{6,4},{7,5},{8,10},{9,11},{10,... | collective-permute-start | bytes 491528 | tf_op jit(solution)/shard_map/ppermute | solution.py:532
  5.7 1.6 %collective-permute-start = (bf16[320,256]{1,0:T(8,128)(2,1)S(1)}, bf16[320,256]{1,0:T(8,128)(2,1)S(1)}, u32[]{:S(2)}, u32[]{:S(2)}) collective-permute-start(bf16[320,256]{1,0:T(8,128)(2,1)S(1)} %constant_dynamic-slice_fusion), channel_id=1, source_target_pairs={{0,1},{1,0},{2,3},{3,2},{4,5},{5,4},{6,7},{7,6},{8,9},{9,8},{10,11... | collective-permute-start | bytes 491528 | tf_op jit(solution)/shard_map/ppermute | solution.py:532
  7.9 5.6 %shard_map.146 = (f32[40,128]{1,0:T(8,128)}, f32[128,128]{1,0:T(8,128)}, f32[128,128]{1,0:T(8,128)}, bf16[2640,128]{1,0:T(8,128)(2,1)}, bf16[128,2560]{1,0:T(8,1...) custom-call(bf16[128,2560]{1,0:T(8,128)(2,1)} %bitcast.33, ...), custom_call_target="tpu_custom_call" | custom-call | flops 6000000000 | bytes 1000 | tf_op jit(solution)/shard_map/pallas_call | solution.py:81
  16.6 1.8 %collective-permute-start.4 = (bf16[80,128]{1,0:T(8,128)(2,1)}, bf16[80,128]{1,0:T(8,128)(2,1)S(1)}, u32[]{:S(2)}, u32[]{:S(2)}) collective-permute-start(bf16[80,128]{1,0:T(8,128)(2,1)} %get-tuple-element.49), channel_id=1, source_target_pairs={{0,2},{1,3},{2,0},{3,1},{4,6},{5,7},{6,4},{7,5},{8,10},{9,11},{10,... | collective-permute-start | bytes 61448 | tf_op jit(solution)/shard_map/ppermute | solution.py:532
  21.4 2.7 %collective-permute-done.5.refs_4_ = bf16[80,128]{1,0:T(8,128)(2,1)S(1)} collective-permute-done((bf16[80,128]{1,0:T(8,128)(2,1)}, bf16[80,128]{1,0:T(8,128)(2,1)S(1)}, u32[]{:S(2)}, u32[]{:S(2)}) %collective-permute-start.5) | collective-permute-done | bytes 20512 | tf_op jit(solution)/shard_map/ppermute | solution.py:532
  25.9 1.9 %collective-permute-done.6.refs_6_ = bf16[3,320,256]{2,1,0:T(8,128)(2,1)S(1)} collective-permute-done((bf16[3,320,256]{2,1,0:T(8,128)(2,1)S(1)}, bf16[3,320,256]{2,1,0:T(8,128)(2,1)S(1)}, u32[]{:S(2)}, u32[]{:S(2)}) %collective-permute-start.6) | collective-permute-done | bytes 491552 | tf_op jit(solution)/shard_map/ppermute | solution.py:532
  29.1 2.5 %collective-permute-start.11 = (bf16[640,128]{1,0:T(8,128)(2,1)S(1)}, bf16[640,128]{1,0:T(8,128)(2,1)S(1)}, u32[]{:S(2)}, u32[]{:S(2)}) collective-permute-start(bf16[640,128]{1,0:T(8,128)(2,1)S(1)} %shard_map.148.refs_3_.refs_0_), channel_id=1, source_target_pairs={{0,24},{4,28},{8,16},{12,20},{16,8},{20,12},{24,0},{28,4},{1,25},{... | collective-permute-start | bytes 491528 | tf_op jit(solution)/shard_map/ppermute | solution.py:532
  34.3 1.6 %collective-permute-start.8 = (bf16[1328,128]{1,0:T(8,128)(2,1)S(1)}, bf16[1328,128]{1,0:T(8,128)(2,1)S(1)}, u32[]{:S(2)}, u32[]{:S(2)}) collective-permute-start(bf16[1328,128]{1,0:T(8,128)(2,1)S(1)} %shard_map.151.refs_4_.refs_0_), channel_id=1, source_target_pairs={{0,8},{4,12},{8,0},{12,4},{16,24},{20,28},{24,16},{28,20},{1,9},{5... | collective-permute-start | bytes 1019912 | tf_op jit(solution)/shard_map/ppermute | solution.py:672
  37.1 3.0 %collective-permute-done.10.refs_2_ = bf16[640,128]{1,0:T(8,128)(2,1)S(1)} collective-permute-done((bf16[640,128]{1,0:T(8,128)(2,1)S(1)}, bf16[640,128]{1,0:T(8,128)(2,1)S(1)}, u32[]{:S(2)}, u32[]{:S(2)}) %collective-permute-start.10) | collective-permute-done | bytes 163872 | tf_op jit(solution)/shard_map/ppermute | solution.py:532
  40.9 2.6 %shard_map.152 = (f32[128,1280]{1,0:T(8,128)S(1)}, f32[128,128]{1,0:T(8,128)S(1)}, f32[20,128]{1,0:T(8,128)S(1)}, f32[20,128]{1,0:T(8,128)S(1)}) custom-call(bf16[128,2560]{1,0:T(8,128)(2,1)S(1)} %bitcast.35, bf16[128,2560]{1,0:T(8,128)(2,1)S(1)} %bitcast.31, bf16[128,256]{1,0:T(8,128)(2,1)S(1)} %get-tuple-element.51.refs_2_.refs_1_, ...), custom_call_target="tpu_custom_call" | custom-call | flops 8999999488 | bytes 1000 | tf_op jit(solution)/shard_map/pallas_call | solution.py:81
  44.3 2.7 %shard_map.154.refs_3_.refs_0_ = bf16[896,128]{1,0:T(8,128)(2,1)S(1)} custom-call(bf16[4,640,128]{2,1,0:T(8,128)(2,1)S(1)} %bitcast.43, bf16[4,640,128]{2,1,0:T(8,128)(2,1)S(1)} %collective-permute-done.12.refs_1_.refs_5_, bf16[2560,896]{1,0:T(8,128)(2,1)S(1)} %bitcast.26, bf16[2560,896]{1,0:T(8,128)(2,1)S(1)} %bitcast.29, ...), custom_call_target="tpu_custom_call" | custom-call | flops 3000000000 | bytes 1000 | tf_op jit(solution)/shard_map/pallas_call | solution.py:492
  47.2 1.8 %collective-permute-start.16 = (bf16[896,128]{1,0:T(8,128)(2,1)S(1)}, bf16[896,128]{1,0:T(8,128)(2,1)S(1)}, u32[]{:S(2)}, u32[]{:S(2)}) collective-permute-start(bf16[896,128]{1,0:T(8,128)(2,1)S(1)} %shard_map.154.refs_3_.refs_0_), channel_id=1, source_target_pairs={{0,2},{1,3},{2,0},{3,1},{4,6},{5,7},{6,4},{7,5},{8,10},{9,11},{10,... | collective-permute-start | bytes 688136 | tf_op jit(solution)/shard_map/ppermute | solution.py:532
  50.8 1.6 %collective-permute-start.15 = (bf16[1280,128]{1,0:T(8,128)(2,1)S(1)}, bf16[1280,128]{1,0:T(8,128)(2,1)S(1)}, u32[]{:S(2)}, u32[]{:S(2)}) collective-permute-start(bf16[1280,128]{1,0:T(8,128)(2,1)S(1)} %shard_map.158), channel_id=1, source_target_pairs={{0,8},{4,12},{8,0},{12,4},{16,24},{20,28},{24,16},{28,20},{1,9},{5... | collective-permute-start | bytes 983048 | tf_op jit(solution)/shard_map/ppermute | solution.py:532
  52.3 2.6 %shard_map.156 = (f32[128,1280]{1,0:T(8,128)S(1)}, f32[128,128]{1,0:T(8,128)S(1)}, f32[20,128]{1,0:T(8,128)S(1)}, f32[20,128]{1,0:T(8,128)S(1)}) custom-call(bf16[128,2560]{1,0:T(8,128)(2,1)S(1)} %bitcast.36, bf16[128,2560]{1,0:T(8,128)(2,1)S(1)} %bitcast.32, bf16[128,256]{1,0:T(8,128)(2,1)S(1)} %get-tuple-element.51.refs_2_.refs_1_, ...), custom_call_target="tpu_custom_call" | custom-call | flops 8999999488 | bytes 1000 | tf_op jit(solution)/shard_map/pallas_call | solution.py:81
  55.1 2.9 %collective-permute-done.17.refs_7_.refs_1_ = bf16[896,128]{1,0:T(8,128)(2,1)S(1)} collective-permute-done((bf16[896,128]{1,0:T(8,128)(2,1)S(1)}, bf16[896,128]{1,0:T(8,128)(2,1)S(1)}, u32[]{:S(2)}, u32[]{:S(2)}) %collective-permute-start.17) | collective-permute-done | bytes 229408 | tf_op jit(solution)/shard_map/ppermute | solution.py:532
  58.0 2.3 %collective-permute-done.16.refs_6_.refs_0_ = bf16[896,128]{1,0:T(8,128)(2,1)S(1)} collective-permute-done((bf16[896,128]{1,0:T(8,128)(2,1)S(1)}, bf16[896,128]{1,0:T(8,128)(2,1)S(1)}, u32[]{:S(2)}, u32[]{:S(2)}) %collective-permute-start.16) | collective-permute-done | bytes 229408 | tf_op jit(solution)/shard_map/ppermute | solution.py:532
  60.7 1.6 %collective-permute-done.18.refs_2_.refs_8_ = bf16[1280,128]{1,0:T(8,128)(2,1)S(1)} collective-permute-done((bf16[1280,128]{1,0:T(8,128)(2,1)S(1)}, bf16[1280,128]{1,0:T(8,128)(2,1)S(1)}, u32[]{:S(2)}, u32[]{:S(2)}) %collective-permute-start.18) | collective-permute-done | bytes 327712 | tf_op jit(solution)/shard_map/ppermute | solution.py:532
  62.7 1.6 %collective-permute-start.19 = (bf16[1,128,256]{2,1,0:T(8,128)(2,1)S(1)}, bf16[1,128,256]{2,1,0:T(8,128)(2,1)S(1)}, u32[]{:S(2)}, u32[]{:S(2)}) collective-permute-start(bf16[1,128,256]{2,1,0:T(8,128)(2,1)S(1)} %bitcast.46), channel_id=1, source_target_pairs={{0,8},{4,12},{8,0},{12,4},{16,24},{20,28},{24,16},{28,20},{1,9},{5... | collective-permute-start | bytes 196616 | tf_op jit(solution)/shard_map/ppermute | solution.py:532
  64.6 2.4 %collective-permute-done.19.refs_1_.refs_4_ = bf16[1,128,256]{2,1,0:T(8,128)(2,1)S(1)} collective-permute-done((bf16[1,128,256]{2,1,0:T(8,128)(2,1)S(1)}, bf16[1,128,256]{2,1,0:T(8,128)(2,1)S(1)}, u32[]{:S(2)}, u32[]{:S(2)}) %collective-permute-start.19) | collective-permute-done | bytes 65568 | tf_op jit(solution)/shard_map/ppermute | solution.py:532
  67.0 1.8 %collective-permute-start.20 = (bf16[2,128,256]{2,1,0:T(8,128)(2,1)S(1)}, bf16[2,128,256]{2,1,0:T(8,128)(2,1)S(1)}, u32[]{:S(2)}, u32[]{:S(2)}) collective-permute-start(bf16[2,128,256]{2,1,0:T(8,128)(2,1)S(1)} %shard_map.162), channel_id=1, source_target_pairs={{0,16},{4,20},{8,24},{12,28},{16,0},{20,4},{24,8},{28,12},{1,17},{... | collective-permute-start | bytes 393224 | tf_op jit(solution)/shard_map/ppermute | solution.py:532
  68.8 2.6 %shard_map.161 = (bf16[128,2560]{1,0:T(8,128)(2,1)}, f32[40,128]{1,0:T(8,128)}, f32[40,128]{1,0:T(8,128)}) custom-call(bf16[128,2560]{1,0:T(8,128)(2,1)S(1)} %bitcast.37, bf16[128,256]{1,0:T(8,128)(2,1)S(1)} %get-tuple-element.51.refs_2_.refs_1_, f32[40,128]{1,0:T(8,128)S(1)} %copy-done.13, f32[40,128]{1,0:T(8,128)S(1)} %bitcast.50, ...), custom_call_target="tpu_custom_call" | custom-call | flops 8999999488 | bytes 1000 | tf_op jit(solution)/shard_map/pallas_call | solution.py:81
  75.6 2.6 %collective-permute-start.24 = (bf16[80,256]{1,0:T(8,128)(2,1)S(1)}, bf16[80,256]{1,0:T(8,128)(2,1)S(1)}, u32[]{:S(2)}, u32[]{:S(2)}) collective-permute-start(bf16[80,256]{1,0:T(8,128)(2,1)S(1)} %get-tuple-element.81), channel_id=1, source_target_pairs={{0,2},{1,3},{2,0},{3,1},{4,6},{5,7},{6,4},{7,5},{8,10},{9,11},{10,... | collective-permute-start | bytes 122888 | tf_op jit(solution)/shard_map/ppermute | solution.py:532
  79.7 2.3 %shard_map.166 = bf16[896,640]{1,0:T(8,128)(2,1)} custom-call(bf16[896,128]{1,0:T(8,128)(2,1)S(1)} %shard_map.154.refs_3_.refs_0_, bf16[896,128]{1,0:T(8,128)(2,1)S(1)} %collective-permute-done.17.refs_7_.refs_1_, bf16[896,128]{1,0:T(8,128)(2,1)S(1)} %shard_map.163.refs_2_, bf16[896,128]{1,0:T(8,128)(2,1)S(1)} %collective-permute-done.21.refs_7_.refs_3_, ...), custom_call_target="tpu_custom_call" | custom-call | flops 3000000000 | bytes 1000 | tf_op jit(solution)/shard_map/pallas_call | solution.py:81
  82.1 2.0 %collective-permute-done.25 = bf16[80,256]{1,0:T(8,128)(2,1)S(1)} collective-permute-done((bf16[80,256]{1,0:T(8,128)(2,1)S(1)}, bf16[80,256]{1,0:T(8,128)(2,1)S(1)}, u32[]{:S(2)}, u32[]{:S(2)}) %collective-permute-start.25) | collective-permute-done | bytes 40992 | tf_op jit(solution)/shard_map/ppermute | solution.py:532
  (98 shorter events, 24.9 us)
Async XLA Ops:
  1.6 12.0 %collective-permute-start.1 = (bf16[320,256]{1,0:T(8,128)(2,1)S(1)}, bf16[320,256]{1,0:T(8,128)(2,1)S(1)}, u32[]{:S(2)}, u32[]{:S(2)}) collective-permute-start(bf16[320,256]{1,0:T(8,128)(2,1)S(1)} %constant_dynamic-slice_fusion), channel_id=1, source_target_pairs={{0,2},{1,3},{2,0},{3,1},{4,6},{5,7},{6,4},{7,5},{8,10},{9,11},{10,... | collective-permute-start | bytes 491528 | tf_op jit(solution)/shard_map/ppermute | solution.py:532
  5.7 20.1 %collective-permute-start = (bf16[320,256]{1,0:T(8,128)(2,1)S(1)}, bf16[320,256]{1,0:T(8,128)(2,1)S(1)}, u32[]{:S(2)}, u32[]{:S(2)}) collective-permute-start(bf16[320,256]{1,0:T(8,128)(2,1)S(1)} %constant_dynamic-slice_fusion), channel_id=1, source_target_pairs={{0,1},{1,0},{2,3},{3,2},{4,5},{5,4},{6,7},{7,6},{8,9},{9,8},{10,11... | collective-permute-start | bytes 491528 | tf_op jit(solution)/shard_map/ppermute | solution.py:532
  14.5 11.4 %collective-permute-start.2 = (bf16[320,256]{1,0:T(8,128)(2,1)S(1)}, bf16[320,256]{1,0:T(8,128)(2,1)S(1)}, u32[]{:S(2)}, u32[]{:S(2)}) collective-permute-start(bf16[320,256]{1,0:T(8,128)(2,1)S(1)} %shard_map.147.refs_1_.refs_4_), channel_id=1, source_target_pairs={{0,1},{1,0},{2,3},{3,2},{4,5},{5,4},{6,7},{7,6},{8,9},{9,8},{10,11... | collective-permute-start | bytes 491528 | tf_op jit(solution)/shard_map/ppermute | solution.py:532
  15.0 5.5 %collective-permute-start.3 = (bf16[80,128]{1,0:T(8,128)(2,1)}, bf16[80,128]{1,0:T(8,128)(2,1)S(1)}, u32[]{:S(2)}, u32[]{:S(2)}) collective-permute-start(bf16[80,128]{1,0:T(8,128)(2,1)} %get-tuple-element.48), channel_id=1, source_target_pairs={{0,1},{1,0},{2,3},{3,2},{4,5},{5,4},{6,7},{7,6},{8,9},{9,8},{10,11... | collective-permute-start | bytes 61448 | tf_op jit(solution)/shard_map/ppermute | solution.py:532
  16.6 4.9 %collective-permute-start.4 = (bf16[80,128]{1,0:T(8,128)(2,1)}, bf16[80,128]{1,0:T(8,128)(2,1)S(1)}, u32[]{:S(2)}, u32[]{:S(2)}) collective-permute-start(bf16[80,128]{1,0:T(8,128)(2,1)} %get-tuple-element.49), channel_id=1, source_target_pairs={{0,2},{1,3},{2,0},{3,1},{4,6},{5,7},{6,4},{7,5},{8,10},{9,11},{10,... | collective-permute-start | bytes 61448 | tf_op jit(solution)/shard_map/ppermute | solution.py:532
  18.4 5.8 %collective-permute-start.5 = (bf16[80,128]{1,0:T(8,128)(2,1)}, bf16[80,128]{1,0:T(8,128)(2,1)S(1)}, u32[]{:S(2)}, u32[]{:S(2)}) collective-permute-start(bf16[80,128]{1,0:T(8,128)(2,1)} %get-tuple-element.50), channel_id=1, source_target_pairs={{0,3},{1,2},{2,1},{3,0},{4,7},{5,6},{6,5},{7,4},{8,11},{9,10},{10,... | collective-permute-start | bytes 61448 | tf_op jit(solution)/shard_map/ppermute | solution.py:532
  25.9 1.9 %collective-permute-start.6 = (bf16[3,320,256]{2,1,0:T(8,128)(2,1)S(1)}, bf16[3,320,256]{2,1,0:T(8,128)(2,1)S(1)}, u32[]{:S(2)}, u32[]{:S(2)}) collective-permute-start(bf16[3,320,256]{2,1,0:T(8,128)(2,1)S(1)} %bitcast.45), channel_id=1, source_target_pairs={{0,4},{4,0},{8,12},{12,8},{16,20},{20,16},{24,28},{28,24},{1,5},{5... | collective-permute-start | bytes 1474568 | tf_op jit(solution)/shard_map/ppermute | solution.py:532
  28.9 5.2 %collective-permute-start.7 = (bf16[1328,128]{1,0:T(8,128)(2,1)S(1)}, bf16[1328,128]{1,0:T(8,128)(2,1)S(1)}, u32[]{:S(2)}, u32[]{:S(2)}) collective-permute-start(bf16[1328,128]{1,0:T(8,128)(2,1)S(1)} %get-tuple-element.55), channel_id=1, source_target_pairs={{0,4},{4,0},{8,12},{12,8},{16,20},{20,16},{24,28},{28,24},{1,5},{5... | collective-permute-start | bytes 1019912 | tf_op jit(solution)/shard_map/ppermute | solution.py:532
  29.1 8.0 %collective-permute-start.11 = (bf16[640,128]{1,0:T(8,128)(2,1)S(1)}, bf16[640,128]{1,0:T(8,128)(2,1)S(1)}, u32[]{:S(2)}, u32[]{:S(2)}) collective-permute-start(bf16[640,128]{1,0:T(8,128)(2,1)S(1)} %shard_map.148.refs_3_.refs_0_), channel_id=1, source_target_pairs={{0,24},{4,28},{8,16},{12,20},{16,8},{20,12},{24,0},{28,4},{1,25},{... | collective-permute-start | bytes 491528 | tf_op jit(solution)/shard_map/ppermute | solution.py:532
  31.6 8.5 %collective-permute-start.10 = (bf16[640,128]{1,0:T(8,128)(2,1)S(1)}, bf16[640,128]{1,0:T(8,128)(2,1)S(1)}, u32[]{:S(2)}, u32[]{:S(2)}) collective-permute-start(bf16[640,128]{1,0:T(8,128)(2,1)S(1)} %shard_map.148.refs_3_.refs_0_), channel_id=1, source_target_pairs={{0,16},{4,20},{8,24},{12,28},{16,0},{20,4},{24,8},{28,12},{1,17},{... | collective-permute-start | bytes 491528 | tf_op jit(solution)/shard_map/ppermute | solution.py:532
  32.1 8.6 %collective-permute-start.9 = (bf16[640,128]{1,0:T(8,128)(2,1)S(1)}, bf16[640,128]{1,0:T(8,128)(2,1)S(1)}, u32[]{:S(2)}, u32[]{:S(2)}) collective-permute-start(bf16[640,128]{1,0:T(8,128)(2,1)S(1)} %shard_map.148.refs_3_.refs_0_), channel_id=1, source_target_pairs={{0,8},{4,12},{8,0},{12,4},{16,24},{20,28},{24,16},{28,20},{1,9},{5... | collective-permute-start | bytes 491528 | tf_op jit(solution)/shard_map/ppermute | solution.py:532
  32.6 16.4 %collective-permute-start.13 = (bf16[1280,128]{1,0:T(8,128)(2,1)S(1)}, bf16[1280,128]{1,0:T(8,128)(2,1)S(1)}, u32[]{:S(2)}, u32[]{:S(2)}) collective-permute-start(bf16[1280,128]{1,0:T(8,128)(2,1)S(1)} %copy-done.17), channel_id=1, source_target_pairs={{0,16},{4,20},{8,24},{12,28},{16,0},{20,4},{24,8},{28,12},{1,17},{... | collective-permute-start | bytes 983048 | tf_op jit(solution)/shard_map/ppermute | solution.py:532
  34.3 14.7 %collective-permute-start.8 = (bf16[1328,128]{1,0:T(8,128)(2,1)S(1)}, bf16[1328,128]{1,0:T(8,128)(2,1)S(1)}, u32[]{:S(2)}, u32[]{:S(2)}) collective-permute-start(bf16[1328,128]{1,0:T(8,128)(2,1)S(1)} %shard_map.151.refs_4_.refs_0_), channel_id=1, source_target_pairs={{0,8},{4,12},{8,0},{12,4},{16,24},{20,28},{24,16},{28,20},{1,9},{5... | collective-permute-start | bytes 1019912 | tf_op jit(solution)/shard_map/ppermute | solution.py:672
  40.7 2.8 %collective-permute-start.12 = (bf16[4,640,128]{2,1,0:T(8,128)(2,1)S(1)}, bf16[4,640,128]{2,1,0:T(8,128)(2,1)S(1)}, u32[]{:S(2)}, u32[]{:S(2)}) collective-permute-start(bf16[4,640,128]{2,1,0:T(8,128)(2,1)S(1)} %bitcast.42), channel_id=1, source_target_pairs={{0,4},{4,0},{8,12},{12,8},{16,20},{20,16},{24,28},{28,24},{1,5},{5... | collective-permute-start | bytes 1966088 | tf_op jit(solution)/shard_map/ppermute | solution.py:532
  47.0 11.0 %collective-permute-start.17 = (bf16[896,128]{1,0:T(8,128)(2,1)S(1)}, bf16[896,128]{1,0:T(8,128)(2,1)S(1)}, u32[]{:S(2)}, u32[]{:S(2)}) collective-permute-start(bf16[896,128]{1,0:T(8,128)(2,1)S(1)} %shard_map.154.refs_3_.refs_0_), channel_id=1, source_target_pairs={{0,1},{1,0},{2,3},{3,2},{4,5},{5,4},{6,7},{7,6},{8,9},{9,8},{10,11... | collective-permute-start | bytes 688136 | tf_op jit(solution)/shard_map/ppermute | solution.py:532
  47.2 13.1 %collective-permute-start.16 = (bf16[896,128]{1,0:T(8,128)(2,1)S(1)}, bf16[896,128]{1,0:T(8,128)(2,1)S(1)}, u32[]{:S(2)}, u32[]{:S(2)}) collective-permute-start(bf16[896,128]{1,0:T(8,128)(2,1)S(1)} %shard_map.154.refs_3_.refs_0_), channel_id=1, source_target_pairs={{0,2},{1,3},{2,0},{3,1},{4,6},{5,7},{6,4},{7,5},{8,10},{9,11},{10,... | collective-permute-start | bytes 688136 | tf_op jit(solution)/shard_map/ppermute | solution.py:532
  49.2 11.1 %collective-permute-start.14 = (bf16[1328,128]{1,0:T(8,128)(2,1)S(1)}, bf16[1328,128]{1,0:T(8,128)(2,1)S(1)}, u32[]{:S(2)}, u32[]{:S(2)}) collective-permute-start(bf16[1328,128]{1,0:T(8,128)(2,1)S(1)} %shard_map.155.refs_8_.refs_2_), channel_id=1, source_target_pairs={{16,0},{20,4},{24,8},{28,12},{17,1},{21,5},{25,9},{29,13},{18,2},{... | collective-permute-start | bytes 1019912 | tf_op jit(solution)/shard_map/ppermute | solution.py:672
  50.8 9.5 %collective-permute-start.15 = (bf16[1280,128]{1,0:T(8,128)(2,1)S(1)}, bf16[1280,128]{1,0:T(8,128)(2,1)S(1)}, u32[]{:S(2)}, u32[]{:S(2)}) collective-permute-start(bf16[1280,128]{1,0:T(8,128)(2,1)S(1)} %shard_map.158), channel_id=1, source_target_pairs={{0,8},{4,12},{8,0},{12,4},{16,24},{20,28},{24,16},{28,20},{1,9},{5... | collective-permute-start | bytes 983048 | tf_op jit(solution)/shard_map/ppermute | solution.py:532
  62.7 4.3 %collective-permute-start.19 = (bf16[1,128,256]{2,1,0:T(8,128)(2,1)S(1)}, bf16[1,128,256]{2,1,0:T(8,128)(2,1)S(1)}, u32[]{:S(2)}, u32[]{:S(2)}) collective-permute-start(bf16[1,128,256]{2,1,0:T(8,128)(2,1)S(1)} %bitcast.46), channel_id=1, source_target_pairs={{0,8},{4,12},{8,0},{12,4},{16,24},{20,28},{24,16},{28,20},{1,9},{5... | collective-permute-start | bytes 196616 | tf_op jit(solution)/shard_map/ppermute | solution.py:532
  64.3 7.4 %collective-permute-start.21 = (bf16[896,128]{1,0:T(8,128)(2,1)S(1)}, bf16[896,128]{1,0:T(8,128)(2,1)S(1)}, u32[]{:S(2)}, u32[]{:S(2)}) collective-permute-start(bf16[896,128]{1,0:T(8,128)(2,1)S(1)} %shard_map.163.refs_2_), channel_id=1, source_target_pairs={{0,1},{1,0},{2,3},{3,2},{4,5},{5,4},{6,7},{7,6},{8,9},{9,8},{10,11... | collective-permute-start | bytes 688136 | tf_op jit(solution)/shard_map/ppermute | solution.py:532
  67.0 5.0 %collective-permute-start.20 = (bf16[2,128,256]{2,1,0:T(8,128)(2,1)S(1)}, bf16[2,128,256]{2,1,0:T(8,128)(2,1)S(1)}, u32[]{:S(2)}, u32[]{:S(2)}) collective-permute-start(bf16[2,128,256]{2,1,0:T(8,128)(2,1)S(1)} %shard_map.162), channel_id=1, source_target_pairs={{0,16},{4,20},{8,24},{12,28},{16,0},{20,4},{24,8},{28,12},{1,17},{... | collective-permute-start | bytes 393224 | tf_op jit(solution)/shard_map/ppermute | solution.py:532
  75.3 6.8 %collective-permute-start.23 = (bf16[80,256]{1,0:T(8,128)(2,1)S(1)}, bf16[80,256]{1,0:T(8,128)(2,1)S(1)}, u32[]{:S(2)}, u32[]{:S(2)}) collective-permute-start(bf16[80,256]{1,0:T(8,128)(2,1)S(1)} %get-tuple-element.80), channel_id=1, source_target_pairs={{0,1},{1,0},{2,3},{3,2},{4,5},{5,4},{6,7},{7,6},{8,9},{9,8},{10,11... | collective-permute-start | bytes 122888 | tf_op jit(solution)/shard_map/ppermute | solution.py:532
  75.6 6.5 %collective-permute-start.24 = (bf16[80,256]{1,0:T(8,128)(2,1)S(1)}, bf16[80,256]{1,0:T(8,128)(2,1)S(1)}, u32[]{:S(2)}, u32[]{:S(2)}) collective-permute-start(bf16[80,256]{1,0:T(8,128)(2,1)S(1)} %get-tuple-element.81), channel_id=1, source_target_pairs={{0,2},{1,3},{2,0},{3,1},{4,6},{5,7},{6,4},{7,5},{8,10},{9,11},{10,... | collective-permute-start | bytes 122888 | tf_op jit(solution)/shard_map/ppermute | solution.py:532
  78.2 5.8 %collective-permute-start.25 = (bf16[80,256]{1,0:T(8,128)(2,1)S(1)}, bf16[80,256]{1,0:T(8,128)(2,1)S(1)}, u32[]{:S(2)}, u32[]{:S(2)}) collective-permute-start(bf16[80,256]{1,0:T(8,128)(2,1)S(1)} %get-tuple-element.82), channel_id=1, source_target_pairs={{0,3},{1,2},{2,1},{3,0},{4,7},{5,6},{6,5},{7,4},{8,11},{9,10},{10,... | collective-permute-start | bytes 122888 | tf_op jit(solution)/shard_map/ppermute | solution.py:532
  (24 other events, 152.1 us)

commit v9 on v8

--- a/solution.py
+++ b/solution.py
@@ -114,8 +114,8 @@
     for t in range(width // LANES):
         rows_ref[t * slots : (t + 1) * slots, :] = rows[:, t * LANES : (t + 1) * LANES]
     grads = dot(jnp.where(hit, weight, 0.0).astype(BF16), dy_ref[...], 0, 0).astype(BF16)
-    n_dp = len(out_refs) - 1
     held = out_refs[-1]
+    n_dp = held.shape[0]
     piece = width // n_dp
     for i in range(n_dp):
         for t, low in enumerate(range(i * piece, (i + 1) * piece, LANES)):
@@ -125,8 +125,14 @@
                 block = jnp.concatenate([block, fill], axis=1)
             held[i, t * slots : (t + 1) * slots, :] = block
     place = lax.axis_index("dp")
-    for s, out in enumerate(out_refs[:-1]):
-        out[...] = held[place ^ s]
+    s = 0
+    for start in range(width // LANES * slots, rows_ref.shape[0], held.shape[1]):
+        rows_ref[start : start + held.shape[1], :] = held[place ^ s]
+        s += 1
+    for out in out_refs[:-1]:
+        for start in range(0, out.shape[0], held.shape[1]):
+            out[start : start + held.shape[1], :] = held[place ^ s]
+            s += 1
 
 
 def high_low(values):
@@ -135,15 +141,15 @@
 
 
 def prep_kernel(
-    n_dp, x_ref, dy_ref, ldt_ref, stept_ref, h_ref, slot_ref, count_ref, gate_ref,
+    n_deals, x_ref, dy_ref, ldt_ref, stept_ref, h_ref, slot_ref, count_ref, gate_ref,
     cumt_ref, cum_ref, step_ref, dyt_ref, xs_ref, carried_ref, rows_ref, *rest,
 ):
-    outs, xt_ref, held_ref = rest[n_dp:-2], rest[-2], rest[-1]
+    outs, xt_ref, held_ref = rest[n_deals:-2], rest[-2], rest[-1]
     length, width = x_ref.shape
     heads = ldt_ref.shape[0]
     size = width // heads
     _, chip, n_chip = core_and_chip()
-    picked(x_ref, dy_ref, slot_ref, count_ref, gate_ref, rows_ref, (*rest[:n_dp], held_ref))
+    picked(x_ref, dy_ref, slot_ref, count_ref, gate_ref, rows_ref, (*rest[:n_deals], held_ref))
     pad = jnp.zeros((LANES - heads, length), F32)
     cumt = dot(ldt_ref[...], triangle(length, lambda a, b: a <= b), 1, 0, HI)
     cumt_ref[...] = cumt
@@ -200,6 +206,37 @@
     return out.reshape(count, out.shape[0] // count, *out.shape[1:])
 
 
+def pack_kernel(w_ref, one_ref, two_ref, out_ref):
+    w_rows, rows = w_ref.shape[0], two_ref.shape[0] // 2
+    for i in range(2):
+        out_ref[i * w_rows : (i + 1) * w_rows, :] = w_ref[:, i * LANES : (i + 1) * LANES]
+    out_ref[2 * w_rows : 2 * w_rows + rows, :] = one_ref[one_ref.shape[0] - rows :, :]
+    out_ref[2 * w_rows + rows :, :] = two_ref[rows:, :]
+
+
+def packed(arrays, rows, after):
+    total = 2 * arrays[0].shape[0] + 2 * rows
+    return call(pack_kernel, [shape((total, LANES), BF16)], 0.2, tuple(arrays), after)[0]
+
+
+def stack_w_kernel(*refs):
+    out = refs[-1]
+    rows = out.shape[1]
+    for i, ref in enumerate(refs[:-1]):
+        wide = ref.shape[1] == out.shape[2]
+        out[i] = ref[...] if wide else unpacked(ref, rows)
+
+
+def unpacked(ref, rows):
+    return jnp.concatenate([ref[:rows, :], ref[rows : 2 * rows, :]], axis=1)
+
+
+def stack_w(arrays, rows):
+    return call(
+        stack_w_kernel, [shape((len(arrays), rows, 2 * LANES), BF16)], 0.2, tuple(arrays)
+    )[0]
+
+
 def project_kernel(n_mine, many, *refs):
     x_ref, dyt_ref, own_ref = refs[:3]
     mine, other = refs[3 : 3 + n_mine], refs[3 + n_mine]
@@ -211,7 +248,8 @@
     w_ref[rows_at(place, share), :] = own_ref[...]
     for i in range(n_mine):
         source = place ^ (i + 1)
-        w_ref[rows_at(source * 2 + core, half), :] = mine[i][...]
+        wide = mine[i].shape[1] == w_ref.shape[1]
+        w_ref[rows_at(source * 2 + core, half), :] = mine[i][...] if wide else unpacked(mine[i], half)
         w_ref[rows_at(source * 2 + 1 - core, half), :] = other[i]
     bc = dot(x_ref[...], w_ref[...], 1, 0).astype(BF16)
     bc_ref[...] = bc
@@ -375,7 +413,8 @@
     (x_ref, bc_ref, cumt_ref, stept_ref, cum_ref, step_ref, h_ref, own_ref, recv_ref,
      w_ref, dbc_ref) = refs[:11]
     dx_refs, ex_refs, st_refs = (refs[11 + i * parts : 11 + (i + 1) * parts] for i in range(3))
-    in_ref, decay_ref, grad_ref, r_ref, edge_ref = refs[11 + 3 * parts :]
+    in_ref, decay_ref, grad_ref, token_ref, r_ref, edge_ref = refs[11 + 3 * parts :]
+    token_ref[...] = jnp.zeros_like(token_ref)
     core, _, _ = core_and_chip()
     length, width = x_ref.shape
     heads = cumt_ref.shape[0]
@@ -449,8 +488,8 @@
         out[...] = held[place ^ (s + 1)].astype(BF16)
 
 
-def expert_kernel(flip, slots, a_ref, b_ref, gate_ref, up_ref, out_ref, *scratch):
-    rows_ref, gate_acc, up_acc = scratch
+def expert_kernel(flip, slots, a_ref, b_ref, gate_ref, up_ref, *refs):
+    outs, (rows_ref, gate_acc, up_acc) = refs[:-3], refs[-3:]
     step = pl.program_id(0)
     n_chip = a_ref.shape[0]
 
@@ -474,7 +513,12 @@
     @pl.when(step == pl.num_programs(0) - 1)
     def _():
         weighted = jax.nn.silu(gate_acc[...]) * up_acc[...]
-        out_ref[...] = (weighted.T if flip else weighted).astype(BF16)
+        weighted = (weighted.T if flip else weighted).astype(BF16)
+        outs[0][...] = weighted
+        at = 0
+        for out in outs[1:]:
+            out[...] = weighted[at : at + out.shape[0]]
+            at += out.shape[0]
 
 
 def expert(a, b, w_gate, w_up, slots, flip, after):
@@ -482,7 +526,8 @@
     total = 2 * n_chip * slots
     width, hidden = w_gate.shape
     depth = 512
-    out = (hidden, total) if flip else (total, hidden)
+    rows, lanes = (hidden, total) if flip else (total, hidden)
+    outs = [(rows, lanes), (rows // 2, lanes), (rows // 2, lanes)]
 
     def body(*refs):
         expert_kernel(flip, slots, *refs[:4], *refs[4 + len(after) :])
@@ -491,11 +536,11 @@
     block = pl.BlockSpec((depth, hidden), lambda i: (i, 0))
     return pl.pallas_call(
         body,
-        out_shape=shape(out, BF16),
+        out_shape=[shape(o, BF16) for o in outs],
         grid=(width // depth,),
         in_specs=[whole, whole, block, block]
         + [pl.BlockSpec(memory_space=pl.ANY)] * len(after),
-        out_specs=pl.BlockSpec(out, lambda i: (0, 0)),
+        out_specs=[pl.BlockSpec(o, lambda i: (0, 0)) for o in outs],
         scratch_shapes=[
             pltpu.VMEM((total, width), BF16),
             pltpu.VMEM((total, hidden), F32),
@@ -579,12 +624,14 @@
     flip = w_gate.shape[2] % LANES == 0
 
     grad_rows = -(-piece // LANES) * capacity
-    w_half = lax.dynamic_slice_in_dim(w_bc, core * (share // 2), share // 2, 0)
+    w_rows = share // 2
+    w_half = lax.dynamic_slice_in_dim(w_bc, core * w_rows, w_rows, 0)
 
     in_rows = width // LANES * capacity
     blocks = [1, 1, 2] if n_chip == 4 else [1] * n_chip
+    base, groups = (2, [2]) if n_dp == 4 else (0, [1] * n_dp)
     cumt, cum, steps, dyt, xs, carried, rows, *xt = call(
-        lambda *refs: prep_kernel(n_dp, *refs),
+        lambda *refs: prep_kernel(len(groups), *refs),
         [
             shape((heads, length), F32),
             shape((length, LANES), F32),
@@ -593,8 +640,8 @@
             shape((length, width), BF16),
             shape((length, half), F32),
         ]
-        + [shape((in_rows, LANES), BF16)]
-        + [shape((grad_rows, LANES), BF16)] * n_dp
+        + [shape((in_rows + base * grad_rows, LANES), BF16)]
+        + [shape((k * grad_rows, LANES), BF16) for k in groups]
         + [shape((k * width // n_chip, length), BF16) for k in blocks],
         2.0,
         (x, dy, ldt, stept, h_in, slot_rows[0], slot_counts, slot_gates[0]),
@@ -605,14 +652,28 @@
         fetch=(0, 1, 2, 3, 4),
         limit=60,
     )
-    w_far = xored(w_half, "dp", n_dp // 2)
-    mine = gathered(w_half, "dp", n_dp // 2)[1:]
-    mine += gathered(joined([w_far], after=(cumt,)), "dp", n_dp // 2)
-    deals, xt = xt[:n_dp], xt[n_dp:]
-    deals = deals[:1] + [xored(d, "dp", s + 1) for s, d in enumerate(deals[1:])]
-    payload = joined([rows, *deals])
+    deals, xt = xt[: len(groups)], xt[len(groups) :]
+    if n_dp == 4:
+        w_far, w_near = xored(w_half, "dp", 2), xored(w_half, "dp", 1)
+        deal_2 = xored(deals[0], "dp", 2)
+        ride = packed([w_far, rows, deal_2], grad_rows, (w_near,))
+        ride = xored(ride, "dp", 1)
+        mine = [w_near, w_far, ride]
+        payload = joined(
+            [rows, ride, deal_2, ride],
+            ranges=[
+                (0, in_rows + grad_rows),
+                (2 * w_rows, 2 * w_rows + grad_rows),
+                (0, grad_rows),
+                (2 * w_rows + grad_rows, 2 * w_rows + 2 * grad_rows),
+            ],
+        )
+    else:
+        mine = gathered(w_half, "dp", n_dp)[1:]
+        deals = deals[:1] + [xored(d, "dp", s + 1) for s, d in enumerate(deals[1:])]
+        payload = joined([rows, *deals])
     rows_in = chips([payload] * n_chip)
-    other = swapped(stacked(mine, after=(payload,)))
+    other = swapped(stack_w(mine, w_rows))
     w_whole, bc, keep, send = call(
         lambda *refs: project_kernel(n_dp - 1, many, *refs),
         [
@@ -634,9 +695,6 @@
             (keep, recv),
         )[0]
     ]
-    rows_a = stacked(rows_in, after=(climbs[0],))
-    rows_b = swapped(rows_a)
-    weighted = expert(rows_a, rows_b, w_gate[0], w_up[0], capacity, flip, (climbs[0],))
     if n_chip == 4:
         x_rows = width // n_chip
         over_y = xored(xt[2], "tm", 4)
@@ -644,7 +702,7 @@
     parts = 2
     tiles = width // LANES // parts
     dxs, exs, owns = [], [], []
-    later = ()
+    later = (climbs[0],)
     mixed = jnp.zeros((length, length), F32)
     for i in range(parts):
         dx, mixed, ex, own = call(
@@ -661,7 +719,7 @@
             scratch=[pltpu.VMEM((heads, length), F32)],
         )
         if i == 0:
-            held = (dx, weighted, *((over_y,) if n_chip == 4 else ()))
+            held = (over_y, dx) if n_chip == 4 else (dx,)
             arrived = []
             bit = 1
             while bit < n_chip:
@@ -682,6 +740,11 @@
                     )
                 bit *= 2
             later = (climbs[-1],)
+            rows_a = stacked(rows_in, after=later)
+            rows_b = swapped(rows_a)
+            weighted, low, high = expert(
+                rows_a, rows_b, w_gate[0], w_up[0], capacity, flip, later
+            )
         dxs.append(dx)
         exs.append(ex)
         owns.append(own)
@@ -701,9 +764,10 @@
     else:
         columns_in = chips(xt)
         places = [(i, 0) for i in range(n_chip)]
-    far = xored(weighted, "dp", n_dp // 2)
+    low = xored(low, "dp", n_dp // 2)
+    high = xored(high, "dp", n_dp // 2)
     near = gathered(weighted, "dp", n_dp // 2)
-    held += (far, *near[1:])
+    held += (low, weighted)
     r_own, r_send = call(
         lambda *refs: carry_kernel(many, size, len(arrived), *refs),
         [shape((part, half), BF16)] * 2,
@@ -712,41 +776,42 @@
         after=held,
     )
     r_recv = swapped(r_send)
-    fars = gathered(joined([far], (r_own,)), "dp", n_dp // 2)
+    fars = gathered(joined([low, high]), "dp", n_dp // 2)
     d_bc = call(db_kernel, [shape((length, columns), BF16)], 0.3, (xs, r_own, r_recv, db, dc))[0]
     d_bcs = [d_bc.reshape(1, length, columns)]
     while 2 ** (len(d_bcs) - 1) < n_chip:
         level = 2 ** (len(d_bcs) - 1)
-        sent = d_bcs[0] if level == 1 else joined(d_bcs)
+        sent = d_bcs[0] if level == 1 else joined(d_bcs, (high,))
         d_bcs.append(xored(sent, "tm", 2 * level))
-    d_in, d_decay, d_step = call(
+    d_in, d_decay, d_step, token = call(
         lambda *refs: finish_kernel(parts, *refs),
         [
             shape((length, width), BF16),
             shape((heads, length), F32),
             shape((heads, length), F32),
+            shape((8, LANES), F32),
         ],
         3.0,
         (x, bc, cumt, stept, cum, steps, h_in, r_own, r_recv, w_whole, d_bc,
          *dxs, *exs, *owns),
         scratch=[pltpu.VMEM((width, half), BF16), pltpu.VMEM((heads, half), F32)],
     )
-    w_rows = width // (2 * n_chip)
+    out_rows = width // (2 * n_chip)
     term, term_send = call(
         lambda *refs: term_kernel(places, len(columns_in), *refs),
-        [shape((w_rows, columns), F32), shape((w_rows, columns), BF16)],
+        [shape((out_rows, columns), F32), shape((out_rows, columns), BF16)],
         0.5,
         (*columns_in, *d_bcs),
-        after=(d_in, *fars[1:]),
-        scratch=[pltpu.VMEM((2, w_rows, columns), F32)],
+        after=(token, *fars[1:], *near[1:]),
+        scratch=[pltpu.VMEM((2, out_rows, columns), F32)],
     )
     final = call(
         deal_kernel,
-        [shape((w_rows // n_dp, columns), F32)]
-        + [shape((w_rows // n_dp, columns), BF16)] * (n_dp - 1),
+        [shape((out_rows // n_dp, columns), F32)]
+        + [shape((out_rows // n_dp, columns), BF16)] * (n_dp - 1),
         0.3,
         (term, swapped(term_send)),
-        scratch=[pltpu.VMEM((n_dp, w_rows // n_dp, columns), F32)],
+        scratch=[pltpu.VMEM((n_dp, out_rows // n_dp, columns), F32)],
     )
     w_bc_grad = final[0]
     for s in range(1, n_dp):

time: 85.1 us -> 90.4 us (1.062)
  waiting for transfers between devices: 24.2 us -> 38.9 us
  starting transfers between devices: 31.2 us -> 24.2 us
  local copies, waits for them, and re-layouts: 5.36 us -> 3.03 us
    ppermute x24 -> x23, waiting for transfers between devices: 24.2 us -> 33.8 us  [xored(): return lax.ppermute(array, axis, [(i, i ^ mask) for i in range(count)])]
    ppermute x24 -> x23, starting transfers between devices: 28.2 us -> 21.1 us  [xored(): return lax.ppermute(array, axis, [(i, i ^ mask) for i in range(count)])]
    ppermute x2, waiting for transfers between devices: 0.01 us -> 5.16 us  [per_device(): arrived.append(lax.ppermute(climbs[-1], 'tm', moves))]
    unnamed x44 -> x40, local copies, waits for them, and re-layouts: 4.42 us -> 2.1 us
  transfers between devices with their start and end apart: 26 -> 25, of which waited for: 15 -> 13; matrix products, arithmetic and copies ran while one was open for 0% -> 0% of each run, Pallas kernels for 23% -> 22%
where the time goes in v9:
time: 90.4 us; the launch traced here: 90.2 us
  waiting for transfers between devices  38.9 us (43%)
  starting transfers between devices  24.2 us (27%)
  Pallas kernels  21.7 us (24%)
  local copies, waits for them, and re-layouts  3.03 us (3%)
  between operations  1.69 us (2%)
    ppermute x23, waiting for transfers between devices, xored(): return lax.ppermute(array, axis, [(i, i ^ mask) for i in range(count)])  33.8 us
    ppermute x23, starting transfers between devices, xored(): return lax.ppermute(array, axis, [(i, i ^ mask) for i in range(count)])  21.1 us
    pallas_call x20, Pallas kernels, call(): pl.pallas_call(body, out_shape=outs, in_specs=specs + [pl.BlockSpec(memor...  18.9 us
    ppermute x2, waiting for transfers between devices, per_device(): arrived.append(lax.ppermute(climbs[-1], 'tm', moves))  5.16 us
    ppermute x2, starting transfers between devices, per_device(): arrived.append(lax.ppermute(climbs[-1], 'tm', moves))  3.03 us
    pallas_call x1, Pallas kernels, expert(): pl.pallas_call(body, out_shape=[shape(o, BF16) for o in outs], grid=(widt...  2.76 us
    unnamed x40, local copies, waits for them, and re-layouts  2.1 us
  transfers between devices with their start and end apart: 25, of which 13 were waited for; matrix products, arithmetic and copies ran while one was open for 0% of the time, Pallas kernels for 22%

profile of v9, /device:TPU:0, one launch (start us, length us, event | category | flops | bytes accessed | tf_op | source)
XLA Modules:
  0.0 90.2 jit_solution(12090305144272080820)
XLA Ops:
  1.6 3.1 %collective-permute-start = (bf16[320,256]{1,0:T(8,128)(2,1)S(1)}, bf16[320,256]{1,0:T(8,128)(2,1)S(1)}, u32[]{:S(2)}, u32[]{:S(2)}) collective-permute-start(bf16[320,256]{1,0:T(8,128)(2,1)S(1)} %constant_dynamic-slice_fusion), channel_id=1, source_target_pairs={{0,1},{1,0},{2,3},{3,2},{4,5},{5,4},{6,7},{7,6},{8,9},{9,8},{10,11... | collective-permute-start | bytes 491528 | tf_op jit(solution)/shard_map/ppermute | solution.py:577
  4.7 2.6 %collective-permute-start.1 = (bf16[320,256]{1,0:T(8,128)(2,1)S(1)}, bf16[320,256]{1,0:T(8,128)(2,1)S(1)}, u32[]{:S(2)}, u32[]{:S(2)}) collective-permute-start(bf16[320,256]{1,0:T(8,128)(2,1)S(1)} %constant_dynamic-slice_fusion), channel_id=1, source_target_pairs={{0,2},{1,3},{2,0},{3,1},{4,6},{5,7},{6,4},{7,5},{8,10},{9,11},{10,... | collective-permute-start | bytes 491528 | tf_op jit(solution)/shard_map/ppermute | solution.py:577
  7.9 5.7 %shard_map.146 = (f32[40,128]{1,0:T(8,128)}, f32[128,128]{1,0:T(8,128)}, f32[128,128]{1,0:T(8,128)}, bf16[2640,128]{1,0:T(8,128)(2,1)}, bf16[128,2560]{1,0:T(8,1...) custom-call(bf16[128,2560]{1,0:T(8,128)(2,1)} %bitcast.32, ...), custom_call_target="tpu_custom_call" | custom-call | flops 6000000000 | bytes 1000 | tf_op jit(solution)/shard_map/pallas_call | solution.py:81
  14.1 5.1 %collective-permute-done.2.refs_2_ = bf16[160,128]{1,0:T(8,128)(2,1)S(1)} collective-permute-done((bf16[160,128]{1,0:T(8,128)(2,1)}, bf16[160,128]{1,0:T(8,128)(2,1)S(1)}, u32[]{:S(2)}, u32[]{:S(2)}) %collective-permute-start.2) | collective-permute-done | bytes 40992 | tf_op jit(solution)/shard_map/ppermute | solution.py:577
  20.3 5.6 %collective-permute-done.3.refs_2_.refs_5_.refs_1_.refs_3_ = bf16[800,128]{1,0:T(8,128)(2,1)S(1)} collective-permute-done((bf16[800,128]{1,0:T(8,128)(2,1)S(1)}, bf16[800,128]{1,0:T(8,128)(2,1)S(1)}, u32[]{:S(2)}, u32[]{:S(2)}) %collective-permute-start.3) | collective-permute-done | bytes 204832 | tf_op jit(solution)/shard_map/ppermute | solution.py:577
  26.0 1.9 %collective-permute-done.4.refs_6_ = bf16[3,320,256]{2,1,0:T(8,128)(2,1)S(1)} collective-permute-done((bf16[3,320,256]{2,1,0:T(8,128)(2,1)S(1)}, bf16[3,320,256]{2,1,0:T(8,128)(2,1)S(1)}, u32[]{:S(2)}, u32[]{:S(2)}) %collective-permute-start.4) | collective-permute-done | bytes 491552 | tf_op jit(solution)/shard_map/ppermute | solution.py:577
  30.3 1.5 %collective-permute-start.7 = (bf16[1280,128]{1,0:T(8,128)(2,1)S(1)}, bf16[1280,128]{1,0:T(8,128)(2,1)S(1)}, u32[]{:S(2)}, u32[]{:S(2)}) collective-permute-start(bf16[1280,128]{1,0:T(8,128)(2,1)S(1)} %copy-done.15), channel_id=1, source_target_pairs={{0,16},{4,20},{8,24},{12,28},{16,0},{20,4},{24,8},{28,12},{1,17},{... | collective-permute-start | bytes 983048 | tf_op jit(solution)/shard_map/ppermute | solution.py:577
  31.9 1.6 %collective-permute-start.10 = (bf16[640,128]{1,0:T(8,128)(2,1)S(1)}, bf16[640,128]{1,0:T(8,128)(2,1)S(1)}, u32[]{:S(2)}, u32[]{:S(2)}) collective-permute-start(bf16[640,128]{1,0:T(8,128)(2,1)S(1)} %shard_map.156.refs_0_), channel_id=1, source_target_pairs={{0,8},{4,12},{8,0},{12,4},{16,24},{20,28},{24,16},{28,20},{1,9},{5... | collective-permute-start | bytes 491528 | tf_op jit(solution)/shard_map/ppermute | solution.py:577
  35.6 1.6 %collective-permute-start.6 = (bf16[1328,128]{1,0:T(8,128)(2,1)S(1)}, bf16[1328,128]{1,0:T(8,128)(2,1)S(1)}, u32[]{:S(2)}, u32[]{:S(2)}) collective-permute-start(bf16[1328,128]{1,0:T(8,128)(2,1)S(1)} %shard_map.150.refs_8_.refs_0_), channel_id=1, source_target_pairs={{0,8},{4,12},{8,0},{12,4},{16,24},{20,28},{24,16},{28,20},{1,9},{5... | collective-permute-start | bytes 1019912 | tf_op jit(solution)/shard_map/ppermute | solution.py:730
  37.2 2.6 %shard_map.151 = (f32[128,1280]{1,0:T(8,128)S(1)}, f32[128,128]{1,0:T(8,128)S(1)}, f32[20,128]{1,0:T(8,128)S(1)}, f32[20,128]{1,0:T(8,128)S(1)}) custom-call(bf16[128,2560]{1,0:T(8,128)(2,1)S(1)} %bitcast.34, bf16[128,2560]{1,0:T(8,128)(2,1)S(1)} %bitcast.30, bf16[128,256]{1,0:T(8,128)(2,1)S(1)} %get-tuple-element.48.refs_2_.refs_1_, ...), custom_call_target="tpu_custom_call" | custom-call | flops 8999999488 | bytes 1000 | tf_op jit(solution)/shard_map/pallas_call | solution.py:81
  39.8 4.5 %collective-permute-done.7.refs_2_.refs_1_ = bf16[1280,128]{1,0:T(8,128)(2,1)S(1)} collective-permute-done((bf16[1280,128]{1,0:T(8,128)(2,1)S(1)}, bf16[1280,128]{1,0:T(8,128)(2,1)S(1)}, u32[]{:S(2)}, u32[]{:S(2)}) %collective-permute-start.7) | collective-permute-done | bytes 327712 | tf_op jit(solution)/shard_map/ppermute | solution.py:577
  44.4 4.6 %collective-permute-done.6.refs_1_.refs_0_ = bf16[1328,128]{1,0:T(8,128)(2,1)S(1)} collective-permute-done((bf16[1328,128]{1,0:T(8,128)(2,1)S(1)}, bf16[1328,128]{1,0:T(8,128)(2,1)S(1)}, u32[]{:S(2)}, u32[]{:S(2)}) %collective-permute-start.6) | collective-permute-done | bytes 340000 | tf_op jit(solution)/shard_map/ppermute | solution.py:730
  50.8 1.6 %collective-permute-start.9 = (bf16[1280,128]{1,0:T(8,128)(2,1)S(1)}, bf16[1280,128]{1,0:T(8,128)(2,1)S(1)}, u32[]{:S(2)}, u32[]{:S(2)}) collective-permute-start(bf16[1280,128]{1,0:T(8,128)(2,1)S(1)} %shard_map.155), channel_id=1, source_target_pairs={{0,8},{4,12},{8,0},{12,4},{16,24},{20,28},{24,16},{28,20},{1,9},{5... | collective-permute-start | bytes 983048 | tf_op jit(solution)/shard_map/ppermute | solution.py:577
  52.4 2.8 %shard_map.158 = (bf16[896,128]{1,0:T(8,128)(2,1)S(1)}, bf16[448,128]{1,0:T(8,128)(2,1)S(1)}, bf16[448,128]{1,0:T(8,128)(2,1)S(1)}) custom-call(bf16[4,640,128]{2,1,0:T(8,128)(2,1)S(1)} %bitcast.42, bf16[4,640,128]{2,1,0:T(8,128)(2,1)S(1)} %collective-permute-done.13.refs_1_.refs_5_, bf16[2560,896]{1,0:T(8,128)(2,1)S(1)} %bitcast.25, ...), custom_call_target="tpu_custom_call" | custom-call | flops 3000000000 | bytes 1000 | tf_op jit(solution)/shard_map/pallas_call | solution.py:537
  55.3 2.6 %shard_map.153 = (f32[128,1280]{1,0:T(8,128)S(1)}, f32[128,128]{1,0:T(8,128)S(1)}, f32[20,128]{1,0:T(8,128)S(1)}, f32[20,128]{1,0:T(8,128)S(1)}) custom-call(bf16[128,2560]{1,0:T(8,128)(2,1)S(1)} %bitcast.35, bf16[128,2560]{1,0:T(8,128)(2,1)S(1)} %bitcast.31, bf16[128,256]{1,0:T(8,128)(2,1)S(1)} %get-tuple-element.48.refs_2_.refs_1_, ...), custom_call_target="tpu_custom_call" | custom-call | flops 8999999488 | bytes 1000 | tf_op jit(solution)/shard_map/pallas_call | solution.py:81
  58.1 2.9 %collective-permute-done.9.refs_5_.refs_1_ = bf16[1280,128]{1,0:T(8,128)(2,1)S(1)} collective-permute-done((bf16[1280,128]{1,0:T(8,128)(2,1)S(1)}, bf16[1280,128]{1,0:T(8,128)(2,1)S(1)}, u32[]{:S(2)}, u32[]{:S(2)}) %collective-permute-start.9) | collective-permute-done | bytes 327712 | tf_op jit(solution)/shard_map/ppermute | solution.py:577
  61.6 1.9 %collective-permute-done.14.refs_6_.refs_0_ = bf16[448,128]{1,0:T(8,128)(2,1)S(1)} collective-permute-done((bf16[448,128]{1,0:T(8,128)(2,1)S(1)}, bf16[448,128]{1,0:T(8,128)(2,1)S(1)}, u32[]{:S(2)}, u32[]{:S(2)}) %collective-permute-start.14) | collective-permute-done | bytes 114720 | tf_op jit(solution)/shard_map/ppermute | solution.py:577
  64.0 1.5 %collective-permute-done.15.refs_2_.refs_8_ = bf16[1280,128]{1,0:T(8,128)(2,1)S(1)} collective-permute-done((bf16[1280,128]{1,0:T(8,128)(2,1)S(1)}, bf16[1280,128]{1,0:T(8,128)(2,1)S(1)}, u32[]{:S(2)}, u32[]{:S(2)}) %collective-permute-start.15) | collective-permute-done | bytes 327712 | tf_op jit(solution)/shard_map/ppermute | solution.py:577
  66.4 4.2 %collective-permute-done.17.refs_2_.refs_1_ = bf16[448,128]{1,0:T(8,128)(2,1)S(1)} collective-permute-done((bf16[448,128]{1,0:T(8,128)(2,1)S(1)}, bf16[448,128]{1,0:T(8,128)(2,1)S(1)}, u32[]{:S(2)}, u32[]{:S(2)}) %collective-permute-start.17) | collective-permute-done | bytes 114720 | tf_op jit(solution)/shard_map/ppermute | solution.py:577
  70.7 2.4 %collective-permute-start.18 = (bf16[2,128,256]{2,1,0:T(8,128)(2,1)S(1)}, bf16[2,128,256]{2,1,0:T(8,128)(2,1)S(1)}, u32[]{:S(2)}, u32[]{:S(2)}) collective-permute-start(bf16[2,128,256]{2,1,0:T(8,128)(2,1)S(1)} %shard_map.162), channel_id=1, source_target_pairs={{0,16},{4,20},{8,24},{12,28},{16,0},{20,4},{24,8},{28,12},{1,17},{... | collective-permute-start | bytes 393224 | tf_op jit(solution)/shard_map/ppermute | solution.py:577
  73.2 2.6 %shard_map.161 = (bf16[128,2560]{1,0:T(8,128)(2,1)}, f32[40,128]{1,0:T(8,128)}, f32[40,128]{1,0:T(8,128)}, f32[8,128]{1,0:T(8,128)S(1)}) custom-call(bf16[128,2560]{1,0:T(8,128)(2,1)S(1)} %bitcast.36, bf16[128,256]{1,0:T(8,128)(2,1)S(1)} %get-tuple-element.48.refs_2_.refs_1_, f32[40,128]{1,0:T(8,128)S(1)} %copy-done.14, f32[40,128]{1,0:T(8,128)S(1)} %bitcast.48, ...), custom_call_target="tpu_custom_call" | custom-call | flops 8999999488 | bytes 1000 | tf_op jit(solution)/shard_map/pallas_call | solution.py:81
  75.8 4.5 %collective-permute-done.19.refs_7_.refs_3_ = bf16[896,128]{1,0:T(8,128)(2,1)S(1)} collective-permute-done((bf16[896,128]{1,0:T(8,128)(2,1)S(1)}, bf16[896,128]{1,0:T(8,128)(2,1)S(1)}, u32[]{:S(2)}, u32[]{:S(2)}) %collective-permute-start.19) | collective-permute-done | bytes 229408 | tf_op jit(solution)/shard_map/ppermute | solution.py:577
  83.5 3.4 %collective-permute-start.22 = (bf16[80,256]{1,0:T(8,128)(2,1)S(1)}, bf16[80,256]{1,0:T(8,128)(2,1)S(1)}, u32[]{:S(2)}, u32[]{:S(2)}) collective-permute-start(bf16[80,256]{1,0:T(8,128)(2,1)S(1)} %get-tuple-element.82), channel_id=1, source_target_pairs={{0,1},{1,0},{2,3},{3,2},{4,5},{5,4},{6,7},{7,6},{8,9},{9,8},{10,11... | collective-permute-start | bytes 122888 | tf_op jit(solution)/shard_map/ppermute | solution.py:577
  86.9 2.3 %shard_map.166 = bf16[896,640]{1,0:T(8,128)(2,1)} custom-call(bf16[896,128]{1,0:T(8,128)(2,1)S(1)} %get-tuple-element.62.refs_7_.refs_0_, bf16[896,128]{1,0:T(8,128)(2,1)S(1)} %collective-permute-done.20.refs_8_.refs_1_, bf16[896,128]{1,0:T(8,128)(2,1)S(1)} %shard_map.163.refs_2_, bf16[896,128]{1,0:T(8,128)(2,1)S(1)} %collective-permute-done.19.refs_7_.refs_3_, ...), custom_call_target="tpu_custom_call" | custom-call | flops 3000000000 | bytes 1000 | tf_op jit(solution)/shard_map/pallas_call | solution.py:81
  (92 shorter events, 15.5 us)
Async XLA Ops:
  1.6 17.6 %collective-permute-start = (bf16[320,256]{1,0:T(8,128)(2,1)S(1)}, bf16[320,256]{1,0:T(8,128)(2,1)S(1)}, u32[]{:S(2)}, u32[]{:S(2)}) collective-permute-start(bf16[320,256]{1,0:T(8,128)(2,1)S(1)} %constant_dynamic-slice_fusion), channel_id=1, source_target_pairs={{0,1},{1,0},{2,3},{3,2},{4,5},{5,4},{6,7},{7,6},{8,9},{9,8},{10,11... | collective-permute-start | bytes 491528 | tf_op jit(solution)/shard_map/ppermute | solution.py:577
  4.7 14.5 %collective-permute-start.1 = (bf16[320,256]{1,0:T(8,128)(2,1)S(1)}, bf16[320,256]{1,0:T(8,128)(2,1)S(1)}, u32[]{:S(2)}, u32[]{:S(2)}) collective-permute-start(bf16[320,256]{1,0:T(8,128)(2,1)S(1)} %constant_dynamic-slice_fusion), channel_id=1, source_target_pairs={{0,2},{1,3},{2,0},{3,1},{4,6},{5,7},{6,4},{7,5},{8,10},{9,11},{10,... | collective-permute-start | bytes 491528 | tf_op jit(solution)/shard_map/ppermute | solution.py:577
  13.6 5.5 %collective-permute-start.2 = (bf16[160,128]{1,0:T(8,128)(2,1)}, bf16[160,128]{1,0:T(8,128)(2,1)S(1)}, u32[]{:S(2)}, u32[]{:S(2)}) collective-permute-start(bf16[160,128]{1,0:T(8,128)(2,1)} %get-tuple-element.47), channel_id=1, source_target_pairs={{0,2},{1,3},{2,0},{3,1},{4,6},{5,7},{6,4},{7,5},{8,10},{9,11},{10,... | collective-permute-start | bytes 122888 | tf_op jit(solution)/shard_map/ppermute | solution.py:577
  20.1 5.8 %collective-permute-start.3 = (bf16[800,128]{1,0:T(8,128)(2,1)S(1)}, bf16[800,128]{1,0:T(8,128)(2,1)S(1)}, u32[]{:S(2)}, u32[]{:S(2)}) collective-permute-start(bf16[800,128]{1,0:T(8,128)(2,1)S(1)} %shard_map.147), channel_id=1, source_target_pairs={{0,1},{1,0},{2,3},{3,2},{4,5},{5,4},{6,7},{7,6},{8,9},{9,8},{10,11... | collective-permute-start | bytes 614408 | tf_op jit(solution)/shard_map/ppermute | solution.py:577
  26.0 1.9 %collective-permute-start.4 = (bf16[3,320,256]{2,1,0:T(8,128)(2,1)S(1)}, bf16[3,320,256]{2,1,0:T(8,128)(2,1)S(1)}, u32[]{:S(2)}, u32[]{:S(2)}) collective-permute-start(bf16[3,320,256]{2,1,0:T(8,128)(2,1)S(1)} %shard_map.148), channel_id=1, source_target_pairs={{0,4},{4,0},{8,12},{12,8},{16,20},{20,16},{24,28},{28,24},{1,5},{5... | collective-permute-start | bytes 1474568 | tf_op jit(solution)/shard_map/ppermute | solution.py:577
  30.1 5.3 %collective-permute-start.5 = (bf16[1328,128]{1,0:T(8,128)(2,1)S(1)}, bf16[1328,128]{1,0:T(8,128)(2,1)S(1)}, u32[]{:S(2)}, u32[]{:S(2)}) collective-permute-start(bf16[1328,128]{1,0:T(8,128)(2,1)S(1)} %get-tuple-element.53), channel_id=1, source_target_pairs={{0,4},{4,0},{8,12},{12,8},{16,20},{20,16},{24,28},{28,24},{1,5},{5... | collective-permute-start | bytes 1019912 | tf_op jit(solution)/shard_map/ppermute | solution.py:577
  30.3 14.1 %collective-permute-start.7 = (bf16[1280,128]{1,0:T(8,128)(2,1)S(1)}, bf16[1280,128]{1,0:T(8,128)(2,1)S(1)}, u32[]{:S(2)}, u32[]{:S(2)}) collective-permute-start(bf16[1280,128]{1,0:T(8,128)(2,1)S(1)} %copy-done.15), channel_id=1, source_target_pairs={{0,16},{4,20},{8,24},{12,28},{16,0},{20,4},{24,8},{28,12},{1,17},{... | collective-permute-start | bytes 983048 | tf_op jit(solution)/shard_map/ppermute | solution.py:577
  31.9 17.3 %collective-permute-start.10 = (bf16[640,128]{1,0:T(8,128)(2,1)S(1)}, bf16[640,128]{1,0:T(8,128)(2,1)S(1)}, u32[]{:S(2)}, u32[]{:S(2)}) collective-permute-start(bf16[640,128]{1,0:T(8,128)(2,1)S(1)} %shard_map.156.refs_0_), channel_id=1, source_target_pairs={{0,8},{4,12},{8,0},{12,4},{16,24},{20,28},{24,16},{28,20},{1,9},{5... | collective-permute-start | bytes 491528 | tf_op jit(solution)/shard_map/ppermute | solution.py:577
  33.4 15.7 %collective-permute-start.11 = (bf16[640,128]{1,0:T(8,128)(2,1)S(1)}, bf16[640,128]{1,0:T(8,128)(2,1)S(1)}, u32[]{:S(2)}, u32[]{:S(2)}) collective-permute-start(bf16[640,128]{1,0:T(8,128)(2,1)S(1)} %shard_map.156.refs_0_), channel_id=1, source_target_pairs={{0,16},{4,20},{8,24},{12,28},{16,0},{20,4},{24,8},{28,12},{1,17},{... | collective-permute-start | bytes 491528 | tf_op jit(solution)/shard_map/ppermute | solution.py:577
  33.9 15.2 %collective-permute-start.12 = (bf16[640,128]{1,0:T(8,128)(2,1)S(1)}, bf16[640,128]{1,0:T(8,128)(2,1)S(1)}, u32[]{:S(2)}, u32[]{:S(2)}) collective-permute-start(bf16[640,128]{1,0:T(8,128)(2,1)S(1)} %shard_map.156.refs_0_), channel_id=1, source_target_pairs={{0,24},{4,28},{8,16},{12,20},{16,8},{20,12},{24,0},{28,4},{1,25},{... | collective-permute-start | bytes 491528 | tf_op jit(solution)/shard_map/ppermute | solution.py:577
  35.6 13.3 %collective-permute-start.6 = (bf16[1328,128]{1,0:T(8,128)(2,1)S(1)}, bf16[1328,128]{1,0:T(8,128)(2,1)S(1)}, u32[]{:S(2)}, u32[]{:S(2)}) collective-permute-start(bf16[1328,128]{1,0:T(8,128)(2,1)S(1)} %shard_map.150.refs_8_.refs_0_), channel_id=1, source_target_pairs={{0,8},{4,12},{8,0},{12,4},{16,24},{20,28},{24,16},{28,20},{1,9},{5... | collective-permute-start | bytes 1019912 | tf_op jit(solution)/shard_map/ppermute | solution.py:730
  49.2 3.2 %collective-permute-start.13 = (bf16[4,640,128]{2,1,0:T(8,128)(2,1)S(1)}, bf16[4,640,128]{2,1,0:T(8,128)(2,1)S(1)}, u32[]{:S(2)}, u32[]{:S(2)}) collective-permute-start(bf16[4,640,128]{2,1,0:T(8,128)(2,1)S(1)} %bitcast.41), channel_id=1, source_target_pairs={{0,4},{4,0},{8,12},{12,8},{16,20},{20,16},{24,28},{28,24},{1,5},{5... | collective-permute-start | bytes 1966088 | tf_op jit(solution)/shard_map/ppermute | solution.py:577
  49.3 12.3 %collective-permute-start.8 = (bf16[1328,128]{1,0:T(8,128)(2,1)S(1)}, bf16[1328,128]{1,0:T(8,128)(2,1)S(1)}, u32[]{:S(2)}, u32[]{:S(2)}) collective-permute-start(bf16[1328,128]{1,0:T(8,128)(2,1)S(1)} %shard_map.152.refs_8_.refs_2_.refs_4_), channel_id=1, source_target_pairs={{16,0},{20,4},{24,8},{28,12},{17,1},{21,5},{25,9},{29,13},{18,2},{... | collective-permute-start | bytes 1019912 | tf_op jit(solution)/shard_map/ppermute | solution.py:730
  50.8 10.2 %collective-permute-start.9 = (bf16[1280,128]{1,0:T(8,128)(2,1)S(1)}, bf16[1280,128]{1,0:T(8,128)(2,1)S(1)}, u32[]{:S(2)}, u32[]{:S(2)}) collective-permute-start(bf16[1280,128]{1,0:T(8,128)(2,1)S(1)} %shard_map.155), channel_id=1, source_target_pairs={{0,8},{4,12},{8,0},{12,4},{16,24},{20,28},{24,16},{28,20},{1,9},{5... | collective-permute-start | bytes 983048 | tf_op jit(solution)/shard_map/ppermute | solution.py:577
  55.2 8.3 %collective-permute-start.14 = (bf16[448,128]{1,0:T(8,128)(2,1)S(1)}, bf16[448,128]{1,0:T(8,128)(2,1)S(1)}, u32[]{:S(2)}, u32[]{:S(2)}) collective-permute-start(bf16[448,128]{1,0:T(8,128)(2,1)S(1)} %get-tuple-element.61), channel_id=1, source_target_pairs={{0,2},{1,3},{2,0},{3,1},{4,6},{5,7},{6,4},{7,5},{8,10},{9,11},{10,... | collective-permute-start | bytes 344072 | tf_op jit(solution)/shard_map/ppermute | solution.py:577
  63.8 1.7 %collective-permute-start.15 = (bf16[1280,128]{1,0:T(8,128)(2,1)S(1)}, bf16[1280,128]{1,0:T(8,128)(2,1)S(1)}, u32[]{:S(2)}, u32[]{:S(2)}) collective-permute-start(bf16[1280,128]{1,0:T(8,128)(2,1)S(1)} %get-tuple-element.64), channel_id=1, source_target_pairs={{0,4},{4,0},{8,12},{12,8},{16,20},{20,16},{24,28},{28,24},{1,5},{5... | collective-permute-start | bytes 983048 | tf_op jit(solution)/shard_map/ppermute | solution.py:577
  63.9 6.7 %collective-permute-start.17 = (bf16[448,128]{1,0:T(8,128)(2,1)S(1)}, bf16[448,128]{1,0:T(8,128)(2,1)S(1)}, u32[]{:S(2)}, u32[]{:S(2)}) collective-permute-start(bf16[448,128]{1,0:T(8,128)(2,1)S(1)} %get-tuple-element.77), channel_id=1, source_target_pairs={{0,2},{1,3},{2,0},{3,1},{4,6},{5,7},{6,4},{7,5},{8,10},{9,11},{10,... | collective-permute-start | bytes 344072 | tf_op jit(solution)/shard_map/ppermute | solution.py:577
  65.9 4.9 %collective-permute-start.16 = (bf16[1,128,256]{2,1,0:T(8,128)(2,1)S(1)}, bf16[1,128,256]{2,1,0:T(8,128)(2,1)S(1)}, u32[]{:S(2)}, u32[]{:S(2)}) collective-permute-start(bf16[1,128,256]{2,1,0:T(8,128)(2,1)S(1)} %bitcast.44), channel_id=1, source_target_pairs={{0,8},{4,12},{8,0},{12,4},{16,24},{20,28},{24,16},{28,20},{1,9},{5... | collective-permute-start | bytes 196616 | tf_op jit(solution)/shard_map/ppermute | solution.py:577
  66.4 9.4 %collective-permute-start.20 = (bf16[896,128]{1,0:T(8,128)(2,1)S(1)}, bf16[896,128]{1,0:T(8,128)(2,1)S(1)}, u32[]{:S(2)}, u32[]{:S(2)}) collective-permute-start(bf16[896,128]{1,0:T(8,128)(2,1)S(1)} %get-tuple-element.62.refs_7_.refs_0_), channel_id=1, source_target_pairs={{0,1},{1,0},{2,3},{3,2},{4,5},{5,4},{6,7},{7,6},{8,9},{9,8},{10,11... | collective-permute-start | bytes 688136 | tf_op jit(solution)/shard_map/ppermute | solution.py:577
  70.6 9.7 %collective-permute-start.19 = (bf16[896,128]{1,0:T(8,128)(2,1)S(1)}, bf16[896,128]{1,0:T(8,128)(2,1)S(1)}, u32[]{:S(2)}, u32[]{:S(2)}) collective-permute-start(bf16[896,128]{1,0:T(8,128)(2,1)S(1)} %shard_map.163.refs_2_), channel_id=1, source_target_pairs={{0,1},{1,0},{2,3},{3,2},{4,5},{5,4},{6,7},{7,6},{8,9},{9,8},{10,11... | collective-permute-start | bytes 688136 | tf_op jit(solution)/shard_map/ppermute | solution.py:577
  70.7 9.6 %collective-permute-start.18 = (bf16[2,128,256]{2,1,0:T(8,128)(2,1)S(1)}, bf16[2,128,256]{2,1,0:T(8,128)(2,1)S(1)}, u32[]{:S(2)}, u32[]{:S(2)}) collective-permute-start(bf16[2,128,256]{2,1,0:T(8,128)(2,1)S(1)} %shard_map.162), channel_id=1, source_target_pairs={{0,16},{4,20},{8,24},{12,28},{16,0},{20,4},{24,8},{28,12},{1,17},{... | collective-permute-start | bytes 393224 | tf_op jit(solution)/shard_map/ppermute | solution.py:577
  82.5 6.8 %collective-permute-start.24 = (bf16[80,256]{1,0:T(8,128)(2,1)S(1)}, bf16[80,256]{1,0:T(8,128)(2,1)S(1)}, u32[]{:S(2)}, u32[]{:S(2)}) collective-permute-start(bf16[80,256]{1,0:T(8,128)(2,1)S(1)} %get-tuple-element.84), channel_id=1, source_target_pairs={{0,3},{1,2},{2,1},{3,0},{4,7},{5,6},{6,5},{7,4},{8,11},{9,10},{10,... | collective-permute-start | bytes 122888 | tf_op jit(solution)/shard_map/ppermute | solution.py:577
  83.5 6.0 %collective-permute-start.23 = (bf16[80,256]{1,0:T(8,128)(2,1)S(1)}, bf16[80,256]{1,0:T(8,128)(2,1)S(1)}, u32[]{:S(2)}, u32[]{:S(2)}) collective-permute-start(bf16[80,256]{1,0:T(8,128)(2,1)S(1)} %get-tuple-element.83), channel_id=1, source_target_pairs={{0,2},{1,3},{2,0},{3,1},{4,6},{5,7},{6,4},{7,5},{8,10},{9,11},{10,... | collective-permute-start | bytes 122888 | tf_op jit(solution)/shard_map/ppermute | solution.py:577
  83.5 6.0 %collective-permute-start.22 = (bf16[80,256]{1,0:T(8,128)(2,1)S(1)}, bf16[80,256]{1,0:T(8,128)(2,1)S(1)}, u32[]{:S(2)}, u32[]{:S(2)}) collective-permute-start(bf16[80,256]{1,0:T(8,128)(2,1)S(1)} %get-tuple-element.82), channel_id=1, source_target_pairs={{0,1},{1,0},{2,3},{3,2},{4,5},{5,4},{6,7},{7,6},{8,9},{9,8},{10,11... | collective-permute-start | bytes 122888 | tf_op jit(solution)/shard_map/ppermute | solution.py:577
  (21 other events, 185.2 us)

commit v10 on v8

--- a/solution.py
+++ b/solution.py
@@ -114,8 +114,8 @@
     for t in range(width // LANES):
         rows_ref[t * slots : (t + 1) * slots, :] = rows[:, t * LANES : (t + 1) * LANES]
     grads = dot(jnp.where(hit, weight, 0.0).astype(BF16), dy_ref[...], 0, 0).astype(BF16)
-    n_dp = len(out_refs) - 1
     held = out_refs[-1]
+    n_dp = held.shape[0]
     piece = width // n_dp
     for i in range(n_dp):
         for t, low in enumerate(range(i * piece, (i + 1) * piece, LANES)):
@@ -125,8 +125,11 @@
                 block = jnp.concatenate([block, fill], axis=1)
             held[i, t * slots : (t + 1) * slots, :] = block
     place = lax.axis_index("dp")
-    for s, out in enumerate(out_refs[:-1]):
-        out[...] = held[place ^ s]
+    s = 0
+    for out in out_refs[:-1]:
+        for start in range(0, out.shape[0], held.shape[1]):
+            out[start : start + held.shape[1], :] = held[place ^ s]
+            s += 1
 
 
 def high_low(values):
@@ -135,15 +138,15 @@
 
 
 def prep_kernel(
-    n_dp, x_ref, dy_ref, ldt_ref, stept_ref, h_ref, slot_ref, count_ref, gate_ref,
+    n_deals, x_ref, dy_ref, ldt_ref, stept_ref, h_ref, slot_ref, count_ref, gate_ref,
     cumt_ref, cum_ref, step_ref, dyt_ref, xs_ref, carried_ref, rows_ref, *rest,
 ):
-    outs, xt_ref, held_ref = rest[n_dp:-2], rest[-2], rest[-1]
+    outs, xt_ref, held_ref = rest[n_deals:-2], rest[-2], rest[-1]
     length, width = x_ref.shape
     heads = ldt_ref.shape[0]
     size = width // heads
     _, chip, n_chip = core_and_chip()
-    picked(x_ref, dy_ref, slot_ref, count_ref, gate_ref, rows_ref, (*rest[:n_dp], held_ref))
+    picked(x_ref, dy_ref, slot_ref, count_ref, gate_ref, rows_ref, (*rest[:n_deals], held_ref))
     pad = jnp.zeros((LANES - heads, length), F32)
     cumt = dot(ldt_ref[...], triangle(length, lambda a, b: a <= b), 1, 0, HI)
     cumt_ref[...] = cumt
@@ -375,7 +378,8 @@
     (x_ref, bc_ref, cumt_ref, stept_ref, cum_ref, step_ref, h_ref, own_ref, recv_ref,
      w_ref, dbc_ref) = refs[:11]
     dx_refs, ex_refs, st_refs = (refs[11 + i * parts : 11 + (i + 1) * parts] for i in range(3))
-    in_ref, decay_ref, grad_ref, r_ref, edge_ref = refs[11 + 3 * parts :]
+    in_ref, decay_ref, grad_ref, token_ref, r_ref, edge_ref = refs[11 + 3 * parts :]
+    token_ref[...] = jnp.zeros_like(token_ref)
     core, _, _ = core_and_chip()
     length, width = x_ref.shape
     heads = cumt_ref.shape[0]
@@ -583,8 +587,9 @@
 
     in_rows = width // LANES * capacity
     blocks = [1, 1, 2] if n_chip == 4 else [1] * n_chip
+    groups = [2, 2] if n_dp == 4 else [1] * n_dp
     cumt, cum, steps, dyt, xs, carried, rows, *xt = call(
-        lambda *refs: prep_kernel(n_dp, *refs),
+        lambda *refs: prep_kernel(len(groups), *refs),
         [
             shape((heads, length), F32),
             shape((length, LANES), F32),
@@ -594,7 +599,7 @@
             shape((length, half), F32),
         ]
         + [shape((in_rows, LANES), BF16)]
-        + [shape((grad_rows, LANES), BF16)] * n_dp
+        + [shape((k * grad_rows, LANES), BF16) for k in groups]
         + [shape((k * width // n_chip, length), BF16) for k in blocks],
         2.0,
         (x, dy, ldt, stept, h_in, slot_rows[0], slot_counts, slot_gates[0]),
@@ -605,14 +610,23 @@
         fetch=(0, 1, 2, 3, 4),
         limit=60,
     )
+    rows_in = chips([rows] * n_chip)
+    deals, xt = xt[: len(groups)], xt[len(groups) :]
+    if n_dp == 4:
+        one = (0, grad_rows), (grad_rows, 2 * grad_rows)
+        over_2 = xored(deals[1], "dp", 2)
+        over_1 = xored(joined([deals[0], over_2], ranges=[one[1], one[1]]), "dp", 1)
+        dealt = joined([deals[0], over_1, over_2, over_1], (), [one[0], one[0], one[0], one[1]])
+        first_hop, second_hop = (over_2,), (over_1,)
+    else:
+        first_hop = second_hop = ()
+        dealt = joined(deals[:1] + [xored(d, "dp", s + 1) for s, d in enumerate(deals[1:])])
     w_far = xored(w_half, "dp", n_dp // 2)
     mine = gathered(w_half, "dp", n_dp // 2)[1:]
-    mine += gathered(joined([w_far], after=(cumt,)), "dp", n_dp // 2)
-    deals, xt = xt[:n_dp], xt[n_dp:]
-    deals = deals[:1] + [xored(d, "dp", s + 1) for s, d in enumerate(deals[1:])]
-    payload = joined([rows, *deals])
-    rows_in = chips([payload] * n_chip)
-    other = swapped(stacked(mine, after=(payload,)))
+    mine += gathered(joined([w_far], after=(rows,)), "dp", n_dp // 2)
+    other = swapped(stacked(mine, after=tuple(rows_in[1:])))
+    rows_a = stacked(rows_in, after=(other,))
+    rows_b = swapped(rows_a)
     w_whole, bc, keep, send = call(
         lambda *refs: project_kernel(n_dp - 1, many, *refs),
         [
@@ -623,6 +637,7 @@
         ],
         1.0,
         (x, dyt, w_bc, *mine, other),
+        after=first_hop,
     )
     recv = swapped(send)
     hidden = w_gate.shape[2]
@@ -632,19 +647,18 @@
             [shape((part + up16(2 * many), half), BF16)],
             0.5,
             (keep, recv),
+            after=second_hop,
         )[0]
     ]
-    rows_a = stacked(rows_in, after=(climbs[0],))
-    rows_b = swapped(rows_a)
     weighted = expert(rows_a, rows_b, w_gate[0], w_up[0], capacity, flip, (climbs[0],))
     if n_chip == 4:
         x_rows = width // n_chip
-        over_y = xored(xt[2], "tm", 4)
+        over_y = xored(joined([xt[2], dealt], (climbs[0],)), "tm", 4)
 
     parts = 2
     tiles = width // LANES // parts
     dxs, exs, owns = [], [], []
-    later = ()
+    later = (weighted,)
     mixed = jnp.zeros((length, length), F32)
     for i in range(parts):
         dx, mixed, ex, own = call(
@@ -655,7 +669,7 @@
                 shape((heads // parts, length), F32),
                 shape((heads // parts, length), F32),
             ],
-            3.0,
+            1.0,
             (x, dy, bc, cumt, cum, steps, h_in, mixed),
             after=later,
             scratch=[pltpu.VMEM((heads, length), F32)],
@@ -697,9 +711,15 @@
         over_x = xored(joined([xt[1], over_y], later, [(0, x_rows), (x_rows, 2 * x_rows)]), "tm", 2)
         columns_in = [xt[0], over_x, over_y]
         places = [(0, 0), (1, 0), (2, 0), (1, x_rows)]
+        from_y = (2 * x_rows, over_y.shape[0])
+        grads = joined([dealt, over_y], (later[0],), [(0, dealt.shape[0]), from_y])
+        grads = [dealt, xored(grads, "tm", 2), over_y]
+        spans = [(0, dealt.shape[0]), (0, dealt.shape[0]), from_y, (dealt.shape[0], 2 * dealt.shape[0])]
+        grads = joined([grads[0], grads[1], grads[2], grads[1]], (), spans)
         held += (over_x,)
     else:
         columns_in = chips(xt)
+        grads = joined(chips([dealt] * n_chip))
         places = [(i, 0) for i in range(n_chip)]
     far = xored(weighted, "dp", n_dp // 2)
     near = gathered(weighted, "dp", n_dp // 2)
@@ -711,6 +731,8 @@
         (*arrived, keep, recv),
         after=held,
     )
+    grads_a = grads.reshape(n_chip, grads.shape[0] // n_chip, LANES)
+    grads_b = swapped(grads_a)
     r_recv = swapped(r_send)
     fars = gathered(joined([far], (r_own,)), "dp", n_dp // 2)
     d_bc = call(db_kernel, [shape((length, columns), BF16)], 0.3, (xs, r_own, r_recv, db, dc))[0]
@@ -719,12 +741,13 @@
         level = 2 ** (len(d_bcs) - 1)
         sent = d_bcs[0] if level == 1 else joined(d_bcs)
         d_bcs.append(xored(sent, "tm", 2 * level))
-    d_in, d_decay, d_step = call(
+    d_in, d_decay, d_step, token = call(
         lambda *refs: finish_kernel(parts, *refs),
         [
             shape((length, width), BF16),
             shape((heads, length), F32),
             shape((heads, length), F32),
+            shape((8, LANES), F32),
         ],
         3.0,
         (x, bc, cumt, stept, cum, steps, h_in, r_own, r_recv, w_whole, d_bc,
@@ -737,7 +760,7 @@
         [shape((w_rows, columns), F32), shape((w_rows, columns), BF16)],
         0.5,
         (*columns_in, *d_bcs),
-        after=(d_in, *fars[1:]),
+        after=(token, *fars[1:]),
         scratch=[pltpu.VMEM((2, w_rows, columns), F32)],
     )
     final = call(
@@ -756,7 +779,7 @@
         lambda *refs: down_kernel(n_dp, flip, capacity, grad_rows, *refs),
         [shape((hidden, piece), BF16)],
         1.0,
-        (*near, *fars, rows_a, rows_b),
+        (*near, *fars, grads_a, grads_b),
         after=(final[0],),
     )[0]
     return (d_in[None], d_decay.T[None], d_step.T[None], w_bc_grad, w_down_grad[None])

time: 85.1 us -> 84 us (0.987)
  local copies, waits for them, and re-layouts: 5.36 us -> 3.04 us
  starting transfers between devices: 31.2 us -> 33 us
    ppermute x24 -> x25, starting transfers between devices: 28.2 us -> 30.9 us  [xored(): return lax.ppermute(array, axis, [(i, i ^ mask) for i in range(count)])]
    unnamed x44 -> x40, local copies, waits for them, and re-layouts: 4.42 us -> 2.1 us
    ppermute x24 -> x25, waiting for transfers between devices: 24.2 us -> 23.1 us  [xored(): return lax.ppermute(array, axis, [(i, i ^ mask) for i in range(count)])]
    ppermute x2, starting transfers between devices: 3.03 us -> 2.07 us  [per_device(): arrived.append(lax.ppermute(climbs[-1], 'tm', moves))]
    pallas_call x20 -> x24, Pallas kernels: 18.8 us -> 18.9 us  [call(): pl.pallas_call(body, out_shape=outs, in_specs=specs + [pl.BlockSpec(memor...]
  transfers between devices with their start and end apart: 26 -> 27, of which waited for: 15 -> 13; matrix products, arithmetic and copies ran while one was open for 0% -> 0% of each run, Pallas kernels for 23% -> 24%
where the time goes in v10:
time: 84 us; the launch traced here: 83.7 us
  starting transfers between devices  33 us (39%)
  waiting for transfers between devices  23.6 us (28%)
  Pallas kernels  21.7 us (26%)
  local copies, waits for them, and re-layouts  3.04 us (4%)
  between operations  1.7 us (2%)
    ppermute x25, starting transfers between devices, xored(): return lax.ppermute(array, axis, [(i, i ^ mask) for i in range(count)])  30.9 us
    ppermute x25, waiting for transfers between devices, xored(): return lax.ppermute(array, axis, [(i, i ^ mask) for i in range(count)])  23.1 us
    pallas_call x24, Pallas kernels, call(): pl.pallas_call(body, out_shape=outs, in_specs=specs + [pl.BlockSpec(memor...  18.9 us
    pallas_call x1, Pallas kernels, expert(): pl.pallas_call(body, out_shape=shape(out, BF16), grid=(width // depth,),...  2.75 us
    unnamed x40, local copies, waits for them, and re-layouts  2.1 us
    ppermute x2, starting transfers between devices, per_device(): arrived.append(lax.ppermute(climbs[-1], 'tm', moves))  2.07 us
  transfers between devices with their start and end apart: 27, of which 13 were waited for; matrix products, arithmetic and copies ran while one was open for 0% of the time, Pallas kernels for 24%

profile of v10, /device:TPU:0, one launch (start us, length us, event | category | flops | bytes accessed | tf_op | source)
XLA Modules:
  0.0 83.7 jit_solution(9037833087060505252)
XLA Ops:
  1.6 3.1 %collective-permute-start = (bf16[320,256]{1,0:T(8,128)(2,1)S(1)}, bf16[320,256]{1,0:T(8,128)(2,1)S(1)}, u32[]{:S(2)}, u32[]{:S(2)}) collective-permute-start(bf16[320,256]{1,0:T(8,128)(2,1)S(1)} %constant_dynamic-slice_fusion), channel_id=1, source_target_pairs={{0,1},{1,0},{2,3},{3,2},{4,5},{5,4},{6,7},{7,6},{8,9},{9,8},{10,11... | collective-permute-start | bytes 491528 | tf_op jit(solution)/shard_map/ppermute | solution.py:536
  4.7 2.6 %collective-permute-start.1 = (bf16[320,256]{1,0:T(8,128)(2,1)S(1)}, bf16[320,256]{1,0:T(8,128)(2,1)S(1)}, u32[]{:S(2)}, u32[]{:S(2)}) collective-permute-start(bf16[320,256]{1,0:T(8,128)(2,1)S(1)} %constant_dynamic-slice_fusion), channel_id=1, source_target_pairs={{0,2},{1,3},{2,0},{3,1},{4,6},{5,7},{6,4},{7,5},{8,10},{9,11},{10,... | collective-permute-start | bytes 491528 | tf_op jit(solution)/shard_map/ppermute | solution.py:536
  7.9 5.7 %shard_map.146 = (f32[40,128]{1,0:T(8,128)}, f32[128,128]{1,0:T(8,128)}, f32[128,128]{1,0:T(8,128)}, bf16[2640,128]{1,0:T(8,128)(2,1)}, bf16[128,2560]{1,0:T(8,1...) custom-call(bf16[128,2560]{1,0:T(8,128)(2,1)} %bitcast.34, ...), custom_call_target="tpu_custom_call" | custom-call | flops 6000000000 | bytes 1000 | tf_op jit(solution)/shard_map/pallas_call | solution.py:81
  19.7 1.8 %collective-permute-done.3.refs_3_.refs_1_ = bf16[320,128]{1,0:T(8,128)(2,1)S(1)} collective-permute-done((bf16[320,128]{1,0:T(8,128)(2,1)S(1)}, bf16[320,128]{1,0:T(8,128)(2,1)S(1)}, u32[]{:S(2)}, u32[]{:S(2)}) %collective-permute-start.3) | collective-permute-done | bytes 81952 | tf_op jit(solution)/shard_map/ppermute | solution.py:536
  22.8 1.8 %collective-permute-done.5.refs_5_.refs_3_ = bf16[320,128]{1,0:T(8,128)(2,1)S(1)} collective-permute-done((bf16[320,128]{1,0:T(8,128)(2,1)S(1)}, bf16[320,128]{1,0:T(8,128)(2,1)S(1)}, u32[]{:S(2)}, u32[]{:S(2)}) %collective-permute-start.5) | collective-permute-done | bytes 81952 | tf_op jit(solution)/shard_map/ppermute | solution.py:536
  24.7 2.7 %collective-permute-start.7 = (bf16[160,128]{1,0:T(8,128)(2,1)}, bf16[160,128]{1,0:T(8,128)(2,1)S(1)}, u32[]{:S(2)}, u32[]{:S(2)}) collective-permute-start(bf16[160,128]{1,0:T(8,128)(2,1)} %get-tuple-element.45), channel_id=1, source_target_pairs={{0,2},{1,3},{2,0},{3,1},{4,6},{5,7},{6,4},{7,5},{8,10},{9,11},{10,... | collective-permute-start | bytes 122888 | tf_op jit(solution)/shard_map/ppermute | solution.py:536
  27.3 2.5 %collective-permute-done.7.refs_7_.refs_1_.refs_2_ = bf16[160,128]{1,0:T(8,128)(2,1)S(1)} collective-permute-done((bf16[160,128]{1,0:T(8,128)(2,1)}, bf16[160,128]{1,0:T(8,128)(2,1)S(1)}, u32[]{:S(2)}, u32[]{:S(2)}) %collective-permute-start.7) | collective-permute-done | bytes 40992 | tf_op jit(solution)/shard_map/ppermute | solution.py:536
  32.7 1.6 %collective-permute-start.9 = (bf16[160,128]{1,0:T(8,128)(2,1)S(1)}, bf16[160,128]{1,0:T(8,128)(2,1)S(1)}, u32[]{:S(2)}, u32[]{:S(2)}) collective-permute-start(bf16[160,128]{1,0:T(8,128)(2,1)S(1)} %shard_map.150), channel_id=1, source_target_pairs={{0,1},{1,0},{2,3},{3,2},{4,5},{5,4},{6,7},{7,6},{8,9},{9,8},{10,11... | collective-permute-start | bytes 122888 | tf_op jit(solution)/shard_map/ppermute | solution.py:536
  34.4 2.4 %collective-permute-done.9.refs_2_.refs_1_.refs_3_ = bf16[160,128]{1,0:T(8,128)(2,1)S(1)} collective-permute-done((bf16[160,128]{1,0:T(8,128)(2,1)S(1)}, bf16[160,128]{1,0:T(8,128)(2,1)S(1)}, u32[]{:S(2)}, u32[]{:S(2)}) %collective-permute-start.9) | collective-permute-done | bytes 40992 | tf_op jit(solution)/shard_map/ppermute | solution.py:536
  38.3 2.8 %shard_map.153.refs_8_.refs_3_.refs_0_ = bf16[896,128]{1,0:T(8,128)(2,1)S(1)} custom-call(bf16[4,320,128]{2,1,0:T(8,128)(2,1)S(1)} %bitcast.47, bf16[4,320,128]{2,1,0:T(8,128)(2,1)S(1)} %collective-permute-done.11.refs_1_, bf16[2560,896]{1,0:T(8,128)(2,1)S(1)} %bitcast.27, bf16[2560,896]{1,0:T(8,128)(2,1)S(1)} %bitcast.30, ...), custom_call_target="tpu_custom_call" | custom-call | flops 3000000000 | bytes 1000 | tf_op jit(solution)/shard_map/pallas_call | solution.py:496
  41.1 2.6 %collective-permute-start.15 = (bf16[896,128]{1,0:T(8,128)(2,1)S(1)}, bf16[896,128]{1,0:T(8,128)(2,1)S(1)}, u32[]{:S(2)}, u32[]{:S(2)}) collective-permute-start(bf16[896,128]{1,0:T(8,128)(2,1)S(1)} %shard_map.153.refs_8_.refs_3_.refs_0_), channel_id=1, source_target_pairs={{0,2},{1,3},{2,0},{3,1},{4,6},{5,7},{6,4},{7,5},{8,10},{9,11},{10,... | collective-permute-start | bytes 688136 | tf_op jit(solution)/shard_map/ppermute | solution.py:536
  43.8 2.6 %shard_map.154 = (f32[128,1280]{1,0:T(8,128)S(1)}, f32[128,128]{1,0:T(8,128)S(1)}, f32[20,128]{1,0:T(8,128)S(1)}, f32[20,128]{1,0:T(8,128)S(1)}) custom-call(bf16[128,2560]{1,0:T(8,128)(2,1)S(1)} %bitcast.36, bf16[128,2560]{1,0:T(8,128)(2,1)S(1)} %bitcast.32, bf16[128,256]{1,0:T(8,128)(2,1)S(1)} %get-tuple-element.46.refs_2_.refs_1_, ...), custom_call_target="tpu_custom_call" | custom-call | flops 3000000000 | bytes 1000 | tf_op jit(solution)/shard_map/pallas_call | solution.py:81
  49.4 1.6 %collective-permute-start.14 = (bf16[1280,128]{1,0:T(8,128)(2,1)S(1)}, bf16[1280,128]{1,0:T(8,128)(2,1)S(1)}, u32[]{:S(2)}, u32[]{:S(2)}) collective-permute-start(bf16[1280,128]{1,0:T(8,128)(2,1)S(1)} %shard_map.160), channel_id=1, source_target_pairs={{0,8},{4,12},{8,0},{12,4},{16,24},{20,28},{24,16},{28,20},{1,9},{5... | collective-permute-start | bytes 983048 | tf_op jit(solution)/shard_map/ppermute | solution.py:536
  50.9 2.5 %shard_map.158 = (f32[128,1280]{1,0:T(8,128)S(1)}, f32[128,128]{1,0:T(8,128)S(1)}, f32[20,128]{1,0:T(8,128)S(1)}, f32[20,128]{1,0:T(8,128)S(1)}) custom-call(bf16[128,2560]{1,0:T(8,128)(2,1)S(1)} %bitcast.37, bf16[128,2560]{1,0:T(8,128)(2,1)S(1)} %bitcast.33, bf16[128,256]{1,0:T(8,128)(2,1)S(1)} %get-tuple-element.46.refs_2_.refs_1_, ...), custom_call_target="tpu_custom_call" | custom-call | flops 3000000000 | bytes 1000 | tf_op jit(solution)/shard_map/pallas_call | solution.py:81
  53.8 3.0 %collective-permute-done.14.refs_5_.refs_1_ = bf16[1280,128]{1,0:T(8,128)(2,1)S(1)} collective-permute-done((bf16[1280,128]{1,0:T(8,128)(2,1)S(1)}, bf16[1280,128]{1,0:T(8,128)(2,1)S(1)}, u32[]{:S(2)}, u32[]{:S(2)}) %collective-permute-start.14) | collective-permute-done | bytes 327712 | tf_op jit(solution)/shard_map/ppermute | solution.py:536
  57.8 1.6 %collective-permute-start.25 = (bf16[640,128]{1,0:T(8,128)(2,1)S(1)}, bf16[640,128]{1,0:T(8,128)(2,1)S(1)}, u32[]{:S(2)}, u32[]{:S(2)}) collective-permute-start(bf16[640,128]{1,0:T(8,128)(2,1)S(1)} %shard_map.168), channel_id=1, source_target_pairs={{0,8},{4,12},{8,0},{12,4},{16,24},{20,28},{24,16},{28,20},{1,9},{5... | collective-permute-start | bytes 491528 | tf_op jit(solution)/shard_map/ppermute | solution.py:536
  59.7 1.6 %collective-permute-start.18 = (bf16[1,128,256]{2,1,0:T(8,128)(2,1)S(1)}, bf16[1,128,256]{2,1,0:T(8,128)(2,1)S(1)}, u32[]{:S(2)}, u32[]{:S(2)}) collective-permute-start(bf16[1,128,256]{2,1,0:T(8,128)(2,1)S(1)} %bitcast.48), channel_id=1, source_target_pairs={{0,8},{4,12},{8,0},{12,4},{16,24},{20,28},{24,16},{28,20},{1,9},{5... | collective-permute-start | bytes 196616 | tf_op jit(solution)/shard_map/ppermute | solution.py:536
  61.2 3.6 %collective-permute-done.25.refs_1_.refs_3_ = bf16[640,128]{1,0:T(8,128)(2,1)S(1)} collective-permute-done((bf16[640,128]{1,0:T(8,128)(2,1)S(1)}, bf16[640,128]{1,0:T(8,128)(2,1)S(1)}, u32[]{:S(2)}, u32[]{:S(2)}) %collective-permute-start.25) | collective-permute-done | bytes 163872 | tf_op jit(solution)/shard_map/ppermute | solution.py:536
  65.0 1.6 %collective-permute-start.20 = (bf16[896,128]{1,0:T(8,128)(2,1)S(1)}, bf16[896,128]{1,0:T(8,128)(2,1)S(1)}, u32[]{:S(2)}, u32[]{:S(2)}) collective-permute-start(bf16[896,128]{1,0:T(8,128)(2,1)S(1)} %shard_map.165.refs_2_), channel_id=1, source_target_pairs={{0,1},{1,0},{2,3},{3,2},{4,5},{5,4},{6,7},{7,6},{8,9},{9,8},{10,11... | collective-permute-start | bytes 688136 | tf_op jit(solution)/shard_map/ppermute | solution.py:536
  66.6 1.9 %collective-permute-start.19 = (bf16[2,128,256]{2,1,0:T(8,128)(2,1)S(1)}, bf16[2,128,256]{2,1,0:T(8,128)(2,1)S(1)}, u32[]{:S(2)}, u32[]{:S(2)}) collective-permute-start(bf16[2,128,256]{2,1,0:T(8,128)(2,1)S(1)} %shard_map.164), channel_id=1, source_target_pairs={{0,16},{4,20},{8,24},{12,28},{16,0},{20,4},{24,8},{28,12},{1,17},{... | collective-permute-start | bytes 393224 | tf_op jit(solution)/shard_map/ppermute | solution.py:536
  68.6 2.6 %shard_map.163 = (bf16[128,2560]{1,0:T(8,128)(2,1)}, f32[40,128]{1,0:T(8,128)}, f32[40,128]{1,0:T(8,128)}, f32[8,128]{1,0:T(8,128)S(1)}) custom-call(bf16[128,2560]{1,0:T(8,128)(2,1)S(1)} %bitcast.38, bf16[128,256]{1,0:T(8,128)(2,1)S(1)} %get-tuple-element.46.refs_2_.refs_1_, f32[40,128]{1,0:T(8,128)S(1)} %copy-done.15, f32[40,128]{1,0:T(8,128)S(1)} %bitcast.52, ...), custom_call_target="tpu_custom_call" | custom-call | flops 8999999488 | bytes 1000 | tf_op jit(solution)/shard_map/pallas_call | solution.py:81
  71.2 1.8 %collective-permute-done.20.refs_7_.refs_3_ = bf16[896,128]{1,0:T(8,128)(2,1)S(1)} collective-permute-done((bf16[896,128]{1,0:T(8,128)(2,1)S(1)}, bf16[896,128]{1,0:T(8,128)(2,1)S(1)}, u32[]{:S(2)}, u32[]{:S(2)}) %collective-permute-start.20) | collective-permute-done | bytes 229408 | tf_op jit(solution)/shard_map/ppermute | solution.py:536
  75.1 2.6 %collective-permute-start.24 = (bf16[80,256]{1,0:T(8,128)(2,1)S(1)}, bf16[80,256]{1,0:T(8,128)(2,1)S(1)}, u32[]{:S(2)}, u32[]{:S(2)}) collective-permute-start(bf16[80,256]{1,0:T(8,128)(2,1)S(1)} %get-tuple-element.80), channel_id=1, source_target_pairs={{0,3},{1,2},{2,1},{3,0},{4,7},{5,6},{6,5},{7,4},{8,11},{9,10},{10,... | collective-permute-start | bytes 122888 | tf_op jit(solution)/shard_map/ppermute | solution.py:536
  79.6 2.4 %shard_map.170 = bf16[896,640]{1,0:T(8,128)(2,1)} custom-call(bf16[896,128]{1,0:T(8,128)(2,1)S(1)} %shard_map.153.refs_8_.refs_3_.refs_0_, bf16[896,128]{1,0:T(8,128)(2,1)S(1)} %collective-permute-done.16.refs_7_.refs_1_, bf16[896,128]{1,0:T(8,128)(2,1)S(1)} %shard_map.165.refs_2_, bf16[896,128]{1,0:T(8,128)(2,1)S(1)} %collective-permute-done.20.refs_7_.refs_3_, ...), custom_call_target="tpu_custom_call" | custom-call | flops 3000000000 | bytes 1000 | tf_op jit(solution)/shard_map/pallas_call | solution.py:81
  (100 shorter events, 23.1 us)
Async XLA Ops:
  1.6 23.0 %collective-permute-start = (bf16[320,256]{1,0:T(8,128)(2,1)S(1)}, bf16[320,256]{1,0:T(8,128)(2,1)S(1)}, u32[]{:S(2)}, u32[]{:S(2)}) collective-permute-start(bf16[320,256]{1,0:T(8,128)(2,1)S(1)} %constant_dynamic-slice_fusion), channel_id=1, source_target_pairs={{0,1},{1,0},{2,3},{3,2},{4,5},{5,4},{6,7},{7,6},{8,9},{9,8},{10,11... | collective-permute-start | bytes 491528 | tf_op jit(solution)/shard_map/ppermute | solution.py:536
  4.7 10.1 %collective-permute-start.1 = (bf16[320,256]{1,0:T(8,128)(2,1)S(1)}, bf16[320,256]{1,0:T(8,128)(2,1)S(1)}, u32[]{:S(2)}, u32[]{:S(2)}) collective-permute-start(bf16[320,256]{1,0:T(8,128)(2,1)S(1)} %constant_dynamic-slice_fusion), channel_id=1, source_target_pairs={{0,2},{1,3},{2,0},{3,1},{4,6},{5,7},{6,4},{7,5},{8,10},{9,11},{10,... | collective-permute-start | bytes 491528 | tf_op jit(solution)/shard_map/ppermute | solution.py:536
  15.7 8.9 %collective-permute-start.2 = (bf16[320,256]{1,0:T(8,128)(2,1)S(1)}, bf16[320,256]{1,0:T(8,128)(2,1)S(1)}, u32[]{:S(2)}, u32[]{:S(2)}) collective-permute-start(bf16[320,256]{1,0:T(8,128)(2,1)S(1)} %shard_map.147.refs_1_.refs_4_), channel_id=1, source_target_pairs={{0,1},{1,0},{2,3},{3,2},{4,5},{5,4},{6,7},{7,6},{8,9},{9,8},{10,11... | collective-permute-start | bytes 491528 | tf_op jit(solution)/shard_map/ppermute | solution.py:536
  16.2 5.3 %collective-permute-start.3 = (bf16[320,128]{1,0:T(8,128)(2,1)S(1)}, bf16[320,128]{1,0:T(8,128)(2,1)S(1)}, u32[]{:S(2)}, u32[]{:S(2)}) collective-permute-start(bf16[320,128]{1,0:T(8,128)(2,1)S(1)} %copy-done.4), channel_id=1, source_target_pairs={{0,8},{4,12},{8,0},{12,4},{16,24},{20,28},{24,16},{28,20},{1,9},{5... | collective-permute-start | bytes 245768 | tf_op jit(solution)/shard_map/ppermute | solution.py:536
  17.7 5.1 %collective-permute-start.4 = (bf16[320,128]{1,0:T(8,128)(2,1)S(1)}, bf16[320,128]{1,0:T(8,128)(2,1)S(1)}, u32[]{:S(2)}, u32[]{:S(2)}) collective-permute-start(bf16[320,128]{1,0:T(8,128)(2,1)S(1)} %copy-done.4), channel_id=1, source_target_pairs={{0,16},{4,20},{8,24},{12,28},{16,0},{20,4},{24,8},{28,12},{1,17},{... | collective-permute-start | bytes 245768 | tf_op jit(solution)/shard_map/ppermute | solution.py:536
  19.2 5.3 %collective-permute-start.5 = (bf16[320,128]{1,0:T(8,128)(2,1)S(1)}, bf16[320,128]{1,0:T(8,128)(2,1)S(1)}, u32[]{:S(2)}, u32[]{:S(2)}) collective-permute-start(bf16[320,128]{1,0:T(8,128)(2,1)S(1)} %copy-done.4), channel_id=1, source_target_pairs={{0,24},{4,28},{8,16},{12,20},{16,8},{20,12},{24,0},{28,4},{1,25},{... | collective-permute-start | bytes 245768 | tf_op jit(solution)/shard_map/ppermute | solution.py:536
  24.6 5.3 %collective-permute-start.6 = (bf16[3,320,256]{2,1,0:T(8,128)(2,1)S(1)}, bf16[3,320,256]{2,1,0:T(8,128)(2,1)S(1)}, u32[]{:S(2)}, u32[]{:S(2)}) collective-permute-start(bf16[3,320,256]{2,1,0:T(8,128)(2,1)S(1)} %bitcast.43), channel_id=1, source_target_pairs={{0,4},{4,0},{8,12},{12,8},{16,20},{20,16},{24,28},{28,24},{1,5},{5... | collective-permute-start | bytes 1474568 | tf_op jit(solution)/shard_map/ppermute | solution.py:536
  24.7 5.2 %collective-permute-start.7 = (bf16[160,128]{1,0:T(8,128)(2,1)}, bf16[160,128]{1,0:T(8,128)(2,1)S(1)}, u32[]{:S(2)}, u32[]{:S(2)}) collective-permute-start(bf16[160,128]{1,0:T(8,128)(2,1)} %get-tuple-element.45), channel_id=1, source_target_pairs={{0,2},{1,3},{2,0},{3,1},{4,6},{5,7},{6,4},{7,5},{8,10},{9,11},{10,... | collective-permute-start | bytes 122888 | tf_op jit(solution)/shard_map/ppermute | solution.py:536
  32.0 4.8 %collective-permute-start.8 = (bf16[1328,128]{1,0:T(8,128)(2,1)S(1)}, bf16[1328,128]{1,0:T(8,128)(2,1)S(1)}, u32[]{:S(2)}, u32[]{:S(2)}) collective-permute-start(bf16[1328,128]{1,0:T(8,128)(2,1)S(1)} %get-tuple-element.51), channel_id=1, source_target_pairs={{0,4},{4,0},{8,12},{12,8},{16,20},{20,16},{24,28},{28,24},{1,5},{5... | collective-permute-start | bytes 1019912 | tf_op jit(solution)/shard_map/ppermute | solution.py:536
  32.1 6.1 %collective-permute-start.11 = (bf16[4,320,128]{2,1,0:T(8,128)(2,1)S(1)}, bf16[4,320,128]{2,1,0:T(8,128)(2,1)S(1)}, u32[]{:S(2)}, u32[]{:S(2)}) collective-permute-start(bf16[4,320,128]{2,1,0:T(8,128)(2,1)S(1)} %bitcast.46), channel_id=1, source_target_pairs={{0,4},{4,0},{8,12},{12,8},{16,20},{20,16},{24,28},{28,24},{1,5},{5... | collective-permute-start | bytes 983048 | tf_op jit(solution)/shard_map/ppermute | solution.py:536
  37.0 9.4 %collective-permute-start.10 = (bf16[1328,128]{1,0:T(8,128)(2,1)S(1)}, bf16[1328,128]{1,0:T(8,128)(2,1)S(1)}, u32[]{:S(2)}, u32[]{:S(2)}) collective-permute-start(bf16[1328,128]{1,0:T(8,128)(2,1)S(1)} %shard_map.151.refs_4_.refs_2_.refs_0_), channel_id=1, source_target_pairs={{0,8},{4,12},{8,0},{12,4},{16,24},{20,28},{24,16},{28,20},{1,9},{5... | collective-permute-start | bytes 1019912 | tf_op jit(solution)/shard_map/ppermute | solution.py:686
  37.6 10.0 %collective-permute-start.12 = (bf16[1600,128]{1,0:T(8,128)(2,1)S(1)}, bf16[1600,128]{1,0:T(8,128)(2,1)S(1)}, u32[]{:S(2)}, u32[]{:S(2)}) collective-permute-start(bf16[1600,128]{1,0:T(8,128)(2,1)S(1)} %shard_map.156), channel_id=1, source_target_pairs={{0,16},{4,20},{8,24},{12,28},{16,0},{20,4},{24,8},{28,12},{1,17},{... | collective-permute-start | bytes 1228808 | tf_op jit(solution)/shard_map/ppermute | solution.py:536
  41.1 12.7 %collective-permute-start.15 = (bf16[896,128]{1,0:T(8,128)(2,1)S(1)}, bf16[896,128]{1,0:T(8,128)(2,1)S(1)}, u32[]{:S(2)}, u32[]{:S(2)}) collective-permute-start(bf16[896,128]{1,0:T(8,128)(2,1)S(1)} %shard_map.153.refs_8_.refs_3_.refs_0_), channel_id=1, source_target_pairs={{0,2},{1,3},{2,0},{3,1},{4,6},{5,7},{6,4},{7,5},{8,10},{9,11},{10,... | collective-permute-start | bytes 688136 | tf_op jit(solution)/shard_map/ppermute | solution.py:536
  43.7 10.0 %collective-permute-start.16 = (bf16[896,128]{1,0:T(8,128)(2,1)S(1)}, bf16[896,128]{1,0:T(8,128)(2,1)S(1)}, u32[]{:S(2)}, u32[]{:S(2)}) collective-permute-start(bf16[896,128]{1,0:T(8,128)(2,1)S(1)} %shard_map.153.refs_8_.refs_3_.refs_0_), channel_id=1, source_target_pairs={{0,1},{1,0},{2,3},{3,2},{4,5},{5,4},{6,7},{7,6},{8,9},{9,8},{10,11... | collective-permute-start | bytes 688136 | tf_op jit(solution)/shard_map/ppermute | solution.py:536
  47.9 9.5 %collective-permute-start.13 = (bf16[1328,128]{1,0:T(8,128)(2,1)S(1)}, bf16[1328,128]{1,0:T(8,128)(2,1)S(1)}, u32[]{:S(2)}, u32[]{:S(2)}) collective-permute-start(bf16[1328,128]{1,0:T(8,128)(2,1)S(1)} %shard_map.157.refs_8_.refs_2_), channel_id=1, source_target_pairs={{16,0},{20,4},{24,8},{28,12},{17,1},{21,5},{25,9},{29,13},{18,2},{... | collective-permute-start | bytes 1019912 | tf_op jit(solution)/shard_map/ppermute | solution.py:686
  49.4 7.4 %collective-permute-start.14 = (bf16[1280,128]{1,0:T(8,128)(2,1)S(1)}, bf16[1280,128]{1,0:T(8,128)(2,1)S(1)}, u32[]{:S(2)}, u32[]{:S(2)}) collective-permute-start(bf16[1280,128]{1,0:T(8,128)(2,1)S(1)} %shard_map.160), channel_id=1, source_target_pairs={{0,8},{4,12},{8,0},{12,4},{16,24},{20,28},{24,16},{28,20},{1,9},{5... | collective-permute-start | bytes 983048 | tf_op jit(solution)/shard_map/ppermute | solution.py:536
  57.8 7.1 %collective-permute-start.25 = (bf16[640,128]{1,0:T(8,128)(2,1)S(1)}, bf16[640,128]{1,0:T(8,128)(2,1)S(1)}, u32[]{:S(2)}, u32[]{:S(2)}) collective-permute-start(bf16[640,128]{1,0:T(8,128)(2,1)S(1)} %shard_map.168), channel_id=1, source_target_pairs={{0,8},{4,12},{8,0},{12,4},{16,24},{20,28},{24,16},{28,20},{1,9},{5... | collective-permute-start | bytes 491528 | tf_op jit(solution)/shard_map/ppermute | solution.py:536
  59.7 6.9 %collective-permute-start.18 = (bf16[1,128,256]{2,1,0:T(8,128)(2,1)S(1)}, bf16[1,128,256]{2,1,0:T(8,128)(2,1)S(1)}, u32[]{:S(2)}, u32[]{:S(2)}) collective-permute-start(bf16[1,128,256]{2,1,0:T(8,128)(2,1)S(1)} %bitcast.48), channel_id=1, source_target_pairs={{0,8},{4,12},{8,0},{12,4},{16,24},{20,28},{24,16},{28,20},{1,9},{5... | collective-permute-start | bytes 196616 | tf_op jit(solution)/shard_map/ppermute | solution.py:536
  64.8 14.8 %collective-permute-start.26 = (bf16[4,320,128]{2,1,0:T(8,128)(2,1)S(1)}, bf16[4,320,128]{2,1,0:T(8,128)(2,1)S(1)}, u32[]{:S(2)}, u32[]{:S(2)}) collective-permute-start(bf16[4,320,128]{2,1,0:T(8,128)(2,1)S(1)} %bitcast.44), channel_id=1, source_target_pairs={{0,4},{4,0},{8,12},{12,8},{16,20},{20,16},{24,28},{28,24},{1,5},{5... | collective-permute-start | bytes 983048 | tf_op jit(solution)/shard_map/ppermute | solution.py:536
  65.0 8.1 %collective-permute-start.20 = (bf16[896,128]{1,0:T(8,128)(2,1)S(1)}, bf16[896,128]{1,0:T(8,128)(2,1)S(1)}, u32[]{:S(2)}, u32[]{:S(2)}) collective-permute-start(bf16[896,128]{1,0:T(8,128)(2,1)S(1)} %shard_map.165.refs_2_), channel_id=1, source_target_pairs={{0,1},{1,0},{2,3},{3,2},{4,5},{5,4},{6,7},{7,6},{8,9},{9,8},{10,11... | collective-permute-start | bytes 688136 | tf_op jit(solution)/shard_map/ppermute | solution.py:536
  66.6 6.4 %collective-permute-start.19 = (bf16[2,128,256]{2,1,0:T(8,128)(2,1)S(1)}, bf16[2,128,256]{2,1,0:T(8,128)(2,1)S(1)}, u32[]{:S(2)}, u32[]{:S(2)}) collective-permute-start(bf16[2,128,256]{2,1,0:T(8,128)(2,1)S(1)} %shard_map.164), channel_id=1, source_target_pairs={{0,16},{4,20},{8,24},{12,28},{16,0},{20,4},{24,8},{28,12},{1,17},{... | collective-permute-start | bytes 393224 | tf_op jit(solution)/shard_map/ppermute | solution.py:536
  75.1 6.8 %collective-permute-start.24 = (bf16[80,256]{1,0:T(8,128)(2,1)S(1)}, bf16[80,256]{1,0:T(8,128)(2,1)S(1)}, u32[]{:S(2)}, u32[]{:S(2)}) collective-permute-start(bf16[80,256]{1,0:T(8,128)(2,1)S(1)} %get-tuple-element.80), channel_id=1, source_target_pairs={{0,3},{1,2},{2,1},{3,0},{4,7},{5,6},{6,5},{7,4},{8,11},{9,10},{10,... | collective-permute-start | bytes 122888 | tf_op jit(solution)/shard_map/ppermute | solution.py:536
  77.7 5.3 %collective-permute-start.23 = (bf16[80,256]{1,0:T(8,128)(2,1)S(1)}, bf16[80,256]{1,0:T(8,128)(2,1)S(1)}, u32[]{:S(2)}, u32[]{:S(2)}) collective-permute-start(bf16[80,256]{1,0:T(8,128)(2,1)S(1)} %get-tuple-element.79), channel_id=1, source_target_pairs={{0,2},{1,3},{2,0},{3,1},{4,6},{5,7},{6,4},{7,5},{8,10},{9,11},{10,... | collective-permute-start | bytes 122888 | tf_op jit(solution)/shard_map/ppermute | solution.py:536
  78.3 4.8 %collective-permute-start.22 = (bf16[80,256]{1,0:T(8,128)(2,1)S(1)}, bf16[80,256]{1,0:T(8,128)(2,1)S(1)}, u32[]{:S(2)}, u32[]{:S(2)}) collective-permute-start(bf16[80,256]{1,0:T(8,128)(2,1)S(1)} %get-tuple-element.78), channel_id=1, source_target_pairs={{0,1},{1,0},{2,3},{3,2},{4,5},{5,4},{6,7},{7,6},{8,9},{9,8},{10,11... | collective-permute-start | bytes 122888 | tf_op jit(solution)/shard_map/ppermute | solution.py:536
  (23 other events, 132.6 us)

commit v11 on v10

--- a/solution.py
+++ b/solution.py
@@ -185,21 +185,21 @@
         at += stop - start
 
 
-def joined(arrays, after=(), ranges=None):
+def joined(arrays, after=(), ranges=None, cost=0.2):
     ranges = ranges or [(0, a.shape[0]) for a in arrays]
     dims = (sum(stop - start for start, stop in ranges), *arrays[0].shape[1:])
     return call(
         lambda *refs: join_kernel(ranges, *refs),
         [shape(dims, arrays[0].dtype)],
-        0.2,
+        cost,
         tuple(arrays),
         after=after,
     )[0]
 
 
-def stacked(arrays, after=(), ranges=None):
+def stacked(arrays, after=(), ranges=None, cost=0.2):
     count = len(arrays)
-    out = joined(arrays, after, ranges)
+    out = joined(arrays, after, ranges, cost)
     return out.reshape(count, out.shape[0] // count, *out.shape[1:])
 
 
@@ -506,7 +506,7 @@
             pltpu.VMEM((total, hidden), F32),
         ],
         cost_estimate=pl.CostEstimate(
-            flops=int(3e9), bytes_accessed=1000, transcendentals=0
+            flops=int(1e9), bytes_accessed=1000, transcendentals=0
         ),
         compiler_params=pltpu.CompilerParams(vmem_limit_bytes=20 * 1024 * 1024),
     )(a, b, w_gate, w_up, *after)
@@ -615,18 +615,14 @@
     if n_dp == 4:
         one = (0, grad_rows), (grad_rows, 2 * grad_rows)
         over_2 = xored(deals[1], "dp", 2)
-        over_1 = xored(joined([deals[0], over_2], ranges=[one[1], one[1]]), "dp", 1)
-        dealt = joined([deals[0], over_1, over_2, over_1], (), [one[0], one[0], one[0], one[1]])
-        first_hop, second_hop = (over_2,), (over_1,)
+        early = (over_2,)
     else:
-        first_hop = second_hop = ()
-        dealt = joined(deals[:1] + [xored(d, "dp", s + 1) for s, d in enumerate(deals[1:])])
+        early = ()
+        source, spans = deals[:1] + [xored(d, "dp", s + 1) for s, d in enumerate(deals[1:])], None
     w_far = xored(w_half, "dp", n_dp // 2)
     mine = gathered(w_half, "dp", n_dp // 2)[1:]
     mine += gathered(joined([w_far], after=(rows,)), "dp", n_dp // 2)
-    other = swapped(stacked(mine, after=tuple(rows_in[1:])))
-    rows_a = stacked(rows_in, after=(other,))
-    rows_b = swapped(rows_a)
+    other = swapped(stacked(mine, after=(*rows_in[1:3],), cost=1.0))
     w_whole, bc, keep, send = call(
         lambda *refs: project_kernel(n_dp - 1, many, *refs),
         [
@@ -637,7 +633,6 @@
         ],
         1.0,
         (x, dyt, w_bc, *mine, other),
-        after=first_hop,
     )
     recv = swapped(send)
     hidden = w_gate.shape[2]
@@ -647,13 +642,14 @@
             [shape((part + up16(2 * many), half), BF16)],
             0.5,
             (keep, recv),
-            after=second_hop,
         )[0]
     ]
+    rows_a = stacked(rows_in, after=(climbs[0],))
+    rows_b = swapped(rows_a)
     weighted = expert(rows_a, rows_b, w_gate[0], w_up[0], capacity, flip, (climbs[0],))
     if n_chip == 4:
         x_rows = width // n_chip
-        over_y = xored(joined([xt[2], dealt], (climbs[0],)), "tm", 4)
+        over_y = xored(xt[2], "tm", 4)
 
     parts = 2
     tiles = width // LANES // parts
@@ -669,13 +665,13 @@
                 shape((heads // parts, length), F32),
                 shape((heads // parts, length), F32),
             ],
-            1.0,
+            0.7,
             (x, dy, bc, cumt, cum, steps, h_in, mixed),
             after=later,
             scratch=[pltpu.VMEM((heads, length), F32)],
         )
         if i == 0:
-            held = (dx, weighted, *((over_y,) if n_chip == 4 else ()))
+            held = (dx, weighted, *early, *((over_y,) if n_chip == 4 else ()))
             arrived = []
             bit = 1
             while bit < n_chip:
@@ -707,19 +703,18 @@
     )
 
     held = (dc,)
+    if n_dp == 4:
+        over_1 = xored(joined([deals[0], over_2], later, [one[1], one[1]]), "dp", 1)
+        source, spans = [deals[0], over_1, over_2, over_1], [one[0], one[0], one[0], one[1]]
+    dealt = joined(source, later, spans)
+    held += (dealt,)
     if n_chip == 4:
         over_x = xored(joined([xt[1], over_y], later, [(0, x_rows), (x_rows, 2 * x_rows)]), "tm", 2)
         columns_in = [xt[0], over_x, over_y]
         places = [(0, 0), (1, 0), (2, 0), (1, x_rows)]
-        from_y = (2 * x_rows, over_y.shape[0])
-        grads = joined([dealt, over_y], (later[0],), [(0, dealt.shape[0]), from_y])
-        grads = [dealt, xored(grads, "tm", 2), over_y]
-        spans = [(0, dealt.shape[0]), (0, dealt.shape[0]), from_y, (dealt.shape[0], 2 * dealt.shape[0])]
-        grads = joined([grads[0], grads[1], grads[2], grads[1]], (), spans)
         held += (over_x,)
     else:
         columns_in = chips(xt)
-        grads = joined(chips([dealt] * n_chip))
         places = [(i, 0) for i in range(n_chip)]
     far = xored(weighted, "dp", n_dp // 2)
     near = gathered(weighted, "dp", n_dp // 2)
@@ -731,15 +726,21 @@
         (*arrived, keep, recv),
         after=held,
     )
-    grads_a = grads.reshape(n_chip, grads.shape[0] // n_chip, LANES)
-    grads_b = swapped(grads_a)
     r_recv = swapped(r_send)
+    if n_chip == 4:
+        grads_y = xored(dealt, "tm", 4)
+        grads_x = xored(joined([dealt, grads_y], (r_own,)), "tm", 2)
+        rest = dealt.shape[0]
+        grads = [dealt, grads_x, grads_y, grads_x]
+        spans = [(0, rest), (0, rest), (0, rest), (rest, 2 * rest)]
+    else:
+        grads, spans = chips([dealt] * n_chip), None
     fars = gathered(joined([far], (r_own,)), "dp", n_dp // 2)
     d_bc = call(db_kernel, [shape((length, columns), BF16)], 0.3, (xs, r_own, r_recv, db, dc))[0]
     d_bcs = [d_bc.reshape(1, length, columns)]
     while 2 ** (len(d_bcs) - 1) < n_chip:
         level = 2 ** (len(d_bcs) - 1)
-        sent = d_bcs[0] if level == 1 else joined(d_bcs)
+        sent = d_bcs[0] if level == 1 else joined(d_bcs, tuple(fars[1:]))
         d_bcs.append(xored(sent, "tm", 2 * level))
     d_in, d_decay, d_step, token = call(
         lambda *refs: finish_kernel(parts, *refs),
@@ -760,7 +761,7 @@
         [shape((w_rows, columns), F32), shape((w_rows, columns), BF16)],
         0.5,
         (*columns_in, *d_bcs),
-        after=(token, *fars[1:]),
+        after=(token,),
         scratch=[pltpu.VMEM((2, w_rows, columns), F32)],
     )
     final = call(
@@ -775,6 +776,8 @@
     for s in range(1, n_dp):
         w_bc_grad = w_bc_grad + xored(final[s], "dp", s).astype(F32)
 
+    grads_a = stacked(grads, (token,), spans)
+    grads_b = swapped(grads_a)
     w_down_grad = call(
         lambda *refs: down_kernel(n_dp, flip, capacity, grad_rows, *refs),
         [shape((hidden, piece), BF16)],

time: 84 us -> 79.8 us (0.950)
  waiting for transfers between devices: 23.6 us -> 19.3 us
  starting transfers between devices: 33 us -> 34.3 us
  local copies, waits for them, and re-layouts: 3.04 us -> 1.95 us
    ppermute x25 -> x26, waiting for transfers between devices: 23.1 us -> 18.7 us  [xored(): return lax.ppermute(array, axis, [(i, i ^ mask) for i in range(count)])]
    ppermute x25 -> x26, starting transfers between devices: 30.9 us -> 32.3 us  [xored(): return lax.ppermute(array, axis, [(i, i ^ mask) for i in range(count)])]
    unnamed x40 -> x44, local copies, waits for them, and re-layouts: 2.1 us -> 1.02 us
    pallas_call x24 -> x23, Pallas kernels: 18.9 us -> 18.8 us  [call(): pl.pallas_call(body, out_shape=outs, in_specs=specs + [pl.BlockSpec(memor...]
  transfers between devices with their start and end apart: 27 -> 28, of which waited for: 13 -> 12; matrix products, arithmetic and copies ran while one was open for 0% -> 0% of each run, Pallas kernels for 24% -> 25%
where the time goes in v11:
time: 79.8 us; the launch traced here: 79.6 us
  starting transfers between devices  34.3 us (43%)
  Pallas kernels  21.6 us (27%)
  waiting for transfers between devices  19.3 us (24%)
  local copies, waits for them, and re-layouts  1.95 us (2%)
  between operations  1.74 us (2%)
    ppermute x26, starting transfers between devices, xored(): return lax.ppermute(array, axis, [(i, i ^ mask) for i in range(count)])  32.3 us
    pallas_call x23, Pallas kernels, call(): pl.pallas_call(body, out_shape=outs, in_specs=specs + [pl.BlockSpec(memor...  18.8 us
    ppermute x26, waiting for transfers between devices, xored(): return lax.ppermute(array, axis, [(i, i ^ mask) for i in range(count)])  18.7 us
    pallas_call x1, Pallas kernels, expert(): pl.pallas_call(body, out_shape=shape(out, BF16), grid=(width // depth,),...  2.75 us
    ppermute x2, starting transfers between devices, per_device(): arrived.append(lax.ppermute(climbs[-1], 'tm', moves))  2.07 us
  transfers between devices with their start and end apart: 28, of which 12 were waited for; matrix products, arithmetic and copies ran while one was open for 0% of the time, Pallas kernels for 25%

profile of v11, /device:TPU:0, one launch (start us, length us, event | category | flops | bytes accessed | tf_op | source)
XLA Modules:
  0.0 79.6 jit_solution(7081168172407290816)
XLA Ops:
  1.6 4.1 %collective-permute-start.1 = (bf16[320,256]{1,0:T(8,128)(2,1)S(1)}, bf16[320,256]{1,0:T(8,128)(2,1)S(1)}, u32[]{:S(2)}, u32[]{:S(2)}) collective-permute-start(bf16[320,256]{1,0:T(8,128)(2,1)S(1)} %constant_dynamic-slice_fusion), channel_id=1, source_target_pairs={{0,2},{1,3},{2,0},{3,1},{4,6},{5,7},{6,4},{7,5},{8,10},{9,11},{10,... | collective-permute-start | bytes 491528 | tf_op jit(solution)/shard_map/ppermute | solution.py:536
  5.7 1.6 %collective-permute-start = (bf16[320,256]{1,0:T(8,128)(2,1)S(1)}, bf16[320,256]{1,0:T(8,128)(2,1)S(1)}, u32[]{:S(2)}, u32[]{:S(2)}) collective-permute-start(bf16[320,256]{1,0:T(8,128)(2,1)S(1)} %constant_dynamic-slice_fusion), channel_id=1, source_target_pairs={{0,1},{1,0},{2,3},{3,2},{4,5},{5,4},{6,7},{7,6},{8,9},{9,8},{10,11... | collective-permute-start | bytes 491528 | tf_op jit(solution)/shard_map/ppermute | solution.py:536
  7.9 5.6 %shard_map.146 = (f32[40,128]{1,0:T(8,128)}, f32[128,128]{1,0:T(8,128)}, f32[128,128]{1,0:T(8,128)}, bf16[2640,128]{1,0:T(8,128)(2,1)}, bf16[128,2560]{1,0:T(8,1...) custom-call(bf16[128,2560]{1,0:T(8,128)(2,1)} %bitcast.36, ...), custom_call_target="tpu_custom_call" | custom-call | flops 6000000000 | bytes 1000 | tf_op jit(solution)/shard_map/pallas_call | solution.py:81
  15.1 1.5 %collective-permute-start.3 = (bf16[320,128]{1,0:T(8,128)(2,1)S(1)}, bf16[320,128]{1,0:T(8,128)(2,1)S(1)}, u32[]{:S(2)}, u32[]{:S(2)}) collective-permute-start(bf16[320,128]{1,0:T(8,128)(2,1)S(1)} %copy-done.4), channel_id=1, source_target_pairs={{0,8},{4,12},{8,0},{12,4},{16,24},{20,28},{24,16},{28,20},{1,9},{5... | collective-permute-start | bytes 245768 | tf_op jit(solution)/shard_map/ppermute | solution.py:536
  16.6 1.5 %collective-permute-start.4 = (bf16[320,128]{1,0:T(8,128)(2,1)S(1)}, bf16[320,128]{1,0:T(8,128)(2,1)S(1)}, u32[]{:S(2)}, u32[]{:S(2)}) collective-permute-start(bf16[320,128]{1,0:T(8,128)(2,1)S(1)} %copy-done.4), channel_id=1, source_target_pairs={{0,16},{4,20},{8,24},{12,28},{16,0},{20,4},{24,8},{28,12},{1,17},{... | collective-permute-start | bytes 245768 | tf_op jit(solution)/shard_map/ppermute | solution.py:536
  19.6 1.5 %collective-permute-done.4.refs_4_.refs_2_ = bf16[320,128]{1,0:T(8,128)(2,1)S(1)} collective-permute-done((bf16[320,128]{1,0:T(8,128)(2,1)S(1)}, bf16[320,128]{1,0:T(8,128)(2,1)S(1)}, u32[]{:S(2)}, u32[]{:S(2)}) %collective-permute-start.4) | collective-permute-done | bytes 81952 | tf_op jit(solution)/shard_map/ppermute | solution.py:536
  21.2 1.9 %collective-permute-done.5.refs_6_ = bf16[3,320,256]{2,1,0:T(8,128)(2,1)S(1)} collective-permute-done((bf16[3,320,256]{2,1,0:T(8,128)(2,1)S(1)}, bf16[3,320,256]{2,1,0:T(8,128)(2,1)S(1)}, u32[]{:S(2)}, u32[]{:S(2)}) %collective-permute-start.5) | collective-permute-done | bytes 491552 | tf_op jit(solution)/shard_map/ppermute | solution.py:536
  24.3 1.5 %collective-permute-start.8 = (bf16[320,128]{1,0:T(8,128)(2,1)S(1)}, bf16[320,128]{1,0:T(8,128)(2,1)S(1)}, u32[]{:S(2)}, u32[]{:S(2)}) collective-permute-start(bf16[320,128]{1,0:T(8,128)(2,1)S(1)} %copy-done.5), channel_id=1, source_target_pairs={{0,24},{4,28},{8,16},{12,20},{16,8},{20,12},{24,0},{28,4},{1,25},{... | collective-permute-start | bytes 245768 | tf_op jit(solution)/shard_map/ppermute | solution.py:536
  26.0 3.9 %collective-permute-done.8.refs_3_ = bf16[320,128]{1,0:T(8,128)(2,1)S(1)} collective-permute-done((bf16[320,128]{1,0:T(8,128)(2,1)S(1)}, bf16[320,128]{1,0:T(8,128)(2,1)S(1)}, u32[]{:S(2)}, u32[]{:S(2)}) %collective-permute-start.8) | collective-permute-done | bytes 81952 | tf_op jit(solution)/shard_map/ppermute | solution.py:536
  30.7 1.5 %collective-permute-start.11 = (bf16[1280,128]{1,0:T(8,128)(2,1)S(1)}, bf16[1280,128]{1,0:T(8,128)(2,1)S(1)}, u32[]{:S(2)}, u32[]{:S(2)}) collective-permute-start(bf16[1280,128]{1,0:T(8,128)(2,1)S(1)} %copy-done.16), channel_id=1, source_target_pairs={{0,16},{4,20},{8,24},{12,28},{16,0},{20,4},{24,8},{28,12},{1,17},{... | collective-permute-start | bytes 983048 | tf_op jit(solution)/shard_map/ppermute | solution.py:536
  32.2 3.4 %collective-permute-start.10 = (bf16[160,128]{1,0:T(8,128)(2,1)S(1)}, bf16[160,128]{1,0:T(8,128)(2,1)S(1)}, u32[]{:S(2)}, u32[]{:S(2)}) collective-permute-start(bf16[160,128]{1,0:T(8,128)(2,1)S(1)} %copy-done.17), channel_id=1, source_target_pairs={{0,2},{1,3},{2,0},{3,1},{4,6},{5,7},{6,4},{7,5},{8,10},{9,11},{10,... | collective-permute-start | bytes 122888 | tf_op jit(solution)/shard_map/ppermute | solution.py:536
  35.7 2.8 %shard_map.152.refs_8_.refs_3_.refs_0_ = bf16[896,128]{1,0:T(8,128)(2,1)S(1)} custom-call(bf16[4,320,128]{2,1,0:T(8,128)(2,1)S(1)} %bitcast.32, bf16[4,320,128]{2,1,0:T(8,128)(2,1)S(1)} %collective-permute-done.9.refs_1_, bf16[2560,896]{1,0:T(8,128)(2,1)S(1)} %bitcast.27, bf16[2560,896]{1,0:T(8,128)(2,1)S(1)} %bitcast.30, ...), custom_call_target="tpu_custom_call" | custom-call | flops 1000000000 | bytes 1000 | tf_op jit(solution)/shard_map/pallas_call | solution.py:496
  39.8 2.6 %shard_map.153 = (f32[128,1280]{1,0:T(8,128)S(1)}, f32[128,128]{1,0:T(8,128)S(1)}, f32[20,128]{1,0:T(8,128)S(1)}, f32[20,128]{1,0:T(8,128)S(1)}) custom-call(bf16[128,2560]{1,0:T(8,128)(2,1)S(1)} %bitcast.38, bf16[128,2560]{1,0:T(8,128)(2,1)S(1)} %bitcast.34, bf16[128,256]{1,0:T(8,128)(2,1)S(1)} %get-tuple-element.45.refs_2_.refs_1_, ...), custom_call_target="tpu_custom_call" | custom-call | flops 2100000000 | bytes 1000 | tf_op jit(solution)/shard_map/pallas_call | solution.py:81
  42.6 1.5 %collective-permute-start.12 = (bf16[1328,128]{1,0:T(8,128)(2,1)S(1)}, bf16[1328,128]{1,0:T(8,128)(2,1)S(1)}, u32[]{:S(2)}, u32[]{:S(2)}) collective-permute-start(bf16[1328,128]{1,0:T(8,128)(2,1)S(1)} %shard_map.154.refs_8_.refs_2_.refs_4_), channel_id=1, source_target_pairs={{16,0},{20,4},{24,8},{28,12},{17,1},{21,5},{25,9},{29,13},{18,2},{... | collective-permute-start | bytes 1019912 | tf_op jit(solution)/shard_map/ppermute | solution.py:682
  46.6 2.5 %shard_map.155 = (f32[128,1280]{1,0:T(8,128)S(1)}, f32[128,128]{1,0:T(8,128)S(1)}, f32[20,128]{1,0:T(8,128)S(1)}, f32[20,128]{1,0:T(8,128)S(1)}) custom-call(bf16[128,2560]{1,0:T(8,128)(2,1)S(1)} %bitcast.39, bf16[128,2560]{1,0:T(8,128)(2,1)S(1)} %bitcast.35, bf16[128,256]{1,0:T(8,128)(2,1)S(1)} %get-tuple-element.45.refs_2_.refs_1_, ...), custom_call_target="tpu_custom_call" | custom-call | flops 2100000000 | bytes 1000 | tf_op jit(solution)/shard_map/pallas_call | solution.py:81
  49.4 2.5 %collective-permute-done.13.refs_1_.refs_3_ = bf16[160,128]{1,0:T(8,128)(2,1)S(1)} collective-permute-done((bf16[160,128]{1,0:T(8,128)(2,1)S(1)}, bf16[160,128]{1,0:T(8,128)(2,1)S(1)}, u32[]{:S(2)}, u32[]{:S(2)}) %collective-permute-start.13) | collective-permute-done | bytes 40992 | tf_op jit(solution)/shard_map/ppermute | solution.py:536
  55.1 1.8 %collective-permute-start.25 = (bf16[320,128]{1,0:T(8,128)(2,1)S(1)}, bf16[320,128]{1,0:T(8,128)(2,1)S(1)}, u32[]{:S(2)}, u32[]{:S(2)}) collective-permute-start(bf16[320,128]{1,0:T(8,128)(2,1)S(1)} %shard_map.158.refs_5_.refs_0_), channel_id=1, source_target_pairs={{0,16},{4,20},{8,24},{12,28},{16,0},{20,4},{24,8},{28,12},{1,17},{... | collective-permute-start | bytes 245768 | tf_op jit(solution)/shard_map/ppermute | solution.py:536
  57.3 1.5 %collective-permute-start.18 = (bf16[1,128,256]{2,1,0:T(8,128)(2,1)S(1)}, bf16[1,128,256]{2,1,0:T(8,128)(2,1)S(1)}, u32[]{:S(2)}, u32[]{:S(2)}) collective-permute-start(bf16[1,128,256]{2,1,0:T(8,128)(2,1)S(1)} %bitcast.48), channel_id=1, source_target_pairs={{0,8},{4,12},{8,0},{12,4},{16,24},{20,28},{24,16},{28,20},{1,9},{5... | collective-permute-start | bytes 196616 | tf_op jit(solution)/shard_map/ppermute | solution.py:536
  59.7 1.6 %collective-permute-start.26 = (bf16[640,128]{1,0:T(8,128)(2,1)S(1)}, bf16[640,128]{1,0:T(8,128)(2,1)S(1)}, u32[]{:S(2)}, u32[]{:S(2)}) collective-permute-start(bf16[640,128]{1,0:T(8,128)(2,1)S(1)} %shard_map.167), channel_id=1, source_target_pairs={{0,8},{4,12},{8,0},{12,4},{16,24},{20,28},{24,16},{28,20},{1,9},{5... | collective-permute-start | bytes 491528 | tf_op jit(solution)/shard_map/ppermute | solution.py:536
  62.2 1.9 %collective-permute-start.20 = (bf16[2,128,256]{2,1,0:T(8,128)(2,1)S(1)}, bf16[2,128,256]{2,1,0:T(8,128)(2,1)S(1)}, u32[]{:S(2)}, u32[]{:S(2)}) collective-permute-start(bf16[2,128,256]{2,1,0:T(8,128)(2,1)S(1)} %shard_map.164), channel_id=1, source_target_pairs={{0,16},{4,20},{8,24},{12,28},{16,0},{20,4},{24,8},{28,12},{1,17},{... | collective-permute-start | bytes 393224 | tf_op jit(solution)/shard_map/ppermute | solution.py:536
  64.1 2.7 %shard_map.162 = (bf16[128,2560]{1,0:T(8,128)(2,1)}, f32[40,128]{1,0:T(8,128)}, f32[40,128]{1,0:T(8,128)}, f32[8,128]{1,0:T(8,128)S(1)}) custom-call(bf16[128,2560]{1,0:T(8,128)(2,1)S(1)} %bitcast.40, bf16[128,256]{1,0:T(8,128)(2,1)S(1)} %get-tuple-element.45.refs_2_.refs_1_, f32[40,128]{1,0:T(8,128)S(1)} %copy-done.15, f32[40,128]{1,0:T(8,128)S(1)} %bitcast.52, ...), custom_call_target="tpu_custom_call" | custom-call | flops 8999999488 | bytes 1000 | tf_op jit(solution)/shard_map/pallas_call | solution.py:81
  70.5 2.6 %collective-permute-start.23 = (bf16[80,256]{1,0:T(8,128)(2,1)S(1)}, bf16[80,256]{1,0:T(8,128)(2,1)S(1)}, u32[]{:S(2)}, u32[]{:S(2)}) collective-permute-start(bf16[80,256]{1,0:T(8,128)(2,1)S(1)} %get-tuple-element.79), channel_id=1, source_target_pairs={{0,2},{1,3},{2,0},{3,1},{4,6},{5,7},{6,4},{7,5},{8,10},{9,11},{10,... | collective-permute-start | bytes 122888 | tf_op jit(solution)/shard_map/ppermute | solution.py:536
  74.0 2.4 %shard_map.169 = bf16[896,640]{1,0:T(8,128)(2,1)} custom-call(bf16[896,128]{1,0:T(8,128)(2,1)S(1)} %shard_map.152.refs_8_.refs_3_.refs_0_, bf16[896,128]{1,0:T(8,128)(2,1)S(1)} %collective-permute-done.16.refs_8_.refs_1_, bf16[896,128]{1,0:T(8,128)(2,1)S(1)} %shard_map.163.refs_2_, bf16[896,128]{1,0:T(8,128)(2,1)S(1)} %collective-permute-done.19.refs_2_.refs_3_, ...), custom_call_target="tpu_custom_call" | custom-call | flops 3000000000 | bytes 1000 | tf_op jit(solution)/shard_map/pallas_call | solution.py:81
  76.4 2.5 %collective-permute-done.24 = bf16[80,256]{1,0:T(8,128)(2,1)S(1)} collective-permute-done((bf16[80,256]{1,0:T(8,128)(2,1)S(1)}, bf16[80,256]{1,0:T(8,128)(2,1)S(1)}, u32[]{:S(2)}, u32[]{:S(2)}) %collective-permute-start.24) | collective-permute-done | bytes 40992 | tf_op jit(solution)/shard_map/ppermute | solution.py:536
  (105 shorter events, 21.1 us)
Async XLA Ops:
  1.6 12.0 %collective-permute-start.1 = (bf16[320,256]{1,0:T(8,128)(2,1)S(1)}, bf16[320,256]{1,0:T(8,128)(2,1)S(1)}, u32[]{:S(2)}, u32[]{:S(2)}) collective-permute-start(bf16[320,256]{1,0:T(8,128)(2,1)S(1)} %constant_dynamic-slice_fusion), channel_id=1, source_target_pairs={{0,2},{1,3},{2,0},{3,1},{4,6},{5,7},{6,4},{7,5},{8,10},{9,11},{10,... | collective-permute-start | bytes 491528 | tf_op jit(solution)/shard_map/ppermute | solution.py:536
  5.7 15.4 %collective-permute-start = (bf16[320,256]{1,0:T(8,128)(2,1)S(1)}, bf16[320,256]{1,0:T(8,128)(2,1)S(1)}, u32[]{:S(2)}, u32[]{:S(2)}) collective-permute-start(bf16[320,256]{1,0:T(8,128)(2,1)S(1)} %constant_dynamic-slice_fusion), channel_id=1, source_target_pairs={{0,1},{1,0},{2,3},{3,2},{4,5},{5,4},{6,7},{7,6},{8,9},{9,8},{10,11... | collective-permute-start | bytes 491528 | tf_op jit(solution)/shard_map/ppermute | solution.py:536
  14.5 6.6 %collective-permute-start.2 = (bf16[320,256]{1,0:T(8,128)(2,1)S(1)}, bf16[320,256]{1,0:T(8,128)(2,1)S(1)}, u32[]{:S(2)}, u32[]{:S(2)}) collective-permute-start(bf16[320,256]{1,0:T(8,128)(2,1)S(1)} %shard_map.147.refs_1_.refs_4_), channel_id=1, source_target_pairs={{0,1},{1,0},{2,3},{3,2},{4,5},{5,4},{6,7},{7,6},{8,9},{9,8},{10,11... | collective-permute-start | bytes 491528 | tf_op jit(solution)/shard_map/ppermute | solution.py:536
  15.1 4.4 %collective-permute-start.3 = (bf16[320,128]{1,0:T(8,128)(2,1)S(1)}, bf16[320,128]{1,0:T(8,128)(2,1)S(1)}, u32[]{:S(2)}, u32[]{:S(2)}) collective-permute-start(bf16[320,128]{1,0:T(8,128)(2,1)S(1)} %copy-done.4), channel_id=1, source_target_pairs={{0,8},{4,12},{8,0},{12,4},{16,24},{20,28},{24,16},{28,20},{1,9},{5... | collective-permute-start | bytes 245768 | tf_op jit(solution)/shard_map/ppermute | solution.py:536
  16.6 4.4 %collective-permute-start.4 = (bf16[320,128]{1,0:T(8,128)(2,1)S(1)}, bf16[320,128]{1,0:T(8,128)(2,1)S(1)}, u32[]{:S(2)}, u32[]{:S(2)}) collective-permute-start(bf16[320,128]{1,0:T(8,128)(2,1)S(1)} %copy-done.4), channel_id=1, source_target_pairs={{0,16},{4,20},{8,24},{12,28},{16,0},{20,4},{24,8},{28,12},{1,17},{... | collective-permute-start | bytes 245768 | tf_op jit(solution)/shard_map/ppermute | solution.py:536
  24.3 5.6 %collective-permute-start.8 = (bf16[320,128]{1,0:T(8,128)(2,1)S(1)}, bf16[320,128]{1,0:T(8,128)(2,1)S(1)}, u32[]{:S(2)}, u32[]{:S(2)}) collective-permute-start(bf16[320,128]{1,0:T(8,128)(2,1)S(1)} %copy-done.5), channel_id=1, source_target_pairs={{0,24},{4,28},{8,16},{12,20},{16,8},{20,12},{24,0},{28,4},{1,25},{... | collective-permute-start | bytes 245768 | tf_op jit(solution)/shard_map/ppermute | solution.py:536
  30.0 5.6 %collective-permute-start.9 = (bf16[4,320,128]{2,1,0:T(8,128)(2,1)S(1)}, bf16[4,320,128]{2,1,0:T(8,128)(2,1)S(1)}, u32[]{:S(2)}, u32[]{:S(2)}) collective-permute-start(bf16[4,320,128]{2,1,0:T(8,128)(2,1)S(1)} %bitcast.31), channel_id=1, source_target_pairs={{0,4},{4,0},{8,12},{12,8},{16,20},{20,16},{24,28},{28,24},{1,5},{5... | collective-permute-start | bytes 983048 | tf_op jit(solution)/shard_map/ppermute | solution.py:536
  30.1 12.3 %collective-permute-start.7 = (bf16[1328,128]{1,0:T(8,128)(2,1)S(1)}, bf16[1328,128]{1,0:T(8,128)(2,1)S(1)}, u32[]{:S(2)}, u32[]{:S(2)}) collective-permute-start(bf16[1328,128]{1,0:T(8,128)(2,1)S(1)} %shard_map.150.refs_4_.refs_0_), channel_id=1, source_target_pairs={{0,8},{4,12},{8,0},{12,4},{16,24},{20,28},{24,16},{28,20},{1,9},{5... | collective-permute-start | bytes 1019912 | tf_op jit(solution)/shard_map/ppermute | solution.py:682
  30.7 11.7 %collective-permute-start.11 = (bf16[1280,128]{1,0:T(8,128)(2,1)S(1)}, bf16[1280,128]{1,0:T(8,128)(2,1)S(1)}, u32[]{:S(2)}, u32[]{:S(2)}) collective-permute-start(bf16[1280,128]{1,0:T(8,128)(2,1)S(1)} %copy-done.16), channel_id=1, source_target_pairs={{0,16},{4,20},{8,24},{12,28},{16,0},{20,4},{24,8},{28,12},{1,17},{... | collective-permute-start | bytes 983048 | tf_op jit(solution)/shard_map/ppermute | solution.py:536
  32.2 10.2 %collective-permute-start.10 = (bf16[160,128]{1,0:T(8,128)(2,1)S(1)}, bf16[160,128]{1,0:T(8,128)(2,1)S(1)}, u32[]{:S(2)}, u32[]{:S(2)}) collective-permute-start(bf16[160,128]{1,0:T(8,128)(2,1)S(1)} %copy-done.17), channel_id=1, source_target_pairs={{0,2},{1,3},{2,0},{3,1},{4,6},{5,7},{6,4},{7,5},{8,10},{9,11},{10,... | collective-permute-start | bytes 122888 | tf_op jit(solution)/shard_map/ppermute | solution.py:536
  38.4 13.4 %collective-permute-start.15 = (bf16[896,128]{1,0:T(8,128)(2,1)S(1)}, bf16[896,128]{1,0:T(8,128)(2,1)S(1)}, u32[]{:S(2)}, u32[]{:S(2)}) collective-permute-start(bf16[896,128]{1,0:T(8,128)(2,1)S(1)} %shard_map.152.refs_8_.refs_3_.refs_0_), channel_id=1, source_target_pairs={{0,2},{1,3},{2,0},{3,1},{4,6},{5,7},{6,4},{7,5},{8,10},{9,11},{10,... | collective-permute-start | bytes 688136 | tf_op jit(solution)/shard_map/ppermute | solution.py:536
  38.5 13.4 %collective-permute-start.16 = (bf16[896,128]{1,0:T(8,128)(2,1)S(1)}, bf16[896,128]{1,0:T(8,128)(2,1)S(1)}, u32[]{:S(2)}, u32[]{:S(2)}) collective-permute-start(bf16[896,128]{1,0:T(8,128)(2,1)S(1)} %shard_map.152.refs_8_.refs_3_.refs_0_), channel_id=1, source_target_pairs={{0,1},{1,0},{2,3},{3,2},{4,5},{5,4},{6,7},{7,6},{8,9},{9,8},{10,11... | collective-permute-start | bytes 688136 | tf_op jit(solution)/shard_map/ppermute | solution.py:536
  42.6 11.1 %collective-permute-start.12 = (bf16[1328,128]{1,0:T(8,128)(2,1)S(1)}, bf16[1328,128]{1,0:T(8,128)(2,1)S(1)}, u32[]{:S(2)}, u32[]{:S(2)}) collective-permute-start(bf16[1328,128]{1,0:T(8,128)(2,1)S(1)} %shard_map.154.refs_8_.refs_2_.refs_4_), channel_id=1, source_target_pairs={{16,0},{20,4},{24,8},{28,12},{17,1},{21,5},{25,9},{29,13},{18,2},{... | collective-permute-start | bytes 1019912 | tf_op jit(solution)/shard_map/ppermute | solution.py:682
  44.1 9.0 %collective-permute-start.14 = (bf16[1280,128]{1,0:T(8,128)(2,1)S(1)}, bf16[1280,128]{1,0:T(8,128)(2,1)S(1)}, u32[]{:S(2)}, u32[]{:S(2)}) collective-permute-start(bf16[1280,128]{1,0:T(8,128)(2,1)S(1)} %shard_map.159), channel_id=1, source_target_pairs={{0,8},{4,12},{8,0},{12,4},{16,24},{20,28},{24,16},{28,20},{1,9},{5... | collective-permute-start | bytes 983048 | tf_op jit(solution)/shard_map/ppermute | solution.py:536
  45.5 6.4 %collective-permute-start.13 = (bf16[160,128]{1,0:T(8,128)(2,1)S(1)}, bf16[160,128]{1,0:T(8,128)(2,1)S(1)}, u32[]{:S(2)}, u32[]{:S(2)}) collective-permute-start(bf16[160,128]{1,0:T(8,128)(2,1)S(1)} %shard_map.157), channel_id=1, source_target_pairs={{0,1},{1,0},{2,3},{3,2},{4,5},{5,4},{6,7},{7,6},{8,9},{9,8},{10,11... | collective-permute-start | bytes 122888 | tf_op jit(solution)/shard_map/ppermute | solution.py:536
  54.2 8.1 %collective-permute-start.19 = (bf16[896,128]{1,0:T(8,128)(2,1)S(1)}, bf16[896,128]{1,0:T(8,128)(2,1)S(1)}, u32[]{:S(2)}, u32[]{:S(2)}) collective-permute-start(bf16[896,128]{1,0:T(8,128)(2,1)S(1)} %shard_map.163.refs_2_), channel_id=1, source_target_pairs={{0,1},{1,0},{2,3},{3,2},{4,5},{5,4},{6,7},{7,6},{8,9},{9,8},{10,11... | collective-permute-start | bytes 688136 | tf_op jit(solution)/shard_map/ppermute | solution.py:536
  55.1 4.6 %collective-permute-start.25 = (bf16[320,128]{1,0:T(8,128)(2,1)S(1)}, bf16[320,128]{1,0:T(8,128)(2,1)S(1)}, u32[]{:S(2)}, u32[]{:S(2)}) collective-permute-start(bf16[320,128]{1,0:T(8,128)(2,1)S(1)} %shard_map.158.refs_5_.refs_0_), channel_id=1, source_target_pairs={{0,16},{4,20},{8,24},{12,28},{16,0},{20,4},{24,8},{28,12},{1,17},{... | collective-permute-start | bytes 245768 | tf_op jit(solution)/shard_map/ppermute | solution.py:536
  57.3 5.0 %collective-permute-start.18 = (bf16[1,128,256]{2,1,0:T(8,128)(2,1)S(1)}, bf16[1,128,256]{2,1,0:T(8,128)(2,1)S(1)}, u32[]{:S(2)}, u32[]{:S(2)}) collective-permute-start(bf16[1,128,256]{2,1,0:T(8,128)(2,1)S(1)} %bitcast.48), channel_id=1, source_target_pairs={{0,8},{4,12},{8,0},{12,4},{16,24},{20,28},{24,16},{28,20},{1,9},{5... | collective-permute-start | bytes 196616 | tf_op jit(solution)/shard_map/ppermute | solution.py:536
  59.7 7.0 %collective-permute-start.26 = (bf16[640,128]{1,0:T(8,128)(2,1)S(1)}, bf16[640,128]{1,0:T(8,128)(2,1)S(1)}, u32[]{:S(2)}, u32[]{:S(2)}) collective-permute-start(bf16[640,128]{1,0:T(8,128)(2,1)S(1)} %shard_map.167), channel_id=1, source_target_pairs={{0,8},{4,12},{8,0},{12,4},{16,24},{20,28},{24,16},{28,20},{1,9},{5... | collective-permute-start | bytes 491528 | tf_op jit(solution)/shard_map/ppermute | solution.py:536
  62.2 5.2 %collective-permute-start.20 = (bf16[2,128,256]{2,1,0:T(8,128)(2,1)S(1)}, bf16[2,128,256]{2,1,0:T(8,128)(2,1)S(1)}, u32[]{:S(2)}, u32[]{:S(2)}) collective-permute-start(bf16[2,128,256]{2,1,0:T(8,128)(2,1)S(1)} %shard_map.164), channel_id=1, source_target_pairs={{0,16},{4,20},{8,24},{12,28},{16,0},{20,4},{24,8},{28,12},{1,17},{... | collective-permute-start | bytes 393224 | tf_op jit(solution)/shard_map/ppermute | solution.py:536
  66.8 7.2 %collective-permute-start.27 = (bf16[4,320,128]{2,1,0:T(8,128)(2,1)S(1)}, bf16[4,320,128]{2,1,0:T(8,128)(2,1)S(1)}, u32[]{:S(2)}, u32[]{:S(2)}) collective-permute-start(bf16[4,320,128]{2,1,0:T(8,128)(2,1)S(1)} %bitcast.46), channel_id=1, source_target_pairs={{0,4},{4,0},{8,12},{12,8},{16,20},{20,16},{24,28},{28,24},{1,5},{5... | collective-permute-start | bytes 983048 | tf_op jit(solution)/shard_map/ppermute | solution.py:536
  69.6 6.8 %collective-permute-start.22 = (bf16[80,256]{1,0:T(8,128)(2,1)S(1)}, bf16[80,256]{1,0:T(8,128)(2,1)S(1)}, u32[]{:S(2)}, u32[]{:S(2)}) collective-permute-start(bf16[80,256]{1,0:T(8,128)(2,1)S(1)} %get-tuple-element.78), channel_id=1, source_target_pairs={{0,1},{1,0},{2,3},{3,2},{4,5},{5,4},{6,7},{7,6},{8,9},{9,8},{10,11... | collective-permute-start | bytes 122888 | tf_op jit(solution)/shard_map/ppermute | solution.py:536
  70.5 5.9 %collective-permute-start.23 = (bf16[80,256]{1,0:T(8,128)(2,1)S(1)}, bf16[80,256]{1,0:T(8,128)(2,1)S(1)}, u32[]{:S(2)}, u32[]{:S(2)}) collective-permute-start(bf16[80,256]{1,0:T(8,128)(2,1)S(1)} %get-tuple-element.79), channel_id=1, source_target_pairs={{0,2},{1,3},{2,0},{3,1},{4,6},{5,7},{6,4},{7,5},{8,10},{9,11},{10,... | collective-permute-start | bytes 122888 | tf_op jit(solution)/shard_map/ppermute | solution.py:536
  73.1 5.8 %collective-permute-start.24 = (bf16[80,256]{1,0:T(8,128)(2,1)S(1)}, bf16[80,256]{1,0:T(8,128)(2,1)S(1)}, u32[]{:S(2)}, u32[]{:S(2)}) collective-permute-start(bf16[80,256]{1,0:T(8,128)(2,1)S(1)} %get-tuple-element.80), channel_id=1, source_target_pairs={{0,3},{1,2},{2,1},{3,0},{4,7},{5,6},{6,5},{7,4},{8,11},{9,10},{10,... | collective-permute-start | bytes 122888 | tf_op jit(solution)/shard_map/ppermute | solution.py:536
  (26 other events, 150.6 us)

commit v12 on v11

--- a/solution.py
+++ b/solution.py
@@ -453,6 +453,13 @@
         out[...] = held[place ^ (s + 1)].astype(BF16)
 
 
+def sum_kernel(*refs):
+    total = refs[0][...]
+    for ref in refs[1:-1]:
+        total = total + ref[...].astype(F32)
+    refs[-1][...] = total
+
+
 def expert_kernel(flip, slots, a_ref, b_ref, gate_ref, up_ref, out_ref, *scratch):
     rows_ref, gate_acc, up_acc = scratch
     step = pl.program_id(0)
@@ -514,7 +521,8 @@
 
 def down_kernel(n_dp, flip, slots, grad_rows, *refs):
     pieces = refs[:n_dp]
-    a_ref, b_ref, out_ref = refs[n_dp:]
+    a_ref, b_ref, out_ref, token_ref = refs[n_dp:]
+    token_ref[...] = jnp.zeros_like(token_ref)
     n_chip = a_ref.shape[0]
     piece = out_ref.shape[1]
     base = a_ref.shape[1] - n_dp * grad_rows
@@ -622,7 +630,7 @@
     w_far = xored(w_half, "dp", n_dp // 2)
     mine = gathered(w_half, "dp", n_dp // 2)[1:]
     mine += gathered(joined([w_far], after=(rows,)), "dp", n_dp // 2)
-    other = swapped(stacked(mine, after=(*rows_in[1:3],), cost=1.0))
+    other = swapped(stacked(mine, after=(*rows_in[1:4],), cost=1.0))
     w_whole, bc, keep, send = call(
         lambda *refs: project_kernel(n_dp - 1, many, *refs),
         [
@@ -654,7 +662,25 @@
     parts = 2
     tiles = width // LANES // parts
     dxs, exs, owns = [], [], []
-    later = (weighted,)
+    held = (weighted, *early, *((over_y,) if n_chip == 4 else ()))
+    arrived = []
+    bit = 1
+    while bit < n_chip:
+        last = bit * 2 == n_chip
+        moves = [(k, k ^ (2 * bit)) for k in range(2 * n_chip) if not last or k & (2 * bit)]
+        arrived.append(lax.ppermute(climbs[-1], "tm", moves))
+        if not last:
+            climbs.append(
+                call(
+                    lambda *refs, bit=bit: climb_kernel(many, size, bit, *refs),
+                    [shape((part + up16(2 * many), half), BF16)],
+                    0.5,
+                    (climbs[-1], arrived[-1]),
+                    after=held,
+                )[0]
+            )
+        bit *= 2
+    later = (climbs[-1],)
     mixed = jnp.zeros((length, length), F32)
     for i in range(parts):
         dx, mixed, ex, own = call(
@@ -670,28 +696,6 @@
             after=later,
             scratch=[pltpu.VMEM((heads, length), F32)],
         )
-        if i == 0:
-            held = (dx, weighted, *early, *((over_y,) if n_chip == 4 else ()))
-            arrived = []
-            bit = 1
-            while bit < n_chip:
-                last = bit * 2 == n_chip
-                moves = [
-                    (k, k ^ (2 * bit)) for k in range(2 * n_chip) if not last or k & (2 * bit)
-                ]
-                arrived.append(lax.ppermute(climbs[-1], "tm", moves))
-                if not last:
-                    climbs.append(
-                        call(
-                            lambda *refs, bit=bit: climb_kernel(many, size, bit, *refs),
-                            [shape((part + up16(2 * many), half), BF16)],
-                            0.5,
-                            (climbs[-1], arrived[-1]),
-                            after=held,
-                        )[0]
-                    )
-                bit *= 2
-            later = (climbs[-1],)
         dxs.append(dx)
         exs.append(ex)
         owns.append(own)
@@ -729,9 +733,7 @@
     r_recv = swapped(r_send)
     if n_chip == 4:
         grads_y = xored(dealt, "tm", 4)
-        grads_x = xored(joined([dealt, grads_y], (r_own,)), "tm", 2)
         rest = dealt.shape[0]
-        grads = [dealt, grads_x, grads_y, grads_x]
         spans = [(0, rest), (0, rest), (0, rest), (rest, 2 * rest)]
     else:
         grads, spans = chips([dealt] * n_chip), None
@@ -740,7 +742,7 @@
     d_bcs = [d_bc.reshape(1, length, columns)]
     while 2 ** (len(d_bcs) - 1) < n_chip:
         level = 2 ** (len(d_bcs) - 1)
-        sent = d_bcs[0] if level == 1 else joined(d_bcs, tuple(fars[1:]))
+        sent = d_bcs[0] if level == 1 else joined(d_bcs)
         d_bcs.append(xored(sent, "tm", 2 * level))
     d_in, d_decay, d_step, token = call(
         lambda *refs: finish_kernel(parts, *refs),
@@ -753,6 +755,7 @@
         3.0,
         (x, bc, cumt, stept, cum, steps, h_in, r_own, r_recv, w_whole, d_bc,
          *dxs, *exs, *owns),
+        after=tuple(fars[1:]),
         scratch=[pltpu.VMEM((width, half), BF16), pltpu.VMEM((heads, half), F32)],
     )
     w_rows = width // (2 * n_chip)
@@ -772,19 +775,21 @@
         (term, swapped(term_send)),
         scratch=[pltpu.VMEM((n_dp, w_rows // n_dp, columns), F32)],
     )
-    w_bc_grad = final[0]
-    for s in range(1, n_dp):
-        w_bc_grad = w_bc_grad + xored(final[s], "dp", s).astype(F32)
-
+    final = list(final[:1]) + [xored(f, "dp", s + 1) for s, f in enumerate(final[1:])]
+
+    if n_chip == 4:
+        grads_x = xored(joined([dealt, grads_y], (sent,)), "tm", 2)
+        grads = [dealt, grads_x, grads_y, grads_x]
     grads_a = stacked(grads, (token,), spans)
     grads_b = swapped(grads_a)
-    w_down_grad = call(
+    w_down_grad, done = call(
         lambda *refs: down_kernel(n_dp, flip, capacity, grad_rows, *refs),
-        [shape((hidden, piece), BF16)],
+        [shape((hidden, piece), BF16), shape((8, LANES), F32)],
         1.0,
         (*near, *fars, grads_a, grads_b),
         after=(final[0],),
-    )[0]
+    )
+    w_bc_grad = call(sum_kernel, [shape(final[0].shape, F32)], 0.1, final, (done,))[0]
     return (d_in[None], d_decay.T[None], d_step.T[None], w_bc_grad, w_down_grad[None])
 
 

time: 79.8 us -> 77.5 us (0.971)
  waiting for transfers between devices: 19.3 us -> 17.7 us
    ppermute x26, waiting for transfers between devices: 18.7 us -> 17.1 us  [xored(): return lax.ppermute(array, axis, [(i, i ^ mask) for i in range(count)])]
    pallas_call x23 -> x24, Pallas kernels: 18.8 us -> 19.5 us  [call(): pl.pallas_call(body, out_shape=outs, in_specs=specs + [pl.BlockSpec(memor...]
  transfers between devices with their start and end apart: 28 -> 28, of which waited for: 12 -> 13; matrix products, arithmetic and copies ran while one was open for 0% -> 0% of each run, Pallas kernels for 25% -> 26%
where the time goes in v12:
time: 77.5 us; the launch traced here: 77.3 us
  starting transfers between devices  33.6 us (43%)
  Pallas kernels  22.3 us (29%)
  waiting for transfers between devices  17.7 us (23%)
  local copies, waits for them, and re-layouts  1.95 us (3%)
  between operations  1.74 us (2%)
    ppermute x26, starting transfers between devices, xored(): return lax.ppermute(array, axis, [(i, i ^ mask) for i in range(count)])  31.6 us
    pallas_call x24, Pallas kernels, call(): pl.pallas_call(body, out_shape=outs, in_specs=specs + [pl.BlockSpec(memor...  19.5 us
    ppermute x26, waiting for transfers between devices, xored(): return lax.ppermute(array, axis, [(i, i ^ mask) for i in range(count)])  17.1 us
    pallas_call x1, Pallas kernels, expert(): pl.pallas_call(body, out_shape=shape(out, BF16), grid=(width // depth,),...  2.75 us
    ppermute x2, starting transfers between devices, per_device(): arrived.append(lax.ppermute(climbs[-1], 'tm', moves))  2.02 us
  transfers between devices with their start and end apart: 28, of which 13 were waited for; matrix products, arithmetic and copies ran while one was open for 0% of the time, Pallas kernels for 26%

profile of v12, /device:TPU:0, one launch (start us, length us, event | category | flops | bytes accessed | tf_op | source)
XLA Modules:
  0.0 77.3 jit_solution(4372576104347254297)
XLA Ops:
  1.6 4.1 %collective-permute-start.1 = (bf16[320,256]{1,0:T(8,128)(2,1)S(1)}, bf16[320,256]{1,0:T(8,128)(2,1)S(1)}, u32[]{:S(2)}, u32[]{:S(2)}) collective-permute-start(bf16[320,256]{1,0:T(8,128)(2,1)S(1)} %constant_dynamic-slice_fusion), channel_id=1, source_target_pairs={{0,2},{1,3},{2,0},{3,1},{4,6},{5,7},{6,4},{7,5},{8,10},{9,11},{10,... | collective-permute-start | bytes 491528 | tf_op jit(solution)/shard_map/ppermute | solution.py:544
  5.7 1.6 %collective-permute-start = (bf16[320,256]{1,0:T(8,128)(2,1)S(1)}, bf16[320,256]{1,0:T(8,128)(2,1)S(1)}, u32[]{:S(2)}, u32[]{:S(2)}) collective-permute-start(bf16[320,256]{1,0:T(8,128)(2,1)S(1)} %constant_dynamic-slice_fusion), channel_id=1, source_target_pairs={{0,1},{1,0},{2,3},{3,2},{4,5},{5,4},{6,7},{7,6},{8,9},{9,8},{10,11... | collective-permute-start | bytes 491528 | tf_op jit(solution)/shard_map/ppermute | solution.py:544
  7.9 5.6 %shard_map.146 = (f32[40,128]{1,0:T(8,128)}, f32[128,128]{1,0:T(8,128)}, f32[128,128]{1,0:T(8,128)}, bf16[2640,128]{1,0:T(8,128)(2,1)}, bf16[128,2560]{1,0:T(8,1...) custom-call(bf16[128,2560]{1,0:T(8,128)(2,1)} %bitcast.36, ...), custom_call_target="tpu_custom_call" | custom-call | flops 6000000000 | bytes 1000 | tf_op jit(solution)/shard_map/pallas_call | solution.py:81
  15.1 1.5 %collective-permute-start.3 = (bf16[320,128]{1,0:T(8,128)(2,1)S(1)}, bf16[320,128]{1,0:T(8,128)(2,1)S(1)}, u32[]{:S(2)}, u32[]{:S(2)}) collective-permute-start(bf16[320,128]{1,0:T(8,128)(2,1)S(1)} %copy-done.4), channel_id=1, source_target_pairs={{0,8},{4,12},{8,0},{12,4},{16,24},{20,28},{24,16},{28,20},{1,9},{5... | collective-permute-start | bytes 245768 | tf_op jit(solution)/shard_map/ppermute | solution.py:544
  16.6 1.5 %collective-permute-start.4 = (bf16[320,128]{1,0:T(8,128)(2,1)S(1)}, bf16[320,128]{1,0:T(8,128)(2,1)S(1)}, u32[]{:S(2)}, u32[]{:S(2)}) collective-permute-start(bf16[320,128]{1,0:T(8,128)(2,1)S(1)} %copy-done.4), channel_id=1, source_target_pairs={{0,16},{4,20},{8,24},{12,28},{16,0},{20,4},{24,8},{28,12},{1,17},{... | collective-permute-start | bytes 245768 | tf_op jit(solution)/shard_map/ppermute | solution.py:544
  19.6 2.4 %collective-permute-done.4.refs_4_.refs_2_ = bf16[320,128]{1,0:T(8,128)(2,1)S(1)} collective-permute-done((bf16[320,128]{1,0:T(8,128)(2,1)S(1)}, bf16[320,128]{1,0:T(8,128)(2,1)S(1)}, u32[]{:S(2)}, u32[]{:S(2)}) %collective-permute-start.4) | collective-permute-done | bytes 81952 | tf_op jit(solution)/shard_map/ppermute | solution.py:544
  21.9 1.5 %collective-permute-done.5.refs_5_.refs_3_ = bf16[320,128]{1,0:T(8,128)(2,1)S(1)} collective-permute-done((bf16[320,128]{1,0:T(8,128)(2,1)S(1)}, bf16[320,128]{1,0:T(8,128)(2,1)S(1)}, u32[]{:S(2)}, u32[]{:S(2)}) %collective-permute-start.5) | collective-permute-done | bytes 81952 | tf_op jit(solution)/shard_map/ppermute | solution.py:544
  23.6 1.9 %collective-permute-done.6.refs_6_ = bf16[3,320,256]{2,1,0:T(8,128)(2,1)S(1)} collective-permute-done((bf16[3,320,256]{2,1,0:T(8,128)(2,1)S(1)}, bf16[3,320,256]{2,1,0:T(8,128)(2,1)S(1)}, u32[]{:S(2)}, u32[]{:S(2)}) %collective-permute-start.6) | collective-permute-done | bytes 491552 | tf_op jit(solution)/shard_map/ppermute | solution.py:544
  26.8 1.5 %collective-permute-done.7.refs_1_.refs_3_ = bf16[1328,128]{1,0:T(8,128)(2,1)S(1)} collective-permute-done((bf16[1328,128]{1,0:T(8,128)(2,1)S(1)}, bf16[1328,128]{1,0:T(8,128)(2,1)S(1)}, u32[]{:S(2)}, u32[]{:S(2)}) %collective-permute-start.7) | collective-permute-done | bytes 340000 | tf_op jit(solution)/shard_map/ppermute | solution.py:544
  29.9 3.4 %collective-permute-start.10 = (bf16[160,128]{1,0:T(8,128)(2,1)S(1)}, bf16[160,128]{1,0:T(8,128)(2,1)S(1)}, u32[]{:S(2)}, u32[]{:S(2)}) collective-permute-start(bf16[160,128]{1,0:T(8,128)(2,1)S(1)} %copy-done.17), channel_id=1, source_target_pairs={{0,2},{1,3},{2,0},{3,1},{4,6},{5,7},{6,4},{7,5},{8,10},{9,11},{10,... | collective-permute-start | bytes 122888 | tf_op jit(solution)/shard_map/ppermute | solution.py:544
  33.4 2.8 %shard_map.152.refs_2_.refs_0_ = bf16[896,128]{1,0:T(8,128)(2,1)S(1)} custom-call(bf16[4,320,128]{2,1,0:T(8,128)(2,1)S(1)} %bitcast.32, bf16[4,320,128]{2,1,0:T(8,128)(2,1)S(1)} %collective-permute-done.9.refs_1_, bf16[2560,896]{1,0:T(8,128)(2,1)S(1)} %bitcast.27, bf16[2560,896]{1,0:T(8,128)(2,1)S(1)} %bitcast.30, ...), custom_call_target="tpu_custom_call" | custom-call | flops 1000000000 | bytes 1000 | tf_op jit(solution)/shard_map/pallas_call | solution.py:503
  37.1 1.8 %collective-permute-done.11.refs_4_.refs_1_.refs_2_ = bf16[1280,128]{1,0:T(8,128)(2,1)S(1)} collective-permute-done((bf16[1280,128]{1,0:T(8,128)(2,1)S(1)}, bf16[1280,128]{1,0:T(8,128)(2,1)S(1)}, u32[]{:S(2)}, u32[]{:S(2)}) %collective-permute-start.11) | collective-permute-done | bytes 327712 | tf_op jit(solution)/shard_map/ppermute | solution.py:544
  39.1 1.5 %collective-permute-start.12 = (bf16[1328,128]{1,0:T(8,128)(2,1)S(1)}, bf16[1328,128]{1,0:T(8,128)(2,1)S(1)}, u32[]{:S(2)}, u32[]{:S(2)}) collective-permute-start(bf16[1328,128]{1,0:T(8,128)(2,1)S(1)} %shard_map.153.refs_8_.refs_2_.refs_4_), channel_id=1, source_target_pairs={{16,0},{20,4},{24,8},{28,12},{17,1},{21,5},{25,9},{29,13},{18,2},{... | collective-permute-start | bytes 1019912 | tf_op jit(solution)/shard_map/ppermute | solution.py:671
  40.7 1.6 %collective-permute-start.14 = (bf16[1280,128]{1,0:T(8,128)(2,1)S(1)}, bf16[1280,128]{1,0:T(8,128)(2,1)S(1)}, u32[]{:S(2)}, u32[]{:S(2)}) collective-permute-start(bf16[1280,128]{1,0:T(8,128)(2,1)S(1)} %shard_map.159), channel_id=1, source_target_pairs={{0,8},{4,12},{8,0},{12,4},{16,24},{20,28},{24,16},{28,20},{1,9},{5... | collective-permute-start | bytes 983048 | tf_op jit(solution)/shard_map/ppermute | solution.py:544
  43.8 2.6 %shard_map.154 = (f32[128,1280]{1,0:T(8,128)S(1)}, f32[128,128]{1,0:T(8,128)S(1)}, f32[20,128]{1,0:T(8,128)S(1)}, f32[20,128]{1,0:T(8,128)S(1)}) custom-call(bf16[128,2560]{1,0:T(8,128)(2,1)S(1)} %bitcast.38, bf16[128,2560]{1,0:T(8,128)(2,1)S(1)} %bitcast.34, bf16[128,256]{1,0:T(8,128)(2,1)S(1)} %get-tuple-element.47.refs_2_.refs_1_, ...), custom_call_target="tpu_custom_call" | custom-call | flops 2100000000 | bytes 1000 | tf_op jit(solution)/shard_map/pallas_call | solution.py:81
  46.4 2.6 %shard_map.155 = (f32[128,1280]{1,0:T(8,128)S(1)}, f32[128,128]{1,0:T(8,128)S(1)}, f32[20,128]{1,0:T(8,128)S(1)}, f32[20,128]{1,0:T(8,128)S(1)}) custom-call(bf16[128,2560]{1,0:T(8,128)(2,1)S(1)} %bitcast.39, bf16[128,2560]{1,0:T(8,128)(2,1)S(1)} %bitcast.35, bf16[128,256]{1,0:T(8,128)(2,1)S(1)} %get-tuple-element.47.refs_2_.refs_1_, ...), custom_call_target="tpu_custom_call" | custom-call | flops 2100000000 | bytes 1000 | tf_op jit(solution)/shard_map/pallas_call | solution.py:81
  50.9 1.5 %collective-permute-start.18 = (bf16[896,128]{1,0:T(8,128)(2,1)S(1)}, bf16[896,128]{1,0:T(8,128)(2,1)S(1)}, u32[]{:S(2)}, u32[]{:S(2)}) collective-permute-start(bf16[896,128]{1,0:T(8,128)(2,1)S(1)} %shard_map.162.refs_2_), channel_id=1, source_target_pairs={{0,1},{1,0},{2,3},{3,2},{4,5},{5,4},{6,7},{7,6},{8,9},{9,8},{10,11... | collective-permute-start | bytes 688136 | tf_op jit(solution)/shard_map/ppermute | solution.py:544
  54.1 1.8 %collective-permute-start.25 = (bf16[320,128]{1,0:T(8,128)(2,1)S(1)}, bf16[320,128]{1,0:T(8,128)(2,1)S(1)}, u32[]{:S(2)}, u32[]{:S(2)}) collective-permute-start(bf16[320,128]{1,0:T(8,128)(2,1)S(1)} %shard_map.158.refs_5_.refs_0_), channel_id=1, source_target_pairs={{0,16},{4,20},{8,24},{12,28},{16,0},{20,4},{24,8},{28,12},{1,17},{... | collective-permute-start | bytes 245768 | tf_op jit(solution)/shard_map/ppermute | solution.py:544
  57.2 1.9 %collective-permute-start.20 = (bf16[2,128,256]{2,1,0:T(8,128)(2,1)S(1)}, bf16[2,128,256]{2,1,0:T(8,128)(2,1)S(1)}, u32[]{:S(2)}, u32[]{:S(2)}) collective-permute-start(bf16[2,128,256]{2,1,0:T(8,128)(2,1)S(1)} %shard_map.164.refs_2_), channel_id=1, source_target_pairs={{0,16},{4,20},{8,24},{12,28},{16,0},{20,4},{24,8},{28,12},{1,17},{... | collective-permute-start | bytes 393224 | tf_op jit(solution)/shard_map/ppermute | solution.py:544
  60.3 2.7 %shard_map.163 = (bf16[128,2560]{1,0:T(8,128)(2,1)}, f32[40,128]{1,0:T(8,128)}, f32[40,128]{1,0:T(8,128)}, f32[8,128]{1,0:T(8,128)S(1)}) custom-call(bf16[128,2560]{1,0:T(8,128)(2,1)S(1)} %bitcast.40, bf16[128,256]{1,0:T(8,128)(2,1)S(1)} %get-tuple-element.47.refs_2_.refs_1_, f32[40,128]{1,0:T(8,128)S(1)} %copy-done.15, f32[40,128]{1,0:T(8,128)S(1)} %bitcast.52, ...), custom_call_target="tpu_custom_call" | custom-call | flops 8999999488 | bytes 1000 | tf_op jit(solution)/shard_map/pallas_call | solution.py:81
  66.8 1.6 %collective-permute-start.22 = (bf16[80,256]{1,0:T(8,128)(2,1)S(1)}, bf16[80,256]{1,0:T(8,128)(2,1)S(1)}, u32[]{:S(2)}, u32[]{:S(2)}) collective-permute-start(bf16[80,256]{1,0:T(8,128)(2,1)S(1)} %get-tuple-element.80), channel_id=1, source_target_pairs={{0,1},{1,0},{2,3},{3,2},{4,5},{5,4},{6,7},{7,6},{8,9},{9,8},{10,11... | collective-permute-start | bytes 122888 | tf_op jit(solution)/shard_map/ppermute | solution.py:544
  68.4 2.4 %collective-permute-start.23 = (bf16[80,256]{1,0:T(8,128)(2,1)S(1)}, bf16[80,256]{1,0:T(8,128)(2,1)S(1)}, u32[]{:S(2)}, u32[]{:S(2)}) collective-permute-start(bf16[80,256]{1,0:T(8,128)(2,1)S(1)} %get-tuple-element.81), channel_id=1, source_target_pairs={{0,2},{1,3},{2,0},{3,1},{4,6},{5,7},{6,4},{7,5},{8,10},{9,11},{10,... | collective-permute-start | bytes 122888 | tf_op jit(solution)/shard_map/ppermute | solution.py:544
  71.8 2.4 %shard_map.169 = (bf16[896,640]{1,0:T(8,128)(2,1)}, f32[8,128]{1,0:T(8,128)S(1)}) custom-call(bf16[896,128]{1,0:T(8,128)(2,1)S(1)} %shard_map.152.refs_2_.refs_0_, bf16[896,128]{1,0:T(8,128)(2,1)S(1)} %collective-permute-done.16.refs_8_.refs_1_, bf16[896,128]{1,0:T(8,128)(2,1)S(1)} %shard_map.162.refs_2_, ...), custom_call_target="tpu_custom_call" | custom-call | flops 3000000000 | bytes 1000 | tf_op jit(solution)/shard_map/pallas_call | solution.py:81
  74.1 2.5 %collective-permute-done.24.refs_3_ = bf16[80,256]{1,0:T(8,128)(2,1)S(1)} collective-permute-done((bf16[80,256]{1,0:T(8,128)(2,1)S(1)}, bf16[80,256]{1,0:T(8,128)(2,1)S(1)}, u32[]{:S(2)}, u32[]{:S(2)}) %collective-permute-start.24) | collective-permute-done | bytes 40992 | tf_op jit(solution)/shard_map/ppermute | solution.py:544
  (105 shorter events, 21.1 us)
Async XLA Ops:
  1.6 12.0 %collective-permute-start.1 = (bf16[320,256]{1,0:T(8,128)(2,1)S(1)}, bf16[320,256]{1,0:T(8,128)(2,1)S(1)}, u32[]{:S(2)}, u32[]{:S(2)}) collective-permute-start(bf16[320,256]{1,0:T(8,128)(2,1)S(1)} %constant_dynamic-slice_fusion), channel_id=1, source_target_pairs={{0,2},{1,3},{2,0},{3,1},{4,6},{5,7},{6,4},{7,5},{8,10},{9,11},{10,... | collective-permute-start | bytes 491528 | tf_op jit(solution)/shard_map/ppermute | solution.py:544
  5.7 17.8 %collective-permute-start = (bf16[320,256]{1,0:T(8,128)(2,1)S(1)}, bf16[320,256]{1,0:T(8,128)(2,1)S(1)}, u32[]{:S(2)}, u32[]{:S(2)}) collective-permute-start(bf16[320,256]{1,0:T(8,128)(2,1)S(1)} %constant_dynamic-slice_fusion), channel_id=1, source_target_pairs={{0,1},{1,0},{2,3},{3,2},{4,5},{5,4},{6,7},{7,6},{8,9},{9,8},{10,11... | collective-permute-start | bytes 491528 | tf_op jit(solution)/shard_map/ppermute | solution.py:544
  14.5 9.0 %collective-permute-start.2 = (bf16[320,256]{1,0:T(8,128)(2,1)S(1)}, bf16[320,256]{1,0:T(8,128)(2,1)S(1)}, u32[]{:S(2)}, u32[]{:S(2)}) collective-permute-start(bf16[320,256]{1,0:T(8,128)(2,1)S(1)} %shard_map.147.refs_1_.refs_4_), channel_id=1, source_target_pairs={{0,1},{1,0},{2,3},{3,2},{4,5},{5,4},{6,7},{7,6},{8,9},{9,8},{10,11... | collective-permute-start | bytes 491528 | tf_op jit(solution)/shard_map/ppermute | solution.py:544
  15.1 4.4 %collective-permute-start.3 = (bf16[320,128]{1,0:T(8,128)(2,1)S(1)}, bf16[320,128]{1,0:T(8,128)(2,1)S(1)}, u32[]{:S(2)}, u32[]{:S(2)}) collective-permute-start(bf16[320,128]{1,0:T(8,128)(2,1)S(1)} %copy-done.4), channel_id=1, source_target_pairs={{0,8},{4,12},{8,0},{12,4},{16,24},{20,28},{24,16},{28,20},{1,9},{5... | collective-permute-start | bytes 245768 | tf_op jit(solution)/shard_map/ppermute | solution.py:544
  16.6 5.3 %collective-permute-start.4 = (bf16[320,128]{1,0:T(8,128)(2,1)S(1)}, bf16[320,128]{1,0:T(8,128)(2,1)S(1)}, u32[]{:S(2)}, u32[]{:S(2)}) collective-permute-start(bf16[320,128]{1,0:T(8,128)(2,1)S(1)} %copy-done.4), channel_id=1, source_target_pairs={{0,16},{4,20},{8,24},{12,28},{16,0},{20,4},{24,8},{28,12},{1,17},{... | collective-permute-start | bytes 245768 | tf_op jit(solution)/shard_map/ppermute | solution.py:544
  18.1 5.3 %collective-permute-start.5 = (bf16[320,128]{1,0:T(8,128)(2,1)S(1)}, bf16[320,128]{1,0:T(8,128)(2,1)S(1)}, u32[]{:S(2)}, u32[]{:S(2)}) collective-permute-start(bf16[320,128]{1,0:T(8,128)(2,1)S(1)} %copy-done.4), channel_id=1, source_target_pairs={{0,24},{4,28},{8,16},{12,20},{16,8},{20,12},{24,0},{28,4},{1,25},{... | collective-permute-start | bytes 245768 | tf_op jit(solution)/shard_map/ppermute | solution.py:544
  28.5 4.8 %collective-permute-start.9 = (bf16[4,320,128]{2,1,0:T(8,128)(2,1)S(1)}, bf16[4,320,128]{2,1,0:T(8,128)(2,1)S(1)}, u32[]{:S(2)}, u32[]{:S(2)}) collective-permute-start(bf16[4,320,128]{2,1,0:T(8,128)(2,1)S(1)} %bitcast.31), channel_id=1, source_target_pairs={{0,4},{4,0},{8,12},{12,8},{16,20},{20,16},{24,28},{28,24},{1,5},{5... | collective-permute-start | bytes 983048 | tf_op jit(solution)/shard_map/ppermute | solution.py:544
  28.7 10.3 %collective-permute-start.8 = (bf16[1328,128]{1,0:T(8,128)(2,1)S(1)}, bf16[1328,128]{1,0:T(8,128)(2,1)S(1)}, u32[]{:S(2)}, u32[]{:S(2)}) collective-permute-start(bf16[1328,128]{1,0:T(8,128)(2,1)S(1)} %shard_map.150.refs_4_.refs_0_), channel_id=1, source_target_pairs={{0,8},{4,12},{8,0},{12,4},{16,24},{20,28},{24,16},{28,20},{1,9},{5... | collective-permute-start | bytes 1019912 | tf_op jit(solution)/shard_map/ppermute | solution.py:671
  29.3 9.7 %collective-permute-start.11 = (bf16[1280,128]{1,0:T(8,128)(2,1)S(1)}, bf16[1280,128]{1,0:T(8,128)(2,1)S(1)}, u32[]{:S(2)}, u32[]{:S(2)}) collective-permute-start(bf16[1280,128]{1,0:T(8,128)(2,1)S(1)} %copy-done.16), channel_id=1, source_target_pairs={{0,16},{4,20},{8,24},{12,28},{16,0},{20,4},{24,8},{28,12},{1,17},{... | collective-permute-start | bytes 983048 | tf_op jit(solution)/shard_map/ppermute | solution.py:544
  29.9 7.2 %collective-permute-start.10 = (bf16[160,128]{1,0:T(8,128)(2,1)S(1)}, bf16[160,128]{1,0:T(8,128)(2,1)S(1)}, u32[]{:S(2)}, u32[]{:S(2)}) collective-permute-start(bf16[160,128]{1,0:T(8,128)(2,1)S(1)} %copy-done.17), channel_id=1, source_target_pairs={{0,2},{1,3},{2,0},{3,1},{4,6},{5,7},{6,4},{7,5},{8,10},{9,11},{10,... | collective-permute-start | bytes 122888 | tf_op jit(solution)/shard_map/ppermute | solution.py:544
  36.2 13.5 %collective-permute-start.15 = (bf16[896,128]{1,0:T(8,128)(2,1)S(1)}, bf16[896,128]{1,0:T(8,128)(2,1)S(1)}, u32[]{:S(2)}, u32[]{:S(2)}) collective-permute-start(bf16[896,128]{1,0:T(8,128)(2,1)S(1)} %shard_map.152.refs_2_.refs_0_), channel_id=1, source_target_pairs={{0,2},{1,3},{2,0},{3,1},{4,6},{5,7},{6,4},{7,5},{8,10},{9,11},{10,... | collective-permute-start | bytes 688136 | tf_op jit(solution)/shard_map/ppermute | solution.py:544
  36.5 13.2 %collective-permute-start.16 = (bf16[896,128]{1,0:T(8,128)(2,1)S(1)}, bf16[896,128]{1,0:T(8,128)(2,1)S(1)}, u32[]{:S(2)}, u32[]{:S(2)}) collective-permute-start(bf16[896,128]{1,0:T(8,128)(2,1)S(1)} %shard_map.152.refs_2_.refs_0_), channel_id=1, source_target_pairs={{0,1},{1,0},{2,3},{3,2},{4,5},{5,4},{6,7},{7,6},{8,9},{9,8},{10,11... | collective-permute-start | bytes 688136 | tf_op jit(solution)/shard_map/ppermute | solution.py:544
  39.1 11.3 %collective-permute-start.12 = (bf16[1328,128]{1,0:T(8,128)(2,1)S(1)}, bf16[1328,128]{1,0:T(8,128)(2,1)S(1)}, u32[]{:S(2)}, u32[]{:S(2)}) collective-permute-start(bf16[1328,128]{1,0:T(8,128)(2,1)S(1)} %shard_map.153.refs_8_.refs_2_.refs_4_), channel_id=1, source_target_pairs={{16,0},{20,4},{24,8},{28,12},{17,1},{21,5},{25,9},{29,13},{18,2},{... | collective-permute-start | bytes 1019912 | tf_op jit(solution)/shard_map/ppermute | solution.py:671
  40.7 9.2 %collective-permute-start.14 = (bf16[1280,128]{1,0:T(8,128)(2,1)S(1)}, bf16[1280,128]{1,0:T(8,128)(2,1)S(1)}, u32[]{:S(2)}, u32[]{:S(2)}) collective-permute-start(bf16[1280,128]{1,0:T(8,128)(2,1)S(1)} %shard_map.159), channel_id=1, source_target_pairs={{0,8},{4,12},{8,0},{12,4},{16,24},{20,28},{24,16},{28,20},{1,9},{5... | collective-permute-start | bytes 983048 | tf_op jit(solution)/shard_map/ppermute | solution.py:544
  42.2 7.4 %collective-permute-start.13 = (bf16[160,128]{1,0:T(8,128)(2,1)S(1)}, bf16[160,128]{1,0:T(8,128)(2,1)S(1)}, u32[]{:S(2)}, u32[]{:S(2)}) collective-permute-start(bf16[160,128]{1,0:T(8,128)(2,1)S(1)} %shard_map.157), channel_id=1, source_target_pairs={{0,1},{1,0},{2,3},{3,2},{4,5},{5,4},{6,7},{7,6},{8,9},{9,8},{10,11... | collective-permute-start | bytes 122888 | tf_op jit(solution)/shard_map/ppermute | solution.py:544
  50.9 9.4 %collective-permute-start.18 = (bf16[896,128]{1,0:T(8,128)(2,1)S(1)}, bf16[896,128]{1,0:T(8,128)(2,1)S(1)}, u32[]{:S(2)}, u32[]{:S(2)}) collective-permute-start(bf16[896,128]{1,0:T(8,128)(2,1)S(1)} %shard_map.162.refs_2_), channel_id=1, source_target_pairs={{0,1},{1,0},{2,3},{3,2},{4,5},{5,4},{6,7},{7,6},{8,9},{9,8},{10,11... | collective-permute-start | bytes 688136 | tf_op jit(solution)/shard_map/ppermute | solution.py:544
  52.8 4.3 %collective-permute-start.19 = (bf16[1,128,256]{2,1,0:T(8,128)(2,1)S(1)}, bf16[1,128,256]{2,1,0:T(8,128)(2,1)S(1)}, u32[]{:S(2)}, u32[]{:S(2)}) collective-permute-start(bf16[1,128,256]{2,1,0:T(8,128)(2,1)S(1)} %bitcast.48), channel_id=1, source_target_pairs={{0,8},{4,12},{8,0},{12,4},{16,24},{20,28},{24,16},{28,20},{1,9},{5... | collective-permute-start | bytes 196616 | tf_op jit(solution)/shard_map/ppermute | solution.py:544
  54.1 5.0 %collective-permute-start.25 = (bf16[320,128]{1,0:T(8,128)(2,1)S(1)}, bf16[320,128]{1,0:T(8,128)(2,1)S(1)}, u32[]{:S(2)}, u32[]{:S(2)}) collective-permute-start(bf16[320,128]{1,0:T(8,128)(2,1)S(1)} %shard_map.158.refs_5_.refs_0_), channel_id=1, source_target_pairs={{0,16},{4,20},{8,24},{12,28},{16,0},{20,4},{24,8},{28,12},{1,17},{... | collective-permute-start | bytes 245768 | tf_op jit(solution)/shard_map/ppermute | solution.py:544
  57.2 7.4 %collective-permute-start.20 = (bf16[2,128,256]{2,1,0:T(8,128)(2,1)S(1)}, bf16[2,128,256]{2,1,0:T(8,128)(2,1)S(1)}, u32[]{:S(2)}, u32[]{:S(2)}) collective-permute-start(bf16[2,128,256]{2,1,0:T(8,128)(2,1)S(1)} %shard_map.164.refs_2_), channel_id=1, source_target_pairs={{0,16},{4,20},{8,24},{12,28},{16,0},{20,4},{24,8},{28,12},{1,17},{... | collective-permute-start | bytes 393224 | tf_op jit(solution)/shard_map/ppermute | solution.py:544
  59.1 5.4 %collective-permute-start.26 = (bf16[640,128]{1,0:T(8,128)(2,1)S(1)}, bf16[640,128]{1,0:T(8,128)(2,1)S(1)}, u32[]{:S(2)}, u32[]{:S(2)}) collective-permute-start(bf16[640,128]{1,0:T(8,128)(2,1)S(1)} %shard_map.167), channel_id=1, source_target_pairs={{0,8},{4,12},{8,0},{12,4},{16,24},{20,28},{24,16},{28,20},{1,9},{5... | collective-permute-start | bytes 491528 | tf_op jit(solution)/shard_map/ppermute | solution.py:544
  64.5 7.3 %collective-permute-start.27 = (bf16[4,320,128]{2,1,0:T(8,128)(2,1)S(1)}, bf16[4,320,128]{2,1,0:T(8,128)(2,1)S(1)}, u32[]{:S(2)}, u32[]{:S(2)}) collective-permute-start(bf16[4,320,128]{2,1,0:T(8,128)(2,1)S(1)} %bitcast.46), channel_id=1, source_target_pairs={{0,4},{4,0},{8,12},{12,8},{16,20},{20,16},{24,28},{28,24},{1,5},{5... | collective-permute-start | bytes 983048 | tf_op jit(solution)/shard_map/ppermute | solution.py:544
  66.8 7.3 %collective-permute-start.22 = (bf16[80,256]{1,0:T(8,128)(2,1)S(1)}, bf16[80,256]{1,0:T(8,128)(2,1)S(1)}, u32[]{:S(2)}, u32[]{:S(2)}) collective-permute-start(bf16[80,256]{1,0:T(8,128)(2,1)S(1)} %get-tuple-element.80), channel_id=1, source_target_pairs={{0,1},{1,0},{2,3},{3,2},{4,5},{5,4},{6,7},{7,6},{8,9},{9,8},{10,11... | collective-permute-start | bytes 122888 | tf_op jit(solution)/shard_map/ppermute | solution.py:544
  68.4 5.7 %collective-permute-start.23 = (bf16[80,256]{1,0:T(8,128)(2,1)S(1)}, bf16[80,256]{1,0:T(8,128)(2,1)S(1)}, u32[]{:S(2)}, u32[]{:S(2)}) collective-permute-start(bf16[80,256]{1,0:T(8,128)(2,1)S(1)} %get-tuple-element.81), channel_id=1, source_target_pairs={{0,2},{1,3},{2,0},{3,1},{4,6},{5,7},{6,4},{7,5},{8,10},{9,11},{10,... | collective-permute-start | bytes 122888 | tf_op jit(solution)/shard_map/ppermute | solution.py:544
  70.8 5.8 %collective-permute-start.24 = (bf16[80,256]{1,0:T(8,128)(2,1)S(1)}, bf16[80,256]{1,0:T(8,128)(2,1)S(1)}, u32[]{:S(2)}, u32[]{:S(2)}) collective-permute-start(bf16[80,256]{1,0:T(8,128)(2,1)S(1)} %get-tuple-element.82), channel_id=1, source_target_pairs={{0,3},{1,2},{2,1},{3,0},{4,7},{5,6},{6,5},{7,4},{8,11},{9,10},{10,... | collective-permute-start | bytes 122888 | tf_op jit(solution)/shard_map/ppermute | solution.py:544
  (26 other events, 148.3 us)

commit v13 on v12

--- a/solution.py
+++ b/solution.py
@@ -138,25 +138,37 @@
 
 
 def prep_kernel(
-    n_deals, x_ref, dy_ref, ldt_ref, stept_ref, h_ref, slot_ref, count_ref, gate_ref,
-    cumt_ref, cum_ref, step_ref, dyt_ref, xs_ref, carried_ref, rows_ref, *rest,
+    n_deals, x_ref, dy_ref, ldt_ref, stept_ref, slot_ref, count_ref, gate_ref,
+    cumt_ref, cum_ref, dyt_ref, rows_ref, *rest,
 ):
-    outs, xt_ref, held_ref = rest[n_deals:-2], rest[-2], rest[-1]
     length, width = x_ref.shape
     heads = ldt_ref.shape[0]
     size = width // heads
-    _, chip, n_chip = core_and_chip()
-    picked(x_ref, dy_ref, slot_ref, count_ref, gate_ref, rows_ref, (*rest[:n_deals], held_ref))
-    pad = jnp.zeros((LANES - heads, length), F32)
+    picked(x_ref, dy_ref, slot_ref, count_ref, gate_ref, rows_ref, rest)
     cumt = dot(ldt_ref[...], triangle(length, lambda a, b: a <= b), 1, 0, HI)
     cumt_ref[...] = cumt
-    cum = jnp.concatenate([cumt, pad], axis=0).T
-    step = jnp.concatenate([stept_ref[...], pad], axis=0).T
-    cum_ref[...] = cum
-    step_ref[...] = step
-    start = jnp.exp(cum)
-    into_end = jnp.exp(cum[length - 1 : length] - cum) * step
-    table = jnp.concatenate([halves(start), halves(into_end)], axis=0)
+    pad = jnp.zeros((LANES - heads, length), F32)
+    cum_ref[...] = jnp.concatenate([cumt - jnp.log(stept_ref[...]), pad], axis=0).T
+    start = jnp.exp(jnp.concatenate([cumt, pad], axis=0).T)
+    table = halves(start)
+    for j in range(width // LANES):
+        span = slice(j * LANES, (j + 1) * LANES)
+        dys = dy_ref[:, span].astype(F32) * dot(table, to_lanes(j, size), 1, 0)
+        dyt_ref[span, :] = dys.T.astype(BF16)
+    decay = jnp.broadcast_to(jnp.exp(cumt[:, length - 1 : length]), (heads, LANES))
+    dyt_ref[width : width + 2 * heads, :] = jnp.concatenate(high_low(decay), axis=0).astype(BF16)
+
+
+def scale_kernel(x_ref, dy_ref, h_ref, cumt_ref, cum_ref, xs_ref, carried_ref, token_ref, *rest):
+    outs, xt_ref = rest[:-1], rest[-1]
+    length, width = x_ref.shape
+    heads = cumt_ref.shape[0]
+    size = width // heads
+    _, chip, n_chip = core_and_chip()
+    pad = jnp.zeros((LANES - heads, length), F32)
+    cum = jnp.concatenate([cumt_ref[...], pad], axis=0).T
+    into_end = jnp.exp(cum[length - 1 : length] - cum_ref[...])
+    table = jnp.concatenate([halves(jnp.exp(cum)), halves(into_end)], axis=0)
     carried = jnp.zeros(carried_ref.shape, F32)
     for j in range(width // LANES):
         span = slice(j * LANES, (j + 1) * LANES)
@@ -164,12 +176,10 @@
         x_f = x_ref[:, span].astype(F32)
         xt_ref[span, :] = x_f.T.astype(BF16)
         xs_ref[:, span] = (x_f * scale[length:]).astype(BF16)
-        dys = dy_ref[:, span].astype(F32) * scale[:length]
-        dyt_ref[span, :] = dys.T.astype(BF16)
-        carried = carried + dot(dys.astype(BF16), h_ref[span, :], 1, 0)
+        dys = (dy_ref[:, span].astype(F32) * scale[:length]).astype(BF16)
+        carried = carried + dot(dys, h_ref[span, :], 1, 0)
     carried_ref[...] = carried
-    decay = jnp.broadcast_to(jnp.exp(cumt[:, length - 1 : length]), (heads, LANES))
-    dyt_ref[width : width + 2 * heads, :] = jnp.concatenate(high_low(decay), axis=0).astype(BF16)
+    token_ref[...] = jnp.zeros_like(token_ref)
     block = width // n_chip
     s = 0
     for out in outs:
@@ -310,7 +320,7 @@
 
 
 def intra_kernel(
-    first, many, x_ref, dy_ref, bc_ref, cumt_ref, cum_ref, step_ref, h_ref, before_ref,
+    first, many, x_ref, dy_ref, bc_ref, cumt_ref, cum_ref, h_ref, before_ref,
     dx_ref, mixed_ref, ex_ref, own_ref, rowm_ref,
 ):
     length, width = x_ref.shape
@@ -333,21 +343,18 @@
         dy_h = jnp.concatenate([dy_p * m for m in lane_bf], axis=0)
         cross = dot(x_p, dy_h, 1, 1)
         kern = []
-        wide = None
         for i in range(per):
             h = j * per + i
             diff = cumt_ref[h : h + 1, :] - cum_ref[:, h : h + 1]
             seg = jnp.exp(jnp.where(upper, diff, -1e30))
-            kern.append((seg * scores).astype(BF16))
-            step = jnp.broadcast_to(step_ref[:, h : h + 1], (length, LANES))
-            wide = step if i == 0 else jnp.where(lane < i * size, wide, step)
-            scaled = seg * cross[:, i * length : (i + 1) * length] * step
-            mixed = mixed + scaled
-            full = scaled * scores
+            part = cross[:, i * length : (i + 1) * length]
+            mixed = mixed + seg * part
+            seg = seg * scores
+            kern.append(seg.astype(BF16))
+            full = seg * part
             rowm_ref[h : h + 1, :] = jnp.sum(full, axis=0, keepdims=True)
             own = jnp.where(lane == h, jnp.sum(full, axis=1, keepdims=True), own)
-        back = dot(jnp.concatenate(kern, axis=1), dy_h, 1, 0)
-        dx_ref[:, out_span] = back * wide
+        dx_ref[:, out_span] = dot(jnp.concatenate(kern, axis=1), dy_h, 1, 0)
         seen = dy_p.astype(F32) * dot(c_rows, h_ref[span, :], 1, 1)
         reach = reach + dot(to_heads(j, heads, size), halves(seen), 1, 1)
     mixed_ref[...] = mixed
@@ -375,10 +382,10 @@
 
 
 def finish_kernel(parts, *refs):
-    (x_ref, bc_ref, cumt_ref, stept_ref, cum_ref, step_ref, h_ref, own_ref, recv_ref,
-     w_ref, dbc_ref) = refs[:11]
-    dx_refs, ex_refs, st_refs = (refs[11 + i * parts : 11 + (i + 1) * parts] for i in range(3))
-    in_ref, decay_ref, grad_ref, token_ref, r_ref, edge_ref = refs[11 + 3 * parts :]
+    (x_ref, bc_ref, cumt_ref, stept_ref, cum_ref, h_ref, own_ref, recv_ref,
+     w_ref, dbc_ref) = refs[:10]
+    dx_refs, ex_refs, st_refs = (refs[10 + i * parts : 10 + (i + 1) * parts] for i in range(3))
+    in_ref, decay_ref, grad_ref, token_ref, r_ref, edge_ref = refs[10 + 3 * parts :]
     token_ref[...] = jnp.zeros_like(token_ref)
     core, _, _ = core_and_chip()
     length, width = x_ref.shape
@@ -387,8 +394,9 @@
     part = width // 2
     r_ref[rows_at(core, part), :] = own_ref[...]
     r_ref[rows_at(1 - core, part), :] = recv_ref[...]
-    cum = cum_ref[...]
-    table = halves(jnp.exp(cum[length - 1 : length] - cum) * step_ref[...])
+    pad = jnp.zeros((LANES - heads, length), F32)
+    total = jnp.concatenate([cumt_ref[...], pad], axis=0).T[length - 1 : length]
+    table = halves(jnp.exp(total - cum_ref[...]))
     seen = jnp.zeros((heads, length), F32)
     b_rows = bc_ref[:, :LANES]
     d_bc = dbc_ref[...]
@@ -596,30 +604,37 @@
     in_rows = width // LANES * capacity
     blocks = [1, 1, 2] if n_chip == 4 else [1] * n_chip
     groups = [2, 2] if n_dp == 4 else [1] * n_dp
-    cumt, cum, steps, dyt, xs, carried, rows, *xt = call(
+    cumt, cum, dyt, rows, *deals = call(
         lambda *refs: prep_kernel(len(groups), *refs),
         [
             shape((heads, length), F32),
             shape((length, LANES), F32),
-            shape((length, LANES), F32),
             shape((width + up16(2 * heads), length), BF16),
-            shape((length, width), BF16),
-            shape((length, half), F32),
+            shape((in_rows, LANES), BF16),
         ]
-        + [shape((in_rows, LANES), BF16)]
-        + [shape((k * grad_rows, LANES), BF16) for k in groups]
+        + [shape((k * grad_rows, LANES), BF16) for k in groups],
+        1.5,
+        (x, dy, ldt, stept, slot_rows[0], slot_counts, slot_gates[0]),
+        scratch=[pltpu.VMEM((n_dp, grad_rows, LANES), BF16)],
+        fetch=(0, 1, 2, 3),
+        limit=60,
+    )
+    rows_in = chips([rows] * n_chip)
+    w_far = xored(w_half, "dp", n_dp // 2)
+    mine = gathered(w_half, "dp", n_dp // 2)[1:]
+    w_copy = joined([w_far], after=(rows,))
+    mine += gathered(w_copy, "dp", n_dp // 2)
+    xs, carried, scaled, *xt = call(
+        scale_kernel,
+        [shape((length, width), BF16), shape((length, half), F32), shape((8, LANES), F32)]
         + [shape((k * width // n_chip, length), BF16) for k in blocks],
-        2.0,
-        (x, dy, ldt, stept, h_in, slot_rows[0], slot_counts, slot_gates[0]),
-        scratch=[
-            pltpu.VMEM((width, length), BF16),
-            pltpu.VMEM((n_dp, grad_rows, LANES), BF16),
-        ],
+        1.5,
+        (x, dy, h_in, cumt, cum),
+        after=(rows,),
+        scratch=[pltpu.VMEM((width, length), BF16)],
         fetch=(0, 1, 2, 3, 4),
         limit=60,
     )
-    rows_in = chips([rows] * n_chip)
-    deals, xt = xt[: len(groups)], xt[len(groups) :]
     if n_dp == 4:
         one = (0, grad_rows), (grad_rows, 2 * grad_rows)
         over_2 = xored(deals[1], "dp", 2)
@@ -627,10 +642,7 @@
     else:
         early = ()
         source, spans = deals[:1] + [xored(d, "dp", s + 1) for s, d in enumerate(deals[1:])], None
-    w_far = xored(w_half, "dp", n_dp // 2)
-    mine = gathered(w_half, "dp", n_dp // 2)[1:]
-    mine += gathered(joined([w_far], after=(rows,)), "dp", n_dp // 2)
-    other = swapped(stacked(mine, after=(*rows_in[1:4],), cost=1.0))
+    other = swapped(stacked(mine, after=(*rows_in[1:4], scaled), cost=1.0))
     w_whole, bc, keep, send = call(
         lambda *refs: project_kernel(n_dp - 1, many, *refs),
         [
@@ -662,12 +674,12 @@
     parts = 2
     tiles = width // LANES // parts
     dxs, exs, owns = [], [], []
-    held = (weighted, *early, *((over_y,) if n_chip == 4 else ()))
+    held = (weighted, *early)
     arrived = []
     bit = 1
     while bit < n_chip:
         last = bit * 2 == n_chip
-        moves = [(k, k ^ (2 * bit)) for k in range(2 * n_chip) if not last or k & (2 * bit)]
+        moves = [(k, k ^ (2 * bit)) for k in range(2 * n_chip)]
         arrived.append(lax.ppermute(climbs[-1], "tm", moves))
         if not last:
             climbs.append(
@@ -692,7 +704,7 @@
                 shape((heads // parts, length), F32),
             ],
             0.7,
-            (x, dy, bc, cumt, cum, steps, h_in, mixed),
+            (x, dy, bc, cumt, cum, h_in, mixed),
             after=later,
             scratch=[pltpu.VMEM((heads, length), F32)],
         )
@@ -753,7 +765,7 @@
             shape((8, LANES), F32),
         ],
         3.0,
-        (x, bc, cumt, stept, cum, steps, h_in, r_own, r_recv, w_whole, d_bc,
+        (x, bc, cumt, stept, cum, h_in, r_own, r_recv, w_whole, d_bc,
          *dxs, *exs, *owns),
         after=tuple(fars[1:]),
         scratch=[pltpu.VMEM((width, half), BF16), pltpu.VMEM((heads, half), F32)],
@@ -780,7 +792,7 @@
     if n_chip == 4:
         grads_x = xored(joined([dealt, grads_y], (sent,)), "tm", 2)
         grads = [dealt, grads_x, grads_y, grads_x]
-    grads_a = stacked(grads, (token,), spans)
+    grads_a = stacked(grads, (term,), spans)
     grads_b = swapped(grads_a)
     w_down_grad, done = call(
         lambda *refs: down_kernel(n_dp, flip, capacity, grad_rows, *refs),

time: 77.5 us -> 74.1 us (0.956)
  starting transfers between devices: 33.6 us -> 30.6 us
  waiting for transfers between devices: 17.7 us -> 15.2 us
  Pallas kernels: 22.3 us -> 23.6 us
    ppermute x26, starting transfers between devices: 31.6 us -> 27.6 us  [xored(): return lax.ppermute(array, axis, [(i, i ^ mask) for i in range(count)])]
    ppermute x26, waiting for transfers between devices: 17.1 us -> 14.9 us  [xored(): return lax.ppermute(array, axis, [(i, i ^ mask) for i in range(count)])]
    pallas_call x24 -> x25, Pallas kernels: 19.5 us -> 20.7 us  [call(): pl.pallas_call(body, out_shape=outs, in_specs=specs + [pl.BlockSpec(memor...]
    ppermute x2, starting transfers between devices: 2.02 us -> 3.09 us  [per_device(): arrived.append(lax.ppermute(climbs[-1], 'tm', moves))]
  transfers between devices with their start and end apart: 28 -> 28, of which waited for: 13 -> 12; matrix products, arithmetic and copies ran while one was open for 0% -> 0% of each run, Pallas kernels for 26% -> 29%
where the time goes in v13:
time: 74.1 us; the launch traced here: 73.8 us
  starting transfers between devices  30.6 us (41%)
  Pallas kernels  23.6 us (32%)
  waiting for transfers between devices  15.2 us (21%)
  local copies, waits for them, and re-layouts  2.64 us (4%)
  between operations  1.71 us (2%)
    ppermute x26, starting transfers between devices, xored(): return lax.ppermute(array, axis, [(i, i ^ mask) for i in range(count)])  27.6 us
    pallas_call x25, Pallas kernels, call(): pl.pallas_call(body, out_shape=outs, in_specs=specs + [pl.BlockSpec(memor...  20.7 us
    ppermute x26, waiting for transfers between devices, xored(): return lax.ppermute(array, axis, [(i, i ^ mask) for i in range(count)])  14.9 us
    ppermute x2, starting transfers between devices, per_device(): arrived.append(lax.ppermute(climbs[-1], 'tm', moves))  3.09 us
    pallas_call x1, Pallas kernels, expert(): pl.pallas_call(body, out_shape=shape(out, BF16), grid=(width // depth,),...  2.93 us
    unnamed x44, local copies, waits for them, and re-layouts  1.7 us
  transfers between devices with their start and end apart: 28, of which 12 were waited for; matrix products, arithmetic and copies ran while one was open for 0% of the time, Pallas kernels for 29%

profile of v13, /device:TPU:0, one launch (start us, length us, event | category | flops | bytes accessed | tf_op | source)
XLA Modules:
  0.0 73.8 jit_solution(8311993546505130306)
XLA Ops:
  1.6 4.1 %collective-permute-start.1 = (bf16[320,256]{1,0:T(8,128)(2,1)S(1)}, bf16[320,256]{1,0:T(8,128)(2,1)S(1)}, u32[]{:S(2)}, u32[]{:S(2)}) collective-permute-start(bf16[320,256]{1,0:T(8,128)(2,1)S(1)} %constant_dynamic-slice_fusion), channel_id=1, source_target_pairs={{0,2},{1,3},{2,0},{3,1},{4,6},{5,7},{6,4},{7,5},{8,10},{9,11},{10,... | collective-permute-start | bytes 491528 | tf_op jit(solution)/shard_map/ppermute | solution.py:552
  5.7 1.6 %collective-permute-start = (bf16[320,256]{1,0:T(8,128)(2,1)S(1)}, bf16[320,256]{1,0:T(8,128)(2,1)S(1)}, u32[]{:S(2)}, u32[]{:S(2)}) collective-permute-start(bf16[320,256]{1,0:T(8,128)(2,1)S(1)} %constant_dynamic-slice_fusion), channel_id=1, source_target_pairs={{0,1},{1,0},{2,3},{3,2},{4,5},{5,4},{6,7},{7,6},{8,9},{9,8},{10,11... | collective-permute-start | bytes 491528 | tf_op jit(solution)/shard_map/ppermute | solution.py:552
  7.9 3.9 %shard_map.146 = (f32[40,128]{1,0:T(8,128)}, f32[128,128]{1,0:T(8,128)}, bf16[2640,128]{1,0:T(8,128)(2,1)}, bf16[320,128]{1,0:T(8,128)(2,1)}, bf16[160,128]{1,0:T(8,128)(2,1)}, /*index=5*/bf16[160,128]{1,0:T(8,128)(2,1)}) custom-call(bf16[128,2560]{1,0:T(8,128)(2,1)} %bitcast.37, bf16[128,2560]{1,0:T(8,128)(2,1)} %bitcast.33, f32[40,128]{1,0:T(8,128)} %bitcast.55, ...), custom_call_target="tpu_custom_call" | custom-call | flops 4499999744 | bytes 1000 | tf_op jit(solution)/shard_map/pallas_call | solution.py:81
  11.9 1.6 %collective-permute-start.3 = (bf16[320,128]{1,0:T(8,128)(2,1)}, bf16[320,128]{1,0:T(8,128)(2,1)S(1)}, u32[]{:S(2)}, u32[]{:S(2)}) collective-permute-start(bf16[320,128]{1,0:T(8,128)(2,1)} %get-tuple-element.46.refs_1_.refs_5_.refs_0_), channel_id=1, source_target_pairs={{0,8},{4,12},{8,0},{12,4},{16,24},{20,28},{24,16},{28,20},{1,9},{5... | collective-permute-start | bytes 245768 | tf_op jit(solution)/shard_map/ppermute | solution.py:552
  13.4 1.5 %collective-permute-start.4 = (bf16[320,128]{1,0:T(8,128)(2,1)}, bf16[320,128]{1,0:T(8,128)(2,1)S(1)}, u32[]{:S(2)}, u32[]{:S(2)}) collective-permute-start(bf16[320,128]{1,0:T(8,128)(2,1)} %get-tuple-element.46.refs_1_.refs_5_.refs_0_), channel_id=1, source_target_pairs={{0,16},{4,20},{8,24},{12,28},{16,0},{20,4},{24,8},{28,12},{1,17},{... | collective-permute-start | bytes 245768 | tf_op jit(solution)/shard_map/ppermute | solution.py:552
  16.9 4.1 %shard_map.148 = (bf16[128,2560]{1,0:T(8,128)(2,1)}, f32[128,128]{1,0:T(8,128)}, f32[8,128]{1,0:T(8,128)}, bf16[640,128]{1,0:T(8,128)(2,1)}, bf16[640,128]{1,0:T(8,128)(2,1)}, /*index=5*/bf16[1280,128]{1,0:T(8,128)(2,1)}) custom-call(bf16[128,2560]{1,0:T(8,128)(2,1)} %bitcast.38, bf16[128,2560]{1,0:T(8,128)(2,1)} %bitcast.34, bf16[2560,128]{1,0:T(8,128)(2,1)} %bitcast.43, ...), custom_call_target="tpu_custom_call" | custom-call | flops 4499999744 | bytes 1000 | tf_op jit(solution)/shard_map/pallas_call | solution.py:81
  22.5 1.9 %collective-permute-done.6.refs_6_ = bf16[3,320,256]{2,1,0:T(8,128)(2,1)S(1)} collective-permute-done((bf16[3,320,256]{2,1,0:T(8,128)(2,1)S(1)}, bf16[3,320,256]{2,1,0:T(8,128)(2,1)S(1)}, u32[]{:S(2)}, u32[]{:S(2)}) %collective-permute-start.6) | collective-permute-done | bytes 491552 | tf_op jit(solution)/shard_map/ppermute | solution.py:552
  25.7 1.5 %collective-permute-done.7.refs_1_.refs_3_ = bf16[1328,128]{1,0:T(8,128)(2,1)S(1)} collective-permute-done((bf16[1328,128]{1,0:T(8,128)(2,1)S(1)}, bf16[1328,128]{1,0:T(8,128)(2,1)S(1)}, u32[]{:S(2)}, u32[]{:S(2)}) %collective-permute-start.7) | collective-permute-done | bytes 340000 | tf_op jit(solution)/shard_map/ppermute | solution.py:552
  27.7 1.5 %collective-permute-start.8 = (bf16[1328,128]{1,0:T(8,128)(2,1)S(1)}, bf16[1328,128]{1,0:T(8,128)(2,1)S(1)}, u32[]{:S(2)}, u32[]{:S(2)}) collective-permute-start(bf16[1328,128]{1,0:T(8,128)(2,1)S(1)} %shard_map.151.refs_4_.refs_0_), channel_id=1, source_target_pairs={{0,8},{4,12},{8,0},{12,4},{16,24},{20,28},{24,16},{28,20},{1,9},{5... | collective-permute-start | bytes 1019912 | tf_op jit(solution)/shard_map/ppermute | solution.py:683
  29.2 1.5 %collective-permute-start.13 = (bf16[1280,128]{1,0:T(8,128)(2,1)S(1)}, bf16[1280,128]{1,0:T(8,128)(2,1)S(1)}, u32[]{:S(2)}, u32[]{:S(2)}) collective-permute-start(bf16[1280,128]{1,0:T(8,128)(2,1)S(1)} %copy-done.16), channel_id=1, source_target_pairs={{0,16},{4,20},{8,24},{12,28},{16,0},{20,4},{24,8},{28,12},{1,17},{... | collective-permute-start | bytes 983048 | tf_op jit(solution)/shard_map/ppermute | solution.py:552
  31.8 2.9 %shard_map.153.refs_2_.refs_0_ = bf16[896,128]{1,0:T(8,128)(2,1)S(1)} custom-call(bf16[4,320,128]{2,1,0:T(8,128)(2,1)S(1)} %bitcast.32, bf16[4,320,128]{2,1,0:T(8,128)(2,1)S(1)} %collective-permute-done.9.refs_1_, bf16[2560,896]{1,0:T(8,128)(2,1)S(1)} %bitcast.27, bf16[2560,896]{1,0:T(8,128)(2,1)S(1)} %bitcast.30, ...), custom_call_target="tpu_custom_call" | custom-call | flops 1000000000 | bytes 1000 | tf_op jit(solution)/shard_map/pallas_call | solution.py:511
  34.8 1.9 %collective-permute-start.15 = (bf16[896,128]{1,0:T(8,128)(2,1)S(1)}, bf16[896,128]{1,0:T(8,128)(2,1)S(1)}, u32[]{:S(2)}, u32[]{:S(2)}) collective-permute-start(bf16[896,128]{1,0:T(8,128)(2,1)S(1)} %shard_map.153.refs_2_.refs_0_), channel_id=1, source_target_pairs={{0,2},{1,3},{2,0},{3,1},{4,6},{5,7},{6,4},{7,5},{8,10},{9,11},{10,... | collective-permute-start | bytes 688136 | tf_op jit(solution)/shard_map/ppermute | solution.py:552
  38.1 1.6 %collective-permute-start.11 = (bf16[1328,128]{1,0:T(8,128)(2,1)S(1)}, bf16[1328,128]{1,0:T(8,128)(2,1)S(1)}, u32[]{:S(2)}, u32[]{:S(2)}) collective-permute-start(bf16[1328,128]{1,0:T(8,128)(2,1)S(1)} %shard_map.154.refs_7_.refs_2_.refs_4_), channel_id=1, source_target_pairs={{0,16},{4,20},{8,24},{12,28},{16,0},{20,4},{24,8},{28,12},{1,17},{... | collective-permute-start | bytes 1019912 | tf_op jit(solution)/shard_map/ppermute | solution.py:683
  39.7 1.6 %collective-permute-start.14 = (bf16[1280,128]{1,0:T(8,128)(2,1)S(1)}, bf16[1280,128]{1,0:T(8,128)(2,1)S(1)}, u32[]{:S(2)}, u32[]{:S(2)}) collective-permute-start(bf16[1280,128]{1,0:T(8,128)(2,1)S(1)} %shard_map.160), channel_id=1, source_target_pairs={{0,8},{4,12},{8,0},{12,4},{16,24},{20,28},{24,16},{28,20},{1,9},{5... | collective-permute-start | bytes 983048 | tf_op jit(solution)/shard_map/ppermute | solution.py:552
  42.2 2.0 %shard_map.155 = (f32[128,1280]{1,0:T(8,128)S(1)}, f32[128,128]{1,0:T(8,128)S(1)}, f32[20,128]{1,0:T(8,128)S(1)}, f32[20,128]{1,0:T(8,128)S(1)}) custom-call(bf16[128,2560]{1,0:T(8,128)(2,1)S(1)} %bitcast.40, bf16[128,2560]{1,0:T(8,128)(2,1)S(1)} %bitcast.35, bf16[128,256]{1,0:T(8,128)(2,1)S(1)} %get-tuple-element.50.refs_2_.refs_1_, ...), custom_call_target="tpu_custom_call" | custom-call | flops 2100000000 | bytes 1000 | tf_op jit(solution)/shard_map/pallas_call | solution.py:81
  44.2 2.0 %shard_map.156 = (f32[128,1280]{1,0:T(8,128)S(1)}, f32[128,128]{1,0:T(8,128)S(1)}, f32[20,128]{1,0:T(8,128)S(1)}, f32[20,128]{1,0:T(8,128)S(1)}) custom-call(bf16[128,2560]{1,0:T(8,128)(2,1)S(1)} %bitcast.41, bf16[128,2560]{1,0:T(8,128)(2,1)S(1)} %bitcast.36, bf16[128,256]{1,0:T(8,128)(2,1)S(1)} %get-tuple-element.50.refs_2_.refs_1_, ...), custom_call_target="tpu_custom_call" | custom-call | flops 2100000000 | bytes 1000 | tf_op jit(solution)/shard_map/pallas_call | solution.py:81
  46.4 2.2 %collective-permute-done.12.refs_1_.refs_3_ = bf16[160,128]{1,0:T(8,128)(2,1)S(1)} collective-permute-done((bf16[160,128]{1,0:T(8,128)(2,1)S(1)}, bf16[160,128]{1,0:T(8,128)(2,1)S(1)}, u32[]{:S(2)}, u32[]{:S(2)}) %collective-permute-start.12) | collective-permute-done | bytes 40992 | tf_op jit(solution)/shard_map/ppermute | solution.py:552
  51.1 1.5 %collective-permute-start.19 = (bf16[1,128,256]{2,1,0:T(8,128)(2,1)S(1)}, bf16[1,128,256]{2,1,0:T(8,128)(2,1)S(1)}, u32[]{:S(2)}, u32[]{:S(2)}) collective-permute-start(bf16[1,128,256]{2,1,0:T(8,128)(2,1)S(1)} %bitcast.50), channel_id=1, source_target_pairs={{0,8},{4,12},{8,0},{12,4},{16,24},{20,28},{24,16},{28,20},{1,9},{5... | collective-permute-start | bytes 196616 | tf_op jit(solution)/shard_map/ppermute | solution.py:552
  53.1 2.3 %collective-permute-done.19.refs_1_.refs_4_ = bf16[1,128,256]{2,1,0:T(8,128)(2,1)S(1)} collective-permute-done((bf16[1,128,256]{2,1,0:T(8,128)(2,1)S(1)}, bf16[1,128,256]{2,1,0:T(8,128)(2,1)S(1)}, u32[]{:S(2)}, u32[]{:S(2)}) %collective-permute-start.19) | collective-permute-done | bytes 65568 | tf_op jit(solution)/shard_map/ppermute | solution.py:552
  57.7 2.6 %shard_map.164 = (bf16[128,2560]{1,0:T(8,128)(2,1)}, f32[40,128]{1,0:T(8,128)}, f32[40,128]{1,0:T(8,128)}, f32[8,128]{1,0:T(8,128)S(1)}) custom-call(bf16[128,2560]{1,0:T(8,128)(2,1)S(1)} %bitcast.42, bf16[128,256]{1,0:T(8,128)(2,1)S(1)} %get-tuple-element.50.refs_2_.refs_1_, f32[40,128]{1,0:T(8,128)S(1)} %copy-done.14, f32[40,128]{1,0:T(8,128)S(1)} %bitcast.54, ...), custom_call_target="tpu_custom_call" | custom-call | flops 8999999488 | bytes 1000 | tf_op jit(solution)/shard_map/pallas_call | solution.py:81
  65.4 2.0 %collective-permute-start.23 = (bf16[80,256]{1,0:T(8,128)(2,1)S(1)}, bf16[80,256]{1,0:T(8,128)(2,1)S(1)}, u32[]{:S(2)}, u32[]{:S(2)}) collective-permute-start(bf16[80,256]{1,0:T(8,128)(2,1)S(1)} %get-tuple-element.81), channel_id=1, source_target_pairs={{0,2},{1,3},{2,0},{3,1},{4,6},{5,7},{6,4},{7,5},{8,10},{9,11},{10,... | collective-permute-start | bytes 122888 | tf_op jit(solution)/shard_map/ppermute | solution.py:552
  67.4 1.5 %collective-permute-start.24 = (bf16[80,256]{1,0:T(8,128)(2,1)S(1)}, bf16[80,256]{1,0:T(8,128)(2,1)S(1)}, u32[]{:S(2)}, u32[]{:S(2)}) collective-permute-start(bf16[80,256]{1,0:T(8,128)(2,1)S(1)} %get-tuple-element.82), channel_id=1, source_target_pairs={{0,3},{1,2},{2,1},{3,0},{4,7},{5,6},{6,5},{7,4},{8,11},{9,10},{10,... | collective-permute-start | bytes 122888 | tf_op jit(solution)/shard_map/ppermute | solution.py:552
  68.9 2.4 %shard_map.170 = (bf16[896,640]{1,0:T(8,128)(2,1)}, f32[8,128]{1,0:T(8,128)S(1)}) custom-call(bf16[896,128]{1,0:T(8,128)(2,1)S(1)} %shard_map.153.refs_2_.refs_0_, bf16[896,128]{1,0:T(8,128)(2,1)S(1)} %collective-permute-done.16.refs_8_.refs_1_, bf16[896,128]{1,0:T(8,128)(2,1)S(1)} %shard_map.163.refs_2_, ...), custom_call_target="tpu_custom_call" | custom-call | flops 3000000000 | bytes 1000 | tf_op jit(solution)/shard_map/pallas_call | solution.py:81
  71.3 1.9 %collective-permute-done.24.refs_3_ = bf16[80,256]{1,0:T(8,128)(2,1)S(1)} collective-permute-done((bf16[80,256]{1,0:T(8,128)(2,1)S(1)}, bf16[80,256]{1,0:T(8,128)(2,1)S(1)}, u32[]{:S(2)}, u32[]{:S(2)}) %collective-permute-start.24) | collective-permute-done | bytes 40992 | tf_op jit(solution)/shard_map/ppermute | solution.py:552
  (106 shorter events, 20.6 us)
Async XLA Ops:
  1.6 13.8 %collective-permute-start.1 = (bf16[320,256]{1,0:T(8,128)(2,1)S(1)}, bf16[320,256]{1,0:T(8,128)(2,1)S(1)}, u32[]{:S(2)}, u32[]{:S(2)}) collective-permute-start(bf16[320,256]{1,0:T(8,128)(2,1)S(1)} %constant_dynamic-slice_fusion), channel_id=1, source_target_pairs={{0,2},{1,3},{2,0},{3,1},{4,6},{5,7},{6,4},{7,5},{8,10},{9,11},{10,... | collective-permute-start | bytes 491528 | tf_op jit(solution)/shard_map/ppermute | solution.py:552
  5.7 15.3 %collective-permute-start = (bf16[320,256]{1,0:T(8,128)(2,1)S(1)}, bf16[320,256]{1,0:T(8,128)(2,1)S(1)}, u32[]{:S(2)}, u32[]{:S(2)}) collective-permute-start(bf16[320,256]{1,0:T(8,128)(2,1)S(1)} %constant_dynamic-slice_fusion), channel_id=1, source_target_pairs={{0,1},{1,0},{2,3},{3,2},{4,5},{5,4},{6,7},{7,6},{8,9},{9,8},{10,11... | collective-permute-start | bytes 491528 | tf_op jit(solution)/shard_map/ppermute | solution.py:552
  11.9 9.1 %collective-permute-start.3 = (bf16[320,128]{1,0:T(8,128)(2,1)}, bf16[320,128]{1,0:T(8,128)(2,1)S(1)}, u32[]{:S(2)}, u32[]{:S(2)}) collective-permute-start(bf16[320,128]{1,0:T(8,128)(2,1)} %get-tuple-element.46.refs_1_.refs_5_.refs_0_), channel_id=1, source_target_pairs={{0,8},{4,12},{8,0},{12,4},{16,24},{20,28},{24,16},{28,20},{1,9},{5... | collective-permute-start | bytes 245768 | tf_op jit(solution)/shard_map/ppermute | solution.py:552
  13.4 7.6 %collective-permute-start.4 = (bf16[320,128]{1,0:T(8,128)(2,1)}, bf16[320,128]{1,0:T(8,128)(2,1)S(1)}, u32[]{:S(2)}, u32[]{:S(2)}) collective-permute-start(bf16[320,128]{1,0:T(8,128)(2,1)} %get-tuple-element.46.refs_1_.refs_5_.refs_0_), channel_id=1, source_target_pairs={{0,16},{4,20},{8,24},{12,28},{16,0},{20,4},{24,8},{28,12},{1,17},{... | collective-permute-start | bytes 245768 | tf_op jit(solution)/shard_map/ppermute | solution.py:552
  14.9 6.1 %collective-permute-start.5 = (bf16[320,128]{1,0:T(8,128)(2,1)}, bf16[320,128]{1,0:T(8,128)(2,1)S(1)}, u32[]{:S(2)}, u32[]{:S(2)}) collective-permute-start(bf16[320,128]{1,0:T(8,128)(2,1)} %get-tuple-element.46.refs_1_.refs_5_.refs_0_), channel_id=1, source_target_pairs={{0,24},{4,28},{8,16},{12,20},{16,8},{20,12},{24,0},{28,4},{1,25},{... | collective-permute-start | bytes 245768 | tf_op jit(solution)/shard_map/ppermute | solution.py:552
  16.3 5.4 %collective-permute-start.2 = (bf16[320,256]{1,0:T(8,128)(2,1)S(1)}, bf16[320,256]{1,0:T(8,128)(2,1)S(1)}, u32[]{:S(2)}, u32[]{:S(2)}) collective-permute-start(bf16[320,256]{1,0:T(8,128)(2,1)S(1)} %shard_map.147.refs_1_.refs_4_), channel_id=1, source_target_pairs={{0,1},{1,0},{2,3},{3,2},{4,5},{5,4},{6,7},{7,6},{8,9},{9,8},{10,11... | collective-permute-start | bytes 491528 | tf_op jit(solution)/shard_map/ppermute | solution.py:552
  27.5 4.3 %collective-permute-start.9 = (bf16[4,320,128]{2,1,0:T(8,128)(2,1)S(1)}, bf16[4,320,128]{2,1,0:T(8,128)(2,1)S(1)}, u32[]{:S(2)}, u32[]{:S(2)}) collective-permute-start(bf16[4,320,128]{2,1,0:T(8,128)(2,1)S(1)} %bitcast.31), channel_id=1, source_target_pairs={{0,4},{4,0},{8,12},{12,8},{16,20},{20,16},{24,28},{28,24},{1,5},{5... | collective-permute-start | bytes 983048 | tf_op jit(solution)/shard_map/ppermute | solution.py:552
  27.7 10.3 %collective-permute-start.8 = (bf16[1328,128]{1,0:T(8,128)(2,1)S(1)}, bf16[1328,128]{1,0:T(8,128)(2,1)S(1)}, u32[]{:S(2)}, u32[]{:S(2)}) collective-permute-start(bf16[1328,128]{1,0:T(8,128)(2,1)S(1)} %shard_map.151.refs_4_.refs_0_), channel_id=1, source_target_pairs={{0,8},{4,12},{8,0},{12,4},{16,24},{20,28},{24,16},{28,20},{1,9},{5... | collective-permute-start | bytes 1019912 | tf_op jit(solution)/shard_map/ppermute | solution.py:683
  29.2 10.5 %collective-permute-start.13 = (bf16[1280,128]{1,0:T(8,128)(2,1)S(1)}, bf16[1280,128]{1,0:T(8,128)(2,1)S(1)}, u32[]{:S(2)}, u32[]{:S(2)}) collective-permute-start(bf16[1280,128]{1,0:T(8,128)(2,1)S(1)} %copy-done.16), channel_id=1, source_target_pairs={{0,16},{4,20},{8,24},{12,28},{16,0},{20,4},{24,8},{28,12},{1,17},{... | collective-permute-start | bytes 983048 | tf_op jit(solution)/shard_map/ppermute | solution.py:552
  30.7 6.9 %collective-permute-start.10 = (bf16[160,128]{1,0:T(8,128)(2,1)S(1)}, bf16[160,128]{1,0:T(8,128)(2,1)S(1)}, u32[]{:S(2)}, u32[]{:S(2)}) collective-permute-start(bf16[160,128]{1,0:T(8,128)(2,1)S(1)} %copy-done.17), channel_id=1, source_target_pairs={{0,2},{1,3},{2,0},{3,1},{4,6},{5,7},{6,4},{7,5},{8,10},{9,11},{10,... | collective-permute-start | bytes 122888 | tf_op jit(solution)/shard_map/ppermute | solution.py:552
  34.8 13.8 %collective-permute-start.15 = (bf16[896,128]{1,0:T(8,128)(2,1)S(1)}, bf16[896,128]{1,0:T(8,128)(2,1)S(1)}, u32[]{:S(2)}, u32[]{:S(2)}) collective-permute-start(bf16[896,128]{1,0:T(8,128)(2,1)S(1)} %shard_map.153.refs_2_.refs_0_), channel_id=1, source_target_pairs={{0,2},{1,3},{2,0},{3,1},{4,6},{5,7},{6,4},{7,5},{8,10},{9,11},{10,... | collective-permute-start | bytes 688136 | tf_op jit(solution)/shard_map/ppermute | solution.py:552
  36.7 11.9 %collective-permute-start.16 = (bf16[896,128]{1,0:T(8,128)(2,1)S(1)}, bf16[896,128]{1,0:T(8,128)(2,1)S(1)}, u32[]{:S(2)}, u32[]{:S(2)}) collective-permute-start(bf16[896,128]{1,0:T(8,128)(2,1)S(1)} %shard_map.153.refs_2_.refs_0_), channel_id=1, source_target_pairs={{0,1},{1,0},{2,3},{3,2},{4,5},{5,4},{6,7},{7,6},{8,9},{9,8},{10,11... | collective-permute-start | bytes 688136 | tf_op jit(solution)/shard_map/ppermute | solution.py:552
  38.1 10.6 %collective-permute-start.11 = (bf16[1328,128]{1,0:T(8,128)(2,1)S(1)}, bf16[1328,128]{1,0:T(8,128)(2,1)S(1)}, u32[]{:S(2)}, u32[]{:S(2)}) collective-permute-start(bf16[1328,128]{1,0:T(8,128)(2,1)S(1)} %shard_map.154.refs_7_.refs_2_.refs_4_), channel_id=1, source_target_pairs={{0,16},{4,20},{8,24},{12,28},{16,0},{20,4},{24,8},{28,12},{1,17},{... | collective-permute-start | bytes 1019912 | tf_op jit(solution)/shard_map/ppermute | solution.py:683
  39.7 9.0 %collective-permute-start.14 = (bf16[1280,128]{1,0:T(8,128)(2,1)S(1)}, bf16[1280,128]{1,0:T(8,128)(2,1)S(1)}, u32[]{:S(2)}, u32[]{:S(2)}) collective-permute-start(bf16[1280,128]{1,0:T(8,128)(2,1)S(1)} %shard_map.160), channel_id=1, source_target_pairs={{0,8},{4,12},{8,0},{12,4},{16,24},{20,28},{24,16},{28,20},{1,9},{5... | collective-permute-start | bytes 983048 | tf_op jit(solution)/shard_map/ppermute | solution.py:552
  41.3 7.4 %collective-permute-start.12 = (bf16[160,128]{1,0:T(8,128)(2,1)S(1)}, bf16[160,128]{1,0:T(8,128)(2,1)S(1)}, u32[]{:S(2)}, u32[]{:S(2)}) collective-permute-start(bf16[160,128]{1,0:T(8,128)(2,1)S(1)} %shard_map.158), channel_id=1, source_target_pairs={{0,1},{1,0},{2,3},{3,2},{4,5},{5,4},{6,7},{7,6},{8,9},{9,8},{10,11... | collective-permute-start | bytes 122888 | tf_op jit(solution)/shard_map/ppermute | solution.py:552
  49.1 8.5 %collective-permute-start.18 = (bf16[896,128]{1,0:T(8,128)(2,1)S(1)}, bf16[896,128]{1,0:T(8,128)(2,1)S(1)}, u32[]{:S(2)}, u32[]{:S(2)}) collective-permute-start(bf16[896,128]{1,0:T(8,128)(2,1)S(1)} %shard_map.163.refs_2_), channel_id=1, source_target_pairs={{0,1},{1,0},{2,3},{3,2},{4,5},{5,4},{6,7},{7,6},{8,9},{9,8},{10,11... | collective-permute-start | bytes 688136 | tf_op jit(solution)/shard_map/ppermute | solution.py:552
  51.1 4.3 %collective-permute-start.19 = (bf16[1,128,256]{2,1,0:T(8,128)(2,1)S(1)}, bf16[1,128,256]{2,1,0:T(8,128)(2,1)S(1)}, u32[]{:S(2)}, u32[]{:S(2)}) collective-permute-start(bf16[1,128,256]{2,1,0:T(8,128)(2,1)S(1)} %bitcast.50), channel_id=1, source_target_pairs={{0,8},{4,12},{8,0},{12,4},{16,24},{20,28},{24,16},{28,20},{1,9},{5... | collective-permute-start | bytes 196616 | tf_op jit(solution)/shard_map/ppermute | solution.py:552
  52.6 4.4 %collective-permute-start.25 = (bf16[320,128]{1,0:T(8,128)(2,1)S(1)}, bf16[320,128]{1,0:T(8,128)(2,1)S(1)}, u32[]{:S(2)}, u32[]{:S(2)}) collective-permute-start(bf16[320,128]{1,0:T(8,128)(2,1)S(1)} %shard_map.159.refs_5_.refs_0_), channel_id=1, source_target_pairs={{0,16},{4,20},{8,24},{12,28},{16,0},{20,4},{24,8},{28,12},{1,17},{... | collective-permute-start | bytes 245768 | tf_op jit(solution)/shard_map/ppermute | solution.py:552
  55.4 5.0 %collective-permute-start.20 = (bf16[2,128,256]{2,1,0:T(8,128)(2,1)S(1)}, bf16[2,128,256]{2,1,0:T(8,128)(2,1)S(1)}, u32[]{:S(2)}, u32[]{:S(2)}) collective-permute-start(bf16[2,128,256]{2,1,0:T(8,128)(2,1)S(1)} %shard_map.165.refs_2_), channel_id=1, source_target_pairs={{0,16},{4,20},{8,24},{12,28},{16,0},{20,4},{24,8},{28,12},{1,17},{... | collective-permute-start | bytes 393224 | tf_op jit(solution)/shard_map/ppermute | solution.py:552
  57.1 5.4 %collective-permute-start.26 = (bf16[640,128]{1,0:T(8,128)(2,1)S(1)}, bf16[640,128]{1,0:T(8,128)(2,1)S(1)}, u32[]{:S(2)}, u32[]{:S(2)}) collective-permute-start(bf16[640,128]{1,0:T(8,128)(2,1)S(1)} %shard_map.168), channel_id=1, source_target_pairs={{0,8},{4,12},{8,0},{12,4},{16,24},{20,28},{24,16},{28,20},{1,9},{5... | collective-permute-start | bytes 491528 | tf_op jit(solution)/shard_map/ppermute | solution.py:552
  62.5 6.4 %collective-permute-start.27 = (bf16[4,320,128]{2,1,0:T(8,128)(2,1)S(1)}, bf16[4,320,128]{2,1,0:T(8,128)(2,1)S(1)}, u32[]{:S(2)}, u32[]{:S(2)}) collective-permute-start(bf16[4,320,128]{2,1,0:T(8,128)(2,1)S(1)} %bitcast.48), channel_id=1, source_target_pairs={{0,4},{4,0},{8,12},{12,8},{16,20},{20,16},{24,28},{28,24},{1,5},{5... | collective-permute-start | bytes 983048 | tf_op jit(solution)/shard_map/ppermute | solution.py:552
  64.5 6.8 %collective-permute-start.22 = (bf16[80,256]{1,0:T(8,128)(2,1)S(1)}, bf16[80,256]{1,0:T(8,128)(2,1)S(1)}, u32[]{:S(2)}, u32[]{:S(2)}) collective-permute-start(bf16[80,256]{1,0:T(8,128)(2,1)S(1)} %get-tuple-element.80), channel_id=1, source_target_pairs={{0,1},{1,0},{2,3},{3,2},{4,5},{5,4},{6,7},{7,6},{8,9},{9,8},{10,11... | collective-permute-start | bytes 122888 | tf_op jit(solution)/shard_map/ppermute | solution.py:552
  65.4 5.9 %collective-permute-start.23 = (bf16[80,256]{1,0:T(8,128)(2,1)S(1)}, bf16[80,256]{1,0:T(8,128)(2,1)S(1)}, u32[]{:S(2)}, u32[]{:S(2)}) collective-permute-start(bf16[80,256]{1,0:T(8,128)(2,1)S(1)} %get-tuple-element.81), channel_id=1, source_target_pairs={{0,2},{1,3},{2,0},{3,1},{4,6},{5,7},{6,4},{7,5},{8,10},{9,11},{10,... | collective-permute-start | bytes 122888 | tf_op jit(solution)/shard_map/ppermute | solution.py:552
  67.4 5.8 %collective-permute-start.24 = (bf16[80,256]{1,0:T(8,128)(2,1)S(1)}, bf16[80,256]{1,0:T(8,128)(2,1)S(1)}, u32[]{:S(2)}, u32[]{:S(2)}) collective-permute-start(bf16[80,256]{1,0:T(8,128)(2,1)S(1)} %get-tuple-element.82), channel_id=1, source_target_pairs={{0,3},{1,2},{2,1},{3,0},{4,7},{5,6},{6,5},{7,4},{8,11},{9,10},{10,... | collective-permute-start | bytes 122888 | tf_op jit(solution)/shard_map/ppermute | solution.py:552
  (26 other events, 113.7 us)

commit v14 on v13

--- a/solution.py
+++ b/solution.py
@@ -529,17 +529,20 @@
 
 def down_kernel(n_dp, flip, slots, grad_rows, *refs):
     pieces = refs[:n_dp]
-    a_ref, b_ref, out_ref, token_ref = refs[n_dp:]
+    g_ref, out_ref, token_ref = refs[n_dp:]
     token_ref[...] = jnp.zeros_like(token_ref)
-    n_chip = a_ref.shape[0]
+    n_chip = g_ref.shape[0]
     piece = out_ref.shape[1]
-    base = a_ref.shape[1] - n_dp * grad_rows
     total = None
     for s in range(n_dp):
         columns = []
         for t in range(grad_rows // slots):
-            row = base + s * grad_rows + t * slots
-            blocks = [r[i, row : row + slots, :] for r in (a_ref, b_ref) for i in range(n_chip)]
+            row = s * grad_rows + t * slots
+            blocks = [
+                g_ref[i, half + row : half + row + slots, :]
+                for half in (0, n_dp * grad_rows)
+                for i in range(n_chip)
+            ]
             columns.append(jnp.concatenate(blocks, axis=0))
         right = jnp.concatenate(columns, axis=1)[:, :piece]
         part = dot(pieces[s][...], right, 1 if flip else 0, 0)
@@ -674,6 +677,10 @@
     parts = 2
     tiles = width // LANES // parts
     dxs, exs, owns = [], [], []
+    if n_dp == 4:
+        over_1 = xored(joined([deals[0], over_2], (weighted,), [one[1], one[1]]), "dp", 1)
+        early += (over_1,)
+        source, spans = [deals[0], over_1, over_2, over_1], [one[0], one[0], one[0], one[1]]
     held = (weighted, *early)
     arrived = []
     bit = 1
@@ -719,11 +726,9 @@
     )
 
     held = (dc,)
-    if n_dp == 4:
-        over_1 = xored(joined([deals[0], over_2], later, [one[1], one[1]]), "dp", 1)
-        source, spans = [deals[0], over_1, over_2, over_1], [one[0], one[0], one[0], one[1]]
     dealt = joined(source, later, spans)
-    held += (dealt,)
+    dealt_all = joined([dealt, swapped(dealt)])
+    held += (dealt_all,)
     if n_chip == 4:
         over_x = xored(joined([xt[1], over_y], later, [(0, x_rows), (x_rows, 2 * x_rows)]), "tm", 2)
         columns_in = [xt[0], over_x, over_y]
@@ -743,19 +748,24 @@
         after=held,
     )
     r_recv = swapped(r_send)
-    if n_chip == 4:
-        grads_y = xored(dealt, "tm", 4)
-        rest = dealt.shape[0]
-        spans = [(0, rest), (0, rest), (0, rest), (rest, 2 * rest)]
-    else:
-        grads, spans = chips([dealt] * n_chip), None
     fars = gathered(joined([far], (r_own,)), "dp", n_dp // 2)
     d_bc = call(db_kernel, [shape((length, columns), BF16)], 0.3, (xs, r_own, r_recv, db, dc))[0]
     d_bcs = [d_bc.reshape(1, length, columns)]
+    if n_chip == 4:
+        grads_y = xored(dealt_all, "tm", 4)
     while 2 ** (len(d_bcs) - 1) < n_chip:
         level = 2 ** (len(d_bcs) - 1)
         sent = d_bcs[0] if level == 1 else joined(d_bcs)
         d_bcs.append(xored(sent, "tm", 2 * level))
+    both = ()
+    if n_chip == 4:
+        both = (joined([dealt_all, grads_y], (sent,)),)
+        grads_x = xored(both[0], "tm", 2)
+        rest = dealt_all.shape[0]
+        grads = [dealt_all, grads_x, grads_y, grads_x]
+        spans = [(0, rest), (0, rest), (0, rest), (rest, 2 * rest)]
+    else:
+        grads, spans = chips([dealt_all] * n_chip), None
     d_in, d_decay, d_step, token = call(
         lambda *refs: finish_kernel(parts, *refs),
         [
@@ -764,10 +774,10 @@
             shape((heads, length), F32),
             shape((8, LANES), F32),
         ],
-        3.0,
+        1.0,
         (x, bc, cumt, stept, cum, h_in, r_own, r_recv, w_whole, d_bc,
          *dxs, *exs, *owns),
-        after=tuple(fars[1:]),
+        after=(*fars[1:], *both),
         scratch=[pltpu.VMEM((width, half), BF16), pltpu.VMEM((heads, half), F32)],
     )
     w_rows = width // (2 * n_chip)
@@ -789,16 +799,12 @@
     )
     final = list(final[:1]) + [xored(f, "dp", s + 1) for s, f in enumerate(final[1:])]
 
-    if n_chip == 4:
-        grads_x = xored(joined([dealt, grads_y], (sent,)), "tm", 2)
-        grads = [dealt, grads_x, grads_y, grads_x]
-    grads_a = stacked(grads, (term,), spans)
-    grads_b = swapped(grads_a)
+    grads = stacked(grads, (term,), spans)
     w_down_grad, done = call(
         lambda *refs: down_kernel(n_dp, flip, capacity, grad_rows, *refs),
         [shape((hidden, piece), BF16), shape((8, LANES), F32)],
         1.0,
-        (*near, *fars, grads_a, grads_b),
+        (*near, *fars, grads),
         after=(final[0],),
     )
     w_bc_grad = call(sum_kernel, [shape(final[0].shape, F32)], 0.1, final, (done,))[0]

time: 74.1 us -> 72.9 us (0.984)
  waiting for transfers between devices: 15.2 us -> 14.4 us
    ppermute x26, starting transfers between devices: 27.6 us -> 26.7 us  [xored(): return lax.ppermute(array, axis, [(i, i ^ mask) for i in range(count)])]
    pallas_call x25 -> x26, Pallas kernels: 20.7 us -> 20.7 us  [call(): pl.pallas_call(body, out_shape=outs, in_specs=specs + [pl.BlockSpec(memor...]
  transfers between devices with their start and end apart: 28 -> 28, of which waited for: 12 -> 10; matrix products, arithmetic and copies ran while one was open for 0% -> 0% of each run, Pallas kernels for 29% -> 29%
where the time goes in v14:
time: 72.9 us; the launch traced here: 72.6 us
  starting transfers between devices  30.3 us (42%)
  Pallas kernels  23.6 us (32%)
  waiting for transfers between devices  14.4 us (20%)
  local copies, waits for them, and re-layouts  2.63 us (4%)
  between operations  1.74 us (2%)
    ppermute x26, starting transfers between devices, xored(): return lax.ppermute(array, axis, [(i, i ^ mask) for i in range(count)])  26.7 us
    pallas_call x26, Pallas kernels, call(): pl.pallas_call(body, out_shape=outs, in_specs=specs + [pl.BlockSpec(memor...  20.7 us
    ppermute x26, waiting for transfers between devices, xored(): return lax.ppermute(array, axis, [(i, i ^ mask) for i in range(count)])  14.4 us
    ppermute x2, starting transfers between devices, per_device(): arrived.append(lax.ppermute(climbs[-1], 'tm', moves))  3.59 us
    pallas_call x1, Pallas kernels, expert(): pl.pallas_call(body, out_shape=shape(out, BF16), grid=(width // depth,),...  2.93 us
    unnamed x44, local copies, waits for them, and re-layouts  1.7 us
  transfers between devices with their start and end apart: 28, of which 10 were waited for; matrix products, arithmetic and copies ran while one was open for 0% of the time, Pallas kernels for 29%

profile of v14, /device:TPU:0, one launch (start us, length us, event | category | flops | bytes accessed | tf_op | source)
XLA Modules:
  0.0 72.6 jit_solution(9524149096513185115)
XLA Ops:
  1.6 4.1 %collective-permute-start.1 = (bf16[320,256]{1,0:T(8,128)(2,1)S(1)}, bf16[320,256]{1,0:T(8,128)(2,1)S(1)}, u32[]{:S(2)}, u32[]{:S(2)}) collective-permute-start(bf16[320,256]{1,0:T(8,128)(2,1)S(1)} %constant_dynamic-slice_fusion), channel_id=1, source_target_pairs={{0,2},{1,3},{2,0},{3,1},{4,6},{5,7},{6,4},{7,5},{8,10},{9,11},{10,... | collective-permute-start | bytes 491528 | tf_op jit(solution)/shard_map/ppermute | solution.py:555
  5.7 1.6 %collective-permute-start = (bf16[320,256]{1,0:T(8,128)(2,1)S(1)}, bf16[320,256]{1,0:T(8,128)(2,1)S(1)}, u32[]{:S(2)}, u32[]{:S(2)}) collective-permute-start(bf16[320,256]{1,0:T(8,128)(2,1)S(1)} %constant_dynamic-slice_fusion), channel_id=1, source_target_pairs={{0,1},{1,0},{2,3},{3,2},{4,5},{5,4},{6,7},{7,6},{8,9},{9,8},{10,11... | collective-permute-start | bytes 491528 | tf_op jit(solution)/shard_map/ppermute | solution.py:555
  7.9 3.9 %shard_map.146 = (f32[40,128]{1,0:T(8,128)}, f32[128,128]{1,0:T(8,128)}, bf16[2640,128]{1,0:T(8,128)(2,1)}, bf16[320,128]{1,0:T(8,128)(2,1)}, bf16[160,128]{1,0:T(8,128)(2,1)}, /*index=5*/bf16[160,128]{1,0:T(8,128)(2,1)}) custom-call(bf16[128,2560]{1,0:T(8,128)(2,1)} %bitcast.37, bf16[128,2560]{1,0:T(8,128)(2,1)} %bitcast.33, f32[40,128]{1,0:T(8,128)} %bitcast.54, ...), custom_call_target="tpu_custom_call" | custom-call | flops 4499999744 | bytes 1000 | tf_op jit(solution)/shard_map/pallas_call | solution.py:81
  11.9 1.6 %collective-permute-start.3 = (bf16[320,128]{1,0:T(8,128)(2,1)}, bf16[320,128]{1,0:T(8,128)(2,1)S(1)}, u32[]{:S(2)}, u32[]{:S(2)}) collective-permute-start(bf16[320,128]{1,0:T(8,128)(2,1)} %get-tuple-element.46.refs_1_.refs_5_.refs_0_), channel_id=1, source_target_pairs={{0,8},{4,12},{8,0},{12,4},{16,24},{20,28},{24,16},{28,20},{1,9},{5... | collective-permute-start | bytes 245768 | tf_op jit(solution)/shard_map/ppermute | solution.py:555
  13.4 1.5 %collective-permute-start.4 = (bf16[320,128]{1,0:T(8,128)(2,1)}, bf16[320,128]{1,0:T(8,128)(2,1)S(1)}, u32[]{:S(2)}, u32[]{:S(2)}) collective-permute-start(bf16[320,128]{1,0:T(8,128)(2,1)} %get-tuple-element.46.refs_1_.refs_5_.refs_0_), channel_id=1, source_target_pairs={{0,16},{4,20},{8,24},{12,28},{16,0},{20,4},{24,8},{28,12},{1,17},{... | collective-permute-start | bytes 245768 | tf_op jit(solution)/shard_map/ppermute | solution.py:555
  16.9 4.1 %shard_map.148 = (bf16[128,2560]{1,0:T(8,128)(2,1)}, f32[128,128]{1,0:T(8,128)}, f32[8,128]{1,0:T(8,128)}, bf16[640,128]{1,0:T(8,128)(2,1)}, bf16[640,128]{1,0:T(8,128)(2,1)}, /*index=5*/bf16[1280,128]{1,0:T(8,128)(2,1)}) custom-call(bf16[128,2560]{1,0:T(8,128)(2,1)} %bitcast.38, bf16[128,2560]{1,0:T(8,128)(2,1)} %bitcast.34, bf16[2560,128]{1,0:T(8,128)(2,1)} %bitcast.43, ...), custom_call_target="tpu_custom_call" | custom-call | flops 4499999744 | bytes 1000 | tf_op jit(solution)/shard_map/pallas_call | solution.py:81
  22.5 1.9 %collective-permute-done.6.refs_6_ = bf16[3,320,256]{2,1,0:T(8,128)(2,1)S(1)} collective-permute-done((bf16[3,320,256]{2,1,0:T(8,128)(2,1)S(1)}, bf16[3,320,256]{2,1,0:T(8,128)(2,1)S(1)}, u32[]{:S(2)}, u32[]{:S(2)}) %collective-permute-start.6) | collective-permute-done | bytes 491552 | tf_op jit(solution)/shard_map/ppermute | solution.py:555
  25.7 1.5 %collective-permute-done.7.refs_1_.refs_3_ = bf16[1328,128]{1,0:T(8,128)(2,1)S(1)} collective-permute-done((bf16[1328,128]{1,0:T(8,128)(2,1)S(1)}, bf16[1328,128]{1,0:T(8,128)(2,1)S(1)}, u32[]{:S(2)}, u32[]{:S(2)}) %collective-permute-start.7) | collective-permute-done | bytes 340000 | tf_op jit(solution)/shard_map/ppermute | solution.py:555
  27.7 1.5 %collective-permute-start.8 = (bf16[1328,128]{1,0:T(8,128)(2,1)S(1)}, bf16[1328,128]{1,0:T(8,128)(2,1)S(1)}, u32[]{:S(2)}, u32[]{:S(2)}) collective-permute-start(bf16[1328,128]{1,0:T(8,128)(2,1)S(1)} %shard_map.151.refs_4_.refs_0_), channel_id=1, source_target_pairs={{0,8},{4,12},{8,0},{12,4},{16,24},{20,28},{24,16},{28,20},{1,9},{5... | collective-permute-start | bytes 1019912 | tf_op jit(solution)/shard_map/ppermute | solution.py:690
  30.3 1.5 %collective-permute-start.14 = (bf16[1280,128]{1,0:T(8,128)(2,1)S(1)}, bf16[1280,128]{1,0:T(8,128)(2,1)S(1)}, u32[]{:S(2)}, u32[]{:S(2)}) collective-permute-start(bf16[1280,128]{1,0:T(8,128)(2,1)S(1)} %copy-done.16), channel_id=1, source_target_pairs={{0,16},{4,20},{8,24},{12,28},{16,0},{20,4},{24,8},{28,12},{1,17},{... | collective-permute-start | bytes 983048 | tf_op jit(solution)/shard_map/ppermute | solution.py:555
  31.9 2.9 %shard_map.153.refs_2_.refs_0_ = bf16[896,128]{1,0:T(8,128)(2,1)S(1)} custom-call(bf16[4,320,128]{2,1,0:T(8,128)(2,1)S(1)} %bitcast.32, bf16[4,320,128]{2,1,0:T(8,128)(2,1)S(1)} %collective-permute-done.9.refs_1_, bf16[2560,896]{1,0:T(8,128)(2,1)S(1)} %bitcast.27, bf16[2560,896]{1,0:T(8,128)(2,1)S(1)} %bitcast.30, ...), custom_call_target="tpu_custom_call" | custom-call | flops 1000000000 | bytes 1000 | tf_op jit(solution)/shard_map/pallas_call | solution.py:511
  34.9 1.8 %collective-permute-start.11 = (bf16[160,128]{1,0:T(8,128)(2,1)S(1)}, bf16[160,128]{1,0:T(8,128)(2,1)S(1)}, u32[]{:S(2)}, u32[]{:S(2)}) collective-permute-start(bf16[160,128]{1,0:T(8,128)(2,1)S(1)} %shard_map.154), channel_id=1, source_target_pairs={{0,1},{1,0},{2,3},{3,2},{4,5},{5,4},{6,7},{7,6},{8,9},{9,8},{10,11... | collective-permute-start | bytes 122888 | tf_op jit(solution)/shard_map/ppermute | solution.py:555
  37.7 1.1 %collective-permute-start.17 = (bf16[896,128]{1,0:T(8,128)(2,1)S(1)}, bf16[896,128]{1,0:T(8,128)(2,1)S(1)}, u32[]{:S(2)}, u32[]{:S(2)}) collective-permute-start(bf16[896,128]{1,0:T(8,128)(2,1)S(1)} %shard_map.153.refs_2_.refs_0_), channel_id=1, source_target_pairs={{0,1},{1,0},{2,3},{3,2},{4,5},{5,4},{6,7},{7,6},{8,9},{9,8},{10,11... | collective-permute-start | bytes 688136 | tf_op jit(solution)/shard_map/ppermute | solution.py:555
  39.1 2.1 %collective-permute-start.12 = (bf16[1328,128]{1,0:T(8,128)(2,1)S(1)}, bf16[1328,128]{1,0:T(8,128)(2,1)S(1)}, u32[]{:S(2)}, u32[]{:S(2)}) collective-permute-start(bf16[1328,128]{1,0:T(8,128)(2,1)S(1)} %shard_map.155.refs_7_.refs_4_.refs_2_), channel_id=1, source_target_pairs={{0,16},{4,20},{8,24},{12,28},{16,0},{20,4},{24,8},{28,12},{1,17},{... | collective-permute-start | bytes 1019912 | tf_op jit(solution)/shard_map/ppermute | solution.py:690
  41.8 2.0 %shard_map.156 = (f32[128,1280]{1,0:T(8,128)S(1)}, f32[128,128]{1,0:T(8,128)S(1)}, f32[20,128]{1,0:T(8,128)S(1)}, f32[20,128]{1,0:T(8,128)S(1)}) custom-call(bf16[128,2560]{1,0:T(8,128)(2,1)S(1)} %bitcast.40, bf16[128,2560]{1,0:T(8,128)(2,1)S(1)} %bitcast.35, bf16[128,256]{1,0:T(8,128)(2,1)S(1)} %get-tuple-element.50.refs_2_.refs_1_, ...), custom_call_target="tpu_custom_call" | custom-call | flops 2100000000 | bytes 1000 | tf_op jit(solution)/shard_map/pallas_call | solution.py:81
  43.7 2.0 %shard_map.157 = (f32[128,1280]{1,0:T(8,128)S(1)}, f32[128,128]{1,0:T(8,128)S(1)}, f32[20,128]{1,0:T(8,128)S(1)}, f32[20,128]{1,0:T(8,128)S(1)}) custom-call(bf16[128,2560]{1,0:T(8,128)(2,1)S(1)} %bitcast.41, bf16[128,2560]{1,0:T(8,128)(2,1)S(1)} %bitcast.36, bf16[128,256]{1,0:T(8,128)(2,1)S(1)} %get-tuple-element.50.refs_2_.refs_1_, ...), custom_call_target="tpu_custom_call" | custom-call | flops 2100000000 | bytes 1000 | tf_op jit(solution)/shard_map/pallas_call | solution.py:81
  46.0 3.1 %collective-permute-done.16.refs_7_.refs_0_ = bf16[896,128]{1,0:T(8,128)(2,1)S(1)} collective-permute-done((bf16[896,128]{1,0:T(8,128)(2,1)S(1)}, bf16[896,128]{1,0:T(8,128)(2,1)S(1)}, u32[]{:S(2)}, u32[]{:S(2)}) %collective-permute-start.16) | collective-permute-done | bytes 229408 | tf_op jit(solution)/shard_map/ppermute | solution.py:555
  50.5 1.7 %collective-permute-start.19 = (bf16[896,128]{1,0:T(8,128)(2,1)S(1)}, bf16[896,128]{1,0:T(8,128)(2,1)S(1)}, u32[]{:S(2)}, u32[]{:S(2)}) collective-permute-start(bf16[896,128]{1,0:T(8,128)(2,1)S(1)} %shard_map.164.refs_2_), channel_id=1, source_target_pairs={{0,1},{1,0},{2,3},{3,2},{4,5},{5,4},{6,7},{7,6},{8,9},{9,8},{10,11... | collective-permute-start | bytes 688136 | tf_op jit(solution)/shard_map/ppermute | solution.py:555
  53.1 3.7 %collective-permute-done.21.refs_1_.refs_4_ = bf16[1,128,256]{2,1,0:T(8,128)(2,1)S(1)} collective-permute-done((bf16[1,128,256]{2,1,0:T(8,128)(2,1)S(1)}, bf16[1,128,256]{2,1,0:T(8,128)(2,1)S(1)}, u32[]{:S(2)}, u32[]{:S(2)}) %collective-permute-start.21) | collective-permute-done | bytes 65568 | tf_op jit(solution)/shard_map/ppermute | solution.py:555
  58.5 2.6 %shard_map.167 = (bf16[128,2560]{1,0:T(8,128)(2,1)}, f32[40,128]{1,0:T(8,128)}, f32[40,128]{1,0:T(8,128)}, f32[8,128]{1,0:T(8,128)S(1)}) custom-call(bf16[128,2560]{1,0:T(8,128)(2,1)S(1)} %bitcast.42, bf16[128,256]{1,0:T(8,128)(2,1)S(1)} %get-tuple-element.50.refs_2_.refs_1_, f32[40,128]{1,0:T(8,128)S(1)} %copy-done.14, f32[40,128]{1,0:T(8,128)S(1)} %bitcast.52, ...), custom_call_target="tpu_custom_call" | custom-call | flops 3000000000 | bytes 1000 | tf_op jit(solution)/shard_map/pallas_call | solution.py:81
  62.6 1.4 %collective-permute-done.23.refs_1_ = bf16[320,256]{1,0:T(8,128)(2,1)S(1)} collective-permute-done((bf16[320,256]{1,0:T(8,128)(2,1)S(1)}, bf16[320,256]{1,0:T(8,128)(2,1)S(1)}, u32[]{:S(2)}, u32[]{:S(2)}) %collective-permute-start.23) | collective-permute-done | bytes 163872 | tf_op jit(solution)/shard_map/ppermute | solution.py:555
  64.6 1.6 %collective-permute-start.25 = (bf16[80,256]{1,0:T(8,128)(2,1)S(1)}, bf16[80,256]{1,0:T(8,128)(2,1)S(1)}, u32[]{:S(2)}, u32[]{:S(2)}) collective-permute-start(bf16[80,256]{1,0:T(8,128)(2,1)S(1)} %get-tuple-element.81), channel_id=1, source_target_pairs={{0,2},{1,3},{2,0},{3,1},{4,6},{5,7},{6,4},{7,5},{8,10},{9,11},{10,... | collective-permute-start | bytes 122888 | tf_op jit(solution)/shard_map/ppermute | solution.py:555
  66.2 2.3 %collective-permute-start.26 = (bf16[80,256]{1,0:T(8,128)(2,1)S(1)}, bf16[80,256]{1,0:T(8,128)(2,1)S(1)}, u32[]{:S(2)}, u32[]{:S(2)}) collective-permute-start(bf16[80,256]{1,0:T(8,128)(2,1)S(1)} %get-tuple-element.82), channel_id=1, source_target_pairs={{0,3},{1,2},{2,1},{3,0},{4,7},{5,6},{6,5},{7,4},{8,11},{9,10},{10,... | collective-permute-start | bytes 122888 | tf_op jit(solution)/shard_map/ppermute | solution.py:555
  68.5 2.4 %shard_map.171 = (bf16[896,640]{1,0:T(8,128)(2,1)}, f32[8,128]{1,0:T(8,128)S(1)}) custom-call(bf16[896,128]{1,0:T(8,128)(2,1)S(1)} %shard_map.153.refs_2_.refs_0_, bf16[896,128]{1,0:T(8,128)(2,1)S(1)} %collective-permute-done.17.refs_8_.refs_1_, bf16[896,128]{1,0:T(8,128)(2,1)S(1)} %shard_map.164.refs_2_, ...), custom_call_target="tpu_custom_call" | custom-call | flops 3000000000 | bytes 1000 | tf_op jit(solution)/shard_map/pallas_call | solution.py:81
  (107 shorter events, 17.2 us)
Async XLA Ops:
  1.6 13.8 %collective-permute-start.1 = (bf16[320,256]{1,0:T(8,128)(2,1)S(1)}, bf16[320,256]{1,0:T(8,128)(2,1)S(1)}, u32[]{:S(2)}, u32[]{:S(2)}) collective-permute-start(bf16[320,256]{1,0:T(8,128)(2,1)S(1)} %constant_dynamic-slice_fusion), channel_id=1, source_target_pairs={{0,2},{1,3},{2,0},{3,1},{4,6},{5,7},{6,4},{7,5},{8,10},{9,11},{10,... | collective-permute-start | bytes 491528 | tf_op jit(solution)/shard_map/ppermute | solution.py:555
  5.7 15.3 %collective-permute-start = (bf16[320,256]{1,0:T(8,128)(2,1)S(1)}, bf16[320,256]{1,0:T(8,128)(2,1)S(1)}, u32[]{:S(2)}, u32[]{:S(2)}) collective-permute-start(bf16[320,256]{1,0:T(8,128)(2,1)S(1)} %constant_dynamic-slice_fusion), channel_id=1, source_target_pairs={{0,1},{1,0},{2,3},{3,2},{4,5},{5,4},{6,7},{7,6},{8,9},{9,8},{10,11... | collective-permute-start | bytes 491528 | tf_op jit(solution)/shard_map/ppermute | solution.py:555
  11.9 9.1 %collective-permute-start.3 = (bf16[320,128]{1,0:T(8,128)(2,1)}, bf16[320,128]{1,0:T(8,128)(2,1)S(1)}, u32[]{:S(2)}, u32[]{:S(2)}) collective-permute-start(bf16[320,128]{1,0:T(8,128)(2,1)} %get-tuple-element.46.refs_1_.refs_5_.refs_0_), channel_id=1, source_target_pairs={{0,8},{4,12},{8,0},{12,4},{16,24},{20,28},{24,16},{28,20},{1,9},{5... | collective-permute-start | bytes 245768 | tf_op jit(solution)/shard_map/ppermute | solution.py:555
  13.4 7.6 %collective-permute-start.4 = (bf16[320,128]{1,0:T(8,128)(2,1)}, bf16[320,128]{1,0:T(8,128)(2,1)S(1)}, u32[]{:S(2)}, u32[]{:S(2)}) collective-permute-start(bf16[320,128]{1,0:T(8,128)(2,1)} %get-tuple-element.46.refs_1_.refs_5_.refs_0_), channel_id=1, source_target_pairs={{0,16},{4,20},{8,24},{12,28},{16,0},{20,4},{24,8},{28,12},{1,17},{... | collective-permute-start | bytes 245768 | tf_op jit(solution)/shard_map/ppermute | solution.py:555
  14.9 6.1 %collective-permute-start.5 = (bf16[320,128]{1,0:T(8,128)(2,1)}, bf16[320,128]{1,0:T(8,128)(2,1)S(1)}, u32[]{:S(2)}, u32[]{:S(2)}) collective-permute-start(bf16[320,128]{1,0:T(8,128)(2,1)} %get-tuple-element.46.refs_1_.refs_5_.refs_0_), channel_id=1, source_target_pairs={{0,24},{4,28},{8,16},{12,20},{16,8},{20,12},{24,0},{28,4},{1,25},{... | collective-permute-start | bytes 245768 | tf_op jit(solution)/shard_map/ppermute | solution.py:555
  16.3 5.4 %collective-permute-start.2 = (bf16[320,256]{1,0:T(8,128)(2,1)S(1)}, bf16[320,256]{1,0:T(8,128)(2,1)S(1)}, u32[]{:S(2)}, u32[]{:S(2)}) collective-permute-start(bf16[320,256]{1,0:T(8,128)(2,1)S(1)} %shard_map.147.refs_1_.refs_4_), channel_id=1, source_target_pairs={{0,1},{1,0},{2,3},{3,2},{4,5},{5,4},{6,7},{7,6},{8,9},{9,8},{10,11... | collective-permute-start | bytes 491528 | tf_op jit(solution)/shard_map/ppermute | solution.py:555
  27.5 4.3 %collective-permute-start.9 = (bf16[4,320,128]{2,1,0:T(8,128)(2,1)S(1)}, bf16[4,320,128]{2,1,0:T(8,128)(2,1)S(1)}, u32[]{:S(2)}, u32[]{:S(2)}) collective-permute-start(bf16[4,320,128]{2,1,0:T(8,128)(2,1)S(1)} %bitcast.31), channel_id=1, source_target_pairs={{0,4},{4,0},{8,12},{12,8},{16,20},{20,16},{24,28},{28,24},{1,5},{5... | collective-permute-start | bytes 983048 | tf_op jit(solution)/shard_map/ppermute | solution.py:555
  27.7 11.1 %collective-permute-start.8 = (bf16[1328,128]{1,0:T(8,128)(2,1)S(1)}, bf16[1328,128]{1,0:T(8,128)(2,1)S(1)}, u32[]{:S(2)}, u32[]{:S(2)}) collective-permute-start(bf16[1328,128]{1,0:T(8,128)(2,1)S(1)} %shard_map.151.refs_4_.refs_0_), channel_id=1, source_target_pairs={{0,8},{4,12},{8,0},{12,4},{16,24},{20,28},{24,16},{28,20},{1,9},{5... | collective-permute-start | bytes 1019912 | tf_op jit(solution)/shard_map/ppermute | solution.py:690
  29.2 5.6 %collective-permute-start.10 = (bf16[160,128]{1,0:T(8,128)(2,1)S(1)}, bf16[160,128]{1,0:T(8,128)(2,1)S(1)}, u32[]{:S(2)}, u32[]{:S(2)}) collective-permute-start(bf16[160,128]{1,0:T(8,128)(2,1)S(1)} %copy-done.17), channel_id=1, source_target_pairs={{0,2},{1,3},{2,0},{3,1},{4,6},{5,7},{6,4},{7,5},{8,10},{9,11},{10,... | collective-permute-start | bytes 122888 | tf_op jit(solution)/shard_map/ppermute | solution.py:555
  30.3 11.0 %collective-permute-start.14 = (bf16[1280,128]{1,0:T(8,128)(2,1)S(1)}, bf16[1280,128]{1,0:T(8,128)(2,1)S(1)}, u32[]{:S(2)}, u32[]{:S(2)}) collective-permute-start(bf16[1280,128]{1,0:T(8,128)(2,1)S(1)} %copy-done.16), channel_id=1, source_target_pairs={{0,16},{4,20},{8,24},{12,28},{16,0},{20,4},{24,8},{28,12},{1,17},{... | collective-permute-start | bytes 983048 | tf_op jit(solution)/shard_map/ppermute | solution.py:555
  34.9 4.1 %collective-permute-start.11 = (bf16[160,128]{1,0:T(8,128)(2,1)S(1)}, bf16[160,128]{1,0:T(8,128)(2,1)S(1)}, u32[]{:S(2)}, u32[]{:S(2)}) collective-permute-start(bf16[160,128]{1,0:T(8,128)(2,1)S(1)} %shard_map.154), channel_id=1, source_target_pairs={{0,1},{1,0},{2,3},{3,2},{4,5},{5,4},{6,7},{7,6},{8,9},{9,8},{10,11... | collective-permute-start | bytes 122888 | tf_op jit(solution)/shard_map/ppermute | solution.py:555
  36.7 12.3 %collective-permute-start.16 = (bf16[896,128]{1,0:T(8,128)(2,1)S(1)}, bf16[896,128]{1,0:T(8,128)(2,1)S(1)}, u32[]{:S(2)}, u32[]{:S(2)}) collective-permute-start(bf16[896,128]{1,0:T(8,128)(2,1)S(1)} %shard_map.153.refs_2_.refs_0_), channel_id=1, source_target_pairs={{0,2},{1,3},{2,0},{3,1},{4,6},{5,7},{6,4},{7,5},{8,10},{9,11},{10,... | collective-permute-start | bytes 688136 | tf_op jit(solution)/shard_map/ppermute | solution.py:555
  37.7 11.4 %collective-permute-start.17 = (bf16[896,128]{1,0:T(8,128)(2,1)S(1)}, bf16[896,128]{1,0:T(8,128)(2,1)S(1)}, u32[]{:S(2)}, u32[]{:S(2)}) collective-permute-start(bf16[896,128]{1,0:T(8,128)(2,1)S(1)} %shard_map.153.refs_2_.refs_0_), channel_id=1, source_target_pairs={{0,1},{1,0},{2,3},{3,2},{4,5},{5,4},{6,7},{7,6},{8,9},{9,8},{10,11... | collective-permute-start | bytes 688136 | tf_op jit(solution)/shard_map/ppermute | solution.py:555
  39.1 9.9 %collective-permute-start.12 = (bf16[1328,128]{1,0:T(8,128)(2,1)S(1)}, bf16[1328,128]{1,0:T(8,128)(2,1)S(1)}, u32[]{:S(2)}, u32[]{:S(2)}) collective-permute-start(bf16[1328,128]{1,0:T(8,128)(2,1)S(1)} %shard_map.155.refs_7_.refs_4_.refs_2_), channel_id=1, source_target_pairs={{0,16},{4,20},{8,24},{12,28},{16,0},{20,4},{24,8},{28,12},{1,17},{... | collective-permute-start | bytes 1019912 | tf_op jit(solution)/shard_map/ppermute | solution.py:690
  41.3 7.8 %collective-permute-start.15 = (bf16[1280,128]{1,0:T(8,128)(2,1)S(1)}, bf16[1280,128]{1,0:T(8,128)(2,1)S(1)}, u32[]{:S(2)}, u32[]{:S(2)}) collective-permute-start(bf16[1280,128]{1,0:T(8,128)(2,1)S(1)} %shard_map.161), channel_id=1, source_target_pairs={{0,8},{4,12},{8,0},{12,4},{16,24},{20,28},{24,16},{28,20},{1,9},{5... | collective-permute-start | bytes 983048 | tf_op jit(solution)/shard_map/ppermute | solution.py:555
  41.7 4.2 %collective-permute-start.13 = (bf16[320,128]{1,0:T(8,128)(2,1)S(1)}, bf16[320,128]{1,0:T(8,128)(2,1)S(1)}, u32[]{:S(2)}, u32[]{:S(2)}) collective-permute-start(bf16[320,128]{1,0:T(8,128)(2,1)S(1)} %shard_map.159.refs_0_), channel_id=1, source_target_pairs={{0,4},{4,0},{8,12},{12,8},{16,20},{20,16},{24,28},{28,24},{1,5},{5... | collective-permute-start | bytes 245768 | tf_op jit(solution)/shard_map/ppermute | solution.py:555
  49.5 7.9 %collective-permute-start.20 = (bf16[640,128]{1,0:T(8,128)(2,1)S(1)}, bf16[640,128]{1,0:T(8,128)(2,1)S(1)}, u32[]{:S(2)}, u32[]{:S(2)}) collective-permute-start(bf16[640,128]{1,0:T(8,128)(2,1)S(1)} %shard_map.160.refs_5_.refs_0_), channel_id=1, source_target_pairs={{0,16},{4,20},{8,24},{12,28},{16,0},{20,4},{24,8},{28,12},{1,17},{... | collective-permute-start | bytes 491528 | tf_op jit(solution)/shard_map/ppermute | solution.py:555
  50.5 8.0 %collective-permute-start.19 = (bf16[896,128]{1,0:T(8,128)(2,1)S(1)}, bf16[896,128]{1,0:T(8,128)(2,1)S(1)}, u32[]{:S(2)}, u32[]{:S(2)}) collective-permute-start(bf16[896,128]{1,0:T(8,128)(2,1)S(1)} %shard_map.164.refs_2_), channel_id=1, source_target_pairs={{0,1},{1,0},{2,3},{3,2},{4,5},{5,4},{6,7},{7,6},{8,9},{9,8},{10,11... | collective-permute-start | bytes 688136 | tf_op jit(solution)/shard_map/ppermute | solution.py:555
  52.5 4.3 %collective-permute-start.21 = (bf16[1,128,256]{2,1,0:T(8,128)(2,1)S(1)}, bf16[1,128,256]{2,1,0:T(8,128)(2,1)S(1)}, u32[]{:S(2)}, u32[]{:S(2)}) collective-permute-start(bf16[1,128,256]{2,1,0:T(8,128)(2,1)S(1)} %bitcast.48), channel_id=1, source_target_pairs={{0,8},{4,12},{8,0},{12,4},{16,24},{20,28},{24,16},{28,20},{1,9},{5... | collective-permute-start | bytes 196616 | tf_op jit(solution)/shard_map/ppermute | solution.py:555
  56.8 5.0 %collective-permute-start.22 = (bf16[2,128,256]{2,1,0:T(8,128)(2,1)S(1)}, bf16[2,128,256]{2,1,0:T(8,128)(2,1)S(1)}, u32[]{:S(2)}, u32[]{:S(2)}) collective-permute-start(bf16[2,128,256]{2,1,0:T(8,128)(2,1)S(1)} %shard_map.165.refs_2_), channel_id=1, source_target_pairs={{0,16},{4,20},{8,24},{12,28},{16,0},{20,4},{24,8},{28,12},{1,17},{... | collective-permute-start | bytes 393224 | tf_op jit(solution)/shard_map/ppermute | solution.py:555
  57.4 11.0 %collective-permute-start.27 = (bf16[1280,128]{1,0:T(8,128)(2,1)S(1)}, bf16[1280,128]{1,0:T(8,128)(2,1)S(1)}, u32[]{:S(2)}, u32[]{:S(2)}) collective-permute-start(bf16[1280,128]{1,0:T(8,128)(2,1)S(1)} %shard_map.166.refs_17_), channel_id=1, source_target_pairs={{0,8},{4,12},{8,0},{12,4},{16,24},{20,28},{24,16},{28,20},{1,9},{5... | collective-permute-start | bytes 983048 | tf_op jit(solution)/shard_map/ppermute | solution.py:555
  64.0 6.9 %collective-permute-start.24 = (bf16[80,256]{1,0:T(8,128)(2,1)S(1)}, bf16[80,256]{1,0:T(8,128)(2,1)S(1)}, u32[]{:S(2)}, u32[]{:S(2)}) collective-permute-start(bf16[80,256]{1,0:T(8,128)(2,1)S(1)} %get-tuple-element.80), channel_id=1, source_target_pairs={{0,1},{1,0},{2,3},{3,2},{4,5},{5,4},{6,7},{7,6},{8,9},{9,8},{10,11... | collective-permute-start | bytes 122888 | tf_op jit(solution)/shard_map/ppermute | solution.py:555
  64.6 6.5 %collective-permute-start.25 = (bf16[80,256]{1,0:T(8,128)(2,1)S(1)}, bf16[80,256]{1,0:T(8,128)(2,1)S(1)}, u32[]{:S(2)}, u32[]{:S(2)}) collective-permute-start(bf16[80,256]{1,0:T(8,128)(2,1)S(1)} %get-tuple-element.81), channel_id=1, source_target_pairs={{0,2},{1,3},{2,0},{3,1},{4,6},{5,7},{6,4},{7,5},{8,10},{9,11},{10,... | collective-permute-start | bytes 122888 | tf_op jit(solution)/shard_map/ppermute | solution.py:555
  66.2 5.8 %collective-permute-start.26 = (bf16[80,256]{1,0:T(8,128)(2,1)S(1)}, bf16[80,256]{1,0:T(8,128)(2,1)S(1)}, u32[]{:S(2)}, u32[]{:S(2)}) collective-permute-start(bf16[80,256]{1,0:T(8,128)(2,1)S(1)} %get-tuple-element.82), channel_id=1, source_target_pairs={{0,3},{1,2},{2,1},{3,0},{4,7},{5,6},{6,5},{7,4},{8,11},{9,10},{10,... | collective-permute-start | bytes 122888 | tf_op jit(solution)/shard_map/ppermute | solution.py:555
  (26 other events, 111.9 us)

commit v15 on v14

--- a/solution.py
+++ b/solution.py
@@ -622,11 +622,14 @@
         fetch=(0, 1, 2, 3),
         limit=60,
     )
-    rows_in = chips([rows] * n_chip)
     w_far = xored(w_half, "dp", n_dp // 2)
     mine = gathered(w_half, "dp", n_dp // 2)[1:]
     w_copy = joined([w_far], after=(rows,))
     mine += gathered(w_copy, "dp", n_dp // 2)
+    rows_in = [rows]
+    while 2 ** (len(rows_in) - 1) < n_chip:
+        rows_sent = joined(rows_in, (w_copy,)) if rows_in[1:] else rows
+        rows_in.append(xored(rows_sent, "tm", 2 ** len(rows_in)))
     xs, carried, scaled, *xt = call(
         scale_kernel,
         [shape((length, width), BF16), shape((length, half), F32), shape((8, LANES), F32)]
@@ -645,7 +648,7 @@
     else:
         early = ()
         source, spans = deals[:1] + [xored(d, "dp", s + 1) for s, d in enumerate(deals[1:])], None
-    other = swapped(stacked(mine, after=(*rows_in[1:4], scaled), cost=1.0))
+    other = swapped(stacked(mine, after=(rows_in[-1], scaled), cost=1.0))
     w_whole, bc, keep, send = call(
         lambda *refs: project_kernel(n_dp - 1, many, *refs),
         [
@@ -667,7 +670,7 @@
             (keep, recv),
         )[0]
     ]
-    rows_a = stacked(rows_in, after=(climbs[0],))
+    rows_a = joined(rows_in, (climbs[0],)).reshape(n_chip, in_rows, LANES)
     rows_b = swapped(rows_a)
     weighted = expert(rows_a, rows_b, w_gate[0], w_up[0], capacity, flip, (climbs[0],))
     if n_chip == 4:
@@ -748,8 +751,8 @@
         after=held,
     )
     r_recv = swapped(r_send)
-    fars = gathered(joined([far], (r_own,)), "dp", n_dp // 2)
     d_bc = call(db_kernel, [shape((length, columns), BF16)], 0.3, (xs, r_own, r_recv, db, dc))[0]
+    fars = gathered(joined([far], (d_bc,)), "dp", n_dp // 2)
     d_bcs = [d_bc.reshape(1, length, columns)]
     if n_chip == 4:
         grads_y = xored(dealt_all, "tm", 4)
@@ -777,7 +780,7 @@
         1.0,
         (x, bc, cumt, stept, cum, h_in, r_own, r_recv, w_whole, d_bc,
          *dxs, *exs, *owns),
-        after=(*fars[1:], *both),
+        after=both,
         scratch=[pltpu.VMEM((width, half), BF16), pltpu.VMEM((heads, half), F32)],
     )
     w_rows = width // (2 * n_chip)
@@ -786,7 +789,7 @@
         [shape((w_rows, columns), F32), shape((w_rows, columns), BF16)],
         0.5,
         (*columns_in, *d_bcs),
-        after=(token,),
+        after=(token, *fars[1:]),
         scratch=[pltpu.VMEM((2, w_rows, columns), F32)],
     )
     final = call(
@@ -799,7 +802,7 @@
     )
     final = list(final[:1]) + [xored(f, "dp", s + 1) for s, f in enumerate(final[1:])]
 
-    grads = stacked(grads, (term,), spans)
+    grads = stacked(grads, (final[0],), spans)
     w_down_grad, done = call(
         lambda *refs: down_kernel(n_dp, flip, capacity, grad_rows, *refs),
         [shape((hidden, piece), BF16), shape((8, LANES), F32)],

time: 72.9 us -> 73.3 us (level)
  waiting for transfers between devices: 14.4 us -> 15.6 us
  starting transfers between devices: 30.3 us -> 29.4 us
    ppermute x26 -> x25, waiting for transfers between devices: 14.4 us -> 15.6 us  [xored(): return lax.ppermute(array, axis, [(i, i ^ mask) for i in range(count)])]
    ppermute x2, starting transfers between devices: 3.59 us -> 2.36 us  [per_device(): arrived.append(lax.ppermute(climbs[-1], 'tm', moves))]
    ppermute x26 -> x25, starting transfers between devices: 26.7 us -> 27 us  [xored(): return lax.ppermute(array, axis, [(i, i ^ mask) for i in range(count)])]
    pallas_call x26 -> x27, Pallas kernels: 20.7 us -> 20.7 us  [call(): pl.pallas_call(body, out_shape=outs, in_specs=specs + [pl.BlockSpec(memor...]
  transfers between devices with their start and end apart: 28 -> 27, of which waited for: 10 -> 11; matrix products, arithmetic and copies ran while one was open for 0% -> 0% of each run, Pallas kernels for 29% -> 29%
where the time goes in v15:
time: 73.3 us; the launch traced here: 73 us
  starting transfers between devices  29.4 us (40%)
  Pallas kernels  23.7 us (32%)
  waiting for transfers between devices  15.6 us (21%)
  local copies, waits for them, and re-layouts  2.61 us (4%)
  between operations  1.72 us (2%)
    ppermute x25, starting transfers between devices, xored(): return lax.ppermute(array, axis, [(i, i ^ mask) for i in range(count)])  27 us
    pallas_call x27, Pallas kernels, call(): pl.pallas_call(body, out_shape=outs, in_specs=specs + [pl.BlockSpec(memor...  20.7 us
    ppermute x25, waiting for transfers between devices, xored(): return lax.ppermute(array, axis, [(i, i ^ mask) for i in range(count)])  15.6 us
    pallas_call x1, Pallas kernels, expert(): pl.pallas_call(body, out_shape=shape(out, BF16), grid=(width // depth,),...  2.93 us
    ppermute x2, starting transfers between devices, per_device(): arrived.append(lax.ppermute(climbs[-1], 'tm', moves))  2.36 us
    unnamed x44, local copies, waits for them, and re-layouts  1.67 us
  transfers between devices with their start and end apart: 27, of which 11 were waited for; matrix products, arithmetic and copies ran while one was open for 0% of the time, Pallas kernels for 29%

profile of v15, /device:TPU:0, one launch (start us, length us, event | category | flops | bytes accessed | tf_op | source)
XLA Modules:
  0.0 73.0 jit_solution(3623348809995302733)
XLA Ops:
  1.6 4.1 %collective-permute-start.1 = (bf16[320,256]{1,0:T(8,128)(2,1)S(1)}, bf16[320,256]{1,0:T(8,128)(2,1)S(1)}, u32[]{:S(2)}, u32[]{:S(2)}) collective-permute-start(bf16[320,256]{1,0:T(8,128)(2,1)S(1)} %constant_dynamic-slice_fusion), channel_id=1, source_target_pairs={{0,2},{1,3},{2,0},{3,1},{4,6},{5,7},{6,4},{7,5},{8,10},{9,11},{10,... | collective-permute-start | bytes 491528 | tf_op jit(solution)/shard_map/ppermute | solution.py:555
  6.3 4.0 %shard_map.146 = (f32[40,128]{1,0:T(8,128)}, f32[128,128]{1,0:T(8,128)}, bf16[2640,128]{1,0:T(8,128)(2,1)}, bf16[320,128]{1,0:T(8,128)(2,1)}, bf16[160,128]{1,0:T(8,128)(2,1)}, /*index=5*/bf16[160,128]{1,0:T(8,128)(2,1)}) custom-call(bf16[128,2560]{1,0:T(8,128)(2,1)} %bitcast.37, bf16[128,2560]{1,0:T(8,128)(2,1)} %bitcast.33, f32[40,128]{1,0:T(8,128)} %bitcast.54, ...), custom_call_target="tpu_custom_call" | custom-call | flops 4499999744 | bytes 1000 | tf_op jit(solution)/shard_map/pallas_call | solution.py:81
  10.3 1.5 %collective-permute-start.3 = (bf16[320,128]{1,0:T(8,128)(2,1)}, bf16[320,128]{1,0:T(8,128)(2,1)S(1)}, u32[]{:S(2)}, u32[]{:S(2)}) collective-permute-start(bf16[320,128]{1,0:T(8,128)(2,1)} %get-tuple-element.46.refs_1_.refs_0_.refs_5_), channel_id=1, source_target_pairs={{0,8},{4,12},{8,0},{12,4},{16,24},{20,28},{24,16},{28,20},{1,9},{5... | collective-permute-start | bytes 245768 | tf_op jit(solution)/shard_map/ppermute | solution.py:555
  11.8 1.6 %collective-permute-start = (bf16[320,256]{1,0:T(8,128)(2,1)S(1)}, bf16[320,256]{1,0:T(8,128)(2,1)S(1)}, u32[]{:S(2)}, u32[]{:S(2)}) collective-permute-start(bf16[320,256]{1,0:T(8,128)(2,1)S(1)} %constant_dynamic-slice_fusion), channel_id=1, source_target_pairs={{0,1},{1,0},{2,3},{3,2},{4,5},{5,4},{6,7},{7,6},{8,9},{9,8},{10,11... | collective-permute-start | bytes 491528 | tf_op jit(solution)/shard_map/ppermute | solution.py:555
  15.1 1.6 %collective-permute-start.4 = (bf16[640,128]{1,0:T(8,128)(2,1)S(1)}, bf16[640,128]{1,0:T(8,128)(2,1)S(1)}, u32[]{:S(2)}, u32[]{:S(2)}) collective-permute-start(bf16[640,128]{1,0:T(8,128)(2,1)S(1)} %shard_map.148), channel_id=1, source_target_pairs={{0,16},{4,20},{8,24},{12,28},{16,0},{20,4},{24,8},{28,12},{1,17},{... | collective-permute-start | bytes 491528 | tf_op jit(solution)/shard_map/ppermute | solution.py:555
  16.7 4.1 %shard_map.149 = (bf16[128,2560]{1,0:T(8,128)(2,1)}, f32[128,128]{1,0:T(8,128)}, f32[8,128]{1,0:T(8,128)}, bf16[640,128]{1,0:T(8,128)(2,1)}, bf16[640,128]{1,0:T(8,128)(2,1)}, /*index=5*/bf16[1280,128]{1,0:T(8,128)(2,1)}) custom-call(bf16[128,2560]{1,0:T(8,128)(2,1)} %bitcast.38, bf16[128,2560]{1,0:T(8,128)(2,1)} %bitcast.34, bf16[2560,128]{1,0:T(8,128)(2,1)} %bitcast.43, ...), custom_call_target="tpu_custom_call" | custom-call | flops 4499999744 | bytes 1000 | tf_op jit(solution)/shard_map/pallas_call | solution.py:81
  21.8 1.9 %collective-permute-done.5.refs_6_ = bf16[3,320,256]{2,1,0:T(8,128)(2,1)S(1)} collective-permute-done((bf16[3,320,256]{2,1,0:T(8,128)(2,1)S(1)}, bf16[3,320,256]{2,1,0:T(8,128)(2,1)S(1)}, u32[]{:S(2)}, u32[]{:S(2)}) %collective-permute-start.5) | collective-permute-done | bytes 491552 | tf_op jit(solution)/shard_map/ppermute | solution.py:555
  25.0 1.5 %collective-permute-done.6.refs_1_.refs_3_ = bf16[1328,128]{1,0:T(8,128)(2,1)S(1)} collective-permute-done((bf16[1328,128]{1,0:T(8,128)(2,1)S(1)}, bf16[1328,128]{1,0:T(8,128)(2,1)S(1)}, u32[]{:S(2)}, u32[]{:S(2)}) %collective-permute-start.6) | collective-permute-done | bytes 340000 | tf_op jit(solution)/shard_map/ppermute | solution.py:555
  26.9 1.5 %collective-permute-start.7 = (bf16[1328,128]{1,0:T(8,128)(2,1)S(1)}, bf16[1328,128]{1,0:T(8,128)(2,1)S(1)}, u32[]{:S(2)}, u32[]{:S(2)}) collective-permute-start(bf16[1328,128]{1,0:T(8,128)(2,1)S(1)} %shard_map.152.refs_3_.refs_4_.refs_0_), channel_id=1, source_target_pairs={{0,8},{4,12},{8,0},{12,4},{16,24},{20,28},{24,16},{28,20},{1,9},{5... | collective-permute-start | bytes 1019912 | tf_op jit(solution)/shard_map/ppermute | solution.py:693
  28.5 3.4 %collective-permute-start.9 = (bf16[160,128]{1,0:T(8,128)(2,1)S(1)}, bf16[160,128]{1,0:T(8,128)(2,1)S(1)}, u32[]{:S(2)}, u32[]{:S(2)}) collective-permute-start(bf16[160,128]{1,0:T(8,128)(2,1)S(1)} %copy-done.17), channel_id=1, source_target_pairs={{0,2},{1,3},{2,0},{3,1},{4,6},{5,7},{6,4},{7,5},{8,10},{9,11},{10,... | collective-permute-start | bytes 122888 | tf_op jit(solution)/shard_map/ppermute | solution.py:555
  31.9 1.5 %collective-permute-start.13 = (bf16[1280,128]{1,0:T(8,128)(2,1)S(1)}, bf16[1280,128]{1,0:T(8,128)(2,1)S(1)}, u32[]{:S(2)}, u32[]{:S(2)}) collective-permute-start(bf16[1280,128]{1,0:T(8,128)(2,1)S(1)} %copy-done.16), channel_id=1, source_target_pairs={{0,16},{4,20},{8,24},{12,28},{16,0},{20,4},{24,8},{28,12},{1,17},{... | collective-permute-start | bytes 983048 | tf_op jit(solution)/shard_map/ppermute | solution.py:555
  33.4 2.9 %shard_map.154.refs_2_.refs_0_ = bf16[896,128]{1,0:T(8,128)(2,1)S(1)} custom-call(bf16[4,320,128]{2,1,0:T(8,128)(2,1)S(1)} %bitcast.32, bf16[4,320,128]{2,1,0:T(8,128)(2,1)S(1)} %collective-permute-done.8.refs_1_, bf16[2560,896]{1,0:T(8,128)(2,1)S(1)} %bitcast.27, bf16[2560,896]{1,0:T(8,128)(2,1)S(1)} %bitcast.30, ...), custom_call_target="tpu_custom_call" | custom-call | flops 1000000000 | bytes 1000 | tf_op jit(solution)/shard_map/pallas_call | solution.py:511
  38.9 2.9 %collective-permute-done.10.refs_4_.refs_1_.refs_3_ = bf16[160,128]{1,0:T(8,128)(2,1)S(1)} collective-permute-done((bf16[160,128]{1,0:T(8,128)(2,1)S(1)}, bf16[160,128]{1,0:T(8,128)(2,1)S(1)}, u32[]{:S(2)}, u32[]{:S(2)}) %collective-permute-start.10) | collective-permute-done | bytes 40992 | tf_op jit(solution)/shard_map/ppermute | solution.py:555
  43.6 2.0 %shard_map.157 = (f32[128,1280]{1,0:T(8,128)S(1)}, f32[128,128]{1,0:T(8,128)S(1)}, f32[20,128]{1,0:T(8,128)S(1)}, f32[20,128]{1,0:T(8,128)S(1)}) custom-call(bf16[128,2560]{1,0:T(8,128)(2,1)S(1)} %bitcast.40, bf16[128,2560]{1,0:T(8,128)(2,1)S(1)} %bitcast.35, bf16[128,256]{1,0:T(8,128)(2,1)S(1)} %get-tuple-element.50.refs_2_.refs_1_, ...), custom_call_target="tpu_custom_call" | custom-call | flops 2100000000 | bytes 1000 | tf_op jit(solution)/shard_map/pallas_call | solution.py:81
  45.5 2.0 %shard_map.158 = (f32[128,1280]{1,0:T(8,128)S(1)}, f32[128,128]{1,0:T(8,128)S(1)}, f32[20,128]{1,0:T(8,128)S(1)}, f32[20,128]{1,0:T(8,128)S(1)}) custom-call(bf16[128,2560]{1,0:T(8,128)(2,1)S(1)} %bitcast.41, bf16[128,2560]{1,0:T(8,128)(2,1)S(1)} %bitcast.36, bf16[128,256]{1,0:T(8,128)(2,1)S(1)} %get-tuple-element.50.refs_2_.refs_1_, ...), custom_call_target="tpu_custom_call" | custom-call | flops 2100000000 | bytes 1000 | tf_op jit(solution)/shard_map/pallas_call | solution.py:81
  47.8 1.7 %collective-permute-done.15.refs_7_.refs_0_ = bf16[896,128]{1,0:T(8,128)(2,1)S(1)} collective-permute-done((bf16[896,128]{1,0:T(8,128)(2,1)S(1)}, bf16[896,128]{1,0:T(8,128)(2,1)S(1)}, u32[]{:S(2)}, u32[]{:S(2)}) %collective-permute-start.15) | collective-permute-done | bytes 229408 | tf_op jit(solution)/shard_map/ppermute | solution.py:555
  50.4 1.5 %collective-permute-start.18 = (bf16[640,128]{1,0:T(8,128)(2,1)S(1)}, bf16[640,128]{1,0:T(8,128)(2,1)S(1)}, u32[]{:S(2)}, u32[]{:S(2)}) collective-permute-start(bf16[640,128]{1,0:T(8,128)(2,1)S(1)} %shard_map.161.refs_5_.refs_0_), channel_id=1, source_target_pairs={{0,16},{4,20},{8,24},{12,28},{16,0},{20,4},{24,8},{28,12},{1,17},{... | collective-permute-start | bytes 491528 | tf_op jit(solution)/shard_map/ppermute | solution.py:555
  53.3 3.4 %collective-permute-done.19.refs_1_.refs_4_ = bf16[1,128,256]{2,1,0:T(8,128)(2,1)S(1)} collective-permute-done((bf16[1,128,256]{2,1,0:T(8,128)(2,1)S(1)}, bf16[1,128,256]{2,1,0:T(8,128)(2,1)S(1)}, u32[]{:S(2)}, u32[]{:S(2)}) %collective-permute-start.19) | collective-permute-done | bytes 65568 | tf_op jit(solution)/shard_map/ppermute | solution.py:555
  56.7 1.5 %collective-permute-start.20 = (bf16[2,128,256]{2,1,0:T(8,128)(2,1)S(1)}, bf16[2,128,256]{2,1,0:T(8,128)(2,1)S(1)}, u32[]{:S(2)}, u32[]{:S(2)}) collective-permute-start(bf16[2,128,256]{2,1,0:T(8,128)(2,1)S(1)} %shard_map.165.refs_2_), channel_id=1, source_target_pairs={{0,16},{4,20},{8,24},{12,28},{16,0},{20,4},{24,8},{28,12},{1,17},{... | collective-permute-start | bytes 393224 | tf_op jit(solution)/shard_map/ppermute | solution.py:555
  58.8 2.6 %shard_map.167 = (bf16[128,2560]{1,0:T(8,128)(2,1)}, f32[40,128]{1,0:T(8,128)}, f32[40,128]{1,0:T(8,128)}, f32[8,128]{1,0:T(8,128)S(1)}) custom-call(bf16[128,2560]{1,0:T(8,128)(2,1)S(1)} %bitcast.42, bf16[128,256]{1,0:T(8,128)(2,1)S(1)} %get-tuple-element.50.refs_2_.refs_1_, f32[40,128]{1,0:T(8,128)S(1)} %copy-done.14, f32[40,128]{1,0:T(8,128)S(1)} %bitcast.52, ...), custom_call_target="tpu_custom_call" | custom-call | flops 3000000000 | bytes 1000 | tf_op jit(solution)/shard_map/pallas_call | solution.py:81
  64.2 2.4 %collective-permute-start.24 = (bf16[80,256]{1,0:T(8,128)(2,1)S(1)}, bf16[80,256]{1,0:T(8,128)(2,1)S(1)}, u32[]{:S(2)}, u32[]{:S(2)}) collective-permute-start(bf16[80,256]{1,0:T(8,128)(2,1)S(1)} %get-tuple-element.81), channel_id=1, source_target_pairs={{0,2},{1,3},{2,0},{3,1},{4,6},{5,7},{6,4},{7,5},{8,10},{9,11},{10,... | collective-permute-start | bytes 122888 | tf_op jit(solution)/shard_map/ppermute | solution.py:555
  66.6 1.8 %collective-permute-start.25 = (bf16[80,256]{1,0:T(8,128)(2,1)S(1)}, bf16[80,256]{1,0:T(8,128)(2,1)S(1)}, u32[]{:S(2)}, u32[]{:S(2)}) collective-permute-start(bf16[80,256]{1,0:T(8,128)(2,1)S(1)} %get-tuple-element.82), channel_id=1, source_target_pairs={{0,3},{1,2},{2,1},{3,0},{4,7},{5,6},{6,5},{7,4},{8,11},{9,10},{10,... | collective-permute-start | bytes 122888 | tf_op jit(solution)/shard_map/ppermute | solution.py:555
  68.4 2.4 %shard_map.172 = (bf16[896,640]{1,0:T(8,128)(2,1)}, f32[8,128]{1,0:T(8,128)S(1)}) custom-call(bf16[896,128]{1,0:T(8,128)(2,1)S(1)} %shard_map.154.refs_2_.refs_0_, bf16[896,128]{1,0:T(8,128)(2,1)S(1)} %collective-permute-done.16.refs_8_.refs_1_, bf16[896,128]{1,0:T(8,128)(2,1)S(1)} %shard_map.168.refs_2_, ...), custom_call_target="tpu_custom_call" | custom-call | flops 3000000000 | bytes 1000 | tf_op jit(solution)/shard_map/pallas_call | solution.py:81
  70.8 1.6 %collective-permute-done.25.refs_3_ = bf16[80,256]{1,0:T(8,128)(2,1)S(1)} collective-permute-done((bf16[80,256]{1,0:T(8,128)(2,1)S(1)}, bf16[80,256]{1,0:T(8,128)(2,1)S(1)}, u32[]{:S(2)}, u32[]{:S(2)}) %collective-permute-start.25) | collective-permute-done | bytes 40992 | tf_op jit(solution)/shard_map/ppermute | solution.py:555
  (106 shorter events, 15.9 us)
Async XLA Ops:
  1.6 11.8 %collective-permute-start.1 = (bf16[320,256]{1,0:T(8,128)(2,1)S(1)}, bf16[320,256]{1,0:T(8,128)(2,1)S(1)}, u32[]{:S(2)}, u32[]{:S(2)}) collective-permute-start(bf16[320,256]{1,0:T(8,128)(2,1)S(1)} %constant_dynamic-slice_fusion), channel_id=1, source_target_pairs={{0,2},{1,3},{2,0},{3,1},{4,6},{5,7},{6,4},{7,5},{8,10},{9,11},{10,... | collective-permute-start | bytes 491528 | tf_op jit(solution)/shard_map/ppermute | solution.py:555
  10.3 4.8 %collective-permute-start.3 = (bf16[320,128]{1,0:T(8,128)(2,1)}, bf16[320,128]{1,0:T(8,128)(2,1)S(1)}, u32[]{:S(2)}, u32[]{:S(2)}) collective-permute-start(bf16[320,128]{1,0:T(8,128)(2,1)} %get-tuple-element.46.refs_1_.refs_0_.refs_5_), channel_id=1, source_target_pairs={{0,8},{4,12},{8,0},{12,4},{16,24},{20,28},{24,16},{28,20},{1,9},{5... | collective-permute-start | bytes 245768 | tf_op jit(solution)/shard_map/ppermute | solution.py:555
  11.8 9.0 %collective-permute-start = (bf16[320,256]{1,0:T(8,128)(2,1)S(1)}, bf16[320,256]{1,0:T(8,128)(2,1)S(1)}, u32[]{:S(2)}, u32[]{:S(2)}) collective-permute-start(bf16[320,256]{1,0:T(8,128)(2,1)S(1)} %constant_dynamic-slice_fusion), channel_id=1, source_target_pairs={{0,1},{1,0},{2,3},{3,2},{4,5},{5,4},{6,7},{7,6},{8,9},{9,8},{10,11... | collective-permute-start | bytes 491528 | tf_op jit(solution)/shard_map/ppermute | solution.py:555
  14.3 6.7 %collective-permute-start.2 = (bf16[320,256]{1,0:T(8,128)(2,1)S(1)}, bf16[320,256]{1,0:T(8,128)(2,1)S(1)}, u32[]{:S(2)}, u32[]{:S(2)}) collective-permute-start(bf16[320,256]{1,0:T(8,128)(2,1)S(1)} %shard_map.147.refs_2_.refs_1_.refs_4_), channel_id=1, source_target_pairs={{0,1},{1,0},{2,3},{3,2},{4,5},{5,4},{6,7},{7,6},{8,9},{9,8},{10,11... | collective-permute-start | bytes 491528 | tf_op jit(solution)/shard_map/ppermute | solution.py:555
  15.1 5.9 %collective-permute-start.4 = (bf16[640,128]{1,0:T(8,128)(2,1)S(1)}, bf16[640,128]{1,0:T(8,128)(2,1)S(1)}, u32[]{:S(2)}, u32[]{:S(2)}) collective-permute-start(bf16[640,128]{1,0:T(8,128)(2,1)S(1)} %shard_map.148), channel_id=1, source_target_pairs={{0,16},{4,20},{8,24},{12,28},{16,0},{20,4},{24,8},{28,12},{1,17},{... | collective-permute-start | bytes 491528 | tf_op jit(solution)/shard_map/ppermute | solution.py:555
  21.7 1.9 %collective-permute-start.5 = (bf16[3,320,256]{2,1,0:T(8,128)(2,1)S(1)}, bf16[3,320,256]{2,1,0:T(8,128)(2,1)S(1)}, u32[]{:S(2)}, u32[]{:S(2)}) collective-permute-start(bf16[3,320,256]{2,1,0:T(8,128)(2,1)S(1)} %bitcast.47), channel_id=1, source_target_pairs={{0,4},{4,0},{8,12},{12,8},{16,20},{20,16},{24,28},{28,24},{1,5},{5... | collective-permute-start | bytes 1474568 | tf_op jit(solution)/shard_map/ppermute | solution.py:555
  26.7 6.7 %collective-permute-start.8 = (bf16[4,320,128]{2,1,0:T(8,128)(2,1)S(1)}, bf16[4,320,128]{2,1,0:T(8,128)(2,1)S(1)}, u32[]{:S(2)}, u32[]{:S(2)}) collective-permute-start(bf16[4,320,128]{2,1,0:T(8,128)(2,1)S(1)} %bitcast.31), channel_id=1, source_target_pairs={{0,4},{4,0},{8,12},{12,8},{16,20},{20,16},{24,28},{28,24},{1,5},{5... | collective-permute-start | bytes 983048 | tf_op jit(solution)/shard_map/ppermute | solution.py:555
  26.9 12.0 %collective-permute-start.7 = (bf16[1328,128]{1,0:T(8,128)(2,1)S(1)}, bf16[1328,128]{1,0:T(8,128)(2,1)S(1)}, u32[]{:S(2)}, u32[]{:S(2)}) collective-permute-start(bf16[1328,128]{1,0:T(8,128)(2,1)S(1)} %shard_map.152.refs_3_.refs_4_.refs_0_), channel_id=1, source_target_pairs={{0,8},{4,12},{8,0},{12,4},{16,24},{20,28},{24,16},{28,20},{1,9},{5... | collective-permute-start | bytes 1019912 | tf_op jit(solution)/shard_map/ppermute | solution.py:693
  28.5 7.9 %collective-permute-start.9 = (bf16[160,128]{1,0:T(8,128)(2,1)S(1)}, bf16[160,128]{1,0:T(8,128)(2,1)S(1)}, u32[]{:S(2)}, u32[]{:S(2)}) collective-permute-start(bf16[160,128]{1,0:T(8,128)(2,1)S(1)} %copy-done.17), channel_id=1, source_target_pairs={{0,2},{1,3},{2,0},{3,1},{4,6},{5,7},{6,4},{7,5},{8,10},{9,11},{10,... | collective-permute-start | bytes 122888 | tf_op jit(solution)/shard_map/ppermute | solution.py:555
  31.9 11.0 %collective-permute-start.13 = (bf16[1280,128]{1,0:T(8,128)(2,1)S(1)}, bf16[1280,128]{1,0:T(8,128)(2,1)S(1)}, u32[]{:S(2)}, u32[]{:S(2)}) collective-permute-start(bf16[1280,128]{1,0:T(8,128)(2,1)S(1)} %copy-done.16), channel_id=1, source_target_pairs={{0,16},{4,20},{8,24},{12,28},{16,0},{20,4},{24,8},{28,12},{1,17},{... | collective-permute-start | bytes 983048 | tf_op jit(solution)/shard_map/ppermute | solution.py:555
  36.5 5.3 %collective-permute-start.10 = (bf16[160,128]{1,0:T(8,128)(2,1)S(1)}, bf16[160,128]{1,0:T(8,128)(2,1)S(1)}, u32[]{:S(2)}, u32[]{:S(2)}) collective-permute-start(bf16[160,128]{1,0:T(8,128)(2,1)S(1)} %shard_map.155), channel_id=1, source_target_pairs={{0,1},{1,0},{2,3},{3,2},{4,5},{5,4},{6,7},{7,6},{8,9},{9,8},{10,11... | collective-permute-start | bytes 122888 | tf_op jit(solution)/shard_map/ppermute | solution.py:555
  36.9 12.7 %collective-permute-start.15 = (bf16[896,128]{1,0:T(8,128)(2,1)S(1)}, bf16[896,128]{1,0:T(8,128)(2,1)S(1)}, u32[]{:S(2)}, u32[]{:S(2)}) collective-permute-start(bf16[896,128]{1,0:T(8,128)(2,1)S(1)} %shard_map.154.refs_2_.refs_0_), channel_id=1, source_target_pairs={{0,2},{1,3},{2,0},{3,1},{4,6},{5,7},{6,4},{7,5},{8,10},{9,11},{10,... | collective-permute-start | bytes 688136 | tf_op jit(solution)/shard_map/ppermute | solution.py:555
  37.6 11.9 %collective-permute-start.16 = (bf16[896,128]{1,0:T(8,128)(2,1)S(1)}, bf16[896,128]{1,0:T(8,128)(2,1)S(1)}, u32[]{:S(2)}, u32[]{:S(2)}) collective-permute-start(bf16[896,128]{1,0:T(8,128)(2,1)S(1)} %shard_map.154.refs_2_.refs_0_), channel_id=1, source_target_pairs={{0,1},{1,0},{2,3},{3,2},{4,5},{5,4},{6,7},{7,6},{8,9},{9,8},{10,11... | collective-permute-start | bytes 688136 | tf_op jit(solution)/shard_map/ppermute | solution.py:555
  42.0 8.0 %collective-permute-start.11 = (bf16[1328,128]{1,0:T(8,128)(2,1)S(1)}, bf16[1328,128]{1,0:T(8,128)(2,1)S(1)}, u32[]{:S(2)}, u32[]{:S(2)}) collective-permute-start(bf16[1328,128]{1,0:T(8,128)(2,1)S(1)} %shard_map.156.refs_7_.refs_4_.refs_2_), channel_id=1, source_target_pairs={{0,16},{4,20},{8,24},{12,28},{16,0},{20,4},{24,8},{28,12},{1,17},{... | collective-permute-start | bytes 1019912 | tf_op jit(solution)/shard_map/ppermute | solution.py:693
  42.9 7.1 %collective-permute-start.14 = (bf16[1280,128]{1,0:T(8,128)(2,1)S(1)}, bf16[1280,128]{1,0:T(8,128)(2,1)S(1)}, u32[]{:S(2)}, u32[]{:S(2)}) collective-permute-start(bf16[1280,128]{1,0:T(8,128)(2,1)S(1)} %shard_map.162), channel_id=1, source_target_pairs={{0,8},{4,12},{8,0},{12,4},{16,24},{20,28},{24,16},{28,20},{1,9},{5... | collective-permute-start | bytes 983048 | tf_op jit(solution)/shard_map/ppermute | solution.py:555
  43.5 4.2 %collective-permute-start.12 = (bf16[320,128]{1,0:T(8,128)(2,1)S(1)}, bf16[320,128]{1,0:T(8,128)(2,1)S(1)}, u32[]{:S(2)}, u32[]{:S(2)}) collective-permute-start(bf16[320,128]{1,0:T(8,128)(2,1)S(1)} %shard_map.160.refs_0_), channel_id=1, source_target_pairs={{0,4},{4,0},{8,12},{12,8},{16,20},{20,16},{24,28},{28,24},{1,5},{5... | collective-permute-start | bytes 245768 | tf_op jit(solution)/shard_map/ppermute | solution.py:555
  50.4 7.8 %collective-permute-start.18 = (bf16[640,128]{1,0:T(8,128)(2,1)S(1)}, bf16[640,128]{1,0:T(8,128)(2,1)S(1)}, u32[]{:S(2)}, u32[]{:S(2)}) collective-permute-start(bf16[640,128]{1,0:T(8,128)(2,1)S(1)} %shard_map.161.refs_5_.refs_0_), channel_id=1, source_target_pairs={{0,16},{4,20},{8,24},{12,28},{16,0},{20,4},{24,8},{28,12},{1,17},{... | collective-permute-start | bytes 491528 | tf_op jit(solution)/shard_map/ppermute | solution.py:555
  52.4 4.3 %collective-permute-start.19 = (bf16[1,128,256]{2,1,0:T(8,128)(2,1)S(1)}, bf16[1,128,256]{2,1,0:T(8,128)(2,1)S(1)}, u32[]{:S(2)}, u32[]{:S(2)}) collective-permute-start(bf16[1,128,256]{2,1,0:T(8,128)(2,1)S(1)} %bitcast.48), channel_id=1, source_target_pairs={{0,8},{4,12},{8,0},{12,4},{16,24},{20,28},{24,16},{28,20},{1,9},{5... | collective-permute-start | bytes 196616 | tf_op jit(solution)/shard_map/ppermute | solution.py:555
  53.0 8.7 %collective-permute-start.21 = (bf16[896,128]{1,0:T(8,128)(2,1)S(1)}, bf16[896,128]{1,0:T(8,128)(2,1)S(1)}, u32[]{:S(2)}, u32[]{:S(2)}) collective-permute-start(bf16[896,128]{1,0:T(8,128)(2,1)S(1)} %shard_map.168.refs_2_), channel_id=1, source_target_pairs={{0,1},{1,0},{2,3},{3,2},{4,5},{5,4},{6,7},{7,6},{8,9},{9,8},{10,11... | collective-permute-start | bytes 688136 | tf_op jit(solution)/shard_map/ppermute | solution.py:555
  56.7 5.0 %collective-permute-start.20 = (bf16[2,128,256]{2,1,0:T(8,128)(2,1)S(1)}, bf16[2,128,256]{2,1,0:T(8,128)(2,1)S(1)}, u32[]{:S(2)}, u32[]{:S(2)}) collective-permute-start(bf16[2,128,256]{2,1,0:T(8,128)(2,1)S(1)} %shard_map.165.refs_2_), channel_id=1, source_target_pairs={{0,16},{4,20},{8,24},{12,28},{16,0},{20,4},{24,8},{28,12},{1,17},{... | collective-permute-start | bytes 393224 | tf_op jit(solution)/shard_map/ppermute | solution.py:555
  58.2 10.1 %collective-permute-start.26 = (bf16[1280,128]{1,0:T(8,128)(2,1)S(1)}, bf16[1280,128]{1,0:T(8,128)(2,1)S(1)}, u32[]{:S(2)}, u32[]{:S(2)}) collective-permute-start(bf16[1280,128]{1,0:T(8,128)(2,1)S(1)} %shard_map.166.refs_16_), channel_id=1, source_target_pairs={{0,8},{4,12},{8,0},{12,4},{16,24},{20,28},{24,16},{28,20},{1,9},{5... | collective-permute-start | bytes 983048 | tf_op jit(solution)/shard_map/ppermute | solution.py:555
  63.9 6.9 %collective-permute-start.23 = (bf16[80,256]{1,0:T(8,128)(2,1)S(1)}, bf16[80,256]{1,0:T(8,128)(2,1)S(1)}, u32[]{:S(2)}, u32[]{:S(2)}) collective-permute-start(bf16[80,256]{1,0:T(8,128)(2,1)S(1)} %get-tuple-element.80), channel_id=1, source_target_pairs={{0,1},{1,0},{2,3},{3,2},{4,5},{5,4},{6,7},{7,6},{8,9},{9,8},{10,11... | collective-permute-start | bytes 122888 | tf_op jit(solution)/shard_map/ppermute | solution.py:555
  64.2 6.6 %collective-permute-start.24 = (bf16[80,256]{1,0:T(8,128)(2,1)S(1)}, bf16[80,256]{1,0:T(8,128)(2,1)S(1)}, u32[]{:S(2)}, u32[]{:S(2)}) collective-permute-start(bf16[80,256]{1,0:T(8,128)(2,1)S(1)} %get-tuple-element.81), channel_id=1, source_target_pairs={{0,2},{1,3},{2,0},{3,1},{4,6},{5,7},{6,4},{7,5},{8,10},{9,11},{10,... | collective-permute-start | bytes 122888 | tf_op jit(solution)/shard_map/ppermute | solution.py:555
  66.6 5.8 %collective-permute-start.25 = (bf16[80,256]{1,0:T(8,128)(2,1)S(1)}, bf16[80,256]{1,0:T(8,128)(2,1)S(1)}, u32[]{:S(2)}, u32[]{:S(2)}) collective-permute-start(bf16[80,256]{1,0:T(8,128)(2,1)S(1)} %get-tuple-element.82), channel_id=1, source_target_pairs={{0,3},{1,2},{2,1},{3,0},{4,7},{5,6},{6,5},{7,4},{8,11},{9,10},{10,... | collective-permute-start | bytes 122888 | tf_op jit(solution)/shard_map/ppermute | solution.py:555
  (25 other events, 117.8 us)

commit v16 on v15

--- a/solution.py
+++ b/solution.py
@@ -104,17 +104,8 @@
     return pl.ds(pl.multiple_of(index * size, align), size)
 
 
-def picked(x_ref, dy_ref, slot_ref, count_ref, gate_ref, rows_ref, out_refs):
-    length, width = x_ref.shape
-    slots = slot_ref.shape[1]
-    hit = iota((length, slots), 0) == slot_ref[...]
-    live = iota((1, slots), 1) < count_ref[...]
-    weight = jnp.where(live, gate_ref[...].astype(F32), 0.0)
-    rows = dot(where_one(hit).astype(BF16), x_ref[...], 0, 0).astype(BF16)
-    for t in range(width // LANES):
-        rows_ref[t * slots : (t + 1) * slots, :] = rows[:, t * LANES : (t + 1) * LANES]
-    grads = dot(jnp.where(hit, weight, 0.0).astype(BF16), dy_ref[...], 0, 0).astype(BF16)
-    held = out_refs[-1]
+def dealt_blocks(grads, held, out_refs):
+    slots, width = grads.shape
     n_dp = held.shape[0]
     piece = width // n_dp
     for i in range(n_dp):
@@ -126,37 +117,82 @@
             held[i, t * slots : (t + 1) * slots, :] = block
     place = lax.axis_index("dp")
     s = 0
-    for out in out_refs[:-1]:
+    for out in out_refs:
         for start in range(0, out.shape[0], held.shape[1]):
             out[start : start + held.shape[1], :] = held[place ^ s]
             s += 1
 
 
+def columns_of(ref, index, wide):
+    return ref.at[:, pl.ds(pl.multiple_of(index * wide, LANES), wide)]
+
+
+def rows_of(ref, index, high):
+    return ref.at[pl.ds(pl.multiple_of(index * high, LANES), high), :]
+
+
 def high_low(values):
     high = values.astype(BF16).astype(F32)
     return [high, values - high]
 
 
 def prep_kernel(
-    n_deals, x_ref, dy_ref, ldt_ref, stept_ref, slot_ref, count_ref, gate_ref,
-    cumt_ref, cum_ref, dyt_ref, rows_ref, *rest,
+    n_deals, x_hbm, dy_hbm, ldt_ref, stept_ref, slot_ref, count_ref, gate_ref,
+    cumt_ref, cum_ref, dyt_hbm, rows_ref, *rest,
 ):
-    length, width = x_ref.shape
+    deal_refs = rest[:n_deals]
+    held_ref, x_buf, dy_buf, dyt_buf, extra_buf, in_sems, out_sems = rest[n_deals:]
+    parts, length, wide = x_buf.shape
+    arrivals = []
+    for c in range(parts):
+        pair = [
+            pltpu.make_async_copy(columns_of(ref, c, wide), buf.at[c], in_sems.at[k, c])
+            for k, (ref, buf) in enumerate(((x_hbm, x_buf), (dy_hbm, dy_buf)))
+        ]
+        for copy in pair:
+            copy.start()
+        arrivals.append(pair)
     heads = ldt_ref.shape[0]
-    size = width // heads
-    picked(x_ref, dy_ref, slot_ref, count_ref, gate_ref, rows_ref, rest)
+    size = parts * wide // heads
+    slots = slot_ref.shape[1]
+    hit = iota((length, slots), 0) == slot_ref[...]
+    live = iota((1, slots), 1) < count_ref[...]
+    weight = jnp.where(live, gate_ref[...].astype(F32), 0.0)
+    pick = where_one(hit).astype(BF16)
+    scaled = jnp.where(hit, weight, 0.0).astype(BF16)
     cumt = dot(ldt_ref[...], triangle(length, lambda a, b: a <= b), 1, 0, HI)
     cumt_ref[...] = cumt
     pad = jnp.zeros((LANES - heads, length), F32)
     cum_ref[...] = jnp.concatenate([cumt - jnp.log(stept_ref[...]), pad], axis=0).T
-    start = jnp.exp(jnp.concatenate([cumt, pad], axis=0).T)
-    table = halves(start)
-    for j in range(width // LANES):
-        span = slice(j * LANES, (j + 1) * LANES)
-        dys = dy_ref[:, span].astype(F32) * dot(table, to_lanes(j, size), 1, 0)
-        dyt_ref[span, :] = dys.T.astype(BF16)
+    table = halves(jnp.exp(jnp.concatenate([cumt, pad], axis=0).T))
     decay = jnp.broadcast_to(jnp.exp(cumt[:, length - 1 : length]), (heads, LANES))
-    dyt_ref[width : width + 2 * heads, :] = jnp.concatenate(high_low(decay), axis=0).astype(BF16)
+    extra_buf[...] = jnp.concatenate(high_low(decay), axis=0).astype(BF16)
+    leaving = [
+        pltpu.make_async_copy(
+            extra_buf, dyt_hbm.at[pl.ds(parts * wide, 2 * heads), :], out_sems.at[parts]
+        )
+    ]
+    leaving[0].start()
+    grads = []
+    for c in range(parts):
+        arrivals[c][0].wait()
+        rows = dot(pick, x_buf[c], 0, 0).astype(BF16)
+        for t in range(wide // LANES):
+            at = (c * (wide // LANES) + t) * slots
+            rows_ref[at : at + slots, :] = rows[:, t * LANES : (t + 1) * LANES]
+        arrivals[c][1].wait()
+        grads.append(dot(scaled, dy_buf[c], 0, 0).astype(BF16))
+        for t in range(wide // LANES):
+            span = slice(t * LANES, (t + 1) * LANES)
+            wanted = to_lanes(c * (wide // LANES) + t, size)
+            dys = dy_buf[c, :, span].astype(F32) * dot(table, wanted, 1, 0)
+            dyt_buf[c, span, :] = dys.T.astype(BF16)
+        copy = pltpu.make_async_copy(dyt_buf.at[c], rows_of(dyt_hbm, c, wide), out_sems.at[c])
+        copy.start()
+        leaving.append(copy)
+    dealt_blocks(jnp.concatenate(grads, axis=1), held_ref, deal_refs)
+    for copy in leaving:
+        copy.wait()
 
 
 def scale_kernel(x_ref, dy_ref, h_ref, cumt_ref, cum_ref, xs_ref, carried_ref, token_ref, *rest):
@@ -186,6 +222,78 @@
         for start in range(0, out.shape[0], block):
             out[start : start + block, :] = xt_ref[rows_at(chip ^ s, block), :]
             s += 1
+
+
+def scale4_kernel(
+    x_hbm, dy_hbm, h_hbm, cumt_ref, cum_ref, xs_hbm, carried_ref, token_ref, *rest
+):
+    outs = rest[:-8]
+    x_buf, dy_buf, h_buf, xs_buf, xt_buf, in_sems, xs_sems, xt_sems = rest[-8:]
+    parts, length, wide = x_buf.shape
+    _, chip, _ = core_and_chip()
+    arrivals = []
+    for s in range(parts):
+        sources = (
+            (columns_of(x_hbm, chip ^ s, wide), x_buf),
+            (columns_of(dy_hbm, chip ^ s, wide), dy_buf),
+            (rows_of(h_hbm, chip ^ s, wide), h_buf),
+        )
+        three = [
+            pltpu.make_async_copy(source, buf.at[s], in_sems.at[k, s])
+            for k, (source, buf) in enumerate(sources)
+        ]
+        for copy in three:
+            copy.start()
+        arrivals.append(three)
+    heads = cumt_ref.shape[0]
+    size = parts * wide // heads
+    pad = jnp.zeros((LANES - heads, length), F32)
+    cum = jnp.concatenate([cumt_ref[...], pad], axis=0).T
+    into_end = jnp.exp(cum[length - 1 : length] - cum_ref[...])
+    table = jnp.concatenate([halves(jnp.exp(cum)), halves(into_end)], axis=0)
+    carried = jnp.zeros(carried_ref.shape, F32)
+    token_ref[...] = jnp.zeros_like(token_ref)
+    targets = [(out, at) for out in outs for at in range(0, out.shape[0], wide)]
+    leaving = []
+    for s in range(parts):
+        for copy in arrivals[s]:
+            copy.wait()
+        for t in range(wide // LANES):
+            span = slice(t * LANES, (t + 1) * LANES)
+            scale = dot(table, to_lanes((chip ^ s) * (wide // LANES) + t, size), 1, 0)
+            x_f = x_buf[s, :, span].astype(F32)
+            xt_buf[s, span, :] = x_f.T.astype(BF16)
+            xs_buf[s, :, span] = (x_f * scale[length:]).astype(BF16)
+            dys = (dy_buf[s, :, span].astype(F32) * scale[:length]).astype(BF16)
+            carried = carried + dot(dys, h_buf[s, span, :], 1, 0)
+        out, at = targets[s]
+        pair = [
+            pltpu.make_async_copy(xs_buf.at[s], columns_of(xs_hbm, chip ^ s, wide), xs_sems.at[s]),
+            pltpu.make_async_copy(xt_buf.at[s], out.at[pl.ds(at, wide), :], xt_sems.at[s]),
+        ]
+        for copy in pair:
+            copy.start()
+        leaving += pair
+    carried_ref[...] = carried
+    for copy in leaving:
+        copy.wait()
+
+
+def early(kernel, outs, raw_outs, cost, args, raw_args, scratch):
+    def spec(raw):
+        return pl.BlockSpec(memory_space=pl.ANY if raw else pltpu.VMEM)
+
+    return pl.pallas_call(
+        kernel,
+        out_shape=outs,
+        in_specs=[spec(i in raw_args) for i in range(len(args))],
+        out_specs=[spec(i in raw_outs) for i in range(len(outs))],
+        scratch_shapes=scratch,
+        cost_estimate=pl.CostEstimate(
+            flops=int(cost * 3e9), bytes_accessed=1000, transcendentals=0
+        ),
+        compiler_params=pltpu.CompilerParams(vmem_limit_bytes=60 * 1024 * 1024),
+    )(*args)
 
 
 def join_kernel(ranges, *refs):
@@ -607,7 +715,10 @@
     in_rows = width // LANES * capacity
     blocks = [1, 1, 2] if n_chip == 4 else [1] * n_chip
     groups = [2, 2] if n_dp == 4 else [1] * n_dp
-    cumt, cum, dyt, rows, *deals = call(
+    cuts = 4
+    wide = width // cuts
+    dma = pltpu.SemaphoreType.DMA
+    cumt, cum, dyt, rows, *deals = early(
         lambda *refs: prep_kernel(len(groups), *refs),
         [
             shape((heads, length), F32),
@@ -616,11 +727,19 @@
             shape((in_rows, LANES), BF16),
         ]
         + [shape((k * grad_rows, LANES), BF16) for k in groups],
+        (2,),
         1.5,
         (x, dy, ldt, stept, slot_rows[0], slot_counts, slot_gates[0]),
-        scratch=[pltpu.VMEM((n_dp, grad_rows, LANES), BF16)],
-        fetch=(0, 1, 2, 3),
-        limit=60,
+        (0, 1),
+        [
+            pltpu.VMEM((n_dp, grad_rows, LANES), BF16),
+            pltpu.VMEM((cuts, length, wide), BF16),
+            pltpu.VMEM((cuts, length, wide), BF16),
+            pltpu.VMEM((cuts, wide, length), BF16),
+            pltpu.VMEM((2 * heads, LANES), BF16),
+            dma((2, cuts)),
+            dma((cuts + 1,)),
+        ],
     )
     w_far = xored(w_half, "dp", n_dp // 2)
     mine = gathered(w_half, "dp", n_dp // 2)[1:]
@@ -630,23 +749,43 @@
     while 2 ** (len(rows_in) - 1) < n_chip:
         rows_sent = joined(rows_in, (w_copy,)) if rows_in[1:] else rows
         rows_in.append(xored(rows_sent, "tm", 2 ** len(rows_in)))
-    xs, carried, scaled, *xt = call(
-        scale_kernel,
-        [shape((length, width), BF16), shape((length, half), F32), shape((8, LANES), F32)]
-        + [shape((k * width // n_chip, length), BF16) for k in blocks],
-        1.5,
-        (x, dy, h_in, cumt, cum),
-        after=(rows,),
-        scratch=[pltpu.VMEM((width, length), BF16)],
-        fetch=(0, 1, 2, 3, 4),
-        limit=60,
-    )
+    scale_outs = [shape((length, width), BF16), shape((length, half), F32), shape((8, LANES), F32)]
+    scale_outs += [shape((k * width // n_chip, length), BF16) for k in blocks]
+    if n_chip == cuts:
+        xs, carried, scaled, *xt = early(
+            scale4_kernel,
+            scale_outs,
+            (0, 3, 4, 5),
+            1.5,
+            (x, dy, h_in, cumt, cum),
+            (0, 1, 2),
+            [
+                pltpu.VMEM((cuts, length, wide), BF16),
+                pltpu.VMEM((cuts, length, wide), BF16),
+                pltpu.VMEM((cuts, wide, half), BF16),
+                pltpu.VMEM((cuts, length, wide), BF16),
+                pltpu.VMEM((cuts, wide, length), BF16),
+                dma((3, cuts)),
+                dma((cuts,)),
+                dma((cuts,)),
+            ],
+        )
+    else:
+        xs, carried, scaled, *xt = call(
+            scale_kernel,
+            scale_outs,
+            1.5,
+            (x, dy, h_in, cumt, cum),
+            scratch=[pltpu.VMEM((width, length), BF16)],
+            fetch=(0, 1, 2, 3, 4),
+            limit=60,
+        )
     if n_dp == 4:
         one = (0, grad_rows), (grad_rows, 2 * grad_rows)
         over_2 = xored(deals[1], "dp", 2)
-        early = (over_2,)
+        hops = (over_2,)
     else:
-        early = ()
+        hops = ()
         source, spans = deals[:1] + [xored(d, "dp", s + 1) for s, d in enumerate(deals[1:])], None
     other = swapped(stacked(mine, after=(rows_in[-1], scaled), cost=1.0))
     w_whole, bc, keep, send = call(
@@ -682,9 +821,9 @@
     dxs, exs, owns = [], [], []
     if n_dp == 4:
         over_1 = xored(joined([deals[0], over_2], (weighted,), [one[1], one[1]]), "dp", 1)
-        early += (over_1,)
+        hops += (over_1,)
         source, spans = [deals[0], over_1, over_2, over_1], [one[0], one[0], one[0], one[1]]
-    held = (weighted, *early)
+    held = (weighted, *hops)
     arrived = []
     bit = 1
     while bit < n_chip:

time: 73.3 us -> 74.1 us (1.011)
  Pallas kernels: 23.7 us -> 26.3 us
  starting transfers between devices: 29.4 us -> 27.2 us
    pallas_call x0 -> x2, Pallas kernels: none -> 10.7 us  [early(): pl.pallas_call(kernel, out_shape=outs, in_specs=[spec(i in raw_args) for...]
    pallas_call x27 -> x25, Pallas kernels: 20.7 us -> 12.7 us  [call(): pl.pallas_call(body, out_shape=outs, in_specs=specs + [pl.BlockSpec(memor...]
    ppermute x25, starting transfers between devices: 27 us -> 24.4 us  [xored(): return lax.ppermute(array, axis, [(i, i ^ mask) for i in range(count)])]
  transfers between devices with their start and end apart: 27 -> 27, of which waited for: 11 -> 13; matrix products, arithmetic and copies ran while one was open for 0% -> 0% of each run, Pallas kernels for 29% -> 32%
where the time goes in v16:
time: 74.1 us; the launch traced here: 73.8 us
  starting transfers between devices  27.2 us (37%)
  Pallas kernels  26.3 us (35%)
  waiting for transfers between devices  16 us (22%)
  local copies, waits for them, and re-layouts  2.6 us (4%)
  between operations  1.74 us (2%)
    ppermute x25, starting transfers between devices, xored(): return lax.ppermute(array, axis, [(i, i ^ mask) for i in range(count)])  24.4 us
    ppermute x25, waiting for transfers between devices, xored(): return lax.ppermute(array, axis, [(i, i ^ mask) for i in range(count)])  16 us
    pallas_call x25, Pallas kernels, call(): pl.pallas_call(body, out_shape=outs, in_specs=specs + [pl.BlockSpec(memor...  12.7 us
    pallas_call x2, Pallas kernels, early(): pl.pallas_call(kernel, out_shape=outs, in_specs=[spec(i in raw_args) for...  10.7 us
    pallas_call x1, Pallas kernels, expert(): pl.pallas_call(body, out_shape=shape(out, BF16), grid=(width // depth,),...  2.92 us
    ppermute x2, starting transfers between devices, per_device(): arrived.append(lax.ppermute(climbs[-1], 'tm', moves))  2.75 us
    unnamed x44, local copies, waits for them, and re-layouts  1.66 us
  transfers between devices with their start and end apart: 27, of which 13 were waited for; matrix products, arithmetic and copies ran while one was open for 0% of the time, Pallas kernels for 32%

profile of v16, /device:TPU:0, one launch (start us, length us, event | category | flops | bytes accessed | tf_op | source)
XLA Modules:
  0.0 73.8 jit_solution(12906874367658912228)
XLA Ops:
  1.6 4.1 %collective-permute-start.1 = (bf16[320,256]{1,0:T(8,128)(2,1)S(1)}, bf16[320,256]{1,0:T(8,128)(2,1)S(1)}, u32[]{:S(2)}, u32[]{:S(2)}) collective-permute-start(bf16[320,256]{1,0:T(8,128)(2,1)S(1)} %constant_dynamic-slice_fusion), channel_id=1, source_target_pairs={{0,2},{1,3},{2,0},{3,1},{4,6},{5,7},{6,4},{7,5},{8,10},{9,11},{10,... | collective-permute-start | bytes 491528 | tf_op jit(solution)/shard_map/ppermute | solution.py:663
  6.3 5.1 %shard_map.146 = (f32[40,128]{1,0:T(8,128)}, f32[128,128]{1,0:T(8,128)}, bf16[2640,128]{1,0:T(8,128)(2,1)}, bf16[320,128]{1,0:T(8,128)(2,1)}, bf16[160,128]{1,0:T(8,128)(2,1)}, /*index=5*/bf16[160,128]{1,0:T(8,128)(2,1)}) custom-call(bf16[128,2560]{1,0:T(8,128)(2,1)} %bitcast.37, bf16[128,2560]{1,0:T(8,128)(2,1)} %bitcast.33, f32[40,128]{1,0:T(8,128)} %bitcast.54, ...), custom_call_target="tpu_custom_call" | custom-call | flops 4499999744 | bytes 1000 | tf_op jit(solution)/shard_map/pallas_call | solution.py:286
  11.4 1.6 %collective-permute-start.3 = (bf16[320,128]{1,0:T(8,128)(2,1)}, bf16[320,128]{1,0:T(8,128)(2,1)S(1)}, u32[]{:S(2)}, u32[]{:S(2)}) collective-permute-start(bf16[320,128]{1,0:T(8,128)(2,1)} %get-tuple-element.46.refs_1_.refs_0_), channel_id=1, source_target_pairs={{0,8},{4,12},{8,0},{12,4},{16,24},{20,28},{24,16},{28,20},{1,9},{5... | collective-permute-start | bytes 245768 | tf_op jit(solution)/shard_map/ppermute | solution.py:663
  13.0 1.6 %collective-permute-start = (bf16[320,256]{1,0:T(8,128)(2,1)S(1)}, bf16[320,256]{1,0:T(8,128)(2,1)S(1)}, u32[]{:S(2)}, u32[]{:S(2)}) collective-permute-start(bf16[320,256]{1,0:T(8,128)(2,1)S(1)} %constant_dynamic-slice_fusion), channel_id=1, source_target_pairs={{0,1},{1,0},{2,3},{3,2},{4,5},{5,4},{6,7},{7,6},{8,9},{9,8},{10,11... | collective-permute-start | bytes 491528 | tf_op jit(solution)/shard_map/ppermute | solution.py:663
  16.2 1.6 %collective-permute-start.4 = (bf16[640,128]{1,0:T(8,128)(2,1)S(1)}, bf16[640,128]{1,0:T(8,128)(2,1)S(1)}, u32[]{:S(2)}, u32[]{:S(2)}) collective-permute-start(bf16[640,128]{1,0:T(8,128)(2,1)S(1)} %shard_map.148), channel_id=1, source_target_pairs={{0,16},{4,20},{8,24},{12,28},{16,0},{20,4},{24,8},{28,12},{1,17},{... | collective-permute-start | bytes 491528 | tf_op jit(solution)/shard_map/ppermute | solution.py:663
  17.8 5.6 %shard_map.149 = (bf16[128,2560]{1,0:T(8,128)(2,1)}, f32[128,128]{1,0:T(8,128)}, f32[8,128]{1,0:T(8,128)}, bf16[640,128]{1,0:T(8,128)(2,1)}, bf16[640,128]{1,0:T(8,128)(2,1)}, /*index=5*/bf16[1280,128]{1,0:T(8,128)(2,1)}) custom-call(bf16[128,2560]{1,0:T(8,128)(2,1)} %bitcast.38, bf16[128,2560]{1,0:T(8,128)(2,1)} %bitcast.34, bf16[2560,128]{1,0:T(8,128)(2,1)} %bitcast.43, ...), custom_call_target="tpu_custom_call" | custom-call | flops 4499999744 | bytes 1000 | tf_op jit(solution)/shard_map/pallas_call | solution.py:286
  24.2 1.9 %collective-permute-done.5.refs_6_ = bf16[3,320,256]{2,1,0:T(8,128)(2,1)S(1)} collective-permute-done((bf16[3,320,256]{2,1,0:T(8,128)(2,1)S(1)}, bf16[3,320,256]{2,1,0:T(8,128)(2,1)S(1)}, u32[]{:S(2)}, u32[]{:S(2)}) %collective-permute-start.5) | collective-permute-done | bytes 491552 | tf_op jit(solution)/shard_map/ppermute | solution.py:663
  27.3 1.5 %collective-permute-done.6.refs_1_.refs_3_ = bf16[1328,128]{1,0:T(8,128)(2,1)S(1)} collective-permute-done((bf16[1328,128]{1,0:T(8,128)(2,1)S(1)}, bf16[1328,128]{1,0:T(8,128)(2,1)S(1)}, u32[]{:S(2)}, u32[]{:S(2)}) %collective-permute-start.6) | collective-permute-done | bytes 340000 | tf_op jit(solution)/shard_map/ppermute | solution.py:663
  29.3 1.5 %collective-permute-start.7 = (bf16[1328,128]{1,0:T(8,128)(2,1)S(1)}, bf16[1328,128]{1,0:T(8,128)(2,1)S(1)}, u32[]{:S(2)}, u32[]{:S(2)}) collective-permute-start(bf16[1328,128]{1,0:T(8,128)(2,1)S(1)} %shard_map.152.refs_3_.refs_4_.refs_0_), channel_id=1, source_target_pairs={{0,8},{4,12},{8,0},{12,4},{16,24},{20,28},{24,16},{28,20},{1,9},{5... | collective-permute-start | bytes 1019912 | tf_op jit(solution)/shard_map/ppermute | solution.py:832
  30.8 2.4 %collective-permute-start.9 = (bf16[160,128]{1,0:T(8,128)(2,1)S(1)}, bf16[160,128]{1,0:T(8,128)(2,1)S(1)}, u32[]{:S(2)}, u32[]{:S(2)}) collective-permute-start(bf16[160,128]{1,0:T(8,128)(2,1)S(1)} %copy-done.17), channel_id=1, source_target_pairs={{0,2},{1,3},{2,0},{3,1},{4,6},{5,7},{6,4},{7,5},{8,10},{9,11},{10,... | collective-permute-start | bytes 122888 | tf_op jit(solution)/shard_map/ppermute | solution.py:663
  33.8 2.9 %shard_map.154.refs_2_.refs_0_ = bf16[896,128]{1,0:T(8,128)(2,1)S(1)} custom-call(bf16[4,320,128]{2,1,0:T(8,128)(2,1)S(1)} %bitcast.32, bf16[4,320,128]{2,1,0:T(8,128)(2,1)S(1)} %collective-permute-done.8.refs_1_, bf16[2560,896]{1,0:T(8,128)(2,1)S(1)} %bitcast.27, bf16[2560,896]{1,0:T(8,128)(2,1)S(1)} %bitcast.30, ...), custom_call_target="tpu_custom_call" | custom-call | flops 1000000000 | bytes 1000 | tf_op jit(solution)/shard_map/pallas_call | solution.py:619
  37.4 1.6 %collective-permute-start.15 = (bf16[896,128]{1,0:T(8,128)(2,1)S(1)}, bf16[896,128]{1,0:T(8,128)(2,1)S(1)}, u32[]{:S(2)}, u32[]{:S(2)}) collective-permute-start(bf16[896,128]{1,0:T(8,128)(2,1)S(1)} %shard_map.154.refs_2_.refs_0_), channel_id=1, source_target_pairs={{0,2},{1,3},{2,0},{3,1},{4,6},{5,7},{6,4},{7,5},{8,10},{9,11},{10,... | collective-permute-start | bytes 688136 | tf_op jit(solution)/shard_map/ppermute | solution.py:663
  39.0 1.3 %collective-permute-start.16 = (bf16[896,128]{1,0:T(8,128)(2,1)S(1)}, bf16[896,128]{1,0:T(8,128)(2,1)S(1)}, u32[]{:S(2)}, u32[]{:S(2)}) collective-permute-start(bf16[896,128]{1,0:T(8,128)(2,1)S(1)} %shard_map.154.refs_2_.refs_0_), channel_id=1, source_target_pairs={{0,1},{1,0},{2,3},{3,2},{4,5},{5,4},{6,7},{7,6},{8,9},{9,8},{10,11... | collective-permute-start | bytes 688136 | tf_op jit(solution)/shard_map/ppermute | solution.py:663
  40.2 2.1 %collective-permute-done.10.refs_4_.refs_1_.refs_3_ = bf16[160,128]{1,0:T(8,128)(2,1)S(1)} collective-permute-done((bf16[160,128]{1,0:T(8,128)(2,1)S(1)}, bf16[160,128]{1,0:T(8,128)(2,1)S(1)}, u32[]{:S(2)}, u32[]{:S(2)}) %collective-permute-start.10) | collective-permute-done | bytes 40992 | tf_op jit(solution)/shard_map/ppermute | solution.py:663
  42.6 1.2 %collective-permute-start.11 = (bf16[1328,128]{1,0:T(8,128)(2,1)S(1)}, bf16[1328,128]{1,0:T(8,128)(2,1)S(1)}, u32[]{:S(2)}, u32[]{:S(2)}) collective-permute-start(bf16[1328,128]{1,0:T(8,128)(2,1)S(1)} %shard_map.156.refs_7_.refs_4_.refs_2_), channel_id=1, source_target_pairs={{0,16},{4,20},{8,24},{12,28},{16,0},{20,4},{24,8},{28,12},{1,17},{... | collective-permute-start | bytes 1019912 | tf_op jit(solution)/shard_map/ppermute | solution.py:832
  44.5 2.0 %shard_map.157 = (f32[128,1280]{1,0:T(8,128)S(1)}, f32[128,128]{1,0:T(8,128)S(1)}, f32[20,128]{1,0:T(8,128)S(1)}, f32[20,128]{1,0:T(8,128)S(1)}) custom-call(bf16[128,2560]{1,0:T(8,128)(2,1)S(1)} %bitcast.40, bf16[128,2560]{1,0:T(8,128)(2,1)S(1)} %bitcast.35, bf16[128,256]{1,0:T(8,128)(2,1)S(1)} %get-tuple-element.50.refs_2_.refs_1_, ...), custom_call_target="tpu_custom_call" | custom-call | flops 2100000000 | bytes 1000 | tf_op jit(solution)/shard_map/pallas_call | solution.py:81
  46.4 2.0 %shard_map.158 = (f32[128,1280]{1,0:T(8,128)S(1)}, f32[128,128]{1,0:T(8,128)S(1)}, f32[20,128]{1,0:T(8,128)S(1)}, f32[20,128]{1,0:T(8,128)S(1)}) custom-call(bf16[128,2560]{1,0:T(8,128)(2,1)S(1)} %bitcast.41, bf16[128,2560]{1,0:T(8,128)(2,1)S(1)} %bitcast.36, bf16[128,256]{1,0:T(8,128)(2,1)S(1)} %get-tuple-element.50.refs_2_.refs_1_, ...), custom_call_target="tpu_custom_call" | custom-call | flops 2100000000 | bytes 1000 | tf_op jit(solution)/shard_map/pallas_call | solution.py:81
  54.9 3.1 %collective-permute-done.19.refs_1_.refs_4_ = bf16[1,128,256]{2,1,0:T(8,128)(2,1)S(1)} collective-permute-done((bf16[1,128,256]{2,1,0:T(8,128)(2,1)S(1)}, bf16[1,128,256]{2,1,0:T(8,128)(2,1)S(1)}, u32[]{:S(2)}, u32[]{:S(2)}) %collective-permute-start.19) | collective-permute-done | bytes 65568 | tf_op jit(solution)/shard_map/ppermute | solution.py:663
  59.2 2.6 %shard_map.167 = (bf16[128,2560]{1,0:T(8,128)(2,1)}, f32[40,128]{1,0:T(8,128)}, f32[40,128]{1,0:T(8,128)}, f32[8,128]{1,0:T(8,128)S(1)}) custom-call(bf16[128,2560]{1,0:T(8,128)(2,1)S(1)} %bitcast.42, bf16[128,256]{1,0:T(8,128)(2,1)S(1)} %get-tuple-element.50.refs_2_.refs_1_, f32[40,128]{1,0:T(8,128)S(1)} %copy-done.14, f32[40,128]{1,0:T(8,128)S(1)} %bitcast.52, ...), custom_call_target="tpu_custom_call" | custom-call | flops 3000000000 | bytes 1000 | tf_op jit(solution)/shard_map/pallas_call | solution.py:81
  61.8 1.2 %collective-permute-done.20.refs_5_ = bf16[2,128,256]{2,1,0:T(8,128)(2,1)S(1)} collective-permute-done((bf16[2,128,256]{2,1,0:T(8,128)(2,1)S(1)}, bf16[2,128,256]{2,1,0:T(8,128)(2,1)S(1)}, u32[]{:S(2)}, u32[]{:S(2)}) %collective-permute-start.20) | collective-permute-done | bytes 131104 | tf_op jit(solution)/shard_map/ppermute | solution.py:663
  63.7 1.4 %collective-permute-done.22.refs_1_ = bf16[320,256]{1,0:T(8,128)(2,1)S(1)} collective-permute-done((bf16[320,256]{1,0:T(8,128)(2,1)S(1)}, bf16[320,256]{1,0:T(8,128)(2,1)S(1)}, u32[]{:S(2)}, u32[]{:S(2)}) %collective-permute-start.22) | collective-permute-done | bytes 163872 | tf_op jit(solution)/shard_map/ppermute | solution.py:663
  65.5 1.7 %collective-permute-start.24 = (bf16[80,256]{1,0:T(8,128)(2,1)S(1)}, bf16[80,256]{1,0:T(8,128)(2,1)S(1)}, u32[]{:S(2)}, u32[]{:S(2)}) collective-permute-start(bf16[80,256]{1,0:T(8,128)(2,1)S(1)} %get-tuple-element.81), channel_id=1, source_target_pairs={{0,2},{1,3},{2,0},{3,1},{4,6},{5,7},{6,4},{7,5},{8,10},{9,11},{10,... | collective-permute-start | bytes 122888 | tf_op jit(solution)/shard_map/ppermute | solution.py:663
  67.3 2.3 %collective-permute-start.25 = (bf16[80,256]{1,0:T(8,128)(2,1)S(1)}, bf16[80,256]{1,0:T(8,128)(2,1)S(1)}, u32[]{:S(2)}, u32[]{:S(2)}) collective-permute-start(bf16[80,256]{1,0:T(8,128)(2,1)S(1)} %get-tuple-element.82), channel_id=1, source_target_pairs={{0,3},{1,2},{2,1},{3,0},{4,7},{5,6},{6,5},{7,4},{8,11},{9,10},{10,... | collective-permute-start | bytes 122888 | tf_op jit(solution)/shard_map/ppermute | solution.py:663
  69.6 2.4 %shard_map.172 = (bf16[896,640]{1,0:T(8,128)(2,1)}, f32[8,128]{1,0:T(8,128)S(1)}) custom-call(bf16[896,128]{1,0:T(8,128)(2,1)S(1)} %shard_map.154.refs_2_.refs_0_, bf16[896,128]{1,0:T(8,128)(2,1)S(1)} %collective-permute-done.16.refs_8_.refs_1_, bf16[896,128]{1,0:T(8,128)(2,1)S(1)} %shard_map.168.refs_2_, ...), custom_call_target="tpu_custom_call" | custom-call | flops 3000000000 | bytes 1000 | tf_op jit(solution)/shard_map/pallas_call | solution.py:81
  (106 shorter events, 17.6 us)
Async XLA Ops:
  1.6 13.0 %collective-permute-start.1 = (bf16[320,256]{1,0:T(8,128)(2,1)S(1)}, bf16[320,256]{1,0:T(8,128)(2,1)S(1)}, u32[]{:S(2)}, u32[]{:S(2)}) collective-permute-start(bf16[320,256]{1,0:T(8,128)(2,1)S(1)} %constant_dynamic-slice_fusion), channel_id=1, source_target_pairs={{0,2},{1,3},{2,0},{3,1},{4,6},{5,7},{6,4},{7,5},{8,10},{9,11},{10,... | collective-permute-start | bytes 491528 | tf_op jit(solution)/shard_map/ppermute | solution.py:663
  11.4 4.7 %collective-permute-start.3 = (bf16[320,128]{1,0:T(8,128)(2,1)}, bf16[320,128]{1,0:T(8,128)(2,1)S(1)}, u32[]{:S(2)}, u32[]{:S(2)}) collective-permute-start(bf16[320,128]{1,0:T(8,128)(2,1)} %get-tuple-element.46.refs_1_.refs_0_), channel_id=1, source_target_pairs={{0,8},{4,12},{8,0},{12,4},{16,24},{20,28},{24,16},{28,20},{1,9},{5... | collective-permute-start | bytes 245768 | tf_op jit(solution)/shard_map/ppermute | solution.py:663
  13.0 10.3 %collective-permute-start = (bf16[320,256]{1,0:T(8,128)(2,1)S(1)}, bf16[320,256]{1,0:T(8,128)(2,1)S(1)}, u32[]{:S(2)}, u32[]{:S(2)}) collective-permute-start(bf16[320,256]{1,0:T(8,128)(2,1)S(1)} %constant_dynamic-slice_fusion), channel_id=1, source_target_pairs={{0,1},{1,0},{2,3},{3,2},{4,5},{5,4},{6,7},{7,6},{8,9},{9,8},{10,11... | collective-permute-start | bytes 491528 | tf_op jit(solution)/shard_map/ppermute | solution.py:663
  15.5 7.9 %collective-permute-start.2 = (bf16[320,256]{1,0:T(8,128)(2,1)S(1)}, bf16[320,256]{1,0:T(8,128)(2,1)S(1)}, u32[]{:S(2)}, u32[]{:S(2)}) collective-permute-start(bf16[320,256]{1,0:T(8,128)(2,1)S(1)} %shard_map.147.refs_2_.refs_1_.refs_4_), channel_id=1, source_target_pairs={{0,1},{1,0},{2,3},{3,2},{4,5},{5,4},{6,7},{7,6},{8,9},{9,8},{10,11... | collective-permute-start | bytes 491528 | tf_op jit(solution)/shard_map/ppermute | solution.py:663
  16.2 7.2 %collective-permute-start.4 = (bf16[640,128]{1,0:T(8,128)(2,1)S(1)}, bf16[640,128]{1,0:T(8,128)(2,1)S(1)}, u32[]{:S(2)}, u32[]{:S(2)}) collective-permute-start(bf16[640,128]{1,0:T(8,128)(2,1)S(1)} %shard_map.148), channel_id=1, source_target_pairs={{0,16},{4,20},{8,24},{12,28},{16,0},{20,4},{24,8},{28,12},{1,17},{... | collective-permute-start | bytes 491528 | tf_op jit(solution)/shard_map/ppermute | solution.py:663
  24.1 1.9 %collective-permute-start.5 = (bf16[3,320,256]{2,1,0:T(8,128)(2,1)S(1)}, bf16[3,320,256]{2,1,0:T(8,128)(2,1)S(1)}, u32[]{:S(2)}, u32[]{:S(2)}) collective-permute-start(bf16[3,320,256]{2,1,0:T(8,128)(2,1)S(1)} %bitcast.47), channel_id=1, source_target_pairs={{0,4},{4,0},{8,12},{12,8},{16,20},{20,16},{24,28},{28,24},{1,5},{5... | collective-permute-start | bytes 1474568 | tf_op jit(solution)/shard_map/ppermute | solution.py:663
  29.1 4.6 %collective-permute-start.8 = (bf16[4,320,128]{2,1,0:T(8,128)(2,1)S(1)}, bf16[4,320,128]{2,1,0:T(8,128)(2,1)S(1)}, u32[]{:S(2)}, u32[]{:S(2)}) collective-permute-start(bf16[4,320,128]{2,1,0:T(8,128)(2,1)S(1)} %bitcast.31), channel_id=1, source_target_pairs={{0,4},{4,0},{8,12},{12,8},{16,20},{20,16},{24,28},{28,24},{1,5},{5... | collective-permute-start | bytes 983048 | tf_op jit(solution)/shard_map/ppermute | solution.py:663
  29.3 10.9 %collective-permute-start.7 = (bf16[1328,128]{1,0:T(8,128)(2,1)S(1)}, bf16[1328,128]{1,0:T(8,128)(2,1)S(1)}, u32[]{:S(2)}, u32[]{:S(2)}) collective-permute-start(bf16[1328,128]{1,0:T(8,128)(2,1)S(1)} %shard_map.152.refs_3_.refs_4_.refs_0_), channel_id=1, source_target_pairs={{0,8},{4,12},{8,0},{12,4},{16,24},{20,28},{24,16},{28,20},{1,9},{5... | collective-permute-start | bytes 1019912 | tf_op jit(solution)/shard_map/ppermute | solution.py:832
  30.8 5.9 %collective-permute-start.9 = (bf16[160,128]{1,0:T(8,128)(2,1)S(1)}, bf16[160,128]{1,0:T(8,128)(2,1)S(1)}, u32[]{:S(2)}, u32[]{:S(2)}) collective-permute-start(bf16[160,128]{1,0:T(8,128)(2,1)S(1)} %copy-done.17), channel_id=1, source_target_pairs={{0,2},{1,3},{2,0},{3,1},{4,6},{5,7},{6,4},{7,5},{8,10},{9,11},{10,... | collective-permute-start | bytes 122888 | tf_op jit(solution)/shard_map/ppermute | solution.py:663
  33.2 10.6 %collective-permute-start.13 = (bf16[1280,128]{1,0:T(8,128)(2,1)S(1)}, bf16[1280,128]{1,0:T(8,128)(2,1)S(1)}, u32[]{:S(2)}, u32[]{:S(2)}) collective-permute-start(bf16[1280,128]{1,0:T(8,128)(2,1)S(1)} %copy-done.16), channel_id=1, source_target_pairs={{0,16},{4,20},{8,24},{12,28},{16,0},{20,4},{24,8},{28,12},{1,17},{... | collective-permute-start | bytes 983048 | tf_op jit(solution)/shard_map/ppermute | solution.py:663
  36.8 5.6 %collective-permute-start.10 = (bf16[160,128]{1,0:T(8,128)(2,1)S(1)}, bf16[160,128]{1,0:T(8,128)(2,1)S(1)}, u32[]{:S(2)}, u32[]{:S(2)}) collective-permute-start(bf16[160,128]{1,0:T(8,128)(2,1)S(1)} %shard_map.155), channel_id=1, source_target_pairs={{0,1},{1,0},{2,3},{3,2},{4,5},{5,4},{6,7},{7,6},{8,9},{9,8},{10,11... | collective-permute-start | bytes 122888 | tf_op jit(solution)/shard_map/ppermute | solution.py:663
  37.4 12.5 %collective-permute-start.15 = (bf16[896,128]{1,0:T(8,128)(2,1)S(1)}, bf16[896,128]{1,0:T(8,128)(2,1)S(1)}, u32[]{:S(2)}, u32[]{:S(2)}) collective-permute-start(bf16[896,128]{1,0:T(8,128)(2,1)S(1)} %shard_map.154.refs_2_.refs_0_), channel_id=1, source_target_pairs={{0,2},{1,3},{2,0},{3,1},{4,6},{5,7},{6,4},{7,5},{8,10},{9,11},{10,... | collective-permute-start | bytes 688136 | tf_op jit(solution)/shard_map/ppermute | solution.py:663
  39.0 11.3 %collective-permute-start.16 = (bf16[896,128]{1,0:T(8,128)(2,1)S(1)}, bf16[896,128]{1,0:T(8,128)(2,1)S(1)}, u32[]{:S(2)}, u32[]{:S(2)}) collective-permute-start(bf16[896,128]{1,0:T(8,128)(2,1)S(1)} %shard_map.154.refs_2_.refs_0_), channel_id=1, source_target_pairs={{0,1},{1,0},{2,3},{3,2},{4,5},{5,4},{6,7},{7,6},{8,9},{9,8},{10,11... | collective-permute-start | bytes 688136 | tf_op jit(solution)/shard_map/ppermute | solution.py:663
  42.6 8.7 %collective-permute-start.11 = (bf16[1328,128]{1,0:T(8,128)(2,1)S(1)}, bf16[1328,128]{1,0:T(8,128)(2,1)S(1)}, u32[]{:S(2)}, u32[]{:S(2)}) collective-permute-start(bf16[1328,128]{1,0:T(8,128)(2,1)S(1)} %shard_map.156.refs_7_.refs_4_.refs_2_), channel_id=1, source_target_pairs={{0,16},{4,20},{8,24},{12,28},{16,0},{20,4},{24,8},{28,12},{1,17},{... | collective-permute-start | bytes 1019912 | tf_op jit(solution)/shard_map/ppermute | solution.py:832
  43.8 7.4 %collective-permute-start.14 = (bf16[1280,128]{1,0:T(8,128)(2,1)S(1)}, bf16[1280,128]{1,0:T(8,128)(2,1)S(1)}, u32[]{:S(2)}, u32[]{:S(2)}) collective-permute-start(bf16[1280,128]{1,0:T(8,128)(2,1)S(1)} %shard_map.162), channel_id=1, source_target_pairs={{0,8},{4,12},{8,0},{12,4},{16,24},{20,28},{24,16},{28,20},{1,9},{5... | collective-permute-start | bytes 983048 | tf_op jit(solution)/shard_map/ppermute | solution.py:663
  44.4 4.2 %collective-permute-start.12 = (bf16[320,128]{1,0:T(8,128)(2,1)S(1)}, bf16[320,128]{1,0:T(8,128)(2,1)S(1)}, u32[]{:S(2)}, u32[]{:S(2)}) collective-permute-start(bf16[320,128]{1,0:T(8,128)(2,1)S(1)} %shard_map.160.refs_0_), channel_id=1, source_target_pairs={{0,4},{4,0},{8,12},{12,8},{16,20},{20,16},{24,28},{28,24},{1,5},{5... | collective-permute-start | bytes 245768 | tf_op jit(solution)/shard_map/ppermute | solution.py:663
  51.7 6.9 %collective-permute-start.18 = (bf16[640,128]{1,0:T(8,128)(2,1)S(1)}, bf16[640,128]{1,0:T(8,128)(2,1)S(1)}, u32[]{:S(2)}, u32[]{:S(2)}) collective-permute-start(bf16[640,128]{1,0:T(8,128)(2,1)S(1)} %shard_map.161.refs_5_.refs_0_), channel_id=1, source_target_pairs={{0,16},{4,20},{8,24},{12,28},{16,0},{20,4},{24,8},{28,12},{1,17},{... | collective-permute-start | bytes 491528 | tf_op jit(solution)/shard_map/ppermute | solution.py:663
  53.6 4.3 %collective-permute-start.19 = (bf16[1,128,256]{2,1,0:T(8,128)(2,1)S(1)}, bf16[1,128,256]{2,1,0:T(8,128)(2,1)S(1)}, u32[]{:S(2)}, u32[]{:S(2)}) collective-permute-start(bf16[1,128,256]{2,1,0:T(8,128)(2,1)S(1)} %bitcast.48), channel_id=1, source_target_pairs={{0,8},{4,12},{8,0},{12,4},{16,24},{20,28},{24,16},{28,20},{1,9},{5... | collective-permute-start | bytes 196616 | tf_op jit(solution)/shard_map/ppermute | solution.py:663
  54.2 8.8 %collective-permute-start.21 = (bf16[896,128]{1,0:T(8,128)(2,1)S(1)}, bf16[896,128]{1,0:T(8,128)(2,1)S(1)}, u32[]{:S(2)}, u32[]{:S(2)}) collective-permute-start(bf16[896,128]{1,0:T(8,128)(2,1)S(1)} %shard_map.168.refs_2_), channel_id=1, source_target_pairs={{0,1},{1,0},{2,3},{3,2},{4,5},{5,4},{6,7},{7,6},{8,9},{9,8},{10,11... | collective-permute-start | bytes 688136 | tf_op jit(solution)/shard_map/ppermute | solution.py:663
  58.0 5.0 %collective-permute-start.20 = (bf16[2,128,256]{2,1,0:T(8,128)(2,1)S(1)}, bf16[2,128,256]{2,1,0:T(8,128)(2,1)S(1)}, u32[]{:S(2)}, u32[]{:S(2)}) collective-permute-start(bf16[2,128,256]{2,1,0:T(8,128)(2,1)S(1)} %shard_map.165.refs_2_), channel_id=1, source_target_pairs={{0,16},{4,20},{8,24},{12,28},{16,0},{20,4},{24,8},{28,12},{1,17},{... | collective-permute-start | bytes 393224 | tf_op jit(solution)/shard_map/ppermute | solution.py:663
  58.6 10.9 %collective-permute-start.26 = (bf16[1280,128]{1,0:T(8,128)(2,1)S(1)}, bf16[1280,128]{1,0:T(8,128)(2,1)S(1)}, u32[]{:S(2)}, u32[]{:S(2)}) collective-permute-start(bf16[1280,128]{1,0:T(8,128)(2,1)S(1)} %shard_map.166.refs_16_), channel_id=1, source_target_pairs={{0,8},{4,12},{8,0},{12,4},{16,24},{20,28},{24,16},{28,20},{1,9},{5... | collective-permute-start | bytes 983048 | tf_op jit(solution)/shard_map/ppermute | solution.py:663
  65.1 6.9 %collective-permute-start.23 = (bf16[80,256]{1,0:T(8,128)(2,1)S(1)}, bf16[80,256]{1,0:T(8,128)(2,1)S(1)}, u32[]{:S(2)}, u32[]{:S(2)}) collective-permute-start(bf16[80,256]{1,0:T(8,128)(2,1)S(1)} %get-tuple-element.80), channel_id=1, source_target_pairs={{0,1},{1,0},{2,3},{3,2},{4,5},{5,4},{6,7},{7,6},{8,9},{9,8},{10,11... | collective-permute-start | bytes 122888 | tf_op jit(solution)/shard_map/ppermute | solution.py:663
  65.5 6.6 %collective-permute-start.24 = (bf16[80,256]{1,0:T(8,128)(2,1)S(1)}, bf16[80,256]{1,0:T(8,128)(2,1)S(1)}, u32[]{:S(2)}, u32[]{:S(2)}) collective-permute-start(bf16[80,256]{1,0:T(8,128)(2,1)S(1)} %get-tuple-element.81), channel_id=1, source_target_pairs={{0,2},{1,3},{2,0},{3,1},{4,6},{5,7},{6,4},{7,5},{8,10},{9,11},{10,... | collective-permute-start | bytes 122888 | tf_op jit(solution)/shard_map/ppermute | solution.py:663
  67.3 5.8 %collective-permute-start.25 = (bf16[80,256]{1,0:T(8,128)(2,1)S(1)}, bf16[80,256]{1,0:T(8,128)(2,1)S(1)}, u32[]{:S(2)}, u32[]{:S(2)}) collective-permute-start(bf16[80,256]{1,0:T(8,128)(2,1)S(1)} %get-tuple-element.82), channel_id=1, source_target_pairs={{0,3},{1,2},{2,1},{3,0},{4,7},{5,6},{6,5},{7,4},{8,11},{9,10},{10,... | collective-permute-start | bytes 122888 | tf_op jit(solution)/shard_map/ppermute | solution.py:663
  (25 other events, 111.9 us)

commit v17 on v14

--- a/solution.py
+++ b/solution.py
@@ -468,63 +468,35 @@
     refs[-1][...] = total
 
 
-def expert_kernel(flip, slots, a_ref, b_ref, gate_ref, up_ref, out_ref, *scratch):
-    rows_ref, gate_acc, up_acc = scratch
-    step = pl.program_id(0)
+def expert_kernel(flip, slots, a_ref, b_ref, gate_ref, up_ref, out_ref, rows_ref):
     n_chip = a_ref.shape[0]
-
-    @pl.when(step == 0)
-    def _():
-        for half, ref in enumerate((a_ref, b_ref)):
-            for i in range(n_chip):
-                row = (half * n_chip + i) * slots
-                for t in range(rows_ref.shape[1] // LANES):
-                    rows_ref[row : row + slots, t * LANES : (t + 1) * LANES] = ref[
-                        i, t * slots : (t + 1) * slots, :
-                    ]
-        gate_acc[...] = jnp.zeros_like(gate_acc)
-        up_acc[...] = jnp.zeros_like(up_acc)
-
-    depth = gate_ref.shape[0]
-    rows = rows_ref[:, rows_at(step, depth, LANES)]
-    gate_acc[...] += dot(rows, gate_ref[...], 1, 0)
-    up_acc[...] += dot(rows, up_ref[...], 1, 0)
-
-    @pl.when(step == pl.num_programs(0) - 1)
-    def _():
-        weighted = jax.nn.silu(gate_acc[...]) * up_acc[...]
-        out_ref[...] = (weighted.T if flip else weighted).astype(BF16)
+    width = rows_ref.shape[1]
+    for half, ref in enumerate((a_ref, b_ref)):
+        for i in range(n_chip):
+            row = (half * n_chip + i) * slots
+            for t in range(width // LANES):
+                rows_ref[row : row + slots, t * LANES : (t + 1) * LANES] = ref[
+                    i, t * slots : (t + 1) * slots, :
+                ]
+    gate = dot(rows_ref[...], gate_ref[...], 1, 0)
+    up = dot(rows_ref[...], up_ref[...], 1, 0)
+    weighted = jax.nn.silu(gate) * up
+    out_ref[...] = (weighted.T if flip else weighted).astype(BF16)
 
 
 def expert(a, b, w_gate, w_up, slots, flip, after):
-    n_chip = a.shape[0]
-    total = 2 * n_chip * slots
+    total = 2 * a.shape[0] * slots
     width, hidden = w_gate.shape
-    depth = 512
     out = (hidden, total) if flip else (total, hidden)
-
-    def body(*refs):
-        expert_kernel(flip, slots, *refs[:4], *refs[4 + len(after) :])
-
-    whole = pl.BlockSpec(a.shape, lambda i: (0, 0, 0))
-    block = pl.BlockSpec((depth, hidden), lambda i: (i, 0))
-    return pl.pallas_call(
-        body,
-        out_shape=shape(out, BF16),
-        grid=(width // depth,),
-        in_specs=[whole, whole, block, block]
-        + [pl.BlockSpec(memory_space=pl.ANY)] * len(after),
-        out_specs=pl.BlockSpec(out, lambda i: (0, 0)),
-        scratch_shapes=[
-            pltpu.VMEM((total, width), BF16),
-            pltpu.VMEM((total, hidden), F32),
-            pltpu.VMEM((total, hidden), F32),
-        ],
-        cost_estimate=pl.CostEstimate(
-            flops=int(1e9), bytes_accessed=1000, transcendentals=0
-        ),
-        compiler_params=pltpu.CompilerParams(vmem_limit_bytes=20 * 1024 * 1024),
-    )(a, b, w_gate, w_up, *after)
+    return call(
+        lambda *refs: expert_kernel(flip, slots, *refs),
+        [shape(out, BF16)],
+        0.35,
+        (a, b, w_gate, w_up),
+        after,
+        [pltpu.VMEM((total, width), BF16)],
+        limit=24,
+    )[0]
 
 
 def down_kernel(n_dp, flip, slots, grad_rows, *refs):
@@ -797,7 +769,7 @@
         (term, swapped(term_send)),
         scratch=[pltpu.VMEM((n_dp, w_rows // n_dp, columns), F32)],
     )
-    final = list(final[:1]) + [xored(f, "dp", s + 1) for s, f in enumerate(final[1:])]
+    final = [final[0]] + [xored(final[s], "dp", s) for s in reversed(range(1, n_dp))]
 
     grads = stacked(grads, (term,), spans)
     w_down_grad, done = call(

time: 72.9 us -> 72.2 us (level)
  waiting for transfers between devices: 14.4 us -> 15.5 us
  Pallas kernels: 23.6 us -> 22.6 us
  starting transfers between devices: 30.3 us -> 29.5 us
    pallas_call x1 -> x0, Pallas kernels: 2.93 us -> none  [expert(): pl.pallas_call(body, out_shape=shape(out, BF16), grid=(width // depth,),...]
    pallas_call x26 -> x27, Pallas kernels: 20.7 us -> 22.6 us  [call(): pl.pallas_call(body, out_shape=outs, in_specs=specs + [pl.BlockSpec(memor...]
    ppermute x26, waiting for transfers between devices: 14.4 us -> 15.1 us  [xored(): return lax.ppermute(array, axis, [(i, i ^ mask) for i in range(count)])]
  transfers between devices with their start and end apart: 28 -> 28, of which waited for: 10 -> 13; matrix products, arithmetic and copies ran while one was open for 0% -> 0% of each run, Pallas kernels for 29% -> 28%
where the time goes in v17:
time: 72.2 us; the launch traced here: 71.9 us
  starting transfers between devices  29.5 us (41%)
  Pallas kernels  22.6 us (31%)
  waiting for transfers between devices  15.5 us (21%)
  local copies, waits for them, and re-layouts  2.63 us (4%)
  between operations  1.71 us (2%)
    ppermute x26, starting transfers between devices, xored(): return lax.ppermute(array, axis, [(i, i ^ mask) for i in range(count)])  26.3 us
    pallas_call x27, Pallas kernels, call(): pl.pallas_call(body, out_shape=outs, in_specs=specs + [pl.BlockSpec(memor...  22.6 us
    ppermute x26, waiting for transfers between devices, xored(): return lax.ppermute(array, axis, [(i, i ^ mask) for i in range(count)])  15.1 us
    ppermute x2, starting transfers between devices, per_device(): arrived.append(lax.ppermute(climbs[-1], 'tm', moves))  3.12 us
    unnamed x44, local copies, waits for them, and re-layouts  1.69 us
  transfers between devices with their start and end apart: 28, of which 13 were waited for; matrix products, arithmetic and copies ran while one was open for 0% of the time, Pallas kernels for 28%

profile of v17, /device:TPU:0, one launch (start us, length us, event | category | flops | bytes accessed | tf_op | source)
XLA Modules:
  0.0 71.9 jit_solution(458635596843390505)
XLA Ops:
  1.6 4.1 %collective-permute-start.1 = (bf16[320,256]{1,0:T(8,128)(2,1)S(1)}, bf16[320,256]{1,0:T(8,128)(2,1)S(1)}, u32[]{:S(2)}, u32[]{:S(2)}) collective-permute-start(bf16[320,256]{1,0:T(8,128)(2,1)S(1)} %constant_dynamic-slice_fusion), channel_id=1, source_target_pairs={{0,2},{1,3},{2,0},{3,1},{4,6},{5,7},{6,4},{7,5},{8,10},{9,11},{10,... | collective-permute-start | bytes 491528 | tf_op jit(solution)/shard_map/ppermute | solution.py:527
  5.7 1.6 %collective-permute-start = (bf16[320,256]{1,0:T(8,128)(2,1)S(1)}, bf16[320,256]{1,0:T(8,128)(2,1)S(1)}, u32[]{:S(2)}, u32[]{:S(2)}) collective-permute-start(bf16[320,256]{1,0:T(8,128)(2,1)S(1)} %constant_dynamic-slice_fusion), channel_id=1, source_target_pairs={{0,1},{1,0},{2,3},{3,2},{4,5},{5,4},{6,7},{7,6},{8,9},{9,8},{10,11... | collective-permute-start | bytes 491528 | tf_op jit(solution)/shard_map/ppermute | solution.py:527
  7.9 3.9 %shard_map.146 = (f32[40,128]{1,0:T(8,128)}, f32[128,128]{1,0:T(8,128)}, bf16[2640,128]{1,0:T(8,128)(2,1)}, bf16[320,128]{1,0:T(8,128)(2,1)}, bf16[160,128]{1,0:T(8,128)(2,1)}, /*index=5*/bf16[160,128]{1,0:T(8,128)(2,1)}) custom-call(bf16[128,2560]{1,0:T(8,128)(2,1)} %bitcast.37, bf16[128,2560]{1,0:T(8,128)(2,1)} %bitcast.33, f32[40,128]{1,0:T(8,128)} %bitcast.54, ...), custom_call_target="tpu_custom_call" | custom-call | flops 4499999744 | bytes 1000 | tf_op jit(solution)/shard_map/pallas_call | solution.py:81
  11.9 1.6 %collective-permute-start.3 = (bf16[320,128]{1,0:T(8,128)(2,1)}, bf16[320,128]{1,0:T(8,128)(2,1)S(1)}, u32[]{:S(2)}, u32[]{:S(2)}) collective-permute-start(bf16[320,128]{1,0:T(8,128)(2,1)} %get-tuple-element.46.refs_1_.refs_5_.refs_0_), channel_id=1, source_target_pairs={{0,8},{4,12},{8,0},{12,4},{16,24},{20,28},{24,16},{28,20},{1,9},{5... | collective-permute-start | bytes 245768 | tf_op jit(solution)/shard_map/ppermute | solution.py:527
  13.4 1.5 %collective-permute-start.4 = (bf16[320,128]{1,0:T(8,128)(2,1)}, bf16[320,128]{1,0:T(8,128)(2,1)S(1)}, u32[]{:S(2)}, u32[]{:S(2)}) collective-permute-start(bf16[320,128]{1,0:T(8,128)(2,1)} %get-tuple-element.46.refs_1_.refs_5_.refs_0_), channel_id=1, source_target_pairs={{0,16},{4,20},{8,24},{12,28},{16,0},{20,4},{24,8},{28,12},{1,17},{... | collective-permute-start | bytes 245768 | tf_op jit(solution)/shard_map/ppermute | solution.py:527
  16.9 4.1 %shard_map.148 = (bf16[128,2560]{1,0:T(8,128)(2,1)}, f32[128,128]{1,0:T(8,128)}, f32[8,128]{1,0:T(8,128)}, bf16[640,128]{1,0:T(8,128)(2,1)}, bf16[640,128]{1,0:T(8,128)(2,1)}, /*index=5*/bf16[1280,128]{1,0:T(8,128)(2,1)}) custom-call(bf16[128,2560]{1,0:T(8,128)(2,1)} %bitcast.38, bf16[128,2560]{1,0:T(8,128)(2,1)} %bitcast.34, bf16[2560,128]{1,0:T(8,128)(2,1)} %bitcast.43, ...), custom_call_target="tpu_custom_call" | custom-call | flops 4499999744 | bytes 1000 | tf_op jit(solution)/shard_map/pallas_call | solution.py:81
  22.5 1.9 %collective-permute-done.6.refs_6_ = bf16[3,320,256]{2,1,0:T(8,128)(2,1)S(1)} collective-permute-done((bf16[3,320,256]{2,1,0:T(8,128)(2,1)S(1)}, bf16[3,320,256]{2,1,0:T(8,128)(2,1)S(1)}, u32[]{:S(2)}, u32[]{:S(2)}) %collective-permute-start.6) | collective-permute-done | bytes 491552 | tf_op jit(solution)/shard_map/ppermute | solution.py:527
  25.7 1.5 %collective-permute-done.7.refs_1_.refs_3_ = bf16[1328,128]{1,0:T(8,128)(2,1)S(1)} collective-permute-done((bf16[1328,128]{1,0:T(8,128)(2,1)S(1)}, bf16[1328,128]{1,0:T(8,128)(2,1)S(1)}, u32[]{:S(2)}, u32[]{:S(2)}) %collective-permute-start.7) | collective-permute-done | bytes 340000 | tf_op jit(solution)/shard_map/ppermute | solution.py:527
  27.7 1.5 %collective-permute-start.8 = (bf16[1328,128]{1,0:T(8,128)(2,1)S(1)}, bf16[1328,128]{1,0:T(8,128)(2,1)S(1)}, u32[]{:S(2)}, u32[]{:S(2)}) collective-permute-start(bf16[1328,128]{1,0:T(8,128)(2,1)S(1)} %shard_map.151.refs_4_.refs_0_), channel_id=1, source_target_pairs={{0,8},{4,12},{8,0},{12,4},{16,24},{20,28},{24,16},{28,20},{1,9},{5... | collective-permute-start | bytes 1019912 | tf_op jit(solution)/shard_map/ppermute | solution.py:662
  30.3 1.5 %collective-permute-start.14 = (bf16[1280,128]{1,0:T(8,128)(2,1)S(1)}, bf16[1280,128]{1,0:T(8,128)(2,1)S(1)}, u32[]{:S(2)}, u32[]{:S(2)}) collective-permute-start(bf16[1280,128]{1,0:T(8,128)(2,1)S(1)} %copy-done.16), channel_id=1, source_target_pairs={{0,16},{4,20},{8,24},{12,28},{16,0},{20,4},{24,8},{28,12},{1,17},{... | collective-permute-start | bytes 983048 | tf_op jit(solution)/shard_map/ppermute | solution.py:527
  31.9 1.7 %shard_map.153.refs_2_.refs_0_ = bf16[896,128]{1,0:T(8,128)(2,1)S(1)} custom-call(bf16[4,320,128]{2,1,0:T(8,128)(2,1)S(1)} %bitcast.32, bf16[4,320,128]{2,1,0:T(8,128)(2,1)S(1)} %collective-permute-done.9.refs_1_, bf16[2560,896]{1,0:T(8,128)(2,1)S(1)} %bitcast.27, bf16[2560,896]{1,0:T(8,128)(2,1)S(1)} %bitcast.30, ...), custom_call_target="tpu_custom_call" | custom-call | flops 1050000000 | bytes 1000 | tf_op jit(solution)/shard_map/pallas_call | solution.py:81
  35.5 1.7 %collective-permute-start.16 = (bf16[896,128]{1,0:T(8,128)(2,1)S(1)}, bf16[896,128]{1,0:T(8,128)(2,1)S(1)}, u32[]{:S(2)}, u32[]{:S(2)}) collective-permute-start(bf16[896,128]{1,0:T(8,128)(2,1)S(1)} %shard_map.153.refs_2_.refs_0_), channel_id=1, source_target_pairs={{0,2},{1,3},{2,0},{3,1},{4,6},{5,7},{6,4},{7,5},{8,10},{9,11},{10,... | collective-permute-start | bytes 688136 | tf_op jit(solution)/shard_map/ppermute | solution.py:527
  37.9 1.6 %collective-permute-done.11.refs_4_.refs_1_.refs_3_ = bf16[160,128]{1,0:T(8,128)(2,1)S(1)} collective-permute-done((bf16[160,128]{1,0:T(8,128)(2,1)S(1)}, bf16[160,128]{1,0:T(8,128)(2,1)S(1)}, u32[]{:S(2)}, u32[]{:S(2)}) %collective-permute-start.11) | collective-permute-done | bytes 40992 | tf_op jit(solution)/shard_map/ppermute | solution.py:527
  39.7 1.6 %collective-permute-start.12 = (bf16[1328,128]{1,0:T(8,128)(2,1)S(1)}, bf16[1328,128]{1,0:T(8,128)(2,1)S(1)}, u32[]{:S(2)}, u32[]{:S(2)}) collective-permute-start(bf16[1328,128]{1,0:T(8,128)(2,1)S(1)} %shard_map.155.refs_7_.refs_4_.refs_2_), channel_id=1, source_target_pairs={{0,16},{4,20},{8,24},{12,28},{16,0},{20,4},{24,8},{28,12},{1,17},{... | collective-permute-start | bytes 1019912 | tf_op jit(solution)/shard_map/ppermute | solution.py:662
  42.0 2.0 %shard_map.156 = (f32[128,1280]{1,0:T(8,128)S(1)}, f32[128,128]{1,0:T(8,128)S(1)}, f32[20,128]{1,0:T(8,128)S(1)}, f32[20,128]{1,0:T(8,128)S(1)}) custom-call(bf16[128,2560]{1,0:T(8,128)(2,1)S(1)} %bitcast.40, bf16[128,2560]{1,0:T(8,128)(2,1)S(1)} %bitcast.35, bf16[128,256]{1,0:T(8,128)(2,1)S(1)} %get-tuple-element.50.refs_2_.refs_1_, ...), custom_call_target="tpu_custom_call" | custom-call | flops 2100000000 | bytes 1000 | tf_op jit(solution)/shard_map/pallas_call | solution.py:81
  44.0 2.0 %shard_map.157 = (f32[128,1280]{1,0:T(8,128)S(1)}, f32[128,128]{1,0:T(8,128)S(1)}, f32[20,128]{1,0:T(8,128)S(1)}, f32[20,128]{1,0:T(8,128)S(1)}) custom-call(bf16[128,2560]{1,0:T(8,128)(2,1)S(1)} %bitcast.41, bf16[128,2560]{1,0:T(8,128)(2,1)S(1)} %bitcast.36, bf16[128,256]{1,0:T(8,128)(2,1)S(1)} %get-tuple-element.50.refs_2_.refs_1_, ...), custom_call_target="tpu_custom_call" | custom-call | flops 2100000000 | bytes 1000 | tf_op jit(solution)/shard_map/pallas_call | solution.py:81
  46.2 1.9 %collective-permute-done.16.refs_7_.refs_0_ = bf16[896,128]{1,0:T(8,128)(2,1)S(1)} collective-permute-done((bf16[896,128]{1,0:T(8,128)(2,1)S(1)}, bf16[896,128]{1,0:T(8,128)(2,1)S(1)}, u32[]{:S(2)}, u32[]{:S(2)}) %collective-permute-start.16) | collective-permute-done | bytes 229408 | tf_op jit(solution)/shard_map/ppermute | solution.py:527
  50.4 1.8 %collective-permute-start.19 = (bf16[896,128]{1,0:T(8,128)(2,1)S(1)}, bf16[896,128]{1,0:T(8,128)(2,1)S(1)}, u32[]{:S(2)}, u32[]{:S(2)}) collective-permute-start(bf16[896,128]{1,0:T(8,128)(2,1)S(1)} %shard_map.164.refs_2_), channel_id=1, source_target_pairs={{0,1},{1,0},{2,3},{3,2},{4,5},{5,4},{6,7},{7,6},{8,9},{9,8},{10,11... | collective-permute-start | bytes 688136 | tf_op jit(solution)/shard_map/ppermute | solution.py:527
  53.1 3.7 %collective-permute-done.21.refs_1_.refs_4_ = bf16[1,128,256]{2,1,0:T(8,128)(2,1)S(1)} collective-permute-done((bf16[1,128,256]{2,1,0:T(8,128)(2,1)S(1)}, bf16[1,128,256]{2,1,0:T(8,128)(2,1)S(1)}, u32[]{:S(2)}, u32[]{:S(2)}) %collective-permute-start.21) | collective-permute-done | bytes 65568 | tf_op jit(solution)/shard_map/ppermute | solution.py:527
  58.5 2.8 %shard_map.167 = (bf16[128,2560]{1,0:T(8,128)(2,1)}, f32[40,128]{1,0:T(8,128)}, f32[40,128]{1,0:T(8,128)}, f32[8,128]{1,0:T(8,128)S(1)}) custom-call(bf16[128,2560]{1,0:T(8,128)(2,1)S(1)} %bitcast.42, bf16[128,256]{1,0:T(8,128)(2,1)S(1)} %get-tuple-element.50.refs_2_.refs_1_, f32[40,128]{1,0:T(8,128)S(1)} %copy-done.14, f32[40,128]{1,0:T(8,128)S(1)} %bitcast.52, ...), custom_call_target="tpu_custom_call" | custom-call | flops 3000000000 | bytes 1000 | tf_op jit(solution)/shard_map/pallas_call | solution.py:81
  62.5 1.4 %collective-permute-done.23.refs_1_ = bf16[320,256]{1,0:T(8,128)(2,1)S(1)} collective-permute-done((bf16[320,256]{1,0:T(8,128)(2,1)S(1)}, bf16[320,256]{1,0:T(8,128)(2,1)S(1)}, u32[]{:S(2)}, u32[]{:S(2)}) %collective-permute-start.23) | collective-permute-done | bytes 163872 | tf_op jit(solution)/shard_map/ppermute | solution.py:527
  64.0 1.6 %collective-permute-start.24 = (bf16[80,256]{1,0:T(8,128)(2,1)S(1)}, bf16[80,256]{1,0:T(8,128)(2,1)S(1)}, u32[]{:S(2)}, u32[]{:S(2)}) collective-permute-start(bf16[80,256]{1,0:T(8,128)(2,1)S(1)} %get-tuple-element.80), channel_id=1, source_target_pairs={{0,3},{1,2},{2,1},{3,0},{4,7},{5,6},{6,5},{7,4},{8,11},{9,10},{10,... | collective-permute-start | bytes 122888 | tf_op jit(solution)/shard_map/ppermute | solution.py:527
  66.3 2.2 %collective-permute-start.26 = (bf16[80,256]{1,0:T(8,128)(2,1)S(1)}, bf16[80,256]{1,0:T(8,128)(2,1)S(1)}, u32[]{:S(2)}, u32[]{:S(2)}) collective-permute-start(bf16[80,256]{1,0:T(8,128)(2,1)S(1)} %get-tuple-element.82), channel_id=1, source_target_pairs={{0,1},{1,0},{2,3},{3,2},{4,5},{5,4},{6,7},{7,6},{8,9},{9,8},{10,11... | collective-permute-start | bytes 122888 | tf_op jit(solution)/shard_map/ppermute | solution.py:527
  68.5 2.4 %shard_map.171 = (bf16[896,640]{1,0:T(8,128)(2,1)}, f32[8,128]{1,0:T(8,128)S(1)}) custom-call(bf16[896,128]{1,0:T(8,128)(2,1)S(1)} %shard_map.153.refs_2_.refs_0_, bf16[896,128]{1,0:T(8,128)(2,1)S(1)} %collective-permute-done.17.refs_8_.refs_1_, bf16[896,128]{1,0:T(8,128)(2,1)S(1)} %shard_map.164.refs_2_, ...), custom_call_target="tpu_custom_call" | custom-call | flops 3000000000 | bytes 1000 | tf_op jit(solution)/shard_map/pallas_call | solution.py:81
  (107 shorter events, 18.6 us)
Async XLA Ops:
  1.6 13.8 %collective-permute-start.1 = (bf16[320,256]{1,0:T(8,128)(2,1)S(1)}, bf16[320,256]{1,0:T(8,128)(2,1)S(1)}, u32[]{:S(2)}, u32[]{:S(2)}) collective-permute-start(bf16[320,256]{1,0:T(8,128)(2,1)S(1)} %constant_dynamic-slice_fusion), channel_id=1, source_target_pairs={{0,2},{1,3},{2,0},{3,1},{4,6},{5,7},{6,4},{7,5},{8,10},{9,11},{10,... | collective-permute-start | bytes 491528 | tf_op jit(solution)/shard_map/ppermute | solution.py:527
  5.7 15.3 %collective-permute-start = (bf16[320,256]{1,0:T(8,128)(2,1)S(1)}, bf16[320,256]{1,0:T(8,128)(2,1)S(1)}, u32[]{:S(2)}, u32[]{:S(2)}) collective-permute-start(bf16[320,256]{1,0:T(8,128)(2,1)S(1)} %constant_dynamic-slice_fusion), channel_id=1, source_target_pairs={{0,1},{1,0},{2,3},{3,2},{4,5},{5,4},{6,7},{7,6},{8,9},{9,8},{10,11... | collective-permute-start | bytes 491528 | tf_op jit(solution)/shard_map/ppermute | solution.py:527
  11.9 9.1 %collective-permute-start.3 = (bf16[320,128]{1,0:T(8,128)(2,1)}, bf16[320,128]{1,0:T(8,128)(2,1)S(1)}, u32[]{:S(2)}, u32[]{:S(2)}) collective-permute-start(bf16[320,128]{1,0:T(8,128)(2,1)} %get-tuple-element.46.refs_1_.refs_5_.refs_0_), channel_id=1, source_target_pairs={{0,8},{4,12},{8,0},{12,4},{16,24},{20,28},{24,16},{28,20},{1,9},{5... | collective-permute-start | bytes 245768 | tf_op jit(solution)/shard_map/ppermute | solution.py:527
  13.4 7.6 %collective-permute-start.4 = (bf16[320,128]{1,0:T(8,128)(2,1)}, bf16[320,128]{1,0:T(8,128)(2,1)S(1)}, u32[]{:S(2)}, u32[]{:S(2)}) collective-permute-start(bf16[320,128]{1,0:T(8,128)(2,1)} %get-tuple-element.46.refs_1_.refs_5_.refs_0_), channel_id=1, source_target_pairs={{0,16},{4,20},{8,24},{12,28},{16,0},{20,4},{24,8},{28,12},{1,17},{... | collective-permute-start | bytes 245768 | tf_op jit(solution)/shard_map/ppermute | solution.py:527
  14.9 6.1 %collective-permute-start.5 = (bf16[320,128]{1,0:T(8,128)(2,1)}, bf16[320,128]{1,0:T(8,128)(2,1)S(1)}, u32[]{:S(2)}, u32[]{:S(2)}) collective-permute-start(bf16[320,128]{1,0:T(8,128)(2,1)} %get-tuple-element.46.refs_1_.refs_5_.refs_0_), channel_id=1, source_target_pairs={{0,24},{4,28},{8,16},{12,20},{16,8},{20,12},{24,0},{28,4},{1,25},{... | collective-permute-start | bytes 245768 | tf_op jit(solution)/shard_map/ppermute | solution.py:527
  16.3 5.4 %collective-permute-start.2 = (bf16[320,256]{1,0:T(8,128)(2,1)S(1)}, bf16[320,256]{1,0:T(8,128)(2,1)S(1)}, u32[]{:S(2)}, u32[]{:S(2)}) collective-permute-start(bf16[320,256]{1,0:T(8,128)(2,1)S(1)} %shard_map.147.refs_1_.refs_4_), channel_id=1, source_target_pairs={{0,1},{1,0},{2,3},{3,2},{4,5},{5,4},{6,7},{7,6},{8,9},{9,8},{10,11... | collective-permute-start | bytes 491528 | tf_op jit(solution)/shard_map/ppermute | solution.py:527
  27.5 4.3 %collective-permute-start.9 = (bf16[4,320,128]{2,1,0:T(8,128)(2,1)S(1)}, bf16[4,320,128]{2,1,0:T(8,128)(2,1)S(1)}, u32[]{:S(2)}, u32[]{:S(2)}) collective-permute-start(bf16[4,320,128]{2,1,0:T(8,128)(2,1)S(1)} %bitcast.31), channel_id=1, source_target_pairs={{0,4},{4,0},{8,12},{12,8},{16,20},{20,16},{24,28},{28,24},{1,5},{5... | collective-permute-start | bytes 983048 | tf_op jit(solution)/shard_map/ppermute | solution.py:527
  27.7 10.3 %collective-permute-start.8 = (bf16[1328,128]{1,0:T(8,128)(2,1)S(1)}, bf16[1328,128]{1,0:T(8,128)(2,1)S(1)}, u32[]{:S(2)}, u32[]{:S(2)}) collective-permute-start(bf16[1328,128]{1,0:T(8,128)(2,1)S(1)} %shard_map.151.refs_4_.refs_0_), channel_id=1, source_target_pairs={{0,8},{4,12},{8,0},{12,4},{16,24},{20,28},{24,16},{28,20},{1,9},{5... | collective-permute-start | bytes 1019912 | tf_op jit(solution)/shard_map/ppermute | solution.py:662
  29.2 5.3 %collective-permute-start.10 = (bf16[160,128]{1,0:T(8,128)(2,1)S(1)}, bf16[160,128]{1,0:T(8,128)(2,1)S(1)}, u32[]{:S(2)}, u32[]{:S(2)}) collective-permute-start(bf16[160,128]{1,0:T(8,128)(2,1)S(1)} %copy-done.17), channel_id=1, source_target_pairs={{0,2},{1,3},{2,0},{3,1},{4,6},{5,7},{6,4},{7,5},{8,10},{9,11},{10,... | collective-permute-start | bytes 122888 | tf_op jit(solution)/shard_map/ppermute | solution.py:527
  30.3 11.0 %collective-permute-start.14 = (bf16[1280,128]{1,0:T(8,128)(2,1)S(1)}, bf16[1280,128]{1,0:T(8,128)(2,1)S(1)}, u32[]{:S(2)}, u32[]{:S(2)}) collective-permute-start(bf16[1280,128]{1,0:T(8,128)(2,1)S(1)} %copy-done.16), channel_id=1, source_target_pairs={{0,16},{4,20},{8,24},{12,28},{16,0},{20,4},{24,8},{28,12},{1,17},{... | collective-permute-start | bytes 983048 | tf_op jit(solution)/shard_map/ppermute | solution.py:527
  34.6 5.0 %collective-permute-start.11 = (bf16[160,128]{1,0:T(8,128)(2,1)S(1)}, bf16[160,128]{1,0:T(8,128)(2,1)S(1)}, u32[]{:S(2)}, u32[]{:S(2)}) collective-permute-start(bf16[160,128]{1,0:T(8,128)(2,1)S(1)} %shard_map.154), channel_id=1, source_target_pairs={{0,1},{1,0},{2,3},{3,2},{4,5},{5,4},{6,7},{7,6},{8,9},{9,8},{10,11... | collective-permute-start | bytes 122888 | tf_op jit(solution)/shard_map/ppermute | solution.py:527
  35.5 12.7 %collective-permute-start.16 = (bf16[896,128]{1,0:T(8,128)(2,1)S(1)}, bf16[896,128]{1,0:T(8,128)(2,1)S(1)}, u32[]{:S(2)}, u32[]{:S(2)}) collective-permute-start(bf16[896,128]{1,0:T(8,128)(2,1)S(1)} %shard_map.153.refs_2_.refs_0_), channel_id=1, source_target_pairs={{0,2},{1,3},{2,0},{3,1},{4,6},{5,7},{6,4},{7,5},{8,10},{9,11},{10,... | collective-permute-start | bytes 688136 | tf_op jit(solution)/shard_map/ppermute | solution.py:527
  37.2 11.2 %collective-permute-start.17 = (bf16[896,128]{1,0:T(8,128)(2,1)S(1)}, bf16[896,128]{1,0:T(8,128)(2,1)S(1)}, u32[]{:S(2)}, u32[]{:S(2)}) collective-permute-start(bf16[896,128]{1,0:T(8,128)(2,1)S(1)} %shard_map.153.refs_2_.refs_0_), channel_id=1, source_target_pairs={{0,1},{1,0},{2,3},{3,2},{4,5},{5,4},{6,7},{7,6},{8,9},{9,8},{10,11... | collective-permute-start | bytes 688136 | tf_op jit(solution)/shard_map/ppermute | solution.py:527
  39.7 9.0 %collective-permute-start.12 = (bf16[1328,128]{1,0:T(8,128)(2,1)S(1)}, bf16[1328,128]{1,0:T(8,128)(2,1)S(1)}, u32[]{:S(2)}, u32[]{:S(2)}) collective-permute-start(bf16[1328,128]{1,0:T(8,128)(2,1)S(1)} %shard_map.155.refs_7_.refs_4_.refs_2_), channel_id=1, source_target_pairs={{0,16},{4,20},{8,24},{12,28},{16,0},{20,4},{24,8},{28,12},{1,17},{... | collective-permute-start | bytes 1019912 | tf_op jit(solution)/shard_map/ppermute | solution.py:662
  41.3 7.3 %collective-permute-start.15 = (bf16[1280,128]{1,0:T(8,128)(2,1)S(1)}, bf16[1280,128]{1,0:T(8,128)(2,1)S(1)}, u32[]{:S(2)}, u32[]{:S(2)}) collective-permute-start(bf16[1280,128]{1,0:T(8,128)(2,1)S(1)} %shard_map.161), channel_id=1, source_target_pairs={{0,8},{4,12},{8,0},{12,4},{16,24},{20,28},{24,16},{28,20},{1,9},{5... | collective-permute-start | bytes 983048 | tf_op jit(solution)/shard_map/ppermute | solution.py:527
  42.0 4.2 %collective-permute-start.13 = (bf16[320,128]{1,0:T(8,128)(2,1)S(1)}, bf16[320,128]{1,0:T(8,128)(2,1)S(1)}, u32[]{:S(2)}, u32[]{:S(2)}) collective-permute-start(bf16[320,128]{1,0:T(8,128)(2,1)S(1)} %shard_map.159.refs_0_), channel_id=1, source_target_pairs={{0,4},{4,0},{8,12},{12,8},{16,20},{20,16},{24,28},{28,24},{1,5},{5... | collective-permute-start | bytes 245768 | tf_op jit(solution)/shard_map/ppermute | solution.py:527
  49.1 8.3 %collective-permute-start.20 = (bf16[640,128]{1,0:T(8,128)(2,1)S(1)}, bf16[640,128]{1,0:T(8,128)(2,1)S(1)}, u32[]{:S(2)}, u32[]{:S(2)}) collective-permute-start(bf16[640,128]{1,0:T(8,128)(2,1)S(1)} %shard_map.160.refs_5_.refs_0_), channel_id=1, source_target_pairs={{0,16},{4,20},{8,24},{12,28},{16,0},{20,4},{24,8},{28,12},{1,17},{... | collective-permute-start | bytes 491528 | tf_op jit(solution)/shard_map/ppermute | solution.py:527
  50.4 8.1 %collective-permute-start.19 = (bf16[896,128]{1,0:T(8,128)(2,1)S(1)}, bf16[896,128]{1,0:T(8,128)(2,1)S(1)}, u32[]{:S(2)}, u32[]{:S(2)}) collective-permute-start(bf16[896,128]{1,0:T(8,128)(2,1)S(1)} %shard_map.164.refs_2_), channel_id=1, source_target_pairs={{0,1},{1,0},{2,3},{3,2},{4,5},{5,4},{6,7},{7,6},{8,9},{9,8},{10,11... | collective-permute-start | bytes 688136 | tf_op jit(solution)/shard_map/ppermute | solution.py:527
  52.5 4.3 %collective-permute-start.21 = (bf16[1,128,256]{2,1,0:T(8,128)(2,1)S(1)}, bf16[1,128,256]{2,1,0:T(8,128)(2,1)S(1)}, u32[]{:S(2)}, u32[]{:S(2)}) collective-permute-start(bf16[1,128,256]{2,1,0:T(8,128)(2,1)S(1)} %bitcast.48), channel_id=1, source_target_pairs={{0,8},{4,12},{8,0},{12,4},{16,24},{20,28},{24,16},{28,20},{1,9},{5... | collective-permute-start | bytes 196616 | tf_op jit(solution)/shard_map/ppermute | solution.py:527
  56.8 5.0 %collective-permute-start.22 = (bf16[2,128,256]{2,1,0:T(8,128)(2,1)S(1)}, bf16[2,128,256]{2,1,0:T(8,128)(2,1)S(1)}, u32[]{:S(2)}, u32[]{:S(2)}) collective-permute-start(bf16[2,128,256]{2,1,0:T(8,128)(2,1)S(1)} %shard_map.165.refs_2_), channel_id=1, source_target_pairs={{0,16},{4,20},{8,24},{12,28},{16,0},{20,4},{24,8},{28,12},{1,17},{... | collective-permute-start | bytes 393224 | tf_op jit(solution)/shard_map/ppermute | solution.py:527
  57.4 11.0 %collective-permute-start.27 = (bf16[1280,128]{1,0:T(8,128)(2,1)S(1)}, bf16[1280,128]{1,0:T(8,128)(2,1)S(1)}, u32[]{:S(2)}, u32[]{:S(2)}) collective-permute-start(bf16[1280,128]{1,0:T(8,128)(2,1)S(1)} %shard_map.166.refs_17_), channel_id=1, source_target_pairs={{0,8},{4,12},{8,0},{12,4},{16,24},{20,28},{24,16},{28,20},{1,9},{5... | collective-permute-start | bytes 983048 | tf_op jit(solution)/shard_map/ppermute | solution.py:527
  64.0 6.9 %collective-permute-start.24 = (bf16[80,256]{1,0:T(8,128)(2,1)S(1)}, bf16[80,256]{1,0:T(8,128)(2,1)S(1)}, u32[]{:S(2)}, u32[]{:S(2)}) collective-permute-start(bf16[80,256]{1,0:T(8,128)(2,1)S(1)} %get-tuple-element.80), channel_id=1, source_target_pairs={{0,3},{1,2},{2,1},{3,0},{4,7},{5,6},{6,5},{7,4},{8,11},{9,10},{10,... | collective-permute-start | bytes 122888 | tf_op jit(solution)/shard_map/ppermute | solution.py:527
  65.6 5.6 %collective-permute-start.25 = (bf16[80,256]{1,0:T(8,128)(2,1)S(1)}, bf16[80,256]{1,0:T(8,128)(2,1)S(1)}, u32[]{:S(2)}, u32[]{:S(2)}) collective-permute-start(bf16[80,256]{1,0:T(8,128)(2,1)S(1)} %get-tuple-element.81), channel_id=1, source_target_pairs={{0,2},{1,3},{2,0},{3,1},{4,6},{5,7},{6,4},{7,5},{8,10},{9,11},{10,... | collective-permute-start | bytes 122888 | tf_op jit(solution)/shard_map/ppermute | solution.py:527
  66.3 5.0 %collective-permute-start.26 = (bf16[80,256]{1,0:T(8,128)(2,1)S(1)}, bf16[80,256]{1,0:T(8,128)(2,1)S(1)}, u32[]{:S(2)}, u32[]{:S(2)}) collective-permute-start(bf16[80,256]{1,0:T(8,128)(2,1)S(1)} %get-tuple-element.82), channel_id=1, source_target_pairs={{0,1},{1,0},{2,3},{3,2},{4,5},{5,4},{6,7},{7,6},{8,9},{9,8},{10,11... | collective-permute-start | bytes 122888 | tf_op jit(solution)/shard_map/ppermute | solution.py:527
  (26 other events, 115.6 us)

commit v18 on v17

--- a/solution.py
+++ b/solution.py
@@ -154,7 +154,7 @@
     for j in range(width // LANES):
         span = slice(j * LANES, (j + 1) * LANES)
         dys = dy_ref[:, span].astype(F32) * dot(table, to_lanes(j, size), 1, 0)
-        dyt_ref[span, :] = dys.T.astype(BF16)
+        dyt_ref[span, :] = dys.astype(BF16).T
     decay = jnp.broadcast_to(jnp.exp(cumt[:, length - 1 : length]), (heads, LANES))
     dyt_ref[width : width + 2 * heads, :] = jnp.concatenate(high_low(decay), axis=0).astype(BF16)
 
@@ -174,7 +174,7 @@
         span = slice(j * LANES, (j + 1) * LANES)
         scale = dot(table, to_lanes(j, size), 1, 0)
         x_f = x_ref[:, span].astype(F32)
-        xt_ref[span, :] = x_f.T.astype(BF16)
+        xt_ref[span, :] = x_ref[:, span].T
         xs_ref[:, span] = (x_f * scale[length:]).astype(BF16)
         dys = (dy_ref[:, span].astype(F32) * scale[:length]).astype(BF16)
         carried = carried + dot(dys, h_ref[span, :], 1, 0)
@@ -481,7 +481,8 @@
     gate = dot(rows_ref[...], gate_ref[...], 1, 0)
     up = dot(rows_ref[...], up_ref[...], 1, 0)
     weighted = jax.nn.silu(gate) * up
-    out_ref[...] = (weighted.T if flip else weighted).astype(BF16)
+    weighted = weighted.astype(BF16)
+    out_ref[...] = weighted.T if flip else weighted
 
 
 def expert(a, b, w_gate, w_up, slots, flip, after):

time: 72.2 us -> 72.2 us (level)
  no operation moved by 1% of the time
where the time goes in v18:
time: 72.2 us; the launch traced here: 71.9 us
  starting transfers between devices  29.5 us (41%)
  Pallas kernels  22.6 us (31%)
  waiting for transfers between devices  15.5 us (21%)
  local copies, waits for them, and re-layouts  2.63 us (4%)
  between operations  1.71 us (2%)
    ppermute x26, starting transfers between devices, xored(): return lax.ppermute(array, axis, [(i, i ^ mask) for i in range(count)])  26.3 us
    pallas_call x27, Pallas kernels, call(): pl.pallas_call(body, out_shape=outs, in_specs=specs + [pl.BlockSpec(memor...  22.6 us
    ppermute x26, waiting for transfers between devices, xored(): return lax.ppermute(array, axis, [(i, i ^ mask) for i in range(count)])  15.2 us
    ppermute x2, starting transfers between devices, per_device(): arrived.append(lax.ppermute(climbs[-1], 'tm', moves))  3.13 us
    unnamed x44, local copies, waits for them, and re-layouts  1.69 us
  transfers between devices with their start and end apart: 28, of which 13 were waited for; matrix products, arithmetic and copies ran while one was open for 0% of the time, Pallas kernels for 28%

profile of v18, /device:TPU:0, one launch (start us, length us, event | category | flops | bytes accessed | tf_op | source)
XLA Modules:
  0.0 71.9 jit_solution(279627273480026500)
XLA Ops:
  1.6 4.1 %collective-permute-start.1 = (bf16[320,256]{1,0:T(8,128)(2,1)S(1)}, bf16[320,256]{1,0:T(8,128)(2,1)S(1)}, u32[]{:S(2)}, u32[]{:S(2)}) collective-permute-start(bf16[320,256]{1,0:T(8,128)(2,1)S(1)} %constant_dynamic-slice_fusion), channel_id=1, source_target_pairs={{0,2},{1,3},{2,0},{3,1},{4,6},{5,7},{6,4},{7,5},{8,10},{9,11},{10,... | collective-permute-start | bytes 491528 | tf_op jit(solution)/shard_map/ppermute | solution.py:528
  5.7 1.6 %collective-permute-start = (bf16[320,256]{1,0:T(8,128)(2,1)S(1)}, bf16[320,256]{1,0:T(8,128)(2,1)S(1)}, u32[]{:S(2)}, u32[]{:S(2)}) collective-permute-start(bf16[320,256]{1,0:T(8,128)(2,1)S(1)} %constant_dynamic-slice_fusion), channel_id=1, source_target_pairs={{0,1},{1,0},{2,3},{3,2},{4,5},{5,4},{6,7},{7,6},{8,9},{9,8},{10,11... | collective-permute-start | bytes 491528 | tf_op jit(solution)/shard_map/ppermute | solution.py:528
  7.9 3.9 %shard_map.146 = (f32[40,128]{1,0:T(8,128)}, f32[128,128]{1,0:T(8,128)}, bf16[2640,128]{1,0:T(8,128)(2,1)}, bf16[320,128]{1,0:T(8,128)(2,1)}, bf16[160,128]{1,0:T(8,128)(2,1)}, /*index=5*/bf16[160,128]{1,0:T(8,128)(2,1)}) custom-call(bf16[128,2560]{1,0:T(8,128)(2,1)} %bitcast.37, bf16[128,2560]{1,0:T(8,128)(2,1)} %bitcast.33, f32[40,128]{1,0:T(8,128)} %bitcast.54, ...), custom_call_target="tpu_custom_call" | custom-call | flops 4499999744 | bytes 1000 | tf_op jit(solution)/shard_map/pallas_call | solution.py:81
  11.8 1.6 %collective-permute-start.3 = (bf16[320,128]{1,0:T(8,128)(2,1)}, bf16[320,128]{1,0:T(8,128)(2,1)S(1)}, u32[]{:S(2)}, u32[]{:S(2)}) collective-permute-start(bf16[320,128]{1,0:T(8,128)(2,1)} %get-tuple-element.46.refs_1_.refs_5_.refs_0_), channel_id=1, source_target_pairs={{0,8},{4,12},{8,0},{12,4},{16,24},{20,28},{24,16},{28,20},{1,9},{5... | collective-permute-start | bytes 245768 | tf_op jit(solution)/shard_map/ppermute | solution.py:528
  13.4 1.5 %collective-permute-start.4 = (bf16[320,128]{1,0:T(8,128)(2,1)}, bf16[320,128]{1,0:T(8,128)(2,1)S(1)}, u32[]{:S(2)}, u32[]{:S(2)}) collective-permute-start(bf16[320,128]{1,0:T(8,128)(2,1)} %get-tuple-element.46.refs_1_.refs_5_.refs_0_), channel_id=1, source_target_pairs={{0,16},{4,20},{8,24},{12,28},{16,0},{20,4},{24,8},{28,12},{1,17},{... | collective-permute-start | bytes 245768 | tf_op jit(solution)/shard_map/ppermute | solution.py:528
  16.8 4.1 %shard_map.148 = (bf16[128,2560]{1,0:T(8,128)(2,1)}, f32[128,128]{1,0:T(8,128)}, f32[8,128]{1,0:T(8,128)}, bf16[640,128]{1,0:T(8,128)(2,1)}, bf16[640,128]{1,0:T(8,128)(2,1)}, /*index=5*/bf16[1280,128]{1,0:T(8,128)(2,1)}) custom-call(bf16[128,2560]{1,0:T(8,128)(2,1)} %bitcast.38, bf16[128,2560]{1,0:T(8,128)(2,1)} %bitcast.34, bf16[2560,128]{1,0:T(8,128)(2,1)} %bitcast.43, ...), custom_call_target="tpu_custom_call" | custom-call | flops 4499999744 | bytes 1000 | tf_op jit(solution)/shard_map/pallas_call | solution.py:81
  22.5 1.9 %collective-permute-done.6.refs_6_ = bf16[3,320,256]{2,1,0:T(8,128)(2,1)S(1)} collective-permute-done((bf16[3,320,256]{2,1,0:T(8,128)(2,1)S(1)}, bf16[3,320,256]{2,1,0:T(8,128)(2,1)S(1)}, u32[]{:S(2)}, u32[]{:S(2)}) %collective-permute-start.6) | collective-permute-done | bytes 491552 | tf_op jit(solution)/shard_map/ppermute | solution.py:528
  25.7 1.5 %collective-permute-done.7.refs_1_.refs_3_ = bf16[1328,128]{1,0:T(8,128)(2,1)S(1)} collective-permute-done((bf16[1328,128]{1,0:T(8,128)(2,1)S(1)}, bf16[1328,128]{1,0:T(8,128)(2,1)S(1)}, u32[]{:S(2)}, u32[]{:S(2)}) %collective-permute-start.7) | collective-permute-done | bytes 340000 | tf_op jit(solution)/shard_map/ppermute | solution.py:528
  27.6 1.5 %collective-permute-start.8 = (bf16[1328,128]{1,0:T(8,128)(2,1)S(1)}, bf16[1328,128]{1,0:T(8,128)(2,1)S(1)}, u32[]{:S(2)}, u32[]{:S(2)}) collective-permute-start(bf16[1328,128]{1,0:T(8,128)(2,1)S(1)} %shard_map.151.refs_4_.refs_0_), channel_id=1, source_target_pairs={{0,8},{4,12},{8,0},{12,4},{16,24},{20,28},{24,16},{28,20},{1,9},{5... | collective-permute-start | bytes 1019912 | tf_op jit(solution)/shard_map/ppermute | solution.py:663
  30.3 1.5 %collective-permute-start.14 = (bf16[1280,128]{1,0:T(8,128)(2,1)S(1)}, bf16[1280,128]{1,0:T(8,128)(2,1)S(1)}, u32[]{:S(2)}, u32[]{:S(2)}) collective-permute-start(bf16[1280,128]{1,0:T(8,128)(2,1)S(1)} %copy-done.16), channel_id=1, source_target_pairs={{0,16},{4,20},{8,24},{12,28},{16,0},{20,4},{24,8},{28,12},{1,17},{... | collective-permute-start | bytes 983048 | tf_op jit(solution)/shard_map/ppermute | solution.py:528
  31.9 1.7 %shard_map.153.refs_2_.refs_0_ = bf16[896,128]{1,0:T(8,128)(2,1)S(1)} custom-call(bf16[4,320,128]{2,1,0:T(8,128)(2,1)S(1)} %bitcast.32, bf16[4,320,128]{2,1,0:T(8,128)(2,1)S(1)} %collective-permute-done.9.refs_1_, bf16[2560,896]{1,0:T(8,128)(2,1)S(1)} %bitcast.27, bf16[2560,896]{1,0:T(8,128)(2,1)S(1)} %bitcast.30, ...), custom_call_target="tpu_custom_call" | custom-call | flops 1050000000 | bytes 1000 | tf_op jit(solution)/shard_map/pallas_call | solution.py:81
  35.5 1.7 %collective-permute-start.16 = (bf16[896,128]{1,0:T(8,128)(2,1)S(1)}, bf16[896,128]{1,0:T(8,128)(2,1)S(1)}, u32[]{:S(2)}, u32[]{:S(2)}) collective-permute-start(bf16[896,128]{1,0:T(8,128)(2,1)S(1)} %shard_map.153.refs_2_.refs_0_), channel_id=1, source_target_pairs={{0,2},{1,3},{2,0},{3,1},{4,6},{5,7},{6,4},{7,5},{8,10},{9,11},{10,... | collective-permute-start | bytes 688136 | tf_op jit(solution)/shard_map/ppermute | solution.py:528
  37.9 1.6 %collective-permute-done.11.refs_4_.refs_1_.refs_3_ = bf16[160,128]{1,0:T(8,128)(2,1)S(1)} collective-permute-done((bf16[160,128]{1,0:T(8,128)(2,1)S(1)}, bf16[160,128]{1,0:T(8,128)(2,1)S(1)}, u32[]{:S(2)}, u32[]{:S(2)}) %collective-permute-start.11) | collective-permute-done | bytes 40992 | tf_op jit(solution)/shard_map/ppermute | solution.py:528
  39.7 1.6 %collective-permute-start.12 = (bf16[1328,128]{1,0:T(8,128)(2,1)S(1)}, bf16[1328,128]{1,0:T(8,128)(2,1)S(1)}, u32[]{:S(2)}, u32[]{:S(2)}) collective-permute-start(bf16[1328,128]{1,0:T(8,128)(2,1)S(1)} %shard_map.155.refs_7_.refs_4_.refs_2_), channel_id=1, source_target_pairs={{0,16},{4,20},{8,24},{12,28},{16,0},{20,4},{24,8},{28,12},{1,17},{... | collective-permute-start | bytes 1019912 | tf_op jit(solution)/shard_map/ppermute | solution.py:663
  42.0 2.0 %shard_map.156 = (f32[128,1280]{1,0:T(8,128)S(1)}, f32[128,128]{1,0:T(8,128)S(1)}, f32[20,128]{1,0:T(8,128)S(1)}, f32[20,128]{1,0:T(8,128)S(1)}) custom-call(bf16[128,2560]{1,0:T(8,128)(2,1)S(1)} %bitcast.40, bf16[128,2560]{1,0:T(8,128)(2,1)S(1)} %bitcast.35, bf16[128,256]{1,0:T(8,128)(2,1)S(1)} %get-tuple-element.50.refs_2_.refs_1_, ...), custom_call_target="tpu_custom_call" | custom-call | flops 2100000000 | bytes 1000 | tf_op jit(solution)/shard_map/pallas_call | solution.py:81
  44.0 2.0 %shard_map.157 = (f32[128,1280]{1,0:T(8,128)S(1)}, f32[128,128]{1,0:T(8,128)S(1)}, f32[20,128]{1,0:T(8,128)S(1)}, f32[20,128]{1,0:T(8,128)S(1)}) custom-call(bf16[128,2560]{1,0:T(8,128)(2,1)S(1)} %bitcast.41, bf16[128,2560]{1,0:T(8,128)(2,1)S(1)} %bitcast.36, bf16[128,256]{1,0:T(8,128)(2,1)S(1)} %get-tuple-element.50.refs_2_.refs_1_, ...), custom_call_target="tpu_custom_call" | custom-call | flops 2100000000 | bytes 1000 | tf_op jit(solution)/shard_map/pallas_call | solution.py:81
  46.2 1.9 %collective-permute-done.16.refs_7_.refs_0_ = bf16[896,128]{1,0:T(8,128)(2,1)S(1)} collective-permute-done((bf16[896,128]{1,0:T(8,128)(2,1)S(1)}, bf16[896,128]{1,0:T(8,128)(2,1)S(1)}, u32[]{:S(2)}, u32[]{:S(2)}) %collective-permute-start.16) | collective-permute-done | bytes 229408 | tf_op jit(solution)/shard_map/ppermute | solution.py:528
  50.4 1.8 %collective-permute-start.19 = (bf16[896,128]{1,0:T(8,128)(2,1)S(1)}, bf16[896,128]{1,0:T(8,128)(2,1)S(1)}, u32[]{:S(2)}, u32[]{:S(2)}) collective-permute-start(bf16[896,128]{1,0:T(8,128)(2,1)S(1)} %shard_map.164.refs_2_), channel_id=1, source_target_pairs={{0,1},{1,0},{2,3},{3,2},{4,5},{5,4},{6,7},{7,6},{8,9},{9,8},{10,11... | collective-permute-start | bytes 688136 | tf_op jit(solution)/shard_map/ppermute | solution.py:528
  53.1 3.7 %collective-permute-done.21.refs_1_.refs_4_ = bf16[1,128,256]{2,1,0:T(8,128)(2,1)S(1)} collective-permute-done((bf16[1,128,256]{2,1,0:T(8,128)(2,1)S(1)}, bf16[1,128,256]{2,1,0:T(8,128)(2,1)S(1)}, u32[]{:S(2)}, u32[]{:S(2)}) %collective-permute-start.21) | collective-permute-done | bytes 65568 | tf_op jit(solution)/shard_map/ppermute | solution.py:528
  58.5 2.8 %shard_map.167 = (bf16[128,2560]{1,0:T(8,128)(2,1)}, f32[40,128]{1,0:T(8,128)}, f32[40,128]{1,0:T(8,128)}, f32[8,128]{1,0:T(8,128)S(1)}) custom-call(bf16[128,2560]{1,0:T(8,128)(2,1)S(1)} %bitcast.42, bf16[128,256]{1,0:T(8,128)(2,1)S(1)} %get-tuple-element.50.refs_2_.refs_1_, f32[40,128]{1,0:T(8,128)S(1)} %copy-done.14, f32[40,128]{1,0:T(8,128)S(1)} %bitcast.52, ...), custom_call_target="tpu_custom_call" | custom-call | flops 3000000000 | bytes 1000 | tf_op jit(solution)/shard_map/pallas_call | solution.py:81
  62.5 1.4 %collective-permute-done.23.refs_1_ = bf16[320,256]{1,0:T(8,128)(2,1)S(1)} collective-permute-done((bf16[320,256]{1,0:T(8,128)(2,1)S(1)}, bf16[320,256]{1,0:T(8,128)(2,1)S(1)}, u32[]{:S(2)}, u32[]{:S(2)}) %collective-permute-start.23) | collective-permute-done | bytes 163872 | tf_op jit(solution)/shard_map/ppermute | solution.py:528
  64.0 1.6 %collective-permute-start.24 = (bf16[80,256]{1,0:T(8,128)(2,1)S(1)}, bf16[80,256]{1,0:T(8,128)(2,1)S(1)}, u32[]{:S(2)}, u32[]{:S(2)}) collective-permute-start(bf16[80,256]{1,0:T(8,128)(2,1)S(1)} %get-tuple-element.80), channel_id=1, source_target_pairs={{0,3},{1,2},{2,1},{3,0},{4,7},{5,6},{6,5},{7,4},{8,11},{9,10},{10,... | collective-permute-start | bytes 122888 | tf_op jit(solution)/shard_map/ppermute | solution.py:528
  66.2 2.2 %collective-permute-start.26 = (bf16[80,256]{1,0:T(8,128)(2,1)S(1)}, bf16[80,256]{1,0:T(8,128)(2,1)S(1)}, u32[]{:S(2)}, u32[]{:S(2)}) collective-permute-start(bf16[80,256]{1,0:T(8,128)(2,1)S(1)} %get-tuple-element.82), channel_id=1, source_target_pairs={{0,1},{1,0},{2,3},{3,2},{4,5},{5,4},{6,7},{7,6},{8,9},{9,8},{10,11... | collective-permute-start | bytes 122888 | tf_op jit(solution)/shard_map/ppermute | solution.py:528
  68.5 2.4 %shard_map.171 = (bf16[896,640]{1,0:T(8,128)(2,1)}, f32[8,128]{1,0:T(8,128)S(1)}) custom-call(bf16[896,128]{1,0:T(8,128)(2,1)S(1)} %shard_map.153.refs_2_.refs_0_, bf16[896,128]{1,0:T(8,128)(2,1)S(1)} %collective-permute-done.17.refs_8_.refs_1_, bf16[896,128]{1,0:T(8,128)(2,1)S(1)} %shard_map.164.refs_2_, ...), custom_call_target="tpu_custom_call" | custom-call | flops 3000000000 | bytes 1000 | tf_op jit(solution)/shard_map/pallas_call | solution.py:81
  (107 shorter events, 18.7 us)
Async XLA Ops:
  1.6 13.8 %collective-permute-start.1 = (bf16[320,256]{1,0:T(8,128)(2,1)S(1)}, bf16[320,256]{1,0:T(8,128)(2,1)S(1)}, u32[]{:S(2)}, u32[]{:S(2)}) collective-permute-start(bf16[320,256]{1,0:T(8,128)(2,1)S(1)} %constant_dynamic-slice_fusion), channel_id=1, source_target_pairs={{0,2},{1,3},{2,0},{3,1},{4,6},{5,7},{6,4},{7,5},{8,10},{9,11},{10,... | collective-permute-start | bytes 491528 | tf_op jit(solution)/shard_map/ppermute | solution.py:528
  5.7 15.3 %collective-permute-start = (bf16[320,256]{1,0:T(8,128)(2,1)S(1)}, bf16[320,256]{1,0:T(8,128)(2,1)S(1)}, u32[]{:S(2)}, u32[]{:S(2)}) collective-permute-start(bf16[320,256]{1,0:T(8,128)(2,1)S(1)} %constant_dynamic-slice_fusion), channel_id=1, source_target_pairs={{0,1},{1,0},{2,3},{3,2},{4,5},{5,4},{6,7},{7,6},{8,9},{9,8},{10,11... | collective-permute-start | bytes 491528 | tf_op jit(solution)/shard_map/ppermute | solution.py:528
  11.8 9.1 %collective-permute-start.3 = (bf16[320,128]{1,0:T(8,128)(2,1)}, bf16[320,128]{1,0:T(8,128)(2,1)S(1)}, u32[]{:S(2)}, u32[]{:S(2)}) collective-permute-start(bf16[320,128]{1,0:T(8,128)(2,1)} %get-tuple-element.46.refs_1_.refs_5_.refs_0_), channel_id=1, source_target_pairs={{0,8},{4,12},{8,0},{12,4},{16,24},{20,28},{24,16},{28,20},{1,9},{5... | collective-permute-start | bytes 245768 | tf_op jit(solution)/shard_map/ppermute | solution.py:528
  13.4 7.6 %collective-permute-start.4 = (bf16[320,128]{1,0:T(8,128)(2,1)}, bf16[320,128]{1,0:T(8,128)(2,1)S(1)}, u32[]{:S(2)}, u32[]{:S(2)}) collective-permute-start(bf16[320,128]{1,0:T(8,128)(2,1)} %get-tuple-element.46.refs_1_.refs_5_.refs_0_), channel_id=1, source_target_pairs={{0,16},{4,20},{8,24},{12,28},{16,0},{20,4},{24,8},{28,12},{1,17},{... | collective-permute-start | bytes 245768 | tf_op jit(solution)/shard_map/ppermute | solution.py:528
  14.9 6.1 %collective-permute-start.5 = (bf16[320,128]{1,0:T(8,128)(2,1)}, bf16[320,128]{1,0:T(8,128)(2,1)S(1)}, u32[]{:S(2)}, u32[]{:S(2)}) collective-permute-start(bf16[320,128]{1,0:T(8,128)(2,1)} %get-tuple-element.46.refs_1_.refs_5_.refs_0_), channel_id=1, source_target_pairs={{0,24},{4,28},{8,16},{12,20},{16,8},{20,12},{24,0},{28,4},{1,25},{... | collective-permute-start | bytes 245768 | tf_op jit(solution)/shard_map/ppermute | solution.py:528
  16.3 5.4 %collective-permute-start.2 = (bf16[320,256]{1,0:T(8,128)(2,1)S(1)}, bf16[320,256]{1,0:T(8,128)(2,1)S(1)}, u32[]{:S(2)}, u32[]{:S(2)}) collective-permute-start(bf16[320,256]{1,0:T(8,128)(2,1)S(1)} %shard_map.147.refs_1_.refs_4_), channel_id=1, source_target_pairs={{0,1},{1,0},{2,3},{3,2},{4,5},{5,4},{6,7},{7,6},{8,9},{9,8},{10,11... | collective-permute-start | bytes 491528 | tf_op jit(solution)/shard_map/ppermute | solution.py:528
  27.4 4.4 %collective-permute-start.9 = (bf16[4,320,128]{2,1,0:T(8,128)(2,1)S(1)}, bf16[4,320,128]{2,1,0:T(8,128)(2,1)S(1)}, u32[]{:S(2)}, u32[]{:S(2)}) collective-permute-start(bf16[4,320,128]{2,1,0:T(8,128)(2,1)S(1)} %bitcast.31), channel_id=1, source_target_pairs={{0,4},{4,0},{8,12},{12,8},{16,20},{20,16},{24,28},{28,24},{1,5},{5... | collective-permute-start | bytes 983048 | tf_op jit(solution)/shard_map/ppermute | solution.py:528
  27.6 10.3 %collective-permute-start.8 = (bf16[1328,128]{1,0:T(8,128)(2,1)S(1)}, bf16[1328,128]{1,0:T(8,128)(2,1)S(1)}, u32[]{:S(2)}, u32[]{:S(2)}) collective-permute-start(bf16[1328,128]{1,0:T(8,128)(2,1)S(1)} %shard_map.151.refs_4_.refs_0_), channel_id=1, source_target_pairs={{0,8},{4,12},{8,0},{12,4},{16,24},{20,28},{24,16},{28,20},{1,9},{5... | collective-permute-start | bytes 1019912 | tf_op jit(solution)/shard_map/ppermute | solution.py:663
  29.1 5.3 %collective-permute-start.10 = (bf16[160,128]{1,0:T(8,128)(2,1)S(1)}, bf16[160,128]{1,0:T(8,128)(2,1)S(1)}, u32[]{:S(2)}, u32[]{:S(2)}) collective-permute-start(bf16[160,128]{1,0:T(8,128)(2,1)S(1)} %copy-done.17), channel_id=1, source_target_pairs={{0,2},{1,3},{2,0},{3,1},{4,6},{5,7},{6,4},{7,5},{8,10},{9,11},{10,... | collective-permute-start | bytes 122888 | tf_op jit(solution)/shard_map/ppermute | solution.py:528
  30.3 11.0 %collective-permute-start.14 = (bf16[1280,128]{1,0:T(8,128)(2,1)S(1)}, bf16[1280,128]{1,0:T(8,128)(2,1)S(1)}, u32[]{:S(2)}, u32[]{:S(2)}) collective-permute-start(bf16[1280,128]{1,0:T(8,128)(2,1)S(1)} %copy-done.16), channel_id=1, source_target_pairs={{0,16},{4,20},{8,24},{12,28},{16,0},{20,4},{24,8},{28,12},{1,17},{... | collective-permute-start | bytes 983048 | tf_op jit(solution)/shard_map/ppermute | solution.py:528
  34.5 4.9 %collective-permute-start.11 = (bf16[160,128]{1,0:T(8,128)(2,1)S(1)}, bf16[160,128]{1,0:T(8,128)(2,1)S(1)}, u32[]{:S(2)}, u32[]{:S(2)}) collective-permute-start(bf16[160,128]{1,0:T(8,128)(2,1)S(1)} %shard_map.154), channel_id=1, source_target_pairs={{0,1},{1,0},{2,3},{3,2},{4,5},{5,4},{6,7},{7,6},{8,9},{9,8},{10,11... | collective-permute-start | bytes 122888 | tf_op jit(solution)/shard_map/ppermute | solution.py:528
  35.5 12.7 %collective-permute-start.16 = (bf16[896,128]{1,0:T(8,128)(2,1)S(1)}, bf16[896,128]{1,0:T(8,128)(2,1)S(1)}, u32[]{:S(2)}, u32[]{:S(2)}) collective-permute-start(bf16[896,128]{1,0:T(8,128)(2,1)S(1)} %shard_map.153.refs_2_.refs_0_), channel_id=1, source_target_pairs={{0,2},{1,3},{2,0},{3,1},{4,6},{5,7},{6,4},{7,5},{8,10},{9,11},{10,... | collective-permute-start | bytes 688136 | tf_op jit(solution)/shard_map/ppermute | solution.py:528
  37.2 11.2 %collective-permute-start.17 = (bf16[896,128]{1,0:T(8,128)(2,1)S(1)}, bf16[896,128]{1,0:T(8,128)(2,1)S(1)}, u32[]{:S(2)}, u32[]{:S(2)}) collective-permute-start(bf16[896,128]{1,0:T(8,128)(2,1)S(1)} %shard_map.153.refs_2_.refs_0_), channel_id=1, source_target_pairs={{0,1},{1,0},{2,3},{3,2},{4,5},{5,4},{6,7},{7,6},{8,9},{9,8},{10,11... | collective-permute-start | bytes 688136 | tf_op jit(solution)/shard_map/ppermute | solution.py:528
  39.7 9.0 %collective-permute-start.12 = (bf16[1328,128]{1,0:T(8,128)(2,1)S(1)}, bf16[1328,128]{1,0:T(8,128)(2,1)S(1)}, u32[]{:S(2)}, u32[]{:S(2)}) collective-permute-start(bf16[1328,128]{1,0:T(8,128)(2,1)S(1)} %shard_map.155.refs_7_.refs_4_.refs_2_), channel_id=1, source_target_pairs={{0,16},{4,20},{8,24},{12,28},{16,0},{20,4},{24,8},{28,12},{1,17},{... | collective-permute-start | bytes 1019912 | tf_op jit(solution)/shard_map/ppermute | solution.py:663
  41.3 7.3 %collective-permute-start.15 = (bf16[1280,128]{1,0:T(8,128)(2,1)S(1)}, bf16[1280,128]{1,0:T(8,128)(2,1)S(1)}, u32[]{:S(2)}, u32[]{:S(2)}) collective-permute-start(bf16[1280,128]{1,0:T(8,128)(2,1)S(1)} %shard_map.161), channel_id=1, source_target_pairs={{0,8},{4,12},{8,0},{12,4},{16,24},{20,28},{24,16},{28,20},{1,9},{5... | collective-permute-start | bytes 983048 | tf_op jit(solution)/shard_map/ppermute | solution.py:528
  41.9 4.3 %collective-permute-start.13 = (bf16[320,128]{1,0:T(8,128)(2,1)S(1)}, bf16[320,128]{1,0:T(8,128)(2,1)S(1)}, u32[]{:S(2)}, u32[]{:S(2)}) collective-permute-start(bf16[320,128]{1,0:T(8,128)(2,1)S(1)} %shard_map.159.refs_0_), channel_id=1, source_target_pairs={{0,4},{4,0},{8,12},{12,8},{16,20},{20,16},{24,28},{28,24},{1,5},{5... | collective-permute-start | bytes 245768 | tf_op jit(solution)/shard_map/ppermute | solution.py:528
  49.1 8.3 %collective-permute-start.20 = (bf16[640,128]{1,0:T(8,128)(2,1)S(1)}, bf16[640,128]{1,0:T(8,128)(2,1)S(1)}, u32[]{:S(2)}, u32[]{:S(2)}) collective-permute-start(bf16[640,128]{1,0:T(8,128)(2,1)S(1)} %shard_map.160.refs_5_.refs_0_), channel_id=1, source_target_pairs={{0,16},{4,20},{8,24},{12,28},{16,0},{20,4},{24,8},{28,12},{1,17},{... | collective-permute-start | bytes 491528 | tf_op jit(solution)/shard_map/ppermute | solution.py:528
  50.4 8.1 %collective-permute-start.19 = (bf16[896,128]{1,0:T(8,128)(2,1)S(1)}, bf16[896,128]{1,0:T(8,128)(2,1)S(1)}, u32[]{:S(2)}, u32[]{:S(2)}) collective-permute-start(bf16[896,128]{1,0:T(8,128)(2,1)S(1)} %shard_map.164.refs_2_), channel_id=1, source_target_pairs={{0,1},{1,0},{2,3},{3,2},{4,5},{5,4},{6,7},{7,6},{8,9},{9,8},{10,11... | collective-permute-start | bytes 688136 | tf_op jit(solution)/shard_map/ppermute | solution.py:528
  52.5 4.3 %collective-permute-start.21 = (bf16[1,128,256]{2,1,0:T(8,128)(2,1)S(1)}, bf16[1,128,256]{2,1,0:T(8,128)(2,1)S(1)}, u32[]{:S(2)}, u32[]{:S(2)}) collective-permute-start(bf16[1,128,256]{2,1,0:T(8,128)(2,1)S(1)} %bitcast.48), channel_id=1, source_target_pairs={{0,8},{4,12},{8,0},{12,4},{16,24},{20,28},{24,16},{28,20},{1,9},{5... | collective-permute-start | bytes 196616 | tf_op jit(solution)/shard_map/ppermute | solution.py:528
  56.8 5.0 %collective-permute-start.22 = (bf16[2,128,256]{2,1,0:T(8,128)(2,1)S(1)}, bf16[2,128,256]{2,1,0:T(8,128)(2,1)S(1)}, u32[]{:S(2)}, u32[]{:S(2)}) collective-permute-start(bf16[2,128,256]{2,1,0:T(8,128)(2,1)S(1)} %shard_map.165.refs_2_), channel_id=1, source_target_pairs={{0,16},{4,20},{8,24},{12,28},{16,0},{20,4},{24,8},{28,12},{1,17},{... | collective-permute-start | bytes 393224 | tf_op jit(solution)/shard_map/ppermute | solution.py:528
  57.4 11.0 %collective-permute-start.27 = (bf16[1280,128]{1,0:T(8,128)(2,1)S(1)}, bf16[1280,128]{1,0:T(8,128)(2,1)S(1)}, u32[]{:S(2)}, u32[]{:S(2)}) collective-permute-start(bf16[1280,128]{1,0:T(8,128)(2,1)S(1)} %shard_map.166.refs_17_), channel_id=1, source_target_pairs={{0,8},{4,12},{8,0},{12,4},{16,24},{20,28},{24,16},{28,20},{1,9},{5... | collective-permute-start | bytes 983048 | tf_op jit(solution)/shard_map/ppermute | solution.py:528
  64.0 6.9 %collective-permute-start.24 = (bf16[80,256]{1,0:T(8,128)(2,1)S(1)}, bf16[80,256]{1,0:T(8,128)(2,1)S(1)}, u32[]{:S(2)}, u32[]{:S(2)}) collective-permute-start(bf16[80,256]{1,0:T(8,128)(2,1)S(1)} %get-tuple-element.80), channel_id=1, source_target_pairs={{0,3},{1,2},{2,1},{3,0},{4,7},{5,6},{6,5},{7,4},{8,11},{9,10},{10,... | collective-permute-start | bytes 122888 | tf_op jit(solution)/shard_map/ppermute | solution.py:528
  65.6 5.6 %collective-permute-start.25 = (bf16[80,256]{1,0:T(8,128)(2,1)S(1)}, bf16[80,256]{1,0:T(8,128)(2,1)S(1)}, u32[]{:S(2)}, u32[]{:S(2)}) collective-permute-start(bf16[80,256]{1,0:T(8,128)(2,1)S(1)} %get-tuple-element.81), channel_id=1, source_target_pairs={{0,2},{1,3},{2,0},{3,1},{4,6},{5,7},{6,4},{7,5},{8,10},{9,11},{10,... | collective-permute-start | bytes 122888 | tf_op jit(solution)/shard_map/ppermute | solution.py:528
  66.2 5.0 %collective-permute-start.26 = (bf16[80,256]{1,0:T(8,128)(2,1)S(1)}, bf16[80,256]{1,0:T(8,128)(2,1)S(1)}, u32[]{:S(2)}, u32[]{:S(2)}) collective-permute-start(bf16[80,256]{1,0:T(8,128)(2,1)S(1)} %get-tuple-element.82), channel_id=1, source_target_pairs={{0,1},{1,0},{2,3},{3,2},{4,5},{5,4},{6,7},{7,6},{8,9},{9,8},{10,11... | collective-permute-start | bytes 122888 | tf_op jit(solution)/shard_map/ppermute | solution.py:528
  (26 other events, 115.6 us)

commit v19 on v18

--- a/solution.py
+++ b/solution.py
@@ -159,7 +159,7 @@
     dyt_ref[width : width + 2 * heads, :] = jnp.concatenate(high_low(decay), axis=0).astype(BF16)
 
 
-def scale_kernel(x_ref, dy_ref, h_ref, cumt_ref, cum_ref, xs_ref, carried_ref, token_ref, *rest):
+def scale_kernel(x_ref, cumt_ref, cum_ref, xs_ref, token_ref, *rest):
     outs, xt_ref = rest[:-1], rest[-1]
     length, width = x_ref.shape
     heads = cumt_ref.shape[0]
@@ -168,17 +168,12 @@
     pad = jnp.zeros((LANES - heads, length), F32)
     cum = jnp.concatenate([cumt_ref[...], pad], axis=0).T
     into_end = jnp.exp(cum[length - 1 : length] - cum_ref[...])
-    table = jnp.concatenate([halves(jnp.exp(cum)), halves(into_end)], axis=0)
-    carried = jnp.zeros(carried_ref.shape, F32)
+    table = halves(into_end)
     for j in range(width // LANES):
         span = slice(j * LANES, (j + 1) * LANES)
         scale = dot(table, to_lanes(j, size), 1, 0)
-        x_f = x_ref[:, span].astype(F32)
         xt_ref[span, :] = x_ref[:, span].T
-        xs_ref[:, span] = (x_f * scale[length:]).astype(BF16)
-        dys = (dy_ref[:, span].astype(F32) * scale[:length]).astype(BF16)
-        carried = carried + dot(dys, h_ref[span, :], 1, 0)
-    carried_ref[...] = carried
+        xs_ref[:, span] = (x_ref[:, span].astype(F32) * scale).astype(BF16)
     token_ref[...] = jnp.zeros_like(token_ref)
     block = width // n_chip
     s = 0
@@ -364,10 +359,11 @@
     ex_ref[...] = rowm_ref[rows, :] + jnp.exp(cumt_ref[rows, :]) * reach[rows] - own
 
 
-def close_kernel(mixed_ref, bc_ref, carried_ref, db_ref, dc_ref):
+def close_kernel(mixed_ref, bc_ref, dyt_ref, h_ref, db_ref, dc_ref):
+    carried = dot(dyt_ref[: h_ref.shape[0], :], h_ref[...], 0, 0)
     mixed = mixed_ref[...].astype(BF16)
     db_ref[...] = dot(mixed, bc_ref[:, LANES:], 1, 0)
-    dc_ref[...] = (dot(mixed, bc_ref[:, :LANES], 0, 0) + carried_ref[...]).astype(BF16)
+    dc_ref[...] = (dot(mixed, bc_ref[:, :LANES], 0, 0) + carried).astype(BF16)
 
 
 def db_kernel(xs_ref, own_ref, recv_ref, db_ref, dc_ref, out_ref):
@@ -600,15 +596,15 @@
     mine = gathered(w_half, "dp", n_dp // 2)[1:]
     w_copy = joined([w_far], after=(rows,))
     mine += gathered(w_copy, "dp", n_dp // 2)
-    xs, carried, scaled, *xt = call(
+    xs, scaled, *xt = call(
         scale_kernel,
-        [shape((length, width), BF16), shape((length, half), F32), shape((8, LANES), F32)]
+        [shape((length, width), BF16), shape((8, LANES), F32)]
         + [shape((k * width // n_chip, length), BF16) for k in blocks],
         1.5,
-        (x, dy, h_in, cumt, cum),
+        (x, cumt, cum),
         after=(rows,),
         scratch=[pltpu.VMEM((width, length), BF16)],
-        fetch=(0, 1, 2, 3, 4),
+        fetch=(0, 1, 2),
         limit=60,
     )
     if n_dp == 4:
@@ -695,7 +691,7 @@
         close_kernel,
         [shape((length, half), F32), shape((length, half), BF16)],
         0.3,
-        (mixed, bc, carried),
+        (mixed, bc, dyt, h_in),
     )
 
     held = (dc,)

time: 72.2 us -> 72.1 us (level)
  waiting for transfers between devices: 15.5 us -> 17.1 us
  Pallas kernels: 22.6 us -> 21.1 us
    ppermute x26, waiting for transfers between devices: 15.2 us -> 16.7 us  [xored(): return lax.ppermute(array, axis, [(i, i ^ mask) for i in range(count)])]
    pallas_call x27, Pallas kernels: 22.6 us -> 21.1 us  [call(): pl.pallas_call(body, out_shape=outs, in_specs=specs + [pl.BlockSpec(memor...]
    unnamed x44 -> x42, local copies, waits for them, and re-layouts: 1.69 us -> 1.69 us
  transfers between devices with their start and end apart: 28 -> 28, of which waited for: 13 -> 15; matrix products, arithmetic and copies ran while one was open for 0% -> 0% of each run, Pallas kernels for 28% -> 26%
where the time goes in v19:
time: 72.1 us; the launch traced here: 71.9 us
  starting transfers between devices  29.4 us (41%)
  Pallas kernels  21.1 us (29%)
  waiting for transfers between devices  17.1 us (24%)
  local copies, waits for them, and re-layouts  2.63 us (4%)
  between operations  1.67 us (2%)
    ppermute x26, starting transfers between devices, xored(): return lax.ppermute(array, axis, [(i, i ^ mask) for i in range(count)])  26.1 us
    pallas_call x27, Pallas kernels, call(): pl.pallas_call(body, out_shape=outs, in_specs=specs + [pl.BlockSpec(memor...  21.1 us
    ppermute x26, waiting for transfers between devices, xored(): return lax.ppermute(array, axis, [(i, i ^ mask) for i in range(count)])  16.7 us
    ppermute x2, starting transfers between devices, per_device(): arrived.append(lax.ppermute(climbs[-1], 'tm', moves))  3.32 us
    unnamed x42, local copies, waits for them, and re-layouts  1.69 us
  transfers between devices with their start and end apart: 28, of which 15 were waited for; matrix products, arithmetic and copies ran while one was open for 0% of the time, Pallas kernels for 26%

profile of v19, /device:TPU:0, one launch (start us, length us, event | category | flops | bytes accessed | tf_op | source)
XLA Modules:
  0.0 71.9 jit_solution(1361356493064113014)
XLA Ops:
  1.6 4.1 %collective-permute-start.1 = (bf16[320,256]{1,0:T(8,128)(2,1)S(1)}, bf16[320,256]{1,0:T(8,128)(2,1)S(1)}, u32[]{:S(2)}, u32[]{:S(2)}) collective-permute-start(bf16[320,256]{1,0:T(8,128)(2,1)S(1)} %constant_dynamic-slice_fusion), channel_id=1, source_target_pairs={{0,2},{1,3},{2,0},{3,1},{4,6},{5,7},{6,4},{7,5},{8,10},{9,11},{10,... | collective-permute-start | bytes 491528 | tf_op jit(solution)/shard_map/ppermute | solution.py:524
  5.7 1.6 %collective-permute-start = (bf16[320,256]{1,0:T(8,128)(2,1)S(1)}, bf16[320,256]{1,0:T(8,128)(2,1)S(1)}, u32[]{:S(2)}, u32[]{:S(2)}) collective-permute-start(bf16[320,256]{1,0:T(8,128)(2,1)S(1)} %constant_dynamic-slice_fusion), channel_id=1, source_target_pairs={{0,1},{1,0},{2,3},{3,2},{4,5},{5,4},{6,7},{7,6},{8,9},{9,8},{10,11... | collective-permute-start | bytes 491528 | tf_op jit(solution)/shard_map/ppermute | solution.py:524
  7.9 3.9 %shard_map.146 = (f32[40,128]{1,0:T(8,128)}, f32[128,128]{1,0:T(8,128)}, bf16[2640,128]{1,0:T(8,128)(2,1)}, bf16[320,128]{1,0:T(8,128)(2,1)}, bf16[160,128]{1,0:T(8,128)(2,1)}, /*index=5*/bf16[160,128]{1,0:T(8,128)(2,1)}) custom-call(bf16[128,2560]{1,0:T(8,128)(2,1)} %bitcast.36, bf16[128,2560]{1,0:T(8,128)(2,1)} %bitcast.33, f32[40,128]{1,0:T(8,128)} %bitcast.53, ...), custom_call_target="tpu_custom_call" | custom-call | flops 4499999744 | bytes 1000 | tf_op jit(solution)/shard_map/pallas_call | solution.py:81
  11.8 1.6 %collective-permute-start.3 = (bf16[320,128]{1,0:T(8,128)(2,1)}, bf16[320,128]{1,0:T(8,128)(2,1)S(1)}, u32[]{:S(2)}, u32[]{:S(2)}) collective-permute-start(bf16[320,128]{1,0:T(8,128)(2,1)} %get-tuple-element.45.refs_1_.refs_3_.refs_0_), channel_id=1, source_target_pairs={{0,8},{4,12},{8,0},{12,4},{16,24},{20,28},{24,16},{28,20},{1,9},{5... | collective-permute-start | bytes 245768 | tf_op jit(solution)/shard_map/ppermute | solution.py:524
  13.4 1.5 %collective-permute-start.4 = (bf16[320,128]{1,0:T(8,128)(2,1)}, bf16[320,128]{1,0:T(8,128)(2,1)S(1)}, u32[]{:S(2)}, u32[]{:S(2)}) collective-permute-start(bf16[320,128]{1,0:T(8,128)(2,1)} %get-tuple-element.45.refs_1_.refs_3_.refs_0_), channel_id=1, source_target_pairs={{0,16},{4,20},{8,24},{12,28},{16,0},{20,4},{24,8},{28,12},{1,17},{... | collective-permute-start | bytes 245768 | tf_op jit(solution)/shard_map/ppermute | solution.py:524
  16.8 2.6 %shard_map.148 = (bf16[128,2560]{1,0:T(8,128)(2,1)}, f32[8,128]{1,0:T(8,128)}, bf16[640,128]{1,0:T(8,128)(2,1)}, bf16[640,128]{1,0:T(8,128)(2,1)}, bf16[1280,128]{1,0:T(8,128)(2,1)}) custom-call(bf16[128,2560]{1,0:T(8,128)(2,1)} %bitcast.37, f32[40,128]{1,0:T(8,128)} %get-tuple-element.46.refs_1_.refs_3_.refs_2_, ...), custom_call_target="tpu_custom_call" | custom-call | flops 4499999744 | bytes 1000 | tf_op jit(solution)/shard_map/pallas_call | solution.py:81
  22.5 1.9 %collective-permute-done.6.refs_6_ = bf16[3,320,256]{2,1,0:T(8,128)(2,1)S(1)} collective-permute-done((bf16[3,320,256]{2,1,0:T(8,128)(2,1)S(1)}, bf16[3,320,256]{2,1,0:T(8,128)(2,1)S(1)}, u32[]{:S(2)}, u32[]{:S(2)}) %collective-permute-start.6) | collective-permute-done | bytes 491552 | tf_op jit(solution)/shard_map/ppermute | solution.py:524
  25.7 1.5 %collective-permute-done.7.refs_1_.refs_3_ = bf16[1328,128]{1,0:T(8,128)(2,1)S(1)} collective-permute-done((bf16[1328,128]{1,0:T(8,128)(2,1)S(1)}, bf16[1328,128]{1,0:T(8,128)(2,1)S(1)}, u32[]{:S(2)}, u32[]{:S(2)}) %collective-permute-start.7) | collective-permute-done | bytes 340000 | tf_op jit(solution)/shard_map/ppermute | solution.py:524
  27.6 1.5 %collective-permute-start.8 = (bf16[1328,128]{1,0:T(8,128)(2,1)S(1)}, bf16[1328,128]{1,0:T(8,128)(2,1)S(1)}, u32[]{:S(2)}, u32[]{:S(2)}) collective-permute-start(bf16[1328,128]{1,0:T(8,128)(2,1)S(1)} %shard_map.151.refs_4_.refs_0_), channel_id=1, source_target_pairs={{0,8},{4,12},{8,0},{12,4},{16,24},{20,28},{24,16},{28,20},{1,9},{5... | collective-permute-start | bytes 1019912 | tf_op jit(solution)/shard_map/ppermute | solution.py:659
  30.3 1.5 %collective-permute-start.14 = (bf16[1280,128]{1,0:T(8,128)(2,1)S(1)}, bf16[1280,128]{1,0:T(8,128)(2,1)S(1)}, u32[]{:S(2)}, u32[]{:S(2)}) collective-permute-start(bf16[1280,128]{1,0:T(8,128)(2,1)S(1)} %copy-done.15), channel_id=1, source_target_pairs={{0,16},{4,20},{8,24},{12,28},{16,0},{20,4},{24,8},{28,12},{1,17},{... | collective-permute-start | bytes 983048 | tf_op jit(solution)/shard_map/ppermute | solution.py:524
  31.9 1.7 %shard_map.153.refs_2_.refs_0_ = bf16[896,128]{1,0:T(8,128)(2,1)S(1)} custom-call(bf16[4,320,128]{2,1,0:T(8,128)(2,1)S(1)} %bitcast.32, bf16[4,320,128]{2,1,0:T(8,128)(2,1)S(1)} %collective-permute-done.9.refs_1_, bf16[2560,896]{1,0:T(8,128)(2,1)S(1)} %bitcast.27, bf16[2560,896]{1,0:T(8,128)(2,1)S(1)} %bitcast.30, ...), custom_call_target="tpu_custom_call" | custom-call | flops 1050000000 | bytes 1000 | tf_op jit(solution)/shard_map/pallas_call | solution.py:81
  35.5 1.7 %collective-permute-start.16 = (bf16[896,128]{1,0:T(8,128)(2,1)S(1)}, bf16[896,128]{1,0:T(8,128)(2,1)S(1)}, u32[]{:S(2)}, u32[]{:S(2)}) collective-permute-start(bf16[896,128]{1,0:T(8,128)(2,1)S(1)} %shard_map.153.refs_2_.refs_0_), channel_id=1, source_target_pairs={{0,2},{1,3},{2,0},{3,1},{4,6},{5,7},{6,4},{7,5},{8,10},{9,11},{10,... | collective-permute-start | bytes 688136 | tf_op jit(solution)/shard_map/ppermute | solution.py:524
  37.9 1.3 %collective-permute-done.11.refs_4_.refs_1_.refs_3_ = bf16[160,128]{1,0:T(8,128)(2,1)S(1)} collective-permute-done((bf16[160,128]{1,0:T(8,128)(2,1)S(1)}, bf16[160,128]{1,0:T(8,128)(2,1)S(1)}, u32[]{:S(2)}, u32[]{:S(2)}) %collective-permute-start.11) | collective-permute-done | bytes 40992 | tf_op jit(solution)/shard_map/ppermute | solution.py:524
  39.3 1.8 %collective-permute-start.12 = (bf16[1328,128]{1,0:T(8,128)(2,1)S(1)}, bf16[1328,128]{1,0:T(8,128)(2,1)S(1)}, u32[]{:S(2)}, u32[]{:S(2)}) collective-permute-start(bf16[1328,128]{1,0:T(8,128)(2,1)S(1)} %shard_map.155.refs_7_.refs_4_.refs_2_), channel_id=1, source_target_pairs={{0,16},{4,20},{8,24},{12,28},{16,0},{20,4},{24,8},{28,12},{1,17},{... | collective-permute-start | bytes 1019912 | tf_op jit(solution)/shard_map/ppermute | solution.py:659
  41.9 2.0 %shard_map.156 = (f32[128,1280]{1,0:T(8,128)S(1)}, f32[128,128]{1,0:T(8,128)S(1)}, f32[20,128]{1,0:T(8,128)S(1)}, f32[20,128]{1,0:T(8,128)S(1)}) custom-call(bf16[128,2560]{1,0:T(8,128)(2,1)S(1)} %bitcast.39, bf16[128,2560]{1,0:T(8,128)(2,1)S(1)} %bitcast.34, bf16[128,256]{1,0:T(8,128)(2,1)S(1)} %get-tuple-element.49.refs_2_.refs_1_, ...), custom_call_target="tpu_custom_call" | custom-call | flops 2100000000 | bytes 1000 | tf_op jit(solution)/shard_map/pallas_call | solution.py:81
  43.9 2.0 %shard_map.157 = (f32[128,1280]{1,0:T(8,128)S(1)}, f32[128,128]{1,0:T(8,128)S(1)}, f32[20,128]{1,0:T(8,128)S(1)}, f32[20,128]{1,0:T(8,128)S(1)}) custom-call(bf16[128,2560]{1,0:T(8,128)(2,1)S(1)} %bitcast.40, bf16[128,2560]{1,0:T(8,128)(2,1)S(1)} %bitcast.35, bf16[128,256]{1,0:T(8,128)(2,1)S(1)} %get-tuple-element.49.refs_2_.refs_1_, ...), custom_call_target="tpu_custom_call" | custom-call | flops 2100000000 | bytes 1000 | tf_op jit(solution)/shard_map/pallas_call | solution.py:81
  46.3 1.7 %collective-permute-done.16.refs_7_.refs_0_ = bf16[896,128]{1,0:T(8,128)(2,1)S(1)} collective-permute-done((bf16[896,128]{1,0:T(8,128)(2,1)S(1)}, bf16[896,128]{1,0:T(8,128)(2,1)S(1)}, u32[]{:S(2)}, u32[]{:S(2)}) %collective-permute-start.16) | collective-permute-done | bytes 229408 | tf_op jit(solution)/shard_map/ppermute | solution.py:524
  50.3 1.8 %collective-permute-start.19 = (bf16[896,128]{1,0:T(8,128)(2,1)S(1)}, bf16[896,128]{1,0:T(8,128)(2,1)S(1)}, u32[]{:S(2)}, u32[]{:S(2)}) collective-permute-start(bf16[896,128]{1,0:T(8,128)(2,1)S(1)} %shard_map.164.refs_2_), channel_id=1, source_target_pairs={{0,1},{1,0},{2,3},{3,2},{4,5},{5,4},{6,7},{7,6},{8,9},{9,8},{10,11... | collective-permute-start | bytes 688136 | tf_op jit(solution)/shard_map/ppermute | solution.py:524
  53.1 3.7 %collective-permute-done.21.refs_1_.refs_4_ = bf16[1,128,256]{2,1,0:T(8,128)(2,1)S(1)} collective-permute-done((bf16[1,128,256]{2,1,0:T(8,128)(2,1)S(1)}, bf16[1,128,256]{2,1,0:T(8,128)(2,1)S(1)}, u32[]{:S(2)}, u32[]{:S(2)}) %collective-permute-start.21) | collective-permute-done | bytes 65568 | tf_op jit(solution)/shard_map/ppermute | solution.py:524
  58.1 2.6 %shard_map.167 = (bf16[128,2560]{1,0:T(8,128)(2,1)}, f32[40,128]{1,0:T(8,128)}, f32[40,128]{1,0:T(8,128)}, f32[8,128]{1,0:T(8,128)S(1)}) custom-call(bf16[128,2560]{1,0:T(8,128)(2,1)S(1)} %bitcast.41, bf16[128,256]{1,0:T(8,128)(2,1)S(1)} %get-tuple-element.49.refs_2_.refs_1_, f32[40,128]{1,0:T(8,128)S(1)} %copy-done.13, f32[40,128]{1,0:T(8,128)S(1)} %bitcast.51, ...), custom_call_target="tpu_custom_call" | custom-call | flops 3000000000 | bytes 1000 | tf_op jit(solution)/shard_map/pallas_call | solution.py:81
  62.5 1.4 %collective-permute-done.23.refs_1_ = bf16[320,256]{1,0:T(8,128)(2,1)S(1)} collective-permute-done((bf16[320,256]{1,0:T(8,128)(2,1)S(1)}, bf16[320,256]{1,0:T(8,128)(2,1)S(1)}, u32[]{:S(2)}, u32[]{:S(2)}) %collective-permute-start.23) | collective-permute-done | bytes 163872 | tf_op jit(solution)/shard_map/ppermute | solution.py:524
  64.0 1.6 %collective-permute-start.24 = (bf16[80,256]{1,0:T(8,128)(2,1)S(1)}, bf16[80,256]{1,0:T(8,128)(2,1)S(1)}, u32[]{:S(2)}, u32[]{:S(2)}) collective-permute-start(bf16[80,256]{1,0:T(8,128)(2,1)S(1)} %get-tuple-element.78), channel_id=1, source_target_pairs={{0,3},{1,2},{2,1},{3,0},{4,7},{5,6},{6,5},{7,4},{8,11},{9,10},{10,... | collective-permute-start | bytes 122888 | tf_op jit(solution)/shard_map/ppermute | solution.py:524
  66.1 2.4 %collective-permute-start.26 = (bf16[80,256]{1,0:T(8,128)(2,1)S(1)}, bf16[80,256]{1,0:T(8,128)(2,1)S(1)}, u32[]{:S(2)}, u32[]{:S(2)}) collective-permute-start(bf16[80,256]{1,0:T(8,128)(2,1)S(1)} %get-tuple-element.80), channel_id=1, source_target_pairs={{0,1},{1,0},{2,3},{3,2},{4,5},{5,4},{6,7},{7,6},{8,9},{9,8},{10,11... | collective-permute-start | bytes 122888 | tf_op jit(solution)/shard_map/ppermute | solution.py:524
  68.5 2.4 %shard_map.171 = (bf16[896,640]{1,0:T(8,128)(2,1)}, f32[8,128]{1,0:T(8,128)S(1)}) custom-call(bf16[896,128]{1,0:T(8,128)(2,1)S(1)} %shard_map.153.refs_2_.refs_0_, bf16[896,128]{1,0:T(8,128)(2,1)S(1)} %collective-permute-done.17.refs_8_.refs_1_, bf16[896,128]{1,0:T(8,128)(2,1)S(1)} %shard_map.164.refs_2_, ...), custom_call_target="tpu_custom_call" | custom-call | flops 3000000000 | bytes 1000 | tf_op jit(solution)/shard_map/pallas_call | solution.py:81
  (105 shorter events, 20.5 us)
Async XLA Ops:
  1.6 13.8 %collective-permute-start.1 = (bf16[320,256]{1,0:T(8,128)(2,1)S(1)}, bf16[320,256]{1,0:T(8,128)(2,1)S(1)}, u32[]{:S(2)}, u32[]{:S(2)}) collective-permute-start(bf16[320,256]{1,0:T(8,128)(2,1)S(1)} %constant_dynamic-slice_fusion), channel_id=1, source_target_pairs={{0,2},{1,3},{2,0},{3,1},{4,6},{5,7},{6,4},{7,5},{8,10},{9,11},{10,... | collective-permute-start | bytes 491528 | tf_op jit(solution)/shard_map/ppermute | solution.py:524
  5.7 14.8 %collective-permute-start = (bf16[320,256]{1,0:T(8,128)(2,1)S(1)}, bf16[320,256]{1,0:T(8,128)(2,1)S(1)}, u32[]{:S(2)}, u32[]{:S(2)}) collective-permute-start(bf16[320,256]{1,0:T(8,128)(2,1)S(1)} %constant_dynamic-slice_fusion), channel_id=1, source_target_pairs={{0,1},{1,0},{2,3},{3,2},{4,5},{5,4},{6,7},{7,6},{8,9},{9,8},{10,11... | collective-permute-start | bytes 491528 | tf_op jit(solution)/shard_map/ppermute | solution.py:524
  11.8 7.6 %collective-permute-start.3 = (bf16[320,128]{1,0:T(8,128)(2,1)}, bf16[320,128]{1,0:T(8,128)(2,1)S(1)}, u32[]{:S(2)}, u32[]{:S(2)}) collective-permute-start(bf16[320,128]{1,0:T(8,128)(2,1)} %get-tuple-element.45.refs_1_.refs_3_.refs_0_), channel_id=1, source_target_pairs={{0,8},{4,12},{8,0},{12,4},{16,24},{20,28},{24,16},{28,20},{1,9},{5... | collective-permute-start | bytes 245768 | tf_op jit(solution)/shard_map/ppermute | solution.py:524
  13.4 6.1 %collective-permute-start.4 = (bf16[320,128]{1,0:T(8,128)(2,1)}, bf16[320,128]{1,0:T(8,128)(2,1)S(1)}, u32[]{:S(2)}, u32[]{:S(2)}) collective-permute-start(bf16[320,128]{1,0:T(8,128)(2,1)} %get-tuple-element.45.refs_1_.refs_3_.refs_0_), channel_id=1, source_target_pairs={{0,16},{4,20},{8,24},{12,28},{16,0},{20,4},{24,8},{28,12},{1,17},{... | collective-permute-start | bytes 245768 | tf_op jit(solution)/shard_map/ppermute | solution.py:524
  14.9 5.6 %collective-permute-start.5 = (bf16[320,128]{1,0:T(8,128)(2,1)}, bf16[320,128]{1,0:T(8,128)(2,1)S(1)}, u32[]{:S(2)}, u32[]{:S(2)}) collective-permute-start(bf16[320,128]{1,0:T(8,128)(2,1)} %get-tuple-element.45.refs_1_.refs_3_.refs_0_), channel_id=1, source_target_pairs={{0,24},{4,28},{8,16},{12,20},{16,8},{20,12},{24,0},{28,4},{1,25},{... | collective-permute-start | bytes 245768 | tf_op jit(solution)/shard_map/ppermute | solution.py:524
  16.3 5.4 %collective-permute-start.2 = (bf16[320,256]{1,0:T(8,128)(2,1)S(1)}, bf16[320,256]{1,0:T(8,128)(2,1)S(1)}, u32[]{:S(2)}, u32[]{:S(2)}) collective-permute-start(bf16[320,256]{1,0:T(8,128)(2,1)S(1)} %shard_map.147.refs_1_.refs_4_), channel_id=1, source_target_pairs={{0,1},{1,0},{2,3},{3,2},{4,5},{5,4},{6,7},{7,6},{8,9},{9,8},{10,11... | collective-permute-start | bytes 491528 | tf_op jit(solution)/shard_map/ppermute | solution.py:524
  27.4 4.4 %collective-permute-start.9 = (bf16[4,320,128]{2,1,0:T(8,128)(2,1)S(1)}, bf16[4,320,128]{2,1,0:T(8,128)(2,1)S(1)}, u32[]{:S(2)}, u32[]{:S(2)}) collective-permute-start(bf16[4,320,128]{2,1,0:T(8,128)(2,1)S(1)} %bitcast.31), channel_id=1, source_target_pairs={{0,4},{4,0},{8,12},{12,8},{16,20},{20,16},{24,28},{28,24},{1,5},{5... | collective-permute-start | bytes 983048 | tf_op jit(solution)/shard_map/ppermute | solution.py:524
  27.6 10.3 %collective-permute-start.8 = (bf16[1328,128]{1,0:T(8,128)(2,1)S(1)}, bf16[1328,128]{1,0:T(8,128)(2,1)S(1)}, u32[]{:S(2)}, u32[]{:S(2)}) collective-permute-start(bf16[1328,128]{1,0:T(8,128)(2,1)S(1)} %shard_map.151.refs_4_.refs_0_), channel_id=1, source_target_pairs={{0,8},{4,12},{8,0},{12,4},{16,24},{20,28},{24,16},{28,20},{1,9},{5... | collective-permute-start | bytes 1019912 | tf_op jit(solution)/shard_map/ppermute | solution.py:659
  29.1 5.2 %collective-permute-start.10 = (bf16[160,128]{1,0:T(8,128)(2,1)S(1)}, bf16[160,128]{1,0:T(8,128)(2,1)S(1)}, u32[]{:S(2)}, u32[]{:S(2)}) collective-permute-start(bf16[160,128]{1,0:T(8,128)(2,1)S(1)} %copy-done.16), channel_id=1, source_target_pairs={{0,2},{1,3},{2,0},{3,1},{4,6},{5,7},{6,4},{7,5},{8,10},{9,11},{10,... | collective-permute-start | bytes 122888 | tf_op jit(solution)/shard_map/ppermute | solution.py:524
  30.3 10.9 %collective-permute-start.14 = (bf16[1280,128]{1,0:T(8,128)(2,1)S(1)}, bf16[1280,128]{1,0:T(8,128)(2,1)S(1)}, u32[]{:S(2)}, u32[]{:S(2)}) collective-permute-start(bf16[1280,128]{1,0:T(8,128)(2,1)S(1)} %copy-done.15), channel_id=1, source_target_pairs={{0,16},{4,20},{8,24},{12,28},{16,0},{20,4},{24,8},{28,12},{1,17},{... | collective-permute-start | bytes 983048 | tf_op jit(solution)/shard_map/ppermute | solution.py:524
  34.4 4.7 %collective-permute-start.11 = (bf16[160,128]{1,0:T(8,128)(2,1)S(1)}, bf16[160,128]{1,0:T(8,128)(2,1)S(1)}, u32[]{:S(2)}, u32[]{:S(2)}) collective-permute-start(bf16[160,128]{1,0:T(8,128)(2,1)S(1)} %shard_map.154), channel_id=1, source_target_pairs={{0,1},{1,0},{2,3},{3,2},{4,5},{5,4},{6,7},{7,6},{8,9},{9,8},{10,11... | collective-permute-start | bytes 122888 | tf_op jit(solution)/shard_map/ppermute | solution.py:524
  35.5 12.5 %collective-permute-start.16 = (bf16[896,128]{1,0:T(8,128)(2,1)S(1)}, bf16[896,128]{1,0:T(8,128)(2,1)S(1)}, u32[]{:S(2)}, u32[]{:S(2)}) collective-permute-start(bf16[896,128]{1,0:T(8,128)(2,1)S(1)} %shard_map.153.refs_2_.refs_0_), channel_id=1, source_target_pairs={{0,2},{1,3},{2,0},{3,1},{4,6},{5,7},{6,4},{7,5},{8,10},{9,11},{10,... | collective-permute-start | bytes 688136 | tf_op jit(solution)/shard_map/ppermute | solution.py:524
  37.2 11.1 %collective-permute-start.17 = (bf16[896,128]{1,0:T(8,128)(2,1)S(1)}, bf16[896,128]{1,0:T(8,128)(2,1)S(1)}, u32[]{:S(2)}, u32[]{:S(2)}) collective-permute-start(bf16[896,128]{1,0:T(8,128)(2,1)S(1)} %shard_map.153.refs_2_.refs_0_), channel_id=1, source_target_pairs={{0,1},{1,0},{2,3},{3,2},{4,5},{5,4},{6,7},{7,6},{8,9},{9,8},{10,11... | collective-permute-start | bytes 688136 | tf_op jit(solution)/shard_map/ppermute | solution.py:524
  39.3 9.3 %collective-permute-start.12 = (bf16[1328,128]{1,0:T(8,128)(2,1)S(1)}, bf16[1328,128]{1,0:T(8,128)(2,1)S(1)}, u32[]{:S(2)}, u32[]{:S(2)}) collective-permute-start(bf16[1328,128]{1,0:T(8,128)(2,1)S(1)} %shard_map.155.refs_7_.refs_4_.refs_2_), channel_id=1, source_target_pairs={{0,16},{4,20},{8,24},{12,28},{16,0},{20,4},{24,8},{28,12},{1,17},{... | collective-permute-start | bytes 1019912 | tf_op jit(solution)/shard_map/ppermute | solution.py:659
  41.2 7.5 %collective-permute-start.15 = (bf16[1280,128]{1,0:T(8,128)(2,1)S(1)}, bf16[1280,128]{1,0:T(8,128)(2,1)S(1)}, u32[]{:S(2)}, u32[]{:S(2)}) collective-permute-start(bf16[1280,128]{1,0:T(8,128)(2,1)S(1)} %shard_map.161), channel_id=1, source_target_pairs={{0,8},{4,12},{8,0},{12,4},{16,24},{20,28},{24,16},{28,20},{1,9},{5... | collective-permute-start | bytes 983048 | tf_op jit(solution)/shard_map/ppermute | solution.py:524
  41.8 4.4 %collective-permute-start.13 = (bf16[320,128]{1,0:T(8,128)(2,1)S(1)}, bf16[320,128]{1,0:T(8,128)(2,1)S(1)}, u32[]{:S(2)}, u32[]{:S(2)}) collective-permute-start(bf16[320,128]{1,0:T(8,128)(2,1)S(1)} %shard_map.159.refs_0_), channel_id=1, source_target_pairs={{0,4},{4,0},{8,12},{12,8},{16,20},{20,16},{24,28},{28,24},{1,5},{5... | collective-permute-start | bytes 245768 | tf_op jit(solution)/shard_map/ppermute | solution.py:524
  49.1 8.3 %collective-permute-start.20 = (bf16[640,128]{1,0:T(8,128)(2,1)S(1)}, bf16[640,128]{1,0:T(8,128)(2,1)S(1)}, u32[]{:S(2)}, u32[]{:S(2)}) collective-permute-start(bf16[640,128]{1,0:T(8,128)(2,1)S(1)} %shard_map.160.refs_5_.refs_0_), channel_id=1, source_target_pairs={{0,16},{4,20},{8,24},{12,28},{16,0},{20,4},{24,8},{28,12},{1,17},{... | collective-permute-start | bytes 491528 | tf_op jit(solution)/shard_map/ppermute | solution.py:524
  50.3 7.7 %collective-permute-start.19 = (bf16[896,128]{1,0:T(8,128)(2,1)S(1)}, bf16[896,128]{1,0:T(8,128)(2,1)S(1)}, u32[]{:S(2)}, u32[]{:S(2)}) collective-permute-start(bf16[896,128]{1,0:T(8,128)(2,1)S(1)} %shard_map.164.refs_2_), channel_id=1, source_target_pairs={{0,1},{1,0},{2,3},{3,2},{4,5},{5,4},{6,7},{7,6},{8,9},{9,8},{10,11... | collective-permute-start | bytes 688136 | tf_op jit(solution)/shard_map/ppermute | solution.py:524
  52.5 4.3 %collective-permute-start.21 = (bf16[1,128,256]{2,1,0:T(8,128)(2,1)S(1)}, bf16[1,128,256]{2,1,0:T(8,128)(2,1)S(1)}, u32[]{:S(2)}, u32[]{:S(2)}) collective-permute-start(bf16[1,128,256]{2,1,0:T(8,128)(2,1)S(1)} %bitcast.47), channel_id=1, source_target_pairs={{0,8},{4,12},{8,0},{12,4},{16,24},{20,28},{24,16},{28,20},{1,9},{5... | collective-permute-start | bytes 196616 | tf_op jit(solution)/shard_map/ppermute | solution.py:524
  56.8 5.0 %collective-permute-start.22 = (bf16[2,128,256]{2,1,0:T(8,128)(2,1)S(1)}, bf16[2,128,256]{2,1,0:T(8,128)(2,1)S(1)}, u32[]{:S(2)}, u32[]{:S(2)}) collective-permute-start(bf16[2,128,256]{2,1,0:T(8,128)(2,1)S(1)} %shard_map.165.refs_2_), channel_id=1, source_target_pairs={{0,16},{4,20},{8,24},{12,28},{16,0},{20,4},{24,8},{28,12},{1,17},{... | collective-permute-start | bytes 393224 | tf_op jit(solution)/shard_map/ppermute | solution.py:524
  57.4 11.0 %collective-permute-start.27 = (bf16[1280,128]{1,0:T(8,128)(2,1)S(1)}, bf16[1280,128]{1,0:T(8,128)(2,1)S(1)}, u32[]{:S(2)}, u32[]{:S(2)}) collective-permute-start(bf16[1280,128]{1,0:T(8,128)(2,1)S(1)} %shard_map.166.refs_17_), channel_id=1, source_target_pairs={{0,8},{4,12},{8,0},{12,4},{16,24},{20,28},{24,16},{28,20},{1,9},{5... | collective-permute-start | bytes 983048 | tf_op jit(solution)/shard_map/ppermute | solution.py:524
  64.0 6.9 %collective-permute-start.24 = (bf16[80,256]{1,0:T(8,128)(2,1)S(1)}, bf16[80,256]{1,0:T(8,128)(2,1)S(1)}, u32[]{:S(2)}, u32[]{:S(2)}) collective-permute-start(bf16[80,256]{1,0:T(8,128)(2,1)S(1)} %get-tuple-element.78), channel_id=1, source_target_pairs={{0,3},{1,2},{2,1},{3,0},{4,7},{5,6},{6,5},{7,4},{8,11},{9,10},{10,... | collective-permute-start | bytes 122888 | tf_op jit(solution)/shard_map/ppermute | solution.py:524
  65.6 5.6 %collective-permute-start.25 = (bf16[80,256]{1,0:T(8,128)(2,1)S(1)}, bf16[80,256]{1,0:T(8,128)(2,1)S(1)}, u32[]{:S(2)}, u32[]{:S(2)}) collective-permute-start(bf16[80,256]{1,0:T(8,128)(2,1)S(1)} %get-tuple-element.79), channel_id=1, source_target_pairs={{0,2},{1,3},{2,0},{3,1},{4,6},{5,7},{6,4},{7,5},{8,10},{9,11},{10,... | collective-permute-start | bytes 122888 | tf_op jit(solution)/shard_map/ppermute | solution.py:524
  66.1 5.2 %collective-permute-start.26 = (bf16[80,256]{1,0:T(8,128)(2,1)S(1)}, bf16[80,256]{1,0:T(8,128)(2,1)S(1)}, u32[]{:S(2)}, u32[]{:S(2)}) collective-permute-start(bf16[80,256]{1,0:T(8,128)(2,1)S(1)} %get-tuple-element.80), channel_id=1, source_target_pairs={{0,1},{1,0},{2,3},{3,2},{4,5},{5,4},{6,7},{7,6},{8,9},{9,8},{10,11... | collective-permute-start | bytes 122888 | tf_op jit(solution)/shard_map/ppermute | solution.py:524
  (25 other events, 113.3 us)
